TPU v7x, 32 devices: a whole 2x2x4 slice. The times are simulated.
32 devices in a mesh: sec: 4 (over x, core), exp: 4 (over z), tp: 2 (over y).
Axes of the slice: x: 2, y: 2, z: 4, core: 2. Of those that a mesh axis runs over, the one named last changes fastest.
Arguments:
- tokens: bfloat16 [4, 1024, 1024], P('sec', 'exp'), may hold values from -6 to 6
- routes: int32 [4, 1024, 2], P('sec', 'exp'), may hold values from 0 to 3, all different within a row; in each aligned block of 256 rows (0 to 255, 256 to 511, ..., all dimensions but the last counted through in order) at most 192 rows name the same one
- gate_weights: float32 [4, 1024, 2], P('sec', 'exp'), may hold values from 0.1 to 0.9
- moe_gain: float32 [4, 1024], P('sec'), may hold values from 0.25 to 1.75
- attn_gain: float32 [4, 1024], P('sec'), may hold values from 0.25 to 1.75
- expert_in: bfloat16 [4, 4, 1024, 4096], P('sec', 'exp', None, 'tp'), may hold values from -0.1875 to 0.1875
- expert_out: bfloat16 [4, 4, 4096, 1024], P('sec', 'exp', 'tp'), may hold values from -0.09375 to 0.09375
- query_weight: bfloat16 [4, 1024, 1024], P('sec', None, 'tp'), may hold values from -0.1875 to 0.1875
- key_weight: bfloat16 [4, 1024, 1024], P('sec', None, 'tp'), may hold values from -0.1875 to 0.1875
- value_weight: bfloat16 [4, 1024, 1024], P('sec', None, 'tp'), may hold values from -0.1875 to 0.1875
- cotangent: bfloat16 [4, 1024, 1024], P('sec', 'exp', 'tp'), may hold values from -24 to 24
Outputs:
- section_out: bfloat16 [4, 1024, 1024], P('sec', 'exp', 'tp')
- enc_grad: bfloat16 [1024, 1024], P('exp', ('sec', 'tp'))
Inputs may be any that keep to these rules, and one draw needn't show every extreme that they name: `routes`: each token names two different experts; among the 256 tokens of one aligned block of a section no expert is named more than 192 times.
All inputs are finite; a program needn't handle non-finite values.
Results may differ from a plain program's by a relative error of at most 0.025.
Values may be sent and summed in bfloat16 or wider, within the bound.
No kernel may reach another device: no remote copies, remote signals or barrier semaphores. Data moves between devices by JAX's collectives and lax.ppermute only.
A program may use at most 64 MiB of HBM per device.

v0:
```python
import math

import jax
import jax.numpy as jnp
from jax import lax
from jax.sharding import PartitionSpec as P

HD = 128
SEQ = 128


EPS = 1e-05


def spread_2(block, axis, source):
    block = jnp.where(lax.axis_index(axis) == source, block, jnp.zeros_like(block))
    return lax.psum(block, axis)


def normalize(values, gain):
    wide = values.astype(jnp.float32)
    average = jnp.mean(wide, axis=-1, keepdims=True)
    centred = wide - average
    spread = jnp.mean(centred * centred, axis=-1, keepdims=True)
    return centred * lax.rsqrt(spread + EPS) * gain


def slot_table(route_block, experts, capacity):
    flat_routes = route_block.reshape(-1)
    labels = jnp.arange(experts, dtype=jnp.int32)
    onehot = (flat_routes[:, None] == labels[None, :]).astype(jnp.int32)
    before = jnp.cumsum(onehot, axis=0) - onehot
    position = jnp.sum(before * onehot, axis=1)
    slot_index = flat_routes * capacity + position
    targets = jnp.arange(experts * capacity, dtype=jnp.int32)
    table = (targets[:, None] == slot_index[None, :]).astype(jnp.bfloat16)
    return table.reshape(experts * capacity, route_block.shape[0], 2)


def shards(
    tokens,
    routes,
    gate_weights,
    moe_gain,
    attn_gain,
    expert_in,
    expert_out,
    query_weight,
    key_weight,
    value_weight,
    cotangent,
):
    token_rows = tokens[0]
    route_rows = routes[0]
    gate_rows = gate_weights[0]
    token_count = token_rows.shape[0]
    model_width = token_rows.shape[1]
    experts = lax.axis_size("exp")
    capacity = 3 * token_count // experts
    normed = normalize(token_rows, moe_gain[0]).astype(jnp.bfloat16)
    table = slot_table(route_rows, experts, capacity)
    weight_first = expert_in[0, 0]
    weight_second = expert_out[0, 0]
    outgoing = jnp.einsum("jtk,td->jd", table, normed, preferred_element_type=jnp.float32)
    outgoing = outgoing.astype(jnp.bfloat16).reshape(experts, capacity, normed.shape[1])
    arrived = lax.all_to_all(outgoing, "exp", split_axis=0, concat_axis=0, tiled=True)
    sources = arrived.shape[0]
    slot_count = arrived.shape[1]
    row_block = arrived.reshape(sources * slot_count, model_width)
    inner = jnp.maximum(
        jnp.dot(row_block, weight_first, preferred_element_type=jnp.float32), 0.0
    ).astype(jnp.bfloat16)
    partial_value = jnp.dot(inner, weight_second, preferred_element_type=jnp.float32)
    finished = lax.psum_scatter(partial_value, "tp", scatter_dimension=1, tiled=True).astype(
        jnp.bfloat16
    )
    finished = finished.reshape(sources, slot_count, finished.shape[1])
    returned = lax.all_to_all(finished, "exp", split_axis=0, concat_axis=0, tiled=True)
    returned = lax.all_gather(returned, "tp", axis=2, tiled=True)
    picked = jnp.einsum(
        "jtk,jd->tkd",
        table,
        returned.reshape(experts * capacity, model_width),
        preferred_element_type=jnp.float32,
    )
    mixed = (
        token_rows.astype(jnp.float32)
        + gate_rows[:, 0:1] * picked[:, 0, :]
        + gate_rows[:, 1:2] * picked[:, 1, :]
    )
    hidden = mixed.astype(jnp.bfloat16)
    encoder = spread_2(hidden, "sec", 0)
    query_w = query_weight[0]
    key_w = key_weight[0]
    value_w = value_weight[0]
    local_width = query_w.shape[1]
    local_heads = local_width // HD
    sequences = token_count // SEQ
    shape = (sequences, SEQ, local_heads, HD)
    scale = 1.0 / math.sqrt(HD)
    query_in = normalize(hidden, attn_gain[0]).astype(jnp.bfloat16)
    queries = (
        jnp.dot(query_in, query_w, preferred_element_type=jnp.float32)
        .astype(jnp.bfloat16)
        .reshape(shape)
    )
    key_rows = (
        jnp.dot(encoder, key_w, preferred_element_type=jnp.float32)
        .astype(jnp.bfloat16)
        .reshape(shape)
    )
    value_rows = (
        jnp.dot(encoder, value_w, preferred_element_type=jnp.float32)
        .astype(jnp.bfloat16)
        .reshape(shape)
    )
    scores = (
        jnp.einsum("sqhd,skhd->shqk", queries, key_rows, preferred_element_type=jnp.float32) * scale
    )
    powers = jnp.exp(scores)
    probs = powers / jnp.sum(powers, axis=-1, keepdims=True)
    probs_low = probs.astype(jnp.bfloat16)
    context = jnp.einsum(
        "shqk,skhd->sqhd", probs_low, value_rows, preferred_element_type=jnp.float32
    )
    context = context.astype(jnp.bfloat16).reshape(token_count, local_width)
    upstream = cotangent[0].reshape(shape)
    dprobs = jnp.einsum("sqhd,skhd->shqk", upstream, value_rows, preferred_element_type=jnp.float32)
    rowdot = jnp.sum(dprobs * probs, axis=-1, keepdims=True)
    dscores = (probs * (dprobs - rowdot)).astype(jnp.bfloat16)
    dvalues = jnp.einsum("shqk,sqhd->skhd", probs_low, upstream, preferred_element_type=jnp.float32)
    dvalues = dvalues.astype(jnp.bfloat16).reshape(token_count, local_width)
    dkeys = (
        jnp.einsum("shqk,sqhd->skhd", dscores, queries, preferred_element_type=jnp.float32) * scale
    )
    dkeys = dkeys.astype(jnp.bfloat16).reshape(token_count, local_width)
    contract = (((1,), (1,)), ((), ()))
    term = lax.dot_general(dkeys, key_w, contract, preferred_element_type=jnp.float32)
    term = term + lax.dot_general(dvalues, value_w, contract, preferred_element_type=jnp.float32)
    is_encoder = lax.axis_index("sec") == 0
    term = jnp.where(is_encoder, jnp.zeros_like(term), term)
    enc_grad = lax.psum_scatter(
        term.astype(jnp.bfloat16), ("sec", "tp"), scatter_dimension=1, tiled=True
    )
    own_columns = lax.dynamic_slice_in_dim(
        hidden, lax.axis_index("tp") * local_width, local_width, 1
    )
    section_out = jnp.where(is_encoder, own_columns, context)
    return (section_out[None], enc_grad)


def solution(mesh):
    placed = (
        P("sec", "exp", None),
        P("sec", "exp", None),
        P("sec", "exp", None),
        P("sec", None),
        P("sec", None),
        P("sec", "exp", None, "tp"),
        P("sec", "exp", "tp", None),
        P("sec", None, "tp"),
        P("sec", None, "tp"),
        P("sec", None, "tp"),
        P("sec", "exp", "tp"),
    )
    return jax.shard_map(
        shards,
        mesh=mesh,
        in_specs=placed,
        out_specs=(P("sec", "exp", "tp"), P("exp", ("sec", "tp"))),
        check_vma=False,
    )
```

profile of v0, /device:TPU:0, one launch (start us, length us, event | category | flops | bytes accessed | tf_op | source)
XLA Modules:
  0.0 256.2 jit_solution(9789329850392135928)
XLA Ops:
  7.2 0.9 copy.59
  8.2 0.1 eq.71
  8.3 0.1 eq.67
  8.5 1.2 reduce-window.6
  9.7 0.2 slice_reduce_fusion
  9.9 0.2 reduce-window.9
  10.1 0.1 add_bitcast_fusion
  10.2 0.1 reduce_sum.75
  10.4 0.3 convert_reduce_fusion
  10.8 1.2 convert_reduce_fusion.1
  12.0 0.3 fusion.21
  12.3 0.7 convolution_convert_fusion
  13.0 43.2 %all_to_all.10 = bf16[4,192,1024]{2,1,0:T(8,128)(2,1)S(1)} all-to-all(bf16[4,192,1024]{2,1,0:T(8,128)(2,1)S(1)} %bitcast.145), channel_id=1, replica_groups=mesh['sec'=4,'exp'=4,'tp'=2] {'exp'}, dimensions={0} | all-to-all | bytes 3145728 | tf_op jit(solution)/shard_map/all_to_all | solution.py:66
  56.2 3.6 %maximum_convert_fusion = bf16[768,2048]{1,0:T(8,128)(2,1)S(1)} fusion(bf16[768,1024]{1,0:T(8,128)(2,1)S(1)} %bitcast.148, bf16[1,1,1024,2048]{3,2,1,0:T(8,128)(2,1)S(1)} %copy-done.14), kind=kOutput, calls=%fused_computation | convolution fusion | flops 3224371200 | bytes 8912896 | tf_op jit(solution)/shard_map/dot_general | solution.py:71
  59.9 5.1 %fusion = f32[768,1024]{1,0:T(8,128)} fusion(bf16[768,2048]{1,0:T(8,128)(2,1)S(1)} %maximum_convert_fusion, bf16[1,1,2048,1024]{3,2,1,0:T(8,128)(2,1)S(1)} %copy-done.15), kind=kOutput, calls=%fused_computation.1 | convolution fusion | flops 3221225472 | bytes 10485760 | tf_op jit(solution)/shard_map/dot_general | solution.py:73
  65.1 42.6 %reduce-scatter.5.cloned.1.call-done = f32[768,512]{1,0:T(8,128)} async-done(((f32[768,1024]{1,0:T(8,128)}), f32[768,512]{1,0:T(8,128)}) %reduce-scatter.5.cloned.1.call-update) | async-done | bytes 1572880 | tf_op jit(solution)/shard_map/reduce_scatter | solution.py:74
  107.6 1.5 convert_element_type.97
  109.1 24.6 %all_to_all.11 = bf16[4,192,512]{2,1,0:T(8,128)(2,1)} all-to-all(bf16[4,192,512]{2,1,0:T(8,128)(2,1)S(1)} %bitcast.146), channel_id=1, replica_groups=mesh['sec'=4,'exp'=4,'tp'=2] {'exp'}, dimensions={0} | all-to-all | bytes 1572864 | tf_op jit(solution)/shard_map/all_to_all | solution.py:78
  133.8 0.8 reshape_squeeze.4
  134.6 24.6 %all-gather.2.cloned.1.call-done = bf16[4,192,1024]{2,1,0:T(8,128)(2,1)} async-done(((bf16[4,192,512]{2,1,0:T(8,128)(2,1)}), bf16[4,192,1024]{2,1,0:T(8,128)(2,1)}) %all-gather.2.cloned.1.call-update) | async-done | bytes 1572880 | tf_op jit(solution)/shard_map/all_gather | solution.py:79
  159.3 2.4 fusion.7
  161.7 1.3 copy-done.4
  163.1 0.4 convert_reduce_fusion.2
  163.5 0.3 fusion.25
  163.8 0.9 broadcast_select_fusion
  164.6 0.2 reduce-scatter.7.cloned.1.call-start
  164.9 2.1 convolution_convert_fusion.4
  167.1 0.9 copy.71
  167.9 30.0 %all-reduce.2.cloned.1.call-done = bf16[256,1024]{1,0:T(8,128)(2,1)} async-done(((bf16[256,1024]{1,0:T(8,128)(2,1)}), bf16[256,1024]{1,0:T(8,128)(2,1)}) %all-reduce.2.cloned.1.call-update) | async-done | bytes 524304 | tf_op jit(solution)/shard_map/psum | solution.py:17
  198.0 1.5 convolution_convert_fusion.3
  199.5 0.8 reshape.224
  200.3 2.2 fusion.57
  202.4 2.0 fusion.16
  204.4 0.4 convolution_convert_fusion.5
  204.9 2.3 fusion.20
  207.3 2.2 multiply_reduce_fusion
  209.4 1.7 fusion.18
  211.1 0.2 copy.74
  211.3 0.5 fusion.30
  211.8 0.3 copy-done.11
  212.1 0.2 copy.76
  212.3 0.5 fusion.13
  212.8 1.0 copy.80
  213.8 1.5 fusion.19
  215.3 0.2 copy.68
  215.5 0.8 fusion.53
  216.3 31.8 %reduce-scatter.7.cloned.1.call-done = bf16[128,256]{1,0:T(8,128)(2,1)} async-done(((bf16[1024,256]{1,0:T(8,128)(2,1)}), bf16[128,256]{1,0:T(8,128)(2,1)}) %reduce-scatter.7.cloned.1.call-update) | async-done | bytes 65552
  248.1 1.6 copy.81
  (52 shorter events, 0.6 us)
Async XLA Ops:
  7.2 190.8 %copy-start = (bf16[1,1024,512]{2,1,0:T(8,128)(2,1)S(1)}, bf16[1,1024,512]{2,1,0:T(8,128)(2,1)}, u32[]{:S(2)}) copy-start(bf16[1,1024,512]{2,1,0:T(8,128)(2,1)} %param.19) | copy-start | bytes 3145732
  7.2 4.8 %copy-start.1 = (bf16[1,256,1024]{2,1,0:T(8,128)(2,1)S(1)}, bf16[1,256,1024]{2,1,0:T(8,128)(2,1)}, u32[]{:S(2)}) copy-start(bf16[1,256,1024]{2,1,0:T(8,128)(2,1)} %param.11) | copy-start | bytes 1572868
  7.2 5.1 %copy-start.12 = (f32[1,1024]{1,0:T(1,128)S(1)}, f32[1,1024]{1,0:T(1,128)}, u32[]{:S(2)}) copy-start(f32[1,1024]{1,0:T(1,128)} %param.14) | copy-start | bytes 12292
  7.2 100.4 %reduce-scatter.5.cloned.1.call-start = ((), (), s32[]{:S(2)}) async-start(), calls=%async_computation.4 | async-start | bytes 4718592 | tf_op jit(solution)/shard_map/reduce_scatter | solution.py:74
  12.3 43.9 %copy-start.14 = (bf16[1,1,1024,2048]{3,2,1,0:T(8,128)(2,1)S(1)}, bf16[1,1,1024,2048]{3,2,1,0:T(8,128)(2,1)}, u32[]{:S(2)}) copy-start(bf16[1,1,1024,2048]{3,2,1,0:T(8,128)(2,1)} %param.16) | copy-start | bytes 12582916
  56.2 3.6 %copy-start.15 = (bf16[1,1,2048,1024]{3,2,1,0:T(8,128)(2,1)S(1)}, bf16[1,1,2048,1024]{3,2,1,0:T(8,128)(2,1)}, u32[]{:S(2)}) copy-start(bf16[1,1,2048,1024]{3,2,1,0:T(8,128)(2,1)} %param.17) | copy-start | bytes 12582916
  65.0 68.9 %copy-start.10 = (bf16[1,256,512]{2,1,0:T(8,128)(2,1)S(1)}, bf16[1,256,512]{2,1,0:T(8,128)(2,1)}, u32[]{:S(2)}) copy-start(bf16[1,256,512]{2,1,0:T(8,128)(2,1)} %param.21) | copy-start | bytes 786436
  65.0 69.6 %copy-start.13 = (f32[1,256,2]{1,2,0:T(2,128)S(1)}, f32[1,256,2]{1,2,0:T(2,128)}, u32[]{:S(2)}) copy-start(f32[1,256,2]{1,2,0:T(2,128)} %param.13) | copy-start | bytes 6148
  65.0 94.3 %all-gather.2.cloned.1.call-start = ((), (), s32[]{:S(2)}) async-start(), calls=%async_computation.5 | async-start | bytes 2359296 | tf_op jit(solution)/shard_map/all_gather | solution.py:79
  133.8 64.2 %all-reduce.2.cloned.1.call-start = ((), (), s32[]{:S(2)}) async-start(), calls=%async_computation.6 | async-start | bytes 1048576 | tf_op jit(solution)/shard_map/psum | solution.py:17
  161.7 1.4 copy-start.4
  163.1 1.8 copy-start.16
  163.1 1.8 copy-start.17
  164.6 83.4 %reduce-scatter.7.cloned.1.call-start = ((), (), s32[]{:S(2)}) async-start(), calls=%async_computation.7 | async-start | bytes 589824
  199.5 4.9 %copy-start.2 = (bf16[1,1024,512]{2,1,0:T(8,128)(2,1)S(1)}, bf16[1,1024,512]{2,1,0:T(8,128)(2,1)}, u32[]{:S(2)}) copy-start(bf16[1,1024,512]{2,1,0:T(8,128)(2,1)} %param.20) | copy-start | bytes 3145732
  199.5 4.9 %copy-start.3 = (bf16[256,1024]{1,0:T(8,128)(2,1)S(1)}, bf16[256,1024]{1,0:T(8,128)(2,1)}, u32[]{:S(2)}) copy-start(bf16[256,1024]{1,0:T(8,128)(2,1)} %all-reduce.2.cloned.1.call-done) | copy-start | bytes 1572868
  200.3 2.2 copy-start.8
  204.8 2.4 copy-start.5
  204.9 6.2 %copy-start.6 = (bf16[2,128,4,128]{3,2,1,0:T(4,128)(2,1)}, bf16[2,128,4,128]{3,2,1,0:T(4,128)(2,1)S(1)}, u32[]{:S(2)}) copy-start(bf16[2,128,4,128]{3,2,1,0:T(4,128)(2,1)S(1)} %reshape.222) | copy-start | bytes 786436
  204.9 4.5 %copy-start.9 = (bf16[2,128,4,128]{1,3,2,0:T(8,128)(2,1)S(1)}, bf16[2,128,4,128]{1,3,2,0:T(8,128)(2,1)}, u32[]{:S(2)}) copy-start(bf16[2,128,4,128]{1,3,2,0:T(8,128)(2,1)} %copy.71) | copy-start | bytes 786436
  211.1 1.0 copy-start.11
  212.3 1.5 copy-start.7
Sparse Core Ops, SparseCore 0:
  65.1 42.4 reduce-scatter.4
  133.9 25.3 all-gather.1
  164.8 33.1 all-reduce.1
  213.9 34.0 reduce-scatter.6
where the time goes:
time: 257 us; the launch traced here: 256 us
  waiting for transfers between devices  129 us (50%)
  blocking collectives  67.8 us (26%)
  matrix products  28.5 us (11%)
  between operations  14.1 us (5%)
  local copies, waits for them, and re-layouts  9.08 us (4%)
  other arithmetic  7.19 us (3%)
    all_to_all x1, blocking collectives, shards(): lax.all_to_all(outgoing, 'exp', split_axis=0, concat_axis=0, tiled=True)  43.2 us
    reduce_scatter x1, waiting for transfers between devices, shards(): lax.psum_scatter(partial_value, 'tp', scatter_dimension=1, tiled=True)  42.6 us
    unnamed x5, waiting for transfers between devices  31.8 us
    psum x1, waiting for transfers between devices, spread_2(): return lax.psum(block, axis)  30 us
    all_gather x1, waiting for transfers between devices, shards(): returned = lax.all_gather(returned, 'tp', axis=2, tiled=True)  24.6 us
    all_to_all x1, blocking collectives, shards(): lax.all_to_all(finished, 'exp', split_axis=0, concat_axis=0, tiled=True)  24.6 us
    unnamed x39, local copies, waits for them, and re-layouts  5.19 us
  transfers between devices with their start and end apart: 4, of which 4 were waited for; matrix products, arithmetic and copies ran while one was open for 2% of the time, Pallas kernels for 0%

commit v1 on v0

v1 whole, which is shorter than its diff:
```python
import math

import jax
import jax.numpy as jnp
from jax import lax
from jax.sharding import PartitionSpec as P

HD = 128
SEQ = 128


EPS = 1e-05


def swap(block, axis, step):
    size = lax.axis_size(axis)
    return lax.ppermute(block, axis, [(i, i ^ step) for i in range(size)])


def send(block, axis, pairs):
    return lax.ppermute(block, axis, pairs)


def normalize(values, gain):
    wide = values.astype(jnp.float32)
    average = jnp.mean(wide, axis=-1, keepdims=True)
    centred = wide - average
    spread = jnp.mean(centred * centred, axis=-1, keepdims=True)
    return centred * lax.rsqrt(spread + EPS) * gain


def halves(mine, other, tp):
    low = jnp.where(tp == 0, mine, other)
    high = jnp.where(tp == 0, other, mine)
    return jnp.concatenate([low, high], axis=1)


def column_part(block, index, width):
    return lax.dynamic_slice_in_dim(block, index * width, width, 1)


def shards(
    tokens,
    routes,
    gate_weights,
    moe_gain,
    attn_gain,
    expert_in,
    expert_out,
    query_weight,
    key_weight,
    value_weight,
    cotangent,
):
    token_rows = tokens[0]
    route_rows = routes[0]
    gate_rows = gate_weights[0]
    token_count, model_width = token_rows.shape
    experts = lax.axis_size("exp")
    sections = lax.axis_size("sec")
    tp_size = lax.axis_size("tp")
    me = lax.axis_index("exp")
    tp = lax.axis_index("tp")
    sec = lax.axis_index("sec")
    half = model_width // tp_size
    capacity = 3 * token_count // experts
    weight_first = expert_in[0, 0]
    weight_second = expert_out[0, 0]

    normed = normalize(token_rows, moe_gain[0]).astype(jnp.bfloat16)
    normed_half = column_part(normed, tp, half)
    token_half = column_part(token_rows, tp, half)

    labels = jnp.arange(experts, dtype=jnp.int32) ^ me
    named = [(route_rows[:, k : k + 1] == labels[None, :]) for k in range(2)]
    either = named[0] | named[1]
    earlier = jnp.arange(token_count)
    earlier = (earlier[:, None] > earlier[None, :]).astype(jnp.bfloat16)
    before = jnp.dot(
        earlier, either.astype(jnp.bfloat16), preferred_element_type=jnp.float32
    ).astype(jnp.int32)
    place = jnp.where(either, before, -1)
    slots = jnp.arange(capacity, dtype=jnp.int32)
    tables = [
        (place[:, e][:, None] == slots[None, :]).astype(jnp.bfloat16) for e in range(experts)
    ]
    gates = jnp.where(named[0], gate_rows[:, 0:1], 0.0) + jnp.where(
        named[1], gate_rows[:, 1:2], 0.0
    )

    def pick(table, rows):
        return lax.dot_general(
            table, rows, (((0,), (0,)), ((), ())), preferred_element_type=jnp.float32
        ).astype(jnp.bfloat16)

    def expert(rows):
        inner = jnp.maximum(
            jnp.dot(rows, weight_first, preferred_element_type=jnp.float32), 0.0
        ).astype(jnp.bfloat16)
        return jnp.dot(inner, weight_second, preferred_element_type=jnp.float32)

    far = {}
    for k in range(experts - 1, 1, -1):
        far[k] = swap(pick(tables[k], normed_half), "exp", k)
    near = swap(pick(tables[1], normed), "exp", 1)
    rows_in = {0: pick(tables[0], normed), 1: near}
    for k in range(experts - 1, 1, -1):
        rows_in[k] = halves(far[k], swap(far[k], "tp", 1), tp)

    returned = {}
    for k in [0, 1] + list(range(experts - 1, 1, -1)):
        partial = expert(rows_in[k])
        away = column_part(partial, 1 - tp, half).astype(jnp.bfloat16)
        kept = column_part(partial, tp, half)
        total = (kept + swap(away, "tp", 1).astype(jnp.float32)).astype(jnp.bfloat16)
        returned[k] = total if k == 0 else swap(total, "exp", k)

    mixed = token_half.astype(jnp.float32)
    for k in range(experts):
        picked = jnp.dot(tables[k], returned[k], preferred_element_type=jnp.float32)
        mixed = mixed + gates[:, k : k + 1] * picked
    hidden_half = mixed.astype(jnp.bfloat16)

    spread = hidden_half
    step = sections // 2
    while step >= 1:
        moved = send(spread, "sec", [(i, i + step) for i in range(0, sections, 2 * step)])
        spread = jnp.where((sec % (2 * step)) == step, moved, spread)
        step //= 2
    hidden = halves(hidden_half, swap(hidden_half, "tp", 1), tp)
    encoder = halves(spread, swap(spread, "tp", 1), tp)

    query_w = query_weight[0]
    key_w = key_weight[0]
    value_w = value_weight[0]
    local_width = query_w.shape[1]
    local_heads = local_width // HD
    sequences = token_count // SEQ
    shape = (sequences, SEQ, local_heads, HD)
    scale = 1.0 / math.sqrt(HD)
    query_in = normalize(hidden, attn_gain[0]).astype(jnp.bfloat16)
    queries = (
        jnp.dot(query_in, query_w, preferred_element_type=jnp.float32)
        .astype(jnp.bfloat16)
        .reshape(shape)
    )
    key_rows = (
        jnp.dot(encoder, key_w, preferred_element_type=jnp.float32)
        .astype(jnp.bfloat16)
        .reshape(shape)
    )
    value_rows = (
        jnp.dot(encoder, value_w, preferred_element_type=jnp.float32)
        .astype(jnp.bfloat16)
        .reshape(shape)
    )
    scores = (
        jnp.einsum("sqhd,skhd->shqk", queries, key_rows, preferred_element_type=jnp.float32) * scale
    )
    powers = jnp.exp(scores)
    probs = powers / jnp.sum(powers, axis=-1, keepdims=True)
    probs_low = probs.astype(jnp.bfloat16)
    context = jnp.einsum(
        "shqk,skhd->sqhd", probs_low, value_rows, preferred_element_type=jnp.float32
    )
    context = context.astype(jnp.bfloat16).reshape(token_count, local_width)
    upstream = cotangent[0].reshape(shape)
    dprobs = jnp.einsum("sqhd,skhd->shqk", upstream, value_rows, preferred_element_type=jnp.float32)
    rowdot = jnp.sum(dprobs * probs, axis=-1, keepdims=True)
    dscores = (probs * (dprobs - rowdot)).astype(jnp.bfloat16)
    dvalues = jnp.einsum("shqk,sqhd->skhd", probs_low, upstream, preferred_element_type=jnp.float32)
    dvalues = dvalues.astype(jnp.bfloat16).reshape(token_count, local_width)
    dkeys = (
        jnp.einsum("shqk,sqhd->skhd", dscores, queries, preferred_element_type=jnp.float32) * scale
    )
    dkeys = dkeys.astype(jnp.bfloat16).reshape(token_count, local_width)
    contract = (((1,), (1,)), ((), ()))
    term = lax.dot_general(dkeys, key_w, contract, preferred_element_type=jnp.float32)
    term = term + lax.dot_general(dvalues, value_w, contract, preferred_element_type=jnp.float32)
    is_encoder = sec == 0
    term = jnp.where(is_encoder, jnp.zeros_like(term), term)

    own = model_width // (sections * tp_size)
    parts = term.reshape(token_count, sections // 2, 2, tp_size * own)
    side = sec % 2
    mine = lax.dynamic_index_in_dim(parts, side, 2, keepdims=False)
    other = lax.dynamic_index_in_dim(parts, 1 - side, 2, keepdims=False)
    mine = mine + swap(other.astype(jnp.bfloat16), "sec", 1).astype(jnp.float32)
    mine = mine.reshape(token_count, model_width // 2)
    here = (sec // 2) * tp_size + tp
    total = column_part(mine, here, own)
    count = sections // 2 * tp_size
    both = sections * tp_size
    for k in range(1, count):
        pairs = []
        for i in range(both):
            place_of, tp_of = i // tp_size, i % tp_size
            target = ((place_of // 2) * tp_size + tp_of) ^ k
            pairs.append((i, (target // tp_size * 2 + place_of % 2) * tp_size + target % tp_size))
        block = column_part(mine, here ^ k, own).astype(jnp.bfloat16)
        total = total + lax.ppermute(block, ("sec", "tp"), pairs).astype(jnp.float32)
    enc_grad = total.astype(jnp.bfloat16)
    section_out = jnp.where(is_encoder, hidden_half, context)
    return (section_out[None], enc_grad)


def solution(mesh):
    placed = (
        P("sec", "exp", None),
        P("sec", "exp", None),
        P("sec", "exp", None),
        P("sec", None),
        P("sec", None),
        P("sec", "exp", None, "tp"),
        P("sec", "exp", "tp", None),
        P("sec", None, "tp"),
        P("sec", None, "tp"),
        P("sec", None, "tp"),
        P("sec", "exp", "tp"),
    )
    return jax.shard_map(
        shards,
        mesh=mesh,
        in_specs=placed,
        out_specs=(P("sec", "exp", "tp"), P("exp", ("sec", "tp"))),
        check_vma=False,
    )
```

time: 257 us -> 124 us (0.48)
  waiting for transfers between devices: 129 us -> 28.8 us
  blocking collectives: 67.8 us -> 0 us
  starting transfers between devices: 0.34 us -> 29.8 us
  matrix products: 28.5 us -> 42 us
  between operations: 14.1 us -> 1.17 us
  other arithmetic: 7.19 us -> 13 us
    all_to_all x2 -> x0, blocking collectives: 67.8 us -> none  [the longest x1 43.2 us: shards(): lax.all_to_all(outgoing, 'exp', split_axis=0, concat_axis=0, tiled=True)]
    reduce_scatter x1 -> x0, waiting for transfers between devices: 42.6 us -> none  [shards(): lax.psum_scatter(partial_value, 'tp', scatter_dimension=1, tiled=True)]
    unnamed x5 -> x0, waiting for transfers between devices: 31.8 us -> none
    psum x1 -> x0, waiting for transfers between devices: 30 us -> none  [spread_2(): return lax.psum(block, axis)]
    ppermute x0 -> x20, starting transfers between devices: none -> 29.8 us  [the longest x15 20.7 us: swap(): return lax.ppermute(block, axis, [(i, i ^ step) for i in range(size)])]
    ppermute x0 -> x20, waiting for transfers between devices: none -> 28.8 us  [the longest x15 24.8 us: swap(): return lax.ppermute(block, axis, [(i, i ^ step) for i in range(size)])]
    all_gather x1 -> x0, waiting for transfers between devices: 24.6 us -> none  [shards(): returned = lax.all_gather(returned, 'tp', axis=2, tiled=True)]
    dot_general x4 -> x13, matrix products: 11.8 us -> 28.4 us  [the longest x4 21.3 us: expert(): return jnp.dot(inner, weight_second, preferred_element_type=jnp.float32)]
  transfers between devices with their start and end apart: 4 -> 20, of which waited for: 4 -> 10; matrix products, arithmetic and copies ran while one was open for 2% -> 34% of each run, Pallas kernels for 0% -> 0%
where the time goes in v1:
time: 124 us
  matrix products  42 us (34%)
  starting transfers between devices  29.8 us (24%)
  waiting for transfers between devices  28.8 us (23%)
  other arithmetic  13 us (10%)
  local copies, waits for them, and re-layouts  9 us (7%)
    ppermute x15, waiting for transfers between devices, swap(): return lax.ppermute(block, axis, [(i, i ^ step) for i in range(size)])  24.8 us
    dot_general x4, matrix products, expert(): return jnp.dot(inner, weight_second, preferred_element_type=jnp.float32)  21.3 us
    ppermute x15, starting transfers between devices, swap(): return lax.ppermute(block, axis, [(i, i ^ step) for i in range(size)])  20.7 us
    ppermute x2, starting transfers between devices, send(): return lax.ppermute(block, axis, pairs)  4.91 us
    select_n x4, other arithmetic, halves(): low = jnp.where(tp == 0, mine, other)  4.54 us
    ppermute x3, starting transfers between devices, shards(): lax.ppermute(block, ('sec', 'tp'), pairs).astype(jnp.float32)  4.15 us
    convert_element_type x4, local copies, waits for them, and re-layouts, shards(): away = column_part(partial, 1 - tp, half).astype(jnp.bfloat16)  3.52 us
    dot_general x1, matrix products, expert(): jnp.dot(rows, weight_first, preferred_element_type=jnp.float32)  3.41 us
  transfers between devices with their start and end apart: 20, of which 10 were waited for; matrix products, arithmetic and copies ran while one was open for 34% of the time, Pallas kernels for 0%

profile of v1, /device:TPU:0, one launch (start us, length us, event | category | flops | bytes accessed | tf_op | source)
XLA Modules:
  0.0 123.7 jit_solution(12799360280949036983)
XLA Ops:
  0.6 1.3 %convert_reduce_fusion.1 = f32[256]{0:T(256)S(1)} fusion(bf16[1,256,1024]{2,1,0:T(8,128)(2,1)} %param.11), kind=kLoop, calls=%fused_computation.28 | loop fusion | flops 524032 | bytes 525312 | tf_op jit(solution)/shard_map/reduce_sum | solution.py:26
  1.9 1.3 %fusion.60 = f32[256]{0:T(256)S(1)} fusion(bf16[1,256,1024]{2,1,0:T(8,128)(2,1)} %param.11, f32[256]{0:T(256)S(1)} %broadcast_multiply_fusion.1), kind=kLoop, calls=%fused_computation.66 | loop fusion | flops 1048320 | bytes 526336 | tf_op jit(solution)/shard_map/reduce_sum | solution.py:28
  3.3 0.8 fusion.144
  4.2 1.3 %fusion.62 = bf16[256,1024]{1,0:T(8,128)(2,1)S(1)} fusion(bf16[1,256,1024]{2,1,0:T(8,128)(2,1)} %param.11, f32[1024]{0:T(1024)} %bitcast.143, f32[256]{0:T(256)S(1)} %add_rsqrt_fusion.1, f32[256]{0:T(256)S(1)} %broadcast_multiply_fusion.1), kind=kLoop, calls=%fused_computation.68 | loop fusion | flops 1310720 | bytes 1054720 | tf_op jit(solution)/shard_map/convert_element_type | solution.py:70
  5.6 1.0 convolution_convert_fusion.7
  6.6 5.1 %collective-permute-start.8 = (bf16[192,512]{1,0:T(8,128)(2,1)}, bf16[192,512]{1,0:T(8,128)(2,1)}, u32[]{:S(2)}, u32[]{:S(2)}) collective-permute-start(bf16[192,512]{1,0:T(8,128)(2,1)} %convolution_convert_fusion.7), channel_id=1, source_target_pairs={{0,6},{2,4},{4,2},{6,0},{1,7},{3,5},{5,3},{7,1},{8,14},{10,12},{12... | collective-permute-start | bytes 589832 | tf_op jit(solution)/shard_map/ppermute | solution.py:17
  11.6 1.0 convolution_convert_fusion.8
  13.7 3.4 %fusion.37 = bf16[192,2048]{1,0:T(8,128)(2,1)S(1)} fusion(bf16[1,1,1024,2048]{3,2,1,0:T(8,128)(2,1)} %param.16, bf16[256,1024]{1,0:T(8,128)(2,1)S(1)} %fusion.62, s32[256]{0:T(256)S(1)} %bitcast.144), kind=kOutput, calls=%fused_computation.23 | convolution fusion | flops 907001856 | bytes 5506048 | tf_op jit(solution)/shard_map/dot_general | solution.py:98
  17.1 3.2 %fusion.6 = f32[192,1024]{1,0:T(8,128)S(1)} fusion(bf16[192,2048]{1,0:T(8,128)(2,1)S(1)} %fusion.37, bf16[1,1,2048,1024]{3,2,1,0:T(8,128)(2,1)} %param.17), kind=kOutput, calls=%fused_computation.6 | convolution fusion | flops 805306368 | bytes 5767168 | tf_op jit(solution)/shard_map/dot_general | solution.py:100
  20.3 1.8 %collective-permute-start = (bf16[192,512]{1,0:T(8,128)(2,1)S(1)}, bf16[192,512]{1,0:T(8,128)(2,1)S(1)}, u32[]{:S(2)}, u32[]{:S(2)}) collective-permute-start(bf16[192,512]{1,0:T(8,128)(2,1)S(1)} %dynamic-slice_convert_fusion.3), channel_id=1, source_target_pairs={{0,1},{1,0},{2,3},{3,2},{4,5},{5,4},{6,7},{7,6},{8,9},{9,8},{10,11... | collective-permute-start | bytes 589832 | tf_op jit(solution)/shard_map/ppermute | solution.py:17
  22.5 6.2 %collective-permute-done.4 = bf16[192,512]{1,0:T(8,128)(2,1)} collective-permute-done((bf16[192,512]{1,0:T(8,128)(2,1)}, bf16[192,512]{1,0:T(8,128)(2,1)}, u32[]{:S(2)}, u32[]{:S(2)}) %collective-permute-start.4) | collective-permute-done | bytes 196640 | tf_op jit(solution)/shard_map/ppermute | solution.py:17
  28.8 1.5 %collective-permute-start.5 = (bf16[192,512]{1,0:T(8,128)(2,1)}, bf16[192,512]{1,0:T(8,128)(2,1)}, u32[]{:S(2)}, u32[]{:S(2)}) collective-permute-start(bf16[192,512]{1,0:T(8,128)(2,1)} %collective-permute-done.4), channel_id=1, source_target_pairs={{0,1},{1,0},{2,3},{3,2},{4,5},{5,4},{6,7},{7,6},{8,9},{9,8},{10,11... | collective-permute-start | bytes 589832 | tf_op jit(solution)/shard_map/ppermute | solution.py:17
  30.7 1.7 %broadcast_select_fusion.7 = (bf16[192,512]{1,0:T(8,128)(2,1)}, bf16[192,512]{1,0:T(8,128)(2,1)}) fusion(bf16[192,512]{1,0:T(8,128)(2,1)} %collective-permute-done.8, bf16[192,512]{1,0:T(8,128)(2,1)S(1)} %collective-permute-done.9, pred[]{:T(512)S(6)} %eq.131), kind=kLoop, calls=%fused_computation.127 | loop fusion | flops 196608 | bytes 786433 | tf_op jit(solution)/shard_map/jit(_where)/select_n | solution.py:33
  32.4 5.5 %fusion = f32[192,1024]{1,0:T(8,128)S(1)} fusion(bf16[1,1,2048,1024]{3,2,1,0:T(8,128)(2,1)} %param.17, bf16[1,1,1024,2048]{3,2,1,0:T(8,128)(2,1)} %param.16, bf16[192,512]{1,0:T(8,128)(2,1)} %get-tuple-element.14, bf16[192,512]{1,0:T(8,128)(2,1)} %get-tuple-element.13), kind=kOutput, calls=%fused_computation | convolution fusion | flops 1612185600 | bytes 9568256 | tf_op jit(solution)/shard_map/dot_general | solution.py:100
  37.8 0.7 dynamic-slice_convert_fusion
  38.6 1.5 %collective-permute-start.10 = (bf16[192,512]{1,0:T(8,128)(2,1)}, bf16[192,512]{1,0:T(8,128)(2,1)}, u32[]{:S(2)}, u32[]{:S(2)}) collective-permute-start(bf16[192,512]{1,0:T(8,128)(2,1)} %dynamic-slice_convert_fusion), channel_id=1, source_target_pairs={{0,1},{1,0},{2,3},{3,2},{4,5},{5,4},{6,7},{7,6},{8,9},{9,8},{10,11... | collective-permute-start | bytes 589832 | tf_op jit(solution)/shard_map/ppermute | solution.py:17
  40.1 1.8 %broadcast_select_fusion.9 = (bf16[192,512]{1,0:T(8,128)(2,1)}, bf16[192,512]{1,0:T(8,128)(2,1)}) fusion(bf16[192,512]{1,0:T(8,128)(2,1)} %collective-permute-done.4, bf16[192,512]{1,0:T(8,128)(2,1)} %collective-permute-done.5, pred[]{:T(512)S(6)} %eq.131), kind=kLoop, calls=%fused_computation.129 | loop fusion | flops 196608 | bytes 786433 | tf_op jit(solution)/shard_map/jit(_where)/select_n | solution.py:33
  41.9 6.4 %fusion.2 = f32[192,1024]{1,0:T(8,128)} fusion(bf16[1,1,2048,1024]{3,2,1,0:T(8,128)(2,1)} %param.17, bf16[1,1,1024,2048]{3,2,1,0:T(8,128)(2,1)} %param.16, bf16[192,512]{1,0:T(8,128)(2,1)} %get-tuple-element.12, bf16[192,512]{1,0:T(8,128)(2,1)} %get-tuple-element.11), kind=kOutput, calls=%fused_computation.2 | convolution fusion | flops 1612185600 | bytes 9568256 | tf_op jit(solution)/shard_map/dot_general | solution.py:100
  48.2 1.7 %dynamic-slice_convert_fusion.1 = bf16[192,512]{1,0:T(8,128)(2,1)} fusion(f32[192,1024]{1,0:T(8,128)} %fusion.2, s32[]{:T(128)S(6)} %select_n.132), kind=kLoop, calls=%fused_computation.93 | loop fusion | bytes 393220 | tf_op jit(solution)/shard_map/convert_element_type | solution.py:113
  50.4 6.3 %fusion.4 = f32[192,1024]{1,0:T(8,128)} fusion(bf16[1,1,2048,1024]{3,2,1,0:T(8,128)(2,1)} %param.17, bf16[192,1024]{1,0:T(8,128)(2,1)} %collective-permute-done.1, bf16[1,1,1024,2048]{3,2,1,0:T(8,128)(2,1)} %param.16), kind=kOutput, calls=%fused_computation.4 | convolution fusion | flops 1611399168 | bytes 9568256 | tf_op jit(solution)/shard_map/dot_general | solution.py:100
  56.7 1.1 dynamic-slice_convert_fusion.2
  57.8 1.6 %collective-permute-start.2 = (bf16[192,512]{1,0:T(8,128)(2,1)S(1)}, bf16[192,512]{1,0:T(8,128)(2,1)S(1)}, u32[]{:S(2)}, u32[]{:S(2)}) collective-permute-start(bf16[192,512]{1,0:T(8,128)(2,1)S(1)} %dynamic-slice_convert_fusion.2), channel_id=1, source_target_pairs={{0,1},{1,0},{2,3},{3,2},{4,5},{5,4},{6,7},{7,6},{8,9},{9,8},{10,11... | collective-permute-start | bytes 589832 | tf_op jit(solution)/shard_map/ppermute | solution.py:17
  59.4 1.0 add_convert_fusion
  60.4 4.8 %collective-permute-start.11 = (bf16[192,512]{1,0:T(8,128)(2,1)S(1)}, bf16[192,512]{1,0:T(8,128)(2,1)S(1)}, u32[]{:S(2)}, u32[]{:S(2)}) collective-permute-start(bf16[192,512]{1,0:T(8,128)(2,1)S(1)} %add_convert_fusion), channel_id=1, source_target_pairs={{0,6},{2,4},{4,2},{6,0},{1,7},{3,5},{5,3},{7,1},{8,14},{10,12},{12... | collective-permute-start | bytes 589832 | tf_op jit(solution)/shard_map/ppermute | solution.py:17
  65.2 1.1 add_convert_fusion.1
  66.5 1.0 add_convert_fusion.2
  68.2 1.8 %collective-permute-done.11 = bf16[192,512]{1,0:T(8,128)(2,1)S(1)} collective-permute-done((bf16[192,512]{1,0:T(8,128)(2,1)S(1)}, bf16[192,512]{1,0:T(8,128)(2,1)S(1)}, u32[]{:S(2)}, u32[]{:S(2)}) %collective-permute-start.11) | collective-permute-done | bytes 196640 | tf_op jit(solution)/shard_map/ppermute | solution.py:17
  70.2 8.1 %collective-permute-done.7 = bf16[192,512]{1,0:T(8,128)(2,1)S(1)} collective-permute-done((bf16[192,512]{1,0:T(8,128)(2,1)S(1)}, bf16[192,512]{1,0:T(8,128)(2,1)S(1)}, u32[]{:S(2)}, u32[]{:S(2)}) %collective-permute-start.7) | collective-permute-done | bytes 196640 | tf_op jit(solution)/shard_map/ppermute | solution.py:17
  79.8 3.4 %collective-permute-start.12 = (bf16[256,512]{1,0:T(8,128)(2,1)S(1)}, bf16[256,512]{1,0:T(8,128)(2,1)S(1)}, u32[]{:S(2)}, u32[]{:S(2)}) collective-permute-start(bf16[256,512]{1,0:T(8,128)(2,1)S(1)} %fusion.48), channel_id=1, source_target_pairs={{0,16},{1,17},{2,18},{3,19},{4,20},{5,21},{6,22},{7,23}} | collective-permute-start | bytes 786440 | tf_op jit(solution)/shard_map/ppermute | solution.py:21
  83.4 3.1 %collective-permute-done.15 = bf16[256,512]{1,0:T(8,128)(2,1)S(1)} collective-permute-done((bf16[256,512]{1,0:T(8,128)(2,1)S(1)}, bf16[256,512]{1,0:T(8,128)(2,1)S(1)}, u32[]{:S(2)}, u32[]{:S(2)}) %collective-permute-start.15) | collective-permute-done | bytes 262176 | tf_op jit(solution)/shard_map/ppermute | solution.py:17
  87.1 1.5 %collective-permute-start.13 = (bf16[256,512]{1,0:T(8,128)(2,1)S(1)}, bf16[256,512]{1,0:T(8,128)(2,1)S(1)}, u32[]{:S(2)}, u32[]{:S(2)}) collective-permute-start(bf16[256,512]{1,0:T(8,128)(2,1)S(1)} %get-tuple-element.15), channel_id=1, source_target_pairs={{0,8},{16,24},{1,9},{17,25},{2,10},{18,26},{3,11},{19,27},{4,12},{... | collective-permute-start | bytes 786440 | tf_op jit(solution)/shard_map/ppermute | solution.py:21
  89.6 1.6 %collective-permute-start.14 = (bf16[256,512]{1,0:T(8,128)(2,1)S(1)}, bf16[256,512]{1,0:T(8,128)(2,1)}, u32[]{:S(2)}, u32[]{:S(2)}) collective-permute-start(bf16[256,512]{1,0:T(8,128)(2,1)S(1)} %broadcast_select_fusion.1), channel_id=1, source_target_pairs={{0,1},{1,0},{2,3},{3,2},{4,5},{5,4},{6,7},{7,6},{8,9},{9,8},{10,11... | collective-permute-start | bytes 786440 | tf_op jit(solution)/shard_map/ppermute | solution.py:17
  91.2 1.7 %convolution_convert_fusion.5 = bf16[256,512]{1,0:T(8,128)(2,1)S(1)} fusion(bf16[1,1024,512]{2,1,0:T(8,128)(2,1)} %param.18, f32[1024]{0:T(1024)S(1)} %bitcast.158, f32[256]{0:T(256)S(1)} %add_rsqrt_fusion, f32[256]{0:T(256)S(1)} %broadcast_multiply_fusion, bf16[256,512]{1,0:T(8,128)(2,1)S(1)} %get-tuple-element.8, bf16[256,512]{1,0:T(8,128)(2,1)S(1)} %get-tuple-element.7), kind=kOutput, calls=%fused_computation.49 | convolution fusion | flops 270663680 | bytes 1841152 | tf_op jit(solution)/shard_map/dot_general | solution.py:143
  93.2 5.1 %collective-permute-done.14 = bf16[256,512]{1,0:T(8,128)(2,1)} collective-permute-done((bf16[256,512]{1,0:T(8,128)(2,1)S(1)}, bf16[256,512]{1,0:T(8,128)(2,1)}, u32[]{:S(2)}, u32[]{:S(2)}) %collective-permute-start.14) | collective-permute-done | bytes 262176 | tf_op jit(solution)/shard_map/ppermute | solution.py:17
  98.4 1.0 broadcast_select_fusion.5
  100.7 1.0 fusion.43
  101.7 1.1 fusion.100
  102.8 1.5 %convolution_convert_fusion.6 = bf16[256,512]{1,0:T(8,128)(2,1)S(1)} fusion(bf16[1,1024,512]{2,1,0:T(8,128)(2,1)S(1)} %copy-done.2, bf16[256,512]{1,0:T(8,128)(2,1)} %copy-done.6, bf16[256,512]{1,0:T(8,128)(2,1)} %copy-done.5), kind=kOutput, calls=%fused_computation.50 | convolution fusion | flops 269615104 | bytes 1835008 | tf_op jit(solution)/shard_map/dot_general | solution.py:153
  104.3 1.5 %fusion.52 = bf16[2,128,4,128]{3,1,2,0:T(8,128)(2,1)S(1)} fusion(bf16[2,128,4,128]{3,2,1,0:T(4,128)(2,1)S(1)} %reshape_squeeze.3, f32[2,4,128,128]{2,3,1,0:T(8,128)} %fusion.43), kind=kOutput, calls=%fused_computation.57 | convolution fusion | flops 33948800 | bytes 1048576 | tf_op jit(solution)/shard_map/shqk,sqhd->skhd/dot_general | solution.py:171
  105.9 2.1 %multiply_reduce_fusion = (f32[2,4,128]{2,1,0:T(4,128)S(1)}, f32[2,4,128,128]{2,3,1,0:T(8,128)}) fusion(f32[2,4,128,128]{2,3,1,0:T(8,128)} %fusion.100, bf16[2,128,4,128]{3,2,1,0:T(4,128)(2,1)S(1)} %reshape_squeeze.3, bf16[2,128,4,128]{3,2,1,0:T(4,128)(2,1)S(1)} %reshape.63), kind=kOutput, calls=%fused_computation.80 | convolution fusion | flops 33815552 | bytes 1576960 | tf_op jit(solution)/shard_map/sqhd,skhd->shqk/dot_general | solution.py:168
  108.0 1.7 %fusion.50 = bf16[2,128,4,128]{3,1,2,0:T(8,128)(2,1)S(1)} fusion(bf16[2,128,4,128]{1,3,2,0:T(8,128)(2,1)S(1)} %copy.46, f32[2,4,128,128]{2,3,1,0:T(8,128)} %get-tuple-element.29, f32[2,4,128]{2,1,0:T(4,128)S(1)} %get-tuple-element.28, f32[2,4,128,128]{2,3,1,0:T(8,128)} %fusion.43), kind=kOutput, calls=%fused_computation.55 | convolution fusion | flops 34342016 | bytes 1576960 | tf_op jit(solution)/shard_map/shqk,sqhd->skhd/dot_general | solution.py:174
  111.1 0.9 reshape.69
  112.6 1.6 %fusion.51 = bf16[2,128,4,128]{1,3,2,0:T(8,128)(2,1)S(1)} fusion(bf16[2,128,4,128]{3,2,1,0:T(4,128)(2,1)} %copy-done.3, f32[2,4,128,128]{2,3,1,0:T(8,128)} %fusion.43), kind=kOutput, calls=%fused_computation.56 | convolution fusion | flops 33948800 | bytes 1048576 | tf_op jit(solution)/shard_map/shqk,skhd->sqhd/dot_general | solution.py:163
  115.1 3.5 %collective-permute-start.19 = (bf16[256,128]{0,1:T(8,128)(2,1)S(1)}, bf16[256,128]{0,1:T(8,128)(2,1)S(1)}, u32[]{:S(2)}, u32[]{:S(2)}) collective-permute-start(bf16[256,128]{0,1:T(8,128)(2,1)S(1)} %get-tuple-element.5), channel_id=1, source_target_pairs={{0,17},{1,16},{8,25},{9,24},{16,1},{17,0},{24,9},{25,8},{2,19},{3,... | collective-permute-start | bytes 196616 | tf_op jit(solution)/shard_map/ppermute | solution.py:201
  119.3 0.7 fusion.96
  120.0 1.4 %collective-permute-done.19 = bf16[256,128]{0,1:T(8,128)(2,1)S(1)} collective-permute-done((bf16[256,128]{0,1:T(8,128)(2,1)S(1)}, bf16[256,128]{0,1:T(8,128)(2,1)S(1)}, u32[]{:S(2)}, u32[]{:S(2)}) %collective-permute-start.19) | collective-permute-done | bytes 65568 | tf_op jit(solution)/shard_map/ppermute | solution.py:201
  121.4 1.5 %collective-permute-done.18 = bf16[256,128]{0,1:T(8,128)(2,1)S(1)} collective-permute-done((bf16[256,128]{0,1:T(8,128)(2,1)S(1)}, bf16[256,128]{0,1:T(8,128)(2,1)S(1)}, u32[]{:S(2)}, u32[]{:S(2)}) %collective-permute-start.18) | collective-permute-done | bytes 65568 | tf_op jit(solution)/shard_map/ppermute | solution.py:201
  122.9 0.7 copy.55
  (79 shorter events, 11.9 us)
Async XLA Ops:
  0.6 99.5 %copy-start = (bf16[1,1024,512]{2,1,0:T(8,128)(2,1)S(1)}, bf16[1,1024,512]{2,1,0:T(8,128)(2,1)}, u32[]{:S(2)}) copy-start(bf16[1,1024,512]{2,1,0:T(8,128)(2,1)} %param.19) | copy-start | bytes 3145732
  6.6 15.6 %collective-permute-start.8 = (bf16[192,512]{1,0:T(8,128)(2,1)}, bf16[192,512]{1,0:T(8,128)(2,1)}, u32[]{:S(2)}, u32[]{:S(2)}) collective-permute-start(bf16[192,512]{1,0:T(8,128)(2,1)} %convolution_convert_fusion.7), channel_id=1, source_target_pairs={{0,6},{2,4},{4,2},{6,0},{1,7},{3,5},{5,3},{7,1},{8,14},{10,12},{12... | collective-permute-start | bytes 589832 | tf_op jit(solution)/shard_map/ppermute | solution.py:17
  12.6 16.1 %collective-permute-start.4 = (bf16[192,512]{1,0:T(8,128)(2,1)}, bf16[192,512]{1,0:T(8,128)(2,1)}, u32[]{:S(2)}, u32[]{:S(2)}) collective-permute-start(bf16[192,512]{1,0:T(8,128)(2,1)} %convolution_convert_fusion.8), channel_id=1, source_target_pairs={{0,4},{2,6},{4,0},{6,2},{1,5},{3,7},{5,1},{7,3},{8,12},{10,14},{12... | collective-permute-start | bytes 589832 | tf_op jit(solution)/shard_map/ppermute | solution.py:17
  13.0 37.4 %collective-permute-start.1 = (bf16[192,1024]{1,0:T(8,128)(2,1)S(1)}, bf16[192,1024]{1,0:T(8,128)(2,1)}, u32[]{:S(2)}, u32[]{:S(2)}) collective-permute-start(bf16[192,1024]{1,0:T(8,128)(2,1)S(1)} %convolution_convert_fusion), channel_id=1, source_target_pairs={{0,2},{2,0},{4,6},{6,4},{1,3},{3,1},{5,7},{7,5},{8,10},{10,8},{12,... | collective-permute-start | bytes 1179656 | tf_op jit(solution)/shard_map/ppermute | solution.py:17
  17.1 5.0 %copy-start.7 = (f32[1,256,2]{1,2,0:T(2,128)S(1)}, f32[1,256,2]{1,2,0:T(2,128)}, u32[]{:S(2)}) copy-start(f32[1,256,2]{1,2,0:T(2,128)} %param.13) | copy-start | bytes 6148
  20.3 58.6 %collective-permute-start = (bf16[192,512]{1,0:T(8,128)(2,1)S(1)}, bf16[192,512]{1,0:T(8,128)(2,1)S(1)}, u32[]{:S(2)}, u32[]{:S(2)}) collective-permute-start(bf16[192,512]{1,0:T(8,128)(2,1)S(1)} %dynamic-slice_convert_fusion.3), channel_id=1, source_target_pairs={{0,1},{1,0},{2,3},{3,2},{4,5},{5,4},{6,7},{7,6},{8,9},{9,8},{10,11... | collective-permute-start | bytes 589832 | tf_op jit(solution)/shard_map/ppermute | solution.py:17
  22.2 8.5 %collective-permute-start.9 = (bf16[192,512]{1,0:T(8,128)(2,1)}, bf16[192,512]{1,0:T(8,128)(2,1)S(1)}, u32[]{:S(2)}, u32[]{:S(2)}) collective-permute-start(bf16[192,512]{1,0:T(8,128)(2,1)} %collective-permute-done.8), channel_id=1, source_target_pairs={{0,1},{1,0},{2,3},{3,2},{4,5},{5,4},{6,7},{7,6},{8,9},{9,8},{10,11... | collective-permute-start | bytes 589832 | tf_op jit(solution)/shard_map/ppermute | solution.py:17
  28.8 11.3 %collective-permute-start.5 = (bf16[192,512]{1,0:T(8,128)(2,1)}, bf16[192,512]{1,0:T(8,128)(2,1)}, u32[]{:S(2)}, u32[]{:S(2)}) collective-permute-start(bf16[192,512]{1,0:T(8,128)(2,1)} %collective-permute-done.4), channel_id=1, source_target_pairs={{0,1},{1,0},{2,3},{3,2},{4,5},{5,4},{6,7},{7,6},{8,9},{9,8},{10,11... | collective-permute-start | bytes 589832 | tf_op jit(solution)/shard_map/ppermute | solution.py:17
  38.6 20.9 %collective-permute-start.10 = (bf16[192,512]{1,0:T(8,128)(2,1)}, bf16[192,512]{1,0:T(8,128)(2,1)}, u32[]{:S(2)}, u32[]{:S(2)}) collective-permute-start(bf16[192,512]{1,0:T(8,128)(2,1)} %dynamic-slice_convert_fusion), channel_id=1, source_target_pairs={{0,1},{1,0},{2,3},{3,2},{4,5},{5,4},{6,7},{7,6},{8,9},{9,8},{10,11... | collective-permute-start | bytes 589832 | tf_op jit(solution)/shard_map/ppermute | solution.py:17
  49.9 15.3 %collective-permute-start.6 = (bf16[192,512]{1,0:T(8,128)(2,1)}, bf16[192,512]{1,0:T(8,128)(2,1)}, u32[]{:S(2)}, u32[]{:S(2)}) collective-permute-start(bf16[192,512]{1,0:T(8,128)(2,1)} %dynamic-slice_convert_fusion.1), channel_id=1, source_target_pairs={{0,1},{1,0},{2,3},{3,2},{4,5},{5,4},{6,7},{7,6},{8,9},{9,8},{10,11... | collective-permute-start | bytes 589832 | tf_op jit(solution)/shard_map/ppermute | solution.py:17
  56.7 22.2 %copy-start.1 = (bf16[1,256,1024]{2,1,0:T(8,128)(2,1)S(1)}, bf16[1,256,1024]{2,1,0:T(8,128)(2,1)}, u32[]{:S(2)}) copy-start(bf16[1,256,1024]{2,1,0:T(8,128)(2,1)} %param.11) | copy-start | bytes 1572868
  56.7 26.5 %copy-start.4 = (bf16[1,256,512]{2,1,0:T(8,128)(2,1)S(1)}, bf16[1,256,512]{2,1,0:T(8,128)(2,1)}, u32[]{:S(2)}) copy-start(bf16[1,256,512]{2,1,0:T(8,128)(2,1)} %param.21) | copy-start | bytes 786436
  57.8 8.6 %collective-permute-start.2 = (bf16[192,512]{1,0:T(8,128)(2,1)S(1)}, bf16[192,512]{1,0:T(8,128)(2,1)S(1)}, u32[]{:S(2)}, u32[]{:S(2)}) collective-permute-start(bf16[192,512]{1,0:T(8,128)(2,1)S(1)} %dynamic-slice_convert_fusion.2), channel_id=1, source_target_pairs={{0,1},{1,0},{2,3},{3,2},{4,5},{5,4},{6,7},{7,6},{8,9},{9,8},{10,11... | collective-permute-start | bytes 589832 | tf_op jit(solution)/shard_map/ppermute | solution.py:17
  60.4 9.6 %collective-permute-start.11 = (bf16[192,512]{1,0:T(8,128)(2,1)S(1)}, bf16[192,512]{1,0:T(8,128)(2,1)S(1)}, u32[]{:S(2)}, u32[]{:S(2)}) collective-permute-start(bf16[192,512]{1,0:T(8,128)(2,1)S(1)} %add_convert_fusion), channel_id=1, source_target_pairs={{0,6},{2,4},{4,2},{6,0},{1,7},{3,5},{5,3},{7,1},{8,14},{10,12},{12... | collective-permute-start | bytes 589832 | tf_op jit(solution)/shard_map/ppermute | solution.py:17
  66.4 11.9 %collective-permute-start.7 = (bf16[192,512]{1,0:T(8,128)(2,1)S(1)}, bf16[192,512]{1,0:T(8,128)(2,1)S(1)}, u32[]{:S(2)}, u32[]{:S(2)}) collective-permute-start(bf16[192,512]{1,0:T(8,128)(2,1)S(1)} %add_convert_fusion.1), channel_id=1, source_target_pairs={{0,4},{2,6},{4,0},{6,2},{1,5},{3,7},{5,1},{7,3},{8,12},{10,14},{12... | collective-permute-start | bytes 589832 | tf_op jit(solution)/shard_map/ppermute | solution.py:17
  67.5 11.1 %collective-permute-start.3 = (bf16[192,512]{1,0:T(8,128)(2,1)S(1)}, bf16[192,512]{1,0:T(8,128)(2,1)S(1)}, u32[]{:S(2)}, u32[]{:S(2)}) collective-permute-start(bf16[192,512]{1,0:T(8,128)(2,1)S(1)} %add_convert_fusion.2), channel_id=1, source_target_pairs={{0,2},{2,0},{4,6},{6,4},{1,3},{3,1},{5,7},{7,5},{8,10},{10,8},{12,... | collective-permute-start | bytes 589832 | tf_op jit(solution)/shard_map/ppermute | solution.py:17
  70.2 21.0 %copy-start.8 = (f32[1,1024]{1,0:T(1,128)S(1)}, f32[1,1024]{1,0:T(1,128)}, u32[]{:S(2)}) copy-start(f32[1,1024]{1,0:T(1,128)} %param.15) | copy-start | bytes 12292
  79.2 7.2 %collective-permute-start.15 = (bf16[256,512]{1,0:T(8,128)(2,1)S(1)}, bf16[256,512]{1,0:T(8,128)(2,1)S(1)}, u32[]{:S(2)}, u32[]{:S(2)}) collective-permute-start(bf16[256,512]{1,0:T(8,128)(2,1)S(1)} %fusion.48), channel_id=1, source_target_pairs={{0,1},{1,0},{2,3},{3,2},{4,5},{5,4},{6,7},{7,6},{8,9},{9,8},{10,11... | collective-permute-start | bytes 786440 | tf_op jit(solution)/shard_map/ppermute | solution.py:17
  79.8 7.3 %collective-permute-start.12 = (bf16[256,512]{1,0:T(8,128)(2,1)S(1)}, bf16[256,512]{1,0:T(8,128)(2,1)S(1)}, u32[]{:S(2)}, u32[]{:S(2)}) collective-permute-start(bf16[256,512]{1,0:T(8,128)(2,1)S(1)} %fusion.48), channel_id=1, source_target_pairs={{0,16},{1,17},{2,18},{3,19},{4,20},{5,21},{6,22},{7,23}} | collective-permute-start | bytes 786440 | tf_op jit(solution)/shard_map/ppermute | solution.py:21
  87.1 2.4 %collective-permute-start.13 = (bf16[256,512]{1,0:T(8,128)(2,1)S(1)}, bf16[256,512]{1,0:T(8,128)(2,1)S(1)}, u32[]{:S(2)}, u32[]{:S(2)}) collective-permute-start(bf16[256,512]{1,0:T(8,128)(2,1)S(1)} %get-tuple-element.15), channel_id=1, source_target_pairs={{0,8},{16,24},{1,9},{17,25},{2,10},{18,26},{3,11},{19,27},{4,12},{... | collective-permute-start | bytes 786440 | tf_op jit(solution)/shard_map/ppermute | solution.py:21
  89.6 8.8 %collective-permute-start.14 = (bf16[256,512]{1,0:T(8,128)(2,1)S(1)}, bf16[256,512]{1,0:T(8,128)(2,1)}, u32[]{:S(2)}, u32[]{:S(2)}) collective-permute-start(bf16[256,512]{1,0:T(8,128)(2,1)S(1)} %broadcast_select_fusion.1), channel_id=1, source_target_pairs={{0,1},{1,0},{2,3},{3,2},{4,5},{5,4},{6,7},{7,6},{8,9},{9,8},{10,11... | collective-permute-start | bytes 786440 | tf_op jit(solution)/shard_map/ppermute | solution.py:17
  93.0 9.7 %copy-start.2 = (bf16[1,1024,512]{2,1,0:T(8,128)(2,1)S(1)}, bf16[1,1024,512]{2,1,0:T(8,128)(2,1)}, u32[]{:S(2)}) copy-start(bf16[1,1024,512]{2,1,0:T(8,128)(2,1)} %param.20) | copy-start | bytes 3145732
  99.4 0.7 copy-start.5
  99.4 0.8 copy-start.6
  104.3 6.3 %copy-start.3 = (bf16[2,128,4,128]{3,2,1,0:T(4,128)(2,1)}, bf16[2,128,4,128]{3,2,1,0:T(4,128)(2,1)S(1)}, u32[]{:S(2)}) copy-start(bf16[2,128,4,128]{3,2,1,0:T(4,128)(2,1)S(1)} %reshape.63) | copy-start | bytes 786436
  112.5 2.3 %collective-permute-start.16 = (bf16[256,2,256]{2,0,1:T(8,128)(2,1)S(1)}, bf16[256,2,256]{2,0,1:T(8,128)(2,1)S(1)}, u32[]{:S(2)}, u32[]{:S(2)}) collective-permute-start(bf16[256,2,256]{2,0,1:T(8,128)(2,1)S(1)} %bitcast.136), channel_id=1, source_target_pairs={{0,8},{8,0},{16,24},{24,16},{1,9},{9,1},{17,25},{25,17},{2,10},{10... | collective-permute-start | bytes 786440 | tf_op jit(solution)/shard_map/ppermute | solution.py:17
  115.1 6.3 %collective-permute-start.19 = (bf16[256,128]{0,1:T(8,128)(2,1)S(1)}, bf16[256,128]{0,1:T(8,128)(2,1)S(1)}, u32[]{:S(2)}, u32[]{:S(2)}) collective-permute-start(bf16[256,128]{0,1:T(8,128)(2,1)S(1)} %get-tuple-element.5), channel_id=1, source_target_pairs={{0,17},{1,16},{8,25},{9,24},{16,1},{17,0},{24,9},{25,8},{2,19},{3,... | collective-permute-start | bytes 196616 | tf_op jit(solution)/shard_map/ppermute | solution.py:201
  118.6 4.3 %collective-permute-start.18 = (bf16[256,128]{0,1:T(8,128)(2,1)S(1)}, bf16[256,128]{0,1:T(8,128)(2,1)S(1)}, u32[]{:S(2)}, u32[]{:S(2)}) collective-permute-start(bf16[256,128]{0,1:T(8,128)(2,1)S(1)} %get-tuple-element.6), channel_id=1, source_target_pairs={{0,16},{1,17},{8,24},{9,25},{16,0},{17,1},{24,8},{25,9},{2,18},{3,... | collective-permute-start | bytes 196616 | tf_op jit(solution)/shard_map/ppermute | solution.py:201
  118.6 4.3 %collective-permute-start.17 = (bf16[256,128]{0,1:T(8,128)(2,1)S(1)}, bf16[256,128]{0,1:T(8,128)(2,1)S(1)}, u32[]{:S(2)}, u32[]{:S(2)}) collective-permute-start(bf16[256,128]{0,1:T(8,128)(2,1)S(1)} %get-tuple-element.4), channel_id=1, source_target_pairs={{0,1},{1,0},{8,9},{9,8},{16,17},{17,16},{24,25},{25,24},{2,3},{3,2... | collective-permute-start | bytes 196616 | tf_op jit(solution)/shard_map/ppermute | solution.py:201

commit v2 on v0

v2 whole, which is shorter than its diff:
```python
import functools
import math

import jax
import jax.numpy as jnp
from jax import lax
from jax.experimental import pallas as pl
from jax.experimental.pallas import tpu as pltpu
from jax.sharding import PartitionSpec as P

HD = 128
SEQ = 128
EPS = 1e-05

LOW = jnp.bfloat16
WIDE = jnp.float32
VMEM = pl.BlockSpec(memory_space=pltpu.VMEM)
NT = (((1,), (1,)), ((), ()))
TN = (((0,), (0,)), ((), ()))


def matmul(a, b, dims=(((1,), (0,)), ((), ()))):
    return lax.dot_general(a, b, dims, preferred_element_type=WIDE)


def call(body, out_shape, inputs, scratch=(), flops=0, limit=40):
    def size(x):
        return math.prod(x.shape) * jnp.dtype(x.dtype).itemsize

    moved = sum(size(x) for x in inputs) + sum(size(x) for x in out_shape)
    return pl.pallas_call(
        body,
        out_shape=out_shape,
        in_specs=[VMEM] * len(inputs),
        out_specs=[VMEM] * len(out_shape),
        scratch_shapes=list(scratch),
        compiler_params=pltpu.CompilerParams(vmem_limit_bytes=limit * 2**20),
        cost_estimate=pl.CostEstimate(flops=flops, bytes_accessed=moved, transcendentals=0),
    )(*inputs)


def shape_of(dims, kind=LOW):
    return jax.ShapeDtypeStruct(dims, kind)


def part(index, width):
    return pl.ds(pl.multiple_of(index * width, width), width)


def places(routes, me, rows):
    token_count = routes.shape[1]
    labels = lax.broadcasted_iota(jnp.int32, (rows, 1), 0) ^ me
    first = routes[0:1, :] == labels
    second = routes[1:2, :] == labels
    either = first | second
    source = lax.broadcasted_iota(jnp.int32, (token_count, token_count), 0)
    target = lax.broadcasted_iota(jnp.int32, (token_count, token_count), 1)
    earlier = jnp.where(source < target, 1.0, 0.0).astype(LOW)
    before = matmul(jnp.where(either, 1.0, 0.0).astype(LOW), earlier)
    return jnp.where(either, before, -1.0), first, second


def prepare(experts, tokens, routes, gain, *outs):
    far, near, own = outs[:-3], outs[-3], outs[-2]
    normed_ref = outs[-1]
    me = lax.axis_index("exp")
    tp = lax.axis_index("tp")
    token_count, width = tokens.shape
    capacity = own.shape[0]
    half = width // 2
    wide = tokens[...].astype(WIDE)
    average = jnp.mean(wide, axis=-1, keepdims=True)
    centred = wide - average
    spread = jnp.mean(centred * centred, axis=-1, keepdims=True)
    normed_ref[...] = (centred * lax.rsqrt(spread + EPS) * gain[...]).astype(LOW)
    place, _, _ = places(routes[...], me, max(16, experts))
    slots = lax.broadcasted_iota(jnp.int32, (capacity, token_count), 0).astype(WIDE)

    def table(k):
        return jnp.where(place[k : k + 1, :] == slots, 1.0, 0.0).astype(LOW)

    normed_half = normed_ref[:, part(tp, half)]
    for k in range(experts - 1, 1, -1):
        far[k - 2][...] = matmul(table(k), normed_half).astype(LOW)
    normed = normed_ref[...]
    near[...] = matmul(table(1), normed).astype(LOW)
    own[...] = matmul(table(0), normed).astype(LOW)


def mixing(experts, routes, gates, high, low):
    me = lax.axis_index("exp")
    token_count = routes.shape[1]
    capacity = high.shape[2]
    place, first, second = places(routes[...], me, max(16, experts))
    gate = jnp.where(first, gates[0:1, :], 0.0) + jnp.where(second, gates[1:2, :], 0.0)
    place = place.T
    gate = gate.T
    slots = lax.broadcasted_iota(jnp.int32, (token_count, capacity), 1).astype(WIDE)
    for k in range(experts):
        weight = jnp.where(place[:, k : k + 1] == slots, gate[:, k : k + 1], 0.0)
        upper = weight.astype(LOW)
        high[k] = upper
        low[k] = (weight - upper.astype(WIDE)).astype(LOW)


def expert(split, *refs):
    rows, refs = refs[: 1 + split], refs[1 + split :]
    first, second, away, kept, inner = refs
    tp = lax.axis_index("tp")
    width, hidden = first.shape
    half = width // 2
    chunk = min(512, hidden)
    for c in range(hidden // chunk):
        columns = slice(c * chunk, (c + 1) * chunk)
        if split:
            value = matmul(rows[0][...], first[part(tp, half), columns])
            value = value + matmul(rows[1][...], first[part(1 - tp, half), columns])
        else:
            value = matmul(rows[0][...], first[:, columns])
        inner[:, columns] = jnp.maximum(value, 0.0).astype(LOW)
    away[...] = matmul(inner[...], second[:, part(1 - tp, half)]).astype(LOW)
    kept[...] = matmul(inner[...], second[:, part(tp, half)])


def combine(experts, tokens, high, low, *refs):
    returned, out = refs[:-1], refs[-1]
    tp = lax.axis_index("tp")
    half = out.shape[1]
    mixed = tokens[:, part(tp, half)].astype(WIDE)
    for k in range(experts):
        rows = returned[k][...]
        mixed = mixed + (matmul(high[k], rows) + matmul(low[k], rows))
    out[...] = mixed.astype(LOW)


def project(mine, other, gain, weight, out):
    tp = lax.axis_index("tp")
    half = mine.shape[1]
    own = mine[...].astype(WIDE)
    rest = other[...].astype(WIDE)
    average = (
        jnp.sum(own, axis=-1, keepdims=True) + jnp.sum(rest, axis=-1, keepdims=True)
    ) / (2 * half)
    own = own - average
    rest = rest - average
    spread = (
        jnp.sum(own * own, axis=-1, keepdims=True) + jnp.sum(rest * rest, axis=-1, keepdims=True)
    ) / (2 * half)
    factor = lax.rsqrt(spread + EPS)
    own = (own * factor * gain[:, part(tp, half)]).astype(LOW)
    rest = (rest * factor * gain[:, part(1 - tp, half)]).astype(LOW)
    value = matmul(own, weight[part(tp, half), :]) + matmul(rest, weight[part(1 - tp, half), :])
    out[...] = value.astype(LOW)


def attend(
    mine, other, queries, upstream, key_w, value_w, hidden, context, away, kept, keys, values, dkeys, dvalues
):
    tp = lax.axis_index("tp")
    sec = lax.axis_index("sec")
    token_count, half = mine.shape
    width = 2 * half
    scale = 1.0 / math.sqrt(HD)

    @pl.when(sec != 0)
    def _():
        for weight, target in ((key_w, keys), (value_w, values)):
            value = matmul(mine[...], weight[part(tp, half), :])
            value = value + matmul(other[...], weight[part(1 - tp, half), :])
            target[...] = value.astype(LOW)
        for s in range(token_count // SEQ):
            for h in range(queries.shape[1] // HD):
                rows, columns = slice(s * SEQ, (s + 1) * SEQ), slice(h * HD, (h + 1) * HD)
                query, key = queries[rows, columns], keys[rows, columns]
                value, up = values[rows, columns], upstream[rows, columns]
                powers = jnp.exp(matmul(key, query, NT) * scale)
                probs = powers * (1.0 / jnp.sum(powers, axis=0, keepdims=True))
                low = probs.astype(LOW)
                dprobs = matmul(value, up, NT)
                rowdot = jnp.sum(dprobs * probs, axis=0, keepdims=True)
                dscores = (probs * (dprobs - rowdot)).astype(LOW)
                dvalues[rows, columns] = matmul(low, up).astype(LOW)
                dkeys[rows, columns] = (matmul(dscores, query) * scale).astype(LOW)
                context[rows, columns] = matmul(low, value, TN).astype(LOW)
        side = sec % 2
        pairs = lax.axis_size("sec") // 2
        block = width // (2 * pairs)
        for target, parity in ((away, 1 - side), (kept, side)):
            for i in range(pairs):
                rows = part(2 * i + parity, block)
                value = matmul(dkeys[...], key_w[rows, :], NT)
                value = value + matmul(dvalues[...], value_w[rows, :], NT)
                target[:, i * block : (i + 1) * block] = value.astype(target.dtype)

    @pl.when(sec == 0)
    def _():
        context[...] = hidden[...]
        away[...] = jnp.zeros_like(away)
        kept[...] = jnp.zeros_like(kept)


def gather_term(kept, arrived, own, *sent):
    tp = lax.axis_index("tp")
    here = lax.axis_index("sec") // 2 * lax.axis_size("tp") + tp
    width = own.shape[1]
    for k in range(len(sent) + 1):
        columns = part(here ^ k, width)
        value = kept[:, columns] + arrived[:, columns].astype(WIDE)
        if k == 0:
            own[...] = value
        else:
            sent[k - 1][...] = value.astype(LOW)


def swap(block, axis, step):
    size = lax.axis_size(axis)
    return lax.ppermute(block, axis, [(i, i ^ step) for i in range(size)])


def shards(
    tokens,
    routes,
    gate_weights,
    moe_gain,
    attn_gain,
    expert_in,
    expert_out,
    query_weight,
    key_weight,
    value_weight,
    cotangent,
):
    token_rows = tokens[0]
    route_rows = routes[0].T
    gate_rows = gate_weights[0].T
    token_count, model_width = token_rows.shape
    experts = lax.axis_size("exp")
    sections = lax.axis_size("sec")
    tp_size = lax.axis_size("tp")
    sec = lax.axis_index("sec")
    half = model_width // tp_size
    capacity = 3 * token_count // experts
    weight_first = expert_in[0, 0]
    weight_second = expert_out[0, 0]
    units = weight_first.shape[1]

    far_count = experts - 2
    prepared = call(
        functools.partial(prepare, experts),
        [shape_of((capacity, half))] * far_count + [shape_of((capacity, model_width))] * 2,
        [token_rows, route_rows, moe_gain],
        [pltpu.VMEM((token_count, model_width), LOW)],
        flops=2 * 3 * token_count * token_count * model_width,
    )
    far_rows, near_rows, own_rows = prepared[:far_count], prepared[far_count], prepared[-1]
    high, low = call(
        functools.partial(mixing, experts),
        [shape_of((experts, token_count, capacity))] * 2,
        [route_rows, gate_rows],
    )

    def through(rows):
        count = rows[0].shape[0]
        away, kept = call(
            functools.partial(expert, len(rows) - 1),
            [shape_of((count, half)), shape_of((count, half), WIDE)],
            [*rows, weight_first, weight_second],
            [pltpu.VMEM((count, units), LOW)],
            flops=4 * count * model_width * units,
        )
        return (kept + swap(away, "tp", 1).astype(WIDE)).astype(LOW)

    far = {k: swap(far_rows[k - 2], "exp", k) for k in range(experts - 1, 1, -1)}
    near = swap(near_rows, "exp", 1)
    returned = {0: through([own_rows]), 1: swap(through([near]), "exp", 1)}
    middle = max(2, experts // 2 + 1)
    for group in (range(experts - 1, middle - 1, -1), range(middle - 1, 1, -1)):
        group = list(group)
        if not group:
            continue
        if len(group) == 1:
            mine = far[group[0]]
        else:
            mine = jnp.concatenate([far[k] for k in group], axis=0)
        total = through([mine, swap(mine, "tp", 1)])
        for i, k in enumerate(group):
            block = total if len(group) == 1 else total[i * capacity : (i + 1) * capacity]
            returned[k] = swap(block, "exp", k)

    hidden_half = call(
        functools.partial(combine, experts),
        [shape_of((token_count, half))],
        [token_rows, high, low, *(returned[k] for k in range(experts))],
        flops=4 * 3 * token_count * token_count * half,
    )[0]

    hidden_other = swap(hidden_half, "tp", 1)
    mine = hidden_half
    other = hidden_other
    step = sections // 2
    while step >= 2:
        pairs = [(i, i + step) for i in range(0, sections, 2 * step)]
        mine = jnp.where(sec % (2 * step) == step, lax.ppermute(mine, "sec", pairs), mine)
        step //= 2
    if sections > 2:
        pairs = []
        for i in range(2, sections, 2):
            pairs += [(i * tp_size + t, i * tp_size + (t ^ 1)) for t in range(tp_size)]
        other = jnp.where(sec >= 2, lax.ppermute(mine, ("sec", "tp"), pairs), other)
    beside = [(i, i + 1) for i in range(0, sections, 2)]
    mine = jnp.where(sec % 2 == 1, lax.ppermute(mine, "sec", beside), mine)
    other = jnp.where(sec % 2 == 1, lax.ppermute(other, "sec", beside), other)

    local_width = query_weight.shape[2]
    queries = call(
        project,
        [shape_of((token_count, local_width))],
        [hidden_half, hidden_other, attn_gain, query_weight[0]],
        flops=2 * token_count * model_width * local_width,
    )[0]
    context, away, kept = call(
        attend,
        [
            shape_of((token_count, local_width)),
            shape_of((token_count, model_width // 2)),
            shape_of((token_count, model_width // 2), WIDE),
        ],
        [mine, other, queries, cotangent[0], key_weight[0], value_weight[0], hidden_half],
        [pltpu.VMEM((token_count, local_width), LOW)] * 4,
        flops=10 * token_count * model_width * local_width,
    )

    own = model_width // (sections * tp_size)
    count = sections // 2 * tp_size
    both = sections * tp_size
    blocks = call(
        gather_term,
        [shape_of((token_count, own), WIDE)] + [shape_of((token_count, own))] * (count - 1),
        [kept, swap(away, "sec", 1)],
    )
    total = blocks[0]
    for k in range(1, count):
        pairs = []
        for i in range(both):
            section, t = i // tp_size, i % tp_size
            target = (section // 2 * tp_size + t) ^ k
            pairs.append((i, (target // tp_size * 2 + section % 2) * tp_size + target % tp_size))
        total = total + lax.ppermute(blocks[k], ("sec", "tp"), pairs).astype(WIDE)
    return (context[None], total.astype(LOW))


def solution(mesh):
    placed = (
        P("sec", "exp", None),
        P("sec", "exp", None),
        P("sec", "exp", None),
        P("sec", None),
        P("sec", None),
        P("sec", "exp", None, "tp"),
        P("sec", "exp", "tp", None),
        P("sec", None, "tp"),
        P("sec", None, "tp"),
        P("sec", None, "tp"),
        P("sec", "exp", "tp"),
    )
    return jax.shard_map(
        shards,
        mesh=mesh,
        in_specs=placed,
        out_specs=(P("sec", "exp", "tp"), P("exp", ("sec", "tp"))),
        check_vma=False,
    )
```

time: 257 us -> 95.6 us (0.37)
  waiting for transfers between devices: 129 us -> 31.7 us
  blocking collectives: 67.8 us -> 0 us
  starting transfers between devices: 0.34 us -> 43.4 us
  matrix products: 28.5 us -> 0 us
  between operations: 14.1 us -> 0.91 us
  Pallas kernels: 0 us -> 11 us
  other arithmetic: 7.19 us -> 0.96 us
    all_to_all x2 -> x0, blocking collectives: 67.8 us -> none  [the longest x1 43.2 us: shards(): lax.all_to_all(outgoing, 'exp', split_axis=0, concat_axis=0, tiled=True)]
    ppermute x0 -> x21, starting transfers between devices: none -> 43.4 us  [the longest x14 26.8 us: swap(): return lax.ppermute(block, axis, [(i, i ^ step) for i in range(size)])]
    reduce_scatter x1 -> x0, waiting for transfers between devices: 42.6 us -> none  [shards(): lax.psum_scatter(partial_value, 'tp', scatter_dimension=1, tiled=True)]
    unnamed x5 -> x0, waiting for transfers between devices: 31.8 us -> none
    ppermute x0 -> x21, waiting for transfers between devices: none -> 31.7 us  [the longest x14 23.8 us: swap(): return lax.ppermute(block, axis, [(i, i ^ step) for i in range(size)])]
    psum x1 -> x0, waiting for transfers between devices: 30 us -> none  [spread_2(): return lax.psum(block, axis)]
    dot_general x14 -> x0, matrix products: 26.3 us -> none  [the longest x1 5.08 us: shards(): jnp.dot(inner, weight_second, preferred_element_type=jnp.float32)]
    all_gather x1 -> x0, waiting for transfers between devices: 24.6 us -> none  [shards(): returned = lax.all_gather(returned, 'tp', axis=2, tiled=True)]
  transfers between devices with their start and end apart: 4 -> 21, of which waited for: 4 -> 14; matrix products, arithmetic and copies ran while one was open for 2% -> 0% of each run, Pallas kernels for 0% -> 9%
where the time goes in v2:
time: 95.6 us; the launch traced here: 95.3 us
  starting transfers between devices  43.4 us (45%)
  waiting for transfers between devices  31.7 us (33%)
  Pallas kernels  11 us (12%)
  local copies, waits for them, and re-layouts  7.29 us (8%)
  other arithmetic  0.96 us (1%)
    ppermute x14, starting transfers between devices, swap(): return lax.ppermute(block, axis, [(i, i ^ step) for i in range(size)])  26.8 us
    ppermute x14, waiting for transfers between devices, swap(): return lax.ppermute(block, axis, [(i, i ^ step) for i in range(size)])  23.8 us
    pallas_call x10, Pallas kernels, call(): pl.pallas_call(body, out_shape=out_shape, in_specs=[VMEM] * len(inputs),...  11 us
    ppermute x3, starting transfers between devices, shards(): total = total + lax.ppermute(blocks[k], ('sec', 'tp'), pairs).astype(WIDE)  9.73 us
    unnamed x28, local copies, waits for them, and re-layouts  7.29 us
    ppermute x3, waiting for transfers between devices, shards(): total = total + lax.ppermute(blocks[k], ('sec', 'tp'), pairs).astype(WIDE)  3.78 us
    ppermute x1, waiting for transfers between devices, shards(): lax.ppermute(mine, 'sec', pairs)  3.75 us
    ppermute x1, starting transfers between devices, shards(): lax.ppermute(mine, 'sec', pairs)  3.42 us
  transfers between devices with their start and end apart: 21, of which 14 were waited for; matrix products, arithmetic and copies ran while one was open for 0% of the time, Pallas kernels for 9%

profile of v2, /device:TPU:0, one launch (start us, length us, event | category | flops | bytes accessed | tf_op | source)
XLA Modules:
  0.0 95.3 jit_solution(15562389080209073446)
XLA Ops:
  0.6 1.0 %copy-done.5 = bf16[1,256,1024]{2,1,0:T(8,128)(2,1)S(1)} copy-done((bf16[1,256,1024]{2,1,0:T(8,128)(2,1)S(1)}, bf16[1,256,1024]{2,1,0:T(8,128)(2,1)}, u32[]{:S(2)}) %copy-start.5) | copy-done | bytes 524312
  1.7 0.7 copy-done.8
  2.4 0.7 copy-done.13
  3.0 0.9 shard_map.123
  3.9 5.1 %collective-permute-start.8 = (bf16[192,512]{1,0:T(8,128)(2,1)S(1)}, bf16[192,512]{1,0:T(8,128)(2,1)S(1)}, u32[]{:S(2)}, u32[]{:S(2)}) collective-permute-start(bf16[192,512]{1,0:T(8,128)(2,1)S(1)} %get-tuple-element.34), channel_id=1, source_target_pairs={{0,6},{2,4},{4,2},{6,0},{1,7},{3,5},{5,3},{7,1},{8,14},{10,12},{12... | collective-permute-start | bytes 589832 | tf_op jit(solution)/shard_map/ppermute | solution.py:217
  9.1 5.8 %collective-permute-done.8.refs_0_ = bf16[192,512]{1,0:T(8,128)(2,1)S(1)} collective-permute-done((bf16[192,512]{1,0:T(8,128)(2,1)S(1)}, bf16[192,512]{1,0:T(8,128)(2,1)S(1)}, u32[]{:S(2)}, u32[]{:S(2)}) %collective-permute-start.8) | collective-permute-done | bytes 196640 | tf_op jit(solution)/shard_map/ppermute | solution.py:217
  14.9 1.7 %collective-permute-start.9 = (bf16[192,512]{1,0:T(8,128)(2,1)S(1)}, bf16[192,512]{1,0:T(8,128)(2,1)S(1)}, u32[]{:S(2)}, u32[]{:S(2)}) collective-permute-start(bf16[192,512]{1,0:T(8,128)(2,1)S(1)} %collective-permute-done.8.refs_0_), channel_id=1, source_target_pairs={{0,1},{1,0},{2,3},{3,2},{4,5},{5,4},{6,7},{7,6},{8,9},{9,8},{10,11... | collective-permute-start | bytes 589832 | tf_op jit(solution)/shard_map/ppermute | solution.py:217
  16.6 8.0 %collective-permute-start.1 = (bf16[192,1024]{1,0:T(8,128)(2,1)S(1)}, bf16[192,1024]{1,0:T(8,128)(2,1)S(1)}, u32[]{:S(2)}, u32[]{:S(2)}) collective-permute-start(bf16[192,1024]{1,0:T(8,128)(2,1)S(1)} %get-tuple-element.28), channel_id=1, source_target_pairs={{0,2},{2,0},{4,6},{6,4},{1,3},{3,1},{5,7},{7,5},{8,10},{10,8},{12,... | collective-permute-start | bytes 1179656 | tf_op jit(solution)/shard_map/ppermute | solution.py:217
  24.6 1.3 %collective-permute-done.4.refs_0_ = bf16[192,512]{1,0:T(8,128)(2,1)S(1)} collective-permute-done((bf16[192,512]{1,0:T(8,128)(2,1)S(1)}, bf16[192,512]{1,0:T(8,128)(2,1)S(1)}, u32[]{:S(2)}, u32[]{:S(2)}) %collective-permute-start.4) | collective-permute-done | bytes 196640 | tf_op jit(solution)/shard_map/ppermute | solution.py:217
  25.8 1.5 %collective-permute-start.5 = (bf16[192,512]{1,0:T(8,128)(2,1)S(1)}, bf16[192,512]{1,0:T(8,128)(2,1)S(1)}, u32[]{:S(2)}, u32[]{:S(2)}) collective-permute-start(bf16[192,512]{1,0:T(8,128)(2,1)S(1)} %collective-permute-done.4.refs_0_), channel_id=1, source_target_pairs={{0,1},{1,0},{2,3},{3,2},{4,5},{5,4},{6,7},{7,6},{8,9},{9,8},{10,11... | collective-permute-start | bytes 589832 | tf_op jit(solution)/shard_map/ppermute | solution.py:217
  27.4 2.2 %copy-done = bf16[1,1,1024,2048]{3,2,1,0:T(8,128)(2,1)S(1)} copy-done((bf16[1,1,1024,2048]{3,2,1,0:T(8,128)(2,1)S(1)}, bf16[1,1,1024,2048]{3,2,1,0:T(8,128)(2,1)}, u32[]{:S(2)}) %copy-start) | copy-done | bytes 4194328
  29.6 2.2 %copy-done.2 = bf16[1,1,2048,1024]{3,2,1,0:T(8,128)(2,1)S(1)} copy-done((bf16[1,1,2048,1024]{3,2,1,0:T(8,128)(2,1)S(1)}, bf16[1,1,2048,1024]{3,2,1,0:T(8,128)(2,1)}, u32[]{:S(2)}) %copy-start.2) | copy-done | bytes 4194328
  31.8 1.8 %shard_map.124 = (bf16[192,512]{1,0:T(8,128)(2,1)S(1)}, f32[192,512]{1,0:T(8,128)S(1)}) custom-call(bf16[192,1024]{1,0:T(8,128)(2,1)S(1)} %get-tuple-element.25.refs_0_, bf16[1024,2048]{1,0:T(8,128)(2,1)S(1)} %bitcast.14, bf16[2048,1024]{1,0:T(8,128)(2,1)S(1)} %bitcast.18), custom_call_target="tpu_custom_call" | custom-call | flops 1610612736 | bytes 9371648 | tf_op jit(solution)/shard_map/pallas_call | solution.py:31
  33.6 0.6 collective-permute-start
  34.1 0.6 shard_map.122
  34.8 0.5 copy-done.3
  35.2 1.8 %shard_map.127 = (bf16[192,512]{1,0:T(8,128)(2,1)S(1)}, f32[192,512]{1,0:T(8,128)S(1)}) custom-call(bf16[192,512]{1,0:T(8,128)(2,1)S(1)} %collective-permute-done.8.refs_0_, bf16[192,512]{1,0:T(8,128)(2,1)S(1)} %collective-permute-done.9.refs_1_, bf16[1024,2048]{1,0:T(8,128)(2,1)S(1)} %bitcast.15, bf16[2048,1024]{1,0:T(8,128)(2,1)S(1)} %bitcast.19), custom_call_target="tpu_custom_call" | custom-call | flops 1610612736 | bytes 9371648 | tf_op jit(solution)/shard_map/pallas_call | solution.py:31
  37.0 1.1 %collective-permute-start.10 = (bf16[192,512]{1,0:T(8,128)(2,1)S(1)}, bf16[192,512]{1,0:T(8,128)(2,1)S(1)}, u32[]{:S(2)}, u32[]{:S(2)}) collective-permute-start(bf16[192,512]{1,0:T(8,128)(2,1)S(1)} %get-tuple-element.36), channel_id=1, source_target_pairs={{0,1},{1,0},{2,3},{3,2},{4,5},{5,4},{6,7},{7,6},{8,9},{9,8},{10,11... | collective-permute-start | bytes 589832 | tf_op jit(solution)/shard_map/ppermute | solution.py:217
  38.2 1.8 %shard_map.126 = (bf16[192,512]{1,0:T(8,128)(2,1)S(1)}, f32[192,512]{1,0:T(8,128)S(1)}) custom-call(bf16[192,512]{1,0:T(8,128)(2,1)S(1)} %collective-permute-done.4.refs_0_, bf16[192,512]{1,0:T(8,128)(2,1)S(1)} %collective-permute-done.5.refs_1_, bf16[1024,2048]{1,0:T(8,128)(2,1)S(1)} %bitcast.16, bf16[2048,1024]{1,0:T(8,128)(2,1)S(1)} %bitcast.20), custom_call_target="tpu_custom_call" | custom-call | flops 1610612736 | bytes 9371648 | tf_op jit(solution)/shard_map/pallas_call | solution.py:31
  40.0 1.0 %collective-permute-start.6 = (bf16[192,512]{1,0:T(8,128)(2,1)S(1)}, bf16[192,512]{1,0:T(8,128)(2,1)S(1)}, u32[]{:S(2)}, u32[]{:S(2)}) collective-permute-start(bf16[192,512]{1,0:T(8,128)(2,1)S(1)} %get-tuple-element.33), channel_id=1, source_target_pairs={{0,1},{1,0},{2,3},{3,2},{4,5},{5,4},{6,7},{7,6},{8,9},{9,8},{10,11... | collective-permute-start | bytes 589832 | tf_op jit(solution)/shard_map/ppermute | solution.py:217
  41.0 1.8 %shard_map.125 = (bf16[192,512]{1,0:T(8,128)(2,1)S(1)}, f32[192,512]{1,0:T(8,128)S(1)}) custom-call(bf16[192,1024]{1,0:T(8,128)(2,1)S(1)} %collective-permute-done.1.refs_0_, bf16[1024,2048]{1,0:T(8,128)(2,1)S(1)} %bitcast.17, bf16[2048,1024]{1,0:T(8,128)(2,1)S(1)} %bitcast.21), custom_call_target="tpu_custom_call" | custom-call | flops 1610612736 | bytes 9371648 | tf_op jit(solution)/shard_map/pallas_call | solution.py:31
  42.9 1.2 %collective-permute-start.2 = (bf16[192,512]{1,0:T(8,128)(2,1)S(1)}, bf16[192,512]{1,0:T(8,128)(2,1)S(1)}, u32[]{:S(2)}, u32[]{:S(2)}) collective-permute-start(bf16[192,512]{1,0:T(8,128)(2,1)S(1)} %get-tuple-element.30), channel_id=1, source_target_pairs={{0,1},{1,0},{2,3},{3,2},{4,5},{5,4},{6,7},{7,6},{8,9},{9,8},{10,11... | collective-permute-start | bytes 589832 | tf_op jit(solution)/shard_map/ppermute | solution.py:217
  44.0 0.9 collective-permute-done.10
  45.0 2.5 %collective-permute-start.11 = (bf16[192,512]{1,0:T(8,128)(2,1)S(1)}, bf16[192,512]{1,0:T(8,128)(2,1)S(1)}, u32[]{:S(2)}, u32[]{:S(2)}) collective-permute-start(bf16[192,512]{1,0:T(8,128)(2,1)S(1)} %add_convert_fusion), channel_id=1, source_target_pairs={{0,6},{2,4},{4,2},{6,0},{1,7},{3,5},{5,3},{7,1},{8,14},{10,12},{12... | collective-permute-start | bytes 589832 | tf_op jit(solution)/shard_map/ppermute | solution.py:217
  47.5 1.6 %collective-permute-done.6 = bf16[192,512]{1,0:T(8,128)(2,1)S(1)} collective-permute-done((bf16[192,512]{1,0:T(8,128)(2,1)S(1)}, bf16[192,512]{1,0:T(8,128)(2,1)S(1)}, u32[]{:S(2)}, u32[]{:S(2)}) %collective-permute-start.6) | collective-permute-done | bytes 196640 | tf_op jit(solution)/shard_map/ppermute | solution.py:217
  49.3 2.7 %collective-permute-done.2 = bf16[192,512]{1,0:T(8,128)(2,1)S(1)} collective-permute-done((bf16[192,512]{1,0:T(8,128)(2,1)S(1)}, bf16[192,512]{1,0:T(8,128)(2,1)S(1)}, u32[]{:S(2)}, u32[]{:S(2)}) %collective-permute-start.2) | collective-permute-done | bytes 196640 | tf_op jit(solution)/shard_map/ppermute | solution.py:217
  52.0 0.4 collective-permute-start.3
  52.5 1.8 %collective-permute-done.11.refs_3_ = bf16[192,512]{1,0:T(8,128)(2,1)S(1)} collective-permute-done((bf16[192,512]{1,0:T(8,128)(2,1)S(1)}, bf16[192,512]{1,0:T(8,128)(2,1)S(1)}, u32[]{:S(2)}, u32[]{:S(2)}) %collective-permute-start.11) | collective-permute-done | bytes 196640 | tf_op jit(solution)/shard_map/ppermute | solution.py:217
  54.3 7.2 %collective-permute-done.7.refs_2_ = bf16[192,512]{1,0:T(8,128)(2,1)S(1)} collective-permute-done((bf16[192,512]{1,0:T(8,128)(2,1)S(1)}, bf16[192,512]{1,0:T(8,128)(2,1)S(1)}, u32[]{:S(2)}, u32[]{:S(2)}) %collective-permute-start.7) | collective-permute-done | bytes 196640 | tf_op jit(solution)/shard_map/ppermute | solution.py:217
  61.5 0.9 collective-permute-done.3.refs_1_
  62.4 0.7 shard_map.128.mine.hidden
  63.1 3.4 %collective-permute-start.12 = (bf16[256,512]{1,0:T(8,128)(2,1)S(1)}, bf16[256,512]{1,0:T(8,128)(2,1)S(1)}, u32[]{:S(2)}, u32[]{:S(2)}) collective-permute-start(bf16[256,512]{1,0:T(8,128)(2,1)S(1)} %shard_map.128.mine.hidden), channel_id=1, source_target_pairs={{0,16},{1,17},{2,18},{3,19},{4,20},{5,21},{6,22},{7,23}} | collective-permute-start | bytes 786440 | tf_op jit(solution)/shard_map/ppermute | solution.py:303
  66.7 3.7 %collective-permute-done.12 = bf16[256,512]{1,0:T(8,128)(2,1)S(1)} collective-permute-done((bf16[256,512]{1,0:T(8,128)(2,1)S(1)}, bf16[256,512]{1,0:T(8,128)(2,1)S(1)}, u32[]{:S(2)}, u32[]{:S(2)}) %collective-permute-start.12) | collective-permute-done | bytes 262176 | tf_op jit(solution)/shard_map/ppermute | solution.py:303
  70.4 0.7 collective-permute-start.14
  71.2 1.4 %collective-permute-start.13 = (bf16[256,512]{1,0:T(8,128)(2,1)S(1)}, bf16[256,512]{1,0:T(8,128)(2,1)S(1)}, u32[]{:S(2)}, u32[]{:S(2)}) collective-permute-start(bf16[256,512]{1,0:T(8,128)(2,1)S(1)} %broadcast_select_fusion.1), channel_id=1, source_target_pairs={{0,8},{16,24},{1,9},{17,25},{2,10},{18,26},{3,11},{19,27},{4,12},{... | collective-permute-start | bytes 786440 | tf_op jit(solution)/shard_map/ppermute | solution.py:311
  72.6 0.4 collective-permute-done.15.other
  73.0 1.3 %collective-permute-start.16 = (bf16[256,512]{1,0:T(8,128)(2,1)S(1)}, bf16[256,512]{1,0:T(8,128)(2,1)S(1)}, u32[]{:S(2)}, u32[]{:S(2)}) collective-permute-start(bf16[256,512]{1,0:T(8,128)(2,1)S(1)} %broadcast_select_fusion), channel_id=1, source_target_pairs={{0,8},{16,24},{1,9},{17,25},{2,10},{18,26},{3,11},{19,27},{4,12},{... | collective-permute-start | bytes 786440 | tf_op jit(solution)/shard_map/ppermute | solution.py:312
  74.4 0.7 shard_map.129.queries
  75.1 0.4 collective-permute-done.16
  75.5 0.8 shard_map.130
  76.3 3.5 %collective-permute-start.17 = (bf16[256,512]{1,0:T(8,128)(2,1)S(1)}, bf16[256,512]{1,0:T(8,128)(2,1)S(1)}, u32[]{:S(2)}, u32[]{:S(2)}) collective-permute-start(bf16[256,512]{1,0:T(8,128)(2,1)S(1)} %get-tuple-element.39), channel_id=1, source_target_pairs={{0,8},{8,0},{16,24},{24,16},{1,9},{9,1},{17,25},{25,17},{2,10},{10... | collective-permute-start | bytes 786440 | tf_op jit(solution)/shard_map/ppermute | solution.py:217
  79.8 1.2 %collective-permute-done.17.arrived = bf16[256,512]{1,0:T(8,128)(2,1)S(1)} collective-permute-done((bf16[256,512]{1,0:T(8,128)(2,1)S(1)}, bf16[256,512]{1,0:T(8,128)(2,1)S(1)}, u32[]{:S(2)}, u32[]{:S(2)}) %collective-permute-start.17) | collective-permute-done | bytes 262176 | tf_op jit(solution)/shard_map/ppermute | solution.py:217
  81.1 0.1 collective-permute-start.18
  81.2 8.2 %collective-permute-start.19 = (bf16[256,128]{1,0:T(8,128)(2,1)S(1)}, bf16[256,128]{1,0:T(8,128)(2,1)S(1)}, u32[]{:S(2)}, u32[]{:S(2)}) collective-permute-start(bf16[256,128]{1,0:T(8,128)(2,1)S(1)} %get-tuple-element.42), channel_id=1, source_target_pairs={{0,16},{1,17},{8,24},{9,25},{16,0},{17,1},{24,8},{25,9},{2,18},{3,... | collective-permute-start | bytes 196616 | tf_op jit(solution)/shard_map/ppermute | solution.py:348
  89.4 1.4 %collective-permute-start.20 = (bf16[256,128]{1,0:T(8,128)(2,1)S(1)}, bf16[256,128]{1,0:T(8,128)(2,1)S(1)}, u32[]{:S(2)}, u32[]{:S(2)}) collective-permute-start(bf16[256,128]{1,0:T(8,128)(2,1)S(1)} %get-tuple-element.43), channel_id=1, source_target_pairs={{0,17},{1,16},{8,25},{9,24},{16,1},{17,0},{24,9},{25,8},{2,19},{3,... | collective-permute-start | bytes 196616 | tf_op jit(solution)/shard_map/ppermute | solution.py:348
  90.8 1.2 %collective-permute-done.19 = bf16[256,128]{1,0:T(8,128)(2,1)S(1)} collective-permute-done((bf16[256,128]{1,0:T(8,128)(2,1)S(1)}, bf16[256,128]{1,0:T(8,128)(2,1)S(1)}, u32[]{:S(2)}, u32[]{:S(2)}) %collective-permute-start.19) | collective-permute-done | bytes 65568 | tf_op jit(solution)/shard_map/ppermute | solution.py:348
  92.0 2.5 %collective-permute-done.20 = bf16[256,128]{1,0:T(8,128)(2,1)S(1)} collective-permute-done((bf16[256,128]{1,0:T(8,128)(2,1)S(1)}, bf16[256,128]{1,0:T(8,128)(2,1)S(1)}, u32[]{:S(2)}, u32[]{:S(2)}) %collective-permute-start.20) | collective-permute-done | bytes 65568 | tf_op jit(solution)/shard_map/ppermute | solution.py:348
  94.6 0.7 add_convert_fusion.4
  (41 shorter events, 0.6 us)
Async XLA Ops:
  0.6 1.0 %copy-start.5 = (bf16[1,256,1024]{2,1,0:T(8,128)(2,1)S(1)}, bf16[1,256,1024]{2,1,0:T(8,128)(2,1)}, u32[]{:S(2)}) copy-start(bf16[1,256,1024]{2,1,0:T(8,128)(2,1)} %param.11) | copy-start | bytes 1572868
  1.7 0.7 copy-start.8
  2.4 0.7 copy-start.13
  3.9 10.9 %collective-permute-start.8 = (bf16[192,512]{1,0:T(8,128)(2,1)S(1)}, bf16[192,512]{1,0:T(8,128)(2,1)S(1)}, u32[]{:S(2)}, u32[]{:S(2)}) collective-permute-start(bf16[192,512]{1,0:T(8,128)(2,1)S(1)} %get-tuple-element.34), channel_id=1, source_target_pairs={{0,6},{2,4},{4,2},{6,0},{1,7},{3,5},{5,3},{7,1},{8,14},{10,12},{12... | collective-permute-start | bytes 589832 | tf_op jit(solution)/shard_map/ppermute | solution.py:217
  9.1 16.8 %collective-permute-start.4 = (bf16[192,512]{1,0:T(8,128)(2,1)S(1)}, bf16[192,512]{1,0:T(8,128)(2,1)S(1)}, u32[]{:S(2)}, u32[]{:S(2)}) collective-permute-start(bf16[192,512]{1,0:T(8,128)(2,1)S(1)} %get-tuple-element.31), channel_id=1, source_target_pairs={{0,4},{2,6},{4,0},{6,2},{1,5},{3,7},{5,1},{7,3},{8,12},{10,14},{12... | collective-permute-start | bytes 589832 | tf_op jit(solution)/shard_map/ppermute | solution.py:217
  14.9 19.9 %collective-permute-start.9 = (bf16[192,512]{1,0:T(8,128)(2,1)S(1)}, bf16[192,512]{1,0:T(8,128)(2,1)S(1)}, u32[]{:S(2)}, u32[]{:S(2)}) collective-permute-start(bf16[192,512]{1,0:T(8,128)(2,1)S(1)} %collective-permute-done.8.refs_0_), channel_id=1, source_target_pairs={{0,1},{1,0},{2,3},{3,2},{4,5},{5,4},{6,7},{7,6},{8,9},{9,8},{10,11... | collective-permute-start | bytes 589832 | tf_op jit(solution)/shard_map/ppermute | solution.py:217
  16.6 24.4 %collective-permute-start.1 = (bf16[192,1024]{1,0:T(8,128)(2,1)S(1)}, bf16[192,1024]{1,0:T(8,128)(2,1)S(1)}, u32[]{:S(2)}, u32[]{:S(2)}) collective-permute-start(bf16[192,1024]{1,0:T(8,128)(2,1)S(1)} %get-tuple-element.28), channel_id=1, source_target_pairs={{0,2},{2,0},{4,6},{6,4},{1,3},{3,1},{5,7},{7,5},{8,10},{10,8},{12,... | collective-permute-start | bytes 1179656 | tf_op jit(solution)/shard_map/ppermute | solution.py:217
  25.8 12.3 %collective-permute-start.5 = (bf16[192,512]{1,0:T(8,128)(2,1)S(1)}, bf16[192,512]{1,0:T(8,128)(2,1)S(1)}, u32[]{:S(2)}, u32[]{:S(2)}) collective-permute-start(bf16[192,512]{1,0:T(8,128)(2,1)S(1)} %collective-permute-done.4.refs_0_), channel_id=1, source_target_pairs={{0,1},{1,0},{2,3},{3,2},{4,5},{5,4},{6,7},{7,6},{8,9},{9,8},{10,11... | collective-permute-start | bytes 589832 | tf_op jit(solution)/shard_map/ppermute | solution.py:217
  27.4 2.2 %copy-start = (bf16[1,1,1024,2048]{3,2,1,0:T(8,128)(2,1)S(1)}, bf16[1,1,1024,2048]{3,2,1,0:T(8,128)(2,1)}, u32[]{:S(2)}) copy-start(bf16[1,1,1024,2048]{3,2,1,0:T(8,128)(2,1)} %param.16) | copy-start | bytes 12582916
  29.6 2.2 %copy-start.2 = (bf16[1,1,2048,1024]{3,2,1,0:T(8,128)(2,1)S(1)}, bf16[1,1,2048,1024]{3,2,1,0:T(8,128)(2,1)}, u32[]{:S(2)}) copy-start(bf16[1,1,2048,1024]{3,2,1,0:T(8,128)(2,1)} %param.17) | copy-start | bytes 12582916
  31.7 2.4 %copy-start.9 = (f32[1,256,2]{1,2,0:T(2,128)S(1)}, f32[1,256,2]{1,2,0:T(2,128)}, u32[]{:S(2)}) copy-start(f32[1,256,2]{1,2,0:T(2,128)} %param.13) | copy-start | bytes 6148
  31.7 3.0 %copy-start.1 = (bf16[1,1,1024,2048]{3,2,1,0:T(8,128)(2,1)S(1)}, bf16[1,1,1024,2048]{3,2,1,0:T(8,128)(2,1)}, u32[]{:S(2)}) copy-start(bf16[1,1,1024,2048]{3,2,1,0:T(8,128)(2,1)} %param.16) | copy-start | bytes 12582916
  31.8 3.5 %copy-start.3 = (bf16[1,1,2048,1024]{3,2,1,0:T(8,128)(2,1)S(1)}, bf16[1,1,2048,1024]{3,2,1,0:T(8,128)(2,1)}, u32[]{:S(2)}) copy-start(bf16[1,1,2048,1024]{3,2,1,0:T(8,128)(2,1)} %param.17) | copy-start | bytes 12582916
  33.6 18.9 %collective-permute-start = (bf16[192,512]{1,0:T(8,128)(2,1)S(1)}, bf16[192,512]{1,0:T(8,128)(2,1)S(1)}, u32[]{:S(2)}, u32[]{:S(2)}) collective-permute-start(bf16[192,512]{1,0:T(8,128)(2,1)S(1)} %get-tuple-element.27), channel_id=1, source_target_pairs={{0,1},{1,0},{2,3},{3,2},{4,5},{5,4},{6,7},{7,6},{8,9},{9,8},{10,11... | collective-permute-start | bytes 589832 | tf_op jit(solution)/shard_map/ppermute | solution.py:217
  37.0 7.9 %collective-permute-start.10 = (bf16[192,512]{1,0:T(8,128)(2,1)S(1)}, bf16[192,512]{1,0:T(8,128)(2,1)S(1)}, u32[]{:S(2)}, u32[]{:S(2)}) collective-permute-start(bf16[192,512]{1,0:T(8,128)(2,1)S(1)} %get-tuple-element.36), channel_id=1, source_target_pairs={{0,1},{1,0},{2,3},{3,2},{4,5},{5,4},{6,7},{7,6},{8,9},{9,8},{10,11... | collective-permute-start | bytes 589832 | tf_op jit(solution)/shard_map/ppermute | solution.py:217
  40.0 22.4 %copy-start.6 = (bf16[1,256,1024]{2,1,0:T(8,128)(2,1)S(1)}, bf16[1,256,1024]{2,1,0:T(8,128)(2,1)}, u32[]{:S(2)}) copy-start(bf16[1,256,1024]{2,1,0:T(8,128)(2,1)} %param.11) | copy-start | bytes 1572868
  40.0 9.1 %collective-permute-start.6 = (bf16[192,512]{1,0:T(8,128)(2,1)S(1)}, bf16[192,512]{1,0:T(8,128)(2,1)S(1)}, u32[]{:S(2)}, u32[]{:S(2)}) collective-permute-start(bf16[192,512]{1,0:T(8,128)(2,1)S(1)} %get-tuple-element.33), channel_id=1, source_target_pairs={{0,1},{1,0},{2,3},{3,2},{4,5},{5,4},{6,7},{7,6},{8,9},{9,8},{10,11... | collective-permute-start | bytes 589832 | tf_op jit(solution)/shard_map/ppermute | solution.py:217
  42.9 31.5 %copy-start.4 = (bf16[1,1024,512]{2,1,0:T(8,128)(2,1)S(1)}, bf16[1,1024,512]{2,1,0:T(8,128)(2,1)}, u32[]{:S(2)}) copy-start(bf16[1,1024,512]{2,1,0:T(8,128)(2,1)} %param.18) | copy-start | bytes 3145732
  42.9 31.5 %copy-start.7 = (f32[1,1024]{1,0:T(1,128)S(1)}, f32[1,1024]{1,0:T(1,128)}, u32[]{:S(2)}) copy-start(f32[1,1024]{1,0:T(1,128)} %gain.3) | copy-start | bytes 12292
  42.9 9.1 %collective-permute-start.2 = (bf16[192,512]{1,0:T(8,128)(2,1)S(1)}, bf16[192,512]{1,0:T(8,128)(2,1)S(1)}, u32[]{:S(2)}, u32[]{:S(2)}) collective-permute-start(bf16[192,512]{1,0:T(8,128)(2,1)S(1)} %get-tuple-element.30), channel_id=1, source_target_pairs={{0,1},{1,0},{2,3},{3,2},{4,5},{5,4},{6,7},{7,6},{8,9},{9,8},{10,11... | collective-permute-start | bytes 589832 | tf_op jit(solution)/shard_map/ppermute | solution.py:217
  45.0 9.3 %collective-permute-start.11 = (bf16[192,512]{1,0:T(8,128)(2,1)S(1)}, bf16[192,512]{1,0:T(8,128)(2,1)S(1)}, u32[]{:S(2)}, u32[]{:S(2)}) collective-permute-start(bf16[192,512]{1,0:T(8,128)(2,1)S(1)} %add_convert_fusion), channel_id=1, source_target_pairs={{0,6},{2,4},{4,2},{6,0},{1,7},{3,5},{5,3},{7,1},{8,14},{10,12},{12... | collective-permute-start | bytes 589832 | tf_op jit(solution)/shard_map/ppermute | solution.py:217
  49.2 12.3 %collective-permute-start.7 = (bf16[192,512]{1,0:T(8,128)(2,1)S(1)}, bf16[192,512]{1,0:T(8,128)(2,1)S(1)}, u32[]{:S(2)}, u32[]{:S(2)}) collective-permute-start(bf16[192,512]{1,0:T(8,128)(2,1)S(1)} %add_convert_fusion.1), channel_id=1, source_target_pairs={{0,4},{2,6},{4,0},{6,2},{1,5},{3,7},{5,1},{7,3},{8,12},{10,14},{12... | collective-permute-start | bytes 589832 | tf_op jit(solution)/shard_map/ppermute | solution.py:217
  52.0 10.4 %collective-permute-start.3 = (bf16[192,512]{1,0:T(8,128)(2,1)S(1)}, bf16[192,512]{1,0:T(8,128)(2,1)S(1)}, u32[]{:S(2)}, u32[]{:S(2)}) collective-permute-start(bf16[192,512]{1,0:T(8,128)(2,1)S(1)} %add_convert_fusion.2), channel_id=1, source_target_pairs={{0,2},{2,0},{4,6},{6,4},{1,3},{3,1},{5,7},{7,5},{8,10},{10,8},{12,... | collective-permute-start | bytes 589832 | tf_op jit(solution)/shard_map/ppermute | solution.py:217
  52.4 23.1 %copy-start.10 = (bf16[1,1024,512]{2,1,0:T(8,128)(2,1)S(1)}, bf16[1,1024,512]{2,1,0:T(8,128)(2,1)}, u32[]{:S(2)}) copy-start(bf16[1,1024,512]{2,1,0:T(8,128)(2,1)} %param.19) | copy-start | bytes 3145732
  52.4 23.1 %copy-start.12 = (bf16[1,256,512]{2,1,0:T(8,128)(2,1)S(1)}, bf16[1,256,512]{2,1,0:T(8,128)(2,1)}, u32[]{:S(2)}) copy-start(bf16[1,256,512]{2,1,0:T(8,128)(2,1)} %param.21) | copy-start | bytes 786436
  63.1 7.3 %collective-permute-start.12 = (bf16[256,512]{1,0:T(8,128)(2,1)S(1)}, bf16[256,512]{1,0:T(8,128)(2,1)S(1)}, u32[]{:S(2)}, u32[]{:S(2)}) collective-permute-start(bf16[256,512]{1,0:T(8,128)(2,1)S(1)} %shard_map.128.mine.hidden), channel_id=1, source_target_pairs={{0,16},{1,17},{2,18},{3,19},{4,20},{5,21},{6,22},{7,23}} | collective-permute-start | bytes 786440 | tf_op jit(solution)/shard_map/ppermute | solution.py:303
  66.6 6.4 %collective-permute-start.15 = (bf16[256,512]{1,0:T(8,128)(2,1)S(1)}, bf16[256,512]{1,0:T(8,128)(2,1)S(1)}, u32[]{:S(2)}, u32[]{:S(2)}) collective-permute-start(bf16[256,512]{1,0:T(8,128)(2,1)S(1)} %shard_map.128.mine.hidden), channel_id=1, source_target_pairs={{0,1},{1,0},{2,3},{3,2},{4,5},{5,4},{6,7},{7,6},{8,9},{9,8},{10,11... | collective-permute-start | bytes 786440 | tf_op jit(solution)/shard_map/ppermute | solution.py:217
  70.4 2.6 %collective-permute-start.14 = (bf16[256,512]{1,0:T(8,128)(2,1)S(1)}, bf16[256,512]{1,0:T(8,128)(2,1)S(1)}, u32[]{:S(2)}, u32[]{:S(2)}) collective-permute-start(bf16[256,512]{1,0:T(8,128)(2,1)S(1)} %broadcast_select_fusion.1), channel_id=1, source_target_pairs={{16,17},{17,16},{18,19},{19,18},{20,21},{21,20},{22,23},{23,22}} | collective-permute-start | bytes 786440 | tf_op jit(solution)/shard_map/ppermute | solution.py:309
  71.1 4.4 %copy-start.11 = (bf16[1,1024,512]{2,1,0:T(8,128)(2,1)S(1)}, bf16[1,1024,512]{2,1,0:T(8,128)(2,1)}, u32[]{:S(2)}) copy-start(bf16[1,1024,512]{2,1,0:T(8,128)(2,1)} %param.20) | copy-start | bytes 3145732
  71.2 3.9 %collective-permute-start.13 = (bf16[256,512]{1,0:T(8,128)(2,1)S(1)}, bf16[256,512]{1,0:T(8,128)(2,1)S(1)}, u32[]{:S(2)}, u32[]{:S(2)}) collective-permute-start(bf16[256,512]{1,0:T(8,128)(2,1)S(1)} %broadcast_select_fusion.1), channel_id=1, source_target_pairs={{0,8},{16,24},{1,9},{17,25},{2,10},{18,26},{3,11},{19,27},{4,12},{... | collective-permute-start | bytes 786440 | tf_op jit(solution)/shard_map/ppermute | solution.py:311
  73.0 2.4 %collective-permute-start.16 = (bf16[256,512]{1,0:T(8,128)(2,1)S(1)}, bf16[256,512]{1,0:T(8,128)(2,1)S(1)}, u32[]{:S(2)}, u32[]{:S(2)}) collective-permute-start(bf16[256,512]{1,0:T(8,128)(2,1)S(1)} %broadcast_select_fusion), channel_id=1, source_target_pairs={{0,8},{16,24},{1,9},{17,25},{2,10},{18,26},{3,11},{19,27},{4,12},{... | collective-permute-start | bytes 786440 | tf_op jit(solution)/shard_map/ppermute | solution.py:312
  76.3 4.6 %collective-permute-start.17 = (bf16[256,512]{1,0:T(8,128)(2,1)S(1)}, bf16[256,512]{1,0:T(8,128)(2,1)S(1)}, u32[]{:S(2)}, u32[]{:S(2)}) collective-permute-start(bf16[256,512]{1,0:T(8,128)(2,1)S(1)} %get-tuple-element.39), channel_id=1, source_target_pairs={{0,8},{8,0},{16,24},{24,16},{1,9},{9,1},{17,25},{25,17},{2,10},{10... | collective-permute-start | bytes 786440 | tf_op jit(solution)/shard_map/ppermute | solution.py:217
  81.1 9.7 %collective-permute-start.18 = (bf16[256,128]{1,0:T(8,128)(2,1)S(1)}, bf16[256,128]{1,0:T(8,128)(2,1)S(1)}, u32[]{:S(2)}, u32[]{:S(2)}) collective-permute-start(bf16[256,128]{1,0:T(8,128)(2,1)S(1)} %get-tuple-element.41), channel_id=1, source_target_pairs={{0,1},{1,0},{8,9},{9,8},{16,17},{17,16},{24,25},{25,24},{2,3},{3,2... | collective-permute-start | bytes 196616 | tf_op jit(solution)/shard_map/ppermute | solution.py:348
  81.2 10.9 %collective-permute-start.19 = (bf16[256,128]{1,0:T(8,128)(2,1)S(1)}, bf16[256,128]{1,0:T(8,128)(2,1)S(1)}, u32[]{:S(2)}, u32[]{:S(2)}) collective-permute-start(bf16[256,128]{1,0:T(8,128)(2,1)S(1)} %get-tuple-element.42), channel_id=1, source_target_pairs={{0,16},{1,17},{8,24},{9,25},{16,0},{17,1},{24,8},{25,9},{2,18},{3,... | collective-permute-start | bytes 196616 | tf_op jit(solution)/shard_map/ppermute | solution.py:348
  89.4 5.2 %collective-permute-start.20 = (bf16[256,128]{1,0:T(8,128)(2,1)S(1)}, bf16[256,128]{1,0:T(8,128)(2,1)S(1)}, u32[]{:S(2)}, u32[]{:S(2)}) collective-permute-start(bf16[256,128]{1,0:T(8,128)(2,1)S(1)} %get-tuple-element.43), channel_id=1, source_target_pairs={{0,17},{1,16},{8,25},{9,24},{16,1},{17,0},{24,9},{25,8},{2,19},{3,... | collective-permute-start | bytes 196616 | tf_op jit(solution)/shard_map/ppermute | solution.py:348

commit v3 on v2

--- a/solution.py
+++ b/solution.py
@@ -15,6 +15,8 @@
 LOW = jnp.bfloat16
 WIDE = jnp.float32
 VMEM = pl.BlockSpec(memory_space=pltpu.VMEM)
+HBM = pl.BlockSpec(memory_space=pltpu.HBM)
+ANY = pl.BlockSpec(memory_space=pl.ANY)
 NT = (((1,), (1,)), ((), ()))
 TN = (((0,), (0,)), ((), ()))
 
@@ -23,20 +25,28 @@
     return lax.dot_general(a, b, dims, preferred_element_type=WIDE)
 
 
-def call(body, out_shape, inputs, scratch=(), flops=0, limit=40):
+def call(body, out_shape, inputs, scratch=(), flops=0, limit=40, remote=(), after=(), held=()):
     def size(x):
         return math.prod(x.shape) * jnp.dtype(x.dtype).itemsize
 
+    count, results = len(inputs), len(out_shape)
+    extra = len(after) + len(held)
+
+    def run(*refs):
+        outs = refs[count + extra : count + extra + results]
+        return body(*refs[:count], *outs, *refs[count + extra + results + len(held) :])
+
     moved = sum(size(x) for x in inputs) + sum(size(x) for x in out_shape)
     return pl.pallas_call(
-        body,
-        out_shape=out_shape,
-        in_specs=[VMEM] * len(inputs),
-        out_specs=[VMEM] * len(out_shape),
+        run,
+        out_shape=[*out_shape, *(shape_of(x.shape, x.dtype) for x in held)],
+        in_specs=[HBM if i in remote else VMEM for i in range(count)] + [ANY] * extra,
+        out_specs=[VMEM] * results + [ANY] * len(held),
         scratch_shapes=list(scratch),
+        input_output_aliases={count + len(after) + i: results + i for i in range(len(held))},
         compiler_params=pltpu.CompilerParams(vmem_limit_bytes=limit * 2**20),
         cost_estimate=pl.CostEstimate(flops=flops, bytes_accessed=moved, transcendentals=0),
-    )(*inputs)
+    )(*inputs, *after, *held)
 
 
 def shape_of(dims, kind=LOW):
@@ -60,13 +70,16 @@
     return jnp.where(either, before, -1.0), first, second
 
 
+def table(place, k, capacity):
+    slots = lax.broadcasted_iota(jnp.int32, (capacity, place.shape[1]), 0).astype(WIDE)
+    return jnp.where(place[k : k + 1, :] == slots, 1.0, 0.0).astype(LOW)
+
+
 def prepare(experts, tokens, routes, gain, *outs):
-    far, near, own = outs[:-3], outs[-3], outs[-2]
-    normed_ref = outs[-1]
+    far, near, own, normed_ref = outs[:-3], outs[-3], outs[-2], outs[-1]
     me = lax.axis_index("exp")
     tp = lax.axis_index("tp")
-    token_count, width = tokens.shape
-    capacity = own.shape[0]
+    capacity, width = own.shape
     half = width // 2
     wide = tokens[...].astype(WIDE)
     average = jnp.mean(wide, axis=-1, keepdims=True)
@@ -74,17 +87,12 @@
     spread = jnp.mean(centred * centred, axis=-1, keepdims=True)
     normed_ref[...] = (centred * lax.rsqrt(spread + EPS) * gain[...]).astype(LOW)
     place, _, _ = places(routes[...], me, max(16, experts))
-    slots = lax.broadcasted_iota(jnp.int32, (capacity, token_count), 0).astype(WIDE)
-
-    def table(k):
-        return jnp.where(place[k : k + 1, :] == slots, 1.0, 0.0).astype(LOW)
-
     normed_half = normed_ref[:, part(tp, half)]
     for k in range(experts - 1, 1, -1):
-        far[k - 2][...] = matmul(table(k), normed_half).astype(LOW)
+        far[k - 2][...] = matmul(table(place, k, capacity), normed_half).astype(LOW)
     normed = normed_ref[...]
-    near[...] = matmul(table(1), normed).astype(LOW)
-    own[...] = matmul(table(0), normed).astype(LOW)
+    near[...] = matmul(table(place, 1, capacity), normed).astype(LOW)
+    own[...] = matmul(table(place, 0, capacity), normed).astype(LOW)
 
 
 def mixing(experts, routes, gates, high, low):
@@ -120,6 +128,31 @@
         inner[:, columns] = jnp.maximum(value, 0.0).astype(LOW)
     away[...] = matmul(inner[...], second[:, part(1 - tp, half)]).astype(LOW)
     kept[...] = matmul(inner[...], second[:, part(tp, half)])
+
+
+def expert_first(rows, first, second, away, kept, first_here, second_here, inner, arrived):
+    tp = lax.axis_index("tp")
+    width, hidden = first.shape
+    half = width // 2
+    chunk = min(512, hidden)
+    columns = [slice(c * chunk, (c + 1) * chunk) for c in range(hidden // chunk)]
+    loads = [
+        pltpu.make_async_copy(first.at[:, c], first_here.at[:, c], arrived.at[i])
+        for i, c in enumerate(columns)
+    ]
+    loads.append(pltpu.make_async_copy(second, second_here, arrived.at[len(columns)]))
+    for load in loads:
+        load.start()
+    for c, load in zip(columns, loads):
+        load.wait()
+        inner[:, c] = jnp.maximum(matmul(rows[...], first_here[:, c]), 0.0).astype(LOW)
+    loads[-1].wait()
+    away[...] = matmul(inner[...], second_here[:, part(1 - tp, half)]).astype(LOW)
+    kept[...] = matmul(inner[...], second_here[:, part(tp, half)])
+
+
+def idle():
+    pass
 
 
 def combine(experts, tokens, high, low, *refs):
@@ -244,22 +277,46 @@
     weight_second = expert_out[0, 0]
     units = weight_first.shape[1]
 
-    far_count = experts - 2
-    prepared = call(
+    middle = max(2, experts // 2 + 1)
+    groups = [list(range(experts - 1, middle - 1, -1)), list(range(middle - 1, 1, -1))]
+    row_half, row_whole = shape_of((capacity, half)), shape_of((capacity, model_width))
+    *far_rows, near_rows, own_rows = call(
         functools.partial(prepare, experts),
-        [shape_of((capacity, half))] * far_count + [shape_of((capacity, model_width))] * 2,
+        [row_half] * (experts - 2) + [row_whole] * 2,
         [token_rows, route_rows, moe_gain],
         [pltpu.VMEM((token_count, model_width), LOW)],
         flops=2 * 3 * token_count * token_count * model_width,
     )
-    far_rows, near_rows, own_rows = prepared[:far_count], prepared[far_count], prepared[-1]
+    far = {k: swap(far_rows[k - 2], "exp", k) for k in groups[0]}
+    loads = max(1, units // 512) + 1
+    own_away, own_kept, weight_first, weight_second = call(
+        expert_first,
+        [
+            row_half,
+            shape_of((capacity, half), WIDE),
+            shape_of(weight_first.shape),
+            shape_of(weight_second.shape),
+        ],
+        [own_rows, weight_first, weight_second],
+        [pltpu.VMEM((capacity, units), LOW), pltpu.SemaphoreType.DMA((loads,))],
+        flops=4 * capacity * model_width * units,
+        remote=(1, 2),
+        limit=44,
+
+    )
+    far |= {k: swap(far_rows[k - 2], "exp", k) for k in groups[1]}
+    near = swap(near_rows, "exp", 1)
     high, low = call(
         functools.partial(mixing, experts),
         [shape_of((experts, token_count, capacity))] * 2,
         [route_rows, gate_rows],
-    )
-
-    def through(rows):
+        after=[own_away],
+    )
+
+    def total(away, kept):
+        return (kept + swap(away, "tp", 1).astype(WIDE)).astype(LOW)
+
+    def through(rows, after):
         count = rows[0].shape[0]
         away, kept = call(
             functools.partial(expert, len(rows) - 1),
@@ -267,24 +324,23 @@
             [*rows, weight_first, weight_second],
             [pltpu.VMEM((count, units), LOW)],
             flops=4 * count * model_width * units,
+            after=after,
         )
-        return (kept + swap(away, "tp", 1).astype(WIDE)).astype(LOW)
-
-    far = {k: swap(far_rows[k - 2], "exp", k) for k in range(experts - 1, 1, -1)}
-    near = swap(near_rows, "exp", 1)
-    returned = {0: through([own_rows]), 1: swap(through([near]), "exp", 1)}
-    middle = max(2, experts // 2 + 1)
-    for group in (range(experts - 1, middle - 1, -1), range(middle - 1, 1, -1)):
-        group = list(group)
+        return total(away, kept)
+
+    returned = {0: total(own_away, own_kept), 1: swap(through([near], []), "exp", 1)}
+    for group in groups[::-1]:
         if not group:
             continue
         if len(group) == 1:
             mine = far[group[0]]
         else:
             mine = jnp.concatenate([far[k] for k in group], axis=0)
-        total = through([mine, swap(mine, "tp", 1)])
+        if group is groups[1]:
+            mine = call(idle, [], [], after=[own_away], held=[mine])[0]
+        mixed = through([mine, swap(mine, "tp", 1)], [high])
         for i, k in enumerate(group):
-            block = total if len(group) == 1 else total[i * capacity : (i + 1) * capacity]
+            block = mixed if len(group) == 1 else mixed[i * capacity : (i + 1) * capacity]
             returned[k] = swap(block, "exp", k)
 
     hidden_half = call(
@@ -294,22 +350,18 @@
         flops=4 * 3 * token_count * token_count * half,
     )[0]
 
+    first = hidden_half
+    for i in range(1, sections // 2):
+        moved = lax.ppermute(hidden_half, "sec", [(0, 2 * i)])
+        first = jnp.where(sec == 2 * i, moved, first)
+    for i in range(sections // 2 - 1, -1, -1):
+        pairs = [(t, (2 * i + 1) * tp_size + (t ^ 1)) for t in range(tp_size)]
+        moved = lax.ppermute(hidden_half, ("sec", "tp"), pairs)
+        first = jnp.where(sec == 2 * i + 1, moved, first)
     hidden_other = swap(hidden_half, "tp", 1)
-    mine = hidden_half
-    other = hidden_other
-    step = sections // 2
-    while step >= 2:
-        pairs = [(i, i + step) for i in range(0, sections, 2 * step)]
-        mine = jnp.where(sec % (2 * step) == step, lax.ppermute(mine, "sec", pairs), mine)
-        step //= 2
-    if sections > 2:
-        pairs = []
-        for i in range(2, sections, 2):
-            pairs += [(i * tp_size + t, i * tp_size + (t ^ 1)) for t in range(tp_size)]
-        other = jnp.where(sec >= 2, lax.ppermute(mine, ("sec", "tp"), pairs), other)
-    beside = [(i, i + 1) for i in range(0, sections, 2)]
-    mine = jnp.where(sec % 2 == 1, lax.ppermute(mine, "sec", beside), mine)
-    other = jnp.where(sec % 2 == 1, lax.ppermute(other, "sec", beside), other)
+    beside = swap(first, "sec", 1)
+    mine = jnp.where(sec % 2 == 0, first, beside)
+    other = jnp.where(sec % 2 == 0, beside, first)
 
     local_width = query_weight.shape[2]
     queries = call(

time: 95.6 us -> 88.1 us (0.922)
  starting transfers between devices: 43.4 us -> 38.3 us
  local copies, waits for them, and re-layouts: 7.29 us -> 4.36 us
  Pallas kernels: 11 us -> 13.7 us
  waiting for transfers between devices: 31.7 us -> 29.5 us
    ppermute x3, starting transfers between devices: 9.73 us -> 5.48 us  [shards(): total = total + lax.ppermute(blocks[k], ('sec', 'tp'), pairs).astype(WIDE)]
    unnamed x28 -> x24, local copies, waits for them, and re-layouts: 7.29 us -> 4.36 us
    pallas_call x10 -> x11, Pallas kernels: 11 us -> 13.7 us  [call(): pl.pallas_call(run, out_shape=[*out_shape, *(shape_of(x.shape, x.dtype) f...]
    ppermute x4 -> x3, waiting for transfers between devices: 4.12 us -> 1.59 us  [the longest x1 1.59 us: shards(): moved = lax.ppermute(hidden_half, 'sec', [(0, 2 * i)])]
    ppermute x4 -> x3, starting transfers between devices: 6.84 us -> 5.46 us  [the longest x1 2.85 us: shards(): moved = lax.ppermute(hidden_half, 'sec', [(0, 2 * i)])]
    ppermute x14 -> x15, starting transfers between devices: 26.8 us -> 27.3 us  [swap(): return lax.ppermute(block, axis, [(i, i ^ step) for i in range(size)])]
    ppermute x14 -> x15, waiting for transfers between devices: 23.8 us -> 24.2 us  [swap(): return lax.ppermute(block, axis, [(i, i ^ step) for i in range(size)])]
  transfers between devices with their start and end apart: 21 -> 21, of which waited for: 14 -> 10; matrix products, arithmetic and copies ran while one was open for 0% -> 0% of each run, Pallas kernels for 9% -> 13%
where the time goes in v3:
time: 88.1 us; the launch traced here: 87.6 us
  starting transfers between devices  38.3 us (43%)
  waiting for transfers between devices  29.5 us (33%)
  Pallas kernels  13.7 us (16%)
  local copies, waits for them, and re-layouts  4.36 us (5%)
  other arithmetic  0.96 us (1%)
    ppermute x15, starting transfers between devices, swap(): return lax.ppermute(block, axis, [(i, i ^ step) for i in range(size)])  27.3 us
    ppermute x15, waiting for transfers between devices, swap(): return lax.ppermute(block, axis, [(i, i ^ step) for i in range(size)])  24.2 us
    pallas_call x11, Pallas kernels, call(): pl.pallas_call(run, out_shape=[*out_shape, *(shape_of(x.shape, x.dtype) f...  13.7 us
    ppermute x3, starting transfers between devices, shards(): total = total + lax.ppermute(blocks[k], ('sec', 'tp'), pairs).astype(WIDE)  5.48 us
    unnamed x24, local copies, waits for them, and re-layouts  4.36 us
    ppermute x3, waiting for transfers between devices, shards(): total = total + lax.ppermute(blocks[k], ('sec', 'tp'), pairs).astype(WIDE)  3.62 us
    ppermute x1, starting transfers between devices, shards(): moved = lax.ppermute(hidden_half, 'sec', [(0, 2 * i)])  2.85 us
    ppermute x2, starting transfers between devices, shards(): moved = lax.ppermute(hidden_half, ('sec', 'tp'), pairs)  2.61 us
  transfers between devices with their start and end apart: 21, of which 10 were waited for; matrix products, arithmetic and copies ran while one was open for 0% of the time, Pallas kernels for 13%

profile of v3, /device:TPU:0, one launch (start us, length us, event | category | flops | bytes accessed | tf_op | source)
XLA Modules:
  0.0 87.6 jit_solution(3551222487911291734)
XLA Ops:
  0.6 0.0 copy-start.1
  0.6 1.0 %copy-done.1 = bf16[1,256,1024]{2,1,0:T(8,128)(2,1)S(1)} copy-done((bf16[1,256,1024]{2,1,0:T(8,128)(2,1)S(1)}, bf16[1,256,1024]{2,1,0:T(8,128)(2,1)}, u32[]{:S(2)}) %copy-start.1) | copy-done | bytes 524312
  1.7 0.7 copy-done.4
  2.4 0.7 copy-done.10
  3.0 0.9 %shard_map.122 = (bf16[192,512]{1,0:T(8,128)(2,1)S(1)}, bf16[192,512]{1,0:T(8,128)(2,1)S(1)}, bf16[192,1024]{1,0:T(8,128)(2,1)S(1)}, bf16[192,1024]{1,0:T(8,128)(2,1)S(1)}) custom-call(bf16[256,1024]{1,0:T(8,128)(2,1)S(1)} %bitcast.15, s32[2,256]{1,0:T(2,128)S(1)} %bitcast.17, f32[1,1024]{1,0:T(1,128)S(1)} %copy-done.10), custom_call_target="tpu_custom_call" | custom-call | flops 402653184 | bytes 1710080 | tf_op jit(solution)/shard_map/pallas_call | solution.py:40
  3.9 3.1 %collective-permute-start.1 = (bf16[192,1024]{1,0:T(8,128)(2,1)S(1)}, bf16[192,1024]{1,0:T(8,128)(2,1)S(1)}, u32[]{:S(2)}, u32[]{:S(2)}) collective-permute-start(bf16[192,1024]{1,0:T(8,128)(2,1)S(1)} %get-tuple-element.30), channel_id=1, source_target_pairs={{0,2},{2,0},{4,6},{6,4},{1,3},{3,1},{5,7},{7,5},{8,10},{10,8},{12,... | collective-permute-start | bytes 1179656 | tf_op jit(solution)/shard_map/ppermute | solution.py:250
  7.0 2.6 %collective-permute-start.4 = (bf16[192,512]{1,0:T(8,128)(2,1)S(1)}, bf16[192,512]{1,0:T(8,128)(2,1)S(1)}, u32[]{:S(2)}, u32[]{:S(2)}) collective-permute-start(bf16[192,512]{1,0:T(8,128)(2,1)S(1)} %get-tuple-element.35), channel_id=1, source_target_pairs={{0,4},{2,6},{4,0},{6,2},{1,5},{3,7},{5,1},{7,3},{8,12},{10,14},{12... | collective-permute-start | bytes 589832 | tf_op jit(solution)/shard_map/ppermute | solution.py:250
  9.6 4.6 %shard_map.123 = (bf16[192,512]{1,0:T(8,128)(2,1)S(1)}, f32[192,512]{1,0:T(8,128)S(1)}, bf16[1024,2048]{1,0:T(8,128)(2,1)S(1)}, bf16[2048,1024]{1,0:T(8,128)(2,1)S(1)}) custom-call(bf16[192,1024]{1,0:T(8,128)(2,1)S(1)} %get-tuple-element.25.refs_0_, bf16[1024,2048]{1,0:T(8,128)(2,1)} %bitcast.23, bf16[2048,1024]{1,0:T(8,128)(2,1)} %bitcast.24), custom_call_target="tpu_custom_call" | custom-call | flops 1610612736 | bytes 17760256 | tf_op jit(solution)/shard_map/pallas_call | solution.py:40
  14.2 6.6 %collective-permute-done.4.refs_1_ = bf16[192,512]{1,0:T(8,128)(2,1)S(1)} collective-permute-done((bf16[192,512]{1,0:T(8,128)(2,1)S(1)}, bf16[192,512]{1,0:T(8,128)(2,1)S(1)}, u32[]{:S(2)}, u32[]{:S(2)}) %collective-permute-start.4) | collective-permute-done | bytes 196640 | tf_op jit(solution)/shard_map/ppermute | solution.py:250
  20.8 1.5 %collective-permute-start.5 = (bf16[192,512]{1,0:T(8,128)(2,1)S(1)}, bf16[192,512]{1,0:T(8,128)(2,1)S(1)}, u32[]{:S(2)}, u32[]{:S(2)}) collective-permute-start(bf16[192,512]{1,0:T(8,128)(2,1)S(1)} %shard_map.126.refs_0_), channel_id=1, source_target_pairs={{0,1},{1,0},{2,3},{3,2},{4,5},{5,4},{6,7},{7,6},{8,9},{9,8},{10,11... | collective-permute-start | bytes 589832 | tf_op jit(solution)/shard_map/ppermute | solution.py:250
  22.3 0.5 collective-permute-start
  22.8 0.6 shard_map.124
  23.4 3.4 %collective-permute-done.8.refs_0_ = bf16[192,512]{1,0:T(8,128)(2,1)S(1)} collective-permute-done((bf16[192,512]{1,0:T(8,128)(2,1)S(1)}, bf16[192,512]{1,0:T(8,128)(2,1)S(1)}, u32[]{:S(2)}, u32[]{:S(2)}) %collective-permute-start.8) | collective-permute-done | bytes 196640 | tf_op jit(solution)/shard_map/ppermute | solution.py:250
  26.9 1.5 %collective-permute-start.9 = (bf16[192,512]{1,0:T(8,128)(2,1)S(1)}, bf16[192,512]{1,0:T(8,128)(2,1)S(1)}, u32[]{:S(2)}, u32[]{:S(2)}) collective-permute-start(bf16[192,512]{1,0:T(8,128)(2,1)S(1)} %collective-permute-done.8.refs_0_), channel_id=1, source_target_pairs={{0,1},{1,0},{2,3},{3,2},{4,5},{5,4},{6,7},{7,6},{8,9},{9,8},{10,11... | collective-permute-start | bytes 589832 | tf_op jit(solution)/shard_map/ppermute | solution.py:250
  28.4 1.8 %shard_map.125 = (bf16[192,512]{1,0:T(8,128)(2,1)S(1)}, f32[192,512]{1,0:T(8,128)S(1)}) custom-call(bf16[192,1024]{1,0:T(8,128)(2,1)S(1)} %collective-permute-done.1.refs_0_, bf16[1024,2048]{1,0:T(8,128)(2,1)S(1)} %get-tuple-element.31.refs_1_.refs_2_, bf16[2048,1024]{1,0:T(8,128)(2,1)S(1)} %get-tuple-element.32.refs_2_.refs_3_), custom_call_target="tpu_custom_call" | custom-call | flops 1610612736 | bytes 9371648 | tf_op jit(solution)/shard_map/pallas_call | solution.py:40
  30.2 0.6 collective-permute-start.2
  30.8 1.8 %shard_map.127 = (bf16[192,512]{1,0:T(8,128)(2,1)S(1)}, f32[192,512]{1,0:T(8,128)S(1)}) custom-call(bf16[192,512]{1,0:T(8,128)(2,1)S(1)} %shard_map.126.refs_0_, bf16[192,512]{1,0:T(8,128)(2,1)S(1)} %collective-permute-done.5.refs_1_, bf16[1024,2048]{1,0:T(8,128)(2,1)S(1)} %get-tuple-element.31.refs_1_.refs_2_, ...), custom_call_target="tpu_custom_call" | custom-call | flops 1610612736 | bytes 9371648 | tf_op jit(solution)/shard_map/pallas_call | solution.py:40
  32.6 1.6 %collective-permute-start.6 = (bf16[192,512]{1,0:T(8,128)(2,1)S(1)}, bf16[192,512]{1,0:T(8,128)(2,1)S(1)}, u32[]{:S(2)}, u32[]{:S(2)}) collective-permute-start(bf16[192,512]{1,0:T(8,128)(2,1)S(1)} %get-tuple-element.37), channel_id=1, source_target_pairs={{0,1},{1,0},{2,3},{3,2},{4,5},{5,4},{6,7},{7,6},{8,9},{9,8},{10,11... | collective-permute-start | bytes 589832 | tf_op jit(solution)/shard_map/ppermute | solution.py:250
  34.2 0.9 collective-permute-done.9.refs_1_
  35.1 1.8 %shard_map.128 = (bf16[192,512]{1,0:T(8,128)(2,1)S(1)}, f32[192,512]{1,0:T(8,128)S(1)}) custom-call(bf16[192,512]{1,0:T(8,128)(2,1)S(1)} %collective-permute-done.8.refs_0_, bf16[192,512]{1,0:T(8,128)(2,1)S(1)} %collective-permute-done.9.refs_1_, bf16[1024,2048]{1,0:T(8,128)(2,1)S(1)} %get-tuple-element.31.refs_1_.refs_2_, ...), custom_call_target="tpu_custom_call" | custom-call | flops 1610612736 | bytes 9371648 | tf_op jit(solution)/shard_map/pallas_call | solution.py:40
  36.9 0.0 copy-start.3
  36.9 1.6 %collective-permute-start.10 = (bf16[192,512]{1,0:T(8,128)(2,1)S(1)}, bf16[192,512]{1,0:T(8,128)(2,1)S(1)}, u32[]{:S(2)}, u32[]{:S(2)}) collective-permute-start(bf16[192,512]{1,0:T(8,128)(2,1)S(1)} %get-tuple-element.40), channel_id=1, source_target_pairs={{0,1},{1,0},{2,3},{3,2},{4,5},{5,4},{6,7},{7,6},{8,9},{9,8},{10,11... | collective-permute-start | bytes 589832 | tf_op jit(solution)/shard_map/ppermute | solution.py:250
  38.5 0.8 collective-permute-done.2
  39.3 5.6 %collective-permute-start.3 = (bf16[192,512]{1,0:T(8,128)(2,1)S(1)}, bf16[192,512]{1,0:T(8,128)(2,1)S(1)}, u32[]{:S(2)}, u32[]{:S(2)}) collective-permute-start(bf16[192,512]{1,0:T(8,128)(2,1)S(1)} %add_convert_fusion.2), channel_id=1, source_target_pairs={{0,2},{2,0},{4,6},{6,4},{1,3},{3,1},{5,7},{7,5},{8,10},{10,8},{12,... | collective-permute-start | bytes 589832 | tf_op jit(solution)/shard_map/ppermute | solution.py:250
  45.0 2.9 %collective-permute-start.7 = (bf16[192,512]{1,0:T(8,128)(2,1)S(1)}, bf16[192,512]{1,0:T(8,128)(2,1)S(1)}, u32[]{:S(2)}, u32[]{:S(2)}) collective-permute-start(bf16[192,512]{1,0:T(8,128)(2,1)S(1)} %add_convert_fusion.1), channel_id=1, source_target_pairs={{0,4},{2,6},{4,0},{6,2},{1,5},{3,7},{5,1},{7,3},{8,12},{10,14},{12... | collective-permute-start | bytes 589832 | tf_op jit(solution)/shard_map/ppermute | solution.py:250
  47.9 2.5 %collective-permute-start.11 = (bf16[192,512]{1,0:T(8,128)(2,1)S(1)}, bf16[192,512]{1,0:T(8,128)(2,1)S(1)}, u32[]{:S(2)}, u32[]{:S(2)}) collective-permute-start(bf16[192,512]{1,0:T(8,128)(2,1)S(1)} %add_convert_fusion), channel_id=1, source_target_pairs={{0,6},{2,4},{4,2},{6,0},{1,7},{3,5},{5,3},{7,1},{8,14},{10,12},{12... | collective-permute-start | bytes 589832 | tf_op jit(solution)/shard_map/ppermute | solution.py:250
  50.5 9.0 %collective-permute-done.7.refs_5_ = bf16[192,512]{1,0:T(8,128)(2,1)S(1)} collective-permute-done((bf16[192,512]{1,0:T(8,128)(2,1)S(1)}, bf16[192,512]{1,0:T(8,128)(2,1)S(1)}, u32[]{:S(2)}, u32[]{:S(2)}) %collective-permute-start.7) | collective-permute-done | bytes 196640 | tf_op jit(solution)/shard_map/ppermute | solution.py:250
  59.6 0.7 shard_map.129.refs_0_.refs_6_
  60.3 1.3 %collective-permute-start.12 = (bf16[256,512]{1,0:T(8,128)(2,1)S(1)}, bf16[256,512]{1,0:T(8,128)(2,1)S(1)}, u32[]{:S(2)}, u32[]{:S(2)}) collective-permute-start(bf16[256,512]{1,0:T(8,128)(2,1)S(1)} %shard_map.129.refs_0_.refs_6_), channel_id=1, source_target_pairs={{0,9},{1,8},{2,11},{3,10},{4,13},{5,12},{6,15},{7,14}} | collective-permute-start | bytes 786440 | tf_op jit(solution)/shard_map/ppermute | solution.py:359
  61.6 1.3 %collective-permute-start.13 = (bf16[256,512]{1,0:T(8,128)(2,1)S(1)}, bf16[256,512]{1,0:T(8,128)(2,1)S(1)}, u32[]{:S(2)}, u32[]{:S(2)}) collective-permute-start(bf16[256,512]{1,0:T(8,128)(2,1)S(1)} %shard_map.129.refs_0_.refs_6_), channel_id=1, source_target_pairs={{0,25},{1,24},{2,27},{3,26},{4,29},{5,28},{6,31},{7,30}} | collective-permute-start | bytes 786440 | tf_op jit(solution)/shard_map/ppermute | solution.py:359
  62.9 2.9 %collective-permute-start.14 = (bf16[256,512]{1,0:T(8,128)(2,1)S(1)}, bf16[256,512]{1,0:T(8,128)(2,1)}, u32[]{:S(2)}, u32[]{:S(2)}) collective-permute-start(bf16[256,512]{1,0:T(8,128)(2,1)S(1)} %shard_map.129.refs_0_.refs_6_), channel_id=1, source_target_pairs={{0,16},{1,17},{2,18},{3,19},{4,20},{5,21},{6,22},{7,23}} | collective-permute-start | bytes 786440 | tf_op jit(solution)/shard_map/ppermute | solution.py:355
  65.8 1.5 %collective-permute-start.16 = (bf16[256,512]{1,0:T(8,128)(2,1)S(1)}, bf16[256,512]{1,0:T(8,128)(2,1)S(1)}, u32[]{:S(2)}, u32[]{:S(2)}) collective-permute-start(bf16[256,512]{1,0:T(8,128)(2,1)S(1)} %shard_map.129.refs_0_.refs_6_), channel_id=1, source_target_pairs={{0,1},{1,0},{2,3},{3,2},{4,5},{5,4},{6,7},{7,6},{8,9},{9,8},{10,11... | collective-permute-start | bytes 786440 | tf_op jit(solution)/shard_map/ppermute | solution.py:250
  67.3 0.7 copy-done.11
  68.0 1.6 %collective-permute-done.14 = bf16[256,512]{1,0:T(8,128)(2,1)} collective-permute-done((bf16[256,512]{1,0:T(8,128)(2,1)S(1)}, bf16[256,512]{1,0:T(8,128)(2,1)}, u32[]{:S(2)}, u32[]{:S(2)}) %collective-permute-start.14) | collective-permute-done | bytes 262176 | tf_op jit(solution)/shard_map/ppermute | solution.py:355
  69.6 0.1 select_select_fusion
  69.7 0.1 collective-permute-start.15
  69.8 2.4 %collective-permute-done.16.refs_1_ = bf16[256,512]{1,0:T(8,128)(2,1)S(1)} collective-permute-done((bf16[256,512]{1,0:T(8,128)(2,1)S(1)}, bf16[256,512]{1,0:T(8,128)(2,1)S(1)}, u32[]{:S(2)}, u32[]{:S(2)}) %collective-permute-start.16) | collective-permute-done | bytes 262176 | tf_op jit(solution)/shard_map/ppermute | solution.py:250
  72.1 0.7 shard_map.130.refs_2_
  72.9 1.2 %copy-done.8 = bf16[1,1024,512]{2,1,0:T(8,128)(2,1)S(1)} copy-done((bf16[1,1024,512]{2,1,0:T(8,128)(2,1)S(1)}, bf16[1,1024,512]{2,1,0:T(8,128)(2,1)}, u32[]{:S(2)}) %copy-start.8) | copy-done | bytes 1048600
  74.1 0.8 shard_map.131
  74.9 1.7 %collective-permute-start.17 = (bf16[256,512]{1,0:T(8,128)(2,1)S(1)}, bf16[256,512]{1,0:T(8,128)(2,1)S(1)}, u32[]{:S(2)}, u32[]{:S(2)}) collective-permute-start(bf16[256,512]{1,0:T(8,128)(2,1)S(1)} %get-tuple-element.43), channel_id=1, source_target_pairs={{0,8},{8,0},{16,24},{24,16},{1,9},{9,1},{17,25},{25,17},{2,10},{10... | collective-permute-start | bytes 786440 | tf_op jit(solution)/shard_map/ppermute | solution.py:250
  76.6 1.2 %collective-permute-done.17.refs_1_ = bf16[256,512]{1,0:T(8,128)(2,1)S(1)} collective-permute-done((bf16[256,512]{1,0:T(8,128)(2,1)S(1)}, bf16[256,512]{1,0:T(8,128)(2,1)S(1)}, u32[]{:S(2)}, u32[]{:S(2)}) %collective-permute-start.17) | collective-permute-done | bytes 262176 | tf_op jit(solution)/shard_map/ppermute | solution.py:250
  77.7 0.1 shard_map.132
  77.8 4.8 %collective-permute-start.20 = (bf16[256,128]{1,0:T(8,128)(2,1)S(1)}, bf16[256,128]{1,0:T(8,128)(2,1)S(1)}, u32[]{:S(2)}, u32[]{:S(2)}) collective-permute-start(bf16[256,128]{1,0:T(8,128)(2,1)S(1)} %get-tuple-element.47), channel_id=1, source_target_pairs={{0,17},{1,16},{8,25},{9,24},{16,1},{17,0},{24,9},{25,8},{2,19},{3,... | collective-permute-start | bytes 196616 | tf_op jit(solution)/shard_map/ppermute | solution.py:400
  82.7 0.6 collective-permute-start.18
  83.3 1.8 %collective-permute-done.20 = bf16[256,128]{1,0:T(8,128)(2,1)S(1)} collective-permute-done((bf16[256,128]{1,0:T(8,128)(2,1)S(1)}, bf16[256,128]{1,0:T(8,128)(2,1)S(1)}, u32[]{:S(2)}, u32[]{:S(2)}) %collective-permute-start.20) | collective-permute-done | bytes 65568 | tf_op jit(solution)/shard_map/ppermute | solution.py:400
  85.1 1.8 %collective-permute-done.19 = bf16[256,128]{1,0:T(8,128)(2,1)S(1)} collective-permute-done((bf16[256,128]{1,0:T(8,128)(2,1)S(1)}, bf16[256,128]{1,0:T(8,128)(2,1)S(1)}, u32[]{:S(2)}, u32[]{:S(2)}) %collective-permute-start.19) | collective-permute-done | bytes 65568 | tf_op jit(solution)/shard_map/ppermute | solution.py:400
  86.9 0.7 add_convert_fusion.4
  (36 shorter events, 0.3 us)
Async XLA Ops:
  0.6 1.0 %copy-start.1 = (bf16[1,256,1024]{2,1,0:T(8,128)(2,1)S(1)}, bf16[1,256,1024]{2,1,0:T(8,128)(2,1)}, u32[]{:S(2)}) copy-start(bf16[1,256,1024]{2,1,0:T(8,128)(2,1)} %param.11) | copy-start | bytes 1572868
  1.7 0.7 copy-start.4
  2.4 0.7 copy-start.10
  3.9 24.5 %collective-permute-start.1 = (bf16[192,1024]{1,0:T(8,128)(2,1)S(1)}, bf16[192,1024]{1,0:T(8,128)(2,1)S(1)}, u32[]{:S(2)}, u32[]{:S(2)}) collective-permute-start(bf16[192,1024]{1,0:T(8,128)(2,1)S(1)} %get-tuple-element.30), channel_id=1, source_target_pairs={{0,2},{2,0},{4,6},{6,4},{1,3},{3,1},{5,7},{7,5},{8,10},{10,8},{12,... | collective-permute-start | bytes 1179656 | tf_op jit(solution)/shard_map/ppermute | solution.py:250
  7.0 13.8 %collective-permute-start.4 = (bf16[192,512]{1,0:T(8,128)(2,1)S(1)}, bf16[192,512]{1,0:T(8,128)(2,1)S(1)}, u32[]{:S(2)}, u32[]{:S(2)}) collective-permute-start(bf16[192,512]{1,0:T(8,128)(2,1)S(1)} %get-tuple-element.35), channel_id=1, source_target_pairs={{0,4},{2,6},{4,0},{6,2},{1,5},{3,7},{5,1},{7,3},{8,12},{10,14},{12... | collective-permute-start | bytes 589832 | tf_op jit(solution)/shard_map/ppermute | solution.py:250
  9.6 17.2 %collective-permute-start.8 = (bf16[192,512]{1,0:T(8,128)(2,1)S(1)}, bf16[192,512]{1,0:T(8,128)(2,1)S(1)}, u32[]{:S(2)}, u32[]{:S(2)}) collective-permute-start(bf16[192,512]{1,0:T(8,128)(2,1)S(1)} %get-tuple-element.38), channel_id=1, source_target_pairs={{0,6},{2,4},{4,2},{6,0},{1,7},{3,5},{5,3},{7,1},{8,14},{10,12},{12... | collective-permute-start | bytes 589832 | tf_op jit(solution)/shard_map/ppermute | solution.py:250
  9.6 13.2 %copy-start.5 = (s32[1,256,2]{1,2,0:T(2,128)S(1)}, s32[1,256,2]{1,2,0:T(2,128)}, u32[]{:S(2)}) copy-start(s32[1,256,2]{1,2,0:T(2,128)} %param.12) | copy-start | bytes 6148
  9.6 13.2 %copy-start.6 = (f32[1,256,2]{1,2,0:T(2,128)S(1)}, f32[1,256,2]{1,2,0:T(2,128)}, u32[]{:S(2)}) copy-start(f32[1,256,2]{1,2,0:T(2,128)} %param.13) | copy-start | bytes 6148
  20.8 10.0 %collective-permute-start.5 = (bf16[192,512]{1,0:T(8,128)(2,1)S(1)}, bf16[192,512]{1,0:T(8,128)(2,1)S(1)}, u32[]{:S(2)}, u32[]{:S(2)}) collective-permute-start(bf16[192,512]{1,0:T(8,128)(2,1)S(1)} %shard_map.126.refs_0_), channel_id=1, source_target_pairs={{0,1},{1,0},{2,3},{3,2},{4,5},{5,4},{6,7},{7,6},{8,9},{9,8},{10,11... | collective-permute-start | bytes 589832 | tf_op jit(solution)/shard_map/ppermute | solution.py:250
  22.3 28.1 %collective-permute-start = (bf16[192,512]{1,0:T(8,128)(2,1)S(1)}, bf16[192,512]{1,0:T(8,128)(2,1)S(1)}, u32[]{:S(2)}, u32[]{:S(2)}) collective-permute-start(bf16[192,512]{1,0:T(8,128)(2,1)S(1)} %get-tuple-element.26.refs_2_.refs_0_), channel_id=1, source_target_pairs={{0,1},{1,0},{2,3},{3,2},{4,5},{5,4},{6,7},{7,6},{8,9},{9,8},{10,11... | collective-permute-start | bytes 589832 | tf_op jit(solution)/shard_map/ppermute | solution.py:250
  26.9 8.2 %collective-permute-start.9 = (bf16[192,512]{1,0:T(8,128)(2,1)S(1)}, bf16[192,512]{1,0:T(8,128)(2,1)S(1)}, u32[]{:S(2)}, u32[]{:S(2)}) collective-permute-start(bf16[192,512]{1,0:T(8,128)(2,1)S(1)} %collective-permute-done.8.refs_0_), channel_id=1, source_target_pairs={{0,1},{1,0},{2,3},{3,2},{4,5},{5,4},{6,7},{7,6},{8,9},{9,8},{10,11... | collective-permute-start | bytes 589832 | tf_op jit(solution)/shard_map/ppermute | solution.py:250
  30.2 9.1 %collective-permute-start.2 = (bf16[192,512]{1,0:T(8,128)(2,1)S(1)}, bf16[192,512]{1,0:T(8,128)(2,1)S(1)}, u32[]{:S(2)}, u32[]{:S(2)}) collective-permute-start(bf16[192,512]{1,0:T(8,128)(2,1)S(1)} %get-tuple-element.34), channel_id=1, source_target_pairs={{0,1},{1,0},{2,3},{3,2},{4,5},{5,4},{6,7},{7,6},{8,9},{9,8},{10,11... | collective-permute-start | bytes 589832 | tf_op jit(solution)/shard_map/ppermute | solution.py:250
  32.6 27.0 %copy-start.2 = (bf16[1,256,1024]{2,1,0:T(8,128)(2,1)S(1)}, bf16[1,256,1024]{2,1,0:T(8,128)(2,1)}, u32[]{:S(2)}) copy-start(bf16[1,256,1024]{2,1,0:T(8,128)(2,1)} %param.11) | copy-start | bytes 1572868
  32.6 12.3 %collective-permute-start.6 = (bf16[192,512]{1,0:T(8,128)(2,1)S(1)}, bf16[192,512]{1,0:T(8,128)(2,1)S(1)}, u32[]{:S(2)}, u32[]{:S(2)}) collective-permute-start(bf16[192,512]{1,0:T(8,128)(2,1)S(1)} %get-tuple-element.37), channel_id=1, source_target_pairs={{0,1},{1,0},{2,3},{3,2},{4,5},{5,4},{6,7},{7,6},{8,9},{9,8},{10,11... | collective-permute-start | bytes 589832 | tf_op jit(solution)/shard_map/ppermute | solution.py:250
  36.9 35.2 %copy-start = (bf16[1,1024,512]{2,1,0:T(8,128)(2,1)S(1)}, bf16[1,1024,512]{2,1,0:T(8,128)(2,1)}, u32[]{:S(2)}) copy-start(bf16[1,1024,512]{2,1,0:T(8,128)(2,1)} %param.18) | copy-start | bytes 3145732
  36.9 35.2 %copy-start.3 = (f32[1,1024]{1,0:T(1,128)S(1)}, f32[1,1024]{1,0:T(1,128)}, u32[]{:S(2)}) copy-start(f32[1,1024]{1,0:T(1,128)} %refs_2_.3) | copy-start | bytes 12292
  36.9 11.0 %collective-permute-start.10 = (bf16[192,512]{1,0:T(8,128)(2,1)S(1)}, bf16[192,512]{1,0:T(8,128)(2,1)S(1)}, u32[]{:S(2)}, u32[]{:S(2)}) collective-permute-start(bf16[192,512]{1,0:T(8,128)(2,1)S(1)} %get-tuple-element.40), channel_id=1, source_target_pairs={{0,1},{1,0},{2,3},{3,2},{4,5},{5,4},{6,7},{7,6},{8,9},{9,8},{10,11... | collective-permute-start | bytes 589832 | tf_op jit(solution)/shard_map/ppermute | solution.py:250
  39.3 11.2 %collective-permute-start.3 = (bf16[192,512]{1,0:T(8,128)(2,1)S(1)}, bf16[192,512]{1,0:T(8,128)(2,1)S(1)}, u32[]{:S(2)}, u32[]{:S(2)}) collective-permute-start(bf16[192,512]{1,0:T(8,128)(2,1)S(1)} %add_convert_fusion.2), channel_id=1, source_target_pairs={{0,2},{2,0},{4,6},{6,4},{1,3},{3,1},{5,7},{7,5},{8,10},{10,8},{12,... | collective-permute-start | bytes 589832 | tf_op jit(solution)/shard_map/ppermute | solution.py:250
  45.0 14.6 %collective-permute-start.7 = (bf16[192,512]{1,0:T(8,128)(2,1)S(1)}, bf16[192,512]{1,0:T(8,128)(2,1)S(1)}, u32[]{:S(2)}, u32[]{:S(2)}) collective-permute-start(bf16[192,512]{1,0:T(8,128)(2,1)S(1)} %add_convert_fusion.1), channel_id=1, source_target_pairs={{0,4},{2,6},{4,0},{6,2},{1,5},{3,7},{5,1},{7,3},{8,12},{10,14},{12... | collective-permute-start | bytes 589832 | tf_op jit(solution)/shard_map/ppermute | solution.py:250
  47.9 25.0 %copy-start.7 = (bf16[1,1024,512]{2,1,0:T(8,128)(2,1)S(1)}, bf16[1,1024,512]{2,1,0:T(8,128)(2,1)}, u32[]{:S(2)}) copy-start(bf16[1,1024,512]{2,1,0:T(8,128)(2,1)} %param.19) | copy-start | bytes 3145732
  47.9 25.0 %copy-start.9 = (bf16[1,256,512]{2,1,0:T(8,128)(2,1)S(1)}, bf16[1,256,512]{2,1,0:T(8,128)(2,1)}, u32[]{:S(2)}) copy-start(bf16[1,256,512]{2,1,0:T(8,128)(2,1)} %param.21) | copy-start | bytes 786436
  47.9 11.7 %collective-permute-start.11 = (bf16[192,512]{1,0:T(8,128)(2,1)S(1)}, bf16[192,512]{1,0:T(8,128)(2,1)S(1)}, u32[]{:S(2)}, u32[]{:S(2)}) collective-permute-start(bf16[192,512]{1,0:T(8,128)(2,1)S(1)} %add_convert_fusion), channel_id=1, source_target_pairs={{0,6},{2,4},{4,2},{6,0},{1,7},{3,5},{5,3},{7,1},{8,14},{10,12},{12... | collective-permute-start | bytes 589832 | tf_op jit(solution)/shard_map/ppermute | solution.py:250
  60.3 7.0 %collective-permute-start.12 = (bf16[256,512]{1,0:T(8,128)(2,1)S(1)}, bf16[256,512]{1,0:T(8,128)(2,1)S(1)}, u32[]{:S(2)}, u32[]{:S(2)}) collective-permute-start(bf16[256,512]{1,0:T(8,128)(2,1)S(1)} %shard_map.129.refs_0_.refs_6_), channel_id=1, source_target_pairs={{0,9},{1,8},{2,11},{3,10},{4,13},{5,12},{6,15},{7,14}} | collective-permute-start | bytes 786440 | tf_op jit(solution)/shard_map/ppermute | solution.py:359
  61.6 5.7 %collective-permute-start.13 = (bf16[256,512]{1,0:T(8,128)(2,1)S(1)}, bf16[256,512]{1,0:T(8,128)(2,1)S(1)}, u32[]{:S(2)}, u32[]{:S(2)}) collective-permute-start(bf16[256,512]{1,0:T(8,128)(2,1)S(1)} %shard_map.129.refs_0_.refs_6_), channel_id=1, source_target_pairs={{0,25},{1,24},{2,27},{3,26},{4,29},{5,28},{6,31},{7,30}} | collective-permute-start | bytes 786440 | tf_op jit(solution)/shard_map/ppermute | solution.py:359
  62.9 6.7 %collective-permute-start.14 = (bf16[256,512]{1,0:T(8,128)(2,1)S(1)}, bf16[256,512]{1,0:T(8,128)(2,1)}, u32[]{:S(2)}, u32[]{:S(2)}) collective-permute-start(bf16[256,512]{1,0:T(8,128)(2,1)S(1)} %shard_map.129.refs_0_.refs_6_), channel_id=1, source_target_pairs={{0,16},{1,17},{2,18},{3,19},{4,20},{5,21},{6,22},{7,23}} | collective-permute-start | bytes 786440 | tf_op jit(solution)/shard_map/ppermute | solution.py:355
  65.8 6.4 %collective-permute-start.16 = (bf16[256,512]{1,0:T(8,128)(2,1)S(1)}, bf16[256,512]{1,0:T(8,128)(2,1)S(1)}, u32[]{:S(2)}, u32[]{:S(2)}) collective-permute-start(bf16[256,512]{1,0:T(8,128)(2,1)S(1)} %shard_map.129.refs_0_.refs_6_), channel_id=1, source_target_pairs={{0,1},{1,0},{2,3},{3,2},{4,5},{5,4},{6,7},{7,6},{8,9},{9,8},{10,11... | collective-permute-start | bytes 786440 | tf_op jit(solution)/shard_map/ppermute | solution.py:250
  67.3 0.7 copy-start.11
  69.7 3.2 %collective-permute-start.15 = (bf16[256,512]{1,0:T(8,128)(2,1)S(1)}, bf16[256,512]{1,0:T(8,128)(2,1)S(1)}, u32[]{:S(2)}, u32[]{:S(2)}) collective-permute-start(bf16[256,512]{1,0:T(8,128)(2,1)S(1)} %select_select_fusion), channel_id=1, source_target_pairs={{0,8},{8,0},{16,24},{24,16},{1,9},{9,1},{17,25},{25,17},{2,10},{10... | collective-permute-start | bytes 786440 | tf_op jit(solution)/shard_map/ppermute | solution.py:250
  72.9 1.2 %copy-start.8 = (bf16[1,1024,512]{2,1,0:T(8,128)(2,1)S(1)}, bf16[1,1024,512]{2,1,0:T(8,128)(2,1)}, u32[]{:S(2)}) copy-start(bf16[1,1024,512]{2,1,0:T(8,128)(2,1)} %param.20) | copy-start | bytes 3145732
  74.9 2.8 %collective-permute-start.17 = (bf16[256,512]{1,0:T(8,128)(2,1)S(1)}, bf16[256,512]{1,0:T(8,128)(2,1)S(1)}, u32[]{:S(2)}, u32[]{:S(2)}) collective-permute-start(bf16[256,512]{1,0:T(8,128)(2,1)S(1)} %get-tuple-element.43), channel_id=1, source_target_pairs={{0,8},{8,0},{16,24},{24,16},{1,9},{9,1},{17,25},{25,17},{2,10},{10... | collective-permute-start | bytes 786440 | tf_op jit(solution)/shard_map/ppermute | solution.py:250
  77.8 7.3 %collective-permute-start.20 = (bf16[256,128]{1,0:T(8,128)(2,1)S(1)}, bf16[256,128]{1,0:T(8,128)(2,1)S(1)}, u32[]{:S(2)}, u32[]{:S(2)}) collective-permute-start(bf16[256,128]{1,0:T(8,128)(2,1)S(1)} %get-tuple-element.47), channel_id=1, source_target_pairs={{0,17},{1,16},{8,25},{9,24},{16,1},{17,0},{24,9},{25,8},{2,19},{3,... | collective-permute-start | bytes 196616 | tf_op jit(solution)/shard_map/ppermute | solution.py:400
  82.7 4.3 %collective-permute-start.19 = (bf16[256,128]{1,0:T(8,128)(2,1)S(1)}, bf16[256,128]{1,0:T(8,128)(2,1)S(1)}, u32[]{:S(2)}, u32[]{:S(2)}) collective-permute-start(bf16[256,128]{1,0:T(8,128)(2,1)S(1)} %get-tuple-element.46), channel_id=1, source_target_pairs={{0,16},{1,17},{8,24},{9,25},{16,0},{17,1},{24,8},{25,9},{2,18},{3,... | collective-permute-start | bytes 196616 | tf_op jit(solution)/shard_map/ppermute | solution.py:400
  82.7 4.3 %collective-permute-start.18 = (bf16[256,128]{1,0:T(8,128)(2,1)S(1)}, bf16[256,128]{1,0:T(8,128)(2,1)S(1)}, u32[]{:S(2)}, u32[]{:S(2)}) collective-permute-start(bf16[256,128]{1,0:T(8,128)(2,1)S(1)} %get-tuple-element.45), channel_id=1, source_target_pairs={{0,1},{1,0},{8,9},{9,8},{16,17},{17,16},{24,25},{25,24},{2,3},{3,2... | collective-permute-start | bytes 196616 | tf_op jit(solution)/shard_map/ppermute | solution.py:400

commit v4 on v3

--- a/solution.py
+++ b/solution.py
@@ -278,7 +278,7 @@
     units = weight_first.shape[1]
 
     middle = max(2, experts // 2 + 1)
-    groups = [list(range(experts - 1, middle - 1, -1)), list(range(middle - 1, 1, -1))]
+    groups = [list(range(middle - 1, 1, -1)), list(range(experts - 1, middle - 1, -1))]
     row_half, row_whole = shape_of((capacity, half)), shape_of((capacity, model_width))
     *far_rows, near_rows, own_rows = call(
         functools.partial(prepare, experts),
@@ -287,9 +287,30 @@
         [pltpu.VMEM((token_count, model_width), LOW)],
         flops=2 * 3 * token_count * token_count * model_width,
     )
-    far = {k: swap(far_rows[k - 2], "exp", k) for k in groups[0]}
+    def hold(array, after):
+        return call(idle, [], [], after=after, held=[array])[0]
+
+    def joined(group):
+        blocks = [swap(far_rows[k - 2], "exp", k) for k in group]
+        return blocks[0] if len(blocks) == 1 else jnp.concatenate(blocks, axis=0)
+
+    def total(away, kept):
+        return (kept + swap(away, "tp", 1).astype(WIDE)).astype(LOW)
+
+    def through(rows, after):
+        count = rows[0].shape[0]
+        return call(
+            functools.partial(expert, len(rows) - 1),
+            [shape_of((count, half)), shape_of((count, half), WIDE)],
+            [*rows, weight_first, weight_second],
+            [pltpu.VMEM((count, units), LOW)],
+            flops=4 * count * model_width * units,
+            after=after,
+        )
+
+    arriving = [joined(group) for group in groups]
     loads = max(1, units // 512) + 1
-    own_away, own_kept, weight_first, weight_second = call(
+    own_away, own_kept, weight_first, weight_second, near_rows = call(
         expert_first,
         [
             row_half,
@@ -302,46 +323,30 @@
         flops=4 * capacity * model_width * units,
         remote=(1, 2),
         limit=44,
-
-    )
-    far |= {k: swap(far_rows[k - 2], "exp", k) for k in groups[1]}
+        held=[near_rows],
+    )
     near = swap(near_rows, "exp", 1)
+    returned = {0: total(own_away, own_kept)}
+    arriving[0] = hold(arriving[0], [own_away])
+    others = [swap(arriving[0], "tp", 1)]
     high, low = call(
         functools.partial(mixing, experts),
         [shape_of((experts, token_count, capacity))] * 2,
         [route_rows, gate_rows],
-        after=[own_away],
-    )
-
-    def total(away, kept):
-        return (kept + swap(away, "tp", 1).astype(WIDE)).astype(LOW)
-
-    def through(rows, after):
-        count = rows[0].shape[0]
-        away, kept = call(
-            functools.partial(expert, len(rows) - 1),
-            [shape_of((count, half)), shape_of((count, half), WIDE)],
-            [*rows, weight_first, weight_second],
-            [pltpu.VMEM((count, units), LOW)],
-            flops=4 * count * model_width * units,
-            after=after,
-        )
-        return total(away, kept)
-
-    returned = {0: total(own_away, own_kept), 1: swap(through([near], []), "exp", 1)}
-    for group in groups[::-1]:
-        if not group:
-            continue
-        if len(group) == 1:
-            mine = far[group[0]]
-        else:
-            mine = jnp.concatenate([far[k] for k in group], axis=0)
-        if group is groups[1]:
-            mine = call(idle, [], [], after=[own_away], held=[mine])[0]
-        mixed = through([mine, swap(mine, "tp", 1)], [high])
+        after=[arriving[0]],
+    )
+    arriving[1] = hold(arriving[1], [high])
+    others.append(swap(arriving[1], "tp", 1))
+    results = [through([arriving[0], others[0]], [returned[0], arriving[1]])]
+    near_away, near_kept = through([near], [results[0][0]])
+    results.append(through([arriving[1], others[1]], [near_away]))
+    for group, (away, kept) in zip(groups, results):
+        mixed = total(away, kept)
         for i, k in enumerate(group):
             block = mixed if len(group) == 1 else mixed[i * capacity : (i + 1) * capacity]
             returned[k] = swap(block, "exp", k)
+    near_away = hold(near_away, [results[1][0]])
+    returned[1] = swap(total(near_away, near_kept), "exp", 1)
 
     hidden_half = call(
         functools.partial(combine, experts),

time: 88.1 us -> 86.9 us (0.986)
  starting transfers between devices: 38.3 us -> 34.2 us
  waiting for transfers between devices: 29.5 us -> 32.5 us
    ppermute x15, starting transfers between devices: 27.3 us -> 23.6 us  [swap(): return lax.ppermute(block, axis, [(i, i ^ step) for i in range(size)])]
    ppermute x15, waiting for transfers between devices: 24.2 us -> 26.4 us  [swap(): return lax.ppermute(block, axis, [(i, i ^ step) for i in range(size)])]
    ppermute x2, waiting for transfers between devices: 0.01 us -> 1.87 us  [shards(): moved = lax.ppermute(hidden_half, ('sec', 'tp'), pairs)]
    ppermute x1, waiting for transfers between devices: 1.59 us -> 0.01 us  [shards(): moved = lax.ppermute(hidden_half, 'sec', [(0, 2 * i)])]
    ppermute x3, starting transfers between devices: 5.48 us -> 3.89 us  [shards(): total = total + lax.ppermute(blocks[k], ('sec', 'tp'), pairs).astype(WIDE)]
    pallas_call x11 -> x13, Pallas kernels: 13.7 us -> 13.8 us  [call(): pl.pallas_call(run, out_shape=[*out_shape, *(shape_of(x.shape, x.dtype) f...]
  transfers between devices with their start and end apart: 21 -> 21, of which waited for: 10 -> 11; matrix products, arithmetic and copies ran while one was open for 0% -> 0% of each run, Pallas kernels for 13% -> 13%
where the time goes in v4:
time: 86.9 us; the launch traced here: 86.6 us
  starting transfers between devices  34.2 us (39%)
  waiting for transfers between devices  32.5 us (37%)
  Pallas kernels  13.8 us (16%)
  local copies, waits for them, and re-layouts  4.36 us (5%)
  other arithmetic  0.92 us (1%)
    ppermute x15, waiting for transfers between devices, swap(): return lax.ppermute(block, axis, [(i, i ^ step) for i in range(size)])  26.4 us
    ppermute x15, starting transfers between devices, swap(): return lax.ppermute(block, axis, [(i, i ^ step) for i in range(size)])  23.6 us
    pallas_call x13, Pallas kernels, call(): pl.pallas_call(run, out_shape=[*out_shape, *(shape_of(x.shape, x.dtype) f...  13.8 us
    unnamed x24, local copies, waits for them, and re-layouts  4.36 us
    ppermute x3, waiting for transfers between devices, shards(): total = total + lax.ppermute(blocks[k], ('sec', 'tp'), pairs).astype(WIDE)  4.21 us
    ppermute x3, starting transfers between devices, shards(): total = total + lax.ppermute(blocks[k], ('sec', 'tp'), pairs).astype(WIDE)  3.89 us
    ppermute x1, starting transfers between devices, shards(): moved = lax.ppermute(hidden_half, 'sec', [(0, 2 * i)])  3.41 us
    ppermute x2, starting transfers between devices, shards(): moved = lax.ppermute(hidden_half, ('sec', 'tp'), pairs)  3.31 us
  transfers between devices with their start and end apart: 21, of which 11 were waited for; matrix products, arithmetic and copies ran while one was open for 0% of the time, Pallas kernels for 13%

profile of v4, /device:TPU:0, one launch (start us, length us, event | category | flops | bytes accessed | tf_op | source)
XLA Modules:
  0.0 86.6 jit_solution(5180294129316119141)
XLA Ops:
  0.6 1.0 %copy-done.1 = bf16[1,256,1024]{2,1,0:T(8,128)(2,1)S(1)} copy-done((bf16[1,256,1024]{2,1,0:T(8,128)(2,1)S(1)}, bf16[1,256,1024]{2,1,0:T(8,128)(2,1)}, u32[]{:S(2)}) %copy-start.1) | copy-done | bytes 524312
  1.7 0.7 copy-done.4
  2.4 0.7 copy-done.10
  3.0 0.9 %shard_map.122 = (bf16[192,512]{1,0:T(8,128)(2,1)S(1)}, bf16[192,512]{1,0:T(8,128)(2,1)S(1)}, bf16[192,1024]{1,0:T(8,128)(2,1)S(1)}, bf16[192,1024]{1,0:T(8,128)(2,1)S(1)}) custom-call(bf16[256,1024]{1,0:T(8,128)(2,1)S(1)} %bitcast.15, s32[2,256]{1,0:T(2,128)S(1)} %bitcast.17, f32[1,1024]{1,0:T(1,128)S(1)} %copy-done.10), custom_call_target="tpu_custom_call" | custom-call | flops 402653184 | bytes 1710080 | tf_op jit(solution)/shard_map/pallas_call | solution.py:40
  3.9 4.1 %collective-permute-start = (bf16[192,512]{1,0:T(8,128)(2,1)S(1)}, bf16[192,512]{1,0:T(8,128)(2,1)S(1)}, u32[]{:S(2)}, u32[]{:S(2)}) collective-permute-start(bf16[192,512]{1,0:T(8,128)(2,1)S(1)} %get-tuple-element.29), channel_id=1, source_target_pairs={{0,4},{2,6},{4,0},{6,2},{1,5},{3,7},{5,1},{7,3},{8,12},{10,14},{12... | collective-permute-start | bytes 589832 | tf_op jit(solution)/shard_map/ppermute | solution.py:250
  8.0 1.3 %collective-permute-start.4 = (bf16[192,512]{1,0:T(8,128)(2,1)S(1)}, bf16[192,512]{1,0:T(8,128)(2,1)S(1)}, u32[]{:S(2)}, u32[]{:S(2)}) collective-permute-start(bf16[192,512]{1,0:T(8,128)(2,1)S(1)} %get-tuple-element.36), channel_id=1, source_target_pairs={{0,6},{2,4},{4,2},{6,0},{1,7},{3,5},{5,3},{7,1},{8,14},{10,12},{12... | collective-permute-start | bytes 589832 | tf_op jit(solution)/shard_map/ppermute | solution.py:250
  9.4 4.6 %shard_map.123 = (bf16[192,512]{1,0:T(8,128)(2,1)S(1)}, f32[192,512]{1,0:T(8,128)S(1)}, bf16[1024,2048]{1,0:T(8,128)(2,1)S(1)}, bf16[2048,1024]{1,0:T(8,128)(2,1)S(1)}, bf16[192,1024]{1,0:T(8,128)(2,1)S(1)}) custom-call(bf16[192,1024]{1,0:T(8,128)(2,1)S(1)} %get-tuple-element.26.refs_0_, ...), custom_call_target="tpu_custom_call", output_to_operand_aliasing={{4}: (3, {})} | custom-call | flops 1610612736 | bytes 17760256 | tf_op jit(solution)/shard_map/pallas_call | solution.py:40
  14.0 1.6 %collective-permute-start.1 = (bf16[192,512]{1,0:T(8,128)(2,1)S(1)}, bf16[192,512]{1,0:T(8,128)(2,1)S(1)}, u32[]{:S(2)}, u32[]{:S(2)}) collective-permute-start(bf16[192,512]{1,0:T(8,128)(2,1)S(1)} %get-tuple-element.28.refs_0_), channel_id=1, source_target_pairs={{0,1},{1,0},{2,3},{3,2},{4,5},{5,4},{6,7},{7,6},{8,9},{9,8},{10,11... | collective-permute-start | bytes 589832 | tf_op jit(solution)/shard_map/ppermute | solution.py:250
  15.6 0.2 collective-permute-start.2
  15.8 6.4 %collective-permute-done.refs_1_ = bf16[192,512]{1,0:T(8,128)(2,1)S(1)} collective-permute-done((bf16[192,512]{1,0:T(8,128)(2,1)S(1)}, bf16[192,512]{1,0:T(8,128)(2,1)S(1)}, u32[]{:S(2)}, u32[]{:S(2)}) %collective-permute-start) | collective-permute-done | bytes 196640 | tf_op jit(solution)/shard_map/ppermute | solution.py:250
  22.2 1.9 %collective-permute-start.3 = (bf16[192,512]{1,0:T(8,128)(2,1)S(1)}, bf16[192,512]{1,0:T(8,128)(2,1)S(1)}, u32[]{:S(2)}, u32[]{:S(2)}) collective-permute-start(bf16[192,512]{1,0:T(8,128)(2,1)S(1)} %shard_map.124.refs_2_.refs_0_), channel_id=1, source_target_pairs={{0,1},{1,0},{2,3},{3,2},{4,5},{5,4},{6,7},{7,6},{8,9},{9,8},{10,11... | collective-permute-start | bytes 589832 | tf_op jit(solution)/shard_map/ppermute | solution.py:250
  24.1 0.6 shard_map.125
  24.7 0.2 collective-permute-start.5
  25.0 4.6 %collective-permute-done.3.refs_1_ = bf16[192,512]{1,0:T(8,128)(2,1)S(1)} collective-permute-done((bf16[192,512]{1,0:T(8,128)(2,1)S(1)}, bf16[192,512]{1,0:T(8,128)(2,1)S(1)}, u32[]{:S(2)}, u32[]{:S(2)}) %collective-permute-start.3) | collective-permute-done | bytes 196640 | tf_op jit(solution)/shard_map/ppermute | solution.py:250
  29.6 1.8 %shard_map.127 = (bf16[192,512]{1,0:T(8,128)(2,1)S(1)}, f32[192,512]{1,0:T(8,128)S(1)}) custom-call(bf16[192,512]{1,0:T(8,128)(2,1)S(1)} %shard_map.124.refs_2_.refs_0_, bf16[192,512]{1,0:T(8,128)(2,1)S(1)} %collective-permute-done.3.refs_1_, bf16[1024,2048]{1,0:T(8,128)(2,1)S(1)} %get-tuple-element.34.refs_2_.refs_1_, ...), custom_call_target="tpu_custom_call" | custom-call | flops 1610612736 | bytes 9371648 | tf_op jit(solution)/shard_map/pallas_call | solution.py:40
  31.4 1.3 %collective-permute-start.8 = (bf16[192,512]{1,0:T(8,128)(2,1)S(1)}, bf16[192,512]{1,0:T(8,128)(2,1)S(1)}, u32[]{:S(2)}, u32[]{:S(2)}) collective-permute-start(bf16[192,512]{1,0:T(8,128)(2,1)S(1)} %get-tuple-element.37.refs_3_), channel_id=1, source_target_pairs={{0,1},{1,0},{2,3},{3,2},{4,5},{5,4},{6,7},{7,6},{8,9},{9,8},{10,11... | collective-permute-start | bytes 589832 | tf_op jit(solution)/shard_map/ppermute | solution.py:250
  32.8 1.8 %shard_map.128 = (bf16[192,512]{1,0:T(8,128)(2,1)S(1)}, f32[192,512]{1,0:T(8,128)S(1)}) custom-call(bf16[192,1024]{1,0:T(8,128)(2,1)S(1)} %collective-permute-done.2.refs_0_, bf16[1024,2048]{1,0:T(8,128)(2,1)S(1)} %get-tuple-element.34.refs_2_.refs_1_, bf16[2048,1024]{1,0:T(8,128)(2,1)S(1)} %get-tuple-element.35.refs_3_.refs_2_, ...), custom_call_target="tpu_custom_call" | custom-call | flops 1610612736 | bytes 9371648 | tf_op jit(solution)/shard_map/pallas_call | solution.py:40
  34.6 1.8 %shard_map.129 = (bf16[192,512]{1,0:T(8,128)(2,1)S(1)}, f32[192,512]{1,0:T(8,128)S(1)}) custom-call(bf16[192,512]{1,0:T(8,128)(2,1)S(1)} %shard_map.126.refs_5_.refs_0_, bf16[192,512]{1,0:T(8,128)(2,1)S(1)} %collective-permute-done.5.refs_1_, bf16[1024,2048]{1,0:T(8,128)(2,1)S(1)} %get-tuple-element.34.refs_2_.refs_1_, ...), custom_call_target="tpu_custom_call" | custom-call | flops 1610612736 | bytes 9371648 | tf_op jit(solution)/shard_map/pallas_call | solution.py:40
  36.5 0.8 collective-permute-start.10
  37.3 1.3 %collective-permute-start.6 = (bf16[192,512]{1,0:T(8,128)(2,1)S(1)}, bf16[192,512]{1,0:T(8,128)(2,1)S(1)}, u32[]{:S(2)}, u32[]{:S(2)}) collective-permute-start(bf16[192,512]{1,0:T(8,128)(2,1)S(1)} %shard_map.130), channel_id=1, source_target_pairs={{0,1},{1,0},{2,3},{3,2},{4,5},{5,4},{6,7},{7,6},{8,9},{9,8},{10,11... | collective-permute-start | bytes 589832 | tf_op jit(solution)/shard_map/ppermute | solution.py:250
  38.6 1.5 %collective-permute-start.9 = (bf16[192,512]{1,0:T(8,128)(2,1)S(1)}, bf16[192,512]{1,0:T(8,128)(2,1)S(1)}, u32[]{:S(2)}, u32[]{:S(2)}) collective-permute-start(bf16[192,512]{1,0:T(8,128)(2,1)S(1)} %add_convert_fusion.1), channel_id=1, source_target_pairs={{0,4},{2,6},{4,0},{6,2},{1,5},{3,7},{5,1},{7,3},{8,12},{10,14},{12... | collective-permute-start | bytes 589832 | tf_op jit(solution)/shard_map/ppermute | solution.py:250
  40.1 5.5 %collective-permute-done.6 = bf16[192,512]{1,0:T(8,128)(2,1)S(1)} collective-permute-done((bf16[192,512]{1,0:T(8,128)(2,1)S(1)}, bf16[192,512]{1,0:T(8,128)(2,1)S(1)}, u32[]{:S(2)}, u32[]{:S(2)}) %collective-permute-start.6) | collective-permute-done | bytes 196640 | tf_op jit(solution)/shard_map/ppermute | solution.py:250
  45.6 0.4 collective-permute-start.7
  46.1 3.3 %collective-permute-start.11 = (bf16[192,512]{1,0:T(8,128)(2,1)S(1)}, bf16[192,512]{1,0:T(8,128)(2,1)S(1)}, u32[]{:S(2)}, u32[]{:S(2)}) collective-permute-start(bf16[192,512]{1,0:T(8,128)(2,1)S(1)} %add_convert_fusion), channel_id=1, source_target_pairs={{0,6},{2,4},{4,2},{6,0},{1,7},{3,5},{5,3},{7,1},{8,14},{10,12},{12... | collective-permute-start | bytes 589832 | tf_op jit(solution)/shard_map/ppermute | solution.py:250
  49.4 4.3 %collective-permute-done.7.refs_4_ = bf16[192,512]{1,0:T(8,128)(2,1)S(1)} collective-permute-done((bf16[192,512]{1,0:T(8,128)(2,1)S(1)}, bf16[192,512]{1,0:T(8,128)(2,1)S(1)}, u32[]{:S(2)}, u32[]{:S(2)}) %collective-permute-start.7) | collective-permute-done | bytes 196640 | tf_op jit(solution)/shard_map/ppermute | solution.py:250
  53.7 2.6 %collective-permute-done.11.refs_6_ = bf16[192,512]{1,0:T(8,128)(2,1)S(1)} collective-permute-done((bf16[192,512]{1,0:T(8,128)(2,1)S(1)}, bf16[192,512]{1,0:T(8,128)(2,1)S(1)}, u32[]{:S(2)}, u32[]{:S(2)}) %collective-permute-start.11) | collective-permute-done | bytes 196640 | tf_op jit(solution)/shard_map/ppermute | solution.py:250
  56.3 0.7 shard_map.131.refs_0_.refs_6_
  57.0 3.4 %collective-permute-start.14 = (bf16[256,512]{1,0:T(8,128)(2,1)S(1)}, bf16[256,512]{1,0:T(8,128)(2,1)S(1)}, u32[]{:S(2)}, u32[]{:S(2)}) collective-permute-start(bf16[256,512]{1,0:T(8,128)(2,1)S(1)} %shard_map.131.refs_0_.refs_6_), channel_id=1, source_target_pairs={{0,16},{1,17},{2,18},{3,19},{4,20},{5,21},{6,22},{7,23}} | collective-permute-start | bytes 786440 | tf_op jit(solution)/shard_map/ppermute | solution.py:360
  60.4 1.3 %collective-permute-start.13 = (bf16[256,512]{1,0:T(8,128)(2,1)S(1)}, bf16[256,512]{1,0:T(8,128)(2,1)S(1)}, u32[]{:S(2)}, u32[]{:S(2)}) collective-permute-start(bf16[256,512]{1,0:T(8,128)(2,1)S(1)} %shard_map.131.refs_0_.refs_6_), channel_id=1, source_target_pairs={{0,25},{1,24},{2,27},{3,26},{4,29},{5,28},{6,31},{7,30}} | collective-permute-start | bytes 786440 | tf_op jit(solution)/shard_map/ppermute | solution.py:364
  61.7 2.0 %collective-permute-start.12 = (bf16[256,512]{1,0:T(8,128)(2,1)S(1)}, bf16[256,512]{1,0:T(8,128)(2,1)}, u32[]{:S(2)}, u32[]{:S(2)}) collective-permute-start(bf16[256,512]{1,0:T(8,128)(2,1)S(1)} %shard_map.131.refs_0_.refs_6_), channel_id=1, source_target_pairs={{0,9},{1,8},{2,11},{3,10},{4,13},{5,12},{6,15},{7,14}} | collective-permute-start | bytes 786440 | tf_op jit(solution)/shard_map/ppermute | solution.py:364
  63.7 1.5 %collective-permute-start.16 = (bf16[256,512]{1,0:T(8,128)(2,1)S(1)}, bf16[256,512]{1,0:T(8,128)(2,1)S(1)}, u32[]{:S(2)}, u32[]{:S(2)}) collective-permute-start(bf16[256,512]{1,0:T(8,128)(2,1)S(1)} %shard_map.131.refs_0_.refs_6_), channel_id=1, source_target_pairs={{0,1},{1,0},{2,3},{3,2},{4,5},{5,4},{6,7},{7,6},{8,9},{9,8},{10,11... | collective-permute-start | bytes 786440 | tf_op jit(solution)/shard_map/ppermute | solution.py:250
  65.3 1.9 %collective-permute-done.13 = bf16[256,512]{1,0:T(8,128)(2,1)S(1)} collective-permute-done((bf16[256,512]{1,0:T(8,128)(2,1)S(1)}, bf16[256,512]{1,0:T(8,128)(2,1)S(1)}, u32[]{:S(2)}, u32[]{:S(2)}) %collective-permute-start.13) | collective-permute-done | bytes 262176 | tf_op jit(solution)/shard_map/ppermute | solution.py:364
  67.1 0.7 copy-done.11
  67.9 2.0 %collective-permute-start.15 = (bf16[256,512]{1,0:T(8,128)(2,1)S(1)}, bf16[256,512]{1,0:T(8,128)(2,1)S(1)}, u32[]{:S(2)}, u32[]{:S(2)}) collective-permute-start(bf16[256,512]{1,0:T(8,128)(2,1)S(1)} %select_select_fusion), channel_id=1, source_target_pairs={{0,8},{8,0},{16,24},{24,16},{1,9},{9,1},{17,25},{25,17},{2,10},{10... | collective-permute-start | bytes 786440 | tf_op jit(solution)/shard_map/ppermute | solution.py:250
  69.9 1.8 %collective-permute-done.16.refs_1_ = bf16[256,512]{1,0:T(8,128)(2,1)S(1)} collective-permute-done((bf16[256,512]{1,0:T(8,128)(2,1)S(1)}, bf16[256,512]{1,0:T(8,128)(2,1)S(1)}, u32[]{:S(2)}, u32[]{:S(2)}) %collective-permute-start.16) | collective-permute-done | bytes 262176 | tf_op jit(solution)/shard_map/ppermute | solution.py:250
  71.7 0.7 shard_map.132.refs_2_
  72.5 1.2 %copy-done.8 = bf16[1,1024,512]{2,1,0:T(8,128)(2,1)S(1)} copy-done((bf16[1,1024,512]{2,1,0:T(8,128)(2,1)S(1)}, bf16[1,1024,512]{2,1,0:T(8,128)(2,1)}, u32[]{:S(2)}) %copy-start.8) | copy-done | bytes 1048600
  73.7 0.8 shard_map.133
  74.4 2.1 %collective-permute-start.17 = (bf16[256,512]{1,0:T(8,128)(2,1)S(1)}, bf16[256,512]{1,0:T(8,128)(2,1)S(1)}, u32[]{:S(2)}, u32[]{:S(2)}) collective-permute-start(bf16[256,512]{1,0:T(8,128)(2,1)S(1)} %get-tuple-element.45), channel_id=1, source_target_pairs={{0,8},{8,0},{16,24},{24,16},{1,9},{9,1},{17,25},{25,17},{2,10},{10... | collective-permute-start | bytes 786440 | tf_op jit(solution)/shard_map/ppermute | solution.py:250
  76.6 1.2 %collective-permute-done.17.refs_1_ = bf16[256,512]{1,0:T(8,128)(2,1)S(1)} collective-permute-done((bf16[256,512]{1,0:T(8,128)(2,1)S(1)}, bf16[256,512]{1,0:T(8,128)(2,1)S(1)}, u32[]{:S(2)}, u32[]{:S(2)}) %collective-permute-start.17) | collective-permute-done | bytes 262176 | tf_op jit(solution)/shard_map/ppermute | solution.py:250
  77.7 0.1 shard_map.134
  77.8 0.6 collective-permute-start.18
  78.4 2.4 %collective-permute-start.19 = (bf16[256,128]{1,0:T(8,128)(2,1)S(1)}, bf16[256,128]{1,0:T(8,128)(2,1)S(1)}, u32[]{:S(2)}, u32[]{:S(2)}) collective-permute-start(bf16[256,128]{1,0:T(8,128)(2,1)S(1)} %get-tuple-element.48), channel_id=1, source_target_pairs={{0,16},{1,17},{8,24},{9,25},{16,0},{17,1},{24,8},{25,9},{2,18},{3,... | collective-permute-start | bytes 196616 | tf_op jit(solution)/shard_map/ppermute | solution.py:405
  80.8 1.0 %collective-permute-start.20 = (bf16[256,128]{1,0:T(8,128)(2,1)S(1)}, bf16[256,128]{1,0:T(8,128)(2,1)S(1)}, u32[]{:S(2)}, u32[]{:S(2)}) collective-permute-start(bf16[256,128]{1,0:T(8,128)(2,1)S(1)} %get-tuple-element.49), channel_id=1, source_target_pairs={{0,17},{1,16},{8,25},{9,24},{16,1},{17,0},{24,9},{25,8},{2,19},{3,... | collective-permute-start | bytes 196616 | tf_op jit(solution)/shard_map/ppermute | solution.py:405
  81.7 0.5 collective-permute-done.18
  82.3 0.9 %collective-permute-done.19 = bf16[256,128]{1,0:T(8,128)(2,1)S(1)} collective-permute-done((bf16[256,128]{1,0:T(8,128)(2,1)S(1)}, bf16[256,128]{1,0:T(8,128)(2,1)S(1)}, u32[]{:S(2)}, u32[]{:S(2)}) %collective-permute-start.19) | collective-permute-done | bytes 65568 | tf_op jit(solution)/shard_map/ppermute | solution.py:405
  83.2 2.7 %collective-permute-done.20 = bf16[256,128]{1,0:T(8,128)(2,1)S(1)} collective-permute-done((bf16[256,128]{1,0:T(8,128)(2,1)S(1)}, bf16[256,128]{1,0:T(8,128)(2,1)S(1)}, u32[]{:S(2)}, u32[]{:S(2)}) %collective-permute-start.20) | collective-permute-done | bytes 65568 | tf_op jit(solution)/shard_map/ppermute | solution.py:405
  85.9 0.7 add_convert_fusion.4
  (38 shorter events, 0.3 us)
Async XLA Ops:
  0.6 1.0 %copy-start.1 = (bf16[1,256,1024]{2,1,0:T(8,128)(2,1)S(1)}, bf16[1,256,1024]{2,1,0:T(8,128)(2,1)}, u32[]{:S(2)}) copy-start(bf16[1,256,1024]{2,1,0:T(8,128)(2,1)} %param.11) | copy-start | bytes 1572868
  1.7 0.7 copy-start.4
  2.4 0.7 copy-start.10
  3.9 18.3 %collective-permute-start = (bf16[192,512]{1,0:T(8,128)(2,1)S(1)}, bf16[192,512]{1,0:T(8,128)(2,1)S(1)}, u32[]{:S(2)}, u32[]{:S(2)}) collective-permute-start(bf16[192,512]{1,0:T(8,128)(2,1)S(1)} %get-tuple-element.29), channel_id=1, source_target_pairs={{0,4},{2,6},{4,0},{6,2},{1,5},{3,7},{5,1},{7,3},{8,12},{10,14},{12... | collective-permute-start | bytes 589832 | tf_op jit(solution)/shard_map/ppermute | solution.py:250
  8.0 16.7 %collective-permute-start.4 = (bf16[192,512]{1,0:T(8,128)(2,1)S(1)}, bf16[192,512]{1,0:T(8,128)(2,1)S(1)}, u32[]{:S(2)}, u32[]{:S(2)}) collective-permute-start(bf16[192,512]{1,0:T(8,128)(2,1)S(1)} %get-tuple-element.36), channel_id=1, source_target_pairs={{0,6},{2,4},{4,2},{6,0},{1,7},{3,5},{5,3},{7,1},{8,14},{10,12},{12... | collective-permute-start | bytes 589832 | tf_op jit(solution)/shard_map/ppermute | solution.py:250
  9.4 14.7 %copy-start.5 = (s32[1,256,2]{1,2,0:T(2,128)S(1)}, s32[1,256,2]{1,2,0:T(2,128)}, u32[]{:S(2)}) copy-start(s32[1,256,2]{1,2,0:T(2,128)} %param.12) | copy-start | bytes 6148
  9.4 14.7 %copy-start.6 = (f32[1,256,2]{1,2,0:T(2,128)S(1)}, f32[1,256,2]{1,2,0:T(2,128)}, u32[]{:S(2)}) copy-start(f32[1,256,2]{1,2,0:T(2,128)} %param.13) | copy-start | bytes 6148
  14.0 10.9 %collective-permute-start.1 = (bf16[192,512]{1,0:T(8,128)(2,1)S(1)}, bf16[192,512]{1,0:T(8,128)(2,1)S(1)}, u32[]{:S(2)}, u32[]{:S(2)}) collective-permute-start(bf16[192,512]{1,0:T(8,128)(2,1)S(1)} %get-tuple-element.28.refs_0_), channel_id=1, source_target_pairs={{0,1},{1,0},{2,3},{3,2},{4,5},{5,4},{6,7},{7,6},{8,9},{9,8},{10,11... | collective-permute-start | bytes 589832 | tf_op jit(solution)/shard_map/ppermute | solution.py:250
  15.6 17.2 %collective-permute-start.2 = (bf16[192,1024]{1,0:T(8,128)(2,1)S(1)}, bf16[192,1024]{1,0:T(8,128)(2,1)S(1)}, u32[]{:S(2)}, u32[]{:S(2)}) collective-permute-start(bf16[192,1024]{1,0:T(8,128)(2,1)S(1)} %get-tuple-element.33), channel_id=1, source_target_pairs={{0,2},{2,0},{4,6},{6,4},{1,3},{3,1},{5,7},{7,5},{8,10},{10,8},{12,... | collective-permute-start | bytes 1179656 | tf_op jit(solution)/shard_map/ppermute | solution.py:250
  22.2 7.4 %collective-permute-start.3 = (bf16[192,512]{1,0:T(8,128)(2,1)S(1)}, bf16[192,512]{1,0:T(8,128)(2,1)S(1)}, u32[]{:S(2)}, u32[]{:S(2)}) collective-permute-start(bf16[192,512]{1,0:T(8,128)(2,1)S(1)} %shard_map.124.refs_2_.refs_0_), channel_id=1, source_target_pairs={{0,1},{1,0},{2,3},{3,2},{4,5},{5,4},{6,7},{7,6},{8,9},{9,8},{10,11... | collective-permute-start | bytes 589832 | tf_op jit(solution)/shard_map/ppermute | solution.py:250
  24.7 9.9 %collective-permute-start.5 = (bf16[192,512]{1,0:T(8,128)(2,1)S(1)}, bf16[192,512]{1,0:T(8,128)(2,1)S(1)}, u32[]{:S(2)}, u32[]{:S(2)}) collective-permute-start(bf16[192,512]{1,0:T(8,128)(2,1)S(1)} %shard_map.126.refs_5_.refs_0_), channel_id=1, source_target_pairs={{0,1},{1,0},{2,3},{3,2},{4,5},{5,4},{6,7},{7,6},{8,9},{9,8},{10,11... | collective-permute-start | bytes 589832 | tf_op jit(solution)/shard_map/ppermute | solution.py:250
  31.4 7.1 %collective-permute-start.8 = (bf16[192,512]{1,0:T(8,128)(2,1)S(1)}, bf16[192,512]{1,0:T(8,128)(2,1)S(1)}, u32[]{:S(2)}, u32[]{:S(2)}) collective-permute-start(bf16[192,512]{1,0:T(8,128)(2,1)S(1)} %get-tuple-element.37.refs_3_), channel_id=1, source_target_pairs={{0,1},{1,0},{2,3},{3,2},{4,5},{5,4},{6,7},{7,6},{8,9},{9,8},{10,11... | collective-permute-start | bytes 589832 | tf_op jit(solution)/shard_map/ppermute | solution.py:250
  34.6 21.7 %copy-start.2 = (bf16[1,256,1024]{2,1,0:T(8,128)(2,1)S(1)}, bf16[1,256,1024]{2,1,0:T(8,128)(2,1)}, u32[]{:S(2)}) copy-start(bf16[1,256,1024]{2,1,0:T(8,128)(2,1)} %param.11) | copy-start | bytes 1572868
  36.4 35.2 %copy-start = (bf16[1,1024,512]{2,1,0:T(8,128)(2,1)S(1)}, bf16[1,1024,512]{2,1,0:T(8,128)(2,1)}, u32[]{:S(2)}) copy-start(bf16[1,1024,512]{2,1,0:T(8,128)(2,1)} %param.18) | copy-start | bytes 3145732
  36.4 35.2 %copy-start.3 = (f32[1,1024]{1,0:T(1,128)S(1)}, f32[1,1024]{1,0:T(1,128)}, u32[]{:S(2)}) copy-start(f32[1,1024]{1,0:T(1,128)} %refs_2_.3) | copy-start | bytes 12292
  36.5 9.6 %collective-permute-start.10 = (bf16[192,512]{1,0:T(8,128)(2,1)S(1)}, bf16[192,512]{1,0:T(8,128)(2,1)S(1)}, u32[]{:S(2)}, u32[]{:S(2)}) collective-permute-start(bf16[192,512]{1,0:T(8,128)(2,1)S(1)} %get-tuple-element.40.refs_0_), channel_id=1, source_target_pairs={{0,1},{1,0},{2,3},{3,2},{4,5},{5,4},{6,7},{7,6},{8,9},{9,8},{10,11... | collective-permute-start | bytes 589832 | tf_op jit(solution)/shard_map/ppermute | solution.py:250
  37.3 8.3 %collective-permute-start.6 = (bf16[192,512]{1,0:T(8,128)(2,1)S(1)}, bf16[192,512]{1,0:T(8,128)(2,1)S(1)}, u32[]{:S(2)}, u32[]{:S(2)}) collective-permute-start(bf16[192,512]{1,0:T(8,128)(2,1)S(1)} %shard_map.130), channel_id=1, source_target_pairs={{0,1},{1,0},{2,3},{3,2},{4,5},{5,4},{6,7},{7,6},{8,9},{9,8},{10,11... | collective-permute-start | bytes 589832 | tf_op jit(solution)/shard_map/ppermute | solution.py:250
  38.6 10.8 %collective-permute-start.9 = (bf16[192,512]{1,0:T(8,128)(2,1)S(1)}, bf16[192,512]{1,0:T(8,128)(2,1)S(1)}, u32[]{:S(2)}, u32[]{:S(2)}) collective-permute-start(bf16[192,512]{1,0:T(8,128)(2,1)S(1)} %add_convert_fusion.1), channel_id=1, source_target_pairs={{0,4},{2,6},{4,0},{6,2},{1,5},{3,7},{5,1},{7,3},{8,12},{10,14},{12... | collective-permute-start | bytes 589832 | tf_op jit(solution)/shard_map/ppermute | solution.py:250
  45.6 26.8 %copy-start.7 = (bf16[1,1024,512]{2,1,0:T(8,128)(2,1)S(1)}, bf16[1,1024,512]{2,1,0:T(8,128)(2,1)}, u32[]{:S(2)}) copy-start(bf16[1,1024,512]{2,1,0:T(8,128)(2,1)} %param.19) | copy-start | bytes 3145732
  45.6 26.8 %copy-start.9 = (bf16[1,256,512]{2,1,0:T(8,128)(2,1)S(1)}, bf16[1,256,512]{2,1,0:T(8,128)(2,1)}, u32[]{:S(2)}) copy-start(bf16[1,256,512]{2,1,0:T(8,128)(2,1)} %param.21) | copy-start | bytes 786436
  45.6 8.1 %collective-permute-start.7 = (bf16[192,512]{1,0:T(8,128)(2,1)S(1)}, bf16[192,512]{1,0:T(8,128)(2,1)S(1)}, u32[]{:S(2)}, u32[]{:S(2)}) collective-permute-start(bf16[192,512]{1,0:T(8,128)(2,1)S(1)} %add_convert_fusion.2), channel_id=1, source_target_pairs={{0,2},{2,0},{4,6},{6,4},{1,3},{3,1},{5,7},{7,5},{8,10},{10,8},{12,... | collective-permute-start | bytes 589832 | tf_op jit(solution)/shard_map/ppermute | solution.py:250
  46.1 10.2 %collective-permute-start.11 = (bf16[192,512]{1,0:T(8,128)(2,1)S(1)}, bf16[192,512]{1,0:T(8,128)(2,1)S(1)}, u32[]{:S(2)}, u32[]{:S(2)}) collective-permute-start(bf16[192,512]{1,0:T(8,128)(2,1)S(1)} %add_convert_fusion), channel_id=1, source_target_pairs={{0,6},{2,4},{4,2},{6,0},{1,7},{3,5},{5,3},{7,1},{8,14},{10,12},{12... | collective-permute-start | bytes 589832 | tf_op jit(solution)/shard_map/ppermute | solution.py:250
  57.0 8.3 %collective-permute-start.14 = (bf16[256,512]{1,0:T(8,128)(2,1)S(1)}, bf16[256,512]{1,0:T(8,128)(2,1)S(1)}, u32[]{:S(2)}, u32[]{:S(2)}) collective-permute-start(bf16[256,512]{1,0:T(8,128)(2,1)S(1)} %shard_map.131.refs_0_.refs_6_), channel_id=1, source_target_pairs={{0,16},{1,17},{2,18},{3,19},{4,20},{5,21},{6,22},{7,23}} | collective-permute-start | bytes 786440 | tf_op jit(solution)/shard_map/ppermute | solution.py:360
  60.4 6.7 %collective-permute-start.13 = (bf16[256,512]{1,0:T(8,128)(2,1)S(1)}, bf16[256,512]{1,0:T(8,128)(2,1)S(1)}, u32[]{:S(2)}, u32[]{:S(2)}) collective-permute-start(bf16[256,512]{1,0:T(8,128)(2,1)S(1)} %shard_map.131.refs_0_.refs_6_), channel_id=1, source_target_pairs={{0,25},{1,24},{2,27},{3,26},{4,29},{5,28},{6,31},{7,30}} | collective-permute-start | bytes 786440 | tf_op jit(solution)/shard_map/ppermute | solution.py:364
  61.7 6.1 %collective-permute-start.12 = (bf16[256,512]{1,0:T(8,128)(2,1)S(1)}, bf16[256,512]{1,0:T(8,128)(2,1)}, u32[]{:S(2)}, u32[]{:S(2)}) collective-permute-start(bf16[256,512]{1,0:T(8,128)(2,1)S(1)} %shard_map.131.refs_0_.refs_6_), channel_id=1, source_target_pairs={{0,9},{1,8},{2,11},{3,10},{4,13},{5,12},{6,15},{7,14}} | collective-permute-start | bytes 786440 | tf_op jit(solution)/shard_map/ppermute | solution.py:364
  63.7 8.0 %collective-permute-start.16 = (bf16[256,512]{1,0:T(8,128)(2,1)S(1)}, bf16[256,512]{1,0:T(8,128)(2,1)S(1)}, u32[]{:S(2)}, u32[]{:S(2)}) collective-permute-start(bf16[256,512]{1,0:T(8,128)(2,1)S(1)} %shard_map.131.refs_0_.refs_6_), channel_id=1, source_target_pairs={{0,1},{1,0},{2,3},{3,2},{4,5},{5,4},{6,7},{7,6},{8,9},{9,8},{10,11... | collective-permute-start | bytes 786440 | tf_op jit(solution)/shard_map/ppermute | solution.py:250
  67.1 0.7 copy-start.11
  67.9 4.5 %collective-permute-start.15 = (bf16[256,512]{1,0:T(8,128)(2,1)S(1)}, bf16[256,512]{1,0:T(8,128)(2,1)S(1)}, u32[]{:S(2)}, u32[]{:S(2)}) collective-permute-start(bf16[256,512]{1,0:T(8,128)(2,1)S(1)} %select_select_fusion), channel_id=1, source_target_pairs={{0,8},{8,0},{16,24},{24,16},{1,9},{9,1},{17,25},{25,17},{2,10},{10... | collective-permute-start | bytes 786440 | tf_op jit(solution)/shard_map/ppermute | solution.py:250
  72.5 1.2 %copy-start.8 = (bf16[1,1024,512]{2,1,0:T(8,128)(2,1)S(1)}, bf16[1,1024,512]{2,1,0:T(8,128)(2,1)}, u32[]{:S(2)}) copy-start(bf16[1,1024,512]{2,1,0:T(8,128)(2,1)} %param.20) | copy-start | bytes 3145732
  74.4 3.3 %collective-permute-start.17 = (bf16[256,512]{1,0:T(8,128)(2,1)S(1)}, bf16[256,512]{1,0:T(8,128)(2,1)S(1)}, u32[]{:S(2)}, u32[]{:S(2)}) collective-permute-start(bf16[256,512]{1,0:T(8,128)(2,1)S(1)} %get-tuple-element.45), channel_id=1, source_target_pairs={{0,8},{8,0},{16,24},{24,16},{1,9},{9,1},{17,25},{25,17},{2,10},{10... | collective-permute-start | bytes 786440 | tf_op jit(solution)/shard_map/ppermute | solution.py:250
  77.8 4.4 %collective-permute-start.18 = (bf16[256,128]{1,0:T(8,128)(2,1)S(1)}, bf16[256,128]{1,0:T(8,128)(2,1)S(1)}, u32[]{:S(2)}, u32[]{:S(2)}) collective-permute-start(bf16[256,128]{1,0:T(8,128)(2,1)S(1)} %get-tuple-element.47), channel_id=1, source_target_pairs={{0,1},{1,0},{8,9},{9,8},{16,17},{17,16},{24,25},{25,24},{2,3},{3,2... | collective-permute-start | bytes 196616 | tf_op jit(solution)/shard_map/ppermute | solution.py:405
  78.4 4.8 %collective-permute-start.19 = (bf16[256,128]{1,0:T(8,128)(2,1)S(1)}, bf16[256,128]{1,0:T(8,128)(2,1)S(1)}, u32[]{:S(2)}, u32[]{:S(2)}) collective-permute-start(bf16[256,128]{1,0:T(8,128)(2,1)S(1)} %get-tuple-element.48), channel_id=1, source_target_pairs={{0,16},{1,17},{8,24},{9,25},{16,0},{17,1},{24,8},{25,9},{2,18},{3,... | collective-permute-start | bytes 196616 | tf_op jit(solution)/shard_map/ppermute | solution.py:405
  80.8 5.2 %collective-permute-start.20 = (bf16[256,128]{1,0:T(8,128)(2,1)S(1)}, bf16[256,128]{1,0:T(8,128)(2,1)S(1)}, u32[]{:S(2)}, u32[]{:S(2)}) collective-permute-start(bf16[256,128]{1,0:T(8,128)(2,1)S(1)} %get-tuple-element.49), channel_id=1, source_target_pairs={{0,17},{1,16},{8,25},{9,24},{16,1},{17,0},{24,9},{25,8},{2,19},{3,... | collective-permute-start | bytes 196616 | tf_op jit(solution)/shard_map/ppermute | solution.py:405

commit v5 on v4

--- a/solution.py
+++ b/solution.py
@@ -25,7 +25,7 @@
     return lax.dot_general(a, b, dims, preferred_element_type=WIDE)
 
 
-def call(body, out_shape, inputs, scratch=(), flops=0, limit=40, remote=(), after=(), held=()):
+def call(body, out_shape, inputs, scratch=(), flops=0, limit=16, remote=(), after=(), held=()):
     def size(x):
         return math.prod(x.shape) * jnp.dtype(x.dtype).itemsize
 
@@ -130,7 +130,7 @@
     kept[...] = matmul(inner[...], second[:, part(tp, half)])
 
 
-def expert_first(rows, first, second, away, kept, first_here, second_here, inner, arrived):
+def load_and_multiply(rows, first, second, first_here, second_here, inner, arrived, away, kept):
     tp = lax.axis_index("tp")
     width, hidden = first.shape
     half = width // 2
@@ -145,10 +145,34 @@
         load.start()
     for c, load in zip(columns, loads):
         load.wait()
-        inner[:, c] = jnp.maximum(matmul(rows[...], first_here[:, c]), 0.0).astype(LOW)
+        if rows is not None:
+            inner[:, c] = jnp.maximum(matmul(rows[...], first_here[:, c]), 0.0).astype(LOW)
     loads[-1].wait()
-    away[...] = matmul(inner[...], second_here[:, part(1 - tp, half)]).astype(LOW)
-    kept[...] = matmul(inner[...], second_here[:, part(tp, half)])
+    if rows is not None:
+        away[...] = matmul(inner[...], second_here[:, part(1 - tp, half)]).astype(LOW)
+        kept[...] = matmul(inner[...], second_here[:, part(tp, half)])
+
+
+def expert_early(rows, first, second, away, kept, first_here, second_here, inner, arrived):
+    @pl.when(lax.axis_index("sec") % 2 == 1)
+    def _():
+        load_and_multiply(rows, first, second, first_here, second_here, inner, arrived, away, kept)
+
+
+def expert_late(
+    rows, first, second, away_early, kept_early, away, kept, first_here, second_here, inner, arrived
+):
+    odd = lax.axis_index("sec") % 2 == 1
+
+    @pl.when(odd)
+    def _():
+        load_and_multiply(None, first, second, first_here, second_here, inner, arrived, away, kept)
+        away[...] = away_early[...]
+        kept[...] = kept_early[...]
+
+    @pl.when(jnp.logical_not(odd))
+    def _():
+        load_and_multiply(rows, first, second, first_here, second_here, inner, arrived, away, kept)
 
 
 def idle():
@@ -305,21 +329,30 @@
             [*rows, weight_first, weight_second],
             [pltpu.VMEM((count, units), LOW)],
             flops=4 * count * model_width * units,
+            limit=24,
             after=after,
         )
 
+    loads = max(1, units // 512) + 1
+    block_shapes = [row_half, shape_of((capacity, half), WIDE)]
+    weight_shapes = [weight_first.shape, weight_second.shape]
+    weights = [weight_first, weight_second]
+    work = [pltpu.VMEM((capacity, units), LOW), pltpu.SemaphoreType.DMA((loads,))]
+    early_away, early_kept, *far_rows = call(
+        expert_early,
+        block_shapes,
+        [own_rows, *weights],
+        [pltpu.VMEM(dims, LOW) for dims in weight_shapes] + work,
+        remote=(1, 2),
+        limit=50,
+        held=far_rows,
+    )
     arriving = [joined(group) for group in groups]
-    loads = max(1, units // 512) + 1
     own_away, own_kept, weight_first, weight_second, near_rows = call(
-        expert_first,
-        [
-            row_half,
-            shape_of((capacity, half), WIDE),
-            shape_of(weight_first.shape),
-            shape_of(weight_second.shape),
-        ],
-        [own_rows, weight_first, weight_second],
-        [pltpu.VMEM((capacity, units), LOW), pltpu.SemaphoreType.DMA((loads,))],
+        expert_late,
+        block_shapes + [shape_of(dims) for dims in weight_shapes],
+        [own_rows, *weights, early_away, early_kept],
+        work,
         flops=4 * capacity * model_width * units,
         remote=(1, 2),
         limit=44,

time: 86.9 us -> 89.1 us (1.025)
  starting transfers between devices: 34.2 us -> 39.9 us
  waiting for transfers between devices: 32.5 us -> 28.8 us
    ppermute x15, starting transfers between devices: 23.6 us -> 28.6 us  [swap(): return lax.ppermute(block, axis, [(i, i ^ step) for i in range(size)])]
    ppermute x15, waiting for transfers between devices: 26.4 us -> 22.5 us  [swap(): return lax.ppermute(block, axis, [(i, i ^ step) for i in range(size)])]
    pallas_call x13 -> x14, Pallas kernels: 13.8 us -> 13.8 us  [call(): pl.pallas_call(run, out_shape=[*out_shape, *(shape_of(x.shape, x.dtype) f...]
  transfers between devices with their start and end apart: 21 -> 21, of which waited for: 11 -> 9; matrix products, arithmetic and copies ran while one was open for 0% -> 0% of each run, Pallas kernels for 13% -> 13%
where the time goes in v5:
time: 89.1 us; the launch traced here: 88.7 us
  starting transfers between devices  39.9 us (45%)
  waiting for transfers between devices  28.8 us (32%)
  Pallas kernels  13.8 us (15%)
  local copies, waits for them, and re-layouts  4.36 us (5%)
  other arithmetic  0.92 us (1%)
    ppermute x15, starting transfers between devices, swap(): return lax.ppermute(block, axis, [(i, i ^ step) for i in range(size)])  28.6 us
    ppermute x15, waiting for transfers between devices, swap(): return lax.ppermute(block, axis, [(i, i ^ step) for i in range(size)])  22.5 us
    pallas_call x14, Pallas kernels, call(): pl.pallas_call(run, out_shape=[*out_shape, *(shape_of(x.shape, x.dtype) f...  13.8 us
    ppermute x3, starting transfers between devices, shards(): total = total + lax.ppermute(blocks[k], ('sec', 'tp'), pairs).astype(WIDE)  4.65 us
    unnamed x24, local copies, waits for them, and re-layouts  4.36 us
    ppermute x3, waiting for transfers between devices, shards(): total = total + lax.ppermute(blocks[k], ('sec', 'tp'), pairs).astype(WIDE)  3.98 us
    ppermute x1, starting transfers between devices, shards(): moved = lax.ppermute(hidden_half, 'sec', [(0, 2 * i)])  3.41 us
    ppermute x2, starting transfers between devices, shards(): moved = lax.ppermute(hidden_half, ('sec', 'tp'), pairs)  3.3 us
  transfers between devices with their start and end apart: 21, of which 9 were waited for; matrix products, arithmetic and copies ran while one was open for 0% of the time, Pallas kernels for 13%

profile of v5, /device:TPU:0, one launch (start us, length us, event | category | flops | bytes accessed | tf_op | source)
XLA Modules:
  0.0 88.7 jit_solution(12208790289756097569)
XLA Ops:
  0.6 1.0 %copy-done.1 = bf16[1,256,1024]{2,1,0:T(8,128)(2,1)S(1)} copy-done((bf16[1,256,1024]{2,1,0:T(8,128)(2,1)S(1)}, bf16[1,256,1024]{2,1,0:T(8,128)(2,1)}, u32[]{:S(2)}) %copy-start.1) | copy-done | bytes 524312
  1.7 0.7 copy-done.4
  2.4 0.7 copy-done.10
  3.0 0.9 shard_map.122
  3.9 0.1 shard_map.123
  4.0 4.1 %collective-permute-start = (bf16[192,512]{1,0:T(8,128)(2,1)S(1)}, bf16[192,512]{1,0:T(8,128)(2,1)S(1)}, u32[]{:S(2)}, u32[]{:S(2)}) collective-permute-start(bf16[192,512]{1,0:T(8,128)(2,1)S(1)} %get-tuple-element.37), channel_id=1, source_target_pairs={{0,4},{2,6},{4,0},{6,2},{1,5},{3,7},{5,1},{7,3},{8,12},{10,14},{12... | collective-permute-start | bytes 589832 | tf_op jit(solution)/shard_map/ppermute | solution.py:274
  8.1 1.3 %collective-permute-start.4 = (bf16[192,512]{1,0:T(8,128)(2,1)S(1)}, bf16[192,512]{1,0:T(8,128)(2,1)S(1)}, u32[]{:S(2)}, u32[]{:S(2)}) collective-permute-start(bf16[192,512]{1,0:T(8,128)(2,1)S(1)} %get-tuple-element.44), channel_id=1, source_target_pairs={{0,6},{2,4},{4,2},{6,0},{1,7},{3,5},{5,3},{7,1},{8,14},{10,12},{12... | collective-permute-start | bytes 589832 | tf_op jit(solution)/shard_map/ppermute | solution.py:274
  9.5 4.6 %shard_map.124 = (bf16[192,512]{1,0:T(8,128)(2,1)S(1)}, f32[192,512]{1,0:T(8,128)S(1)}, bf16[1024,2048]{1,0:T(8,128)(2,1)S(1)}, bf16[2048,1024]{1,0:T(8,128)(2,1)S(1)}, bf16[192,1024]{1,0:T(8,128)(2,1)S(1)}) custom-call(bf16[192,1024]{1,0:T(8,128)(2,1)S(1)} %get-tuple-element.30.refs_0_, ...), custom_call_target="tpu_custom_call", output_to_operand_aliasing={{4}: (5, {})} | custom-call | flops 1610612736 | bytes 18350080 | tf_op jit(solution)/shard_map/pallas_call | solution.py:40
  14.1 1.6 %collective-permute-start.1 = (bf16[192,512]{1,0:T(8,128)(2,1)S(1)}, bf16[192,512]{1,0:T(8,128)(2,1)S(1)}, u32[]{:S(2)}, u32[]{:S(2)}) collective-permute-start(bf16[192,512]{1,0:T(8,128)(2,1)S(1)} %get-tuple-element.36.refs_0_), channel_id=1, source_target_pairs={{0,1},{1,0},{2,3},{3,2},{4,5},{5,4},{6,7},{7,6},{8,9},{9,8},{10,11... | collective-permute-start | bytes 589832 | tf_op jit(solution)/shard_map/ppermute | solution.py:274
  15.6 0.2 collective-permute-start.2
  15.9 4.9 %collective-permute-done.refs_1_ = bf16[192,512]{1,0:T(8,128)(2,1)S(1)} collective-permute-done((bf16[192,512]{1,0:T(8,128)(2,1)S(1)}, bf16[192,512]{1,0:T(8,128)(2,1)S(1)}, u32[]{:S(2)}, u32[]{:S(2)}) %collective-permute-start) | collective-permute-done | bytes 196640 | tf_op jit(solution)/shard_map/ppermute | solution.py:274
  20.8 2.1 %collective-permute-start.3 = (bf16[192,512]{1,0:T(8,128)(2,1)S(1)}, bf16[192,512]{1,0:T(8,128)(2,1)S(1)}, u32[]{:S(2)}, u32[]{:S(2)}) collective-permute-start(bf16[192,512]{1,0:T(8,128)(2,1)S(1)} %shard_map.125.refs_2_.refs_0_), channel_id=1, source_target_pairs={{0,1},{1,0},{2,3},{3,2},{4,5},{5,4},{6,7},{7,6},{8,9},{9,8},{10,11... | collective-permute-start | bytes 589832 | tf_op jit(solution)/shard_map/ppermute | solution.py:274
  22.9 0.6 shard_map.126
  23.5 0.1 collective-permute-start.5
  23.7 3.1 %collective-permute-done.3.refs_1_ = bf16[192,512]{1,0:T(8,128)(2,1)S(1)} collective-permute-done((bf16[192,512]{1,0:T(8,128)(2,1)S(1)}, bf16[192,512]{1,0:T(8,128)(2,1)S(1)}, u32[]{:S(2)}, u32[]{:S(2)}) %collective-permute-start.3) | collective-permute-done | bytes 196640 | tf_op jit(solution)/shard_map/ppermute | solution.py:274
  26.7 1.8 %shard_map.128 = (bf16[192,512]{1,0:T(8,128)(2,1)S(1)}, f32[192,512]{1,0:T(8,128)S(1)}) custom-call(bf16[192,512]{1,0:T(8,128)(2,1)S(1)} %shard_map.125.refs_2_.refs_0_, bf16[192,512]{1,0:T(8,128)(2,1)S(1)} %collective-permute-done.3.refs_1_, bf16[1024,2048]{1,0:T(8,128)(2,1)S(1)} %get-tuple-element.42.refs_2_.refs_1_, ...), custom_call_target="tpu_custom_call" | custom-call | flops 1610612736 | bytes 9371648 | tf_op jit(solution)/shard_map/pallas_call | solution.py:40
  28.6 2.5 %collective-permute-start.8 = (bf16[192,512]{1,0:T(8,128)(2,1)S(1)}, bf16[192,512]{1,0:T(8,128)(2,1)S(1)}, u32[]{:S(2)}, u32[]{:S(2)}) collective-permute-start(bf16[192,512]{1,0:T(8,128)(2,1)S(1)} %get-tuple-element.45.refs_3_), channel_id=1, source_target_pairs={{0,1},{1,0},{2,3},{3,2},{4,5},{5,4},{6,7},{7,6},{8,9},{9,8},{10,11... | collective-permute-start | bytes 589832 | tf_op jit(solution)/shard_map/ppermute | solution.py:274
  31.1 1.8 %shard_map.129 = (bf16[192,512]{1,0:T(8,128)(2,1)S(1)}, f32[192,512]{1,0:T(8,128)S(1)}) custom-call(bf16[192,1024]{1,0:T(8,128)(2,1)S(1)} %collective-permute-done.2.refs_0_, bf16[1024,2048]{1,0:T(8,128)(2,1)S(1)} %get-tuple-element.42.refs_2_.refs_1_, bf16[2048,1024]{1,0:T(8,128)(2,1)S(1)} %get-tuple-element.43.refs_3_.refs_2_, ...), custom_call_target="tpu_custom_call" | custom-call | flops 1610612736 | bytes 9371648 | tf_op jit(solution)/shard_map/pallas_call | solution.py:40
  32.9 1.8 %shard_map.130 = (bf16[192,512]{1,0:T(8,128)(2,1)S(1)}, f32[192,512]{1,0:T(8,128)S(1)}) custom-call(bf16[192,512]{1,0:T(8,128)(2,1)S(1)} %shard_map.127.refs_5_.refs_0_, bf16[192,512]{1,0:T(8,128)(2,1)S(1)} %collective-permute-done.5.refs_1_, bf16[1024,2048]{1,0:T(8,128)(2,1)S(1)} %get-tuple-element.42.refs_2_.refs_1_, ...), custom_call_target="tpu_custom_call" | custom-call | flops 1610612736 | bytes 9371648 | tf_op jit(solution)/shard_map/pallas_call | solution.py:40
  34.8 1.5 %collective-permute-start.10 = (bf16[192,512]{1,0:T(8,128)(2,1)S(1)}, bf16[192,512]{1,0:T(8,128)(2,1)S(1)}, u32[]{:S(2)}, u32[]{:S(2)}) collective-permute-start(bf16[192,512]{1,0:T(8,128)(2,1)S(1)} %get-tuple-element.48.refs_0_), channel_id=1, source_target_pairs={{0,1},{1,0},{2,3},{3,2},{4,5},{5,4},{6,7},{7,6},{8,9},{9,8},{10,11... | collective-permute-start | bytes 589832 | tf_op jit(solution)/shard_map/ppermute | solution.py:274
  36.2 0.6 collective-permute-start.6
  36.9 4.3 %collective-permute-start.9 = (bf16[192,512]{1,0:T(8,128)(2,1)S(1)}, bf16[192,512]{1,0:T(8,128)(2,1)S(1)}, u32[]{:S(2)}, u32[]{:S(2)}) collective-permute-start(bf16[192,512]{1,0:T(8,128)(2,1)S(1)} %add_convert_fusion.1), channel_id=1, source_target_pairs={{0,4},{2,6},{4,0},{6,2},{1,5},{3,7},{5,1},{7,3},{8,12},{10,14},{12... | collective-permute-start | bytes 589832 | tf_op jit(solution)/shard_map/ppermute | solution.py:274
  41.2 3.8 %collective-permute-done.6 = bf16[192,512]{1,0:T(8,128)(2,1)S(1)} collective-permute-done((bf16[192,512]{1,0:T(8,128)(2,1)S(1)}, bf16[192,512]{1,0:T(8,128)(2,1)S(1)}, u32[]{:S(2)}, u32[]{:S(2)}) %collective-permute-start.6) | collective-permute-done | bytes 196640 | tf_op jit(solution)/shard_map/ppermute | solution.py:274
  45.0 2.9 %collective-permute-start.7 = (bf16[192,512]{1,0:T(8,128)(2,1)S(1)}, bf16[192,512]{1,0:T(8,128)(2,1)S(1)}, u32[]{:S(2)}, u32[]{:S(2)}) collective-permute-start(bf16[192,512]{1,0:T(8,128)(2,1)S(1)} %add_convert_fusion.2), channel_id=1, source_target_pairs={{0,2},{2,0},{4,6},{6,4},{1,3},{3,1},{5,7},{7,5},{8,10},{10,8},{12,... | collective-permute-start | bytes 589832 | tf_op jit(solution)/shard_map/ppermute | solution.py:274
  47.9 2.7 %collective-permute-start.11 = (bf16[192,512]{1,0:T(8,128)(2,1)S(1)}, bf16[192,512]{1,0:T(8,128)(2,1)S(1)}, u32[]{:S(2)}, u32[]{:S(2)}) collective-permute-start(bf16[192,512]{1,0:T(8,128)(2,1)S(1)} %add_convert_fusion), channel_id=1, source_target_pairs={{0,6},{2,4},{4,2},{6,0},{1,7},{3,5},{5,3},{7,1},{8,14},{10,12},{12... | collective-permute-start | bytes 589832 | tf_op jit(solution)/shard_map/ppermute | solution.py:274
  50.6 7.7 %collective-permute-done.7.refs_4_ = bf16[192,512]{1,0:T(8,128)(2,1)S(1)} collective-permute-done((bf16[192,512]{1,0:T(8,128)(2,1)S(1)}, bf16[192,512]{1,0:T(8,128)(2,1)S(1)}, u32[]{:S(2)}, u32[]{:S(2)}) %collective-permute-start.7) | collective-permute-done | bytes 196640 | tf_op jit(solution)/shard_map/ppermute | solution.py:274
  58.4 0.7 shard_map.132.refs_0_.refs_6_
  59.1 3.4 %collective-permute-start.14 = (bf16[256,512]{1,0:T(8,128)(2,1)S(1)}, bf16[256,512]{1,0:T(8,128)(2,1)S(1)}, u32[]{:S(2)}, u32[]{:S(2)}) collective-permute-start(bf16[256,512]{1,0:T(8,128)(2,1)S(1)} %shard_map.132.refs_0_.refs_6_), channel_id=1, source_target_pairs={{0,16},{1,17},{2,18},{3,19},{4,20},{5,21},{6,22},{7,23}} | collective-permute-start | bytes 786440 | tf_op jit(solution)/shard_map/ppermute | solution.py:393
  62.5 1.3 %collective-permute-start.13 = (bf16[256,512]{1,0:T(8,128)(2,1)S(1)}, bf16[256,512]{1,0:T(8,128)(2,1)S(1)}, u32[]{:S(2)}, u32[]{:S(2)}) collective-permute-start(bf16[256,512]{1,0:T(8,128)(2,1)S(1)} %shard_map.132.refs_0_.refs_6_), channel_id=1, source_target_pairs={{0,25},{1,24},{2,27},{3,26},{4,29},{5,28},{6,31},{7,30}} | collective-permute-start | bytes 786440 | tf_op jit(solution)/shard_map/ppermute | solution.py:397
  63.8 2.0 %collective-permute-start.12 = (bf16[256,512]{1,0:T(8,128)(2,1)S(1)}, bf16[256,512]{1,0:T(8,128)(2,1)}, u32[]{:S(2)}, u32[]{:S(2)}) collective-permute-start(bf16[256,512]{1,0:T(8,128)(2,1)S(1)} %shard_map.132.refs_0_.refs_6_), channel_id=1, source_target_pairs={{0,9},{1,8},{2,11},{3,10},{4,13},{5,12},{6,15},{7,14}} | collective-permute-start | bytes 786440 | tf_op jit(solution)/shard_map/ppermute | solution.py:397
  65.8 1.0 %collective-permute-start.16 = (bf16[256,512]{1,0:T(8,128)(2,1)S(1)}, bf16[256,512]{1,0:T(8,128)(2,1)S(1)}, u32[]{:S(2)}, u32[]{:S(2)}) collective-permute-start(bf16[256,512]{1,0:T(8,128)(2,1)S(1)} %shard_map.132.refs_0_.refs_6_), channel_id=1, source_target_pairs={{0,1},{1,0},{2,3},{3,2},{4,5},{5,4},{6,7},{7,6},{8,9},{9,8},{10,11... | collective-permute-start | bytes 786440 | tf_op jit(solution)/shard_map/ppermute | solution.py:274
  66.8 2.4 %collective-permute-done.13 = bf16[256,512]{1,0:T(8,128)(2,1)S(1)} collective-permute-done((bf16[256,512]{1,0:T(8,128)(2,1)S(1)}, bf16[256,512]{1,0:T(8,128)(2,1)S(1)}, u32[]{:S(2)}, u32[]{:S(2)}) %collective-permute-start.13) | collective-permute-done | bytes 262176 | tf_op jit(solution)/shard_map/ppermute | solution.py:397
  69.2 0.7 copy-done.11
  69.9 0.1 select_select_fusion
  70.0 1.5 %collective-permute-start.15 = (bf16[256,512]{1,0:T(8,128)(2,1)S(1)}, bf16[256,512]{1,0:T(8,128)(2,1)S(1)}, u32[]{:S(2)}, u32[]{:S(2)}) collective-permute-start(bf16[256,512]{1,0:T(8,128)(2,1)S(1)} %select_select_fusion), channel_id=1, source_target_pairs={{0,8},{8,0},{16,24},{24,16},{1,9},{9,1},{17,25},{25,17},{2,10},{10... | collective-permute-start | bytes 786440 | tf_op jit(solution)/shard_map/ppermute | solution.py:274
  71.5 1.8 %collective-permute-done.16.refs_1_ = bf16[256,512]{1,0:T(8,128)(2,1)S(1)} collective-permute-done((bf16[256,512]{1,0:T(8,128)(2,1)S(1)}, bf16[256,512]{1,0:T(8,128)(2,1)S(1)}, u32[]{:S(2)}, u32[]{:S(2)}) %collective-permute-start.16) | collective-permute-done | bytes 262176 | tf_op jit(solution)/shard_map/ppermute | solution.py:274
  73.3 0.7 shard_map.133.refs_2_
  74.1 1.2 %copy-done.8 = bf16[1,1024,512]{2,1,0:T(8,128)(2,1)S(1)} copy-done((bf16[1,1024,512]{2,1,0:T(8,128)(2,1)S(1)}, bf16[1,1024,512]{2,1,0:T(8,128)(2,1)}, u32[]{:S(2)}) %copy-start.8) | copy-done | bytes 1048600
  75.3 0.8 shard_map.134
  76.1 2.1 %collective-permute-start.17 = (bf16[256,512]{1,0:T(8,128)(2,1)S(1)}, bf16[256,512]{1,0:T(8,128)(2,1)S(1)}, u32[]{:S(2)}, u32[]{:S(2)}) collective-permute-start(bf16[256,512]{1,0:T(8,128)(2,1)S(1)} %get-tuple-element.53), channel_id=1, source_target_pairs={{0,8},{8,0},{16,24},{24,16},{1,9},{9,1},{17,25},{25,17},{2,10},{10... | collective-permute-start | bytes 786440 | tf_op jit(solution)/shard_map/ppermute | solution.py:274
  78.2 1.2 %collective-permute-done.17.refs_1_ = bf16[256,512]{1,0:T(8,128)(2,1)S(1)} collective-permute-done((bf16[256,512]{1,0:T(8,128)(2,1)S(1)}, bf16[256,512]{1,0:T(8,128)(2,1)S(1)}, u32[]{:S(2)}, u32[]{:S(2)}) %collective-permute-start.17) | collective-permute-done | bytes 262176 | tf_op jit(solution)/shard_map/ppermute | solution.py:274
  79.3 0.1 shard_map.135
  79.4 1.1 %collective-permute-start.18 = (bf16[256,128]{1,0:T(8,128)(2,1)S(1)}, bf16[256,128]{1,0:T(8,128)(2,1)S(1)}, u32[]{:S(2)}, u32[]{:S(2)}) collective-permute-start(bf16[256,128]{1,0:T(8,128)(2,1)S(1)} %get-tuple-element.55), channel_id=1, source_target_pairs={{0,1},{1,0},{8,9},{9,8},{16,17},{17,16},{24,25},{25,24},{2,3},{3,2... | collective-permute-start | bytes 196616 | tf_op jit(solution)/shard_map/ppermute | solution.py:438
  80.5 2.4 %collective-permute-start.19 = (bf16[256,128]{1,0:T(8,128)(2,1)S(1)}, bf16[256,128]{1,0:T(8,128)(2,1)S(1)}, u32[]{:S(2)}, u32[]{:S(2)}) collective-permute-start(bf16[256,128]{1,0:T(8,128)(2,1)S(1)} %get-tuple-element.56), channel_id=1, source_target_pairs={{0,16},{1,17},{8,24},{9,25},{16,0},{17,1},{24,8},{25,9},{2,18},{3,... | collective-permute-start | bytes 196616 | tf_op jit(solution)/shard_map/ppermute | solution.py:438
  82.9 1.2 %collective-permute-start.20 = (bf16[256,128]{1,0:T(8,128)(2,1)S(1)}, bf16[256,128]{1,0:T(8,128)(2,1)S(1)}, u32[]{:S(2)}, u32[]{:S(2)}) collective-permute-start(bf16[256,128]{1,0:T(8,128)(2,1)S(1)} %get-tuple-element.57), channel_id=1, source_target_pairs={{0,17},{1,16},{8,25},{9,24},{16,1},{17,0},{24,9},{25,8},{2,19},{3,... | collective-permute-start | bytes 196616 | tf_op jit(solution)/shard_map/ppermute | solution.py:438
  84.1 1.2 %collective-permute-done.19 = bf16[256,128]{1,0:T(8,128)(2,1)S(1)} collective-permute-done((bf16[256,128]{1,0:T(8,128)(2,1)S(1)}, bf16[256,128]{1,0:T(8,128)(2,1)S(1)}, u32[]{:S(2)}, u32[]{:S(2)}) %collective-permute-start.19) | collective-permute-done | bytes 65568 | tf_op jit(solution)/shard_map/ppermute | solution.py:438
  85.3 2.7 %collective-permute-done.20 = bf16[256,128]{1,0:T(8,128)(2,1)S(1)} collective-permute-done((bf16[256,128]{1,0:T(8,128)(2,1)S(1)}, bf16[256,128]{1,0:T(8,128)(2,1)S(1)}, u32[]{:S(2)}, u32[]{:S(2)}) %collective-permute-start.20) | collective-permute-done | bytes 65568 | tf_op jit(solution)/shard_map/ppermute | solution.py:438
  88.1 0.7 add_convert_fusion.4
  (39 shorter events, 0.3 us)
Async XLA Ops:
  0.6 1.0 %copy-start.1 = (bf16[1,256,1024]{2,1,0:T(8,128)(2,1)S(1)}, bf16[1,256,1024]{2,1,0:T(8,128)(2,1)}, u32[]{:S(2)}) copy-start(bf16[1,256,1024]{2,1,0:T(8,128)(2,1)} %param.11) | copy-start | bytes 1572868
  1.7 0.7 copy-start.4
  2.4 0.7 copy-start.10
  4.0 16.8 %collective-permute-start = (bf16[192,512]{1,0:T(8,128)(2,1)S(1)}, bf16[192,512]{1,0:T(8,128)(2,1)S(1)}, u32[]{:S(2)}, u32[]{:S(2)}) collective-permute-start(bf16[192,512]{1,0:T(8,128)(2,1)S(1)} %get-tuple-element.37), channel_id=1, source_target_pairs={{0,4},{2,6},{4,0},{6,2},{1,5},{3,7},{5,1},{7,3},{8,12},{10,14},{12... | collective-permute-start | bytes 589832 | tf_op jit(solution)/shard_map/ppermute | solution.py:274
  8.1 15.4 %collective-permute-start.4 = (bf16[192,512]{1,0:T(8,128)(2,1)S(1)}, bf16[192,512]{1,0:T(8,128)(2,1)S(1)}, u32[]{:S(2)}, u32[]{:S(2)}) collective-permute-start(bf16[192,512]{1,0:T(8,128)(2,1)S(1)} %get-tuple-element.44), channel_id=1, source_target_pairs={{0,6},{2,4},{4,2},{6,0},{1,7},{3,5},{5,3},{7,1},{8,14},{10,12},{12... | collective-permute-start | bytes 589832 | tf_op jit(solution)/shard_map/ppermute | solution.py:274
  9.5 13.5 %copy-start.5 = (s32[1,256,2]{1,2,0:T(2,128)S(1)}, s32[1,256,2]{1,2,0:T(2,128)}, u32[]{:S(2)}) copy-start(s32[1,256,2]{1,2,0:T(2,128)} %param.12) | copy-start | bytes 6148
  9.5 13.5 %copy-start.6 = (f32[1,256,2]{1,2,0:T(2,128)S(1)}, f32[1,256,2]{1,2,0:T(2,128)}, u32[]{:S(2)}) copy-start(f32[1,256,2]{1,2,0:T(2,128)} %param.13) | copy-start | bytes 6148
  14.1 9.6 %collective-permute-start.1 = (bf16[192,512]{1,0:T(8,128)(2,1)S(1)}, bf16[192,512]{1,0:T(8,128)(2,1)S(1)}, u32[]{:S(2)}, u32[]{:S(2)}) collective-permute-start(bf16[192,512]{1,0:T(8,128)(2,1)S(1)} %get-tuple-element.36.refs_0_), channel_id=1, source_target_pairs={{0,1},{1,0},{2,3},{3,2},{4,5},{5,4},{6,7},{7,6},{8,9},{9,8},{10,11... | collective-permute-start | bytes 589832 | tf_op jit(solution)/shard_map/ppermute | solution.py:274
  15.6 15.4 %collective-permute-start.2 = (bf16[192,1024]{1,0:T(8,128)(2,1)S(1)}, bf16[192,1024]{1,0:T(8,128)(2,1)S(1)}, u32[]{:S(2)}, u32[]{:S(2)}) collective-permute-start(bf16[192,1024]{1,0:T(8,128)(2,1)S(1)} %get-tuple-element.41), channel_id=1, source_target_pairs={{0,2},{2,0},{4,6},{6,4},{1,3},{3,1},{5,7},{7,5},{8,10},{10,8},{12,... | collective-permute-start | bytes 1179656 | tf_op jit(solution)/shard_map/ppermute | solution.py:274
  20.8 6.0 %collective-permute-start.3 = (bf16[192,512]{1,0:T(8,128)(2,1)S(1)}, bf16[192,512]{1,0:T(8,128)(2,1)S(1)}, u32[]{:S(2)}, u32[]{:S(2)}) collective-permute-start(bf16[192,512]{1,0:T(8,128)(2,1)S(1)} %shard_map.125.refs_2_.refs_0_), channel_id=1, source_target_pairs={{0,1},{1,0},{2,3},{3,2},{4,5},{5,4},{6,7},{7,6},{8,9},{9,8},{10,11... | collective-permute-start | bytes 589832 | tf_op jit(solution)/shard_map/ppermute | solution.py:274
  23.5 9.4 %collective-permute-start.5 = (bf16[192,512]{1,0:T(8,128)(2,1)S(1)}, bf16[192,512]{1,0:T(8,128)(2,1)S(1)}, u32[]{:S(2)}, u32[]{:S(2)}) collective-permute-start(bf16[192,512]{1,0:T(8,128)(2,1)S(1)} %shard_map.127.refs_5_.refs_0_), channel_id=1, source_target_pairs={{0,1},{1,0},{2,3},{3,2},{4,5},{5,4},{6,7},{7,6},{8,9},{9,8},{10,11... | collective-permute-start | bytes 589832 | tf_op jit(solution)/shard_map/ppermute | solution.py:274
  28.6 8.3 %collective-permute-start.8 = (bf16[192,512]{1,0:T(8,128)(2,1)S(1)}, bf16[192,512]{1,0:T(8,128)(2,1)S(1)}, u32[]{:S(2)}, u32[]{:S(2)}) collective-permute-start(bf16[192,512]{1,0:T(8,128)(2,1)S(1)} %get-tuple-element.45.refs_3_), channel_id=1, source_target_pairs={{0,1},{1,0},{2,3},{3,2},{4,5},{5,4},{6,7},{7,6},{8,9},{9,8},{10,11... | collective-permute-start | bytes 589832 | tf_op jit(solution)/shard_map/ppermute | solution.py:274
  32.9 25.5 %copy-start.2 = (bf16[1,256,1024]{2,1,0:T(8,128)(2,1)S(1)}, bf16[1,256,1024]{2,1,0:T(8,128)(2,1)}, u32[]{:S(2)}) copy-start(bf16[1,256,1024]{2,1,0:T(8,128)(2,1)} %param.11) | copy-start | bytes 1572868
  34.7 38.5 %copy-start = (bf16[1,1024,512]{2,1,0:T(8,128)(2,1)S(1)}, bf16[1,1024,512]{2,1,0:T(8,128)(2,1)}, u32[]{:S(2)}) copy-start(bf16[1,1024,512]{2,1,0:T(8,128)(2,1)} %param.18) | copy-start | bytes 3145732
  34.8 38.5 %copy-start.3 = (f32[1,1024]{1,0:T(1,128)S(1)}, f32[1,1024]{1,0:T(1,128)}, u32[]{:S(2)}) copy-start(f32[1,1024]{1,0:T(1,128)} %refs_2_.3) | copy-start | bytes 12292
  34.8 13.1 %collective-permute-start.10 = (bf16[192,512]{1,0:T(8,128)(2,1)S(1)}, bf16[192,512]{1,0:T(8,128)(2,1)S(1)}, u32[]{:S(2)}, u32[]{:S(2)}) collective-permute-start(bf16[192,512]{1,0:T(8,128)(2,1)S(1)} %get-tuple-element.48.refs_0_), channel_id=1, source_target_pairs={{0,1},{1,0},{2,3},{3,2},{4,5},{5,4},{6,7},{7,6},{8,9},{9,8},{10,11... | collective-permute-start | bytes 589832 | tf_op jit(solution)/shard_map/ppermute | solution.py:274
  36.2 8.7 %collective-permute-start.6 = (bf16[192,512]{1,0:T(8,128)(2,1)S(1)}, bf16[192,512]{1,0:T(8,128)(2,1)S(1)}, u32[]{:S(2)}, u32[]{:S(2)}) collective-permute-start(bf16[192,512]{1,0:T(8,128)(2,1)S(1)} %shard_map.131), channel_id=1, source_target_pairs={{0,1},{1,0},{2,3},{3,2},{4,5},{5,4},{6,7},{7,6},{8,9},{9,8},{10,11... | collective-permute-start | bytes 589832 | tf_op jit(solution)/shard_map/ppermute | solution.py:274
  36.9 13.7 %collective-permute-start.9 = (bf16[192,512]{1,0:T(8,128)(2,1)S(1)}, bf16[192,512]{1,0:T(8,128)(2,1)S(1)}, u32[]{:S(2)}, u32[]{:S(2)}) collective-permute-start(bf16[192,512]{1,0:T(8,128)(2,1)S(1)} %add_convert_fusion.1), channel_id=1, source_target_pairs={{0,4},{2,6},{4,0},{6,2},{1,5},{3,7},{5,1},{7,3},{8,12},{10,14},{12... | collective-permute-start | bytes 589832 | tf_op jit(solution)/shard_map/ppermute | solution.py:274
  45.0 29.1 %copy-start.7 = (bf16[1,1024,512]{2,1,0:T(8,128)(2,1)S(1)}, bf16[1,1024,512]{2,1,0:T(8,128)(2,1)}, u32[]{:S(2)}) copy-start(bf16[1,1024,512]{2,1,0:T(8,128)(2,1)} %param.19) | copy-start | bytes 3145732
  45.0 29.1 %copy-start.9 = (bf16[1,256,512]{2,1,0:T(8,128)(2,1)S(1)}, bf16[1,256,512]{2,1,0:T(8,128)(2,1)}, u32[]{:S(2)}) copy-start(bf16[1,256,512]{2,1,0:T(8,128)(2,1)} %param.21) | copy-start | bytes 786436
  45.0 13.3 %collective-permute-start.7 = (bf16[192,512]{1,0:T(8,128)(2,1)S(1)}, bf16[192,512]{1,0:T(8,128)(2,1)S(1)}, u32[]{:S(2)}, u32[]{:S(2)}) collective-permute-start(bf16[192,512]{1,0:T(8,128)(2,1)S(1)} %add_convert_fusion.2), channel_id=1, source_target_pairs={{0,2},{2,0},{4,6},{6,4},{1,3},{3,1},{5,7},{7,5},{8,10},{10,8},{12,... | collective-permute-start | bytes 589832 | tf_op jit(solution)/shard_map/ppermute | solution.py:274
  47.9 10.4 %collective-permute-start.11 = (bf16[192,512]{1,0:T(8,128)(2,1)S(1)}, bf16[192,512]{1,0:T(8,128)(2,1)S(1)}, u32[]{:S(2)}, u32[]{:S(2)}) collective-permute-start(bf16[192,512]{1,0:T(8,128)(2,1)S(1)} %add_convert_fusion), channel_id=1, source_target_pairs={{0,6},{2,4},{4,2},{6,0},{1,7},{3,5},{5,3},{7,1},{8,14},{10,12},{12... | collective-permute-start | bytes 589832 | tf_op jit(solution)/shard_map/ppermute | solution.py:274
  59.1 7.8 %collective-permute-start.14 = (bf16[256,512]{1,0:T(8,128)(2,1)S(1)}, bf16[256,512]{1,0:T(8,128)(2,1)S(1)}, u32[]{:S(2)}, u32[]{:S(2)}) collective-permute-start(bf16[256,512]{1,0:T(8,128)(2,1)S(1)} %shard_map.132.refs_0_.refs_6_), channel_id=1, source_target_pairs={{0,16},{1,17},{2,18},{3,19},{4,20},{5,21},{6,22},{7,23}} | collective-permute-start | bytes 786440 | tf_op jit(solution)/shard_map/ppermute | solution.py:393
  62.5 6.7 %collective-permute-start.13 = (bf16[256,512]{1,0:T(8,128)(2,1)S(1)}, bf16[256,512]{1,0:T(8,128)(2,1)S(1)}, u32[]{:S(2)}, u32[]{:S(2)}) collective-permute-start(bf16[256,512]{1,0:T(8,128)(2,1)S(1)} %shard_map.132.refs_0_.refs_6_), channel_id=1, source_target_pairs={{0,25},{1,24},{2,27},{3,26},{4,29},{5,28},{6,31},{7,30}} | collective-permute-start | bytes 786440 | tf_op jit(solution)/shard_map/ppermute | solution.py:397
  63.8 6.1 %collective-permute-start.12 = (bf16[256,512]{1,0:T(8,128)(2,1)S(1)}, bf16[256,512]{1,0:T(8,128)(2,1)}, u32[]{:S(2)}, u32[]{:S(2)}) collective-permute-start(bf16[256,512]{1,0:T(8,128)(2,1)S(1)} %shard_map.132.refs_0_.refs_6_), channel_id=1, source_target_pairs={{0,9},{1,8},{2,11},{3,10},{4,13},{5,12},{6,15},{7,14}} | collective-permute-start | bytes 786440 | tf_op jit(solution)/shard_map/ppermute | solution.py:397
  65.8 7.5 %collective-permute-start.16 = (bf16[256,512]{1,0:T(8,128)(2,1)S(1)}, bf16[256,512]{1,0:T(8,128)(2,1)S(1)}, u32[]{:S(2)}, u32[]{:S(2)}) collective-permute-start(bf16[256,512]{1,0:T(8,128)(2,1)S(1)} %shard_map.132.refs_0_.refs_6_), channel_id=1, source_target_pairs={{0,1},{1,0},{2,3},{3,2},{4,5},{5,4},{6,7},{7,6},{8,9},{9,8},{10,11... | collective-permute-start | bytes 786440 | tf_op jit(solution)/shard_map/ppermute | solution.py:274
  69.2 0.7 copy-start.11
  70.0 4.0 %collective-permute-start.15 = (bf16[256,512]{1,0:T(8,128)(2,1)S(1)}, bf16[256,512]{1,0:T(8,128)(2,1)S(1)}, u32[]{:S(2)}, u32[]{:S(2)}) collective-permute-start(bf16[256,512]{1,0:T(8,128)(2,1)S(1)} %select_select_fusion), channel_id=1, source_target_pairs={{0,8},{8,0},{16,24},{24,16},{1,9},{9,1},{17,25},{25,17},{2,10},{10... | collective-permute-start | bytes 786440 | tf_op jit(solution)/shard_map/ppermute | solution.py:274
  74.1 1.2 %copy-start.8 = (bf16[1,1024,512]{2,1,0:T(8,128)(2,1)S(1)}, bf16[1,1024,512]{2,1,0:T(8,128)(2,1)}, u32[]{:S(2)}) copy-start(bf16[1,1024,512]{2,1,0:T(8,128)(2,1)} %param.20) | copy-start | bytes 3145732
  76.1 3.3 %collective-permute-start.17 = (bf16[256,512]{1,0:T(8,128)(2,1)S(1)}, bf16[256,512]{1,0:T(8,128)(2,1)S(1)}, u32[]{:S(2)}, u32[]{:S(2)}) collective-permute-start(bf16[256,512]{1,0:T(8,128)(2,1)S(1)} %get-tuple-element.53), channel_id=1, source_target_pairs={{0,8},{8,0},{16,24},{24,16},{1,9},{9,1},{17,25},{25,17},{2,10},{10... | collective-permute-start | bytes 786440 | tf_op jit(solution)/shard_map/ppermute | solution.py:274
  79.4 4.7 %collective-permute-start.18 = (bf16[256,128]{1,0:T(8,128)(2,1)S(1)}, bf16[256,128]{1,0:T(8,128)(2,1)S(1)}, u32[]{:S(2)}, u32[]{:S(2)}) collective-permute-start(bf16[256,128]{1,0:T(8,128)(2,1)S(1)} %get-tuple-element.55), channel_id=1, source_target_pairs={{0,1},{1,0},{8,9},{9,8},{16,17},{17,16},{24,25},{25,24},{2,3},{3,2... | collective-permute-start | bytes 196616 | tf_op jit(solution)/shard_map/ppermute | solution.py:438
  80.5 4.8 %collective-permute-start.19 = (bf16[256,128]{1,0:T(8,128)(2,1)S(1)}, bf16[256,128]{1,0:T(8,128)(2,1)S(1)}, u32[]{:S(2)}, u32[]{:S(2)}) collective-permute-start(bf16[256,128]{1,0:T(8,128)(2,1)S(1)} %get-tuple-element.56), channel_id=1, source_target_pairs={{0,16},{1,17},{8,24},{9,25},{16,0},{17,1},{24,8},{25,9},{2,18},{3,... | collective-permute-start | bytes 196616 | tf_op jit(solution)/shard_map/ppermute | solution.py:438
  82.9 5.2 %collective-permute-start.20 = (bf16[256,128]{1,0:T(8,128)(2,1)S(1)}, bf16[256,128]{1,0:T(8,128)(2,1)S(1)}, u32[]{:S(2)}, u32[]{:S(2)}) collective-permute-start(bf16[256,128]{1,0:T(8,128)(2,1)S(1)} %get-tuple-element.57), channel_id=1, source_target_pairs={{0,17},{1,16},{8,25},{9,24},{16,1},{17,0},{24,9},{25,8},{2,19},{3,... | collective-permute-start | bytes 196616 | tf_op jit(solution)/shard_map/ppermute | solution.py:438

commit v6 on v4

--- a/solution.py
+++ b/solution.py
@@ -25,7 +25,7 @@
     return lax.dot_general(a, b, dims, preferred_element_type=WIDE)
 
 
-def call(body, out_shape, inputs, scratch=(), flops=0, limit=40, remote=(), after=(), held=()):
+def call(body, out_shape, inputs, scratch=(), flops=0, limit=16, remote=(), after=(), held=()):
     def size(x):
         return math.prod(x.shape) * jnp.dtype(x.dtype).itemsize
 
@@ -57,15 +57,17 @@
     return pl.ds(pl.multiple_of(index * width, width), width)
 
 
-def places(routes, me, rows):
-    token_count = routes.shape[1]
+def triangle(out):
+    source = lax.broadcasted_iota(jnp.int32, out.shape, 0)
+    target = lax.broadcasted_iota(jnp.int32, out.shape, 1)
+    out[...] = jnp.where(source < target, 1.0, 0.0).astype(LOW)
+
+
+def places(routes, earlier, me, rows):
     labels = lax.broadcasted_iota(jnp.int32, (rows, 1), 0) ^ me
     first = routes[0:1, :] == labels
     second = routes[1:2, :] == labels
     either = first | second
-    source = lax.broadcasted_iota(jnp.int32, (token_count, token_count), 0)
-    target = lax.broadcasted_iota(jnp.int32, (token_count, token_count), 1)
-    earlier = jnp.where(source < target, 1.0, 0.0).astype(LOW)
     before = matmul(jnp.where(either, 1.0, 0.0).astype(LOW), earlier)
     return jnp.where(either, before, -1.0), first, second
 
@@ -75,7 +77,7 @@
     return jnp.where(place[k : k + 1, :] == slots, 1.0, 0.0).astype(LOW)
 
 
-def prepare(experts, tokens, routes, gain, *outs):
+def prepare(experts, tokens, routes, gain, earlier, *outs):
     far, near, own, normed_ref = outs[:-3], outs[-3], outs[-2], outs[-1]
     me = lax.axis_index("exp")
     tp = lax.axis_index("tp")
@@ -86,7 +88,7 @@
     centred = wide - average
     spread = jnp.mean(centred * centred, axis=-1, keepdims=True)
     normed_ref[...] = (centred * lax.rsqrt(spread + EPS) * gain[...]).astype(LOW)
-    place, _, _ = places(routes[...], me, max(16, experts))
+    place, _, _ = places(routes[...], earlier[...], me, max(16, experts))
     normed_half = normed_ref[:, part(tp, half)]
     for k in range(experts - 1, 1, -1):
         far[k - 2][...] = matmul(table(place, k, capacity), normed_half).astype(LOW)
@@ -95,11 +97,11 @@
     own[...] = matmul(table(place, 0, capacity), normed).astype(LOW)
 
 
-def mixing(experts, routes, gates, high, low):
+def mixing(experts, routes, gates, earlier, high, low):
     me = lax.axis_index("exp")
     token_count = routes.shape[1]
     capacity = high.shape[2]
-    place, first, second = places(routes[...], me, max(16, experts))
+    place, first, second = places(routes[...], earlier[...], me, max(16, experts))
     gate = jnp.where(first, gates[0:1, :], 0.0) + jnp.where(second, gates[1:2, :], 0.0)
     place = place.T
     gate = gate.T
@@ -280,10 +282,16 @@
     middle = max(2, experts // 2 + 1)
     groups = [list(range(middle - 1, 1, -1)), list(range(experts - 1, middle - 1, -1))]
     row_half, row_whole = shape_of((capacity, half)), shape_of((capacity, model_width))
+    earlier = call(
+        triangle,
+        [shape_of((token_count, token_count))],
+        [],
+        flops=20 * token_count * token_count * model_width,
+    )[0]
     *far_rows, near_rows, own_rows = call(
         functools.partial(prepare, experts),
         [row_half] * (experts - 2) + [row_whole] * 2,
-        [token_rows, route_rows, moe_gain],
+        [token_rows, route_rows, moe_gain, earlier],
         [pltpu.VMEM((token_count, model_width), LOW)],
         flops=2 * 3 * token_count * token_count * model_width,
     )
@@ -305,12 +313,14 @@
             [*rows, weight_first, weight_second],
             [pltpu.VMEM((count, units), LOW)],
             flops=4 * count * model_width * units,
+            limit=24,
             after=after,
         )
 
-    arriving = [joined(group) for group in groups]
+    arriving = [joined(groups[0])]
+    later = [far_rows[k - 2] for k in groups[1]] + [near_rows]
     loads = max(1, units // 512) + 1
-    own_away, own_kept, weight_first, weight_second, near_rows = call(
+    own_away, own_kept, weight_first, weight_second, *later = call(
         expert_first,
         [
             row_half,
@@ -323,31 +333,35 @@
         flops=4 * capacity * model_width * units,
         remote=(1, 2),
         limit=44,
-        held=[near_rows],
-    )
-    near = swap(near_rows, "exp", 1)
+        held=later,
+    )
+    for k, rows in zip(groups[1], later):
+        far_rows[k - 2] = rows
+    arriving.append(joined(groups[1]))
+    near = swap(later[-1], "exp", 1)
     returned = {0: total(own_away, own_kept)}
     arriving[0] = hold(arriving[0], [own_away])
     others = [swap(arriving[0], "tp", 1)]
     high, low = call(
         functools.partial(mixing, experts),
         [shape_of((experts, token_count, capacity))] * 2,
-        [route_rows, gate_rows],
+        [route_rows, gate_rows, earlier],
         after=[arriving[0]],
     )
-    arriving[1] = hold(arriving[1], [high])
     others.append(swap(arriving[1], "tp", 1))
-    results = [through([arriving[0], others[0]], [returned[0], arriving[1]])]
-    near_away, near_kept = through([near], [results[0][0]])
-    results.append(through([arriving[1], others[1]], [near_away]))
-    for group, (away, kept) in zip(groups, results):
+    def give_back(group, away, kept):
         mixed = total(away, kept)
         for i, k in enumerate(group):
             block = mixed if len(group) == 1 else mixed[i * capacity : (i + 1) * capacity]
             returned[k] = swap(block, "exp", k)
-    near_away = hold(near_away, [results[1][0]])
+        return mixed
+
+    away, kept = through([arriving[0], others[0]], [returned[0], high])
+    near_away, near_kept = through([near], [away])
+    mixed = give_back(groups[0], away, kept)
     returned[1] = swap(total(near_away, near_kept), "exp", 1)
-
+    away, kept = through([arriving[1], others[1]], [near_away, mixed])
+    give_back(groups[1], away, kept)
     hidden_half = call(
         functools.partial(combine, experts),
         [shape_of((token_count, half))],
@@ -355,15 +369,22 @@
         flops=4 * 3 * token_count * token_count * half,
     )[0]
 
+    def exchange(block, pairs):
+        targets = {i: i for i in range(sections * tp_size)}
+        for a, b in pairs:
+            targets |= {a: b, b: a}
+        return lax.ppermute(block, ("sec", "tp"), list(targets.items()))
+
     first = hidden_half
-    for i in range(1, sections // 2):
-        moved = lax.ppermute(hidden_half, "sec", [(0, 2 * i)])
-        first = jnp.where(sec == 2 * i, moved, first)
-    for i in range(sections // 2 - 1, -1, -1):
-        pairs = [(t, (2 * i + 1) * tp_size + (t ^ 1)) for t in range(tp_size)]
-        moved = lax.ppermute(hidden_half, ("sec", "tp"), pairs)
-        first = jnp.where(sec == 2 * i + 1, moved, first)
-    hidden_other = swap(hidden_half, "tp", 1)
+    for i in range(sections // 2 - 1, 0, -1):
+        odd = [(t, (2 * i + 1) * tp_size + (t ^ 1)) for t in range(tp_size)]
+        even = [(t, 2 * i * tp_size + t) for t in range(tp_size)]
+        first = jnp.where(sec == 2 * i + 1, exchange(hidden_half, odd), first)
+        first = jnp.where(sec == 2 * i, exchange(hidden_half, even), first)
+    odd = [(t, tp_size + (t ^ 1)) for t in range(tp_size)]
+    first = jnp.where(sec == 1, exchange(hidden_half, odd), first)
+    halves = [(s * tp_size, s * tp_size + 1) for s in range(1, sections)]
+    hidden_other = exchange(hidden_half, halves)
     beside = swap(first, "sec", 1)
     mine = jnp.where(sec % 2 == 0, first, beside)
     other = jnp.where(sec % 2 == 0, beside, first)

time: 86.9 us -> 86.7 us (level)
  starting transfers between devices: 34.2 us -> 40.6 us
  waiting for transfers between devices: 32.5 us -> 27.3 us
  local copies, waits for them, and re-layouts: 4.36 us -> 2.94 us
    ppermute x15 -> x14, waiting for transfers between devices: 26.4 us -> 16.2 us  [swap(): return lax.ppermute(block, axis, [(i, i ^ step) for i in range(size)])]
    ppermute x3 -> x4, waiting for transfers between devices: 1.88 us -> 6.75 us  [exchange(): return lax.ppermute(block, ('sec', 'tp'), list(targets.items()))]
    ppermute x15 -> x14, starting transfers between devices: 23.6 us -> 28.2 us  [swap(): return lax.ppermute(block, axis, [(i, i ^ step) for i in range(size)])]
    ppermute x3, starting transfers between devices: 3.89 us -> 5.72 us  [shards(): total = total + lax.ppermute(blocks[k], ('sec', 'tp'), pairs).astype(WIDE)]
    unnamed x24 -> x20, local copies, waits for them, and re-layouts: 4.36 us -> 2.94 us
    ppermute x3 -> x4, starting transfers between devices: 6.72 us -> 6.68 us  [exchange(): return lax.ppermute(block, ('sec', 'tp'), list(targets.items()))]
    pallas_call x13 -> x12, Pallas kernels: 13.8 us -> 13.8 us  [call(): pl.pallas_call(run, out_shape=[*out_shape, *(shape_of(x.shape, x.dtype) f...]
  transfers between devices with their start and end apart: 21 -> 21, of which waited for: 11 -> 15; matrix products, arithmetic and copies ran while one was open for 0% -> 0% of each run, Pallas kernels for 13% -> 13%
where the time goes in v6:
time: 86.7 us; the launch traced here: 86.4 us
  starting transfers between devices  40.6 us (47%)
  waiting for transfers between devices  27.3 us (31%)
  Pallas kernels  13.8 us (16%)
  local copies, waits for them, and re-layouts  2.94 us (3%)
  other arithmetic  0.97 us (1%)
  between operations  0.9 us (1%)
    ppermute x14, starting transfers between devices, swap(): return lax.ppermute(block, axis, [(i, i ^ step) for i in range(size)])  28.2 us
    ppermute x14, waiting for transfers between devices, swap(): return lax.ppermute(block, axis, [(i, i ^ step) for i in range(size)])  16.2 us
    pallas_call x12, Pallas kernels, call(): pl.pallas_call(run, out_shape=[*out_shape, *(shape_of(x.shape, x.dtype) f...  13.8 us
    ppermute x4, waiting for transfers between devices, exchange(): return lax.ppermute(block, ('sec', 'tp'), list(targets.items()))  6.75 us
    ppermute x4, starting transfers between devices, exchange(): return lax.ppermute(block, ('sec', 'tp'), list(targets.items()))  6.68 us
    ppermute x3, starting transfers between devices, shards(): total = total + lax.ppermute(blocks[k], ('sec', 'tp'), pairs).astype(WIDE)  5.72 us
    ppermute x3, waiting for transfers between devices, shards(): total = total + lax.ppermute(blocks[k], ('sec', 'tp'), pairs).astype(WIDE)  4.28 us
    unnamed x20, local copies, waits for them, and re-layouts  2.94 us
  transfers between devices with their start and end apart: 21, of which 15 were waited for; matrix products, arithmetic and copies ran while one was open for 0% of the time, Pallas kernels for 13%

profile of v6, /device:TPU:0, one launch (start us, length us, event | category | flops | bytes accessed | tf_op | source)
XLA Modules:
  0.0 86.4 jit_solution(3109638935226361578)
XLA Ops:
  0.7 1.0 %copy-done.1 = bf16[1,256,1024]{2,1,0:T(8,128)(2,1)S(1)} copy-done((bf16[1,256,1024]{2,1,0:T(8,128)(2,1)S(1)}, bf16[1,256,1024]{2,1,0:T(8,128)(2,1)}, u32[]{:S(2)}) %copy-start.1) | copy-done | bytes 524312
  1.7 0.9 %shard_map.123 = (bf16[192,512]{1,0:T(8,128)(2,1)S(1)}, bf16[192,512]{1,0:T(8,128)(2,1)S(1)}, bf16[192,1024]{1,0:T(8,128)(2,1)S(1)}, bf16[192,1024]{1,0:T(8,128)(2,1)S(1)}) custom-call(bf16[256,1024]{1,0:T(8,128)(2,1)S(1)} %bitcast.15, s32[2,256]{1,0:T(2,128)S(1)} %bitcast.17, f32[1,1024]{1,0:T(1,128)S(1)} %copy-done.8, ...), custom_call_target="tpu_custom_call" | custom-call | flops 402653184 | bytes 1841152 | tf_op jit(solution)/shard_map/pallas_call | solution.py:40
  2.6 4.1 %collective-permute-start = (bf16[192,512]{1,0:T(8,128)(2,1)S(1)}, bf16[192,512]{1,0:T(8,128)(2,1)S(1)}, u32[]{:S(2)}, u32[]{:S(2)}) collective-permute-start(bf16[192,512]{1,0:T(8,128)(2,1)S(1)} %get-tuple-element.31), channel_id=1, source_target_pairs={{0,4},{2,6},{4,0},{6,2},{1,5},{3,7},{5,1},{7,3},{8,12},{10,14},{12... | collective-permute-start | bytes 589832 | tf_op jit(solution)/shard_map/ppermute | solution.py:252
  6.7 4.6 %shard_map.124 = (bf16[192,512]{1,0:T(8,128)(2,1)S(1)}, f32[192,512]{1,0:T(8,128)S(1)}, bf16[1024,2048]{1,0:T(8,128)(2,1)S(1)}, bf16[2048,1024]{1,0:T(8,128)(2,1...) custom-call(bf16[192,1024]{1,0:T(8,128)(2,1)S(1)} %get-tuple-element, ...), custom_call_target="tpu_custom_call", output_to_operand_aliasing={{4}: (3, {}), {5}: (4, {})} | custom-call | flops 1610612736 | bytes 17760256 | tf_op jit(solution)/shard_map/pallas_call | solution.py:40
  11.2 1.6 %collective-permute-start.1 = (bf16[192,512]{1,0:T(8,128)(2,1)S(1)}, bf16[192,512]{1,0:T(8,128)(2,1)S(1)}, u32[]{:S(2)}, u32[]{:S(2)}) collective-permute-start(bf16[192,512]{1,0:T(8,128)(2,1)S(1)} %get-tuple-element.30.refs_0_), channel_id=1, source_target_pairs={{0,1},{1,0},{2,3},{3,2},{4,5},{5,4},{6,7},{7,6},{8,9},{9,8},{10,11... | collective-permute-start | bytes 589832 | tf_op jit(solution)/shard_map/ppermute | solution.py:252
  12.8 1.6 %collective-permute-start.2 = (bf16[192,1024]{1,0:T(8,128)(2,1)S(1)}, bf16[192,1024]{1,0:T(8,128)(2,1)S(1)}, u32[]{:S(2)}, u32[]{:S(2)}) collective-permute-start(bf16[192,1024]{1,0:T(8,128)(2,1)S(1)} %get-tuple-element.35), channel_id=1, source_target_pairs={{0,2},{2,0},{4,6},{6,4},{1,3},{3,1},{5,7},{7,5},{8,10},{10,8},{12,... | collective-permute-start | bytes 1179656 | tf_op jit(solution)/shard_map/ppermute | solution.py:252
  14.4 0.2 collective-permute-start.8
  14.6 1.3 %collective-permute-done.refs_1_ = bf16[192,512]{1,0:T(8,128)(2,1)S(1)} collective-permute-done((bf16[192,512]{1,0:T(8,128)(2,1)S(1)}, bf16[192,512]{1,0:T(8,128)(2,1)S(1)}, u32[]{:S(2)}, u32[]{:S(2)}) %collective-permute-start) | collective-permute-done | bytes 196640 | tf_op jit(solution)/shard_map/ppermute | solution.py:252
  15.9 2.4 %collective-permute-start.3 = (bf16[192,512]{1,0:T(8,128)(2,1)S(1)}, bf16[192,512]{1,0:T(8,128)(2,1)S(1)}, u32[]{:S(2)}, u32[]{:S(2)}) collective-permute-start(bf16[192,512]{1,0:T(8,128)(2,1)S(1)} %shard_map.125.refs_3_.refs_0_), channel_id=1, source_target_pairs={{0,1},{1,0},{2,3},{3,2},{4,5},{5,4},{6,7},{7,6},{8,9},{9,8},{10,11... | collective-permute-start | bytes 589832 | tf_op jit(solution)/shard_map/ppermute | solution.py:252
  18.2 0.6 shard_map.126
  18.9 3.0 %collective-permute-done.3.refs_1_ = bf16[192,512]{1,0:T(8,128)(2,1)S(1)} collective-permute-done((bf16[192,512]{1,0:T(8,128)(2,1)S(1)}, bf16[192,512]{1,0:T(8,128)(2,1)S(1)}, u32[]{:S(2)}, u32[]{:S(2)}) %collective-permute-start.3) | collective-permute-done | bytes 196640 | tf_op jit(solution)/shard_map/ppermute | solution.py:252
  21.9 1.9 %shard_map.127 = (bf16[192,512]{1,0:T(8,128)(2,1)S(1)}, f32[192,512]{1,0:T(8,128)S(1)}) custom-call(bf16[192,512]{1,0:T(8,128)(2,1)S(1)} %shard_map.125.refs_3_.refs_0_, bf16[192,512]{1,0:T(8,128)(2,1)S(1)} %collective-permute-done.3.refs_1_, bf16[1024,2048]{1,0:T(8,128)(2,1)S(1)} %get-tuple-element.36.refs_2_.refs_1_, ...), custom_call_target="tpu_custom_call" | custom-call | flops 1610612736 | bytes 9371648 | tf_op jit(solution)/shard_map/pallas_call | solution.py:40
  23.8 2.1 %collective-permute-start.6 = (bf16[192,512]{1,0:T(8,128)(2,1)S(1)}, bf16[192,512]{1,0:T(8,128)(2,1)S(1)}, u32[]{:S(2)}, u32[]{:S(2)}) collective-permute-start(bf16[192,512]{1,0:T(8,128)(2,1)S(1)} %get-tuple-element.38.refs_3_), channel_id=1, source_target_pairs={{0,1},{1,0},{2,3},{3,2},{4,5},{5,4},{6,7},{7,6},{8,9},{9,8},{10,11... | collective-permute-start | bytes 589832 | tf_op jit(solution)/shard_map/ppermute | solution.py:252
  25.9 1.4 %collective-permute-done.8.refs_0_ = bf16[192,512]{1,0:T(8,128)(2,1)S(1)} collective-permute-done((bf16[192,512]{1,0:T(8,128)(2,1)S(1)}, bf16[192,512]{1,0:T(8,128)(2,1)S(1)}, u32[]{:S(2)}, u32[]{:S(2)}) %collective-permute-start.8) | collective-permute-done | bytes 196640 | tf_op jit(solution)/shard_map/ppermute | solution.py:252
  27.2 0.5 collective-permute-start.9
  27.7 0.7 collective-permute-done.2.refs_0_
  28.4 1.8 %shard_map.128 = (bf16[192,512]{1,0:T(8,128)(2,1)S(1)}, f32[192,512]{1,0:T(8,128)S(1)}) custom-call(bf16[192,1024]{1,0:T(8,128)(2,1)S(1)} %collective-permute-done.2.refs_0_, bf16[1024,2048]{1,0:T(8,128)(2,1)S(1)} %get-tuple-element.36.refs_2_.refs_1_, bf16[2048,1024]{1,0:T(8,128)(2,1)S(1)} %get-tuple-element.37.refs_3_.refs_2_, ...), custom_call_target="tpu_custom_call" | custom-call | flops 1610612736 | bytes 9371648 | tf_op jit(solution)/shard_map/pallas_call | solution.py:40
  30.2 1.6 %collective-permute-start.4 = (bf16[192,512]{1,0:T(8,128)(2,1)S(1)}, bf16[192,512]{1,0:T(8,128)(2,1)S(1)}, u32[]{:S(2)}, u32[]{:S(2)}) collective-permute-start(bf16[192,512]{1,0:T(8,128)(2,1)S(1)} %get-tuple-element.40.refs_4_), channel_id=1, source_target_pairs={{0,1},{1,0},{2,3},{3,2},{4,5},{5,4},{6,7},{7,6},{8,9},{9,8},{10,11... | collective-permute-start | bytes 589832 | tf_op jit(solution)/shard_map/ppermute | solution.py:252
  31.9 1.5 %collective-permute-start.7 = (bf16[192,512]{1,0:T(8,128)(2,1)S(1)}, bf16[192,512]{1,0:T(8,128)(2,1)S(1)}, u32[]{:S(2)}, u32[]{:S(2)}) collective-permute-start(bf16[192,512]{1,0:T(8,128)(2,1)S(1)} %add_convert_fusion.1.refs_5_), channel_id=1, source_target_pairs={{0,4},{2,6},{4,0},{6,2},{1,5},{3,7},{5,1},{7,3},{8,12},{10,14},{12... | collective-permute-start | bytes 589832 | tf_op jit(solution)/shard_map/ppermute | solution.py:252
  33.4 1.3 %collective-permute-done.9.refs_1_ = bf16[192,512]{1,0:T(8,128)(2,1)S(1)} collective-permute-done((bf16[192,512]{1,0:T(8,128)(2,1)S(1)}, bf16[192,512]{1,0:T(8,128)(2,1)S(1)}, u32[]{:S(2)}, u32[]{:S(2)}) %collective-permute-start.9) | collective-permute-done | bytes 196640 | tf_op jit(solution)/shard_map/ppermute | solution.py:252
  34.7 1.8 %shard_map.129 = (bf16[192,512]{1,0:T(8,128)(2,1)S(1)}, f32[192,512]{1,0:T(8,128)S(1)}) custom-call(bf16[192,512]{1,0:T(8,128)(2,1)S(1)} %collective-permute-done.8.refs_0_, bf16[192,512]{1,0:T(8,128)(2,1)S(1)} %collective-permute-done.9.refs_1_, bf16[1024,2048]{1,0:T(8,128)(2,1)S(1)} %get-tuple-element.36.refs_2_.refs_1_, ...), custom_call_target="tpu_custom_call" | custom-call | flops 1610612736 | bytes 9371648 | tf_op jit(solution)/shard_map/pallas_call | solution.py:40
  36.6 1.2 %collective-permute-start.10 = (bf16[192,512]{1,0:T(8,128)(2,1)S(1)}, bf16[192,512]{1,0:T(8,128)(2,1)S(1)}, u32[]{:S(2)}, u32[]{:S(2)}) collective-permute-start(bf16[192,512]{1,0:T(8,128)(2,1)S(1)} %get-tuple-element.44), channel_id=1, source_target_pairs={{0,1},{1,0},{2,3},{3,2},{4,5},{5,4},{6,7},{7,6},{8,9},{9,8},{10,11... | collective-permute-start | bytes 589832 | tf_op jit(solution)/shard_map/ppermute | solution.py:252
  37.7 0.8 collective-permute-done.4
  38.6 2.3 %collective-permute-start.5 = (bf16[192,512]{1,0:T(8,128)(2,1)S(1)}, bf16[192,512]{1,0:T(8,128)(2,1)S(1)}, u32[]{:S(2)}, u32[]{:S(2)}) collective-permute-start(bf16[192,512]{1,0:T(8,128)(2,1)S(1)} %add_convert_fusion.2), channel_id=1, source_target_pairs={{0,2},{2,0},{4,6},{6,4},{1,3},{3,1},{5,7},{7,5},{8,10},{10,8},{12,... | collective-permute-start | bytes 589832 | tf_op jit(solution)/shard_map/ppermute | solution.py:252
  41.0 1.3 %collective-permute-done.10 = bf16[192,512]{1,0:T(8,128)(2,1)S(1)} collective-permute-done((bf16[192,512]{1,0:T(8,128)(2,1)S(1)}, bf16[192,512]{1,0:T(8,128)(2,1)S(1)}, u32[]{:S(2)}, u32[]{:S(2)}) %collective-permute-start.10) | collective-permute-done | bytes 196640 | tf_op jit(solution)/shard_map/ppermute | solution.py:252
  42.3 5.2 %collective-permute-start.11 = (bf16[192,512]{1,0:T(8,128)(2,1)S(1)}, bf16[192,512]{1,0:T(8,128)(2,1)S(1)}, u32[]{:S(2)}, u32[]{:S(2)}) collective-permute-start(bf16[192,512]{1,0:T(8,128)(2,1)S(1)} %add_convert_fusion), channel_id=1, source_target_pairs={{0,6},{2,4},{4,2},{6,0},{1,7},{3,5},{5,3},{7,1},{8,14},{10,12},{12... | collective-permute-start | bytes 589832 | tf_op jit(solution)/shard_map/ppermute | solution.py:252
  47.6 1.7 %collective-permute-done.5.refs_4_ = bf16[192,512]{1,0:T(8,128)(2,1)S(1)} collective-permute-done((bf16[192,512]{1,0:T(8,128)(2,1)S(1)}, bf16[192,512]{1,0:T(8,128)(2,1)S(1)}, u32[]{:S(2)}, u32[]{:S(2)}) %collective-permute-start.5) | collective-permute-done | bytes 196640 | tf_op jit(solution)/shard_map/ppermute | solution.py:252
  49.2 2.8 %collective-permute-done.11.refs_6_ = bf16[192,512]{1,0:T(8,128)(2,1)S(1)} collective-permute-done((bf16[192,512]{1,0:T(8,128)(2,1)S(1)}, bf16[192,512]{1,0:T(8,128)(2,1)S(1)}, u32[]{:S(2)}, u32[]{:S(2)}) %collective-permute-start.11) | collective-permute-done | bytes 196640 | tf_op jit(solution)/shard_map/ppermute | solution.py:252
  52.0 0.7 shard_map.130.refs_0_.refs_6_
  52.7 1.9 %collective-permute-start.12 = (bf16[256,512]{1,0:T(8,128)(2,1)S(1)}, bf16[256,512]{1,0:T(8,128)(2,1)S(1)}, u32[]{:S(2)}, u32[]{:S(2)}) collective-permute-start(bf16[256,512]{1,0:T(8,128)(2,1)S(1)} %shard_map.130.refs_0_.refs_6_), channel_id=1, source_target_pairs={{0,9},{1,8},{8,1},{9,0},{16,16},{17,17},{24,24},{25,25},{2,11},{3,... | collective-permute-start | bytes 786440 | tf_op jit(solution)/shard_map/ppermute | solution.py:376
  54.6 2.2 %collective-permute-start.13 = (bf16[256,512]{1,0:T(8,128)(2,1)S(1)}, bf16[256,512]{1,0:T(8,128)(2,1)S(1)}, u32[]{:S(2)}, u32[]{:S(2)}) collective-permute-start(bf16[256,512]{1,0:T(8,128)(2,1)S(1)} %shard_map.130.refs_0_.refs_6_), channel_id=1, source_target_pairs={{0,16},{1,17},{8,8},{9,9},{16,0},{17,1},{24,24},{25,25},{2,18},{3,... | collective-permute-start | bytes 786440 | tf_op jit(solution)/shard_map/ppermute | solution.py:376
  56.8 1.9 %collective-permute-start.14 = (bf16[256,512]{1,0:T(8,128)(2,1)S(1)}, bf16[256,512]{1,0:T(8,128)(2,1)}, u32[]{:S(2)}, u32[]{:S(2)}) collective-permute-start(bf16[256,512]{1,0:T(8,128)(2,1)S(1)} %shard_map.130.refs_0_.refs_6_), channel_id=1, source_target_pairs={{0,25},{1,24},{8,8},{9,9},{16,16},{17,17},{24,1},{25,0},{2,27},{3,... | collective-permute-start | bytes 786440 | tf_op jit(solution)/shard_map/ppermute | solution.py:376
  58.7 0.7 collective-permute-start.16
  59.4 4.1 %collective-permute-done.12 = bf16[256,512]{1,0:T(8,128)(2,1)S(1)} collective-permute-done((bf16[256,512]{1,0:T(8,128)(2,1)S(1)}, bf16[256,512]{1,0:T(8,128)(2,1)S(1)}, u32[]{:S(2)}, u32[]{:S(2)}) %collective-permute-start.12) | collective-permute-done | bytes 262176 | tf_op jit(solution)/shard_map/ppermute | solution.py:376
  63.6 0.7 copy-done.9
  64.3 2.6 %collective-permute-done.14 = bf16[256,512]{1,0:T(8,128)(2,1)} collective-permute-done((bf16[256,512]{1,0:T(8,128)(2,1)S(1)}, bf16[256,512]{1,0:T(8,128)(2,1)}, u32[]{:S(2)}, u32[]{:S(2)}) %collective-permute-start.14) | collective-permute-done | bytes 262176 | tf_op jit(solution)/shard_map/ppermute | solution.py:376
  67.1 0.7 shard_map.131.refs_2_
  67.8 0.8 collective-permute-done.15
  68.6 1.2 %copy-done.6 = bf16[1,1024,512]{2,1,0:T(8,128)(2,1)S(1)} copy-done((bf16[1,1024,512]{2,1,0:T(8,128)(2,1)S(1)}, bf16[1,1024,512]{2,1,0:T(8,128)(2,1)}, u32[]{:S(2)}) %copy-start.6) | copy-done | bytes 1048600
  69.9 0.8 shard_map.132
  70.6 3.9 %collective-permute-start.17 = (bf16[256,512]{1,0:T(8,128)(2,1)S(1)}, bf16[256,512]{1,0:T(8,128)(2,1)S(1)}, u32[]{:S(2)}, u32[]{:S(2)}) collective-permute-start(bf16[256,512]{1,0:T(8,128)(2,1)S(1)} %get-tuple-element.47), channel_id=1, source_target_pairs={{0,8},{8,0},{16,24},{24,16},{1,9},{9,1},{17,25},{25,17},{2,10},{10... | collective-permute-start | bytes 786440 | tf_op jit(solution)/shard_map/ppermute | solution.py:252
  74.5 1.2 %collective-permute-done.17.refs_1_ = bf16[256,512]{1,0:T(8,128)(2,1)S(1)} collective-permute-done((bf16[256,512]{1,0:T(8,128)(2,1)S(1)}, bf16[256,512]{1,0:T(8,128)(2,1)S(1)}, u32[]{:S(2)}, u32[]{:S(2)}) %collective-permute-start.17) | collective-permute-done | bytes 262176 | tf_op jit(solution)/shard_map/ppermute | solution.py:252
  75.8 0.7 collective-permute-start.18
  76.4 4.2 %collective-permute-start.19 = (bf16[256,128]{1,0:T(8,128)(2,1)S(1)}, bf16[256,128]{1,0:T(8,128)(2,1)S(1)}, u32[]{:S(2)}, u32[]{:S(2)}) collective-permute-start(bf16[256,128]{1,0:T(8,128)(2,1)S(1)} %get-tuple-element.50), channel_id=1, source_target_pairs={{0,16},{1,17},{8,24},{9,25},{16,0},{17,1},{24,8},{25,9},{2,18},{3,... | collective-permute-start | bytes 196616 | tf_op jit(solution)/shard_map/ppermute | solution.py:426
  80.6 0.9 %collective-permute-start.20 = (bf16[256,128]{1,0:T(8,128)(2,1)S(1)}, bf16[256,128]{1,0:T(8,128)(2,1)S(1)}, u32[]{:S(2)}, u32[]{:S(2)}) collective-permute-start(bf16[256,128]{1,0:T(8,128)(2,1)S(1)} %get-tuple-element.51), channel_id=1, source_target_pairs={{0,17},{1,16},{8,25},{9,24},{16,1},{17,0},{24,9},{25,8},{2,19},{3,... | collective-permute-start | bytes 196616 | tf_op jit(solution)/shard_map/ppermute | solution.py:426
  81.5 1.4 %collective-permute-done.19 = bf16[256,128]{1,0:T(8,128)(2,1)S(1)} collective-permute-done((bf16[256,128]{1,0:T(8,128)(2,1)S(1)}, bf16[256,128]{1,0:T(8,128)(2,1)S(1)}, u32[]{:S(2)}, u32[]{:S(2)}) %collective-permute-start.19) | collective-permute-done | bytes 65568 | tf_op jit(solution)/shard_map/ppermute | solution.py:426
  82.9 2.9 %collective-permute-done.20 = bf16[256,128]{1,0:T(8,128)(2,1)S(1)} collective-permute-done((bf16[256,128]{1,0:T(8,128)(2,1)S(1)}, bf16[256,128]{1,0:T(8,128)(2,1)S(1)}, u32[]{:S(2)}, u32[]{:S(2)}) %collective-permute-start.20) | collective-permute-done | bytes 65568 | tf_op jit(solution)/shard_map/ppermute | solution.py:426
  85.8 0.7 add_convert_fusion.4
  (33 shorter events, 0.6 us)
Async XLA Ops:
  0.6 1.0 %copy-start.1 = (bf16[1,256,1024]{2,1,0:T(8,128)(2,1)S(1)}, bf16[1,256,1024]{2,1,0:T(8,128)(2,1)}, u32[]{:S(2)}) copy-start(bf16[1,256,1024]{2,1,0:T(8,128)(2,1)} %param.11) | copy-start | bytes 1572868
  0.6 1.0 %copy-start.3 = (s32[1,256,2]{1,2,0:T(2,128)S(1)}, s32[1,256,2]{1,2,0:T(2,128)}, u32[]{:S(2)}) copy-start(s32[1,256,2]{1,2,0:T(2,128)} %param.12) | copy-start | bytes 6148
  0.6 1.0 %copy-start.8 = (f32[1,1024]{1,0:T(1,128)S(1)}, f32[1,1024]{1,0:T(1,128)}, u32[]{:S(2)}) copy-start(f32[1,1024]{1,0:T(1,128)} %refs_2_.2) | copy-start | bytes 12292
  2.6 13.3 %collective-permute-start = (bf16[192,512]{1,0:T(8,128)(2,1)S(1)}, bf16[192,512]{1,0:T(8,128)(2,1)S(1)}, u32[]{:S(2)}, u32[]{:S(2)}) collective-permute-start(bf16[192,512]{1,0:T(8,128)(2,1)S(1)} %get-tuple-element.31), channel_id=1, source_target_pairs={{0,4},{2,6},{4,0},{6,2},{1,5},{3,7},{5,1},{7,3},{8,12},{10,14},{12... | collective-permute-start | bytes 589832 | tf_op jit(solution)/shard_map/ppermute | solution.py:252
  6.7 11.6 %copy-start.4 = (f32[1,256,2]{1,2,0:T(2,128)S(1)}, f32[1,256,2]{1,2,0:T(2,128)}, u32[]{:S(2)}) copy-start(f32[1,256,2]{1,2,0:T(2,128)} %param.13) | copy-start | bytes 6148
  11.2 7.6 %collective-permute-start.1 = (bf16[192,512]{1,0:T(8,128)(2,1)S(1)}, bf16[192,512]{1,0:T(8,128)(2,1)S(1)}, u32[]{:S(2)}, u32[]{:S(2)}) collective-permute-start(bf16[192,512]{1,0:T(8,128)(2,1)S(1)} %get-tuple-element.30.refs_0_), channel_id=1, source_target_pairs={{0,1},{1,0},{2,3},{3,2},{4,5},{5,4},{6,7},{7,6},{8,9},{9,8},{10,11... | collective-permute-start | bytes 589832 | tf_op jit(solution)/shard_map/ppermute | solution.py:252
  12.8 15.6 %collective-permute-start.2 = (bf16[192,1024]{1,0:T(8,128)(2,1)S(1)}, bf16[192,1024]{1,0:T(8,128)(2,1)S(1)}, u32[]{:S(2)}, u32[]{:S(2)}) collective-permute-start(bf16[192,1024]{1,0:T(8,128)(2,1)S(1)} %get-tuple-element.35), channel_id=1, source_target_pairs={{0,2},{2,0},{4,6},{6,4},{1,3},{3,1},{5,7},{7,5},{8,10},{10,8},{12,... | collective-permute-start | bytes 1179656 | tf_op jit(solution)/shard_map/ppermute | solution.py:252
  14.4 12.8 %collective-permute-start.8 = (bf16[192,512]{1,0:T(8,128)(2,1)S(1)}, bf16[192,512]{1,0:T(8,128)(2,1)S(1)}, u32[]{:S(2)}, u32[]{:S(2)}) collective-permute-start(bf16[192,512]{1,0:T(8,128)(2,1)S(1)} %get-tuple-element.42), channel_id=1, source_target_pairs={{0,6},{2,4},{4,2},{6,0},{1,7},{3,5},{5,3},{7,1},{8,14},{10,12},{12... | collective-permute-start | bytes 589832 | tf_op jit(solution)/shard_map/ppermute | solution.py:252
  15.9 6.0 %collective-permute-start.3 = (bf16[192,512]{1,0:T(8,128)(2,1)S(1)}, bf16[192,512]{1,0:T(8,128)(2,1)S(1)}, u32[]{:S(2)}, u32[]{:S(2)}) collective-permute-start(bf16[192,512]{1,0:T(8,128)(2,1)S(1)} %shard_map.125.refs_3_.refs_0_), channel_id=1, source_target_pairs={{0,1},{1,0},{2,3},{3,2},{4,5},{5,4},{6,7},{7,6},{8,9},{9,8},{10,11... | collective-permute-start | bytes 589832 | tf_op jit(solution)/shard_map/ppermute | solution.py:252
  23.8 8.1 %collective-permute-start.6 = (bf16[192,512]{1,0:T(8,128)(2,1)S(1)}, bf16[192,512]{1,0:T(8,128)(2,1)S(1)}, u32[]{:S(2)}, u32[]{:S(2)}) collective-permute-start(bf16[192,512]{1,0:T(8,128)(2,1)S(1)} %get-tuple-element.38.refs_3_), channel_id=1, source_target_pairs={{0,1},{1,0},{2,3},{3,2},{4,5},{5,4},{6,7},{7,6},{8,9},{9,8},{10,11... | collective-permute-start | bytes 589832 | tf_op jit(solution)/shard_map/ppermute | solution.py:252
  27.2 7.5 %collective-permute-start.9 = (bf16[192,512]{1,0:T(8,128)(2,1)S(1)}, bf16[192,512]{1,0:T(8,128)(2,1)S(1)}, u32[]{:S(2)}, u32[]{:S(2)}) collective-permute-start(bf16[192,512]{1,0:T(8,128)(2,1)S(1)} %collective-permute-done.8.refs_0_), channel_id=1, source_target_pairs={{0,1},{1,0},{2,3},{3,2},{4,5},{5,4},{6,7},{7,6},{8,9},{9,8},{10,11... | collective-permute-start | bytes 589832 | tf_op jit(solution)/shard_map/ppermute | solution.py:252
  30.2 8.3 %collective-permute-start.4 = (bf16[192,512]{1,0:T(8,128)(2,1)S(1)}, bf16[192,512]{1,0:T(8,128)(2,1)S(1)}, u32[]{:S(2)}, u32[]{:S(2)}) collective-permute-start(bf16[192,512]{1,0:T(8,128)(2,1)S(1)} %get-tuple-element.40.refs_4_), channel_id=1, source_target_pairs={{0,1},{1,0},{2,3},{3,2},{4,5},{5,4},{6,7},{7,6},{8,9},{9,8},{10,11... | collective-permute-start | bytes 589832 | tf_op jit(solution)/shard_map/ppermute | solution.py:252
  31.9 15.6 %collective-permute-start.7 = (bf16[192,512]{1,0:T(8,128)(2,1)S(1)}, bf16[192,512]{1,0:T(8,128)(2,1)S(1)}, u32[]{:S(2)}, u32[]{:S(2)}) collective-permute-start(bf16[192,512]{1,0:T(8,128)(2,1)S(1)} %add_convert_fusion.1.refs_5_), channel_id=1, source_target_pairs={{0,4},{2,6},{4,0},{6,2},{1,5},{3,7},{5,1},{7,3},{8,12},{10,14},{12... | collective-permute-start | bytes 589832 | tf_op jit(solution)/shard_map/ppermute | solution.py:252
  36.5 30.5 %copy-start = (bf16[1,1024,512]{2,1,0:T(8,128)(2,1)S(1)}, bf16[1,1024,512]{2,1,0:T(8,128)(2,1)}, u32[]{:S(2)}) copy-start(bf16[1,1024,512]{2,1,0:T(8,128)(2,1)} %param.18) | copy-start | bytes 3145732
  36.6 30.5 %copy-start.2 = (f32[1,1024]{1,0:T(1,128)S(1)}, f32[1,1024]{1,0:T(1,128)}, u32[]{:S(2)}) copy-start(f32[1,1024]{1,0:T(1,128)} %refs_2_.3) | copy-start | bytes 12292
  36.6 5.7 %collective-permute-start.10 = (bf16[192,512]{1,0:T(8,128)(2,1)S(1)}, bf16[192,512]{1,0:T(8,128)(2,1)S(1)}, u32[]{:S(2)}, u32[]{:S(2)}) collective-permute-start(bf16[192,512]{1,0:T(8,128)(2,1)S(1)} %get-tuple-element.44), channel_id=1, source_target_pairs={{0,1},{1,0},{2,3},{3,2},{4,5},{5,4},{6,7},{7,6},{8,9},{9,8},{10,11... | collective-permute-start | bytes 589832 | tf_op jit(solution)/shard_map/ppermute | solution.py:252
  38.6 30.0 %copy-start.5 = (bf16[1,1024,512]{2,1,0:T(8,128)(2,1)S(1)}, bf16[1,1024,512]{2,1,0:T(8,128)(2,1)}, u32[]{:S(2)}) copy-start(bf16[1,1024,512]{2,1,0:T(8,128)(2,1)} %param.19) | copy-start | bytes 3145732
  38.6 30.0 %copy-start.7 = (bf16[1,256,512]{2,1,0:T(8,128)(2,1)S(1)}, bf16[1,256,512]{2,1,0:T(8,128)(2,1)}, u32[]{:S(2)}) copy-start(bf16[1,256,512]{2,1,0:T(8,128)(2,1)} %param.21) | copy-start | bytes 786436
  38.6 10.6 %collective-permute-start.5 = (bf16[192,512]{1,0:T(8,128)(2,1)S(1)}, bf16[192,512]{1,0:T(8,128)(2,1)S(1)}, u32[]{:S(2)}, u32[]{:S(2)}) collective-permute-start(bf16[192,512]{1,0:T(8,128)(2,1)S(1)} %add_convert_fusion.2), channel_id=1, source_target_pairs={{0,2},{2,0},{4,6},{6,4},{1,3},{3,1},{5,7},{7,5},{8,10},{10,8},{12,... | collective-permute-start | bytes 589832 | tf_op jit(solution)/shard_map/ppermute | solution.py:252
  42.3 9.6 %collective-permute-start.11 = (bf16[192,512]{1,0:T(8,128)(2,1)S(1)}, bf16[192,512]{1,0:T(8,128)(2,1)S(1)}, u32[]{:S(2)}, u32[]{:S(2)}) collective-permute-start(bf16[192,512]{1,0:T(8,128)(2,1)S(1)} %add_convert_fusion), channel_id=1, source_target_pairs={{0,6},{2,4},{4,2},{6,0},{1,7},{3,5},{5,3},{7,1},{8,14},{10,12},{12... | collective-permute-start | bytes 589832 | tf_op jit(solution)/shard_map/ppermute | solution.py:252
  52.7 10.9 %collective-permute-start.12 = (bf16[256,512]{1,0:T(8,128)(2,1)S(1)}, bf16[256,512]{1,0:T(8,128)(2,1)S(1)}, u32[]{:S(2)}, u32[]{:S(2)}) collective-permute-start(bf16[256,512]{1,0:T(8,128)(2,1)S(1)} %shard_map.130.refs_0_.refs_6_), channel_id=1, source_target_pairs={{0,9},{1,8},{8,1},{9,0},{16,16},{17,17},{24,24},{25,25},{2,11},{3,... | collective-permute-start | bytes 786440 | tf_op jit(solution)/shard_map/ppermute | solution.py:376
  54.6 8.9 %collective-permute-start.13 = (bf16[256,512]{1,0:T(8,128)(2,1)S(1)}, bf16[256,512]{1,0:T(8,128)(2,1)S(1)}, u32[]{:S(2)}, u32[]{:S(2)}) collective-permute-start(bf16[256,512]{1,0:T(8,128)(2,1)S(1)} %shard_map.130.refs_0_.refs_6_), channel_id=1, source_target_pairs={{0,16},{1,17},{8,8},{9,9},{16,0},{17,1},{24,24},{25,25},{2,18},{3,... | collective-permute-start | bytes 786440 | tf_op jit(solution)/shard_map/ppermute | solution.py:376
  56.8 10.1 %collective-permute-start.14 = (bf16[256,512]{1,0:T(8,128)(2,1)S(1)}, bf16[256,512]{1,0:T(8,128)(2,1)}, u32[]{:S(2)}, u32[]{:S(2)}) collective-permute-start(bf16[256,512]{1,0:T(8,128)(2,1)S(1)} %shard_map.130.refs_0_.refs_6_), channel_id=1, source_target_pairs={{0,25},{1,24},{8,8},{9,9},{16,16},{17,17},{24,1},{25,0},{2,27},{3,... | collective-permute-start | bytes 786440 | tf_op jit(solution)/shard_map/ppermute | solution.py:376
  58.7 8.3 %collective-permute-start.16 = (bf16[256,512]{1,0:T(8,128)(2,1)S(1)}, bf16[256,512]{1,0:T(8,128)(2,1)S(1)}, u32[]{:S(2)}, u32[]{:S(2)}) collective-permute-start(bf16[256,512]{1,0:T(8,128)(2,1)S(1)} %shard_map.130.refs_0_.refs_6_), channel_id=1, source_target_pairs={{0,0},{1,1},{8,9},{9,8},{16,17},{17,16},{24,25},{25,24},{2,2},{3,3... | collective-permute-start | bytes 786440 | tf_op jit(solution)/shard_map/ppermute | solution.py:376
  63.6 0.7 copy-start.9
  67.0 1.6 %collective-permute-start.15 = (bf16[256,512]{1,0:T(8,128)(2,1)S(1)}, bf16[256,512]{1,0:T(8,128)(2,1)S(1)}, u32[]{:S(2)}, u32[]{:S(2)}) collective-permute-start(bf16[256,512]{1,0:T(8,128)(2,1)S(1)} %select_select_fusion), channel_id=1, source_target_pairs={{0,8},{8,0},{16,24},{24,16},{1,9},{9,1},{17,25},{25,17},{2,10},{10... | collective-permute-start | bytes 786440 | tf_op jit(solution)/shard_map/ppermute | solution.py:252
  68.6 1.2 %copy-start.6 = (bf16[1,1024,512]{2,1,0:T(8,128)(2,1)S(1)}, bf16[1,1024,512]{2,1,0:T(8,128)(2,1)}, u32[]{:S(2)}) copy-start(bf16[1,1024,512]{2,1,0:T(8,128)(2,1)} %param.20) | copy-start | bytes 3145732
  70.6 5.0 %collective-permute-start.17 = (bf16[256,512]{1,0:T(8,128)(2,1)S(1)}, bf16[256,512]{1,0:T(8,128)(2,1)S(1)}, u32[]{:S(2)}, u32[]{:S(2)}) collective-permute-start(bf16[256,512]{1,0:T(8,128)(2,1)S(1)} %get-tuple-element.47), channel_id=1, source_target_pairs={{0,8},{8,0},{16,24},{24,16},{1,9},{9,1},{17,25},{25,17},{2,10},{10... | collective-permute-start | bytes 786440 | tf_op jit(solution)/shard_map/ppermute | solution.py:252
  75.8 5.7 %collective-permute-start.18 = (bf16[256,128]{1,0:T(8,128)(2,1)S(1)}, bf16[256,128]{1,0:T(8,128)(2,1)S(1)}, u32[]{:S(2)}, u32[]{:S(2)}) collective-permute-start(bf16[256,128]{1,0:T(8,128)(2,1)S(1)} %get-tuple-element.49), channel_id=1, source_target_pairs={{0,1},{1,0},{8,9},{9,8},{16,17},{17,16},{24,25},{25,24},{2,3},{3,2... | collective-permute-start | bytes 196616 | tf_op jit(solution)/shard_map/ppermute | solution.py:426
  76.4 6.4 %collective-permute-start.19 = (bf16[256,128]{1,0:T(8,128)(2,1)S(1)}, bf16[256,128]{1,0:T(8,128)(2,1)S(1)}, u32[]{:S(2)}, u32[]{:S(2)}) collective-permute-start(bf16[256,128]{1,0:T(8,128)(2,1)S(1)} %get-tuple-element.50), channel_id=1, source_target_pairs={{0,16},{1,17},{8,24},{9,25},{16,0},{17,1},{24,8},{25,9},{2,18},{3,... | collective-permute-start | bytes 196616 | tf_op jit(solution)/shard_map/ppermute | solution.py:426
  80.6 5.2 %collective-permute-start.20 = (bf16[256,128]{1,0:T(8,128)(2,1)S(1)}, bf16[256,128]{1,0:T(8,128)(2,1)S(1)}, u32[]{:S(2)}, u32[]{:S(2)}) collective-permute-start(bf16[256,128]{1,0:T(8,128)(2,1)S(1)} %get-tuple-element.51), channel_id=1, source_target_pairs={{0,17},{1,16},{8,25},{9,24},{16,1},{17,0},{24,9},{25,8},{2,19},{3,... | collective-permute-start | bytes 196616 | tf_op jit(solution)/shard_map/ppermute | solution.py:426

commit v7 on v6

--- a/solution.py
+++ b/solution.py
@@ -97,7 +97,15 @@
     own[...] = matmul(table(place, 0, capacity), normed).astype(LOW)
 
 
-def mixing(experts, routes, gates, earlier, high, low):
+def mixing(experts, routes, gates, earlier, *refs):
+    count = (len(refs) - 3) // 2
+    sources, (high, low), targets, arrived = refs[:count], refs[count : count + 2], refs[count + 2 : -1], refs[-1]
+    loads = [
+        pltpu.make_async_copy(source, target, arrived.at[i])
+        for i, (source, target) in enumerate(zip(sources, targets, strict=True))
+    ]
+    for load in loads:
+        load.start()
     me = lax.axis_index("exp")
     token_count = routes.shape[1]
     capacity = high.shape[2]
@@ -111,6 +119,8 @@
         upper = weight.astype(LOW)
         high[k] = upper
         low[k] = (weight - upper.astype(WIDE)).astype(LOW)
+    for load in loads:
+        load.wait()
 
 
 def expert(split, *refs):
@@ -203,20 +213,26 @@
             value = matmul(mine[...], weight[part(tp, half), :])
             value = value + matmul(other[...], weight[part(1 - tp, half), :])
             target[...] = value.astype(LOW)
-        for s in range(token_count // SEQ):
-            for h in range(queries.shape[1] // HD):
-                rows, columns = slice(s * SEQ, (s + 1) * SEQ), slice(h * HD, (h + 1) * HD)
-                query, key = queries[rows, columns], keys[rows, columns]
-                value, up = values[rows, columns], upstream[rows, columns]
-                powers = jnp.exp(matmul(key, query, NT) * scale)
-                probs = powers * (1.0 / jnp.sum(powers, axis=0, keepdims=True))
-                low = probs.astype(LOW)
-                dprobs = matmul(value, up, NT)
-                rowdot = jnp.sum(dprobs * probs, axis=0, keepdims=True)
-                dscores = (probs * (dprobs - rowdot)).astype(LOW)
-                dvalues[rows, columns] = matmul(low, up).astype(LOW)
-                dkeys[rows, columns] = (matmul(dscores, query) * scale).astype(LOW)
-                context[rows, columns] = matmul(low, value, TN).astype(LOW)
+        heads = [
+            (slice(s * SEQ, (s + 1) * SEQ), slice(h * HD, (h + 1) * HD))
+            for s in range(token_count // SEQ)
+            for h in range(queries.shape[1] // HD)
+        ]
+        scores = [matmul(keys[at], queries[at], NT) for at in heads]
+        dprobs = [matmul(values[at], upstream[at], NT) for at in heads]
+        powers = [jnp.exp(x * scale) for x in scores]
+        probs = [x * (1.0 / jnp.sum(x, axis=0, keepdims=True)) for x in powers]
+        lows = [x.astype(LOW) for x in probs]
+        for at, low in zip(heads, lows):
+            dvalues[at] = matmul(low, upstream[at]).astype(LOW)
+        rowdots = [jnp.sum(x * y, axis=0, keepdims=True) for x, y in zip(dprobs, probs)]
+        dscores = [
+            (y * (x - z)).astype(LOW) for x, y, z in zip(dprobs, probs, rowdots)
+        ]
+        for at, dscore in zip(heads, dscores):
+            dkeys[at] = (matmul(dscore, queries[at]) * scale).astype(LOW)
+        for at, low in zip(heads, lows):
+            context[at] = matmul(low, values[at], TN).astype(LOW)
         side = sec % 2
         pairs = lax.axis_size("sec") // 2
         block = width // (2 * pairs)
@@ -342,13 +358,18 @@
     returned = {0: total(own_away, own_kept)}
     arriving[0] = hold(arriving[0], [own_away])
     others = [swap(arriving[0], "tp", 1)]
-    high, low = call(
+    sources = [query_weight[0], key_weight[0], value_weight[0], cotangent[0]]
+    high, low, query_w, key_w, value_w, upstream = call(
         functools.partial(mixing, experts),
-        [shape_of((experts, token_count, capacity))] * 2,
-        [route_rows, gate_rows, earlier],
+        [shape_of((experts, token_count, capacity))] * 2 + [shape_of(x.shape) for x in sources],
+        [route_rows, gate_rows, earlier, *sources],
+        [pltpu.SemaphoreType.DMA((len(sources),))],
+        remote=(3, 4, 5, 6),
+        limit=40,
         after=[arriving[0]],
     )
     others.append(swap(arriving[1], "tp", 1))
+
     def give_back(group, away, kept):
         mixed = total(away, kept)
         for i, k in enumerate(group):
@@ -362,6 +383,7 @@
     returned[1] = swap(total(near_away, near_kept), "exp", 1)
     away, kept = through([arriving[1], others[1]], [near_away, mixed])
     give_back(groups[1], away, kept)
+
     hidden_half = call(
         functools.partial(combine, experts),
         [shape_of((token_count, half))],
@@ -369,31 +391,24 @@
         flops=4 * 3 * token_count * token_count * half,
     )[0]
 
-    def exchange(block, pairs):
-        targets = {i: i for i in range(sections * tp_size)}
-        for a, b in pairs:
-            targets |= {a: b, b: a}
-        return lax.ppermute(block, ("sec", "tp"), list(targets.items()))
-
-    first = hidden_half
-    for i in range(sections // 2 - 1, 0, -1):
-        odd = [(t, (2 * i + 1) * tp_size + (t ^ 1)) for t in range(tp_size)]
-        even = [(t, 2 * i * tp_size + t) for t in range(tp_size)]
-        first = jnp.where(sec == 2 * i + 1, exchange(hidden_half, odd), first)
-        first = jnp.where(sec == 2 * i, exchange(hidden_half, even), first)
-    odd = [(t, tp_size + (t ^ 1)) for t in range(tp_size)]
-    first = jnp.where(sec == 1, exchange(hidden_half, odd), first)
-    halves = [(s * tp_size, s * tp_size + 1) for s in range(1, sections)]
-    hidden_other = exchange(hidden_half, halves)
-    beside = swap(first, "sec", 1)
-    mine = jnp.where(sec % 2 == 0, first, beside)
-    other = jnp.where(sec % 2 == 0, beside, first)
+    beside = swap(hidden_half, "sec", 1)
+    hidden_other = swap(hidden_half, "tp", 1)
+    encoder_half = jnp.where(sec == 1, beside, hidden_half)
+    first = jnp.where(sec == 0, hidden_other, hidden_half)
+    for i in range(1, sections // 2):
+        pairs = [(t, 2 * i * tp_size + t) for t in range(tp_size)]
+        pairs += [(tp_size + t, (2 * i + 1) * tp_size + (t ^ 1)) for t in range(tp_size)]
+        moved = lax.ppermute(encoder_half, ("sec", "tp"), pairs)
+        first = jnp.where(sec // 2 == i, moved, first)
+    second = swap(first, "sec", 1)
+    mine = jnp.where(sec == 1, beside, jnp.where(sec % 2 == 0, first, second))
+    other = jnp.where((sec % 2 == 0) | (sec == 1), second, first)
 
     local_width = query_weight.shape[2]
     queries = call(
         project,
         [shape_of((token_count, local_width))],
-        [hidden_half, hidden_other, attn_gain, query_weight[0]],
+        [hidden_half, hidden_other, attn_gain, query_w],
         flops=2 * token_count * model_width * local_width,
     )[0]
     context, away, kept = call(
@@ -403,7 +418,7 @@
             shape_of((token_count, model_width // 2)),
             shape_of((token_count, model_width // 2), WIDE),
         ],
-        [mine, other, queries, cotangent[0], key_weight[0], value_weight[0], hidden_half],
+        [mine, other, queries, upstream, key_w, value_w, hidden_half],
         [pltpu.VMEM((token_count, local_width), LOW)] * 4,
         flops=10 * token_count * model_width * local_width,
     )

time: 86.7 us -> 83.3 us (0.961)
  starting transfers between devices: 40.6 us -> 37.4 us
  other arithmetic: 0.97 us -> 1.92 us
    ppermute x4 -> x1, waiting for transfers between devices: 6.75 us -> 2.94 us  [shards(): moved = lax.ppermute(encoder_half, ('sec', 'tp'), pairs)]
    ppermute x14 -> x16, waiting for transfers between devices: 16.2 us -> 18.8 us  [swap(): return lax.ppermute(block, axis, [(i, i ^ step) for i in range(size)])]
    ppermute x4 -> x1, starting transfers between devices: 6.68 us -> 4.08 us  [shards(): moved = lax.ppermute(encoder_half, ('sec', 'tp'), pairs)]
    select_n x2 -> x3, other arithmetic: 0.14 us -> 1.07 us  [the longest x1 1 us: shards(): other = jnp.where((sec % 2 == 0) | (sec == 1), second, first)]
    unnamed x20 -> x22, local copies, waits for them, and re-layouts: 2.94 us -> 2.24 us
    ppermute x14 -> x16, starting transfers between devices: 28.2 us -> 28.1 us  [swap(): return lax.ppermute(block, axis, [(i, i ^ step) for i in range(size)])]
  transfers between devices with their start and end apart: 21 -> 20, of which waited for: 15 -> 15; matrix products, arithmetic and copies ran while one was open for 0% -> 0% of each run, Pallas kernels for 13% -> 14%
where the time goes in v7:
time: 83.3 us; the launch traced here: 83 us
  starting transfers between devices  37.4 us (45%)
  waiting for transfers between devices  26.5 us (32%)
  Pallas kernels  14.2 us (17%)
  local copies, waits for them, and re-layouts  2.24 us (3%)
  other arithmetic  1.92 us (2%)
  between operations  0.85 us (1%)
    ppermute x16, starting transfers between devices, swap(): return lax.ppermute(block, axis, [(i, i ^ step) for i in range(size)])  28.1 us
    ppermute x16, waiting for transfers between devices, swap(): return lax.ppermute(block, axis, [(i, i ^ step) for i in range(size)])  18.8 us
    pallas_call x12, Pallas kernels, call(): pl.pallas_call(run, out_shape=[*out_shape, *(shape_of(x.shape, x.dtype) f...  14.2 us
    ppermute x3, starting transfers between devices, shards(): total = total + lax.ppermute(blocks[k], ('sec', 'tp'), pairs).astype(WIDE)  5.22 us
    ppermute x3, waiting for transfers between devices, shards(): total = total + lax.ppermute(blocks[k], ('sec', 'tp'), pairs).astype(WIDE)  4.68 us
    ppermute x1, starting transfers between devices, shards(): moved = lax.ppermute(encoder_half, ('sec', 'tp'), pairs)  4.08 us
    ppermute x1, waiting for transfers between devices, shards(): moved = lax.ppermute(encoder_half, ('sec', 'tp'), pairs)  2.94 us
    unnamed x22, local copies, waits for them, and re-layouts  2.24 us
  transfers between devices with their start and end apart: 20, of which 15 were waited for; matrix products, arithmetic and copies ran while one was open for 0% of the time, Pallas kernels for 14%

profile of v7, /device:TPU:0, one launch (start us, length us, event | category | flops | bytes accessed | tf_op | source)
XLA Modules:
  0.0 83.0 jit_solution(3753701522896281951)
XLA Ops:
  0.7 1.0 %copy-done.3 = bf16[1,256,1024]{2,1,0:T(8,128)(2,1)S(1)} copy-done((bf16[1,256,1024]{2,1,0:T(8,128)(2,1)S(1)}, bf16[1,256,1024]{2,1,0:T(8,128)(2,1)}, u32[]{:S(2)}) %copy-start.3) | copy-done | bytes 524312
  1.7 0.9 %shard_map.123 = (bf16[192,512]{1,0:T(8,128)(2,1)S(1)}, bf16[192,512]{1,0:T(8,128)(2,1)S(1)}, bf16[192,1024]{1,0:T(8,128)(2,1)S(1)}, bf16[192,1024]{1,0:T(8,128)(2,1)S(1)}) custom-call(bf16[256,1024]{1,0:T(8,128)(2,1)S(1)} %bitcast.17, s32[2,256]{1,0:T(2,128)S(1)} %bitcast.20, f32[1,1024]{1,0:T(1,128)S(1)} %copy-done.10, ...), custom_call_target="tpu_custom_call" | custom-call | flops 402653184 | bytes 1841152 | tf_op jit(solution)/shard_map/pallas_call | solution.py:40
  2.6 4.1 %collective-permute-start = (bf16[192,512]{1,0:T(8,128)(2,1)S(1)}, bf16[192,512]{1,0:T(8,128)(2,1)S(1)}, u32[]{:S(2)}, u32[]{:S(2)}) collective-permute-start(bf16[192,512]{1,0:T(8,128)(2,1)S(1)} %get-tuple-element.35), channel_id=1, source_target_pairs={{0,4},{2,6},{4,0},{6,2},{1,5},{3,7},{5,1},{7,3},{8,12},{10,14},{12... | collective-permute-start | bytes 589832 | tf_op jit(solution)/shard_map/ppermute | solution.py:268
  6.7 4.7 %shard_map.124 = (bf16[192,512]{1,0:T(8,128)(2,1)S(1)}, f32[192,512]{1,0:T(8,128)S(1)}, bf16[1024,2048]{1,0:T(8,128)(2,1)S(1)}, bf16[2048,1024]{1,0:T(8,128)(2,1...) custom-call(bf16[192,1024]{1,0:T(8,128)(2,1)S(1)} %get-tuple-element, ...), custom_call_target="tpu_custom_call", output_to_operand_aliasing={{4}: (3, {}), {5}: (4, {})} | custom-call | flops 1610612736 | bytes 17760256 | tf_op jit(solution)/shard_map/pallas_call | solution.py:40
  11.4 1.6 %collective-permute-start.1 = (bf16[192,512]{1,0:T(8,128)(2,1)S(1)}, bf16[192,512]{1,0:T(8,128)(2,1)S(1)}, u32[]{:S(2)}, u32[]{:S(2)}) collective-permute-start(bf16[192,512]{1,0:T(8,128)(2,1)S(1)} %get-tuple-element.34.refs_0_), channel_id=1, source_target_pairs={{0,1},{1,0},{2,3},{3,2},{4,5},{5,4},{6,7},{7,6},{8,9},{9,8},{10,11... | collective-permute-start | bytes 589832 | tf_op jit(solution)/shard_map/ppermute | solution.py:268
  13.0 1.6 %collective-permute-start.2 = (bf16[192,1024]{1,0:T(8,128)(2,1)S(1)}, bf16[192,1024]{1,0:T(8,128)(2,1)S(1)}, u32[]{:S(2)}, u32[]{:S(2)}) collective-permute-start(bf16[192,1024]{1,0:T(8,128)(2,1)S(1)} %get-tuple-element.39), channel_id=1, source_target_pairs={{0,2},{2,0},{4,6},{6,4},{1,3},{3,1},{5,7},{7,5},{8,10},{10,8},{12,... | collective-permute-start | bytes 1179656 | tf_op jit(solution)/shard_map/ppermute | solution.py:268
  14.6 0.2 collective-permute-start.8
  14.8 1.1 %collective-permute-done.refs_1_ = bf16[192,512]{1,0:T(8,128)(2,1)S(1)} collective-permute-done((bf16[192,512]{1,0:T(8,128)(2,1)S(1)}, bf16[192,512]{1,0:T(8,128)(2,1)S(1)}, u32[]{:S(2)}, u32[]{:S(2)}) %collective-permute-start) | collective-permute-done | bytes 196640 | tf_op jit(solution)/shard_map/ppermute | solution.py:268
  15.9 2.2 %collective-permute-start.3 = (bf16[192,512]{1,0:T(8,128)(2,1)S(1)}, bf16[192,512]{1,0:T(8,128)(2,1)S(1)}, u32[]{:S(2)}, u32[]{:S(2)}) collective-permute-start(bf16[192,512]{1,0:T(8,128)(2,1)S(1)} %shard_map.125.refs_7_.refs_0_), channel_id=1, source_target_pairs={{0,1},{1,0},{2,3},{3,2},{4,5},{5,4},{6,7},{7,6},{8,9},{9,8},{10,11... | collective-permute-start | bytes 589832 | tf_op jit(solution)/shard_map/ppermute | solution.py:268
  18.1 0.9 %shard_map.126 = (bf16[4,256,192]{2,1,0:T(8,128)(2,1)S(1)}, bf16[4,256,192]{2,1,0:T(8,128)(2,1)S(1)}, bf16[1024,512]{1,0:T(8,128)(2,1)S(1)}, bf16[1024,512]{1,0:...) custom-call(s32[2,256]{1,0:T(2,128)S(1)} %bitcast.21, f32[2,256]{1,0:T(2,128)S(1)} %bitcast.22, ...), custom_call_target="tpu_custom_call" | custom-call | bytes 7737344 | tf_op jit(solution)/shard_map/pallas_call | solution.py:40
  19.1 3.0 %collective-permute-done.3.refs_1_ = bf16[192,512]{1,0:T(8,128)(2,1)S(1)} collective-permute-done((bf16[192,512]{1,0:T(8,128)(2,1)S(1)}, bf16[192,512]{1,0:T(8,128)(2,1)S(1)}, u32[]{:S(2)}, u32[]{:S(2)}) %collective-permute-start.3) | collective-permute-done | bytes 196640 | tf_op jit(solution)/shard_map/ppermute | solution.py:268
  22.0 1.8 %shard_map.127 = (bf16[192,512]{1,0:T(8,128)(2,1)S(1)}, f32[192,512]{1,0:T(8,128)S(1)}) custom-call(bf16[192,512]{1,0:T(8,128)(2,1)S(1)} %shard_map.125.refs_7_.refs_0_, bf16[192,512]{1,0:T(8,128)(2,1)S(1)} %collective-permute-done.3.refs_1_, bf16[1024,2048]{1,0:T(8,128)(2,1)S(1)} %get-tuple-element.40.refs_2_.refs_1_, ...), custom_call_target="tpu_custom_call" | custom-call | flops 1610612736 | bytes 9371648 | tf_op jit(solution)/shard_map/pallas_call | solution.py:40
  23.9 1.8 %collective-permute-start.6 = (bf16[192,512]{1,0:T(8,128)(2,1)S(1)}, bf16[192,512]{1,0:T(8,128)(2,1)S(1)}, u32[]{:S(2)}, u32[]{:S(2)}) collective-permute-start(bf16[192,512]{1,0:T(8,128)(2,1)S(1)} %get-tuple-element.42.refs_3_), channel_id=1, source_target_pairs={{0,1},{1,0},{2,3},{3,2},{4,5},{5,4},{6,7},{7,6},{8,9},{9,8},{10,11... | collective-permute-start | bytes 589832 | tf_op jit(solution)/shard_map/ppermute | solution.py:268
  25.7 1.7 %collective-permute-done.8.refs_0_ = bf16[192,512]{1,0:T(8,128)(2,1)S(1)} collective-permute-done((bf16[192,512]{1,0:T(8,128)(2,1)S(1)}, bf16[192,512]{1,0:T(8,128)(2,1)S(1)}, u32[]{:S(2)}, u32[]{:S(2)}) %collective-permute-start.8) | collective-permute-done | bytes 196640 | tf_op jit(solution)/shard_map/ppermute | solution.py:268
  27.4 0.5 collective-permute-start.9
  27.9 0.6 collective-permute-done.2.refs_0_
  28.4 1.8 %shard_map.128 = (bf16[192,512]{1,0:T(8,128)(2,1)S(1)}, f32[192,512]{1,0:T(8,128)S(1)}) custom-call(bf16[192,1024]{1,0:T(8,128)(2,1)S(1)} %collective-permute-done.2.refs_0_, bf16[1024,2048]{1,0:T(8,128)(2,1)S(1)} %get-tuple-element.40.refs_2_.refs_1_, bf16[2048,1024]{1,0:T(8,128)(2,1)S(1)} %get-tuple-element.41.refs_3_.refs_2_, ...), custom_call_target="tpu_custom_call" | custom-call | flops 1610612736 | bytes 9371648 | tf_op jit(solution)/shard_map/pallas_call | solution.py:40
  30.3 1.6 %collective-permute-start.4 = (bf16[192,512]{1,0:T(8,128)(2,1)S(1)}, bf16[192,512]{1,0:T(8,128)(2,1)S(1)}, u32[]{:S(2)}, u32[]{:S(2)}) collective-permute-start(bf16[192,512]{1,0:T(8,128)(2,1)S(1)} %get-tuple-element.44.refs_4_), channel_id=1, source_target_pairs={{0,1},{1,0},{2,3},{3,2},{4,5},{5,4},{6,7},{7,6},{8,9},{9,8},{10,11... | collective-permute-start | bytes 589832 | tf_op jit(solution)/shard_map/ppermute | solution.py:268
  31.9 1.6 %collective-permute-start.7 = (bf16[192,512]{1,0:T(8,128)(2,1)S(1)}, bf16[192,512]{1,0:T(8,128)(2,1)S(1)}, u32[]{:S(2)}, u32[]{:S(2)}) collective-permute-start(bf16[192,512]{1,0:T(8,128)(2,1)S(1)} %add_convert_fusion.1.refs_5_), channel_id=1, source_target_pairs={{0,4},{2,6},{4,0},{6,2},{1,5},{3,7},{5,1},{7,3},{8,12},{10,14},{12... | collective-permute-start | bytes 589832 | tf_op jit(solution)/shard_map/ppermute | solution.py:268
  33.6 1.4 %collective-permute-done.9.refs_1_ = bf16[192,512]{1,0:T(8,128)(2,1)S(1)} collective-permute-done((bf16[192,512]{1,0:T(8,128)(2,1)S(1)}, bf16[192,512]{1,0:T(8,128)(2,1)S(1)}, u32[]{:S(2)}, u32[]{:S(2)}) %collective-permute-start.9) | collective-permute-done | bytes 196640 | tf_op jit(solution)/shard_map/ppermute | solution.py:268
  34.9 1.8 %shard_map.129 = (bf16[192,512]{1,0:T(8,128)(2,1)S(1)}, f32[192,512]{1,0:T(8,128)S(1)}) custom-call(bf16[192,512]{1,0:T(8,128)(2,1)S(1)} %collective-permute-done.8.refs_0_, bf16[192,512]{1,0:T(8,128)(2,1)S(1)} %collective-permute-done.9.refs_1_, bf16[1024,2048]{1,0:T(8,128)(2,1)S(1)} %get-tuple-element.40.refs_2_.refs_1_, ...), custom_call_target="tpu_custom_call" | custom-call | flops 1610612736 | bytes 9371648 | tf_op jit(solution)/shard_map/pallas_call | solution.py:40
  36.8 1.3 %collective-permute-start.10 = (bf16[192,512]{1,0:T(8,128)(2,1)S(1)}, bf16[192,512]{1,0:T(8,128)(2,1)S(1)}, u32[]{:S(2)}, u32[]{:S(2)}) collective-permute-start(bf16[192,512]{1,0:T(8,128)(2,1)S(1)} %get-tuple-element.48), channel_id=1, source_target_pairs={{0,1},{1,0},{2,3},{3,2},{4,5},{5,4},{6,7},{7,6},{8,9},{9,8},{10,11... | collective-permute-start | bytes 589832 | tf_op jit(solution)/shard_map/ppermute | solution.py:268
  38.1 0.4 collective-permute-done.4
  38.5 2.6 %collective-permute-start.5 = (bf16[192,512]{1,0:T(8,128)(2,1)S(1)}, bf16[192,512]{1,0:T(8,128)(2,1)S(1)}, u32[]{:S(2)}, u32[]{:S(2)}) collective-permute-start(bf16[192,512]{1,0:T(8,128)(2,1)S(1)} %add_convert_fusion.2), channel_id=1, source_target_pairs={{0,2},{2,0},{4,6},{6,4},{1,3},{3,1},{5,7},{7,5},{8,10},{10,8},{12,... | collective-permute-start | bytes 589832 | tf_op jit(solution)/shard_map/ppermute | solution.py:268
  41.1 1.4 %collective-permute-done.10 = bf16[192,512]{1,0:T(8,128)(2,1)S(1)} collective-permute-done((bf16[192,512]{1,0:T(8,128)(2,1)S(1)}, bf16[192,512]{1,0:T(8,128)(2,1)S(1)}, u32[]{:S(2)}, u32[]{:S(2)}) %collective-permute-start.10) | collective-permute-done | bytes 196640 | tf_op jit(solution)/shard_map/ppermute | solution.py:268
  42.6 4.9 %collective-permute-start.11 = (bf16[192,512]{1,0:T(8,128)(2,1)S(1)}, bf16[192,512]{1,0:T(8,128)(2,1)S(1)}, u32[]{:S(2)}, u32[]{:S(2)}) collective-permute-start(bf16[192,512]{1,0:T(8,128)(2,1)S(1)} %add_convert_fusion), channel_id=1, source_target_pairs={{0,6},{2,4},{4,2},{6,0},{1,7},{3,5},{5,3},{7,1},{8,14},{10,12},{12... | collective-permute-start | bytes 589832 | tf_op jit(solution)/shard_map/ppermute | solution.py:268
  47.5 1.2 %collective-permute-done.5.refs_4_ = bf16[192,512]{1,0:T(8,128)(2,1)S(1)} collective-permute-done((bf16[192,512]{1,0:T(8,128)(2,1)S(1)}, bf16[192,512]{1,0:T(8,128)(2,1)S(1)}, u32[]{:S(2)}, u32[]{:S(2)}) %collective-permute-start.5) | collective-permute-done | bytes 196640 | tf_op jit(solution)/shard_map/ppermute | solution.py:268
  48.7 3.2 %collective-permute-done.11.refs_6_ = bf16[192,512]{1,0:T(8,128)(2,1)S(1)} collective-permute-done((bf16[192,512]{1,0:T(8,128)(2,1)S(1)}, bf16[192,512]{1,0:T(8,128)(2,1)S(1)}, u32[]{:S(2)}, u32[]{:S(2)}) %collective-permute-start.11) | collective-permute-done | bytes 196640 | tf_op jit(solution)/shard_map/ppermute | solution.py:268
  51.9 0.7 shard_map.130.refs_0_.refs_6_
  52.7 1.6 %collective-permute-start.14 = (bf16[256,512]{1,0:T(8,128)(2,1)S(1)}, bf16[256,512]{1,0:T(8,128)(2,1)S(1)}, u32[]{:S(2)}, u32[]{:S(2)}) collective-permute-start(bf16[256,512]{1,0:T(8,128)(2,1)S(1)} %shard_map.130.refs_0_.refs_6_), channel_id=1, source_target_pairs={{0,1},{1,0},{2,3},{3,2},{4,5},{5,4},{6,7},{7,6},{8,9},{9,8},{10,11... | collective-permute-start | bytes 786440 | tf_op jit(solution)/shard_map/ppermute | solution.py:268
  54.3 4.1 %collective-permute-start.13 = (bf16[256,512]{1,0:T(8,128)(2,1)S(1)}, bf16[256,512]{1,0:T(8,128)(2,1)}, u32[]{:S(2)}, u32[]{:S(2)}) collective-permute-start(bf16[256,512]{1,0:T(8,128)(2,1)S(1)} %broadcast_select_fusion.1), channel_id=1, source_target_pairs={{0,16},{1,17},{8,25},{9,24},{2,18},{3,19},{10,27},{11,26},{4,20},{... | collective-permute-start | bytes 786440 | tf_op jit(solution)/shard_map/ppermute | solution.py:401
  58.4 3.0 %collective-permute-done.14.refs_1_ = bf16[256,512]{1,0:T(8,128)(2,1)S(1)} collective-permute-done((bf16[256,512]{1,0:T(8,128)(2,1)S(1)}, bf16[256,512]{1,0:T(8,128)(2,1)S(1)}, u32[]{:S(2)}, u32[]{:S(2)}) %collective-permute-start.14) | collective-permute-done | bytes 262176 | tf_op jit(solution)/shard_map/ppermute | solution.py:268
  61.4 2.9 %collective-permute-done.13 = bf16[256,512]{1,0:T(8,128)(2,1)} collective-permute-done((bf16[256,512]{1,0:T(8,128)(2,1)S(1)}, bf16[256,512]{1,0:T(8,128)(2,1)}, u32[]{:S(2)}, u32[]{:S(2)}) %collective-permute-start.13) | collective-permute-done | bytes 262176 | tf_op jit(solution)/shard_map/ppermute | solution.py:401
  64.4 0.3 collective-permute-start.15
  64.7 0.7 shard_map.131.refs_2_
  65.4 0.8 collective-permute-done.15
  66.1 1.0 %broadcast_select_fusion = (bf16[256,512]{1,0:T(8,128)(2,1)S(1)}, bf16[256,512]{1,0:T(8,128)(2,1)S(1)}) fusion(bf16[256,512]{1,0:T(8,128)(2,1)} %collective-permute-done.15, bf16[256,512]{1,0:T(8,128)(2,1)S(1)} %select_select_fusion.1, pred[]{:T(512)S(6)} %or.3, bf16[256,512]{1,0:T(8,128)(2,1)S(1)} %collective-permute-done.12, pred[]{:T(512)S(6)} %eq.19, ...), kind=kLoop, calls=%fused_computation.6 | loop fusion | flops 393216 | bytes 1310723 | tf_op jit(solution)/shard_map/jit(_where)/select_n | solution.py:405
  67.2 1.2 %copy-done.9 = bf16[1024,512]{1,0:T(8,128)(2,1)S(1)} copy-done((bf16[1024,512]{1,0:T(8,128)(2,1)S(1)}, bf16[1024,512]{1,0:T(8,128)(2,1)}, u32[]{:S(2)}) %copy-start.9) | copy-done | bytes 1048600
  68.4 0.8 shard_map.132
  69.2 2.0 %collective-permute-start.16 = (bf16[256,512]{1,0:T(8,128)(2,1)S(1)}, bf16[256,512]{1,0:T(8,128)(2,1)S(1)}, u32[]{:S(2)}, u32[]{:S(2)}) collective-permute-start(bf16[256,512]{1,0:T(8,128)(2,1)S(1)} %get-tuple-element.55), channel_id=1, source_target_pairs={{0,8},{8,0},{16,24},{24,16},{1,9},{9,1},{17,25},{25,17},{2,10},{10... | collective-permute-start | bytes 786440 | tf_op jit(solution)/shard_map/ppermute | solution.py:268
  71.2 1.2 %collective-permute-done.16.refs_1_ = bf16[256,512]{1,0:T(8,128)(2,1)S(1)} collective-permute-done((bf16[256,512]{1,0:T(8,128)(2,1)S(1)}, bf16[256,512]{1,0:T(8,128)(2,1)S(1)}, u32[]{:S(2)}, u32[]{:S(2)}) %collective-permute-start.16) | collective-permute-done | bytes 262176 | tf_op jit(solution)/shard_map/ppermute | solution.py:268
  72.4 0.1 shard_map.133
  72.5 0.7 collective-permute-start.17
  73.2 4.0 %collective-permute-start.18 = (bf16[256,128]{1,0:T(8,128)(2,1)S(1)}, bf16[256,128]{1,0:T(8,128)(2,1)S(1)}, u32[]{:S(2)}, u32[]{:S(2)}) collective-permute-start(bf16[256,128]{1,0:T(8,128)(2,1)S(1)} %get-tuple-element.58), channel_id=1, source_target_pairs={{0,16},{1,17},{8,24},{9,25},{16,0},{17,1},{24,8},{25,9},{2,18},{3,... | collective-permute-start | bytes 196616 | tf_op jit(solution)/shard_map/ppermute | solution.py:441
  77.2 0.5 collective-permute-start.19
  77.7 1.8 %collective-permute-done.18 = bf16[256,128]{1,0:T(8,128)(2,1)S(1)} collective-permute-done((bf16[256,128]{1,0:T(8,128)(2,1)S(1)}, bf16[256,128]{1,0:T(8,128)(2,1)S(1)}, u32[]{:S(2)}, u32[]{:S(2)}) %collective-permute-start.18) | collective-permute-done | bytes 65568 | tf_op jit(solution)/shard_map/ppermute | solution.py:441
  79.5 2.8 %collective-permute-done.19 = bf16[256,128]{1,0:T(8,128)(2,1)S(1)} collective-permute-done((bf16[256,128]{1,0:T(8,128)(2,1)S(1)}, bf16[256,128]{1,0:T(8,128)(2,1)S(1)}, u32[]{:S(2)}, u32[]{:S(2)}) %collective-permute-start.19) | collective-permute-done | bytes 65568 | tf_op jit(solution)/shard_map/ppermute | solution.py:441
  82.4 0.7 add_convert_fusion.4
  (34 shorter events, 0.4 us)
Async XLA Ops:
  0.6 1.0 %copy-start.3 = (bf16[1,256,1024]{2,1,0:T(8,128)(2,1)S(1)}, bf16[1,256,1024]{2,1,0:T(8,128)(2,1)}, u32[]{:S(2)}) copy-start(bf16[1,256,1024]{2,1,0:T(8,128)(2,1)} %param.11) | copy-start | bytes 1572868
  0.6 1.0 %copy-start.6 = (s32[1,256,2]{1,2,0:T(2,128)S(1)}, s32[1,256,2]{1,2,0:T(2,128)}, u32[]{:S(2)}) copy-start(s32[1,256,2]{1,2,0:T(2,128)} %param.12) | copy-start | bytes 6148
  0.6 1.0 %copy-start.10 = (f32[1,1024]{1,0:T(1,128)S(1)}, f32[1,1024]{1,0:T(1,128)}, u32[]{:S(2)}) copy-start(f32[1,1024]{1,0:T(1,128)} %refs_2_.2) | copy-start | bytes 12292
  2.6 13.3 %collective-permute-start = (bf16[192,512]{1,0:T(8,128)(2,1)S(1)}, bf16[192,512]{1,0:T(8,128)(2,1)S(1)}, u32[]{:S(2)}, u32[]{:S(2)}) collective-permute-start(bf16[192,512]{1,0:T(8,128)(2,1)S(1)} %get-tuple-element.35), channel_id=1, source_target_pairs={{0,4},{2,6},{4,0},{6,2},{1,5},{3,7},{5,1},{7,3},{8,12},{10,14},{12... | collective-permute-start | bytes 589832 | tf_op jit(solution)/shard_map/ppermute | solution.py:268
  6.7 11.4 %copy-start = (bf16[1,1024,512]{2,1,0:T(8,128)(2,1)S(1)}, bf16[1,1024,512]{2,1,0:T(8,128)(2,1)}, u32[]{:S(2)}) copy-start(bf16[1,1024,512]{2,1,0:T(8,128)(2,1)} %param.18) | copy-start | bytes 3145732
  6.7 11.4 %copy-start.1 = (bf16[1,1024,512]{2,1,0:T(8,128)(2,1)S(1)}, bf16[1,1024,512]{2,1,0:T(8,128)(2,1)}, u32[]{:S(2)}) copy-start(bf16[1,1024,512]{2,1,0:T(8,128)(2,1)} %param.19) | copy-start | bytes 3145732
  6.7 11.4 %copy-start.2 = (bf16[1,1024,512]{2,1,0:T(8,128)(2,1)S(1)}, bf16[1,1024,512]{2,1,0:T(8,128)(2,1)}, u32[]{:S(2)}) copy-start(bf16[1,1024,512]{2,1,0:T(8,128)(2,1)} %param.20) | copy-start | bytes 3145732
  6.7 11.4 %copy-start.4 = (bf16[1,256,512]{2,1,0:T(8,128)(2,1)S(1)}, bf16[1,256,512]{2,1,0:T(8,128)(2,1)}, u32[]{:S(2)}) copy-start(bf16[1,256,512]{2,1,0:T(8,128)(2,1)} %param.21) | copy-start | bytes 786436
  6.7 11.4 %copy-start.7 = (f32[1,256,2]{1,2,0:T(2,128)S(1)}, f32[1,256,2]{1,2,0:T(2,128)}, u32[]{:S(2)}) copy-start(f32[1,256,2]{1,2,0:T(2,128)} %param.13) | copy-start | bytes 6148
  11.4 7.6 %collective-permute-start.1 = (bf16[192,512]{1,0:T(8,128)(2,1)S(1)}, bf16[192,512]{1,0:T(8,128)(2,1)S(1)}, u32[]{:S(2)}, u32[]{:S(2)}) collective-permute-start(bf16[192,512]{1,0:T(8,128)(2,1)S(1)} %get-tuple-element.34.refs_0_), channel_id=1, source_target_pairs={{0,1},{1,0},{2,3},{3,2},{4,5},{5,4},{6,7},{7,6},{8,9},{9,8},{10,11... | collective-permute-start | bytes 589832 | tf_op jit(solution)/shard_map/ppermute | solution.py:268
  13.0 15.4 %collective-permute-start.2 = (bf16[192,1024]{1,0:T(8,128)(2,1)S(1)}, bf16[192,1024]{1,0:T(8,128)(2,1)S(1)}, u32[]{:S(2)}, u32[]{:S(2)}) collective-permute-start(bf16[192,1024]{1,0:T(8,128)(2,1)S(1)} %get-tuple-element.39), channel_id=1, source_target_pairs={{0,2},{2,0},{4,6},{6,4},{1,3},{3,1},{5,7},{7,5},{8,10},{10,8},{12,... | collective-permute-start | bytes 1179656 | tf_op jit(solution)/shard_map/ppermute | solution.py:268
  14.6 12.8 %collective-permute-start.8 = (bf16[192,512]{1,0:T(8,128)(2,1)S(1)}, bf16[192,512]{1,0:T(8,128)(2,1)S(1)}, u32[]{:S(2)}, u32[]{:S(2)}) collective-permute-start(bf16[192,512]{1,0:T(8,128)(2,1)S(1)} %get-tuple-element.46), channel_id=1, source_target_pairs={{0,6},{2,4},{4,2},{6,0},{1,7},{3,5},{5,3},{7,1},{8,14},{10,12},{12... | collective-permute-start | bytes 589832 | tf_op jit(solution)/shard_map/ppermute | solution.py:268
  15.9 6.2 %collective-permute-start.3 = (bf16[192,512]{1,0:T(8,128)(2,1)S(1)}, bf16[192,512]{1,0:T(8,128)(2,1)S(1)}, u32[]{:S(2)}, u32[]{:S(2)}) collective-permute-start(bf16[192,512]{1,0:T(8,128)(2,1)S(1)} %shard_map.125.refs_7_.refs_0_), channel_id=1, source_target_pairs={{0,1},{1,0},{2,3},{3,2},{4,5},{5,4},{6,7},{7,6},{8,9},{9,8},{10,11... | collective-permute-start | bytes 589832 | tf_op jit(solution)/shard_map/ppermute | solution.py:268
  19.0 4.9 %copy-start.8 = (bf16[1024,512]{1,0:T(8,128)(2,1)}, bf16[1024,512]{1,0:T(8,128)(2,1)S(1)}, u32[]{:S(2)}) copy-start(bf16[1024,512]{1,0:T(8,128)(2,1)S(1)} %get-tuple-element.52.refs_5_) | copy-start | bytes 3145732
  23.9 8.0 %collective-permute-start.6 = (bf16[192,512]{1,0:T(8,128)(2,1)S(1)}, bf16[192,512]{1,0:T(8,128)(2,1)S(1)}, u32[]{:S(2)}, u32[]{:S(2)}) collective-permute-start(bf16[192,512]{1,0:T(8,128)(2,1)S(1)} %get-tuple-element.42.refs_3_), channel_id=1, source_target_pairs={{0,1},{1,0},{2,3},{3,2},{4,5},{5,4},{6,7},{7,6},{8,9},{9,8},{10,11... | collective-permute-start | bytes 589832 | tf_op jit(solution)/shard_map/ppermute | solution.py:268
  27.4 7.5 %collective-permute-start.9 = (bf16[192,512]{1,0:T(8,128)(2,1)S(1)}, bf16[192,512]{1,0:T(8,128)(2,1)S(1)}, u32[]{:S(2)}, u32[]{:S(2)}) collective-permute-start(bf16[192,512]{1,0:T(8,128)(2,1)S(1)} %collective-permute-done.8.refs_0_), channel_id=1, source_target_pairs={{0,1},{1,0},{2,3},{3,2},{4,5},{5,4},{6,7},{7,6},{8,9},{9,8},{10,11... | collective-permute-start | bytes 589832 | tf_op jit(solution)/shard_map/ppermute | solution.py:268
  30.3 8.2 %collective-permute-start.4 = (bf16[192,512]{1,0:T(8,128)(2,1)S(1)}, bf16[192,512]{1,0:T(8,128)(2,1)S(1)}, u32[]{:S(2)}, u32[]{:S(2)}) collective-permute-start(bf16[192,512]{1,0:T(8,128)(2,1)S(1)} %get-tuple-element.44.refs_4_), channel_id=1, source_target_pairs={{0,1},{1,0},{2,3},{3,2},{4,5},{5,4},{6,7},{7,6},{8,9},{9,8},{10,11... | collective-permute-start | bytes 589832 | tf_op jit(solution)/shard_map/ppermute | solution.py:268
  31.9 15.5 %collective-permute-start.7 = (bf16[192,512]{1,0:T(8,128)(2,1)S(1)}, bf16[192,512]{1,0:T(8,128)(2,1)S(1)}, u32[]{:S(2)}, u32[]{:S(2)}) collective-permute-start(bf16[192,512]{1,0:T(8,128)(2,1)S(1)} %add_convert_fusion.1.refs_5_), channel_id=1, source_target_pairs={{0,4},{2,6},{4,0},{6,2},{1,5},{3,7},{5,1},{7,3},{8,12},{10,14},{12... | collective-permute-start | bytes 589832 | tf_op jit(solution)/shard_map/ppermute | solution.py:268
  36.8 27.9 %copy-start.5 = (f32[1,1024]{1,0:T(1,128)S(1)}, f32[1,1024]{1,0:T(1,128)}, u32[]{:S(2)}) copy-start(f32[1,1024]{1,0:T(1,128)} %refs_2_.3) | copy-start | bytes 12292
  36.8 5.7 %collective-permute-start.10 = (bf16[192,512]{1,0:T(8,128)(2,1)S(1)}, bf16[192,512]{1,0:T(8,128)(2,1)S(1)}, u32[]{:S(2)}, u32[]{:S(2)}) collective-permute-start(bf16[192,512]{1,0:T(8,128)(2,1)S(1)} %get-tuple-element.48), channel_id=1, source_target_pairs={{0,1},{1,0},{2,3},{3,2},{4,5},{5,4},{6,7},{7,6},{8,9},{9,8},{10,11... | collective-permute-start | bytes 589832 | tf_op jit(solution)/shard_map/ppermute | solution.py:268
  38.5 10.2 %collective-permute-start.5 = (bf16[192,512]{1,0:T(8,128)(2,1)S(1)}, bf16[192,512]{1,0:T(8,128)(2,1)S(1)}, u32[]{:S(2)}, u32[]{:S(2)}) collective-permute-start(bf16[192,512]{1,0:T(8,128)(2,1)S(1)} %add_convert_fusion.2), channel_id=1, source_target_pairs={{0,2},{2,0},{4,6},{6,4},{1,3},{3,1},{5,7},{7,5},{8,10},{10,8},{12,... | collective-permute-start | bytes 589832 | tf_op jit(solution)/shard_map/ppermute | solution.py:268
  42.6 9.4 %collective-permute-start.11 = (bf16[192,512]{1,0:T(8,128)(2,1)S(1)}, bf16[192,512]{1,0:T(8,128)(2,1)S(1)}, u32[]{:S(2)}, u32[]{:S(2)}) collective-permute-start(bf16[192,512]{1,0:T(8,128)(2,1)S(1)} %add_convert_fusion), channel_id=1, source_target_pairs={{0,6},{2,4},{4,2},{6,0},{1,7},{3,5},{5,3},{7,1},{8,14},{10,12},{12... | collective-permute-start | bytes 589832 | tf_op jit(solution)/shard_map/ppermute | solution.py:268
  52.6 1.7 %collective-permute-start.12 = (bf16[256,512]{1,0:T(8,128)(2,1)S(1)}, bf16[256,512]{1,0:T(8,128)(2,1)S(1)}, u32[]{:S(2)}, u32[]{:S(2)}) collective-permute-start(bf16[256,512]{1,0:T(8,128)(2,1)S(1)} %shard_map.130.refs_0_.refs_6_), channel_id=1, source_target_pairs={{0,8},{8,0},{16,24},{24,16},{1,9},{9,1},{17,25},{25,17},{2,10},{10... | collective-permute-start | bytes 786440 | tf_op jit(solution)/shard_map/ppermute | solution.py:268
  52.7 8.7 %collective-permute-start.14 = (bf16[256,512]{1,0:T(8,128)(2,1)S(1)}, bf16[256,512]{1,0:T(8,128)(2,1)S(1)}, u32[]{:S(2)}, u32[]{:S(2)}) collective-permute-start(bf16[256,512]{1,0:T(8,128)(2,1)S(1)} %shard_map.130.refs_0_.refs_6_), channel_id=1, source_target_pairs={{0,1},{1,0},{2,3},{3,2},{4,5},{5,4},{6,7},{7,6},{8,9},{9,8},{10,11... | collective-permute-start | bytes 786440 | tf_op jit(solution)/shard_map/ppermute | solution.py:268
  54.3 10.0 %collective-permute-start.13 = (bf16[256,512]{1,0:T(8,128)(2,1)S(1)}, bf16[256,512]{1,0:T(8,128)(2,1)}, u32[]{:S(2)}, u32[]{:S(2)}) collective-permute-start(bf16[256,512]{1,0:T(8,128)(2,1)S(1)} %broadcast_select_fusion.1), channel_id=1, source_target_pairs={{0,16},{1,17},{8,25},{9,24},{2,18},{3,19},{10,27},{11,26},{4,20},{... | collective-permute-start | bytes 786440 | tf_op jit(solution)/shard_map/ppermute | solution.py:401
  64.4 1.7 %collective-permute-start.15 = (bf16[256,512]{1,0:T(8,128)(2,1)S(1)}, bf16[256,512]{1,0:T(8,128)(2,1)}, u32[]{:S(2)}, u32[]{:S(2)}) collective-permute-start(bf16[256,512]{1,0:T(8,128)(2,1)S(1)} %select_select_fusion.1), channel_id=1, source_target_pairs={{0,8},{8,0},{16,24},{24,16},{1,9},{9,1},{17,25},{25,17},{2,10},{10... | collective-permute-start | bytes 786440 | tf_op jit(solution)/shard_map/ppermute | solution.py:268
  67.2 1.2 %copy-start.9 = (bf16[1024,512]{1,0:T(8,128)(2,1)S(1)}, bf16[1024,512]{1,0:T(8,128)(2,1)}, u32[]{:S(2)}) copy-start(bf16[1024,512]{1,0:T(8,128)(2,1)} %copy-done.8) | copy-start | bytes 3145732
  69.2 3.2 %collective-permute-start.16 = (bf16[256,512]{1,0:T(8,128)(2,1)S(1)}, bf16[256,512]{1,0:T(8,128)(2,1)S(1)}, u32[]{:S(2)}, u32[]{:S(2)}) collective-permute-start(bf16[256,512]{1,0:T(8,128)(2,1)S(1)} %get-tuple-element.55), channel_id=1, source_target_pairs={{0,8},{8,0},{16,24},{24,16},{1,9},{9,1},{17,25},{25,17},{2,10},{10... | collective-permute-start | bytes 786440 | tf_op jit(solution)/shard_map/ppermute | solution.py:268
  72.5 5.2 %collective-permute-start.17 = (bf16[256,128]{1,0:T(8,128)(2,1)S(1)}, bf16[256,128]{1,0:T(8,128)(2,1)S(1)}, u32[]{:S(2)}, u32[]{:S(2)}) collective-permute-start(bf16[256,128]{1,0:T(8,128)(2,1)S(1)} %get-tuple-element.57), channel_id=1, source_target_pairs={{0,1},{1,0},{8,9},{9,8},{16,17},{17,16},{24,25},{25,24},{2,3},{3,2... | collective-permute-start | bytes 196616 | tf_op jit(solution)/shard_map/ppermute | solution.py:441
  73.2 6.4 %collective-permute-start.18 = (bf16[256,128]{1,0:T(8,128)(2,1)S(1)}, bf16[256,128]{1,0:T(8,128)(2,1)S(1)}, u32[]{:S(2)}, u32[]{:S(2)}) collective-permute-start(bf16[256,128]{1,0:T(8,128)(2,1)S(1)} %get-tuple-element.58), channel_id=1, source_target_pairs={{0,16},{1,17},{8,24},{9,25},{16,0},{17,1},{24,8},{25,9},{2,18},{3,... | collective-permute-start | bytes 196616 | tf_op jit(solution)/shard_map/ppermute | solution.py:441
  77.2 5.2 %collective-permute-start.19 = (bf16[256,128]{1,0:T(8,128)(2,1)S(1)}, bf16[256,128]{1,0:T(8,128)(2,1)S(1)}, u32[]{:S(2)}, u32[]{:S(2)}) collective-permute-start(bf16[256,128]{1,0:T(8,128)(2,1)S(1)} %get-tuple-element.59), channel_id=1, source_target_pairs={{0,17},{1,16},{8,25},{9,24},{16,1},{17,0},{24,9},{25,8},{2,19},{3,... | collective-permute-start | bytes 196616 | tf_op jit(solution)/shard_map/ppermute | solution.py:441

commit v8 on v7

--- a/solution.py
+++ b/solution.py
@@ -97,15 +97,7 @@
     own[...] = matmul(table(place, 0, capacity), normed).astype(LOW)
 
 
-def mixing(experts, routes, gates, earlier, *refs):
-    count = (len(refs) - 3) // 2
-    sources, (high, low), targets, arrived = refs[:count], refs[count : count + 2], refs[count + 2 : -1], refs[-1]
-    loads = [
-        pltpu.make_async_copy(source, target, arrived.at[i])
-        for i, (source, target) in enumerate(zip(sources, targets, strict=True))
-    ]
-    for load in loads:
-        load.start()
+def mixing(experts, routes, gates, earlier, high, low):
     me = lax.axis_index("exp")
     token_count = routes.shape[1]
     capacity = high.shape[2]
@@ -119,8 +111,6 @@
         upper = weight.astype(LOW)
         high[k] = upper
         low[k] = (weight - upper.astype(WIDE)).astype(LOW)
-    for load in loads:
-        load.wait()
 
 
 def expert(split, *refs):
@@ -178,7 +168,15 @@
     out[...] = mixed.astype(LOW)
 
 
-def project(mine, other, gain, weight, out):
+def project(mine, other, gain, weight, *refs):
+    count = (len(refs) - 2) // 2
+    sources, out, targets, arrived = refs[:count], refs[count], refs[count + 1 : -1], refs[-1]
+    loads = [
+        pltpu.make_async_copy(source, target, arrived.at[i])
+        for i, (source, target) in enumerate(zip(sources, targets, strict=True))
+    ]
+    for load in loads:
+        load.start()
     tp = lax.axis_index("tp")
     half = mine.shape[1]
     own = mine[...].astype(WIDE)
@@ -196,22 +194,39 @@
     rest = (rest * factor * gain[:, part(1 - tp, half)]).astype(LOW)
     value = matmul(own, weight[part(tp, half), :]) + matmul(rest, weight[part(1 - tp, half), :])
     out[...] = value.astype(LOW)
+    for load in loads:
+        load.wait()
+
+
+def choose(own, moved, out):
+    sec = lax.axis_index("sec")
+
+    @pl.when(sec < 2)
+    def _():
+        out[...] = own[...]
+
+    @pl.when(sec >= 2)
+    def _():
+        out[...] = moved[...]
 
 
 def attend(
-    mine, other, queries, upstream, key_w, value_w, hidden, context, away, kept, keys, values, dkeys, dvalues
+    first, second, beside, queries, upstream, key_w, value_w, hidden, context, away, kept, keys, values, dkeys, dvalues
 ):
     tp = lax.axis_index("tp")
     sec = lax.axis_index("sec")
-    token_count, half = mine.shape
+    token_count, half = first.shape
     width = 2 * half
     scale = 1.0 / math.sqrt(HD)
 
     @pl.when(sec != 0)
     def _():
+        even = sec % 2 == 0
+        mine = jnp.where(sec == 1, beside[...], jnp.where(even, first[...], second[...]))
+        other = jnp.where(even | (sec == 1), second[...], first[...])
         for weight, target in ((key_w, keys), (value_w, values)):
-            value = matmul(mine[...], weight[part(tp, half), :])
-            value = value + matmul(other[...], weight[part(1 - tp, half), :])
+            value = matmul(mine, weight[part(tp, half), :])
+            value = value + matmul(other, weight[part(1 - tp, half), :])
             target[...] = value.astype(LOW)
         heads = [
             (slice(s * SEQ, (s + 1) * SEQ), slice(h * HD, (h + 1) * HD))
@@ -358,14 +373,10 @@
     returned = {0: total(own_away, own_kept)}
     arriving[0] = hold(arriving[0], [own_away])
     others = [swap(arriving[0], "tp", 1)]
-    sources = [query_weight[0], key_weight[0], value_weight[0], cotangent[0]]
-    high, low, query_w, key_w, value_w, upstream = call(
+    high, low = call(
         functools.partial(mixing, experts),
-        [shape_of((experts, token_count, capacity))] * 2 + [shape_of(x.shape) for x in sources],
-        [route_rows, gate_rows, earlier, *sources],
-        [pltpu.SemaphoreType.DMA((len(sources),))],
-        remote=(3, 4, 5, 6),
-        limit=40,
+        [shape_of((experts, token_count, capacity))] * 2,
+        [route_rows, gate_rows, earlier],
         after=[arriving[0]],
     )
     others.append(swap(arriving[1], "tp", 1))
@@ -394,23 +405,27 @@
     beside = swap(hidden_half, "sec", 1)
     hidden_other = swap(hidden_half, "tp", 1)
     encoder_half = jnp.where(sec == 1, beside, hidden_half)
-    first = jnp.where(sec == 0, hidden_other, hidden_half)
+    moved = hidden_half
     for i in range(1, sections // 2):
-        pairs = [(t, 2 * i * tp_size + t) for t in range(tp_size)]
-        pairs += [(tp_size + t, (2 * i + 1) * tp_size + (t ^ 1)) for t in range(tp_size)]
-        moved = lax.ppermute(encoder_half, ("sec", "tp"), pairs)
-        first = jnp.where(sec // 2 == i, moved, first)
+        targets = {j: j for j in range(sections * tp_size)}
+        for t in range(tp_size):
+            even, odd = 2 * i * tp_size + t, (2 * i + 1) * tp_size + (t ^ 1)
+            targets |= {t: even, even: t, tp_size + t: odd, odd: tp_size + t}
+        arrived = lax.ppermute(encoder_half, ("sec", "tp"), list(targets.items()))
+        moved = arrived if sections == 4 else jnp.where(sec // 2 == i, arrived, moved)
+    first = call(choose, [shape_of(hidden_half.shape)], [hidden_other, moved])[0]
     second = swap(first, "sec", 1)
-    mine = jnp.where(sec == 1, beside, jnp.where(sec % 2 == 0, first, second))
-    other = jnp.where((sec % 2 == 0) | (sec == 1), second, first)
 
     local_width = query_weight.shape[2]
-    queries = call(
+    sources = [key_weight[0], value_weight[0], cotangent[0]]
+    queries, key_w, value_w, upstream = call(
         project,
-        [shape_of((token_count, local_width))],
-        [hidden_half, hidden_other, attn_gain, query_w],
+        [shape_of((token_count, local_width))] + [shape_of(x.shape) for x in sources],
+        [hidden_half, hidden_other, attn_gain, query_weight[0], *sources],
+        [pltpu.SemaphoreType.DMA((len(sources),))],
         flops=2 * token_count * model_width * local_width,
-    )[0]
+        remote=(4, 5, 6),
+    )
     context, away, kept = call(
         attend,
         [
@@ -418,7 +433,7 @@
             shape_of((token_count, model_width // 2)),
             shape_of((token_count, model_width // 2), WIDE),
         ],
-        [mine, other, queries, upstream, key_w, value_w, hidden_half],
+        [first, second, beside, queries, upstream, key_w, value_w, hidden_half],
         [pltpu.VMEM((token_count, local_width), LOW)] * 4,
         flops=10 * token_count * model_width * local_width,
     )

time: 83.3 us -> 80.7 us (0.969)
  starting transfers between devices: 37.4 us -> 33.8 us
  waiting for transfers between devices: 26.5 us -> 28.1 us
  other arithmetic: 1.92 us -> 0.86 us
    ppermute x16, waiting for transfers between devices: 18.8 us -> 23.1 us  [swap(): return lax.ppermute(block, axis, [(i, i ^ step) for i in range(size)])]
    ppermute x1, waiting for transfers between devices: 2.94 us -> 0.01 us  [shards(): arrived = lax.ppermute(encoder_half, ('sec', 'tp'), list(targets.items()))]
    ppermute x1, starting transfers between devices: 4.08 us -> 1.56 us  [shards(): arrived = lax.ppermute(encoder_half, ('sec', 'tp'), list(targets.items()))]
    ppermute x3, starting transfers between devices: 5.22 us -> 3.57 us  [shards(): total = total + lax.ppermute(blocks[k], ('sec', 'tp'), pairs).astype(WIDE)]
    select_n x2 -> x0, other arithmetic: 1.04 us -> none  [the longest x1 1 us: shards(): other = jnp.where((sec % 2 == 0) | (sec == 1), second, first)]
    pallas_call x12 -> x13, Pallas kernels: 14.2 us -> 14.9 us  [call(): pl.pallas_call(run, out_shape=[*out_shape, *(shape_of(x.shape, x.dtype) f...]
    unnamed x22 -> x18, local copies, waits for them, and re-layouts: 2.24 us -> 1.97 us
  transfers between devices with their start and end apart: 20 -> 20, of which waited for: 15 -> 14; matrix products, arithmetic and copies ran while one was open for 0% -> 0% of each run, Pallas kernels for 14% -> 14%
where the time goes in v8:
time: 80.7 us; the launch traced here: 80.5 us
  starting transfers between devices  33.8 us (42%)
  waiting for transfers between devices  28.1 us (35%)
  Pallas kernels  14.9 us (18%)
  local copies, waits for them, and re-layouts  1.97 us (2%)
  other arithmetic  0.86 us (1%)
  between operations  0.85 us (1%)
    ppermute x16, starting transfers between devices, swap(): return lax.ppermute(block, axis, [(i, i ^ step) for i in range(size)])  28.7 us
    ppermute x16, waiting for transfers between devices, swap(): return lax.ppermute(block, axis, [(i, i ^ step) for i in range(size)])  23.1 us
    pallas_call x13, Pallas kernels, call(): pl.pallas_call(run, out_shape=[*out_shape, *(shape_of(x.shape, x.dtype) f...  14.9 us
    ppermute x3, waiting for transfers between devices, shards(): total = total + lax.ppermute(blocks[k], ('sec', 'tp'), pairs).astype(WIDE)  4.97 us
    ppermute x3, starting transfers between devices, shards(): total = total + lax.ppermute(blocks[k], ('sec', 'tp'), pairs).astype(WIDE)  3.57 us
    unnamed x18, local copies, waits for them, and re-layouts  1.97 us
  transfers between devices with their start and end apart: 20, of which 14 were waited for; matrix products, arithmetic and copies ran while one was open for 0% of the time, Pallas kernels for 14%

profile of v8, /device:TPU:0, one launch (start us, length us, event | category | flops | bytes accessed | tf_op | source)
XLA Modules:
  0.0 80.5 jit_solution(11114402925341178122)
XLA Ops:
  0.7 1.0 %copy-done.3 = bf16[1,256,1024]{2,1,0:T(8,128)(2,1)S(1)} copy-done((bf16[1,256,1024]{2,1,0:T(8,128)(2,1)S(1)}, bf16[1,256,1024]{2,1,0:T(8,128)(2,1)}, u32[]{:S(2)}) %copy-start.3) | copy-done | bytes 524312
  1.7 0.9 %shard_map.123 = (bf16[192,512]{1,0:T(8,128)(2,1)S(1)}, bf16[192,512]{1,0:T(8,128)(2,1)S(1)}, bf16[192,1024]{1,0:T(8,128)(2,1)S(1)}, bf16[192,1024]{1,0:T(8,128)(2,1)S(1)}) custom-call(bf16[256,1024]{1,0:T(8,128)(2,1)S(1)} %bitcast.17, s32[2,256]{1,0:T(2,128)S(1)} %bitcast.20, f32[1,1024]{1,0:T(1,128)S(1)} %copy-done.8, ...), custom_call_target="tpu_custom_call" | custom-call | flops 402653184 | bytes 1841152 | tf_op jit(solution)/shard_map/pallas_call | solution.py:40
  2.6 4.1 %collective-permute-start = (bf16[192,512]{1,0:T(8,128)(2,1)S(1)}, bf16[192,512]{1,0:T(8,128)(2,1)S(1)}, u32[]{:S(2)}, u32[]{:S(2)}) collective-permute-start(bf16[192,512]{1,0:T(8,128)(2,1)S(1)} %get-tuple-element.35), channel_id=1, source_target_pairs={{0,4},{2,6},{4,0},{6,2},{1,5},{3,7},{5,1},{7,3},{8,12},{10,14},{12... | collective-permute-start | bytes 589832 | tf_op jit(solution)/shard_map/ppermute | solution.py:283
  6.7 4.6 %shard_map.124 = (bf16[192,512]{1,0:T(8,128)(2,1)S(1)}, f32[192,512]{1,0:T(8,128)S(1)}, bf16[1024,2048]{1,0:T(8,128)(2,1)S(1)}, bf16[2048,1024]{1,0:T(8,128)(2,1...) custom-call(bf16[192,1024]{1,0:T(8,128)(2,1)S(1)} %get-tuple-element, ...), custom_call_target="tpu_custom_call", output_to_operand_aliasing={{4}: (3, {}), {5}: (4, {})} | custom-call | flops 1610612736 | bytes 17760256 | tf_op jit(solution)/shard_map/pallas_call | solution.py:40
  11.2 1.6 %collective-permute-start.1 = (bf16[192,512]{1,0:T(8,128)(2,1)S(1)}, bf16[192,512]{1,0:T(8,128)(2,1)S(1)}, u32[]{:S(2)}, u32[]{:S(2)}) collective-permute-start(bf16[192,512]{1,0:T(8,128)(2,1)S(1)} %get-tuple-element.34.refs_0_), channel_id=1, source_target_pairs={{0,1},{1,0},{2,3},{3,2},{4,5},{5,4},{6,7},{7,6},{8,9},{9,8},{10,11... | collective-permute-start | bytes 589832 | tf_op jit(solution)/shard_map/ppermute | solution.py:283
  12.8 1.6 %collective-permute-start.2 = (bf16[192,1024]{1,0:T(8,128)(2,1)S(1)}, bf16[192,1024]{1,0:T(8,128)(2,1)S(1)}, u32[]{:S(2)}, u32[]{:S(2)}) collective-permute-start(bf16[192,1024]{1,0:T(8,128)(2,1)S(1)} %get-tuple-element.39), channel_id=1, source_target_pairs={{0,2},{2,0},{4,6},{6,4},{1,3},{3,1},{5,7},{7,5},{8,10},{10,8},{12,... | collective-permute-start | bytes 1179656 | tf_op jit(solution)/shard_map/ppermute | solution.py:283
  14.4 0.2 collective-permute-start.8
  14.6 1.3 %collective-permute-done.refs_1_ = bf16[192,512]{1,0:T(8,128)(2,1)S(1)} collective-permute-done((bf16[192,512]{1,0:T(8,128)(2,1)S(1)}, bf16[192,512]{1,0:T(8,128)(2,1)S(1)}, u32[]{:S(2)}, u32[]{:S(2)}) %collective-permute-start) | collective-permute-done | bytes 196640 | tf_op jit(solution)/shard_map/ppermute | solution.py:283
  15.9 2.4 %collective-permute-start.3 = (bf16[192,512]{1,0:T(8,128)(2,1)S(1)}, bf16[192,512]{1,0:T(8,128)(2,1)S(1)}, u32[]{:S(2)}, u32[]{:S(2)}) collective-permute-start(bf16[192,512]{1,0:T(8,128)(2,1)S(1)} %shard_map.125.refs_3_.refs_0_), channel_id=1, source_target_pairs={{0,1},{1,0},{2,3},{3,2},{4,5},{5,4},{6,7},{7,6},{8,9},{9,8},{10,11... | collective-permute-start | bytes 589832 | tf_op jit(solution)/shard_map/ppermute | solution.py:283
  18.2 0.6 shard_map.126
  18.9 3.0 %collective-permute-done.3.refs_1_ = bf16[192,512]{1,0:T(8,128)(2,1)S(1)} collective-permute-done((bf16[192,512]{1,0:T(8,128)(2,1)S(1)}, bf16[192,512]{1,0:T(8,128)(2,1)S(1)}, u32[]{:S(2)}, u32[]{:S(2)}) %collective-permute-start.3) | collective-permute-done | bytes 196640 | tf_op jit(solution)/shard_map/ppermute | solution.py:283
  21.9 1.8 %shard_map.127 = (bf16[192,512]{1,0:T(8,128)(2,1)S(1)}, f32[192,512]{1,0:T(8,128)S(1)}) custom-call(bf16[192,512]{1,0:T(8,128)(2,1)S(1)} %shard_map.125.refs_3_.refs_0_, bf16[192,512]{1,0:T(8,128)(2,1)S(1)} %collective-permute-done.3.refs_1_, bf16[1024,2048]{1,0:T(8,128)(2,1)S(1)} %get-tuple-element.40.refs_2_.refs_1_, ...), custom_call_target="tpu_custom_call" | custom-call | flops 1610612736 | bytes 9371648 | tf_op jit(solution)/shard_map/pallas_call | solution.py:40
  23.7 2.1 %collective-permute-start.6 = (bf16[192,512]{1,0:T(8,128)(2,1)S(1)}, bf16[192,512]{1,0:T(8,128)(2,1)S(1)}, u32[]{:S(2)}, u32[]{:S(2)}) collective-permute-start(bf16[192,512]{1,0:T(8,128)(2,1)S(1)} %get-tuple-element.42.refs_3_), channel_id=1, source_target_pairs={{0,1},{1,0},{2,3},{3,2},{4,5},{5,4},{6,7},{7,6},{8,9},{9,8},{10,11... | collective-permute-start | bytes 589832 | tf_op jit(solution)/shard_map/ppermute | solution.py:283
  25.8 1.4 %collective-permute-done.8.refs_0_ = bf16[192,512]{1,0:T(8,128)(2,1)S(1)} collective-permute-done((bf16[192,512]{1,0:T(8,128)(2,1)S(1)}, bf16[192,512]{1,0:T(8,128)(2,1)S(1)}, u32[]{:S(2)}, u32[]{:S(2)}) %collective-permute-start.8) | collective-permute-done | bytes 196640 | tf_op jit(solution)/shard_map/ppermute | solution.py:283
  27.2 0.5 collective-permute-start.9
  27.7 0.7 collective-permute-done.2.refs_0_
  28.4 1.8 %shard_map.128 = (bf16[192,512]{1,0:T(8,128)(2,1)S(1)}, f32[192,512]{1,0:T(8,128)S(1)}) custom-call(bf16[192,1024]{1,0:T(8,128)(2,1)S(1)} %collective-permute-done.2.refs_0_, bf16[1024,2048]{1,0:T(8,128)(2,1)S(1)} %get-tuple-element.40.refs_2_.refs_1_, bf16[2048,1024]{1,0:T(8,128)(2,1)S(1)} %get-tuple-element.41.refs_3_.refs_2_, ...), custom_call_target="tpu_custom_call" | custom-call | flops 1610612736 | bytes 9371648 | tf_op jit(solution)/shard_map/pallas_call | solution.py:40
  30.2 1.6 %collective-permute-start.4 = (bf16[192,512]{1,0:T(8,128)(2,1)S(1)}, bf16[192,512]{1,0:T(8,128)(2,1)S(1)}, u32[]{:S(2)}, u32[]{:S(2)}) collective-permute-start(bf16[192,512]{1,0:T(8,128)(2,1)S(1)} %get-tuple-element.44.refs_4_), channel_id=1, source_target_pairs={{0,1},{1,0},{2,3},{3,2},{4,5},{5,4},{6,7},{7,6},{8,9},{9,8},{10,11... | collective-permute-start | bytes 589832 | tf_op jit(solution)/shard_map/ppermute | solution.py:283
  31.9 1.5 %collective-permute-start.7 = (bf16[192,512]{1,0:T(8,128)(2,1)S(1)}, bf16[192,512]{1,0:T(8,128)(2,1)S(1)}, u32[]{:S(2)}, u32[]{:S(2)}) collective-permute-start(bf16[192,512]{1,0:T(8,128)(2,1)S(1)} %add_convert_fusion.1.refs_5_), channel_id=1, source_target_pairs={{0,4},{2,6},{4,0},{6,2},{1,5},{3,7},{5,1},{7,3},{8,12},{10,14},{12... | collective-permute-start | bytes 589832 | tf_op jit(solution)/shard_map/ppermute | solution.py:283
  33.4 1.3 %collective-permute-done.9.refs_1_ = bf16[192,512]{1,0:T(8,128)(2,1)S(1)} collective-permute-done((bf16[192,512]{1,0:T(8,128)(2,1)S(1)}, bf16[192,512]{1,0:T(8,128)(2,1)S(1)}, u32[]{:S(2)}, u32[]{:S(2)}) %collective-permute-start.9) | collective-permute-done | bytes 196640 | tf_op jit(solution)/shard_map/ppermute | solution.py:283
  34.7 1.8 %shard_map.129 = (bf16[192,512]{1,0:T(8,128)(2,1)S(1)}, f32[192,512]{1,0:T(8,128)S(1)}) custom-call(bf16[192,512]{1,0:T(8,128)(2,1)S(1)} %collective-permute-done.8.refs_0_, bf16[192,512]{1,0:T(8,128)(2,1)S(1)} %collective-permute-done.9.refs_1_, bf16[1024,2048]{1,0:T(8,128)(2,1)S(1)} %get-tuple-element.40.refs_2_.refs_1_, ...), custom_call_target="tpu_custom_call" | custom-call | flops 1610612736 | bytes 9371648 | tf_op jit(solution)/shard_map/pallas_call | solution.py:40
  36.5 1.3 %collective-permute-start.10 = (bf16[192,512]{1,0:T(8,128)(2,1)S(1)}, bf16[192,512]{1,0:T(8,128)(2,1)S(1)}, u32[]{:S(2)}, u32[]{:S(2)}) collective-permute-start(bf16[192,512]{1,0:T(8,128)(2,1)S(1)} %get-tuple-element.48), channel_id=1, source_target_pairs={{0,1},{1,0},{2,3},{3,2},{4,5},{5,4},{6,7},{7,6},{8,9},{9,8},{10,11... | collective-permute-start | bytes 589832 | tf_op jit(solution)/shard_map/ppermute | solution.py:283
  37.8 0.7 collective-permute-done.4
  38.5 2.4 %collective-permute-start.5 = (bf16[192,512]{1,0:T(8,128)(2,1)S(1)}, bf16[192,512]{1,0:T(8,128)(2,1)S(1)}, u32[]{:S(2)}, u32[]{:S(2)}) collective-permute-start(bf16[192,512]{1,0:T(8,128)(2,1)S(1)} %add_convert_fusion.2), channel_id=1, source_target_pairs={{0,2},{2,0},{4,6},{6,4},{1,3},{3,1},{5,7},{7,5},{8,10},{10,8},{12,... | collective-permute-start | bytes 589832 | tf_op jit(solution)/shard_map/ppermute | solution.py:283
  41.0 1.3 %collective-permute-done.10 = bf16[192,512]{1,0:T(8,128)(2,1)S(1)} collective-permute-done((bf16[192,512]{1,0:T(8,128)(2,1)S(1)}, bf16[192,512]{1,0:T(8,128)(2,1)S(1)}, u32[]{:S(2)}, u32[]{:S(2)}) %collective-permute-start.10) | collective-permute-done | bytes 196640 | tf_op jit(solution)/shard_map/ppermute | solution.py:283
  42.3 5.2 %collective-permute-start.11 = (bf16[192,512]{1,0:T(8,128)(2,1)S(1)}, bf16[192,512]{1,0:T(8,128)(2,1)S(1)}, u32[]{:S(2)}, u32[]{:S(2)}) collective-permute-start(bf16[192,512]{1,0:T(8,128)(2,1)S(1)} %add_convert_fusion), channel_id=1, source_target_pairs={{0,6},{2,4},{4,2},{6,0},{1,7},{3,5},{5,3},{7,1},{8,14},{10,12},{12... | collective-permute-start | bytes 589832 | tf_op jit(solution)/shard_map/ppermute | solution.py:283
  47.5 1.8 %collective-permute-done.5.refs_4_ = bf16[192,512]{1,0:T(8,128)(2,1)S(1)} collective-permute-done((bf16[192,512]{1,0:T(8,128)(2,1)S(1)}, bf16[192,512]{1,0:T(8,128)(2,1)S(1)}, u32[]{:S(2)}, u32[]{:S(2)}) %collective-permute-start.5) | collective-permute-done | bytes 196640 | tf_op jit(solution)/shard_map/ppermute | solution.py:283
  49.3 2.7 %collective-permute-done.11.refs_6_ = bf16[192,512]{1,0:T(8,128)(2,1)S(1)} collective-permute-done((bf16[192,512]{1,0:T(8,128)(2,1)S(1)}, bf16[192,512]{1,0:T(8,128)(2,1)S(1)}, u32[]{:S(2)}, u32[]{:S(2)}) %collective-permute-start.11) | collective-permute-done | bytes 196640 | tf_op jit(solution)/shard_map/ppermute | solution.py:283
  51.9 0.7 shard_map.130.refs_0_.refs_7_
  52.6 0.1 collective-permute-start.13
  52.7 1.6 %collective-permute-start.12 = (bf16[256,512]{1,0:T(8,128)(2,1)S(1)}, bf16[256,512]{1,0:T(8,128)(2,1)S(1)}, u32[]{:S(2)}, u32[]{:S(2)}) collective-permute-start(bf16[256,512]{1,0:T(8,128)(2,1)S(1)} %shard_map.130.refs_0_.refs_7_), channel_id=1, source_target_pairs={{0,1},{1,0},{2,3},{3,2},{4,5},{5,4},{6,7},{7,6},{8,9},{9,8},{10,11... | collective-permute-start | bytes 786440 | tf_op jit(solution)/shard_map/ppermute | solution.py:283
  54.3 0.0 collective-permute-done.13.refs_2_
  54.4 1.6 %collective-permute-start.14 = (bf16[256,512]{1,0:T(8,128)(2,1)S(1)}, bf16[256,512]{1,0:T(8,128)(2,1)S(1)}, u32[]{:S(2)}, u32[]{:S(2)}) collective-permute-start(bf16[256,512]{1,0:T(8,128)(2,1)S(1)} %broadcast_select_fusion), channel_id=1, source_target_pairs={{0,16},{1,17},{8,25},{9,24},{16,0},{17,1},{24,9},{25,8},{2,18},{3,... | collective-permute-start | bytes 786440 | tf_op jit(solution)/shard_map/ppermute | solution.py:414
  55.9 7.9 %collective-permute-done.12.refs_0_.refs_1_ = bf16[256,512]{1,0:T(8,128)(2,1)S(1)} collective-permute-done((bf16[256,512]{1,0:T(8,128)(2,1)S(1)}, bf16[256,512]{1,0:T(8,128)(2,1)S(1)}, u32[]{:S(2)}, u32[]{:S(2)}) %collective-permute-start.12) | collective-permute-done | bytes 262176 | tf_op jit(solution)/shard_map/ppermute | solution.py:283
  63.8 0.7 collective-permute-start.15
  64.5 0.9 %copy-done.4 = bf16[1,256,512]{2,1,0:T(8,128)(2,1)S(1)} copy-done((bf16[1,256,512]{2,1,0:T(8,128)(2,1)S(1)}, bf16[1,256,512]{2,1,0:T(8,128)(2,1)}, u32[]{:S(2)}) %copy-start.4) | copy-done | bytes 262168
  65.5 0.9 %shard_map.132 = (bf16[256,512]{1,0:T(8,128)(2,1)S(1)}, bf16[1024,512]{1,0:T(8,128)(2,1)S(1)}, bf16[1024,512]{1,0:T(8,128)(2,1)S(1)}, bf16[256,512]{1,0:T(8,128)(2,1)S(1)}) custom-call(bf16[256,512]{1,0:T(8,128)(2,1)S(1)} %shard_map.130.refs_0_.refs_7_, bf16[256,512]{1,0:T(8,128)(2,1)S(1)} %collective-permute-done.12.refs_0_.refs_1_, ...), custom_call_target="tpu_custom_call" | custom-call | flops 268435456 | bytes 6557696 | tf_op jit(solution)/shard_map/pallas_call | solution.py:40
  66.4 1.7 %shard_map.133 = (bf16[256,512]{1,0:T(8,128)(2,1)}, bf16[256,512]{1,0:T(8,128)(2,1)S(1)}, f32[256,512]{1,0:T(8,128)S(1)}) custom-call(bf16[256,512]{1,0:T(8,128)(2,1)S(1)} %shard_map.131.refs_0_, bf16[256,512]{1,0:T(8,128)(2,1)S(1)} %collective-permute-done.15.refs_1_, bf16[256,512]{1,0:T(8,128)(2,1)} %collective-permute-done.13.refs_2_, ...), custom_call_target="tpu_custom_call" | custom-call | flops 1342177280 | bytes 4718592 | tf_op jit(solution)/shard_map/pallas_call | solution.py:40
  68.1 1.9 %collective-permute-start.16 = (bf16[256,512]{1,0:T(8,128)(2,1)S(1)}, bf16[256,512]{1,0:T(8,128)(2,1)S(1)}, u32[]{:S(2)}, u32[]{:S(2)}) collective-permute-start(bf16[256,512]{1,0:T(8,128)(2,1)S(1)} %get-tuple-element.55), channel_id=1, source_target_pairs={{0,8},{8,0},{16,24},{24,16},{1,9},{9,1},{17,25},{25,17},{2,10},{10... | collective-permute-start | bytes 786440 | tf_op jit(solution)/shard_map/ppermute | solution.py:283
  70.0 1.2 %collective-permute-done.16.refs_1_ = bf16[256,512]{1,0:T(8,128)(2,1)S(1)} collective-permute-done((bf16[256,512]{1,0:T(8,128)(2,1)S(1)}, bf16[256,512]{1,0:T(8,128)(2,1)S(1)}, u32[]{:S(2)}, u32[]{:S(2)}) %collective-permute-start.16) | collective-permute-done | bytes 262176 | tf_op jit(solution)/shard_map/ppermute | solution.py:283
  71.2 0.1 shard_map.134
  71.3 1.9 %collective-permute-start.17 = (bf16[256,128]{1,0:T(8,128)(2,1)S(1)}, bf16[256,128]{1,0:T(8,128)(2,1)S(1)}, u32[]{:S(2)}, u32[]{:S(2)}) collective-permute-start(bf16[256,128]{1,0:T(8,128)(2,1)S(1)} %get-tuple-element.57), channel_id=1, source_target_pairs={{0,1},{1,0},{8,9},{9,8},{16,17},{17,16},{24,25},{25,24},{2,3},{3,2... | collective-permute-start | bytes 196616 | tf_op jit(solution)/shard_map/ppermute | solution.py:456
  73.2 1.5 %collective-permute-start.18 = (bf16[256,128]{1,0:T(8,128)(2,1)S(1)}, bf16[256,128]{1,0:T(8,128)(2,1)S(1)}, u32[]{:S(2)}, u32[]{:S(2)}) collective-permute-start(bf16[256,128]{1,0:T(8,128)(2,1)S(1)} %get-tuple-element.58), channel_id=1, source_target_pairs={{0,16},{1,17},{8,24},{9,25},{16,0},{17,1},{24,8},{25,9},{2,18},{3,... | collective-permute-start | bytes 196616 | tf_op jit(solution)/shard_map/ppermute | solution.py:456
  74.7 0.2 collective-permute-start.19
  74.8 0.9 %collective-permute-done.17 = bf16[256,128]{1,0:T(8,128)(2,1)S(1)} collective-permute-done((bf16[256,128]{1,0:T(8,128)(2,1)S(1)}, bf16[256,128]{1,0:T(8,128)(2,1)S(1)}, u32[]{:S(2)}, u32[]{:S(2)}) %collective-permute-start.17) | collective-permute-done | bytes 65568 | tf_op jit(solution)/shard_map/ppermute | solution.py:456
  75.8 2.1 %collective-permute-done.18 = bf16[256,128]{1,0:T(8,128)(2,1)S(1)} collective-permute-done((bf16[256,128]{1,0:T(8,128)(2,1)S(1)}, bf16[256,128]{1,0:T(8,128)(2,1)S(1)}, u32[]{:S(2)}, u32[]{:S(2)}) %collective-permute-start.18) | collective-permute-done | bytes 65568 | tf_op jit(solution)/shard_map/ppermute | solution.py:456
  77.9 1.9 %collective-permute-done.19 = bf16[256,128]{1,0:T(8,128)(2,1)S(1)} collective-permute-done((bf16[256,128]{1,0:T(8,128)(2,1)S(1)}, bf16[256,128]{1,0:T(8,128)(2,1)S(1)}, u32[]{:S(2)}, u32[]{:S(2)}) %collective-permute-start.19) | collective-permute-done | bytes 65568 | tf_op jit(solution)/shard_map/ppermute | solution.py:456
  79.8 0.7 add_convert_fusion.4
  (29 shorter events, 0.3 us)
Async XLA Ops:
  0.6 1.0 %copy-start.3 = (bf16[1,256,1024]{2,1,0:T(8,128)(2,1)S(1)}, bf16[1,256,1024]{2,1,0:T(8,128)(2,1)}, u32[]{:S(2)}) copy-start(bf16[1,256,1024]{2,1,0:T(8,128)(2,1)} %param.11) | copy-start | bytes 1572868
  0.6 1.0 %copy-start.6 = (s32[1,256,2]{1,2,0:T(2,128)S(1)}, s32[1,256,2]{1,2,0:T(2,128)}, u32[]{:S(2)}) copy-start(s32[1,256,2]{1,2,0:T(2,128)} %param.12) | copy-start | bytes 6148
  0.6 1.0 %copy-start.8 = (f32[1,1024]{1,0:T(1,128)S(1)}, f32[1,1024]{1,0:T(1,128)}, u32[]{:S(2)}) copy-start(f32[1,1024]{1,0:T(1,128)} %refs_2_.2) | copy-start | bytes 12292
  2.6 13.3 %collective-permute-start = (bf16[192,512]{1,0:T(8,128)(2,1)S(1)}, bf16[192,512]{1,0:T(8,128)(2,1)S(1)}, u32[]{:S(2)}, u32[]{:S(2)}) collective-permute-start(bf16[192,512]{1,0:T(8,128)(2,1)S(1)} %get-tuple-element.35), channel_id=1, source_target_pairs={{0,4},{2,6},{4,0},{6,2},{1,5},{3,7},{5,1},{7,3},{8,12},{10,14},{12... | collective-permute-start | bytes 589832 | tf_op jit(solution)/shard_map/ppermute | solution.py:283
  6.7 11.6 %copy-start.7 = (f32[1,256,2]{1,2,0:T(2,128)S(1)}, f32[1,256,2]{1,2,0:T(2,128)}, u32[]{:S(2)}) copy-start(f32[1,256,2]{1,2,0:T(2,128)} %param.13) | copy-start | bytes 6148
  11.2 7.6 %collective-permute-start.1 = (bf16[192,512]{1,0:T(8,128)(2,1)S(1)}, bf16[192,512]{1,0:T(8,128)(2,1)S(1)}, u32[]{:S(2)}, u32[]{:S(2)}) collective-permute-start(bf16[192,512]{1,0:T(8,128)(2,1)S(1)} %get-tuple-element.34.refs_0_), channel_id=1, source_target_pairs={{0,1},{1,0},{2,3},{3,2},{4,5},{5,4},{6,7},{7,6},{8,9},{9,8},{10,11... | collective-permute-start | bytes 589832 | tf_op jit(solution)/shard_map/ppermute | solution.py:283
  12.8 15.6 %collective-permute-start.2 = (bf16[192,1024]{1,0:T(8,128)(2,1)S(1)}, bf16[192,1024]{1,0:T(8,128)(2,1)S(1)}, u32[]{:S(2)}, u32[]{:S(2)}) collective-permute-start(bf16[192,1024]{1,0:T(8,128)(2,1)S(1)} %get-tuple-element.39), channel_id=1, source_target_pairs={{0,2},{2,0},{4,6},{6,4},{1,3},{3,1},{5,7},{7,5},{8,10},{10,8},{12,... | collective-permute-start | bytes 1179656 | tf_op jit(solution)/shard_map/ppermute | solution.py:283
  14.4 12.8 %collective-permute-start.8 = (bf16[192,512]{1,0:T(8,128)(2,1)S(1)}, bf16[192,512]{1,0:T(8,128)(2,1)S(1)}, u32[]{:S(2)}, u32[]{:S(2)}) collective-permute-start(bf16[192,512]{1,0:T(8,128)(2,1)S(1)} %get-tuple-element.46), channel_id=1, source_target_pairs={{0,6},{2,4},{4,2},{6,0},{1,7},{3,5},{5,3},{7,1},{8,14},{10,12},{12... | collective-permute-start | bytes 589832 | tf_op jit(solution)/shard_map/ppermute | solution.py:283
  15.9 6.0 %collective-permute-start.3 = (bf16[192,512]{1,0:T(8,128)(2,1)S(1)}, bf16[192,512]{1,0:T(8,128)(2,1)S(1)}, u32[]{:S(2)}, u32[]{:S(2)}) collective-permute-start(bf16[192,512]{1,0:T(8,128)(2,1)S(1)} %shard_map.125.refs_3_.refs_0_), channel_id=1, source_target_pairs={{0,1},{1,0},{2,3},{3,2},{4,5},{5,4},{6,7},{7,6},{8,9},{9,8},{10,11... | collective-permute-start | bytes 589832 | tf_op jit(solution)/shard_map/ppermute | solution.py:283
  23.7 8.2 %collective-permute-start.6 = (bf16[192,512]{1,0:T(8,128)(2,1)S(1)}, bf16[192,512]{1,0:T(8,128)(2,1)S(1)}, u32[]{:S(2)}, u32[]{:S(2)}) collective-permute-start(bf16[192,512]{1,0:T(8,128)(2,1)S(1)} %get-tuple-element.42.refs_3_), channel_id=1, source_target_pairs={{0,1},{1,0},{2,3},{3,2},{4,5},{5,4},{6,7},{7,6},{8,9},{9,8},{10,11... | collective-permute-start | bytes 589832 | tf_op jit(solution)/shard_map/ppermute | solution.py:283
  27.2 7.4 %collective-permute-start.9 = (bf16[192,512]{1,0:T(8,128)(2,1)S(1)}, bf16[192,512]{1,0:T(8,128)(2,1)S(1)}, u32[]{:S(2)}, u32[]{:S(2)}) collective-permute-start(bf16[192,512]{1,0:T(8,128)(2,1)S(1)} %collective-permute-done.8.refs_0_), channel_id=1, source_target_pairs={{0,1},{1,0},{2,3},{3,2},{4,5},{5,4},{6,7},{7,6},{8,9},{9,8},{10,11... | collective-permute-start | bytes 589832 | tf_op jit(solution)/shard_map/ppermute | solution.py:283
  30.2 8.2 %collective-permute-start.4 = (bf16[192,512]{1,0:T(8,128)(2,1)S(1)}, bf16[192,512]{1,0:T(8,128)(2,1)S(1)}, u32[]{:S(2)}, u32[]{:S(2)}) collective-permute-start(bf16[192,512]{1,0:T(8,128)(2,1)S(1)} %get-tuple-element.44.refs_4_), channel_id=1, source_target_pairs={{0,1},{1,0},{2,3},{3,2},{4,5},{5,4},{6,7},{7,6},{8,9},{9,8},{10,11... | collective-permute-start | bytes 589832 | tf_op jit(solution)/shard_map/ppermute | solution.py:283
  31.9 15.6 %collective-permute-start.7 = (bf16[192,512]{1,0:T(8,128)(2,1)S(1)}, bf16[192,512]{1,0:T(8,128)(2,1)S(1)}, u32[]{:S(2)}, u32[]{:S(2)}) collective-permute-start(bf16[192,512]{1,0:T(8,128)(2,1)S(1)} %add_convert_fusion.1.refs_5_), channel_id=1, source_target_pairs={{0,4},{2,6},{4,0},{6,2},{1,5},{3,7},{5,1},{7,3},{8,12},{10,14},{12... | collective-permute-start | bytes 589832 | tf_op jit(solution)/shard_map/ppermute | solution.py:283
  36.5 28.0 %copy-start = (bf16[1,1024,512]{2,1,0:T(8,128)(2,1)S(1)}, bf16[1,1024,512]{2,1,0:T(8,128)(2,1)}, u32[]{:S(2)}) copy-start(bf16[1,1024,512]{2,1,0:T(8,128)(2,1)} %param.18) | copy-start | bytes 3145732
  36.5 28.0 %copy-start.1 = (bf16[1,1024,512]{2,1,0:T(8,128)(2,1)S(1)}, bf16[1,1024,512]{2,1,0:T(8,128)(2,1)}, u32[]{:S(2)}) copy-start(bf16[1,1024,512]{2,1,0:T(8,128)(2,1)} %param.19) | copy-start | bytes 3145732
  36.5 28.0 %copy-start.2 = (bf16[1,1024,512]{2,1,0:T(8,128)(2,1)S(1)}, bf16[1,1024,512]{2,1,0:T(8,128)(2,1)}, u32[]{:S(2)}) copy-start(bf16[1,1024,512]{2,1,0:T(8,128)(2,1)} %param.20) | copy-start | bytes 3145732
  36.5 28.0 %copy-start.5 = (f32[1,1024]{1,0:T(1,128)S(1)}, f32[1,1024]{1,0:T(1,128)}, u32[]{:S(2)}) copy-start(f32[1,1024]{1,0:T(1,128)} %refs_2_.3) | copy-start | bytes 12292
  36.5 5.7 %collective-permute-start.10 = (bf16[192,512]{1,0:T(8,128)(2,1)S(1)}, bf16[192,512]{1,0:T(8,128)(2,1)S(1)}, u32[]{:S(2)}, u32[]{:S(2)}) collective-permute-start(bf16[192,512]{1,0:T(8,128)(2,1)S(1)} %get-tuple-element.48), channel_id=1, source_target_pairs={{0,1},{1,0},{2,3},{3,2},{4,5},{5,4},{6,7},{7,6},{8,9},{9,8},{10,11... | collective-permute-start | bytes 589832 | tf_op jit(solution)/shard_map/ppermute | solution.py:283
  38.5 10.7 %collective-permute-start.5 = (bf16[192,512]{1,0:T(8,128)(2,1)S(1)}, bf16[192,512]{1,0:T(8,128)(2,1)S(1)}, u32[]{:S(2)}, u32[]{:S(2)}) collective-permute-start(bf16[192,512]{1,0:T(8,128)(2,1)S(1)} %add_convert_fusion.2), channel_id=1, source_target_pairs={{0,2},{2,0},{4,6},{6,4},{1,3},{3,1},{5,7},{7,5},{8,10},{10,8},{12,... | collective-permute-start | bytes 589832 | tf_op jit(solution)/shard_map/ppermute | solution.py:283
  42.3 9.6 %collective-permute-start.11 = (bf16[192,512]{1,0:T(8,128)(2,1)S(1)}, bf16[192,512]{1,0:T(8,128)(2,1)S(1)}, u32[]{:S(2)}, u32[]{:S(2)}) collective-permute-start(bf16[192,512]{1,0:T(8,128)(2,1)S(1)} %add_convert_fusion), channel_id=1, source_target_pairs={{0,6},{2,4},{4,2},{6,0},{1,7},{3,5},{5,3},{7,1},{8,14},{10,12},{12... | collective-permute-start | bytes 589832 | tf_op jit(solution)/shard_map/ppermute | solution.py:283
  52.6 1.7 %collective-permute-start.13 = (bf16[256,512]{1,0:T(8,128)(2,1)S(1)}, bf16[256,512]{1,0:T(8,128)(2,1)}, u32[]{:S(2)}, u32[]{:S(2)}) collective-permute-start(bf16[256,512]{1,0:T(8,128)(2,1)S(1)} %shard_map.130.refs_0_.refs_7_), channel_id=1, source_target_pairs={{0,8},{8,0},{16,24},{24,16},{1,9},{9,1},{17,25},{25,17},{2,10},{10... | collective-permute-start | bytes 786440 | tf_op jit(solution)/shard_map/ppermute | solution.py:283
  52.7 11.1 %collective-permute-start.12 = (bf16[256,512]{1,0:T(8,128)(2,1)S(1)}, bf16[256,512]{1,0:T(8,128)(2,1)S(1)}, u32[]{:S(2)}, u32[]{:S(2)}) collective-permute-start(bf16[256,512]{1,0:T(8,128)(2,1)S(1)} %shard_map.130.refs_0_.refs_7_), channel_id=1, source_target_pairs={{0,1},{1,0},{2,3},{3,2},{4,5},{5,4},{6,7},{7,6},{8,9},{9,8},{10,11... | collective-permute-start | bytes 786440 | tf_op jit(solution)/shard_map/ppermute | solution.py:283
  54.4 9.4 %collective-permute-start.14 = (bf16[256,512]{1,0:T(8,128)(2,1)S(1)}, bf16[256,512]{1,0:T(8,128)(2,1)S(1)}, u32[]{:S(2)}, u32[]{:S(2)}) collective-permute-start(bf16[256,512]{1,0:T(8,128)(2,1)S(1)} %broadcast_select_fusion), channel_id=1, source_target_pairs={{0,16},{1,17},{8,25},{9,24},{16,0},{17,1},{24,9},{25,8},{2,18},{3,... | collective-permute-start | bytes 786440 | tf_op jit(solution)/shard_map/ppermute | solution.py:414
  63.8 2.5 %collective-permute-start.15 = (bf16[256,512]{1,0:T(8,128)(2,1)S(1)}, bf16[256,512]{1,0:T(8,128)(2,1)S(1)}, u32[]{:S(2)}, u32[]{:S(2)}) collective-permute-start(bf16[256,512]{1,0:T(8,128)(2,1)S(1)} %shard_map.131.refs_0_), channel_id=1, source_target_pairs={{0,8},{8,0},{16,24},{24,16},{1,9},{9,1},{17,25},{25,17},{2,10},{10... | collective-permute-start | bytes 786440 | tf_op jit(solution)/shard_map/ppermute | solution.py:283
  64.5 1.0 %copy-start.4 = (bf16[1,256,512]{2,1,0:T(8,128)(2,1)S(1)}, bf16[1,256,512]{2,1,0:T(8,128)(2,1)}, u32[]{:S(2)}) copy-start(bf16[1,256,512]{2,1,0:T(8,128)(2,1)} %param.21) | copy-start | bytes 786436
  68.1 3.1 %collective-permute-start.16 = (bf16[256,512]{1,0:T(8,128)(2,1)S(1)}, bf16[256,512]{1,0:T(8,128)(2,1)S(1)}, u32[]{:S(2)}, u32[]{:S(2)}) collective-permute-start(bf16[256,512]{1,0:T(8,128)(2,1)S(1)} %get-tuple-element.55), channel_id=1, source_target_pairs={{0,8},{8,0},{16,24},{24,16},{1,9},{9,1},{17,25},{25,17},{2,10},{10... | collective-permute-start | bytes 786440 | tf_op jit(solution)/shard_map/ppermute | solution.py:283
  71.3 4.5 %collective-permute-start.17 = (bf16[256,128]{1,0:T(8,128)(2,1)S(1)}, bf16[256,128]{1,0:T(8,128)(2,1)S(1)}, u32[]{:S(2)}, u32[]{:S(2)}) collective-permute-start(bf16[256,128]{1,0:T(8,128)(2,1)S(1)} %get-tuple-element.57), channel_id=1, source_target_pairs={{0,1},{1,0},{8,9},{9,8},{16,17},{17,16},{24,25},{25,24},{2,3},{3,2... | collective-permute-start | bytes 196616 | tf_op jit(solution)/shard_map/ppermute | solution.py:456
  73.2 4.7 %collective-permute-start.18 = (bf16[256,128]{1,0:T(8,128)(2,1)S(1)}, bf16[256,128]{1,0:T(8,128)(2,1)S(1)}, u32[]{:S(2)}, u32[]{:S(2)}) collective-permute-start(bf16[256,128]{1,0:T(8,128)(2,1)S(1)} %get-tuple-element.58), channel_id=1, source_target_pairs={{0,16},{1,17},{8,24},{9,25},{16,0},{17,1},{24,8},{25,9},{2,18},{3,... | collective-permute-start | bytes 196616 | tf_op jit(solution)/shard_map/ppermute | solution.py:456
  74.7 5.2 %collective-permute-start.19 = (bf16[256,128]{1,0:T(8,128)(2,1)S(1)}, bf16[256,128]{1,0:T(8,128)(2,1)S(1)}, u32[]{:S(2)}, u32[]{:S(2)}) collective-permute-start(bf16[256,128]{1,0:T(8,128)(2,1)S(1)} %get-tuple-element.59), channel_id=1, source_target_pairs={{0,17},{1,16},{8,25},{9,24},{16,1},{17,0},{24,9},{25,8},{2,19},{3,... | collective-permute-start | bytes 196616 | tf_op jit(solution)/shard_map/ppermute | solution.py:456

commit v9 on v8

--- a/solution.py
+++ b/solution.py
@@ -97,7 +97,9 @@
     own[...] = matmul(table(place, 0, capacity), normed).astype(LOW)
 
 
-def mixing(experts, routes, gates, earlier, high, low):
+def mixing(experts, routes, gates, earlier, upstream, high, low, upstream_here, arrived):
+    load = pltpu.make_async_copy(upstream, upstream_here, arrived)
+    load.start()
     me = lax.axis_index("exp")
     token_count = routes.shape[1]
     capacity = high.shape[2]
@@ -111,6 +113,7 @@
         upper = weight.astype(LOW)
         high[k] = upper
         low[k] = (weight - upper.astype(WIDE)).astype(LOW)
+    load.wait()
 
 
 def expert(split, *refs):
@@ -168,15 +171,7 @@
     out[...] = mixed.astype(LOW)
 
 
-def project(mine, other, gain, weight, *refs):
-    count = (len(refs) - 2) // 2
-    sources, out, targets, arrived = refs[:count], refs[count], refs[count + 1 : -1], refs[-1]
-    loads = [
-        pltpu.make_async_copy(source, target, arrived.at[i])
-        for i, (source, target) in enumerate(zip(sources, targets, strict=True))
-    ]
-    for load in loads:
-        load.start()
+def project(mine, other, gain, weight, out):
     tp = lax.axis_index("tp")
     half = mine.shape[1]
     own = mine[...].astype(WIDE)
@@ -194,24 +189,26 @@
     rest = (rest * factor * gain[:, part(1 - tp, half)]).astype(LOW)
     value = matmul(own, weight[part(tp, half), :]) + matmul(rest, weight[part(1 - tp, half), :])
     out[...] = value.astype(LOW)
-    for load in loads:
-        load.wait()
-
-
-def choose(own, moved, out):
+
+
+def choose(own, moved, beside, out):
     sec = lax.axis_index("sec")
 
-    @pl.when(sec < 2)
+    @pl.when(sec == 0)
     def _():
         out[...] = own[...]
 
+    @pl.when(sec == 1)
+    def _():
+        out[...] = beside[...]
+
     @pl.when(sec >= 2)
     def _():
         out[...] = moved[...]
 
 
 def attend(
-    first, second, beside, queries, upstream, key_w, value_w, hidden, context, away, kept, keys, values, dkeys, dvalues
+    first, second, queries, upstream, key_w, value_w, away, kept, low_ref, values, keys, dkeys, dvalues
 ):
     tp = lax.axis_index("tp")
     sec = lax.axis_index("sec")
@@ -221,12 +218,11 @@
 
     @pl.when(sec != 0)
     def _():
-        even = sec % 2 == 0
-        mine = jnp.where(sec == 1, beside[...], jnp.where(even, first[...], second[...]))
-        other = jnp.where(even | (sec == 1), second[...], first[...])
+        crossed = ((sec > 1) & (sec % 2 == 1)).astype(jnp.int32)
+        place = tp ^ crossed
         for weight, target in ((key_w, keys), (value_w, values)):
-            value = matmul(mine, weight[part(tp, half), :])
-            value = value + matmul(other, weight[part(1 - tp, half), :])
+            value = matmul(first[...], weight[part(place, half), :])
+            value = value + matmul(second[...], weight[part(1 - place, half), :])
             target[...] = value.astype(LOW)
         heads = [
             (slice(s * SEQ, (s + 1) * SEQ), slice(h * HD, (h + 1) * HD))
@@ -246,8 +242,8 @@
         ]
         for at, dscore in zip(heads, dscores):
             dkeys[at] = (matmul(dscore, queries[at]) * scale).astype(LOW)
-        for at, low in zip(heads, lows):
-            context[at] = matmul(low, values[at], TN).astype(LOW)
+        for i, low in enumerate(lows):
+            low_ref[i] = low
         side = sec % 2
         pairs = lax.axis_size("sec") // 2
         block = width // (2 * pairs)
@@ -260,9 +256,24 @@
 
     @pl.when(sec == 0)
     def _():
-        context[...] = hidden[...]
         away[...] = jnp.zeros_like(away)
         kept[...] = jnp.zeros_like(kept)
+
+
+def contexts(low_ref, values, hidden, out):
+    sec = lax.axis_index("sec")
+    head_count = values.shape[1] // HD
+
+    @pl.when(sec == 0)
+    def _():
+        out[...] = hidden[...]
+
+    @pl.when(sec != 0)
+    def _():
+        for i in range(low_ref.shape[0]):
+            s, h = i // head_count, i % head_count
+            at = slice(s * SEQ, (s + 1) * SEQ), slice(h * HD, (h + 1) * HD)
+            out[at] = matmul(low_ref[i], values[at], TN).astype(LOW)
 
 
 def gather_term(kept, arrived, own, *sent):
@@ -349,7 +360,7 @@
         )
 
     arriving = [joined(groups[0])]
-    later = [far_rows[k - 2] for k in groups[1]] + [near_rows]
+    later = [near_rows] + [far_rows[k - 2] for k in groups[1]]
     loads = max(1, units // 512) + 1
     own_away, own_kept, weight_first, weight_second, *later = call(
         expert_first,
@@ -366,17 +377,19 @@
         limit=44,
         held=later,
     )
-    for k, rows in zip(groups[1], later):
+    near = swap(later[0], "exp", 1)
+    for k, rows in zip(groups[1], later[1:]):
         far_rows[k - 2] = rows
     arriving.append(joined(groups[1]))
-    near = swap(later[-1], "exp", 1)
     returned = {0: total(own_away, own_kept)}
     arriving[0] = hold(arriving[0], [own_away])
     others = [swap(arriving[0], "tp", 1)]
-    high, low = call(
+    high, low, upstream = call(
         functools.partial(mixing, experts),
-        [shape_of((experts, token_count, capacity))] * 2,
-        [route_rows, gate_rows, earlier],
+        [shape_of((experts, token_count, capacity))] * 2 + [shape_of(cotangent.shape[1:])],
+        [route_rows, gate_rows, earlier, cotangent[0]],
+        [pltpu.SemaphoreType.DMA],
+        remote=(3,),
         after=[arriving[0]],
     )
     others.append(swap(arriving[1], "tp", 1))
@@ -410,33 +423,38 @@
         targets = {j: j for j in range(sections * tp_size)}
         for t in range(tp_size):
             even, odd = 2 * i * tp_size + t, (2 * i + 1) * tp_size + (t ^ 1)
-            targets |= {t: even, even: t, tp_size + t: odd, odd: tp_size + t}
+            targets |= {t: even, even: t, tp_size + t: odd, odd: tp_size + (t ^ 1)}
         arrived = lax.ppermute(encoder_half, ("sec", "tp"), list(targets.items()))
         moved = arrived if sections == 4 else jnp.where(sec // 2 == i, arrived, moved)
-    first = call(choose, [shape_of(hidden_half.shape)], [hidden_other, moved])[0]
+    first = call(choose, [shape_of(hidden_half.shape)], [hidden_other, moved, beside])[0]
     second = swap(first, "sec", 1)
 
     local_width = query_weight.shape[2]
-    sources = [key_weight[0], value_weight[0], cotangent[0]]
-    queries, key_w, value_w, upstream = call(
+    queries = call(
         project,
-        [shape_of((token_count, local_width))] + [shape_of(x.shape) for x in sources],
-        [hidden_half, hidden_other, attn_gain, query_weight[0], *sources],
-        [pltpu.SemaphoreType.DMA((len(sources),))],
+        [shape_of((token_count, local_width))],
+        [hidden_half, hidden_other, attn_gain, query_weight[0]],
         flops=2 * token_count * model_width * local_width,
-        remote=(4, 5, 6),
-    )
-    context, away, kept = call(
+    )[0]
+    heads = token_count // SEQ * (local_width // HD)
+    away, kept, lows, values = call(
         attend,
         [
-            shape_of((token_count, local_width)),
             shape_of((token_count, model_width // 2)),
             shape_of((token_count, model_width // 2), WIDE),
+            shape_of((heads, SEQ, SEQ)),
+            shape_of((token_count, local_width)),
         ],
-        [first, second, beside, queries, upstream, key_w, value_w, hidden_half],
-        [pltpu.VMEM((token_count, local_width), LOW)] * 4,
+        [first, second, queries, upstream, key_weight[0], value_weight[0]],
+        [pltpu.VMEM((token_count, local_width), LOW)] * 3,
         flops=10 * token_count * model_width * local_width,
     )
+    context = call(
+        contexts,
+        [shape_of((token_count, local_width))],
+        [lows, values, hidden_half],
+        flops=2 * token_count * SEQ * local_width,
+    )[0]
 
     own = model_width // (sections * tp_size)
     count = sections // 2 * tp_size

time: 80.7 us -> 79.8 us (0.989)
  Pallas kernels: 14.9 us -> 13.8 us
    ppermute x16, waiting for transfers between devices: 23.1 us -> 21.5 us  [swap(): return lax.ppermute(block, axis, [(i, i ^ step) for i in range(size)])]
    ppermute x1, waiting for transfers between devices: 0.01 us -> 1.33 us  [shards(): arrived = lax.ppermute(encoder_half, ('sec', 'tp'), list(targets.items()))]
    ppermute x3, starting transfers between devices: 3.57 us -> 4.81 us  [shards(): total = total + lax.ppermute(blocks[k], ('sec', 'tp'), pairs).astype(WIDE)]
    pallas_call x13 -> x14, Pallas kernels: 14.9 us -> 13.8 us  [call(): pl.pallas_call(run, out_shape=[*out_shape, *(shape_of(x.shape, x.dtype) f...]
  transfers between devices with their start and end apart: 20 -> 20, of which waited for: 14 -> 15; matrix products, arithmetic and copies ran while one was open for 0% -> 0% of each run, Pallas kernels for 14% -> 15%
where the time goes in v9:
time: 79.8 us; the launch traced here: 79.6 us
  starting transfers between devices  34.6 us (43%)
  waiting for transfers between devices  27.3 us (34%)
  Pallas kernels  13.8 us (17%)
  local copies, waits for them, and re-layouts  2.24 us (3%)
  other arithmetic  0.85 us (1%)
  between operations  0.85 us (1%)
    ppermute x16, starting transfers between devices, swap(): return lax.ppermute(block, axis, [(i, i ^ step) for i in range(size)])  28.2 us
    ppermute x16, waiting for transfers between devices, swap(): return lax.ppermute(block, axis, [(i, i ^ step) for i in range(size)])  21.5 us
    pallas_call x14, Pallas kernels, call(): pl.pallas_call(run, out_shape=[*out_shape, *(shape_of(x.shape, x.dtype) f...  13.8 us
    ppermute x3, starting transfers between devices, shards(): total = total + lax.ppermute(blocks[k], ('sec', 'tp'), pairs).astype(WIDE)  4.81 us
    ppermute x3, waiting for transfers between devices, shards(): total = total + lax.ppermute(blocks[k], ('sec', 'tp'), pairs).astype(WIDE)  4.44 us
    unnamed x18, local copies, waits for them, and re-layouts  2.24 us
  transfers between devices with their start and end apart: 20, of which 15 were waited for; matrix products, arithmetic and copies ran while one was open for 0% of the time, Pallas kernels for 15%

profile of v9, /device:TPU:0, one launch (start us, length us, event | category | flops | bytes accessed | tf_op | source)
XLA Modules:
  0.0 79.6 jit_solution(2045949187655042128)
XLA Ops:
  0.7 1.0 %copy-done.1 = bf16[1,256,1024]{2,1,0:T(8,128)(2,1)S(1)} copy-done((bf16[1,256,1024]{2,1,0:T(8,128)(2,1)S(1)}, bf16[1,256,1024]{2,1,0:T(8,128)(2,1)}, u32[]{:S(2)}) %copy-start.1) | copy-done | bytes 524312
  1.7 0.9 %shard_map.123 = (bf16[192,512]{1,0:T(8,128)(2,1)S(1)}, bf16[192,512]{1,0:T(8,128)(2,1)S(1)}, bf16[192,1024]{1,0:T(8,128)(2,1)S(1)}, bf16[192,1024]{1,0:T(8,128)(2,1)S(1)}) custom-call(bf16[256,1024]{1,0:T(8,128)(2,1)S(1)} %bitcast.15, s32[2,256]{1,0:T(2,128)S(1)} %bitcast.18, f32[1,1024]{1,0:T(1,128)S(1)} %copy-done.8, ...), custom_call_target="tpu_custom_call" | custom-call | flops 402653184 | bytes 1841152 | tf_op jit(solution)/shard_map/pallas_call | solution.py:40
  2.6 4.1 %collective-permute-start = (bf16[192,512]{1,0:T(8,128)(2,1)S(1)}, bf16[192,512]{1,0:T(8,128)(2,1)S(1)}, u32[]{:S(2)}, u32[]{:S(2)}) collective-permute-start(bf16[192,512]{1,0:T(8,128)(2,1)S(1)} %get-tuple-element.33), channel_id=1, source_target_pairs={{0,4},{2,6},{4,0},{6,2},{1,5},{3,7},{5,1},{7,3},{8,12},{10,14},{12... | collective-permute-start | bytes 589832 | tf_op jit(solution)/shard_map/ppermute | solution.py:294
  6.7 4.6 %shard_map.124 = (bf16[192,512]{1,0:T(8,128)(2,1)S(1)}, f32[192,512]{1,0:T(8,128)S(1)}, bf16[1024,2048]{1,0:T(8,128)(2,1)S(1)}, bf16[2048,1024]{1,0:T(8,128)(2,1...) custom-call(bf16[192,1024]{1,0:T(8,128)(2,1)S(1)} %get-tuple-element, ...), custom_call_target="tpu_custom_call", output_to_operand_aliasing={{4}: (3, {}), {5}: (4, {})} | custom-call | flops 1610612736 | bytes 17760256 | tf_op jit(solution)/shard_map/pallas_call | solution.py:40
  11.3 1.6 %collective-permute-start.1 = (bf16[192,512]{1,0:T(8,128)(2,1)S(1)}, bf16[192,512]{1,0:T(8,128)(2,1)S(1)}, u32[]{:S(2)}, u32[]{:S(2)}) collective-permute-start(bf16[192,512]{1,0:T(8,128)(2,1)S(1)} %get-tuple-element.32.refs_0_), channel_id=1, source_target_pairs={{0,1},{1,0},{2,3},{3,2},{4,5},{5,4},{6,7},{7,6},{8,9},{9,8},{10,11... | collective-permute-start | bytes 589832 | tf_op jit(solution)/shard_map/ppermute | solution.py:294
  12.9 1.6 %collective-permute-start.2 = (bf16[192,1024]{1,0:T(8,128)(2,1)S(1)}, bf16[192,1024]{1,0:T(8,128)(2,1)S(1)}, u32[]{:S(2)}, u32[]{:S(2)}) collective-permute-start(bf16[192,1024]{1,0:T(8,128)(2,1)S(1)} %get-tuple-element.37), channel_id=1, source_target_pairs={{0,2},{2,0},{4,6},{6,4},{1,3},{3,1},{5,7},{7,5},{8,10},{10,8},{12,... | collective-permute-start | bytes 1179656 | tf_op jit(solution)/shard_map/ppermute | solution.py:294
  14.4 0.2 collective-permute-start.8
  14.7 1.2 %collective-permute-done.refs_1_ = bf16[192,512]{1,0:T(8,128)(2,1)S(1)} collective-permute-done((bf16[192,512]{1,0:T(8,128)(2,1)S(1)}, bf16[192,512]{1,0:T(8,128)(2,1)S(1)}, u32[]{:S(2)}, u32[]{:S(2)}) %collective-permute-start) | collective-permute-done | bytes 196640 | tf_op jit(solution)/shard_map/ppermute | solution.py:294
  15.9 2.3 %collective-permute-start.3 = (bf16[192,512]{1,0:T(8,128)(2,1)S(1)}, bf16[192,512]{1,0:T(8,128)(2,1)S(1)}, u32[]{:S(2)}, u32[]{:S(2)}) collective-permute-start(bf16[192,512]{1,0:T(8,128)(2,1)S(1)} %shard_map.125.refs_4_.refs_0_), channel_id=1, source_target_pairs={{0,1},{1,0},{2,3},{3,2},{4,5},{5,4},{6,7},{7,6},{8,9},{9,8},{10,11... | collective-permute-start | bytes 589832 | tf_op jit(solution)/shard_map/ppermute | solution.py:294
  18.2 0.6 shard_map.126
  18.9 3.1 %collective-permute-done.3.refs_1_ = bf16[192,512]{1,0:T(8,128)(2,1)S(1)} collective-permute-done((bf16[192,512]{1,0:T(8,128)(2,1)S(1)}, bf16[192,512]{1,0:T(8,128)(2,1)S(1)}, u32[]{:S(2)}, u32[]{:S(2)}) %collective-permute-start.3) | collective-permute-done | bytes 196640 | tf_op jit(solution)/shard_map/ppermute | solution.py:294
  21.9 1.8 %shard_map.127 = (bf16[192,512]{1,0:T(8,128)(2,1)S(1)}, f32[192,512]{1,0:T(8,128)S(1)}) custom-call(bf16[192,512]{1,0:T(8,128)(2,1)S(1)} %shard_map.125.refs_4_.refs_0_, bf16[192,512]{1,0:T(8,128)(2,1)S(1)} %collective-permute-done.3.refs_1_, bf16[1024,2048]{1,0:T(8,128)(2,1)S(1)} %get-tuple-element.38.refs_2_.refs_1_, ...), custom_call_target="tpu_custom_call" | custom-call | flops 1610612736 | bytes 9371648 | tf_op jit(solution)/shard_map/pallas_call | solution.py:40
  23.8 2.0 %collective-permute-start.6 = (bf16[192,512]{1,0:T(8,128)(2,1)S(1)}, bf16[192,512]{1,0:T(8,128)(2,1)S(1)}, u32[]{:S(2)}, u32[]{:S(2)}) collective-permute-start(bf16[192,512]{1,0:T(8,128)(2,1)S(1)} %get-tuple-element.40.refs_3_), channel_id=1, source_target_pairs={{0,1},{1,0},{2,3},{3,2},{4,5},{5,4},{6,7},{7,6},{8,9},{9,8},{10,11... | collective-permute-start | bytes 589832 | tf_op jit(solution)/shard_map/ppermute | solution.py:294
  25.8 1.5 %collective-permute-done.8.refs_0_ = bf16[192,512]{1,0:T(8,128)(2,1)S(1)} collective-permute-done((bf16[192,512]{1,0:T(8,128)(2,1)S(1)}, bf16[192,512]{1,0:T(8,128)(2,1)S(1)}, u32[]{:S(2)}, u32[]{:S(2)}) %collective-permute-start.8) | collective-permute-done | bytes 196640 | tf_op jit(solution)/shard_map/ppermute | solution.py:294
  27.2 0.5 collective-permute-start.9
  27.8 0.7 collective-permute-done.2.refs_0_
  28.4 1.8 %shard_map.128 = (bf16[192,512]{1,0:T(8,128)(2,1)S(1)}, f32[192,512]{1,0:T(8,128)S(1)}) custom-call(bf16[192,1024]{1,0:T(8,128)(2,1)S(1)} %collective-permute-done.2.refs_0_, bf16[1024,2048]{1,0:T(8,128)(2,1)S(1)} %get-tuple-element.38.refs_2_.refs_1_, bf16[2048,1024]{1,0:T(8,128)(2,1)S(1)} %get-tuple-element.39.refs_3_.refs_2_, ...), custom_call_target="tpu_custom_call" | custom-call | flops 1610612736 | bytes 9371648 | tf_op jit(solution)/shard_map/pallas_call | solution.py:40
  30.2 1.6 %collective-permute-start.4 = (bf16[192,512]{1,0:T(8,128)(2,1)S(1)}, bf16[192,512]{1,0:T(8,128)(2,1)S(1)}, u32[]{:S(2)}, u32[]{:S(2)}) collective-permute-start(bf16[192,512]{1,0:T(8,128)(2,1)S(1)} %get-tuple-element.42.refs_4_), channel_id=1, source_target_pairs={{0,1},{1,0},{2,3},{3,2},{4,5},{5,4},{6,7},{7,6},{8,9},{9,8},{10,11... | collective-permute-start | bytes 589832 | tf_op jit(solution)/shard_map/ppermute | solution.py:294
  31.9 1.5 %collective-permute-start.7 = (bf16[192,512]{1,0:T(8,128)(2,1)S(1)}, bf16[192,512]{1,0:T(8,128)(2,1)S(1)}, u32[]{:S(2)}, u32[]{:S(2)}) collective-permute-start(bf16[192,512]{1,0:T(8,128)(2,1)S(1)} %add_convert_fusion.1.refs_5_), channel_id=1, source_target_pairs={{0,4},{2,6},{4,0},{6,2},{1,5},{3,7},{5,1},{7,3},{8,12},{10,14},{12... | collective-permute-start | bytes 589832 | tf_op jit(solution)/shard_map/ppermute | solution.py:294
  33.4 1.3 %collective-permute-done.9.refs_1_ = bf16[192,512]{1,0:T(8,128)(2,1)S(1)} collective-permute-done((bf16[192,512]{1,0:T(8,128)(2,1)S(1)}, bf16[192,512]{1,0:T(8,128)(2,1)S(1)}, u32[]{:S(2)}, u32[]{:S(2)}) %collective-permute-start.9) | collective-permute-done | bytes 196640 | tf_op jit(solution)/shard_map/ppermute | solution.py:294
  34.7 1.8 %shard_map.129 = (bf16[192,512]{1,0:T(8,128)(2,1)S(1)}, f32[192,512]{1,0:T(8,128)S(1)}) custom-call(bf16[192,512]{1,0:T(8,128)(2,1)S(1)} %collective-permute-done.8.refs_0_, bf16[192,512]{1,0:T(8,128)(2,1)S(1)} %collective-permute-done.9.refs_1_, bf16[1024,2048]{1,0:T(8,128)(2,1)S(1)} %get-tuple-element.38.refs_2_.refs_1_, ...), custom_call_target="tpu_custom_call" | custom-call | flops 1610612736 | bytes 9371648 | tf_op jit(solution)/shard_map/pallas_call | solution.py:40
  36.6 1.4 %collective-permute-start.10 = (bf16[192,512]{1,0:T(8,128)(2,1)S(1)}, bf16[192,512]{1,0:T(8,128)(2,1)S(1)}, u32[]{:S(2)}, u32[]{:S(2)}) collective-permute-start(bf16[192,512]{1,0:T(8,128)(2,1)S(1)} %get-tuple-element.46), channel_id=1, source_target_pairs={{0,1},{1,0},{2,3},{3,2},{4,5},{5,4},{6,7},{7,6},{8,9},{9,8},{10,11... | collective-permute-start | bytes 589832 | tf_op jit(solution)/shard_map/ppermute | solution.py:294
  38.0 0.5 collective-permute-done.4
  38.5 2.5 %collective-permute-start.5 = (bf16[192,512]{1,0:T(8,128)(2,1)S(1)}, bf16[192,512]{1,0:T(8,128)(2,1)S(1)}, u32[]{:S(2)}, u32[]{:S(2)}) collective-permute-start(bf16[192,512]{1,0:T(8,128)(2,1)S(1)} %add_convert_fusion.2), channel_id=1, source_target_pairs={{0,2},{2,0},{4,6},{6,4},{1,3},{3,1},{5,7},{7,5},{8,10},{10,8},{12,... | collective-permute-start | bytes 589832 | tf_op jit(solution)/shard_map/ppermute | solution.py:294
  41.0 1.3 %collective-permute-done.10 = bf16[192,512]{1,0:T(8,128)(2,1)S(1)} collective-permute-done((bf16[192,512]{1,0:T(8,128)(2,1)S(1)}, bf16[192,512]{1,0:T(8,128)(2,1)S(1)}, u32[]{:S(2)}, u32[]{:S(2)}) %collective-permute-start.10) | collective-permute-done | bytes 196640 | tf_op jit(solution)/shard_map/ppermute | solution.py:294
  42.3 5.1 %collective-permute-start.11 = (bf16[192,512]{1,0:T(8,128)(2,1)S(1)}, bf16[192,512]{1,0:T(8,128)(2,1)S(1)}, u32[]{:S(2)}, u32[]{:S(2)}) collective-permute-start(bf16[192,512]{1,0:T(8,128)(2,1)S(1)} %add_convert_fusion), channel_id=1, source_target_pairs={{0,6},{2,4},{4,2},{6,0},{1,7},{3,5},{5,3},{7,1},{8,14},{10,12},{12... | collective-permute-start | bytes 589832 | tf_op jit(solution)/shard_map/ppermute | solution.py:294
  47.5 1.6 %collective-permute-done.5.refs_4_ = bf16[192,512]{1,0:T(8,128)(2,1)S(1)} collective-permute-done((bf16[192,512]{1,0:T(8,128)(2,1)S(1)}, bf16[192,512]{1,0:T(8,128)(2,1)S(1)}, u32[]{:S(2)}, u32[]{:S(2)}) %collective-permute-start.5) | collective-permute-done | bytes 196640 | tf_op jit(solution)/shard_map/ppermute | solution.py:294
  49.1 2.9 %collective-permute-done.11.refs_6_ = bf16[192,512]{1,0:T(8,128)(2,1)S(1)} collective-permute-done((bf16[192,512]{1,0:T(8,128)(2,1)S(1)}, bf16[192,512]{1,0:T(8,128)(2,1)S(1)}, u32[]{:S(2)}, u32[]{:S(2)}) %collective-permute-start.11) | collective-permute-done | bytes 196640 | tf_op jit(solution)/shard_map/ppermute | solution.py:294
  51.9 0.7 shard_map.130.refs_0_.refs_2_
  52.6 0.1 collective-permute-start.13
  52.7 1.6 %collective-permute-start.12 = (bf16[256,512]{1,0:T(8,128)(2,1)S(1)}, bf16[256,512]{1,0:T(8,128)(2,1)S(1)}, u32[]{:S(2)}, u32[]{:S(2)}) collective-permute-start(bf16[256,512]{1,0:T(8,128)(2,1)S(1)} %shard_map.130.refs_0_.refs_2_), channel_id=1, source_target_pairs={{0,1},{1,0},{2,3},{3,2},{4,5},{5,4},{6,7},{7,6},{8,9},{9,8},{10,11... | collective-permute-start | bytes 786440 | tf_op jit(solution)/shard_map/ppermute | solution.py:294
  54.3 1.6 %collective-permute-start.14 = (bf16[256,512]{1,0:T(8,128)(2,1)S(1)}, bf16[256,512]{1,0:T(8,128)(2,1)S(1)}, u32[]{:S(2)}, u32[]{:S(2)}) collective-permute-start(bf16[256,512]{1,0:T(8,128)(2,1)S(1)} %broadcast_select_fusion), channel_id=1, source_target_pairs={{0,16},{1,17},{8,25},{9,24},{16,0},{17,1},{24,8},{25,9},{2,18},{3,... | collective-permute-start | bytes 786440 | tf_op jit(solution)/shard_map/ppermute | solution.py:427
  55.9 5.5 %collective-permute-done.12.refs_0_.refs_1_ = bf16[256,512]{1,0:T(8,128)(2,1)S(1)} collective-permute-done((bf16[256,512]{1,0:T(8,128)(2,1)S(1)}, bf16[256,512]{1,0:T(8,128)(2,1)S(1)}, u32[]{:S(2)}, u32[]{:S(2)}) %collective-permute-start.12) | collective-permute-done | bytes 262176 | tf_op jit(solution)/shard_map/ppermute | solution.py:294
  61.4 1.3 %collective-permute-done.14.refs_1_ = bf16[256,512]{1,0:T(8,128)(2,1)S(1)} collective-permute-done((bf16[256,512]{1,0:T(8,128)(2,1)S(1)}, bf16[256,512]{1,0:T(8,128)(2,1)S(1)}, u32[]{:S(2)}, u32[]{:S(2)}) %collective-permute-start.14) | collective-permute-done | bytes 262176 | tf_op jit(solution)/shard_map/ppermute | solution.py:427
  62.8 0.1 collective-permute-start.15
  62.9 0.7 shard_map.132.refs_2_
  63.6 0.8 %collective-permute-done.15.refs_1_ = bf16[256,512]{1,0:T(8,128)(2,1)S(1)} collective-permute-done((bf16[256,512]{1,0:T(8,128)(2,1)S(1)}, bf16[256,512]{1,0:T(8,128)(2,1)S(1)}, u32[]{:S(2)}, u32[]{:S(2)}) %collective-permute-start.15) | collective-permute-done | bytes 262176 | tf_op jit(solution)/shard_map/ppermute | solution.py:294
  64.4 1.2 %copy-done.7 = bf16[1,1024,512]{2,1,0:T(8,128)(2,1)S(1)} copy-done((bf16[1,1024,512]{2,1,0:T(8,128)(2,1)S(1)}, bf16[1,1024,512]{2,1,0:T(8,128)(2,1)}, u32[]{:S(2)}) %copy-start.7) | copy-done | bytes 1048600
  65.6 0.1 shard_map.133
  65.7 2.0 %collective-permute-start.16 = (bf16[256,512]{1,0:T(8,128)(2,1)S(1)}, bf16[256,512]{1,0:T(8,128)(2,1)S(1)}, u32[]{:S(2)}, u32[]{:S(2)}) collective-permute-start(bf16[256,512]{1,0:T(8,128)(2,1)S(1)} %get-tuple-element.51), channel_id=1, source_target_pairs={{0,8},{8,0},{16,24},{24,16},{1,9},{9,1},{17,25},{25,17},{2,10},{10... | collective-permute-start | bytes 786440 | tf_op jit(solution)/shard_map/ppermute | solution.py:294
  67.7 1.2 %collective-permute-done.16.refs_1_ = bf16[256,512]{1,0:T(8,128)(2,1)S(1)} collective-permute-done((bf16[256,512]{1,0:T(8,128)(2,1)S(1)}, bf16[256,512]{1,0:T(8,128)(2,1)S(1)}, u32[]{:S(2)}, u32[]{:S(2)}) %collective-permute-start.16) | collective-permute-done | bytes 262176 | tf_op jit(solution)/shard_map/ppermute | solution.py:294
  68.9 0.1 shard_map.135
  69.0 1.5 %collective-permute-start.17 = (bf16[256,128]{1,0:T(8,128)(2,1)S(1)}, bf16[256,128]{1,0:T(8,128)(2,1)S(1)}, u32[]{:S(2)}, u32[]{:S(2)}) collective-permute-start(bf16[256,128]{1,0:T(8,128)(2,1)S(1)} %get-tuple-element.53), channel_id=1, source_target_pairs={{0,1},{1,0},{8,9},{9,8},{16,17},{17,16},{24,25},{25,24},{2,3},{3,2... | collective-permute-start | bytes 196616 | tf_op jit(solution)/shard_map/ppermute | solution.py:474
  70.5 3.3 %collective-permute-start.18 = (bf16[256,128]{1,0:T(8,128)(2,1)S(1)}, bf16[256,128]{1,0:T(8,128)(2,1)S(1)}, u32[]{:S(2)}, u32[]{:S(2)}) collective-permute-start(bf16[256,128]{1,0:T(8,128)(2,1)S(1)} %get-tuple-element.54), channel_id=1, source_target_pairs={{0,16},{1,17},{8,24},{9,25},{16,0},{17,1},{24,8},{25,9},{2,18},{3,... | collective-permute-start | bytes 196616 | tf_op jit(solution)/shard_map/ppermute | solution.py:474
  73.8 0.7 shard_map.134
  74.5 1.7 %collective-permute-done.18 = bf16[256,128]{1,0:T(8,128)(2,1)S(1)} collective-permute-done((bf16[256,128]{1,0:T(8,128)(2,1)S(1)}, bf16[256,128]{1,0:T(8,128)(2,1)S(1)}, u32[]{:S(2)}, u32[]{:S(2)}) %collective-permute-start.18) | collective-permute-done | bytes 65568 | tf_op jit(solution)/shard_map/ppermute | solution.py:474
  76.2 2.7 %collective-permute-done.19 = bf16[256,128]{1,0:T(8,128)(2,1)S(1)} collective-permute-done((bf16[256,128]{1,0:T(8,128)(2,1)S(1)}, bf16[256,128]{1,0:T(8,128)(2,1)S(1)}, u32[]{:S(2)}, u32[]{:S(2)}) %collective-permute-start.19) | collective-permute-done | bytes 65568 | tf_op jit(solution)/shard_map/ppermute | solution.py:474
  79.0 0.7 add_convert_fusion.4
  (30 shorter events, 0.3 us)
Async XLA Ops:
  0.6 1.0 %copy-start.1 = (bf16[1,256,1024]{2,1,0:T(8,128)(2,1)S(1)}, bf16[1,256,1024]{2,1,0:T(8,128)(2,1)}, u32[]{:S(2)}) copy-start(bf16[1,256,1024]{2,1,0:T(8,128)(2,1)} %param.11) | copy-start | bytes 1572868
  0.6 1.0 %copy-start.4 = (s32[1,256,2]{1,2,0:T(2,128)S(1)}, s32[1,256,2]{1,2,0:T(2,128)}, u32[]{:S(2)}) copy-start(s32[1,256,2]{1,2,0:T(2,128)} %param.12) | copy-start | bytes 6148
  0.6 1.0 %copy-start.8 = (f32[1,1024]{1,0:T(1,128)S(1)}, f32[1,1024]{1,0:T(1,128)}, u32[]{:S(2)}) copy-start(f32[1,1024]{1,0:T(1,128)} %refs_2_.2) | copy-start | bytes 12292
  2.6 13.3 %collective-permute-start = (bf16[192,512]{1,0:T(8,128)(2,1)S(1)}, bf16[192,512]{1,0:T(8,128)(2,1)S(1)}, u32[]{:S(2)}, u32[]{:S(2)}) collective-permute-start(bf16[192,512]{1,0:T(8,128)(2,1)S(1)} %get-tuple-element.33), channel_id=1, source_target_pairs={{0,4},{2,6},{4,0},{6,2},{1,5},{3,7},{5,1},{7,3},{8,12},{10,14},{12... | collective-permute-start | bytes 589832 | tf_op jit(solution)/shard_map/ppermute | solution.py:294
  6.7 11.5 %copy-start.2 = (bf16[1,256,512]{2,1,0:T(8,128)(2,1)S(1)}, bf16[1,256,512]{2,1,0:T(8,128)(2,1)}, u32[]{:S(2)}) copy-start(bf16[1,256,512]{2,1,0:T(8,128)(2,1)} %param.21) | copy-start | bytes 786436
  6.7 11.5 %copy-start.5 = (f32[1,256,2]{1,2,0:T(2,128)S(1)}, f32[1,256,2]{1,2,0:T(2,128)}, u32[]{:S(2)}) copy-start(f32[1,256,2]{1,2,0:T(2,128)} %param.13) | copy-start | bytes 6148
  11.3 7.5 %collective-permute-start.1 = (bf16[192,512]{1,0:T(8,128)(2,1)S(1)}, bf16[192,512]{1,0:T(8,128)(2,1)S(1)}, u32[]{:S(2)}, u32[]{:S(2)}) collective-permute-start(bf16[192,512]{1,0:T(8,128)(2,1)S(1)} %get-tuple-element.32.refs_0_), channel_id=1, source_target_pairs={{0,1},{1,0},{2,3},{3,2},{4,5},{5,4},{6,7},{7,6},{8,9},{9,8},{10,11... | collective-permute-start | bytes 589832 | tf_op jit(solution)/shard_map/ppermute | solution.py:294
  12.9 15.6 %collective-permute-start.2 = (bf16[192,1024]{1,0:T(8,128)(2,1)S(1)}, bf16[192,1024]{1,0:T(8,128)(2,1)S(1)}, u32[]{:S(2)}, u32[]{:S(2)}) collective-permute-start(bf16[192,1024]{1,0:T(8,128)(2,1)S(1)} %get-tuple-element.37), channel_id=1, source_target_pairs={{0,2},{2,0},{4,6},{6,4},{1,3},{3,1},{5,7},{7,5},{8,10},{10,8},{12,... | collective-permute-start | bytes 1179656 | tf_op jit(solution)/shard_map/ppermute | solution.py:294
  14.4 12.8 %collective-permute-start.8 = (bf16[192,512]{1,0:T(8,128)(2,1)S(1)}, bf16[192,512]{1,0:T(8,128)(2,1)S(1)}, u32[]{:S(2)}, u32[]{:S(2)}) collective-permute-start(bf16[192,512]{1,0:T(8,128)(2,1)S(1)} %get-tuple-element.44), channel_id=1, source_target_pairs={{0,6},{2,4},{4,2},{6,0},{1,7},{3,5},{5,3},{7,1},{8,14},{10,12},{12... | collective-permute-start | bytes 589832 | tf_op jit(solution)/shard_map/ppermute | solution.py:294
  15.9 6.0 %collective-permute-start.3 = (bf16[192,512]{1,0:T(8,128)(2,1)S(1)}, bf16[192,512]{1,0:T(8,128)(2,1)S(1)}, u32[]{:S(2)}, u32[]{:S(2)}) collective-permute-start(bf16[192,512]{1,0:T(8,128)(2,1)S(1)} %shard_map.125.refs_4_.refs_0_), channel_id=1, source_target_pairs={{0,1},{1,0},{2,3},{3,2},{4,5},{5,4},{6,7},{7,6},{8,9},{9,8},{10,11... | collective-permute-start | bytes 589832 | tf_op jit(solution)/shard_map/ppermute | solution.py:294
  23.8 8.1 %collective-permute-start.6 = (bf16[192,512]{1,0:T(8,128)(2,1)S(1)}, bf16[192,512]{1,0:T(8,128)(2,1)S(1)}, u32[]{:S(2)}, u32[]{:S(2)}) collective-permute-start(bf16[192,512]{1,0:T(8,128)(2,1)S(1)} %get-tuple-element.40.refs_3_), channel_id=1, source_target_pairs={{0,1},{1,0},{2,3},{3,2},{4,5},{5,4},{6,7},{7,6},{8,9},{9,8},{10,11... | collective-permute-start | bytes 589832 | tf_op jit(solution)/shard_map/ppermute | solution.py:294
  27.2 7.5 %collective-permute-start.9 = (bf16[192,512]{1,0:T(8,128)(2,1)S(1)}, bf16[192,512]{1,0:T(8,128)(2,1)S(1)}, u32[]{:S(2)}, u32[]{:S(2)}) collective-permute-start(bf16[192,512]{1,0:T(8,128)(2,1)S(1)} %collective-permute-done.8.refs_0_), channel_id=1, source_target_pairs={{0,1},{1,0},{2,3},{3,2},{4,5},{5,4},{6,7},{7,6},{8,9},{9,8},{10,11... | collective-permute-start | bytes 589832 | tf_op jit(solution)/shard_map/ppermute | solution.py:294
  30.2 8.2 %collective-permute-start.4 = (bf16[192,512]{1,0:T(8,128)(2,1)S(1)}, bf16[192,512]{1,0:T(8,128)(2,1)S(1)}, u32[]{:S(2)}, u32[]{:S(2)}) collective-permute-start(bf16[192,512]{1,0:T(8,128)(2,1)S(1)} %get-tuple-element.42.refs_4_), channel_id=1, source_target_pairs={{0,1},{1,0},{2,3},{3,2},{4,5},{5,4},{6,7},{7,6},{8,9},{9,8},{10,11... | collective-permute-start | bytes 589832 | tf_op jit(solution)/shard_map/ppermute | solution.py:294
  31.9 15.6 %collective-permute-start.7 = (bf16[192,512]{1,0:T(8,128)(2,1)S(1)}, bf16[192,512]{1,0:T(8,128)(2,1)S(1)}, u32[]{:S(2)}, u32[]{:S(2)}) collective-permute-start(bf16[192,512]{1,0:T(8,128)(2,1)S(1)} %add_convert_fusion.1.refs_5_), channel_id=1, source_target_pairs={{0,4},{2,6},{4,0},{6,2},{1,5},{3,7},{5,1},{7,3},{8,12},{10,14},{12... | collective-permute-start | bytes 589832 | tf_op jit(solution)/shard_map/ppermute | solution.py:294
  36.5 26.4 %copy-start = (bf16[1,1024,512]{2,1,0:T(8,128)(2,1)S(1)}, bf16[1,1024,512]{2,1,0:T(8,128)(2,1)}, u32[]{:S(2)}) copy-start(bf16[1,1024,512]{2,1,0:T(8,128)(2,1)} %param.18) | copy-start | bytes 3145732
  36.5 26.3 %copy-start.3 = (f32[1,1024]{1,0:T(1,128)S(1)}, f32[1,1024]{1,0:T(1,128)}, u32[]{:S(2)}) copy-start(f32[1,1024]{1,0:T(1,128)} %refs_2_.3) | copy-start | bytes 12292
  36.5 27.8 %copy-start.6 = (bf16[1,1024,512]{2,1,0:T(8,128)(2,1)S(1)}, bf16[1,1024,512]{2,1,0:T(8,128)(2,1)}, u32[]{:S(2)}) copy-start(bf16[1,1024,512]{2,1,0:T(8,128)(2,1)} %param.19) | copy-start | bytes 3145732
  36.6 5.7 %collective-permute-start.10 = (bf16[192,512]{1,0:T(8,128)(2,1)S(1)}, bf16[192,512]{1,0:T(8,128)(2,1)S(1)}, u32[]{:S(2)}, u32[]{:S(2)}) collective-permute-start(bf16[192,512]{1,0:T(8,128)(2,1)S(1)} %get-tuple-element.46), channel_id=1, source_target_pairs={{0,1},{1,0},{2,3},{3,2},{4,5},{5,4},{6,7},{7,6},{8,9},{9,8},{10,11... | collective-permute-start | bytes 589832 | tf_op jit(solution)/shard_map/ppermute | solution.py:294
  38.5 10.6 %collective-permute-start.5 = (bf16[192,512]{1,0:T(8,128)(2,1)S(1)}, bf16[192,512]{1,0:T(8,128)(2,1)S(1)}, u32[]{:S(2)}, u32[]{:S(2)}) collective-permute-start(bf16[192,512]{1,0:T(8,128)(2,1)S(1)} %add_convert_fusion.2), channel_id=1, source_target_pairs={{0,2},{2,0},{4,6},{6,4},{1,3},{3,1},{5,7},{7,5},{8,10},{10,8},{12,... | collective-permute-start | bytes 589832 | tf_op jit(solution)/shard_map/ppermute | solution.py:294
  42.3 9.6 %collective-permute-start.11 = (bf16[192,512]{1,0:T(8,128)(2,1)S(1)}, bf16[192,512]{1,0:T(8,128)(2,1)S(1)}, u32[]{:S(2)}, u32[]{:S(2)}) collective-permute-start(bf16[192,512]{1,0:T(8,128)(2,1)S(1)} %add_convert_fusion), channel_id=1, source_target_pairs={{0,6},{2,4},{4,2},{6,0},{1,7},{3,5},{5,3},{7,1},{8,14},{10,12},{12... | collective-permute-start | bytes 589832 | tf_op jit(solution)/shard_map/ppermute | solution.py:294
  52.6 1.7 %collective-permute-start.13 = (bf16[256,512]{1,0:T(8,128)(2,1)S(1)}, bf16[256,512]{1,0:T(8,128)(2,1)S(1)}, u32[]{:S(2)}, u32[]{:S(2)}) collective-permute-start(bf16[256,512]{1,0:T(8,128)(2,1)S(1)} %shard_map.130.refs_0_.refs_2_), channel_id=1, source_target_pairs={{0,8},{8,0},{16,24},{24,16},{1,9},{9,1},{17,25},{25,17},{2,10},{10... | collective-permute-start | bytes 786440 | tf_op jit(solution)/shard_map/ppermute | solution.py:294
  52.7 8.7 %collective-permute-start.12 = (bf16[256,512]{1,0:T(8,128)(2,1)S(1)}, bf16[256,512]{1,0:T(8,128)(2,1)S(1)}, u32[]{:S(2)}, u32[]{:S(2)}) collective-permute-start(bf16[256,512]{1,0:T(8,128)(2,1)S(1)} %shard_map.130.refs_0_.refs_2_), channel_id=1, source_target_pairs={{0,1},{1,0},{2,3},{3,2},{4,5},{5,4},{6,7},{7,6},{8,9},{9,8},{10,11... | collective-permute-start | bytes 786440 | tf_op jit(solution)/shard_map/ppermute | solution.py:294
  54.3 8.4 %collective-permute-start.14 = (bf16[256,512]{1,0:T(8,128)(2,1)S(1)}, bf16[256,512]{1,0:T(8,128)(2,1)S(1)}, u32[]{:S(2)}, u32[]{:S(2)}) collective-permute-start(bf16[256,512]{1,0:T(8,128)(2,1)S(1)} %broadcast_select_fusion), channel_id=1, source_target_pairs={{0,16},{1,17},{8,25},{9,24},{16,0},{17,1},{24,8},{25,9},{2,18},{3,... | collective-permute-start | bytes 786440 | tf_op jit(solution)/shard_map/ppermute | solution.py:427
  62.8 1.6 %collective-permute-start.15 = (bf16[256,512]{1,0:T(8,128)(2,1)S(1)}, bf16[256,512]{1,0:T(8,128)(2,1)S(1)}, u32[]{:S(2)}, u32[]{:S(2)}) collective-permute-start(bf16[256,512]{1,0:T(8,128)(2,1)S(1)} %shard_map.131.refs_0_), channel_id=1, source_target_pairs={{0,8},{8,0},{16,24},{24,16},{1,9},{9,1},{17,25},{25,17},{2,10},{10... | collective-permute-start | bytes 786440 | tf_op jit(solution)/shard_map/ppermute | solution.py:294
  64.4 1.2 %copy-start.7 = (bf16[1,1024,512]{2,1,0:T(8,128)(2,1)S(1)}, bf16[1,1024,512]{2,1,0:T(8,128)(2,1)}, u32[]{:S(2)}) copy-start(bf16[1,1024,512]{2,1,0:T(8,128)(2,1)} %param.20) | copy-start | bytes 3145732
  65.7 3.2 %collective-permute-start.16 = (bf16[256,512]{1,0:T(8,128)(2,1)S(1)}, bf16[256,512]{1,0:T(8,128)(2,1)S(1)}, u32[]{:S(2)}, u32[]{:S(2)}) collective-permute-start(bf16[256,512]{1,0:T(8,128)(2,1)S(1)} %get-tuple-element.51), channel_id=1, source_target_pairs={{0,8},{8,0},{16,24},{24,16},{1,9},{9,1},{17,25},{25,17},{2,10},{10... | collective-permute-start | bytes 786440 | tf_op jit(solution)/shard_map/ppermute | solution.py:294
  69.0 5.5 %collective-permute-start.17 = (bf16[256,128]{1,0:T(8,128)(2,1)S(1)}, bf16[256,128]{1,0:T(8,128)(2,1)S(1)}, u32[]{:S(2)}, u32[]{:S(2)}) collective-permute-start(bf16[256,128]{1,0:T(8,128)(2,1)S(1)} %get-tuple-element.53), channel_id=1, source_target_pairs={{0,1},{1,0},{8,9},{9,8},{16,17},{17,16},{24,25},{25,24},{2,3},{3,2... | collective-permute-start | bytes 196616 | tf_op jit(solution)/shard_map/ppermute | solution.py:474
  70.5 5.7 %collective-permute-start.18 = (bf16[256,128]{1,0:T(8,128)(2,1)S(1)}, bf16[256,128]{1,0:T(8,128)(2,1)S(1)}, u32[]{:S(2)}, u32[]{:S(2)}) collective-permute-start(bf16[256,128]{1,0:T(8,128)(2,1)S(1)} %get-tuple-element.54), channel_id=1, source_target_pairs={{0,16},{1,17},{8,24},{9,25},{16,0},{17,1},{24,8},{25,9},{2,18},{3,... | collective-permute-start | bytes 196616 | tf_op jit(solution)/shard_map/ppermute | solution.py:474
  73.8 5.2 %collective-permute-start.19 = (bf16[256,128]{1,0:T(8,128)(2,1)S(1)}, bf16[256,128]{1,0:T(8,128)(2,1)S(1)}, u32[]{:S(2)}, u32[]{:S(2)}) collective-permute-start(bf16[256,128]{1,0:T(8,128)(2,1)S(1)} %get-tuple-element.55), channel_id=1, source_target_pairs={{0,17},{1,16},{8,25},{9,24},{16,1},{17,0},{24,9},{25,8},{2,19},{3,... | collective-permute-start | bytes 196616 | tf_op jit(solution)/shard_map/ppermute | solution.py:474

commit v10 on v9

--- a/solution.py
+++ b/solution.py
@@ -11,6 +11,8 @@
 HD = 128
 SEQ = 128
 EPS = 1e-05
+
+WEIGHT = 2
 
 LOW = jnp.bfloat16
 WIDE = jnp.float32
@@ -45,7 +47,9 @@
         scratch_shapes=list(scratch),
         input_output_aliases={count + len(after) + i: results + i for i in range(len(held))},
         compiler_params=pltpu.CompilerParams(vmem_limit_bytes=limit * 2**20),
-        cost_estimate=pl.CostEstimate(flops=flops, bytes_accessed=moved, transcendentals=0),
+        cost_estimate=pl.CostEstimate(
+            flops=WEIGHT * flops, bytes_accessed=WEIGHT * moved, transcendentals=0
+        ),
     )(*inputs, *after, *held)
 
 
@@ -160,6 +164,10 @@
     pass
 
 
+def add(kept, arrived, out):
+    out[...] = (kept[...] + arrived[...].astype(WIDE)).astype(LOW)
+
+
 def combine(experts, tokens, high, low, *refs):
     returned, out = refs[:-1], refs[-1]
     tp = lax.axis_index("tp")
@@ -189,6 +197,18 @@
     rest = (rest * factor * gain[:, part(1 - tp, half)]).astype(LOW)
     value = matmul(own, weight[part(tp, half), :]) + matmul(rest, weight[part(1 - tp, half), :])
     out[...] = value.astype(LOW)
+
+
+def encoder_part(own, beside, out):
+    sec = lax.axis_index("sec")
+
+    @pl.when(sec == 1)
+    def _():
+        out[...] = beside[...]
+
+    @pl.when(sec != 1)
+    def _():
+        out[...] = own[...]
 
 
 def choose(own, moved, beside, out):
@@ -345,7 +365,7 @@
         return blocks[0] if len(blocks) == 1 else jnp.concatenate(blocks, axis=0)
 
     def total(away, kept):
-        return (kept + swap(away, "tp", 1).astype(WIDE)).astype(LOW)
+        return call(add, [shape_of(away.shape)], [kept, swap(away, "tp", 1)])[0]
 
     def through(rows, after):
         count = rows[0].shape[0]
@@ -404,7 +424,8 @@
     away, kept = through([arriving[0], others[0]], [returned[0], high])
     near_away, near_kept = through([near], [away])
     mixed = give_back(groups[0], away, kept)
-    returned[1] = swap(total(near_away, near_kept), "exp", 1)
+    near_total = (near_kept + swap(near_away, "tp", 1).astype(WIDE)).astype(LOW)
+    returned[1] = swap(near_total, "exp", 1)
     away, kept = through([arriving[1], others[1]], [near_away, mixed])
     give_back(groups[1], away, kept)
 
@@ -415,9 +436,9 @@
         flops=4 * 3 * token_count * token_count * half,
     )[0]
 
-    beside = swap(hidden_half, "sec", 1)
+    beside = lax.ppermute(hidden_half, "sec", [(0, 1), (1, 0)] + [(i, i) for i in range(2, sections)])
     hidden_other = swap(hidden_half, "tp", 1)
-    encoder_half = jnp.where(sec == 1, beside, hidden_half)
+    encoder_half = call(encoder_part, [shape_of(hidden_half.shape)], [hidden_half, beside])[0]
     moved = hidden_half
     for i in range(1, sections // 2):
         targets = {j: j for j in range(sections * tp_size)}

time: 79.8 us -> 80.2 us (level)
  waiting for transfers between devices: 27.3 us -> 36.8 us
  starting transfers between devices: 34.6 us -> 26.6 us
  local copies, waits for them, and re-layouts: 2.24 us -> 1.03 us
    ppermute x16 -> x15, waiting for transfers between devices: 21.5 us -> 32.1 us  [swap(): return lax.ppermute(block, axis, [(i, i ^ step) for i in range(size)])]
    ppermute x16 -> x15, starting transfers between devices: 28.2 us -> 21.1 us  [swap(): return lax.ppermute(block, axis, [(i, i ^ step) for i in range(size)])]
    ppermute x0 -> x1, starting transfers between devices: none -> 1.92 us  [shards(): lax.ppermute(hidden_half, 'sec', [(0, 1), (1, 0)] + [(i, i) for i in rang...]
    ppermute x3, waiting for transfers between devices: 4.44 us -> 2.92 us  [shards(): total = total + lax.ppermute(blocks[k], ('sec', 'tp'), pairs).astype(WIDE)]
    ppermute x1, starting transfers between devices: 1.56 us -> 0.06 us  [shards(): arrived = lax.ppermute(encoder_half, ('sec', 'tp'), list(targets.items()))]
    ppermute x3, starting transfers between devices: 4.81 us -> 3.57 us  [shards(): total = total + lax.ppermute(blocks[k], ('sec', 'tp'), pairs).astype(WIDE)]
    unnamed x18, local copies, waits for them, and re-layouts: 2.24 us -> 1.03 us
    pallas_call x14 -> x18, Pallas kernels: 13.8 us -> 14 us  [call(): pl.pallas_call(run, out_shape=[*out_shape, *(shape_of(x.shape, x.dtype) f...]
  transfers between devices with their start and end apart: 20 -> 20, of which waited for: 15 -> 13; matrix products, arithmetic and copies ran while one was open for 0% -> 0% of each run, Pallas kernels for 15% -> 15%
where the time goes in v10:
time: 80.2 us; the launch traced here: 80 us
  waiting for transfers between devices  36.8 us (46%)
  starting transfers between devices  26.6 us (33%)
  Pallas kernels  14 us (17%)
  local copies, waits for them, and re-layouts  1.03 us (1%)
  between operations  0.86 us (1%)
    ppermute x15, waiting for transfers between devices, swap(): return lax.ppermute(block, axis, [(i, i ^ step) for i in range(size)])  32.1 us
    ppermute x15, starting transfers between devices, swap(): return lax.ppermute(block, axis, [(i, i ^ step) for i in range(size)])  21.1 us
    pallas_call x18, Pallas kernels, call(): pl.pallas_call(run, out_shape=[*out_shape, *(shape_of(x.shape, x.dtype) f...  14 us
    ppermute x3, starting transfers between devices, shards(): total = total + lax.ppermute(blocks[k], ('sec', 'tp'), pairs).astype(WIDE)  3.57 us
    ppermute x3, waiting for transfers between devices, shards(): total = total + lax.ppermute(blocks[k], ('sec', 'tp'), pairs).astype(WIDE)  2.92 us
    ppermute x1, starting transfers between devices, shards(): lax.ppermute(hidden_half, 'sec', [(0, 1), (1, 0)] + [(i, i) for i in rang...  1.92 us
  transfers between devices with their start and end apart: 20, of which 13 were waited for; matrix products, arithmetic and copies ran while one was open for 0% of the time, Pallas kernels for 15%

profile of v10, /device:TPU:0, one launch (start us, length us, event | category | flops | bytes accessed | tf_op | source)
XLA Modules:
  0.0 80.0 jit_solution(502393506492724180)
XLA Ops:
  0.7 1.0 %copy-done.6 = bf16[1,256,1024]{2,1,0:T(8,128)(2,1)S(1)} copy-done((bf16[1,256,1024]{2,1,0:T(8,128)(2,1)S(1)}, bf16[1,256,1024]{2,1,0:T(8,128)(2,1)}, u32[]{:S(2)}) %copy-start.6) | copy-done | bytes 524312
  1.7 0.9 %shard_map.123 = (bf16[192,512]{1,0:T(8,128)(2,1)S(1)}, bf16[192,512]{1,0:T(8,128)(2,1)S(1)}, bf16[192,1024]{1,0:T(8,128)(2,1)S(1)}, bf16[192,1024]{1,0:T(8,128)(2,1)S(1)}) custom-call(bf16[256,1024]{1,0:T(8,128)(2,1)S(1)} %bitcast.21, s32[2,256]{1,0:T(2,128)S(1)} %bitcast.15, f32[1,1024]{1,0:T(1,128)S(1)} %copy-done.7, ...), custom_call_target="tpu_custom_call" | custom-call | flops 805306368 | bytes 3682304 | tf_op jit(solution)/shard_map/pallas_call | solution.py:42
  2.6 4.1 %collective-permute-start = (bf16[192,512]{1,0:T(8,128)(2,1)S(1)}, bf16[192,512]{1,0:T(8,128)(2,1)S(1)}, u32[]{:S(2)}, u32[]{:S(2)}) collective-permute-start(bf16[192,512]{1,0:T(8,128)(2,1)S(1)} %get-tuple-element.33), channel_id=1, source_target_pairs={{0,4},{2,6},{4,0},{6,2},{1,5},{3,7},{5,1},{7,3},{8,12},{10,14},{12... | collective-permute-start | bytes 589832 | tf_op jit(solution)/shard_map/ppermute | solution.py:314
  6.7 4.6 %shard_map.124 = (bf16[192,512]{1,0:T(8,128)(2,1)S(1)}, f32[192,512]{1,0:T(8,128)S(1)}, bf16[1024,2048]{1,0:T(8,128)(2,1)S(1)}, bf16[2048,1024]{1,0:T(8,128)(2,1...) custom-call(bf16[192,1024]{1,0:T(8,128)(2,1)S(1)} %get-tuple-element, ...), custom_call_target="tpu_custom_call", output_to_operand_aliasing={{4}: (3, {}), {5}: (4, {})} | custom-call | flops 3221225472 | bytes 35520512 | tf_op jit(solution)/shard_map/pallas_call | solution.py:42
  11.3 1.4 %collective-permute-start.8 = (bf16[192,512]{1,0:T(8,128)(2,1)S(1)}, bf16[192,512]{1,0:T(8,128)(2,1)S(1)}, u32[]{:S(2)}, u32[]{:S(2)}) collective-permute-start(bf16[192,512]{1,0:T(8,128)(2,1)S(1)} %get-tuple-element.44), channel_id=1, source_target_pairs={{0,6},{2,4},{4,2},{6,0},{1,7},{3,5},{5,3},{7,1},{8,14},{10,12},{12... | collective-permute-start | bytes 589832 | tf_op jit(solution)/shard_map/ppermute | solution.py:314
  12.7 1.5 %collective-permute-start.1 = (bf16[192,512]{1,0:T(8,128)(2,1)S(1)}, bf16[192,512]{1,0:T(8,128)(2,1)S(1)}, u32[]{:S(2)}, u32[]{:S(2)}) collective-permute-start(bf16[192,512]{1,0:T(8,128)(2,1)S(1)} %get-tuple-element.32.refs_0_), channel_id=1, source_target_pairs={{0,1},{1,0},{2,3},{3,2},{4,5},{5,4},{6,7},{7,6},{8,9},{9,8},{10,11... | collective-permute-start | bytes 589832 | tf_op jit(solution)/shard_map/ppermute | solution.py:314
  14.2 6.6 %collective-permute-done.refs_1_ = bf16[192,512]{1,0:T(8,128)(2,1)S(1)} collective-permute-done((bf16[192,512]{1,0:T(8,128)(2,1)S(1)}, bf16[192,512]{1,0:T(8,128)(2,1)S(1)}, u32[]{:S(2)}, u32[]{:S(2)}) %collective-permute-start) | collective-permute-done | bytes 196640 | tf_op jit(solution)/shard_map/ppermute | solution.py:314
  20.8 1.9 %collective-permute-start.3 = (bf16[192,512]{1,0:T(8,128)(2,1)S(1)}, bf16[192,512]{1,0:T(8,128)(2,1)S(1)}, u32[]{:S(2)}, u32[]{:S(2)}) collective-permute-start(bf16[192,512]{1,0:T(8,128)(2,1)S(1)} %shard_map.125.refs_4_.refs_0_), channel_id=1, source_target_pairs={{0,1},{1,0},{2,3},{3,2},{4,5},{5,4},{6,7},{7,6},{8,9},{9,8},{10,11... | collective-permute-start | bytes 589832 | tf_op jit(solution)/shard_map/ppermute | solution.py:314
  22.7 0.6 shard_map.126
  23.3 0.2 collective-permute-start.9
  23.6 4.4 %collective-permute-done.3.refs_1_ = bf16[192,512]{1,0:T(8,128)(2,1)S(1)} collective-permute-done((bf16[192,512]{1,0:T(8,128)(2,1)S(1)}, bf16[192,512]{1,0:T(8,128)(2,1)S(1)}, u32[]{:S(2)}, u32[]{:S(2)}) %collective-permute-start.3) | collective-permute-done | bytes 196640 | tf_op jit(solution)/shard_map/ppermute | solution.py:314
  28.1 1.8 %shard_map.128 = (bf16[192,512]{1,0:T(8,128)(2,1)S(1)}, f32[192,512]{1,0:T(8,128)S(1)}) custom-call(bf16[192,512]{1,0:T(8,128)(2,1)S(1)} %shard_map.125.refs_4_.refs_0_, bf16[192,512]{1,0:T(8,128)(2,1)S(1)} %collective-permute-done.3.refs_1_, bf16[1024,2048]{1,0:T(8,128)(2,1)S(1)} %get-tuple-element.38.refs_2_.refs_1_, ...), custom_call_target="tpu_custom_call" | custom-call | flops 3221225472 | bytes 18743296 | tf_op jit(solution)/shard_map/pallas_call | solution.py:42
  29.9 2.5 %collective-permute-start.6 = (bf16[192,512]{1,0:T(8,128)(2,1)S(1)}, bf16[192,512]{1,0:T(8,128)(2,1)S(1)}, u32[]{:S(2)}, u32[]{:S(2)}) collective-permute-start(bf16[192,512]{1,0:T(8,128)(2,1)S(1)} %get-tuple-element.40.refs_3_), channel_id=1, source_target_pairs={{0,1},{1,0},{2,3},{3,2},{4,5},{5,4},{6,7},{7,6},{8,9},{9,8},{10,11... | collective-permute-start | bytes 589832 | tf_op jit(solution)/shard_map/ppermute | solution.py:314
  32.3 1.8 %shard_map.129 = (bf16[192,512]{1,0:T(8,128)(2,1)S(1)}, f32[192,512]{1,0:T(8,128)S(1)}) custom-call(bf16[192,1024]{1,0:T(8,128)(2,1)S(1)} %collective-permute-done.2.refs_0_, bf16[1024,2048]{1,0:T(8,128)(2,1)S(1)} %get-tuple-element.38.refs_2_.refs_1_, bf16[2048,1024]{1,0:T(8,128)(2,1)S(1)} %get-tuple-element.39.refs_3_.refs_2_, ...), custom_call_target="tpu_custom_call" | custom-call | flops 3221225472 | bytes 18743296 | tf_op jit(solution)/shard_map/pallas_call | solution.py:42
  34.2 0.1 collective-permute-start.4
  34.3 3.3 %collective-permute-done.6.refs_1_ = bf16[192,512]{1,0:T(8,128)(2,1)S(1)} collective-permute-done((bf16[192,512]{1,0:T(8,128)(2,1)S(1)}, bf16[192,512]{1,0:T(8,128)(2,1)S(1)}, u32[]{:S(2)}, u32[]{:S(2)}) %collective-permute-start.6) | collective-permute-done | bytes 196640 | tf_op jit(solution)/shard_map/ppermute | solution.py:314
  37.6 0.4 collective-permute-start.7
  38.0 1.8 %shard_map.131 = (bf16[192,512]{1,0:T(8,128)(2,1)S(1)}, f32[192,512]{1,0:T(8,128)S(1)}) custom-call(bf16[192,512]{1,0:T(8,128)(2,1)S(1)} %collective-permute-done.8.refs_0_, bf16[192,512]{1,0:T(8,128)(2,1)S(1)} %collective-permute-done.9.refs_1_, bf16[1024,2048]{1,0:T(8,128)(2,1)S(1)} %get-tuple-element.38.refs_2_.refs_1_, ...), custom_call_target="tpu_custom_call" | custom-call | flops 3221225472 | bytes 18743296 | tf_op jit(solution)/shard_map/pallas_call | solution.py:42
  39.8 0.0 copy-start.3
  39.8 0.0 copy-start.4
  39.8 0.0 copy-start.5
  39.8 2.2 %collective-permute-start.10 = (bf16[192,512]{1,0:T(8,128)(2,1)S(1)}, bf16[192,512]{1,0:T(8,128)(2,1)S(1)}, u32[]{:S(2)}, u32[]{:S(2)}) collective-permute-start(bf16[192,512]{1,0:T(8,128)(2,1)S(1)} %get-tuple-element.46), channel_id=1, source_target_pairs={{0,1},{1,0},{2,3},{3,2},{4,5},{5,4},{6,7},{7,6},{8,9},{9,8},{10,11... | collective-permute-start | bytes 589832 | tf_op jit(solution)/shard_map/ppermute | solution.py:314
  42.1 2.0 %collective-permute-start.5 = (bf16[192,512]{1,0:T(8,128)(2,1)S(1)}, bf16[192,512]{1,0:T(8,128)(2,1)S(1)}, u32[]{:S(2)}, u32[]{:S(2)}) collective-permute-start(bf16[192,512]{1,0:T(8,128)(2,1)S(1)} %add_convert_fusion), channel_id=1, source_target_pairs={{0,2},{2,0},{4,6},{6,4},{1,3},{3,1},{5,7},{7,5},{8,10},{10,8},{12,... | collective-permute-start | bytes 589832 | tf_op jit(solution)/shard_map/ppermute | solution.py:314
  44.1 1.6 %collective-permute-done.10.refs_1_ = bf16[192,512]{1,0:T(8,128)(2,1)S(1)} collective-permute-done((bf16[192,512]{1,0:T(8,128)(2,1)S(1)}, bf16[192,512]{1,0:T(8,128)(2,1)S(1)}, u32[]{:S(2)}, u32[]{:S(2)}) %collective-permute-start.10) | collective-permute-done | bytes 196640 | tf_op jit(solution)/shard_map/ppermute | solution.py:314
  45.8 1.9 %collective-permute-start.11 = (bf16[192,512]{1,0:T(8,128)(2,1)S(1)}, bf16[192,512]{1,0:T(8,128)(2,1)S(1)}, u32[]{:S(2)}, u32[]{:S(2)}) collective-permute-start(bf16[192,512]{1,0:T(8,128)(2,1)S(1)} %shard_map.132), channel_id=1, source_target_pairs={{0,6},{2,4},{4,2},{6,0},{1,7},{3,5},{5,3},{7,1},{8,14},{10,12},{12... | collective-permute-start | bytes 589832 | tf_op jit(solution)/shard_map/ppermute | solution.py:314
  47.7 6.9 %collective-permute-done.5.refs_4_ = bf16[192,512]{1,0:T(8,128)(2,1)S(1)} collective-permute-done((bf16[192,512]{1,0:T(8,128)(2,1)S(1)}, bf16[192,512]{1,0:T(8,128)(2,1)S(1)}, u32[]{:S(2)}, u32[]{:S(2)}) %collective-permute-start.5) | collective-permute-done | bytes 196640 | tf_op jit(solution)/shard_map/ppermute | solution.py:314
  54.6 0.7 shard_map.133.refs_0_.refs_2_
  55.3 1.9 %collective-permute-start.13 = (bf16[256,512]{1,0:T(8,128)(2,1)S(1)}, bf16[256,512]{1,0:T(8,128)(2,1)S(1)}, u32[]{:S(2)}, u32[]{:S(2)}) collective-permute-start(bf16[256,512]{1,0:T(8,128)(2,1)S(1)} %shard_map.133.refs_0_.refs_2_), channel_id=1, source_target_pairs={{0,8},{8,0},{16,16},{24,24},{1,9},{9,1},{17,17},{25,25},{2,10},{10... | collective-permute-start | bytes 786440 | tf_op jit(solution)/shard_map/ppermute | solution.py:439
  57.3 0.9 %collective-permute-start.12 = (bf16[256,512]{1,0:T(8,128)(2,1)S(1)}, bf16[256,512]{1,0:T(8,128)(2,1)S(1)}, u32[]{:S(2)}, u32[]{:S(2)}) collective-permute-start(bf16[256,512]{1,0:T(8,128)(2,1)S(1)} %shard_map.133.refs_0_.refs_2_), channel_id=1, source_target_pairs={{0,1},{1,0},{2,3},{3,2},{4,5},{5,4},{6,7},{7,6},{8,9},{9,8},{10,11... | collective-permute-start | bytes 786440 | tf_op jit(solution)/shard_map/ppermute | solution.py:314
  58.1 0.6 collective-permute-done.13.refs_1_.refs_2_
  58.8 0.1 collective-permute-start.14
  58.8 7.2 %collective-permute-done.12.refs_0_.refs_1_ = bf16[256,512]{1,0:T(8,128)(2,1)S(1)} collective-permute-done((bf16[256,512]{1,0:T(8,128)(2,1)S(1)}, bf16[256,512]{1,0:T(8,128)(2,1)S(1)}, u32[]{:S(2)}, u32[]{:S(2)}) %collective-permute-start.12) | collective-permute-done | bytes 262176 | tf_op jit(solution)/shard_map/ppermute | solution.py:314
  66.0 1.2 %collective-permute-done.14.refs_1_ = bf16[256,512]{1,0:T(8,128)(2,1)S(1)} collective-permute-done((bf16[256,512]{1,0:T(8,128)(2,1)S(1)}, bf16[256,512]{1,0:T(8,128)(2,1)S(1)}, u32[]{:S(2)}, u32[]{:S(2)}) %collective-permute-start.14) | collective-permute-done | bytes 262176 | tf_op jit(solution)/shard_map/ppermute | solution.py:448
  67.2 0.1 collective-permute-start.15
  67.3 0.7 shard_map.136.refs_2_
  68.0 0.8 %collective-permute-done.15.refs_1_ = bf16[256,512]{1,0:T(8,128)(2,1)S(1)} collective-permute-done((bf16[256,512]{1,0:T(8,128)(2,1)S(1)}, bf16[256,512]{1,0:T(8,128)(2,1)S(1)}, u32[]{:S(2)}, u32[]{:S(2)}) %collective-permute-start.15) | collective-permute-done | bytes 262176 | tf_op jit(solution)/shard_map/ppermute | solution.py:314
  68.8 0.1 shard_map.137
  68.9 2.0 %collective-permute-start.16 = (bf16[256,512]{1,0:T(8,128)(2,1)S(1)}, bf16[256,512]{1,0:T(8,128)(2,1)S(1)}, u32[]{:S(2)}, u32[]{:S(2)}) collective-permute-start(bf16[256,512]{1,0:T(8,128)(2,1)S(1)} %get-tuple-element.51), channel_id=1, source_target_pairs={{0,8},{8,0},{16,24},{24,16},{1,9},{9,1},{17,25},{25,17},{2,10},{10... | collective-permute-start | bytes 786440 | tf_op jit(solution)/shard_map/ppermute | solution.py:314
  70.9 1.2 %collective-permute-done.16.refs_1_ = bf16[256,512]{1,0:T(8,128)(2,1)S(1)} collective-permute-done((bf16[256,512]{1,0:T(8,128)(2,1)S(1)}, bf16[256,512]{1,0:T(8,128)(2,1)S(1)}, u32[]{:S(2)}, u32[]{:S(2)}) %collective-permute-start.16) | collective-permute-done | bytes 262176 | tf_op jit(solution)/shard_map/ppermute | solution.py:314
  72.0 0.1 shard_map.139
  72.2 0.9 %collective-permute-start.17 = (bf16[256,128]{1,0:T(8,128)(2,1)S(1)}, bf16[256,128]{1,0:T(8,128)(2,1)S(1)}, u32[]{:S(2)}, u32[]{:S(2)}) collective-permute-start(bf16[256,128]{1,0:T(8,128)(2,1)S(1)} %get-tuple-element.53), channel_id=1, source_target_pairs={{0,1},{1,0},{8,9},{9,8},{16,17},{17,16},{24,25},{25,24},{2,3},{3,2... | collective-permute-start | bytes 196616 | tf_op jit(solution)/shard_map/ppermute | solution.py:495
  73.0 1.1 %collective-permute-start.18 = (bf16[256,128]{1,0:T(8,128)(2,1)S(1)}, bf16[256,128]{1,0:T(8,128)(2,1)S(1)}, u32[]{:S(2)}, u32[]{:S(2)}) collective-permute-start(bf16[256,128]{1,0:T(8,128)(2,1)S(1)} %get-tuple-element.54), channel_id=1, source_target_pairs={{0,16},{1,17},{8,24},{9,25},{16,0},{17,1},{24,8},{25,9},{2,18},{3,... | collective-permute-start | bytes 196616 | tf_op jit(solution)/shard_map/ppermute | solution.py:495
  74.2 1.6 %collective-permute-start.19 = (bf16[256,128]{1,0:T(8,128)(2,1)S(1)}, bf16[256,128]{1,0:T(8,128)(2,1)S(1)}, u32[]{:S(2)}, u32[]{:S(2)}) collective-permute-start(bf16[256,128]{1,0:T(8,128)(2,1)S(1)} %get-tuple-element.55), channel_id=1, source_target_pairs={{0,17},{1,16},{8,25},{9,24},{16,1},{17,0},{24,9},{25,8},{2,19},{3,... | collective-permute-start | bytes 196616 | tf_op jit(solution)/shard_map/ppermute | solution.py:495
  75.7 0.7 shard_map.138
  76.4 0.1 collective-permute-done.17
  76.6 0.7 collective-permute-done.18
  77.3 2.1 %collective-permute-done.19 = bf16[256,128]{1,0:T(8,128)(2,1)S(1)} collective-permute-done((bf16[256,128]{1,0:T(8,128)(2,1)S(1)}, bf16[256,128]{1,0:T(8,128)(2,1)S(1)}, u32[]{:S(2)}, u32[]{:S(2)}) %collective-permute-start.19) | collective-permute-done | bytes 65568 | tf_op jit(solution)/shard_map/ppermute | solution.py:495
  79.4 0.7 add_convert_fusion.1
  (30 shorter events, 0.3 us)
Async XLA Ops:
  0.6 1.0 %copy-start.6 = (bf16[1,256,1024]{2,1,0:T(8,128)(2,1)S(1)}, bf16[1,256,1024]{2,1,0:T(8,128)(2,1)}, u32[]{:S(2)}) copy-start(bf16[1,256,1024]{2,1,0:T(8,128)(2,1)} %param.11) | copy-start | bytes 1572868
  0.6 1.0 %copy-start.1 = (s32[1,256,2]{1,2,0:T(2,128)S(1)}, s32[1,256,2]{1,2,0:T(2,128)}, u32[]{:S(2)}) copy-start(s32[1,256,2]{1,2,0:T(2,128)} %param.12) | copy-start | bytes 6148
  0.6 1.0 %copy-start.7 = (f32[1,1024]{1,0:T(1,128)S(1)}, f32[1,1024]{1,0:T(1,128)}, u32[]{:S(2)}) copy-start(f32[1,1024]{1,0:T(1,128)} %refs_2_.2) | copy-start | bytes 12292
  2.6 18.3 %collective-permute-start = (bf16[192,512]{1,0:T(8,128)(2,1)S(1)}, bf16[192,512]{1,0:T(8,128)(2,1)S(1)}, u32[]{:S(2)}, u32[]{:S(2)}) collective-permute-start(bf16[192,512]{1,0:T(8,128)(2,1)S(1)} %get-tuple-element.33), channel_id=1, source_target_pairs={{0,4},{2,6},{4,0},{6,2},{1,5},{3,7},{5,1},{7,3},{8,12},{10,14},{12... | collective-permute-start | bytes 589832 | tf_op jit(solution)/shard_map/ppermute | solution.py:314
  6.7 16.0 %copy-start = (bf16[1,256,512]{2,1,0:T(8,128)(2,1)S(1)}, bf16[1,256,512]{2,1,0:T(8,128)(2,1)}, u32[]{:S(2)}) copy-start(bf16[1,256,512]{2,1,0:T(8,128)(2,1)} %param.21) | copy-start | bytes 786436
  6.7 16.0 %copy-start.2 = (f32[1,256,2]{1,2,0:T(2,128)S(1)}, f32[1,256,2]{1,2,0:T(2,128)}, u32[]{:S(2)}) copy-start(f32[1,256,2]{1,2,0:T(2,128)} %param.13) | copy-start | bytes 6148
  11.3 12.0 %collective-permute-start.8 = (bf16[192,512]{1,0:T(8,128)(2,1)S(1)}, bf16[192,512]{1,0:T(8,128)(2,1)S(1)}, u32[]{:S(2)}, u32[]{:S(2)}) collective-permute-start(bf16[192,512]{1,0:T(8,128)(2,1)S(1)} %get-tuple-element.44), channel_id=1, source_target_pairs={{0,6},{2,4},{4,2},{6,0},{1,7},{3,5},{5,3},{7,1},{8,14},{10,12},{12... | collective-permute-start | bytes 589832 | tf_op jit(solution)/shard_map/ppermute | solution.py:314
  12.7 10.9 %collective-permute-start.1 = (bf16[192,512]{1,0:T(8,128)(2,1)S(1)}, bf16[192,512]{1,0:T(8,128)(2,1)S(1)}, u32[]{:S(2)}, u32[]{:S(2)}) collective-permute-start(bf16[192,512]{1,0:T(8,128)(2,1)S(1)} %get-tuple-element.32.refs_0_), channel_id=1, source_target_pairs={{0,1},{1,0},{2,3},{3,2},{4,5},{5,4},{6,7},{7,6},{8,9},{9,8},{10,11... | collective-permute-start | bytes 589832 | tf_op jit(solution)/shard_map/ppermute | solution.py:314
  20.8 7.2 %collective-permute-start.3 = (bf16[192,512]{1,0:T(8,128)(2,1)S(1)}, bf16[192,512]{1,0:T(8,128)(2,1)S(1)}, u32[]{:S(2)}, u32[]{:S(2)}) collective-permute-start(bf16[192,512]{1,0:T(8,128)(2,1)S(1)} %shard_map.125.refs_4_.refs_0_), channel_id=1, source_target_pairs={{0,1},{1,0},{2,3},{3,2},{4,5},{5,4},{6,7},{7,6},{8,9},{9,8},{10,11... | collective-permute-start | bytes 589832 | tf_op jit(solution)/shard_map/ppermute | solution.py:314
  22.7 9.6 %collective-permute-start.2 = (bf16[192,1024]{1,0:T(8,128)(2,1)S(1)}, bf16[192,1024]{1,0:T(8,128)(2,1)S(1)}, u32[]{:S(2)}, u32[]{:S(2)}) collective-permute-start(bf16[192,1024]{1,0:T(8,128)(2,1)S(1)} %get-tuple-element.37), channel_id=1, source_target_pairs={{0,2},{2,0},{4,6},{6,4},{1,3},{3,1},{5,7},{7,5},{8,10},{10,8},{12,... | collective-permute-start | bytes 1179656 | tf_op jit(solution)/shard_map/ppermute | solution.py:314
  23.3 14.7 %collective-permute-start.9 = (bf16[192,512]{1,0:T(8,128)(2,1)S(1)}, bf16[192,512]{1,0:T(8,128)(2,1)S(1)}, u32[]{:S(2)}, u32[]{:S(2)}) collective-permute-start(bf16[192,512]{1,0:T(8,128)(2,1)S(1)} %collective-permute-done.8.refs_0_), channel_id=1, source_target_pairs={{0,1},{1,0},{2,3},{3,2},{4,5},{5,4},{6,7},{7,6},{8,9},{9,8},{10,11... | collective-permute-start | bytes 589832 | tf_op jit(solution)/shard_map/ppermute | solution.py:314
  29.9 7.7 %collective-permute-start.6 = (bf16[192,512]{1,0:T(8,128)(2,1)S(1)}, bf16[192,512]{1,0:T(8,128)(2,1)S(1)}, u32[]{:S(2)}, u32[]{:S(2)}) collective-permute-start(bf16[192,512]{1,0:T(8,128)(2,1)S(1)} %get-tuple-element.40.refs_3_), channel_id=1, source_target_pairs={{0,1},{1,0},{2,3},{3,2},{4,5},{5,4},{6,7},{7,6},{8,9},{9,8},{10,11... | collective-permute-start | bytes 589832 | tf_op jit(solution)/shard_map/ppermute | solution.py:314
  34.2 7.9 %collective-permute-start.4 = (bf16[192,512]{1,0:T(8,128)(2,1)S(1)}, bf16[192,512]{1,0:T(8,128)(2,1)S(1)}, u32[]{:S(2)}, u32[]{:S(2)}) collective-permute-start(bf16[192,512]{1,0:T(8,128)(2,1)S(1)} %get-tuple-element.42.refs_4_), channel_id=1, source_target_pairs={{0,1},{1,0},{2,3},{3,2},{4,5},{5,4},{6,7},{7,6},{8,9},{9,8},{10,11... | collective-permute-start | bytes 589832 | tf_op jit(solution)/shard_map/ppermute | solution.py:314
  37.6 10.1 %collective-permute-start.7 = (bf16[192,512]{1,0:T(8,128)(2,1)S(1)}, bf16[192,512]{1,0:T(8,128)(2,1)S(1)}, u32[]{:S(2)}, u32[]{:S(2)}) collective-permute-start(bf16[192,512]{1,0:T(8,128)(2,1)S(1)} %shard_map.130.refs_5_), channel_id=1, source_target_pairs={{0,4},{2,6},{4,0},{6,2},{1,5},{3,7},{5,1},{7,3},{8,12},{10,14},{12... | collective-permute-start | bytes 589832 | tf_op jit(solution)/shard_map/ppermute | solution.py:314
  39.8 27.5 %copy-start.3 = (bf16[1,1024,512]{2,1,0:T(8,128)(2,1)S(1)}, bf16[1,1024,512]{2,1,0:T(8,128)(2,1)}, u32[]{:S(2)}) copy-start(bf16[1,1024,512]{2,1,0:T(8,128)(2,1)} %param.18) | copy-start | bytes 3145732
  39.8 27.5 %copy-start.8 = (f32[1,1024]{1,0:T(1,128)S(1)}, f32[1,1024]{1,0:T(1,128)}, u32[]{:S(2)}) copy-start(f32[1,1024]{1,0:T(1,128)} %refs_2_.3) | copy-start | bytes 12292
  39.8 29.0 %copy-start.4 = (bf16[1,1024,512]{2,1,0:T(8,128)(2,1)S(1)}, bf16[1,1024,512]{2,1,0:T(8,128)(2,1)}, u32[]{:S(2)}) copy-start(bf16[1,1024,512]{2,1,0:T(8,128)(2,1)} %param.19) | copy-start | bytes 3145732
  39.8 29.0 %copy-start.5 = (bf16[1,1024,512]{2,1,0:T(8,128)(2,1)S(1)}, bf16[1,1024,512]{2,1,0:T(8,128)(2,1)}, u32[]{:S(2)}) copy-start(bf16[1,1024,512]{2,1,0:T(8,128)(2,1)} %param.20) | copy-start | bytes 3145732
  39.8 5.9 %collective-permute-start.10 = (bf16[192,512]{1,0:T(8,128)(2,1)S(1)}, bf16[192,512]{1,0:T(8,128)(2,1)S(1)}, u32[]{:S(2)}, u32[]{:S(2)}) collective-permute-start(bf16[192,512]{1,0:T(8,128)(2,1)S(1)} %get-tuple-element.46), channel_id=1, source_target_pairs={{0,1},{1,0},{2,3},{3,2},{4,5},{5,4},{6,7},{7,6},{8,9},{9,8},{10,11... | collective-permute-start | bytes 589832 | tf_op jit(solution)/shard_map/ppermute | solution.py:314
  42.1 12.5 %collective-permute-start.5 = (bf16[192,512]{1,0:T(8,128)(2,1)S(1)}, bf16[192,512]{1,0:T(8,128)(2,1)S(1)}, u32[]{:S(2)}, u32[]{:S(2)}) collective-permute-start(bf16[192,512]{1,0:T(8,128)(2,1)S(1)} %add_convert_fusion), channel_id=1, source_target_pairs={{0,2},{2,0},{4,6},{6,4},{1,3},{3,1},{5,7},{7,5},{8,10},{10,8},{12,... | collective-permute-start | bytes 589832 | tf_op jit(solution)/shard_map/ppermute | solution.py:314
  45.8 8.8 %collective-permute-start.11 = (bf16[192,512]{1,0:T(8,128)(2,1)S(1)}, bf16[192,512]{1,0:T(8,128)(2,1)S(1)}, u32[]{:S(2)}, u32[]{:S(2)}) collective-permute-start(bf16[192,512]{1,0:T(8,128)(2,1)S(1)} %shard_map.132), channel_id=1, source_target_pairs={{0,6},{2,4},{4,2},{6,0},{1,7},{3,5},{5,3},{7,1},{8,14},{10,12},{12... | collective-permute-start | bytes 589832 | tf_op jit(solution)/shard_map/ppermute | solution.py:314
  55.3 3.4 %collective-permute-start.13 = (bf16[256,512]{1,0:T(8,128)(2,1)S(1)}, bf16[256,512]{1,0:T(8,128)(2,1)S(1)}, u32[]{:S(2)}, u32[]{:S(2)}) collective-permute-start(bf16[256,512]{1,0:T(8,128)(2,1)S(1)} %shard_map.133.refs_0_.refs_2_), channel_id=1, source_target_pairs={{0,8},{8,0},{16,16},{24,24},{1,9},{9,1},{17,17},{25,25},{2,10},{10... | collective-permute-start | bytes 786440 | tf_op jit(solution)/shard_map/ppermute | solution.py:439
  57.3 8.8 %collective-permute-start.12 = (bf16[256,512]{1,0:T(8,128)(2,1)S(1)}, bf16[256,512]{1,0:T(8,128)(2,1)S(1)}, u32[]{:S(2)}, u32[]{:S(2)}) collective-permute-start(bf16[256,512]{1,0:T(8,128)(2,1)S(1)} %shard_map.133.refs_0_.refs_2_), channel_id=1, source_target_pairs={{0,1},{1,0},{2,3},{3,2},{4,5},{5,4},{6,7},{7,6},{8,9},{9,8},{10,11... | collective-permute-start | bytes 786440 | tf_op jit(solution)/shard_map/ppermute | solution.py:314
  58.8 8.4 %collective-permute-start.14 = (bf16[256,512]{1,0:T(8,128)(2,1)S(1)}, bf16[256,512]{1,0:T(8,128)(2,1)S(1)}, u32[]{:S(2)}, u32[]{:S(2)}) collective-permute-start(bf16[256,512]{1,0:T(8,128)(2,1)S(1)} %shard_map.134), channel_id=1, source_target_pairs={{0,16},{1,17},{8,25},{9,24},{16,0},{17,1},{24,8},{25,9},{2,18},{3,... | collective-permute-start | bytes 786440 | tf_op jit(solution)/shard_map/ppermute | solution.py:448
  67.2 1.6 %collective-permute-start.15 = (bf16[256,512]{1,0:T(8,128)(2,1)S(1)}, bf16[256,512]{1,0:T(8,128)(2,1)S(1)}, u32[]{:S(2)}, u32[]{:S(2)}) collective-permute-start(bf16[256,512]{1,0:T(8,128)(2,1)S(1)} %shard_map.135.refs_0_), channel_id=1, source_target_pairs={{0,8},{8,0},{16,24},{24,16},{1,9},{9,1},{17,25},{25,17},{2,10},{10... | collective-permute-start | bytes 786440 | tf_op jit(solution)/shard_map/ppermute | solution.py:314
  68.9 3.2 %collective-permute-start.16 = (bf16[256,512]{1,0:T(8,128)(2,1)S(1)}, bf16[256,512]{1,0:T(8,128)(2,1)S(1)}, u32[]{:S(2)}, u32[]{:S(2)}) collective-permute-start(bf16[256,512]{1,0:T(8,128)(2,1)S(1)} %get-tuple-element.51), channel_id=1, source_target_pairs={{0,8},{8,0},{16,24},{24,16},{1,9},{9,1},{17,25},{25,17},{2,10},{10... | collective-permute-start | bytes 786440 | tf_op jit(solution)/shard_map/ppermute | solution.py:314
  72.2 4.4 %collective-permute-start.17 = (bf16[256,128]{1,0:T(8,128)(2,1)S(1)}, bf16[256,128]{1,0:T(8,128)(2,1)S(1)}, u32[]{:S(2)}, u32[]{:S(2)}) collective-permute-start(bf16[256,128]{1,0:T(8,128)(2,1)S(1)} %get-tuple-element.53), channel_id=1, source_target_pairs={{0,1},{1,0},{8,9},{9,8},{16,17},{17,16},{24,25},{25,24},{2,3},{3,2... | collective-permute-start | bytes 196616 | tf_op jit(solution)/shard_map/ppermute | solution.py:495
  73.0 4.3 %collective-permute-start.18 = (bf16[256,128]{1,0:T(8,128)(2,1)S(1)}, bf16[256,128]{1,0:T(8,128)(2,1)S(1)}, u32[]{:S(2)}, u32[]{:S(2)}) collective-permute-start(bf16[256,128]{1,0:T(8,128)(2,1)S(1)} %get-tuple-element.54), channel_id=1, source_target_pairs={{0,16},{1,17},{8,24},{9,25},{16,0},{17,1},{24,8},{25,9},{2,18},{3,... | collective-permute-start | bytes 196616 | tf_op jit(solution)/shard_map/ppermute | solution.py:495
  74.2 5.2 %collective-permute-start.19 = (bf16[256,128]{1,0:T(8,128)(2,1)S(1)}, bf16[256,128]{1,0:T(8,128)(2,1)S(1)}, u32[]{:S(2)}, u32[]{:S(2)}) collective-permute-start(bf16[256,128]{1,0:T(8,128)(2,1)S(1)} %get-tuple-element.55), channel_id=1, source_target_pairs={{0,17},{1,16},{8,25},{9,24},{16,1},{17,0},{24,9},{25,8},{2,19},{3,... | collective-permute-start | bytes 196616 | tf_op jit(solution)/shard_map/ppermute | solution.py:495

commit v11 on v10

--- a/solution.py
+++ b/solution.py
@@ -11,8 +11,6 @@
 HD = 128
 SEQ = 128
 EPS = 1e-05
-
-WEIGHT = 2
 
 LOW = jnp.bfloat16
 WIDE = jnp.float32
@@ -47,9 +45,7 @@
         scratch_shapes=list(scratch),
         input_output_aliases={count + len(after) + i: results + i for i in range(len(held))},
         compiler_params=pltpu.CompilerParams(vmem_limit_bytes=limit * 2**20),
-        cost_estimate=pl.CostEstimate(
-            flops=WEIGHT * flops, bytes_accessed=WEIGHT * moved, transcendentals=0
-        ),
+        cost_estimate=pl.CostEstimate(flops=flops, bytes_accessed=moved, transcendentals=0),
     )(*inputs, *after, *held)
 
 
@@ -364,8 +360,11 @@
         blocks = [swap(far_rows[k - 2], "exp", k) for k in group]
         return blocks[0] if len(blocks) == 1 else jnp.concatenate(blocks, axis=0)
 
-    def total(away, kept):
-        return call(add, [shape_of(away.shape)], [kept, swap(away, "tp", 1)])[0]
+    def total(away, kept, plain=False):
+        arrived = swap(away, "tp", 1)
+        if plain:
+            return (kept + arrived.astype(WIDE)).astype(LOW)
+        return call(add, [shape_of(away.shape)], [kept, arrived])[0]
 
     def through(rows, after):
         count = rows[0].shape[0]
@@ -401,7 +400,7 @@
     for k, rows in zip(groups[1], later[1:]):
         far_rows[k - 2] = rows
     arriving.append(joined(groups[1]))
-    returned = {0: total(own_away, own_kept)}
+    returned = {0: total(own_away, own_kept, plain=True)}
     arriving[0] = hold(arriving[0], [own_away])
     others = [swap(arriving[0], "tp", 1)]
     high, low, upstream = call(
@@ -424,8 +423,7 @@
     away, kept = through([arriving[0], others[0]], [returned[0], high])
     near_away, near_kept = through([near], [away])
     mixed = give_back(groups[0], away, kept)
-    near_total = (near_kept + swap(near_away, "tp", 1).astype(WIDE)).astype(LOW)
-    returned[1] = swap(near_total, "exp", 1)
+    returned[1] = swap(total(near_away, near_kept, plain=True), "exp", 1)
     away, kept = through([arriving[1], others[1]], [near_away, mixed])
     give_back(groups[1], away, kept)
 

time: 80.2 us -> 77.6 us (0.968)
  waiting for transfers between devices: 36.8 us -> 26.9 us
  starting transfers between devices: 26.6 us -> 33.9 us
    ppermute x15, waiting for transfers between devices: 32.1 us -> 22.8 us  [swap(): return lax.ppermute(block, axis, [(i, i ^ step) for i in range(size)])]
    ppermute x15, starting transfers between devices: 21.1 us -> 28.1 us  [swap(): return lax.ppermute(block, axis, [(i, i ^ step) for i in range(size)])]
    pallas_call x18 -> x17, Pallas kernels: 14 us -> 13.9 us  [call(): pl.pallas_call(run, out_shape=[*out_shape, *(shape_of(x.shape, x.dtype) f...]
  transfers between devices with their start and end apart: 20 -> 20, of which waited for: 13 -> 16; matrix products, arithmetic and copies ran while one was open for 0% -> 0% of each run, Pallas kernels for 15% -> 16%
where the time goes in v11:
time: 77.6 us; the launch traced here: 77.4 us
  starting transfers between devices  33.9 us (44%)
  waiting for transfers between devices  26.9 us (35%)
  Pallas kernels  13.9 us (18%)
  local copies, waits for them, and re-layouts  1.03 us (1%)
  between operations  0.86 us (1%)
    ppermute x15, starting transfers between devices, swap(): return lax.ppermute(block, axis, [(i, i ^ step) for i in range(size)])  28.1 us
    ppermute x15, waiting for transfers between devices, swap(): return lax.ppermute(block, axis, [(i, i ^ step) for i in range(size)])  22.8 us
    pallas_call x17, Pallas kernels, call(): pl.pallas_call(run, out_shape=[*out_shape, *(shape_of(x.shape, x.dtype) f...  13.9 us
    ppermute x3, starting transfers between devices, shards(): total = total + lax.ppermute(blocks[k], ('sec', 'tp'), pairs).astype(WIDE)  3.57 us
    ppermute x3, waiting for transfers between devices, shards(): total = total + lax.ppermute(blocks[k], ('sec', 'tp'), pairs).astype(WIDE)  2.82 us
    ppermute x1, starting transfers between devices, shards(): lax.ppermute(hidden_half, 'sec', [(0, 1), (1, 0)] + [(i, i) for i in rang...  1.92 us
  transfers between devices with their start and end apart: 20, of which 16 were waited for; matrix products, arithmetic and copies ran while one was open for 0% of the time, Pallas kernels for 16%

profile of v11, /device:TPU:0, one launch (start us, length us, event | category | flops | bytes accessed | tf_op | source)
XLA Modules:
  0.0 77.4 jit_solution(9256226557427488623)
XLA Ops:
  0.7 1.0 %copy-done.1 = bf16[1,256,1024]{2,1,0:T(8,128)(2,1)S(1)} copy-done((bf16[1,256,1024]{2,1,0:T(8,128)(2,1)S(1)}, bf16[1,256,1024]{2,1,0:T(8,128)(2,1)}, u32[]{:S(2)}) %copy-start.1) | copy-done | bytes 524312
  1.7 0.9 %shard_map.123 = (bf16[192,512]{1,0:T(8,128)(2,1)S(1)}, bf16[192,512]{1,0:T(8,128)(2,1)S(1)}, bf16[192,1024]{1,0:T(8,128)(2,1)S(1)}, bf16[192,1024]{1,0:T(8,128)(2,1)S(1)}) custom-call(bf16[256,1024]{1,0:T(8,128)(2,1)S(1)} %bitcast.15, s32[2,256]{1,0:T(2,128)S(1)} %bitcast.18, f32[1,1024]{1,0:T(1,128)S(1)} %copy-done.8, ...), custom_call_target="tpu_custom_call" | custom-call | flops 402653184 | bytes 1841152 | tf_op jit(solution)/shard_map/pallas_call | solution.py:40
  2.6 4.1 %collective-permute-start = (bf16[192,512]{1,0:T(8,128)(2,1)S(1)}, bf16[192,512]{1,0:T(8,128)(2,1)S(1)}, u32[]{:S(2)}, u32[]{:S(2)}) collective-permute-start(bf16[192,512]{1,0:T(8,128)(2,1)S(1)} %get-tuple-element.33), channel_id=1, source_target_pairs={{0,4},{2,6},{4,0},{6,2},{1,5},{3,7},{5,1},{7,3},{8,12},{10,14},{12... | collective-permute-start | bytes 589832 | tf_op jit(solution)/shard_map/ppermute | solution.py:310
  6.7 4.6 %shard_map.124 = (bf16[192,512]{1,0:T(8,128)(2,1)S(1)}, f32[192,512]{1,0:T(8,128)S(1)}, bf16[1024,2048]{1,0:T(8,128)(2,1)S(1)}, bf16[2048,1024]{1,0:T(8,128)(2,1...) custom-call(bf16[192,1024]{1,0:T(8,128)(2,1)S(1)} %get-tuple-element, ...), custom_call_target="tpu_custom_call", output_to_operand_aliasing={{4}: (3, {}), {5}: (4, {})} | custom-call | flops 1610612736 | bytes 17760256 | tf_op jit(solution)/shard_map/pallas_call | solution.py:40
  11.3 1.6 %collective-permute-start.1 = (bf16[192,512]{1,0:T(8,128)(2,1)S(1)}, bf16[192,512]{1,0:T(8,128)(2,1)S(1)}, u32[]{:S(2)}, u32[]{:S(2)}) collective-permute-start(bf16[192,512]{1,0:T(8,128)(2,1)S(1)} %get-tuple-element.32.refs_0_), channel_id=1, source_target_pairs={{0,1},{1,0},{2,3},{3,2},{4,5},{5,4},{6,7},{7,6},{8,9},{9,8},{10,11... | collective-permute-start | bytes 589832 | tf_op jit(solution)/shard_map/ppermute | solution.py:310
  12.9 1.6 %collective-permute-start.2 = (bf16[192,1024]{1,0:T(8,128)(2,1)S(1)}, bf16[192,1024]{1,0:T(8,128)(2,1)S(1)}, u32[]{:S(2)}, u32[]{:S(2)}) collective-permute-start(bf16[192,1024]{1,0:T(8,128)(2,1)S(1)} %get-tuple-element.37), channel_id=1, source_target_pairs={{0,2},{2,0},{4,6},{6,4},{1,3},{3,1},{5,7},{7,5},{8,10},{10,8},{12,... | collective-permute-start | bytes 1179656 | tf_op jit(solution)/shard_map/ppermute | solution.py:310
  14.4 0.2 collective-permute-start.8
  14.7 1.2 %collective-permute-done.refs_1_ = bf16[192,512]{1,0:T(8,128)(2,1)S(1)} collective-permute-done((bf16[192,512]{1,0:T(8,128)(2,1)S(1)}, bf16[192,512]{1,0:T(8,128)(2,1)S(1)}, u32[]{:S(2)}, u32[]{:S(2)}) %collective-permute-start) | collective-permute-done | bytes 196640 | tf_op jit(solution)/shard_map/ppermute | solution.py:310
  15.9 2.3 %collective-permute-start.3 = (bf16[192,512]{1,0:T(8,128)(2,1)S(1)}, bf16[192,512]{1,0:T(8,128)(2,1)S(1)}, u32[]{:S(2)}, u32[]{:S(2)}) collective-permute-start(bf16[192,512]{1,0:T(8,128)(2,1)S(1)} %shard_map.125.refs_4_.refs_0_), channel_id=1, source_target_pairs={{0,1},{1,0},{2,3},{3,2},{4,5},{5,4},{6,7},{7,6},{8,9},{9,8},{10,11... | collective-permute-start | bytes 589832 | tf_op jit(solution)/shard_map/ppermute | solution.py:310
  18.3 0.6 shard_map.126
  18.9 3.0 %collective-permute-done.3.refs_1_ = bf16[192,512]{1,0:T(8,128)(2,1)S(1)} collective-permute-done((bf16[192,512]{1,0:T(8,128)(2,1)S(1)}, bf16[192,512]{1,0:T(8,128)(2,1)S(1)}, u32[]{:S(2)}, u32[]{:S(2)}) %collective-permute-start.3) | collective-permute-done | bytes 196640 | tf_op jit(solution)/shard_map/ppermute | solution.py:310
  21.9 1.8 %shard_map.127 = (bf16[192,512]{1,0:T(8,128)(2,1)S(1)}, f32[192,512]{1,0:T(8,128)S(1)}) custom-call(bf16[192,512]{1,0:T(8,128)(2,1)S(1)} %shard_map.125.refs_4_.refs_0_, bf16[192,512]{1,0:T(8,128)(2,1)S(1)} %collective-permute-done.3.refs_1_, bf16[1024,2048]{1,0:T(8,128)(2,1)S(1)} %get-tuple-element.38.refs_2_.refs_1_, ...), custom_call_target="tpu_custom_call" | custom-call | flops 1610612736 | bytes 9371648 | tf_op jit(solution)/shard_map/pallas_call | solution.py:40
  23.8 2.0 %collective-permute-start.6 = (bf16[192,512]{1,0:T(8,128)(2,1)S(1)}, bf16[192,512]{1,0:T(8,128)(2,1)S(1)}, u32[]{:S(2)}, u32[]{:S(2)}) collective-permute-start(bf16[192,512]{1,0:T(8,128)(2,1)S(1)} %get-tuple-element.40.refs_3_), channel_id=1, source_target_pairs={{0,1},{1,0},{2,3},{3,2},{4,5},{5,4},{6,7},{7,6},{8,9},{9,8},{10,11... | collective-permute-start | bytes 589832 | tf_op jit(solution)/shard_map/ppermute | solution.py:310
  25.8 1.5 %collective-permute-done.8.refs_0_ = bf16[192,512]{1,0:T(8,128)(2,1)S(1)} collective-permute-done((bf16[192,512]{1,0:T(8,128)(2,1)S(1)}, bf16[192,512]{1,0:T(8,128)(2,1)S(1)}, u32[]{:S(2)}, u32[]{:S(2)}) %collective-permute-start.8) | collective-permute-done | bytes 196640 | tf_op jit(solution)/shard_map/ppermute | solution.py:310
  27.2 0.5 collective-permute-start.9
  27.8 0.7 collective-permute-done.2.refs_0_
  28.4 1.8 %shard_map.128 = (bf16[192,512]{1,0:T(8,128)(2,1)S(1)}, f32[192,512]{1,0:T(8,128)S(1)}) custom-call(bf16[192,1024]{1,0:T(8,128)(2,1)S(1)} %collective-permute-done.2.refs_0_, bf16[1024,2048]{1,0:T(8,128)(2,1)S(1)} %get-tuple-element.38.refs_2_.refs_1_, bf16[2048,1024]{1,0:T(8,128)(2,1)S(1)} %get-tuple-element.39.refs_3_.refs_2_, ...), custom_call_target="tpu_custom_call" | custom-call | flops 1610612736 | bytes 9371648 | tf_op jit(solution)/shard_map/pallas_call | solution.py:40
  30.2 1.6 %collective-permute-start.4 = (bf16[192,512]{1,0:T(8,128)(2,1)S(1)}, bf16[192,512]{1,0:T(8,128)(2,1)S(1)}, u32[]{:S(2)}, u32[]{:S(2)}) collective-permute-start(bf16[192,512]{1,0:T(8,128)(2,1)S(1)} %get-tuple-element.42.refs_4_), channel_id=1, source_target_pairs={{0,1},{1,0},{2,3},{3,2},{4,5},{5,4},{6,7},{7,6},{8,9},{9,8},{10,11... | collective-permute-start | bytes 589832 | tf_op jit(solution)/shard_map/ppermute | solution.py:310
  31.9 1.5 %collective-permute-start.7 = (bf16[192,512]{1,0:T(8,128)(2,1)S(1)}, bf16[192,512]{1,0:T(8,128)(2,1)S(1)}, u32[]{:S(2)}, u32[]{:S(2)}) collective-permute-start(bf16[192,512]{1,0:T(8,128)(2,1)S(1)} %shard_map.129.refs_5_), channel_id=1, source_target_pairs={{0,4},{2,6},{4,0},{6,2},{1,5},{3,7},{5,1},{7,3},{8,12},{10,14},{12... | collective-permute-start | bytes 589832 | tf_op jit(solution)/shard_map/ppermute | solution.py:310
  33.4 1.3 %collective-permute-done.9.refs_1_ = bf16[192,512]{1,0:T(8,128)(2,1)S(1)} collective-permute-done((bf16[192,512]{1,0:T(8,128)(2,1)S(1)}, bf16[192,512]{1,0:T(8,128)(2,1)S(1)}, u32[]{:S(2)}, u32[]{:S(2)}) %collective-permute-start.9) | collective-permute-done | bytes 196640 | tf_op jit(solution)/shard_map/ppermute | solution.py:310
  34.7 1.8 %shard_map.130 = (bf16[192,512]{1,0:T(8,128)(2,1)S(1)}, f32[192,512]{1,0:T(8,128)S(1)}) custom-call(bf16[192,512]{1,0:T(8,128)(2,1)S(1)} %collective-permute-done.8.refs_0_, bf16[192,512]{1,0:T(8,128)(2,1)S(1)} %collective-permute-done.9.refs_1_, bf16[1024,2048]{1,0:T(8,128)(2,1)S(1)} %get-tuple-element.38.refs_2_.refs_1_, ...), custom_call_target="tpu_custom_call" | custom-call | flops 1610612736 | bytes 9371648 | tf_op jit(solution)/shard_map/pallas_call | solution.py:40
  36.6 1.4 %collective-permute-start.10 = (bf16[192,512]{1,0:T(8,128)(2,1)S(1)}, bf16[192,512]{1,0:T(8,128)(2,1)S(1)}, u32[]{:S(2)}, u32[]{:S(2)}) collective-permute-start(bf16[192,512]{1,0:T(8,128)(2,1)S(1)} %get-tuple-element.46), channel_id=1, source_target_pairs={{0,1},{1,0},{2,3},{3,2},{4,5},{5,4},{6,7},{7,6},{8,9},{9,8},{10,11... | collective-permute-start | bytes 589832 | tf_op jit(solution)/shard_map/ppermute | solution.py:310
  38.0 0.5 collective-permute-done.4
  38.5 2.5 %collective-permute-start.5 = (bf16[192,512]{1,0:T(8,128)(2,1)S(1)}, bf16[192,512]{1,0:T(8,128)(2,1)S(1)}, u32[]{:S(2)}, u32[]{:S(2)}) collective-permute-start(bf16[192,512]{1,0:T(8,128)(2,1)S(1)} %add_convert_fusion), channel_id=1, source_target_pairs={{0,2},{2,0},{4,6},{6,4},{1,3},{3,1},{5,7},{7,5},{8,10},{10,8},{12,... | collective-permute-start | bytes 589832 | tf_op jit(solution)/shard_map/ppermute | solution.py:310
  41.0 1.3 %collective-permute-done.10.refs_1_ = bf16[192,512]{1,0:T(8,128)(2,1)S(1)} collective-permute-done((bf16[192,512]{1,0:T(8,128)(2,1)S(1)}, bf16[192,512]{1,0:T(8,128)(2,1)S(1)}, u32[]{:S(2)}, u32[]{:S(2)}) %collective-permute-start.10) | collective-permute-done | bytes 196640 | tf_op jit(solution)/shard_map/ppermute | solution.py:310
  42.3 5.1 %collective-permute-start.11 = (bf16[192,512]{1,0:T(8,128)(2,1)S(1)}, bf16[192,512]{1,0:T(8,128)(2,1)S(1)}, u32[]{:S(2)}, u32[]{:S(2)}) collective-permute-start(bf16[192,512]{1,0:T(8,128)(2,1)S(1)} %shard_map.131), channel_id=1, source_target_pairs={{0,6},{2,4},{4,2},{6,0},{1,7},{3,5},{5,3},{7,1},{8,14},{10,12},{12... | collective-permute-start | bytes 589832 | tf_op jit(solution)/shard_map/ppermute | solution.py:310
  47.5 1.6 %collective-permute-done.5.refs_4_ = bf16[192,512]{1,0:T(8,128)(2,1)S(1)} collective-permute-done((bf16[192,512]{1,0:T(8,128)(2,1)S(1)}, bf16[192,512]{1,0:T(8,128)(2,1)S(1)}, u32[]{:S(2)}, u32[]{:S(2)}) %collective-permute-start.5) | collective-permute-done | bytes 196640 | tf_op jit(solution)/shard_map/ppermute | solution.py:310
  49.1 2.8 %collective-permute-done.11.refs_6_ = bf16[192,512]{1,0:T(8,128)(2,1)S(1)} collective-permute-done((bf16[192,512]{1,0:T(8,128)(2,1)S(1)}, bf16[192,512]{1,0:T(8,128)(2,1)S(1)}, u32[]{:S(2)}, u32[]{:S(2)}) %collective-permute-start.11) | collective-permute-done | bytes 196640 | tf_op jit(solution)/shard_map/ppermute | solution.py:310
  51.9 0.7 shard_map.132.refs_0_.refs_2_
  52.6 1.9 %collective-permute-start.13 = (bf16[256,512]{1,0:T(8,128)(2,1)S(1)}, bf16[256,512]{1,0:T(8,128)(2,1)S(1)}, u32[]{:S(2)}, u32[]{:S(2)}) collective-permute-start(bf16[256,512]{1,0:T(8,128)(2,1)S(1)} %shard_map.132.refs_0_.refs_2_), channel_id=1, source_target_pairs={{0,8},{8,0},{16,16},{24,24},{1,9},{9,1},{17,17},{25,25},{2,10},{10... | collective-permute-start | bytes 786440 | tf_op jit(solution)/shard_map/ppermute | solution.py:437
  54.5 1.6 %collective-permute-start.12 = (bf16[256,512]{1,0:T(8,128)(2,1)S(1)}, bf16[256,512]{1,0:T(8,128)(2,1)S(1)}, u32[]{:S(2)}, u32[]{:S(2)}) collective-permute-start(bf16[256,512]{1,0:T(8,128)(2,1)S(1)} %shard_map.132.refs_0_.refs_2_), channel_id=1, source_target_pairs={{0,1},{1,0},{2,3},{3,2},{4,5},{5,4},{6,7},{7,6},{8,9},{9,8},{10,11... | collective-permute-start | bytes 786440 | tf_op jit(solution)/shard_map/ppermute | solution.py:310
  56.2 0.3 collective-permute-start.14
  56.5 6.9 %collective-permute-done.12.refs_0_.refs_1_ = bf16[256,512]{1,0:T(8,128)(2,1)S(1)} collective-permute-done((bf16[256,512]{1,0:T(8,128)(2,1)S(1)}, bf16[256,512]{1,0:T(8,128)(2,1)S(1)}, u32[]{:S(2)}, u32[]{:S(2)}) %collective-permute-start.12) | collective-permute-done | bytes 262176 | tf_op jit(solution)/shard_map/ppermute | solution.py:310
  63.3 1.3 %collective-permute-done.14.refs_1_ = bf16[256,512]{1,0:T(8,128)(2,1)S(1)} collective-permute-done((bf16[256,512]{1,0:T(8,128)(2,1)S(1)}, bf16[256,512]{1,0:T(8,128)(2,1)S(1)}, u32[]{:S(2)}, u32[]{:S(2)}) %collective-permute-start.14) | collective-permute-done | bytes 262176 | tf_op jit(solution)/shard_map/ppermute | solution.py:446
  64.7 0.1 collective-permute-start.15
  64.8 0.7 shard_map.135.refs_2_
  65.5 0.8 %collective-permute-done.15.refs_1_ = bf16[256,512]{1,0:T(8,128)(2,1)S(1)} collective-permute-done((bf16[256,512]{1,0:T(8,128)(2,1)S(1)}, bf16[256,512]{1,0:T(8,128)(2,1)S(1)}, u32[]{:S(2)}, u32[]{:S(2)}) %collective-permute-start.15) | collective-permute-done | bytes 262176 | tf_op jit(solution)/shard_map/ppermute | solution.py:310
  66.3 2.0 %collective-permute-start.16 = (bf16[256,512]{1,0:T(8,128)(2,1)S(1)}, bf16[256,512]{1,0:T(8,128)(2,1)S(1)}, u32[]{:S(2)}, u32[]{:S(2)}) collective-permute-start(bf16[256,512]{1,0:T(8,128)(2,1)S(1)} %get-tuple-element.51), channel_id=1, source_target_pairs={{0,8},{8,0},{16,24},{24,16},{1,9},{9,1},{17,25},{25,17},{2,10},{10... | collective-permute-start | bytes 786440 | tf_op jit(solution)/shard_map/ppermute | solution.py:310
  68.3 1.2 %collective-permute-done.16.refs_1_ = bf16[256,512]{1,0:T(8,128)(2,1)S(1)} collective-permute-done((bf16[256,512]{1,0:T(8,128)(2,1)S(1)}, bf16[256,512]{1,0:T(8,128)(2,1)S(1)}, u32[]{:S(2)}, u32[]{:S(2)}) %collective-permute-start.16) | collective-permute-done | bytes 262176 | tf_op jit(solution)/shard_map/ppermute | solution.py:310
  69.5 0.1 shard_map.138
  69.6 1.4 %collective-permute-start.17 = (bf16[256,128]{1,0:T(8,128)(2,1)S(1)}, bf16[256,128]{1,0:T(8,128)(2,1)S(1)}, u32[]{:S(2)}, u32[]{:S(2)}) collective-permute-start(bf16[256,128]{1,0:T(8,128)(2,1)S(1)} %get-tuple-element.53), channel_id=1, source_target_pairs={{0,1},{1,0},{8,9},{9,8},{16,17},{17,16},{24,25},{25,24},{2,3},{3,2... | collective-permute-start | bytes 196616 | tf_op jit(solution)/shard_map/ppermute | solution.py:493
  71.0 0.5 collective-permute-start.18
  71.5 1.6 %collective-permute-start.19 = (bf16[256,128]{1,0:T(8,128)(2,1)S(1)}, bf16[256,128]{1,0:T(8,128)(2,1)S(1)}, u32[]{:S(2)}, u32[]{:S(2)}) collective-permute-start(bf16[256,128]{1,0:T(8,128)(2,1)S(1)} %get-tuple-element.55), channel_id=1, source_target_pairs={{0,17},{1,16},{8,25},{9,24},{16,1},{17,0},{24,9},{25,8},{2,19},{3,... | collective-permute-start | bytes 196616 | tf_op jit(solution)/shard_map/ppermute | solution.py:493
  73.2 0.7 shard_map.137
  73.9 0.1 collective-permute-done.17
  74.1 1.8 %collective-permute-done.18 = bf16[256,128]{1,0:T(8,128)(2,1)S(1)} collective-permute-done((bf16[256,128]{1,0:T(8,128)(2,1)S(1)}, bf16[256,128]{1,0:T(8,128)(2,1)S(1)}, u32[]{:S(2)}, u32[]{:S(2)}) %collective-permute-start.18) | collective-permute-done | bytes 65568 | tf_op jit(solution)/shard_map/ppermute | solution.py:493
  75.8 0.9 %collective-permute-done.19 = bf16[256,128]{1,0:T(8,128)(2,1)S(1)} collective-permute-done((bf16[256,128]{1,0:T(8,128)(2,1)S(1)}, bf16[256,128]{1,0:T(8,128)(2,1)S(1)}, u32[]{:S(2)}, u32[]{:S(2)}) %collective-permute-start.19) | collective-permute-done | bytes 65568 | tf_op jit(solution)/shard_map/ppermute | solution.py:493
  76.7 0.7 add_convert_fusion.2
  (30 shorter events, 0.3 us)
Async XLA Ops:
  0.6 1.0 %copy-start.1 = (bf16[1,256,1024]{2,1,0:T(8,128)(2,1)S(1)}, bf16[1,256,1024]{2,1,0:T(8,128)(2,1)}, u32[]{:S(2)}) copy-start(bf16[1,256,1024]{2,1,0:T(8,128)(2,1)} %param.11) | copy-start | bytes 1572868
  0.6 1.0 %copy-start.4 = (s32[1,256,2]{1,2,0:T(2,128)S(1)}, s32[1,256,2]{1,2,0:T(2,128)}, u32[]{:S(2)}) copy-start(s32[1,256,2]{1,2,0:T(2,128)} %param.12) | copy-start | bytes 6148
  0.6 1.0 %copy-start.8 = (f32[1,1024]{1,0:T(1,128)S(1)}, f32[1,1024]{1,0:T(1,128)}, u32[]{:S(2)}) copy-start(f32[1,1024]{1,0:T(1,128)} %refs_2_.2) | copy-start | bytes 12292
  2.6 13.3 %collective-permute-start = (bf16[192,512]{1,0:T(8,128)(2,1)S(1)}, bf16[192,512]{1,0:T(8,128)(2,1)S(1)}, u32[]{:S(2)}, u32[]{:S(2)}) collective-permute-start(bf16[192,512]{1,0:T(8,128)(2,1)S(1)} %get-tuple-element.33), channel_id=1, source_target_pairs={{0,4},{2,6},{4,0},{6,2},{1,5},{3,7},{5,1},{7,3},{8,12},{10,14},{12... | collective-permute-start | bytes 589832 | tf_op jit(solution)/shard_map/ppermute | solution.py:310
  6.7 11.6 %copy-start.2 = (bf16[1,256,512]{2,1,0:T(8,128)(2,1)S(1)}, bf16[1,256,512]{2,1,0:T(8,128)(2,1)}, u32[]{:S(2)}) copy-start(bf16[1,256,512]{2,1,0:T(8,128)(2,1)} %param.21) | copy-start | bytes 786436
  6.7 11.6 %copy-start.5 = (f32[1,256,2]{1,2,0:T(2,128)S(1)}, f32[1,256,2]{1,2,0:T(2,128)}, u32[]{:S(2)}) copy-start(f32[1,256,2]{1,2,0:T(2,128)} %param.13) | copy-start | bytes 6148
  11.3 6.9 %collective-permute-start.1 = (bf16[192,512]{1,0:T(8,128)(2,1)S(1)}, bf16[192,512]{1,0:T(8,128)(2,1)S(1)}, u32[]{:S(2)}, u32[]{:S(2)}) collective-permute-start(bf16[192,512]{1,0:T(8,128)(2,1)S(1)} %get-tuple-element.32.refs_0_), channel_id=1, source_target_pairs={{0,1},{1,0},{2,3},{3,2},{4,5},{5,4},{6,7},{7,6},{8,9},{9,8},{10,11... | collective-permute-start | bytes 589832 | tf_op jit(solution)/shard_map/ppermute | solution.py:310
  12.9 15.6 %collective-permute-start.2 = (bf16[192,1024]{1,0:T(8,128)(2,1)S(1)}, bf16[192,1024]{1,0:T(8,128)(2,1)S(1)}, u32[]{:S(2)}, u32[]{:S(2)}) collective-permute-start(bf16[192,1024]{1,0:T(8,128)(2,1)S(1)} %get-tuple-element.37), channel_id=1, source_target_pairs={{0,2},{2,0},{4,6},{6,4},{1,3},{3,1},{5,7},{7,5},{8,10},{10,8},{12,... | collective-permute-start | bytes 1179656 | tf_op jit(solution)/shard_map/ppermute | solution.py:310
  14.4 12.8 %collective-permute-start.8 = (bf16[192,512]{1,0:T(8,128)(2,1)S(1)}, bf16[192,512]{1,0:T(8,128)(2,1)S(1)}, u32[]{:S(2)}, u32[]{:S(2)}) collective-permute-start(bf16[192,512]{1,0:T(8,128)(2,1)S(1)} %get-tuple-element.44), channel_id=1, source_target_pairs={{0,6},{2,4},{4,2},{6,0},{1,7},{3,5},{5,3},{7,1},{8,14},{10,12},{12... | collective-permute-start | bytes 589832 | tf_op jit(solution)/shard_map/ppermute | solution.py:310
  15.9 6.0 %collective-permute-start.3 = (bf16[192,512]{1,0:T(8,128)(2,1)S(1)}, bf16[192,512]{1,0:T(8,128)(2,1)S(1)}, u32[]{:S(2)}, u32[]{:S(2)}) collective-permute-start(bf16[192,512]{1,0:T(8,128)(2,1)S(1)} %shard_map.125.refs_4_.refs_0_), channel_id=1, source_target_pairs={{0,1},{1,0},{2,3},{3,2},{4,5},{5,4},{6,7},{7,6},{8,9},{9,8},{10,11... | collective-permute-start | bytes 589832 | tf_op jit(solution)/shard_map/ppermute | solution.py:310
  23.8 8.1 %collective-permute-start.6 = (bf16[192,512]{1,0:T(8,128)(2,1)S(1)}, bf16[192,512]{1,0:T(8,128)(2,1)S(1)}, u32[]{:S(2)}, u32[]{:S(2)}) collective-permute-start(bf16[192,512]{1,0:T(8,128)(2,1)S(1)} %get-tuple-element.40.refs_3_), channel_id=1, source_target_pairs={{0,1},{1,0},{2,3},{3,2},{4,5},{5,4},{6,7},{7,6},{8,9},{9,8},{10,11... | collective-permute-start | bytes 589832 | tf_op jit(solution)/shard_map/ppermute | solution.py:310
  27.2 7.5 %collective-permute-start.9 = (bf16[192,512]{1,0:T(8,128)(2,1)S(1)}, bf16[192,512]{1,0:T(8,128)(2,1)S(1)}, u32[]{:S(2)}, u32[]{:S(2)}) collective-permute-start(bf16[192,512]{1,0:T(8,128)(2,1)S(1)} %collective-permute-done.8.refs_0_), channel_id=1, source_target_pairs={{0,1},{1,0},{2,3},{3,2},{4,5},{5,4},{6,7},{7,6},{8,9},{9,8},{10,11... | collective-permute-start | bytes 589832 | tf_op jit(solution)/shard_map/ppermute | solution.py:310
  30.2 8.2 %collective-permute-start.4 = (bf16[192,512]{1,0:T(8,128)(2,1)S(1)}, bf16[192,512]{1,0:T(8,128)(2,1)S(1)}, u32[]{:S(2)}, u32[]{:S(2)}) collective-permute-start(bf16[192,512]{1,0:T(8,128)(2,1)S(1)} %get-tuple-element.42.refs_4_), channel_id=1, source_target_pairs={{0,1},{1,0},{2,3},{3,2},{4,5},{5,4},{6,7},{7,6},{8,9},{9,8},{10,11... | collective-permute-start | bytes 589832 | tf_op jit(solution)/shard_map/ppermute | solution.py:310
  31.9 15.6 %collective-permute-start.7 = (bf16[192,512]{1,0:T(8,128)(2,1)S(1)}, bf16[192,512]{1,0:T(8,128)(2,1)S(1)}, u32[]{:S(2)}, u32[]{:S(2)}) collective-permute-start(bf16[192,512]{1,0:T(8,128)(2,1)S(1)} %shard_map.129.refs_5_), channel_id=1, source_target_pairs={{0,4},{2,6},{4,0},{6,2},{1,5},{3,7},{5,1},{7,3},{8,12},{10,14},{12... | collective-permute-start | bytes 589832 | tf_op jit(solution)/shard_map/ppermute | solution.py:310
  36.5 28.2 %copy-start = (bf16[1,1024,512]{2,1,0:T(8,128)(2,1)S(1)}, bf16[1,1024,512]{2,1,0:T(8,128)(2,1)}, u32[]{:S(2)}) copy-start(bf16[1,1024,512]{2,1,0:T(8,128)(2,1)} %param.18) | copy-start | bytes 3145732
  36.5 28.2 %copy-start.3 = (f32[1,1024]{1,0:T(1,128)S(1)}, f32[1,1024]{1,0:T(1,128)}, u32[]{:S(2)}) copy-start(f32[1,1024]{1,0:T(1,128)} %refs_2_.3) | copy-start | bytes 12292
  36.5 29.7 %copy-start.6 = (bf16[1,1024,512]{2,1,0:T(8,128)(2,1)S(1)}, bf16[1,1024,512]{2,1,0:T(8,128)(2,1)}, u32[]{:S(2)}) copy-start(bf16[1,1024,512]{2,1,0:T(8,128)(2,1)} %param.19) | copy-start | bytes 3145732
  36.6 29.7 %copy-start.7 = (bf16[1,1024,512]{2,1,0:T(8,128)(2,1)S(1)}, bf16[1,1024,512]{2,1,0:T(8,128)(2,1)}, u32[]{:S(2)}) copy-start(bf16[1,1024,512]{2,1,0:T(8,128)(2,1)} %param.20) | copy-start | bytes 3145732
  36.6 5.7 %collective-permute-start.10 = (bf16[192,512]{1,0:T(8,128)(2,1)S(1)}, bf16[192,512]{1,0:T(8,128)(2,1)S(1)}, u32[]{:S(2)}, u32[]{:S(2)}) collective-permute-start(bf16[192,512]{1,0:T(8,128)(2,1)S(1)} %get-tuple-element.46), channel_id=1, source_target_pairs={{0,1},{1,0},{2,3},{3,2},{4,5},{5,4},{6,7},{7,6},{8,9},{9,8},{10,11... | collective-permute-start | bytes 589832 | tf_op jit(solution)/shard_map/ppermute | solution.py:310
  38.5 10.6 %collective-permute-start.5 = (bf16[192,512]{1,0:T(8,128)(2,1)S(1)}, bf16[192,512]{1,0:T(8,128)(2,1)S(1)}, u32[]{:S(2)}, u32[]{:S(2)}) collective-permute-start(bf16[192,512]{1,0:T(8,128)(2,1)S(1)} %add_convert_fusion), channel_id=1, source_target_pairs={{0,2},{2,0},{4,6},{6,4},{1,3},{3,1},{5,7},{7,5},{8,10},{10,8},{12,... | collective-permute-start | bytes 589832 | tf_op jit(solution)/shard_map/ppermute | solution.py:310
  42.3 9.6 %collective-permute-start.11 = (bf16[192,512]{1,0:T(8,128)(2,1)S(1)}, bf16[192,512]{1,0:T(8,128)(2,1)S(1)}, u32[]{:S(2)}, u32[]{:S(2)}) collective-permute-start(bf16[192,512]{1,0:T(8,128)(2,1)S(1)} %shard_map.131), channel_id=1, source_target_pairs={{0,6},{2,4},{4,2},{6,0},{1,7},{3,5},{5,3},{7,1},{8,14},{10,12},{12... | collective-permute-start | bytes 589832 | tf_op jit(solution)/shard_map/ppermute | solution.py:310
  52.6 3.5 %collective-permute-start.13 = (bf16[256,512]{1,0:T(8,128)(2,1)S(1)}, bf16[256,512]{1,0:T(8,128)(2,1)S(1)}, u32[]{:S(2)}, u32[]{:S(2)}) collective-permute-start(bf16[256,512]{1,0:T(8,128)(2,1)S(1)} %shard_map.132.refs_0_.refs_2_), channel_id=1, source_target_pairs={{0,8},{8,0},{16,16},{24,24},{1,9},{9,1},{17,17},{25,25},{2,10},{10... | collective-permute-start | bytes 786440 | tf_op jit(solution)/shard_map/ppermute | solution.py:437
  54.5 8.8 %collective-permute-start.12 = (bf16[256,512]{1,0:T(8,128)(2,1)S(1)}, bf16[256,512]{1,0:T(8,128)(2,1)S(1)}, u32[]{:S(2)}, u32[]{:S(2)}) collective-permute-start(bf16[256,512]{1,0:T(8,128)(2,1)S(1)} %shard_map.132.refs_0_.refs_2_), channel_id=1, source_target_pairs={{0,1},{1,0},{2,3},{3,2},{4,5},{5,4},{6,7},{7,6},{8,9},{9,8},{10,11... | collective-permute-start | bytes 786440 | tf_op jit(solution)/shard_map/ppermute | solution.py:310
  56.2 8.5 %collective-permute-start.14 = (bf16[256,512]{1,0:T(8,128)(2,1)S(1)}, bf16[256,512]{1,0:T(8,128)(2,1)S(1)}, u32[]{:S(2)}, u32[]{:S(2)}) collective-permute-start(bf16[256,512]{1,0:T(8,128)(2,1)S(1)} %shard_map.133), channel_id=1, source_target_pairs={{0,16},{1,17},{8,25},{9,24},{16,0},{17,1},{24,8},{25,9},{2,18},{3,... | collective-permute-start | bytes 786440 | tf_op jit(solution)/shard_map/ppermute | solution.py:446
  64.7 1.6 %collective-permute-start.15 = (bf16[256,512]{1,0:T(8,128)(2,1)S(1)}, bf16[256,512]{1,0:T(8,128)(2,1)S(1)}, u32[]{:S(2)}, u32[]{:S(2)}) collective-permute-start(bf16[256,512]{1,0:T(8,128)(2,1)S(1)} %shard_map.134.refs_0_), channel_id=1, source_target_pairs={{0,8},{8,0},{16,24},{24,16},{1,9},{9,1},{17,25},{25,17},{2,10},{10... | collective-permute-start | bytes 786440 | tf_op jit(solution)/shard_map/ppermute | solution.py:310
  66.3 3.2 %collective-permute-start.16 = (bf16[256,512]{1,0:T(8,128)(2,1)S(1)}, bf16[256,512]{1,0:T(8,128)(2,1)S(1)}, u32[]{:S(2)}, u32[]{:S(2)}) collective-permute-start(bf16[256,512]{1,0:T(8,128)(2,1)S(1)} %get-tuple-element.51), channel_id=1, source_target_pairs={{0,8},{8,0},{16,24},{24,16},{1,9},{9,1},{17,25},{25,17},{2,10},{10... | collective-permute-start | bytes 786440 | tf_op jit(solution)/shard_map/ppermute | solution.py:310
  69.6 4.4 %collective-permute-start.17 = (bf16[256,128]{1,0:T(8,128)(2,1)S(1)}, bf16[256,128]{1,0:T(8,128)(2,1)S(1)}, u32[]{:S(2)}, u32[]{:S(2)}) collective-permute-start(bf16[256,128]{1,0:T(8,128)(2,1)S(1)} %get-tuple-element.53), channel_id=1, source_target_pairs={{0,1},{1,0},{8,9},{9,8},{16,17},{17,16},{24,25},{25,24},{2,3},{3,2... | collective-permute-start | bytes 196616 | tf_op jit(solution)/shard_map/ppermute | solution.py:493
  71.0 4.8 %collective-permute-start.18 = (bf16[256,128]{1,0:T(8,128)(2,1)S(1)}, bf16[256,128]{1,0:T(8,128)(2,1)S(1)}, u32[]{:S(2)}, u32[]{:S(2)}) collective-permute-start(bf16[256,128]{1,0:T(8,128)(2,1)S(1)} %get-tuple-element.54), channel_id=1, source_target_pairs={{0,16},{1,17},{8,24},{9,25},{16,0},{17,1},{24,8},{25,9},{2,18},{3,... | collective-permute-start | bytes 196616 | tf_op jit(solution)/shard_map/ppermute | solution.py:493
  71.5 5.2 %collective-permute-start.19 = (bf16[256,128]{1,0:T(8,128)(2,1)S(1)}, bf16[256,128]{1,0:T(8,128)(2,1)S(1)}, u32[]{:S(2)}, u32[]{:S(2)}) collective-permute-start(bf16[256,128]{1,0:T(8,128)(2,1)S(1)} %get-tuple-element.55), channel_id=1, source_target_pairs={{0,17},{1,16},{8,25},{9,24},{16,1},{17,0},{24,9},{25,8},{2,19},{3,... | collective-permute-start | bytes 196616 | tf_op jit(solution)/shard_map/ppermute | solution.py:493

commit v12 on v11

--- a/solution.py
+++ b/solution.py
@@ -195,32 +195,14 @@
     out[...] = value.astype(LOW)
 
 
-def encoder_part(own, beside, out):
+def choose(own, beside, *refs):
     sec = lax.axis_index("sec")
-
-    @pl.when(sec == 1)
-    def _():
-        out[...] = beside[...]
-
-    @pl.when(sec != 1)
-    def _():
-        out[...] = own[...]
-
-
-def choose(own, moved, beside, out):
-    sec = lax.axis_index("sec")
-
-    @pl.when(sec == 0)
-    def _():
-        out[...] = own[...]
-
-    @pl.when(sec == 1)
-    def _():
-        out[...] = beside[...]
-
-    @pl.when(sec >= 2)
-    def _():
-        out[...] = moved[...]
+    moved, out = refs[:-1], refs[-1]
+    for i, source in enumerate((own, beside, *moved)):
+
+        @pl.when(sec == i)
+        def _():
+            out[...] = source[...]
 
 
 def attend(
@@ -434,18 +416,19 @@
         flops=4 * 3 * token_count * token_count * half,
     )[0]
 
-    beside = lax.ppermute(hidden_half, "sec", [(0, 1), (1, 0)] + [(i, i) for i in range(2, sections)])
     hidden_other = swap(hidden_half, "tp", 1)
-    encoder_half = call(encoder_part, [shape_of(hidden_half.shape)], [hidden_half, beside])[0]
-    moved = hidden_half
-    for i in range(1, sections // 2):
-        targets = {j: j for j in range(sections * tp_size)}
-        for t in range(tp_size):
-            even, odd = 2 * i * tp_size + t, (2 * i + 1) * tp_size + (t ^ 1)
-            targets |= {t: even, even: t, tp_size + t: odd, odd: tp_size + (t ^ 1)}
-        arrived = lax.ppermute(encoder_half, ("sec", "tp"), list(targets.items()))
-        moved = arrived if sections == 4 else jnp.where(sec // 2 == i, arrived, moved)
-    first = call(choose, [shape_of(hidden_half.shape)], [hidden_other, moved, beside])[0]
+
+    def cycle(order, crossed):
+        pairs = [(i, i ^ 1) for i in range(sections * tp_size)]
+        targets = dict(pairs)
+        for a, b in zip(order, order[1:] + order[:1]):
+            for t in range(tp_size):
+                targets[a * tp_size + t] = b * tp_size + (t ^ crossed if a == 0 else t)
+        return lax.ppermute(hidden_half, ("sec", "tp"), list(targets.items()))
+
+    moved = [[cycle([0, 2 * i, 2 * i + 1, 1], 0), cycle([0, 2 * i + 1, 2 * i, 1], 1)] for i in range(1, sections // 2)]
+    beside = swap(hidden_half, "sec", 1)
+    first = call(choose, [shape_of(hidden_half.shape)], [hidden_other, beside, *sum(moved, [])])[0]
     second = swap(first, "sec", 1)
 
     local_width = query_weight.shape[2]

time: 77.6 us -> 77.1 us (level)
    ppermute x15 -> x16, waiting for transfers between devices: 22.8 us -> 18.7 us  [swap(): return lax.ppermute(block, axis, [(i, i ^ step) for i in range(size)])]
    ppermute x2, waiting for transfers between devices: 1.33 us -> 3.35 us  [cycle(): return lax.ppermute(hidden_half, ('sec', 'tp'), list(targets.items()))]
    ppermute x3, waiting for transfers between devices: 2.82 us -> 4.37 us  [shards(): total = total + lax.ppermute(blocks[k], ('sec', 'tp'), pairs).astype(WIDE)]
    ppermute x15 -> x16, starting transfers between devices: 28.1 us -> 28.7 us  [swap(): return lax.ppermute(block, axis, [(i, i ^ step) for i in range(size)])]
    pallas_call x17 -> x16, Pallas kernels: 13.9 us -> 13.9 us  [call(): pl.pallas_call(run, out_shape=[*out_shape, *(shape_of(x.shape, x.dtype) f...]
  transfers between devices with their start and end apart: 20 -> 21, of which waited for: 16 -> 17; matrix products, arithmetic and copies ran while one was open for 0% -> 0% of each run, Pallas kernels for 16% -> 16%
where the time goes in v12:
time: 77.1 us; the launch traced here: 76.9 us
  starting transfers between devices  34 us (44%)
  waiting for transfers between devices  26.4 us (34%)
  Pallas kernels  13.9 us (18%)
  local copies, waits for them, and re-layouts  1.03 us (1%)
  between operations  0.82 us (1%)
    ppermute x16, starting transfers between devices, swap(): return lax.ppermute(block, axis, [(i, i ^ step) for i in range(size)])  28.7 us
    ppermute x16, waiting for transfers between devices, swap(): return lax.ppermute(block, axis, [(i, i ^ step) for i in range(size)])  18.7 us
    pallas_call x16, Pallas kernels, call(): pl.pallas_call(run, out_shape=[*out_shape, *(shape_of(x.shape, x.dtype) f...  13.9 us
    ppermute x3, waiting for transfers between devices, shards(): total = total + lax.ppermute(blocks[k], ('sec', 'tp'), pairs).astype(WIDE)  4.37 us
    ppermute x3, starting transfers between devices, shards(): total = total + lax.ppermute(blocks[k], ('sec', 'tp'), pairs).astype(WIDE)  3.57 us
    ppermute x2, waiting for transfers between devices, cycle(): return lax.ppermute(hidden_half, ('sec', 'tp'), list(targets.items()))  3.35 us
    ppermute x2, starting transfers between devices, cycle(): return lax.ppermute(hidden_half, ('sec', 'tp'), list(targets.items()))  1.79 us
  transfers between devices with their start and end apart: 21, of which 17 were waited for; matrix products, arithmetic and copies ran while one was open for 0% of the time, Pallas kernels for 16%

profile of v12, /device:TPU:0, one launch (start us, length us, event | category | flops | bytes accessed | tf_op | source)
XLA Modules:
  0.0 76.9 jit_solution(1129327223858426454)
XLA Ops:
  0.7 1.0 %copy-done.1 = bf16[1,256,1024]{2,1,0:T(8,128)(2,1)S(1)} copy-done((bf16[1,256,1024]{2,1,0:T(8,128)(2,1)S(1)}, bf16[1,256,1024]{2,1,0:T(8,128)(2,1)}, u32[]{:S(2)}) %copy-start.1) | copy-done | bytes 524312
  1.7 0.9 %shard_map.123 = (bf16[192,512]{1,0:T(8,128)(2,1)S(1)}, bf16[192,512]{1,0:T(8,128)(2,1)S(1)}, bf16[192,1024]{1,0:T(8,128)(2,1)S(1)}, bf16[192,1024]{1,0:T(8,128)(2,1)S(1)}) custom-call(bf16[256,1024]{1,0:T(8,128)(2,1)S(1)} %bitcast.15, s32[2,256]{1,0:T(2,128)S(1)} %bitcast.18, f32[1,1024]{1,0:T(1,128)S(1)} %copy-done.8, ...), custom_call_target="tpu_custom_call" | custom-call | flops 402653184 | bytes 1841152 | tf_op jit(solution)/shard_map/pallas_call | solution.py:40
  2.6 4.1 %collective-permute-start = (bf16[192,512]{1,0:T(8,128)(2,1)S(1)}, bf16[192,512]{1,0:T(8,128)(2,1)S(1)}, u32[]{:S(2)}, u32[]{:S(2)}) collective-permute-start(bf16[192,512]{1,0:T(8,128)(2,1)S(1)} %get-tuple-element.33), channel_id=1, source_target_pairs={{0,4},{2,6},{4,0},{6,2},{1,5},{3,7},{5,1},{7,3},{8,12},{10,14},{12... | collective-permute-start | bytes 589832 | tf_op jit(solution)/shard_map/ppermute | solution.py:292
  6.7 4.6 %shard_map.124 = (bf16[192,512]{1,0:T(8,128)(2,1)S(1)}, f32[192,512]{1,0:T(8,128)S(1)}, bf16[1024,2048]{1,0:T(8,128)(2,1)S(1)}, bf16[2048,1024]{1,0:T(8,128)(2,1...) custom-call(bf16[192,1024]{1,0:T(8,128)(2,1)S(1)} %get-tuple-element, ...), custom_call_target="tpu_custom_call", output_to_operand_aliasing={{4}: (3, {}), {5}: (4, {})} | custom-call | flops 1610612736 | bytes 17760256 | tf_op jit(solution)/shard_map/pallas_call | solution.py:40
  11.3 1.6 %collective-permute-start.1 = (bf16[192,512]{1,0:T(8,128)(2,1)S(1)}, bf16[192,512]{1,0:T(8,128)(2,1)S(1)}, u32[]{:S(2)}, u32[]{:S(2)}) collective-permute-start(bf16[192,512]{1,0:T(8,128)(2,1)S(1)} %get-tuple-element.32.refs_0_), channel_id=1, source_target_pairs={{0,1},{1,0},{2,3},{3,2},{4,5},{5,4},{6,7},{7,6},{8,9},{9,8},{10,11... | collective-permute-start | bytes 589832 | tf_op jit(solution)/shard_map/ppermute | solution.py:292
  12.9 1.6 %collective-permute-start.2 = (bf16[192,1024]{1,0:T(8,128)(2,1)S(1)}, bf16[192,1024]{1,0:T(8,128)(2,1)S(1)}, u32[]{:S(2)}, u32[]{:S(2)}) collective-permute-start(bf16[192,1024]{1,0:T(8,128)(2,1)S(1)} %get-tuple-element.37), channel_id=1, source_target_pairs={{0,2},{2,0},{4,6},{6,4},{1,3},{3,1},{5,7},{7,5},{8,10},{10,8},{12,... | collective-permute-start | bytes 1179656 | tf_op jit(solution)/shard_map/ppermute | solution.py:292
  14.4 0.2 collective-permute-start.8
  14.7 1.2 %collective-permute-done.refs_1_ = bf16[192,512]{1,0:T(8,128)(2,1)S(1)} collective-permute-done((bf16[192,512]{1,0:T(8,128)(2,1)S(1)}, bf16[192,512]{1,0:T(8,128)(2,1)S(1)}, u32[]{:S(2)}, u32[]{:S(2)}) %collective-permute-start) | collective-permute-done | bytes 196640 | tf_op jit(solution)/shard_map/ppermute | solution.py:292
  15.9 2.3 %collective-permute-start.3 = (bf16[192,512]{1,0:T(8,128)(2,1)S(1)}, bf16[192,512]{1,0:T(8,128)(2,1)S(1)}, u32[]{:S(2)}, u32[]{:S(2)}) collective-permute-start(bf16[192,512]{1,0:T(8,128)(2,1)S(1)} %shard_map.125.refs_4_.refs_0_), channel_id=1, source_target_pairs={{0,1},{1,0},{2,3},{3,2},{4,5},{5,4},{6,7},{7,6},{8,9},{9,8},{10,11... | collective-permute-start | bytes 589832 | tf_op jit(solution)/shard_map/ppermute | solution.py:292
  18.3 0.6 shard_map.126
  18.9 3.0 %collective-permute-done.3.refs_1_ = bf16[192,512]{1,0:T(8,128)(2,1)S(1)} collective-permute-done((bf16[192,512]{1,0:T(8,128)(2,1)S(1)}, bf16[192,512]{1,0:T(8,128)(2,1)S(1)}, u32[]{:S(2)}, u32[]{:S(2)}) %collective-permute-start.3) | collective-permute-done | bytes 196640 | tf_op jit(solution)/shard_map/ppermute | solution.py:292
  21.9 1.8 %shard_map.127 = (bf16[192,512]{1,0:T(8,128)(2,1)S(1)}, f32[192,512]{1,0:T(8,128)S(1)}) custom-call(bf16[192,512]{1,0:T(8,128)(2,1)S(1)} %shard_map.125.refs_4_.refs_0_, bf16[192,512]{1,0:T(8,128)(2,1)S(1)} %collective-permute-done.3.refs_1_, bf16[1024,2048]{1,0:T(8,128)(2,1)S(1)} %get-tuple-element.38.refs_2_.refs_1_, ...), custom_call_target="tpu_custom_call" | custom-call | flops 1610612736 | bytes 9371648 | tf_op jit(solution)/shard_map/pallas_call | solution.py:40
  23.8 2.0 %collective-permute-start.6 = (bf16[192,512]{1,0:T(8,128)(2,1)S(1)}, bf16[192,512]{1,0:T(8,128)(2,1)S(1)}, u32[]{:S(2)}, u32[]{:S(2)}) collective-permute-start(bf16[192,512]{1,0:T(8,128)(2,1)S(1)} %get-tuple-element.40.refs_3_), channel_id=1, source_target_pairs={{0,1},{1,0},{2,3},{3,2},{4,5},{5,4},{6,7},{7,6},{8,9},{9,8},{10,11... | collective-permute-start | bytes 589832 | tf_op jit(solution)/shard_map/ppermute | solution.py:292
  25.8 1.5 %collective-permute-done.8.refs_0_ = bf16[192,512]{1,0:T(8,128)(2,1)S(1)} collective-permute-done((bf16[192,512]{1,0:T(8,128)(2,1)S(1)}, bf16[192,512]{1,0:T(8,128)(2,1)S(1)}, u32[]{:S(2)}, u32[]{:S(2)}) %collective-permute-start.8) | collective-permute-done | bytes 196640 | tf_op jit(solution)/shard_map/ppermute | solution.py:292
  27.2 0.5 collective-permute-start.9
  27.8 0.7 collective-permute-done.2.refs_0_
  28.4 1.8 %shard_map.128 = (bf16[192,512]{1,0:T(8,128)(2,1)S(1)}, f32[192,512]{1,0:T(8,128)S(1)}) custom-call(bf16[192,1024]{1,0:T(8,128)(2,1)S(1)} %collective-permute-done.2.refs_0_, bf16[1024,2048]{1,0:T(8,128)(2,1)S(1)} %get-tuple-element.38.refs_2_.refs_1_, bf16[2048,1024]{1,0:T(8,128)(2,1)S(1)} %get-tuple-element.39.refs_3_.refs_2_, ...), custom_call_target="tpu_custom_call" | custom-call | flops 1610612736 | bytes 9371648 | tf_op jit(solution)/shard_map/pallas_call | solution.py:40
  30.2 1.6 %collective-permute-start.4 = (bf16[192,512]{1,0:T(8,128)(2,1)S(1)}, bf16[192,512]{1,0:T(8,128)(2,1)S(1)}, u32[]{:S(2)}, u32[]{:S(2)}) collective-permute-start(bf16[192,512]{1,0:T(8,128)(2,1)S(1)} %get-tuple-element.42.refs_4_), channel_id=1, source_target_pairs={{0,1},{1,0},{2,3},{3,2},{4,5},{5,4},{6,7},{7,6},{8,9},{9,8},{10,11... | collective-permute-start | bytes 589832 | tf_op jit(solution)/shard_map/ppermute | solution.py:292
  31.9 1.5 %collective-permute-start.7 = (bf16[192,512]{1,0:T(8,128)(2,1)S(1)}, bf16[192,512]{1,0:T(8,128)(2,1)S(1)}, u32[]{:S(2)}, u32[]{:S(2)}) collective-permute-start(bf16[192,512]{1,0:T(8,128)(2,1)S(1)} %shard_map.129.refs_5_), channel_id=1, source_target_pairs={{0,4},{2,6},{4,0},{6,2},{1,5},{3,7},{5,1},{7,3},{8,12},{10,14},{12... | collective-permute-start | bytes 589832 | tf_op jit(solution)/shard_map/ppermute | solution.py:292
  33.4 1.3 %collective-permute-done.9.refs_1_ = bf16[192,512]{1,0:T(8,128)(2,1)S(1)} collective-permute-done((bf16[192,512]{1,0:T(8,128)(2,1)S(1)}, bf16[192,512]{1,0:T(8,128)(2,1)S(1)}, u32[]{:S(2)}, u32[]{:S(2)}) %collective-permute-start.9) | collective-permute-done | bytes 196640 | tf_op jit(solution)/shard_map/ppermute | solution.py:292
  34.7 1.8 %shard_map.130 = (bf16[192,512]{1,0:T(8,128)(2,1)S(1)}, f32[192,512]{1,0:T(8,128)S(1)}) custom-call(bf16[192,512]{1,0:T(8,128)(2,1)S(1)} %collective-permute-done.8.refs_0_, bf16[192,512]{1,0:T(8,128)(2,1)S(1)} %collective-permute-done.9.refs_1_, bf16[1024,2048]{1,0:T(8,128)(2,1)S(1)} %get-tuple-element.38.refs_2_.refs_1_, ...), custom_call_target="tpu_custom_call" | custom-call | flops 1610612736 | bytes 9371648 | tf_op jit(solution)/shard_map/pallas_call | solution.py:40
  36.6 1.4 %collective-permute-start.10 = (bf16[192,512]{1,0:T(8,128)(2,1)S(1)}, bf16[192,512]{1,0:T(8,128)(2,1)S(1)}, u32[]{:S(2)}, u32[]{:S(2)}) collective-permute-start(bf16[192,512]{1,0:T(8,128)(2,1)S(1)} %get-tuple-element.46), channel_id=1, source_target_pairs={{0,1},{1,0},{2,3},{3,2},{4,5},{5,4},{6,7},{7,6},{8,9},{9,8},{10,11... | collective-permute-start | bytes 589832 | tf_op jit(solution)/shard_map/ppermute | solution.py:292
  38.0 0.5 collective-permute-done.4
  38.5 2.5 %collective-permute-start.5 = (bf16[192,512]{1,0:T(8,128)(2,1)S(1)}, bf16[192,512]{1,0:T(8,128)(2,1)S(1)}, u32[]{:S(2)}, u32[]{:S(2)}) collective-permute-start(bf16[192,512]{1,0:T(8,128)(2,1)S(1)} %add_convert_fusion), channel_id=1, source_target_pairs={{0,2},{2,0},{4,6},{6,4},{1,3},{3,1},{5,7},{7,5},{8,10},{10,8},{12,... | collective-permute-start | bytes 589832 | tf_op jit(solution)/shard_map/ppermute | solution.py:292
  41.0 1.3 %collective-permute-done.10.refs_1_ = bf16[192,512]{1,0:T(8,128)(2,1)S(1)} collective-permute-done((bf16[192,512]{1,0:T(8,128)(2,1)S(1)}, bf16[192,512]{1,0:T(8,128)(2,1)S(1)}, u32[]{:S(2)}, u32[]{:S(2)}) %collective-permute-start.10) | collective-permute-done | bytes 196640 | tf_op jit(solution)/shard_map/ppermute | solution.py:292
  42.3 5.1 %collective-permute-start.11 = (bf16[192,512]{1,0:T(8,128)(2,1)S(1)}, bf16[192,512]{1,0:T(8,128)(2,1)S(1)}, u32[]{:S(2)}, u32[]{:S(2)}) collective-permute-start(bf16[192,512]{1,0:T(8,128)(2,1)S(1)} %shard_map.131), channel_id=1, source_target_pairs={{0,6},{2,4},{4,2},{6,0},{1,7},{3,5},{5,3},{7,1},{8,14},{10,12},{12... | collective-permute-start | bytes 589832 | tf_op jit(solution)/shard_map/ppermute | solution.py:292
  47.5 1.6 %collective-permute-done.5.refs_4_ = bf16[192,512]{1,0:T(8,128)(2,1)S(1)} collective-permute-done((bf16[192,512]{1,0:T(8,128)(2,1)S(1)}, bf16[192,512]{1,0:T(8,128)(2,1)S(1)}, u32[]{:S(2)}, u32[]{:S(2)}) %collective-permute-start.5) | collective-permute-done | bytes 196640 | tf_op jit(solution)/shard_map/ppermute | solution.py:292
  49.1 2.8 %collective-permute-done.11.refs_6_ = bf16[192,512]{1,0:T(8,128)(2,1)S(1)} collective-permute-done((bf16[192,512]{1,0:T(8,128)(2,1)S(1)}, bf16[192,512]{1,0:T(8,128)(2,1)S(1)}, u32[]{:S(2)}, u32[]{:S(2)}) %collective-permute-start.11) | collective-permute-done | bytes 196640 | tf_op jit(solution)/shard_map/ppermute | solution.py:292
  51.9 0.7 shard_map.132.refs_0_.refs_2_
  52.6 1.6 %collective-permute-start.12 = (bf16[256,512]{1,0:T(8,128)(2,1)S(1)}, bf16[256,512]{1,0:T(8,128)(2,1)S(1)}, u32[]{:S(2)}, u32[]{:S(2)}) collective-permute-start(bf16[256,512]{1,0:T(8,128)(2,1)S(1)} %shard_map.132.refs_0_.refs_2_), channel_id=1, source_target_pairs={{0,1},{1,0},{2,3},{3,2},{4,5},{5,4},{6,7},{7,6},{8,9},{9,8},{10,11... | collective-permute-start | bytes 786440 | tf_op jit(solution)/shard_map/ppermute | solution.py:292
  54.2 1.5 %collective-permute-start.14 = (bf16[256,512]{1,0:T(8,128)(2,1)S(1)}, bf16[256,512]{1,0:T(8,128)(2,1)S(1)}, u32[]{:S(2)}, u32[]{:S(2)}) collective-permute-start(bf16[256,512]{1,0:T(8,128)(2,1)S(1)} %shard_map.132.refs_0_.refs_2_), channel_id=1, source_target_pairs={{0,16},{1,17},{8,0},{9,1},{16,24},{17,25},{24,8},{25,9},{2,18},{3,... | collective-permute-start | bytes 786440 | tf_op jit(solution)/shard_map/ppermute | solution.py:427
  55.7 0.3 collective-permute-start.15
  56.0 3.0 %collective-permute-done.12.refs_0_.refs_1_ = bf16[256,512]{1,0:T(8,128)(2,1)S(1)} collective-permute-done((bf16[256,512]{1,0:T(8,128)(2,1)S(1)}, bf16[256,512]{1,0:T(8,128)(2,1)S(1)}, u32[]{:S(2)}, u32[]{:S(2)}) %collective-permute-start.12) | collective-permute-done | bytes 262176 | tf_op jit(solution)/shard_map/ppermute | solution.py:292
  59.1 0.5 collective-permute-done.14.refs_2_
  59.6 2.8 %collective-permute-done.15.refs_3_ = bf16[256,512]{1,0:T(8,128)(2,1)S(1)} collective-permute-done((bf16[256,512]{1,0:T(8,128)(2,1)S(1)}, bf16[256,512]{1,0:T(8,128)(2,1)S(1)}, u32[]{:S(2)}, u32[]{:S(2)}) %collective-permute-start.15) | collective-permute-done | bytes 262176 | tf_op jit(solution)/shard_map/ppermute | solution.py:427
  62.4 0.4 collective-permute-start.16
  62.9 0.7 shard_map.134.refs_2_
  63.5 0.5 collective-permute-done.16.refs_1_
  64.1 2.2 %collective-permute-start.17 = (bf16[256,512]{1,0:T(8,128)(2,1)S(1)}, bf16[256,512]{1,0:T(8,128)(2,1)S(1)}, u32[]{:S(2)}, u32[]{:S(2)}) collective-permute-start(bf16[256,512]{1,0:T(8,128)(2,1)S(1)} %get-tuple-element.51), channel_id=1, source_target_pairs={{0,8},{8,0},{16,24},{24,16},{1,9},{9,1},{17,25},{25,17},{2,10},{10... | collective-permute-start | bytes 786440 | tf_op jit(solution)/shard_map/ppermute | solution.py:292
  66.3 1.2 %collective-permute-done.17.refs_1_ = bf16[256,512]{1,0:T(8,128)(2,1)S(1)} collective-permute-done((bf16[256,512]{1,0:T(8,128)(2,1)S(1)}, bf16[256,512]{1,0:T(8,128)(2,1)S(1)}, u32[]{:S(2)}, u32[]{:S(2)}) %collective-permute-start.17) | collective-permute-done | bytes 262176 | tf_op jit(solution)/shard_map/ppermute | solution.py:292
  67.5 0.1 shard_map.137
  67.6 0.6 collective-permute-start.18
  68.2 2.9 %collective-permute-start.19 = (bf16[256,128]{1,0:T(8,128)(2,1)S(1)}, bf16[256,128]{1,0:T(8,128)(2,1)S(1)}, u32[]{:S(2)}, u32[]{:S(2)}) collective-permute-start(bf16[256,128]{1,0:T(8,128)(2,1)S(1)} %get-tuple-element.54), channel_id=1, source_target_pairs={{0,16},{1,17},{8,24},{9,25},{16,0},{17,1},{24,8},{25,9},{2,18},{3,... | collective-permute-start | bytes 196616 | tf_op jit(solution)/shard_map/ppermute | solution.py:476
  71.2 0.7 shard_map.136
  71.9 0.1 collective-permute-done.18
  72.0 1.4 %collective-permute-done.19 = bf16[256,128]{1,0:T(8,128)(2,1)S(1)} collective-permute-done((bf16[256,128]{1,0:T(8,128)(2,1)S(1)}, bf16[256,128]{1,0:T(8,128)(2,1)S(1)}, u32[]{:S(2)}, u32[]{:S(2)}) %collective-permute-start.19) | collective-permute-done | bytes 65568 | tf_op jit(solution)/shard_map/ppermute | solution.py:476
  73.5 2.8 %collective-permute-done.20 = bf16[256,128]{1,0:T(8,128)(2,1)S(1)} collective-permute-done((bf16[256,128]{1,0:T(8,128)(2,1)S(1)}, bf16[256,128]{1,0:T(8,128)(2,1)S(1)}, u32[]{:S(2)}, u32[]{:S(2)}) %collective-permute-start.20) | collective-permute-done | bytes 65568 | tf_op jit(solution)/shard_map/ppermute | solution.py:476
  76.2 0.7 add_convert_fusion.2
  (31 shorter events, 0.4 us)
Async XLA Ops:
  0.6 1.0 %copy-start.1 = (bf16[1,256,1024]{2,1,0:T(8,128)(2,1)S(1)}, bf16[1,256,1024]{2,1,0:T(8,128)(2,1)}, u32[]{:S(2)}) copy-start(bf16[1,256,1024]{2,1,0:T(8,128)(2,1)} %param.11) | copy-start | bytes 1572868
  0.6 1.0 %copy-start.4 = (s32[1,256,2]{1,2,0:T(2,128)S(1)}, s32[1,256,2]{1,2,0:T(2,128)}, u32[]{:S(2)}) copy-start(s32[1,256,2]{1,2,0:T(2,128)} %param.12) | copy-start | bytes 6148
  0.6 1.0 %copy-start.8 = (f32[1,1024]{1,0:T(1,128)S(1)}, f32[1,1024]{1,0:T(1,128)}, u32[]{:S(2)}) copy-start(f32[1,1024]{1,0:T(1,128)} %refs_2_.2) | copy-start | bytes 12292
  2.6 13.3 %collective-permute-start = (bf16[192,512]{1,0:T(8,128)(2,1)S(1)}, bf16[192,512]{1,0:T(8,128)(2,1)S(1)}, u32[]{:S(2)}, u32[]{:S(2)}) collective-permute-start(bf16[192,512]{1,0:T(8,128)(2,1)S(1)} %get-tuple-element.33), channel_id=1, source_target_pairs={{0,4},{2,6},{4,0},{6,2},{1,5},{3,7},{5,1},{7,3},{8,12},{10,14},{12... | collective-permute-start | bytes 589832 | tf_op jit(solution)/shard_map/ppermute | solution.py:292
  6.7 11.6 %copy-start.2 = (bf16[1,256,512]{2,1,0:T(8,128)(2,1)S(1)}, bf16[1,256,512]{2,1,0:T(8,128)(2,1)}, u32[]{:S(2)}) copy-start(bf16[1,256,512]{2,1,0:T(8,128)(2,1)} %param.21) | copy-start | bytes 786436
  6.7 11.6 %copy-start.5 = (f32[1,256,2]{1,2,0:T(2,128)S(1)}, f32[1,256,2]{1,2,0:T(2,128)}, u32[]{:S(2)}) copy-start(f32[1,256,2]{1,2,0:T(2,128)} %param.13) | copy-start | bytes 6148
  11.3 6.9 %collective-permute-start.1 = (bf16[192,512]{1,0:T(8,128)(2,1)S(1)}, bf16[192,512]{1,0:T(8,128)(2,1)S(1)}, u32[]{:S(2)}, u32[]{:S(2)}) collective-permute-start(bf16[192,512]{1,0:T(8,128)(2,1)S(1)} %get-tuple-element.32.refs_0_), channel_id=1, source_target_pairs={{0,1},{1,0},{2,3},{3,2},{4,5},{5,4},{6,7},{7,6},{8,9},{9,8},{10,11... | collective-permute-start | bytes 589832 | tf_op jit(solution)/shard_map/ppermute | solution.py:292
  12.9 15.6 %collective-permute-start.2 = (bf16[192,1024]{1,0:T(8,128)(2,1)S(1)}, bf16[192,1024]{1,0:T(8,128)(2,1)S(1)}, u32[]{:S(2)}, u32[]{:S(2)}) collective-permute-start(bf16[192,1024]{1,0:T(8,128)(2,1)S(1)} %get-tuple-element.37), channel_id=1, source_target_pairs={{0,2},{2,0},{4,6},{6,4},{1,3},{3,1},{5,7},{7,5},{8,10},{10,8},{12,... | collective-permute-start | bytes 1179656 | tf_op jit(solution)/shard_map/ppermute | solution.py:292
  14.4 12.8 %collective-permute-start.8 = (bf16[192,512]{1,0:T(8,128)(2,1)S(1)}, bf16[192,512]{1,0:T(8,128)(2,1)S(1)}, u32[]{:S(2)}, u32[]{:S(2)}) collective-permute-start(bf16[192,512]{1,0:T(8,128)(2,1)S(1)} %get-tuple-element.44), channel_id=1, source_target_pairs={{0,6},{2,4},{4,2},{6,0},{1,7},{3,5},{5,3},{7,1},{8,14},{10,12},{12... | collective-permute-start | bytes 589832 | tf_op jit(solution)/shard_map/ppermute | solution.py:292
  15.9 6.0 %collective-permute-start.3 = (bf16[192,512]{1,0:T(8,128)(2,1)S(1)}, bf16[192,512]{1,0:T(8,128)(2,1)S(1)}, u32[]{:S(2)}, u32[]{:S(2)}) collective-permute-start(bf16[192,512]{1,0:T(8,128)(2,1)S(1)} %shard_map.125.refs_4_.refs_0_), channel_id=1, source_target_pairs={{0,1},{1,0},{2,3},{3,2},{4,5},{5,4},{6,7},{7,6},{8,9},{9,8},{10,11... | collective-permute-start | bytes 589832 | tf_op jit(solution)/shard_map/ppermute | solution.py:292
  23.8 8.1 %collective-permute-start.6 = (bf16[192,512]{1,0:T(8,128)(2,1)S(1)}, bf16[192,512]{1,0:T(8,128)(2,1)S(1)}, u32[]{:S(2)}, u32[]{:S(2)}) collective-permute-start(bf16[192,512]{1,0:T(8,128)(2,1)S(1)} %get-tuple-element.40.refs_3_), channel_id=1, source_target_pairs={{0,1},{1,0},{2,3},{3,2},{4,5},{5,4},{6,7},{7,6},{8,9},{9,8},{10,11... | collective-permute-start | bytes 589832 | tf_op jit(solution)/shard_map/ppermute | solution.py:292
  27.2 7.5 %collective-permute-start.9 = (bf16[192,512]{1,0:T(8,128)(2,1)S(1)}, bf16[192,512]{1,0:T(8,128)(2,1)S(1)}, u32[]{:S(2)}, u32[]{:S(2)}) collective-permute-start(bf16[192,512]{1,0:T(8,128)(2,1)S(1)} %collective-permute-done.8.refs_0_), channel_id=1, source_target_pairs={{0,1},{1,0},{2,3},{3,2},{4,5},{5,4},{6,7},{7,6},{8,9},{9,8},{10,11... | collective-permute-start | bytes 589832 | tf_op jit(solution)/shard_map/ppermute | solution.py:292
  30.2 8.2 %collective-permute-start.4 = (bf16[192,512]{1,0:T(8,128)(2,1)S(1)}, bf16[192,512]{1,0:T(8,128)(2,1)S(1)}, u32[]{:S(2)}, u32[]{:S(2)}) collective-permute-start(bf16[192,512]{1,0:T(8,128)(2,1)S(1)} %get-tuple-element.42.refs_4_), channel_id=1, source_target_pairs={{0,1},{1,0},{2,3},{3,2},{4,5},{5,4},{6,7},{7,6},{8,9},{9,8},{10,11... | collective-permute-start | bytes 589832 | tf_op jit(solution)/shard_map/ppermute | solution.py:292
  31.9 15.6 %collective-permute-start.7 = (bf16[192,512]{1,0:T(8,128)(2,1)S(1)}, bf16[192,512]{1,0:T(8,128)(2,1)S(1)}, u32[]{:S(2)}, u32[]{:S(2)}) collective-permute-start(bf16[192,512]{1,0:T(8,128)(2,1)S(1)} %shard_map.129.refs_5_), channel_id=1, source_target_pairs={{0,4},{2,6},{4,0},{6,2},{1,5},{3,7},{5,1},{7,3},{8,12},{10,14},{12... | collective-permute-start | bytes 589832 | tf_op jit(solution)/shard_map/ppermute | solution.py:292
  36.5 26.3 %copy-start = (bf16[1,1024,512]{2,1,0:T(8,128)(2,1)S(1)}, bf16[1,1024,512]{2,1,0:T(8,128)(2,1)}, u32[]{:S(2)}) copy-start(bf16[1,1024,512]{2,1,0:T(8,128)(2,1)} %param.18) | copy-start | bytes 3145732
  36.5 26.3 %copy-start.3 = (f32[1,1024]{1,0:T(1,128)S(1)}, f32[1,1024]{1,0:T(1,128)}, u32[]{:S(2)}) copy-start(f32[1,1024]{1,0:T(1,128)} %refs_2_.3) | copy-start | bytes 12292
  36.5 27.5 %copy-start.6 = (bf16[1,1024,512]{2,1,0:T(8,128)(2,1)S(1)}, bf16[1,1024,512]{2,1,0:T(8,128)(2,1)}, u32[]{:S(2)}) copy-start(bf16[1,1024,512]{2,1,0:T(8,128)(2,1)} %param.19) | copy-start | bytes 3145732
  36.6 27.5 %copy-start.7 = (bf16[1,1024,512]{2,1,0:T(8,128)(2,1)S(1)}, bf16[1,1024,512]{2,1,0:T(8,128)(2,1)}, u32[]{:S(2)}) copy-start(bf16[1,1024,512]{2,1,0:T(8,128)(2,1)} %param.20) | copy-start | bytes 3145732
  36.6 5.7 %collective-permute-start.10 = (bf16[192,512]{1,0:T(8,128)(2,1)S(1)}, bf16[192,512]{1,0:T(8,128)(2,1)S(1)}, u32[]{:S(2)}, u32[]{:S(2)}) collective-permute-start(bf16[192,512]{1,0:T(8,128)(2,1)S(1)} %get-tuple-element.46), channel_id=1, source_target_pairs={{0,1},{1,0},{2,3},{3,2},{4,5},{5,4},{6,7},{7,6},{8,9},{9,8},{10,11... | collective-permute-start | bytes 589832 | tf_op jit(solution)/shard_map/ppermute | solution.py:292
  38.5 10.6 %collective-permute-start.5 = (bf16[192,512]{1,0:T(8,128)(2,1)S(1)}, bf16[192,512]{1,0:T(8,128)(2,1)S(1)}, u32[]{:S(2)}, u32[]{:S(2)}) collective-permute-start(bf16[192,512]{1,0:T(8,128)(2,1)S(1)} %add_convert_fusion), channel_id=1, source_target_pairs={{0,2},{2,0},{4,6},{6,4},{1,3},{3,1},{5,7},{7,5},{8,10},{10,8},{12,... | collective-permute-start | bytes 589832 | tf_op jit(solution)/shard_map/ppermute | solution.py:292
  42.3 9.6 %collective-permute-start.11 = (bf16[192,512]{1,0:T(8,128)(2,1)S(1)}, bf16[192,512]{1,0:T(8,128)(2,1)S(1)}, u32[]{:S(2)}, u32[]{:S(2)}) collective-permute-start(bf16[192,512]{1,0:T(8,128)(2,1)S(1)} %shard_map.131), channel_id=1, source_target_pairs={{0,6},{2,4},{4,2},{6,0},{1,7},{3,5},{5,3},{7,1},{8,14},{10,12},{12... | collective-permute-start | bytes 589832 | tf_op jit(solution)/shard_map/ppermute | solution.py:292
  52.6 6.4 %collective-permute-start.12 = (bf16[256,512]{1,0:T(8,128)(2,1)S(1)}, bf16[256,512]{1,0:T(8,128)(2,1)S(1)}, u32[]{:S(2)}, u32[]{:S(2)}) collective-permute-start(bf16[256,512]{1,0:T(8,128)(2,1)S(1)} %shard_map.132.refs_0_.refs_2_), channel_id=1, source_target_pairs={{0,1},{1,0},{2,3},{3,2},{4,5},{5,4},{6,7},{7,6},{8,9},{9,8},{10,11... | collective-permute-start | bytes 786440 | tf_op jit(solution)/shard_map/ppermute | solution.py:292
  54.2 4.8 %collective-permute-start.13 = (bf16[256,512]{1,0:T(8,128)(2,1)S(1)}, bf16[256,512]{1,0:T(8,128)(2,1)S(1)}, u32[]{:S(2)}, u32[]{:S(2)}) collective-permute-start(bf16[256,512]{1,0:T(8,128)(2,1)S(1)} %shard_map.132.refs_0_.refs_2_), channel_id=1, source_target_pairs={{0,8},{8,0},{16,24},{24,16},{1,9},{9,1},{17,25},{25,17},{2,10},{10... | collective-permute-start | bytes 786440 | tf_op jit(solution)/shard_map/ppermute | solution.py:292
  54.2 5.4 %collective-permute-start.14 = (bf16[256,512]{1,0:T(8,128)(2,1)S(1)}, bf16[256,512]{1,0:T(8,128)(2,1)S(1)}, u32[]{:S(2)}, u32[]{:S(2)}) collective-permute-start(bf16[256,512]{1,0:T(8,128)(2,1)S(1)} %shard_map.132.refs_0_.refs_2_), channel_id=1, source_target_pairs={{0,16},{1,17},{8,0},{9,1},{16,24},{17,25},{24,8},{25,9},{2,18},{3,... | collective-permute-start | bytes 786440 | tf_op jit(solution)/shard_map/ppermute | solution.py:427
  55.7 6.7 %collective-permute-start.15 = (bf16[256,512]{1,0:T(8,128)(2,1)S(1)}, bf16[256,512]{1,0:T(8,128)(2,1)S(1)}, u32[]{:S(2)}, u32[]{:S(2)}) collective-permute-start(bf16[256,512]{1,0:T(8,128)(2,1)S(1)} %shard_map.132.refs_0_.refs_2_), channel_id=1, source_target_pairs={{0,25},{1,24},{8,0},{9,1},{16,8},{17,9},{24,16},{25,17},{2,27},{3,... | collective-permute-start | bytes 786440 | tf_op jit(solution)/shard_map/ppermute | solution.py:427
  62.4 1.6 %collective-permute-start.16 = (bf16[256,512]{1,0:T(8,128)(2,1)S(1)}, bf16[256,512]{1,0:T(8,128)(2,1)S(1)}, u32[]{:S(2)}, u32[]{:S(2)}) collective-permute-start(bf16[256,512]{1,0:T(8,128)(2,1)S(1)} %shard_map.133.refs_0_), channel_id=1, source_target_pairs={{0,8},{8,0},{16,24},{24,16},{1,9},{9,1},{17,25},{25,17},{2,10},{10... | collective-permute-start | bytes 786440 | tf_op jit(solution)/shard_map/ppermute | solution.py:292
  64.1 3.4 %collective-permute-start.17 = (bf16[256,512]{1,0:T(8,128)(2,1)S(1)}, bf16[256,512]{1,0:T(8,128)(2,1)S(1)}, u32[]{:S(2)}, u32[]{:S(2)}) collective-permute-start(bf16[256,512]{1,0:T(8,128)(2,1)S(1)} %get-tuple-element.51), channel_id=1, source_target_pairs={{0,8},{8,0},{16,24},{24,16},{1,9},{9,1},{17,25},{25,17},{2,10},{10... | collective-permute-start | bytes 786440 | tf_op jit(solution)/shard_map/ppermute | solution.py:292
  67.6 4.4 %collective-permute-start.18 = (bf16[256,128]{1,0:T(8,128)(2,1)S(1)}, bf16[256,128]{1,0:T(8,128)(2,1)S(1)}, u32[]{:S(2)}, u32[]{:S(2)}) collective-permute-start(bf16[256,128]{1,0:T(8,128)(2,1)S(1)} %get-tuple-element.53), channel_id=1, source_target_pairs={{0,1},{1,0},{8,9},{9,8},{16,17},{17,16},{24,25},{25,24},{2,3},{3,2... | collective-permute-start | bytes 196616 | tf_op jit(solution)/shard_map/ppermute | solution.py:476
  68.2 5.3 %collective-permute-start.19 = (bf16[256,128]{1,0:T(8,128)(2,1)S(1)}, bf16[256,128]{1,0:T(8,128)(2,1)S(1)}, u32[]{:S(2)}, u32[]{:S(2)}) collective-permute-start(bf16[256,128]{1,0:T(8,128)(2,1)S(1)} %get-tuple-element.54), channel_id=1, source_target_pairs={{0,16},{1,17},{8,24},{9,25},{16,0},{17,1},{24,8},{25,9},{2,18},{3,... | collective-permute-start | bytes 196616 | tf_op jit(solution)/shard_map/ppermute | solution.py:476
  71.1 5.2 %collective-permute-start.20 = (bf16[256,128]{1,0:T(8,128)(2,1)S(1)}, bf16[256,128]{1,0:T(8,128)(2,1)S(1)}, u32[]{:S(2)}, u32[]{:S(2)}) collective-permute-start(bf16[256,128]{1,0:T(8,128)(2,1)S(1)} %get-tuple-element.55), channel_id=1, source_target_pairs={{0,17},{1,16},{8,25},{9,24},{16,1},{17,0},{24,9},{25,8},{2,19},{3,... | collective-permute-start | bytes 196616 | tf_op jit(solution)/shard_map/ppermute | solution.py:476

commit v13 on v12

--- a/solution.py
+++ b/solution.py
@@ -361,7 +361,8 @@
         )
 
     arriving = [joined(groups[0])]
-    later = [near_rows] + [far_rows[k - 2] for k in groups[1]]
+    near = swap(near_rows, "exp", 1)
+    later = [far_rows[k - 2] for k in groups[1]]
     loads = max(1, units // 512) + 1
     own_away, own_kept, weight_first, weight_second, *later = call(
         expert_first,
@@ -378,11 +379,10 @@
         limit=44,
         held=later,
     )
-    near = swap(later[0], "exp", 1)
-    for k, rows in zip(groups[1], later[1:]):
+    for k, rows in zip(groups[1], later):
         far_rows[k - 2] = rows
     arriving.append(joined(groups[1]))
-    returned = {0: total(own_away, own_kept, plain=True)}
+    returned = {0: total(own_away, own_kept)}
     arriving[0] = hold(arriving[0], [own_away])
     others = [swap(arriving[0], "tp", 1)]
     high, low, upstream = call(

time: 77.1 us -> 77.1 us (level)
  starting transfers between devices: 34 us -> 30.5 us
  waiting for transfers between devices: 26.4 us -> 29.9 us
    ppermute x16, waiting for transfers between devices: 18.7 us -> 22.6 us  [swap(): return lax.ppermute(block, axis, [(i, i ^ step) for i in range(size)])]
    ppermute x16, starting transfers between devices: 28.7 us -> 24.8 us  [swap(): return lax.ppermute(block, axis, [(i, i ^ step) for i in range(size)])]
    pallas_call x16 -> x17, Pallas kernels: 13.9 us -> 13.9 us  [call(): pl.pallas_call(run, out_shape=[*out_shape, *(shape_of(x.shape, x.dtype) f...]
  transfers between devices with their start and end apart: 21 -> 21, of which waited for: 17 -> 15; matrix products, arithmetic and copies ran while one was open for 0% -> 0% of each run, Pallas kernels for 16% -> 16%
where the time goes in v13:
time: 77.1 us; the launch traced here: 77 us
  starting transfers between devices  30.5 us (40%)
  waiting for transfers between devices  29.9 us (39%)
  Pallas kernels  13.9 us (18%)
  local copies, waits for them, and re-layouts  1.03 us (1%)
  between operations  0.81 us (1%)
    ppermute x16, starting transfers between devices, swap(): return lax.ppermute(block, axis, [(i, i ^ step) for i in range(size)])  24.8 us
    ppermute x16, waiting for transfers between devices, swap(): return lax.ppermute(block, axis, [(i, i ^ step) for i in range(size)])  22.6 us
    pallas_call x17, Pallas kernels, call(): pl.pallas_call(run, out_shape=[*out_shape, *(shape_of(x.shape, x.dtype) f...  13.9 us
    ppermute x3, waiting for transfers between devices, shards(): total = total + lax.ppermute(blocks[k], ('sec', 'tp'), pairs).astype(WIDE)  4.36 us
    ppermute x3, starting transfers between devices, shards(): total = total + lax.ppermute(blocks[k], ('sec', 'tp'), pairs).astype(WIDE)  3.57 us
    ppermute x2, waiting for transfers between devices, cycle(): return lax.ppermute(hidden_half, ('sec', 'tp'), list(targets.items()))  2.98 us
    ppermute x2, starting transfers between devices, cycle(): return lax.ppermute(hidden_half, ('sec', 'tp'), list(targets.items()))  2.16 us
  transfers between devices with their start and end apart: 21, of which 15 were waited for; matrix products, arithmetic and copies ran while one was open for 0% of the time, Pallas kernels for 16%

profile of v13, /device:TPU:0, one launch (start us, length us, event | category | flops | bytes accessed | tf_op | source)
XLA Modules:
  0.0 77.0 jit_solution(14197996375619557250)
XLA Ops:
  0.7 1.0 %copy-done.1 = bf16[1,256,1024]{2,1,0:T(8,128)(2,1)S(1)} copy-done((bf16[1,256,1024]{2,1,0:T(8,128)(2,1)S(1)}, bf16[1,256,1024]{2,1,0:T(8,128)(2,1)}, u32[]{:S(2)}) %copy-start.1) | copy-done | bytes 524312
  1.7 0.9 %shard_map.123 = (bf16[192,512]{1,0:T(8,128)(2,1)S(1)}, bf16[192,512]{1,0:T(8,128)(2,1)S(1)}, bf16[192,1024]{1,0:T(8,128)(2,1)S(1)}, bf16[192,1024]{1,0:T(8,128)(2,1)S(1)}) custom-call(bf16[256,1024]{1,0:T(8,128)(2,1)S(1)} %bitcast.15, s32[2,256]{1,0:T(2,128)S(1)} %bitcast.18, f32[1,1024]{1,0:T(1,128)S(1)} %copy-done.8, ...), custom_call_target="tpu_custom_call" | custom-call | flops 402653184 | bytes 1841152 | tf_op jit(solution)/shard_map/pallas_call | solution.py:40
  2.6 4.1 %collective-permute-start = (bf16[192,512]{1,0:T(8,128)(2,1)S(1)}, bf16[192,512]{1,0:T(8,128)(2,1)S(1)}, u32[]{:S(2)}, u32[]{:S(2)}) collective-permute-start(bf16[192,512]{1,0:T(8,128)(2,1)S(1)} %get-tuple-element.31), channel_id=1, source_target_pairs={{0,4},{2,6},{4,0},{6,2},{1,5},{3,7},{5,1},{7,3},{8,12},{10,14},{12... | collective-permute-start | bytes 589832 | tf_op jit(solution)/shard_map/ppermute | solution.py:292
  6.7 1.6 %collective-permute-start.2 = (bf16[192,1024]{1,0:T(8,128)(2,1)S(1)}, bf16[192,1024]{1,0:T(8,128)(2,1)S(1)}, u32[]{:S(2)}, u32[]{:S(2)}) collective-permute-start(bf16[192,1024]{1,0:T(8,128)(2,1)S(1)} %get-tuple-element.35), channel_id=1, source_target_pairs={{0,2},{2,0},{4,6},{6,4},{1,3},{3,1},{5,7},{7,5},{8,10},{10,8},{12,... | collective-permute-start | bytes 1179656 | tf_op jit(solution)/shard_map/ppermute | solution.py:292
  8.2 4.6 %shard_map.124 = (bf16[192,512]{1,0:T(8,128)(2,1)S(1)}, f32[192,512]{1,0:T(8,128)S(1)}, bf16[1024,2048]{1,0:T(8,128)(2,1)S(1)}, bf16[2048,1024]{1,0:T(8,128)(2,1)S(1)}, bf16[192,512]{1,0:T(8,128)(2,1)S(1)}) custom-call(bf16[192,1024]{1,0:T(8,128)(2,1)S(1)} %get-tuple-element.28.refs_0_, ...), custom_call_target="tpu_custom_call", output_to_operand_aliasing={{4}: (3, {})} | custom-call | flops 1610612736 | bytes 17760256 | tf_op jit(solution)/shard_map/pallas_call | solution.py:40
  12.9 1.6 %collective-permute-start.1 = (bf16[192,512]{1,0:T(8,128)(2,1)S(1)}, bf16[192,512]{1,0:T(8,128)(2,1)S(1)}, u32[]{:S(2)}, u32[]{:S(2)}) collective-permute-start(bf16[192,512]{1,0:T(8,128)(2,1)S(1)} %get-tuple-element.30.refs_0_), channel_id=1, source_target_pairs={{0,1},{1,0},{2,3},{3,2},{4,5},{5,4},{6,7},{7,6},{8,9},{9,8},{10,11... | collective-permute-start | bytes 589832 | tf_op jit(solution)/shard_map/ppermute | solution.py:292
  14.4 1.4 %collective-permute-done.refs_1_ = bf16[192,512]{1,0:T(8,128)(2,1)S(1)} collective-permute-done((bf16[192,512]{1,0:T(8,128)(2,1)S(1)}, bf16[192,512]{1,0:T(8,128)(2,1)S(1)}, u32[]{:S(2)}, u32[]{:S(2)}) %collective-permute-start) | collective-permute-done | bytes 196640 | tf_op jit(solution)/shard_map/ppermute | solution.py:292
  15.9 1.6 %collective-permute-start.3 = (bf16[192,512]{1,0:T(8,128)(2,1)S(1)}, bf16[192,512]{1,0:T(8,128)(2,1)S(1)}, u32[]{:S(2)}, u32[]{:S(2)}) collective-permute-start(bf16[192,512]{1,0:T(8,128)(2,1)S(1)} %shard_map.125.refs_4_.refs_0_), channel_id=1, source_target_pairs={{0,1},{1,0},{2,3},{3,2},{4,5},{5,4},{6,7},{7,6},{8,9},{9,8},{10,11... | collective-permute-start | bytes 589832 | tf_op jit(solution)/shard_map/ppermute | solution.py:292
  17.5 3.5 %collective-permute-start.8 = (bf16[192,512]{1,0:T(8,128)(2,1)S(1)}, bf16[192,512]{1,0:T(8,128)(2,1)S(1)}, u32[]{:S(2)}, u32[]{:S(2)}) collective-permute-start(bf16[192,512]{1,0:T(8,128)(2,1)S(1)} %get-tuple-element.42), channel_id=1, source_target_pairs={{0,6},{2,4},{4,2},{6,0},{1,7},{3,5},{5,3},{7,1},{8,14},{10,12},{12... | collective-permute-start | bytes 589832 | tf_op jit(solution)/shard_map/ppermute | solution.py:292
  21.0 0.6 shard_map.126
  21.6 1.6 %collective-permute-done.3.refs_1_ = bf16[192,512]{1,0:T(8,128)(2,1)S(1)} collective-permute-done((bf16[192,512]{1,0:T(8,128)(2,1)S(1)}, bf16[192,512]{1,0:T(8,128)(2,1)S(1)}, u32[]{:S(2)}, u32[]{:S(2)}) %collective-permute-start.3) | collective-permute-done | bytes 196640 | tf_op jit(solution)/shard_map/ppermute | solution.py:292
  23.2 1.8 %shard_map.128 = (bf16[192,512]{1,0:T(8,128)(2,1)S(1)}, f32[192,512]{1,0:T(8,128)S(1)}) custom-call(bf16[192,512]{1,0:T(8,128)(2,1)S(1)} %shard_map.125.refs_4_.refs_0_, bf16[192,512]{1,0:T(8,128)(2,1)S(1)} %collective-permute-done.3.refs_1_, bf16[1024,2048]{1,0:T(8,128)(2,1)S(1)} %get-tuple-element.36.refs_2_.refs_1_, ...), custom_call_target="tpu_custom_call" | custom-call | flops 1610612736 | bytes 9371648 | tf_op jit(solution)/shard_map/pallas_call | solution.py:40
  25.0 1.6 %collective-permute-start.6 = (bf16[192,512]{1,0:T(8,128)(2,1)S(1)}, bf16[192,512]{1,0:T(8,128)(2,1)S(1)}, u32[]{:S(2)}, u32[]{:S(2)}) collective-permute-start(bf16[192,512]{1,0:T(8,128)(2,1)S(1)} %get-tuple-element.38.refs_3_), channel_id=1, source_target_pairs={{0,1},{1,0},{2,3},{3,2},{4,5},{5,4},{6,7},{7,6},{8,9},{9,8},{10,11... | collective-permute-start | bytes 589832 | tf_op jit(solution)/shard_map/ppermute | solution.py:292
  26.6 0.5 collective-permute-start.9
  27.1 1.8 %shard_map.129 = (bf16[192,512]{1,0:T(8,128)(2,1)S(1)}, f32[192,512]{1,0:T(8,128)S(1)}) custom-call(bf16[192,1024]{1,0:T(8,128)(2,1)S(1)} %collective-permute-done.2.refs_0_, bf16[1024,2048]{1,0:T(8,128)(2,1)S(1)} %get-tuple-element.36.refs_2_.refs_1_, bf16[2048,1024]{1,0:T(8,128)(2,1)S(1)} %get-tuple-element.37.refs_3_.refs_2_, ...), custom_call_target="tpu_custom_call" | custom-call | flops 1610612736 | bytes 9371648 | tf_op jit(solution)/shard_map/pallas_call | solution.py:40
  29.0 1.6 %collective-permute-start.4 = (bf16[192,512]{1,0:T(8,128)(2,1)S(1)}, bf16[192,512]{1,0:T(8,128)(2,1)S(1)}, u32[]{:S(2)}, u32[]{:S(2)}) collective-permute-start(bf16[192,512]{1,0:T(8,128)(2,1)S(1)} %get-tuple-element.40.refs_4_), channel_id=1, source_target_pairs={{0,1},{1,0},{2,3},{3,2},{4,5},{5,4},{6,7},{7,6},{8,9},{9,8},{10,11... | collective-permute-start | bytes 589832 | tf_op jit(solution)/shard_map/ppermute | solution.py:292
  30.5 2.4 %collective-permute-done.6.refs_1_ = bf16[192,512]{1,0:T(8,128)(2,1)S(1)} collective-permute-done((bf16[192,512]{1,0:T(8,128)(2,1)S(1)}, bf16[192,512]{1,0:T(8,128)(2,1)S(1)}, u32[]{:S(2)}, u32[]{:S(2)}) %collective-permute-start.6) | collective-permute-done | bytes 196640 | tf_op jit(solution)/shard_map/ppermute | solution.py:292
  33.0 0.1 collective-permute-start.7
  33.1 4.0 %collective-permute-done.9.refs_1_ = bf16[192,512]{1,0:T(8,128)(2,1)S(1)} collective-permute-done((bf16[192,512]{1,0:T(8,128)(2,1)S(1)}, bf16[192,512]{1,0:T(8,128)(2,1)S(1)}, u32[]{:S(2)}, u32[]{:S(2)}) %collective-permute-start.9) | collective-permute-done | bytes 196640 | tf_op jit(solution)/shard_map/ppermute | solution.py:292
  37.1 1.8 %shard_map.131 = (bf16[192,512]{1,0:T(8,128)(2,1)S(1)}, f32[192,512]{1,0:T(8,128)S(1)}) custom-call(bf16[192,512]{1,0:T(8,128)(2,1)S(1)} %collective-permute-done.8.refs_0_, bf16[192,512]{1,0:T(8,128)(2,1)S(1)} %collective-permute-done.9.refs_1_, bf16[1024,2048]{1,0:T(8,128)(2,1)S(1)} %get-tuple-element.36.refs_2_.refs_1_, ...), custom_call_target="tpu_custom_call" | custom-call | flops 1610612736 | bytes 9371648 | tf_op jit(solution)/shard_map/pallas_call | solution.py:40
  39.0 1.2 %collective-permute-start.10 = (bf16[192,512]{1,0:T(8,128)(2,1)S(1)}, bf16[192,512]{1,0:T(8,128)(2,1)S(1)}, u32[]{:S(2)}, u32[]{:S(2)}) collective-permute-start(bf16[192,512]{1,0:T(8,128)(2,1)S(1)} %get-tuple-element.44), channel_id=1, source_target_pairs={{0,1},{1,0},{2,3},{3,2},{4,5},{5,4},{6,7},{7,6},{8,9},{9,8},{10,11... | collective-permute-start | bytes 589832 | tf_op jit(solution)/shard_map/ppermute | solution.py:292
  40.2 0.7 collective-permute-done.4
  40.9 0.5 collective-permute-start.5
  41.4 3.3 %collective-permute-done.10.refs_1_ = bf16[192,512]{1,0:T(8,128)(2,1)S(1)} collective-permute-done((bf16[192,512]{1,0:T(8,128)(2,1)S(1)}, bf16[192,512]{1,0:T(8,128)(2,1)S(1)}, u32[]{:S(2)}, u32[]{:S(2)}) %collective-permute-start.10) | collective-permute-done | bytes 196640 | tf_op jit(solution)/shard_map/ppermute | solution.py:292
  44.7 3.1 %collective-permute-start.11 = (bf16[192,512]{1,0:T(8,128)(2,1)S(1)}, bf16[192,512]{1,0:T(8,128)(2,1)S(1)}, u32[]{:S(2)}, u32[]{:S(2)}) collective-permute-start(bf16[192,512]{1,0:T(8,128)(2,1)S(1)} %shard_map.132), channel_id=1, source_target_pairs={{0,6},{2,4},{4,2},{6,0},{1,7},{3,5},{5,3},{7,1},{8,14},{10,12},{12... | collective-permute-start | bytes 589832 | tf_op jit(solution)/shard_map/ppermute | solution.py:292
  47.8 4.5 %collective-permute-done.11.refs_6_ = bf16[192,512]{1,0:T(8,128)(2,1)S(1)} collective-permute-done((bf16[192,512]{1,0:T(8,128)(2,1)S(1)}, bf16[192,512]{1,0:T(8,128)(2,1)S(1)}, u32[]{:S(2)}, u32[]{:S(2)}) %collective-permute-start.11) | collective-permute-done | bytes 196640 | tf_op jit(solution)/shard_map/ppermute | solution.py:292
  52.3 0.7 shard_map.133.refs_0_.refs_2_
  53.0 1.2 %collective-permute-start.12 = (bf16[256,512]{1,0:T(8,128)(2,1)S(1)}, bf16[256,512]{1,0:T(8,128)(2,1)S(1)}, u32[]{:S(2)}, u32[]{:S(2)}) collective-permute-start(bf16[256,512]{1,0:T(8,128)(2,1)S(1)} %shard_map.133.refs_0_.refs_2_), channel_id=1, source_target_pairs={{0,1},{1,0},{2,3},{3,2},{4,5},{5,4},{6,7},{7,6},{8,9},{9,8},{10,11... | collective-permute-start | bytes 786440 | tf_op jit(solution)/shard_map/ppermute | solution.py:292
  54.3 1.5 %collective-permute-start.14 = (bf16[256,512]{1,0:T(8,128)(2,1)S(1)}, bf16[256,512]{1,0:T(8,128)(2,1)S(1)}, u32[]{:S(2)}, u32[]{:S(2)}) collective-permute-start(bf16[256,512]{1,0:T(8,128)(2,1)S(1)} %shard_map.133.refs_0_.refs_2_), channel_id=1, source_target_pairs={{0,16},{1,17},{8,0},{9,1},{16,24},{17,25},{24,8},{25,9},{2,18},{3,... | collective-permute-start | bytes 786440 | tf_op jit(solution)/shard_map/ppermute | solution.py:427
  55.7 0.7 collective-permute-start.15
  56.4 3.0 %collective-permute-done.12.refs_0_.refs_1_ = bf16[256,512]{1,0:T(8,128)(2,1)S(1)} collective-permute-done((bf16[256,512]{1,0:T(8,128)(2,1)S(1)}, bf16[256,512]{1,0:T(8,128)(2,1)S(1)}, u32[]{:S(2)}, u32[]{:S(2)}) %collective-permute-start.12) | collective-permute-done | bytes 262176 | tf_op jit(solution)/shard_map/ppermute | solution.py:292
  59.5 0.2 collective-permute-done.14.refs_2_
  59.6 2.8 %collective-permute-done.15.refs_3_ = bf16[256,512]{1,0:T(8,128)(2,1)S(1)} collective-permute-done((bf16[256,512]{1,0:T(8,128)(2,1)S(1)}, bf16[256,512]{1,0:T(8,128)(2,1)S(1)}, u32[]{:S(2)}, u32[]{:S(2)}) %collective-permute-start.15) | collective-permute-done | bytes 262176 | tf_op jit(solution)/shard_map/ppermute | solution.py:427
  62.5 0.4 collective-permute-start.16
  62.9 0.7 shard_map.135.refs_2_
  63.6 0.5 collective-permute-done.16.refs_1_
  64.1 0.1 shard_map.136
  64.1 2.2 %collective-permute-start.17 = (bf16[256,512]{1,0:T(8,128)(2,1)S(1)}, bf16[256,512]{1,0:T(8,128)(2,1)S(1)}, u32[]{:S(2)}, u32[]{:S(2)}) collective-permute-start(bf16[256,512]{1,0:T(8,128)(2,1)S(1)} %get-tuple-element.49), channel_id=1, source_target_pairs={{0,8},{8,0},{16,24},{24,16},{1,9},{9,1},{17,25},{25,17},{2,10},{10... | collective-permute-start | bytes 786440 | tf_op jit(solution)/shard_map/ppermute | solution.py:292
  66.4 1.2 %collective-permute-done.17.refs_1_ = bf16[256,512]{1,0:T(8,128)(2,1)S(1)} collective-permute-done((bf16[256,512]{1,0:T(8,128)(2,1)S(1)}, bf16[256,512]{1,0:T(8,128)(2,1)S(1)}, u32[]{:S(2)}, u32[]{:S(2)}) %collective-permute-start.17) | collective-permute-done | bytes 262176 | tf_op jit(solution)/shard_map/ppermute | solution.py:292
  67.5 0.1 shard_map.138
  67.6 0.9 %collective-permute-start.18 = (bf16[256,128]{1,0:T(8,128)(2,1)S(1)}, bf16[256,128]{1,0:T(8,128)(2,1)S(1)}, u32[]{:S(2)}, u32[]{:S(2)}) collective-permute-start(bf16[256,128]{1,0:T(8,128)(2,1)S(1)} %get-tuple-element.51), channel_id=1, source_target_pairs={{0,1},{1,0},{8,9},{9,8},{16,17},{17,16},{24,25},{25,24},{2,3},{3,2... | collective-permute-start | bytes 196616 | tf_op jit(solution)/shard_map/ppermute | solution.py:476
  68.6 2.5 %collective-permute-start.19 = (bf16[256,128]{1,0:T(8,128)(2,1)S(1)}, bf16[256,128]{1,0:T(8,128)(2,1)S(1)}, u32[]{:S(2)}, u32[]{:S(2)}) collective-permute-start(bf16[256,128]{1,0:T(8,128)(2,1)S(1)} %get-tuple-element.52), channel_id=1, source_target_pairs={{0,16},{1,17},{8,24},{9,25},{16,0},{17,1},{24,8},{25,9},{2,18},{3,... | collective-permute-start | bytes 196616 | tf_op jit(solution)/shard_map/ppermute | solution.py:476
  71.1 0.1 collective-permute-start.20
  71.2 0.7 shard_map.137
  71.9 0.1 collective-permute-done.18
  72.1 1.4 %collective-permute-done.19 = bf16[256,128]{1,0:T(8,128)(2,1)S(1)} collective-permute-done((bf16[256,128]{1,0:T(8,128)(2,1)S(1)}, bf16[256,128]{1,0:T(8,128)(2,1)S(1)}, u32[]{:S(2)}, u32[]{:S(2)}) %collective-permute-start.19) | collective-permute-done | bytes 65568 | tf_op jit(solution)/shard_map/ppermute | solution.py:476
  73.5 2.8 %collective-permute-done.20 = bf16[256,128]{1,0:T(8,128)(2,1)S(1)} collective-permute-done((bf16[256,128]{1,0:T(8,128)(2,1)S(1)}, bf16[256,128]{1,0:T(8,128)(2,1)S(1)}, u32[]{:S(2)}, u32[]{:S(2)}) %collective-permute-start.20) | collective-permute-done | bytes 65568 | tf_op jit(solution)/shard_map/ppermute | solution.py:476
  76.3 0.7 add_convert_fusion.1
  (31 shorter events, 0.3 us)
Async XLA Ops:
  0.6 1.0 %copy-start.1 = (bf16[1,256,1024]{2,1,0:T(8,128)(2,1)S(1)}, bf16[1,256,1024]{2,1,0:T(8,128)(2,1)}, u32[]{:S(2)}) copy-start(bf16[1,256,1024]{2,1,0:T(8,128)(2,1)} %param.11) | copy-start | bytes 1572868
  0.6 1.0 %copy-start.4 = (s32[1,256,2]{1,2,0:T(2,128)S(1)}, s32[1,256,2]{1,2,0:T(2,128)}, u32[]{:S(2)}) copy-start(s32[1,256,2]{1,2,0:T(2,128)} %param.12) | copy-start | bytes 6148
  0.6 1.0 %copy-start.8 = (f32[1,1024]{1,0:T(1,128)S(1)}, f32[1,1024]{1,0:T(1,128)}, u32[]{:S(2)}) copy-start(f32[1,1024]{1,0:T(1,128)} %refs_2_.2) | copy-start | bytes 12292
  2.6 13.3 %collective-permute-start = (bf16[192,512]{1,0:T(8,128)(2,1)S(1)}, bf16[192,512]{1,0:T(8,128)(2,1)S(1)}, u32[]{:S(2)}, u32[]{:S(2)}) collective-permute-start(bf16[192,512]{1,0:T(8,128)(2,1)S(1)} %get-tuple-element.31), channel_id=1, source_target_pairs={{0,4},{2,6},{4,0},{6,2},{1,5},{3,7},{5,1},{7,3},{8,12},{10,14},{12... | collective-permute-start | bytes 589832 | tf_op jit(solution)/shard_map/ppermute | solution.py:292
  6.7 20.5 %collective-permute-start.2 = (bf16[192,1024]{1,0:T(8,128)(2,1)S(1)}, bf16[192,1024]{1,0:T(8,128)(2,1)S(1)}, u32[]{:S(2)}, u32[]{:S(2)}) collective-permute-start(bf16[192,1024]{1,0:T(8,128)(2,1)S(1)} %get-tuple-element.35), channel_id=1, source_target_pairs={{0,2},{2,0},{4,6},{6,4},{1,3},{3,1},{5,7},{7,5},{8,10},{10,8},{12,... | collective-permute-start | bytes 1179656 | tf_op jit(solution)/shard_map/ppermute | solution.py:292
  8.2 12.7 %copy-start.2 = (bf16[1,256,512]{2,1,0:T(8,128)(2,1)S(1)}, bf16[1,256,512]{2,1,0:T(8,128)(2,1)}, u32[]{:S(2)}) copy-start(bf16[1,256,512]{2,1,0:T(8,128)(2,1)} %param.21) | copy-start | bytes 786436
  8.2 12.7 %copy-start.5 = (f32[1,256,2]{1,2,0:T(2,128)S(1)}, f32[1,256,2]{1,2,0:T(2,128)}, u32[]{:S(2)}) copy-start(f32[1,256,2]{1,2,0:T(2,128)} %param.13) | copy-start | bytes 6148
  12.9 8.7 %collective-permute-start.1 = (bf16[192,512]{1,0:T(8,128)(2,1)S(1)}, bf16[192,512]{1,0:T(8,128)(2,1)S(1)}, u32[]{:S(2)}, u32[]{:S(2)}) collective-permute-start(bf16[192,512]{1,0:T(8,128)(2,1)S(1)} %get-tuple-element.30.refs_0_), channel_id=1, source_target_pairs={{0,1},{1,0},{2,3},{3,2},{4,5},{5,4},{6,7},{7,6},{8,9},{9,8},{10,11... | collective-permute-start | bytes 589832 | tf_op jit(solution)/shard_map/ppermute | solution.py:292
  15.9 7.3 %collective-permute-start.3 = (bf16[192,512]{1,0:T(8,128)(2,1)S(1)}, bf16[192,512]{1,0:T(8,128)(2,1)S(1)}, u32[]{:S(2)}, u32[]{:S(2)}) collective-permute-start(bf16[192,512]{1,0:T(8,128)(2,1)S(1)} %shard_map.125.refs_4_.refs_0_), channel_id=1, source_target_pairs={{0,1},{1,0},{2,3},{3,2},{4,5},{5,4},{6,7},{7,6},{8,9},{9,8},{10,11... | collective-permute-start | bytes 589832 | tf_op jit(solution)/shard_map/ppermute | solution.py:292
  17.5 9.2 %collective-permute-start.8 = (bf16[192,512]{1,0:T(8,128)(2,1)S(1)}, bf16[192,512]{1,0:T(8,128)(2,1)S(1)}, u32[]{:S(2)}, u32[]{:S(2)}) collective-permute-start(bf16[192,512]{1,0:T(8,128)(2,1)S(1)} %get-tuple-element.42), channel_id=1, source_target_pairs={{0,6},{2,4},{4,2},{6,0},{1,7},{3,5},{5,3},{7,1},{8,14},{10,12},{12... | collective-permute-start | bytes 589832 | tf_op jit(solution)/shard_map/ppermute | solution.py:292
  25.0 7.9 %collective-permute-start.6 = (bf16[192,512]{1,0:T(8,128)(2,1)S(1)}, bf16[192,512]{1,0:T(8,128)(2,1)S(1)}, u32[]{:S(2)}, u32[]{:S(2)}) collective-permute-start(bf16[192,512]{1,0:T(8,128)(2,1)S(1)} %get-tuple-element.38.refs_3_), channel_id=1, source_target_pairs={{0,1},{1,0},{2,3},{3,2},{4,5},{5,4},{6,7},{7,6},{8,9},{9,8},{10,11... | collective-permute-start | bytes 589832 | tf_op jit(solution)/shard_map/ppermute | solution.py:292
  26.6 10.5 %collective-permute-start.9 = (bf16[192,512]{1,0:T(8,128)(2,1)S(1)}, bf16[192,512]{1,0:T(8,128)(2,1)S(1)}, u32[]{:S(2)}, u32[]{:S(2)}) collective-permute-start(bf16[192,512]{1,0:T(8,128)(2,1)S(1)} %collective-permute-done.8.refs_0_), channel_id=1, source_target_pairs={{0,1},{1,0},{2,3},{3,2},{4,5},{5,4},{6,7},{7,6},{8,9},{9,8},{10,11... | collective-permute-start | bytes 589832 | tf_op jit(solution)/shard_map/ppermute | solution.py:292
  29.0 11.9 %collective-permute-start.4 = (bf16[192,512]{1,0:T(8,128)(2,1)S(1)}, bf16[192,512]{1,0:T(8,128)(2,1)S(1)}, u32[]{:S(2)}, u32[]{:S(2)}) collective-permute-start(bf16[192,512]{1,0:T(8,128)(2,1)S(1)} %get-tuple-element.40.refs_4_), channel_id=1, source_target_pairs={{0,1},{1,0},{2,3},{3,2},{4,5},{5,4},{6,7},{7,6},{8,9},{9,8},{10,11... | collective-permute-start | bytes 589832 | tf_op jit(solution)/shard_map/ppermute | solution.py:292
  33.0 14.8 %collective-permute-start.7 = (bf16[192,512]{1,0:T(8,128)(2,1)S(1)}, bf16[192,512]{1,0:T(8,128)(2,1)S(1)}, u32[]{:S(2)}, u32[]{:S(2)}) collective-permute-start(bf16[192,512]{1,0:T(8,128)(2,1)S(1)} %shard_map.130.refs_5_), channel_id=1, source_target_pairs={{0,4},{2,6},{4,0},{6,2},{1,5},{3,7},{5,1},{7,3},{8,12},{10,14},{12... | collective-permute-start | bytes 589832 | tf_op jit(solution)/shard_map/ppermute | solution.py:292
  38.9 24.0 %copy-start = (bf16[1,1024,512]{2,1,0:T(8,128)(2,1)S(1)}, bf16[1,1024,512]{2,1,0:T(8,128)(2,1)}, u32[]{:S(2)}) copy-start(bf16[1,1024,512]{2,1,0:T(8,128)(2,1)} %param.18) | copy-start | bytes 3145732
  38.9 24.0 %copy-start.3 = (f32[1,1024]{1,0:T(1,128)S(1)}, f32[1,1024]{1,0:T(1,128)}, u32[]{:S(2)}) copy-start(f32[1,1024]{1,0:T(1,128)} %refs_2_.3) | copy-start | bytes 12292
  38.9 25.2 %copy-start.6 = (bf16[1,1024,512]{2,1,0:T(8,128)(2,1)S(1)}, bf16[1,1024,512]{2,1,0:T(8,128)(2,1)}, u32[]{:S(2)}) copy-start(bf16[1,1024,512]{2,1,0:T(8,128)(2,1)} %param.19) | copy-start | bytes 3145732
  38.9 25.1 %copy-start.7 = (bf16[1,1024,512]{2,1,0:T(8,128)(2,1)S(1)}, bf16[1,1024,512]{2,1,0:T(8,128)(2,1)}, u32[]{:S(2)}) copy-start(bf16[1,1024,512]{2,1,0:T(8,128)(2,1)} %param.20) | copy-start | bytes 3145732
  39.0 5.7 %collective-permute-start.10 = (bf16[192,512]{1,0:T(8,128)(2,1)S(1)}, bf16[192,512]{1,0:T(8,128)(2,1)S(1)}, u32[]{:S(2)}, u32[]{:S(2)}) collective-permute-start(bf16[192,512]{1,0:T(8,128)(2,1)S(1)} %get-tuple-element.44), channel_id=1, source_target_pairs={{0,1},{1,0},{2,3},{3,2},{4,5},{5,4},{6,7},{7,6},{8,9},{9,8},{10,11... | collective-permute-start | bytes 589832 | tf_op jit(solution)/shard_map/ppermute | solution.py:292
  40.9 6.9 %collective-permute-start.5 = (bf16[192,512]{1,0:T(8,128)(2,1)S(1)}, bf16[192,512]{1,0:T(8,128)(2,1)S(1)}, u32[]{:S(2)}, u32[]{:S(2)}) collective-permute-start(bf16[192,512]{1,0:T(8,128)(2,1)S(1)} %add_convert_fusion), channel_id=1, source_target_pairs={{0,2},{2,0},{4,6},{6,4},{1,3},{3,1},{5,7},{7,5},{8,10},{10,8},{12,... | collective-permute-start | bytes 589832 | tf_op jit(solution)/shard_map/ppermute | solution.py:292
  44.7 7.6 %collective-permute-start.11 = (bf16[192,512]{1,0:T(8,128)(2,1)S(1)}, bf16[192,512]{1,0:T(8,128)(2,1)S(1)}, u32[]{:S(2)}, u32[]{:S(2)}) collective-permute-start(bf16[192,512]{1,0:T(8,128)(2,1)S(1)} %shard_map.132), channel_id=1, source_target_pairs={{0,6},{2,4},{4,2},{6,0},{1,7},{3,5},{5,3},{7,1},{8,14},{10,12},{12... | collective-permute-start | bytes 589832 | tf_op jit(solution)/shard_map/ppermute | solution.py:292
  53.0 6.4 %collective-permute-start.12 = (bf16[256,512]{1,0:T(8,128)(2,1)S(1)}, bf16[256,512]{1,0:T(8,128)(2,1)S(1)}, u32[]{:S(2)}, u32[]{:S(2)}) collective-permute-start(bf16[256,512]{1,0:T(8,128)(2,1)S(1)} %shard_map.133.refs_0_.refs_2_), channel_id=1, source_target_pairs={{0,1},{1,0},{2,3},{3,2},{4,5},{5,4},{6,7},{7,6},{8,9},{9,8},{10,11... | collective-permute-start | bytes 786440 | tf_op jit(solution)/shard_map/ppermute | solution.py:292
  54.3 5.2 %collective-permute-start.13 = (bf16[256,512]{1,0:T(8,128)(2,1)S(1)}, bf16[256,512]{1,0:T(8,128)(2,1)S(1)}, u32[]{:S(2)}, u32[]{:S(2)}) collective-permute-start(bf16[256,512]{1,0:T(8,128)(2,1)S(1)} %shard_map.133.refs_0_.refs_2_), channel_id=1, source_target_pairs={{0,8},{8,0},{16,24},{24,16},{1,9},{9,1},{17,25},{25,17},{2,10},{10... | collective-permute-start | bytes 786440 | tf_op jit(solution)/shard_map/ppermute | solution.py:292
  54.3 5.4 %collective-permute-start.14 = (bf16[256,512]{1,0:T(8,128)(2,1)S(1)}, bf16[256,512]{1,0:T(8,128)(2,1)S(1)}, u32[]{:S(2)}, u32[]{:S(2)}) collective-permute-start(bf16[256,512]{1,0:T(8,128)(2,1)S(1)} %shard_map.133.refs_0_.refs_2_), channel_id=1, source_target_pairs={{0,16},{1,17},{8,0},{9,1},{16,24},{17,25},{24,8},{25,9},{2,18},{3,... | collective-permute-start | bytes 786440 | tf_op jit(solution)/shard_map/ppermute | solution.py:427
  55.7 6.7 %collective-permute-start.15 = (bf16[256,512]{1,0:T(8,128)(2,1)S(1)}, bf16[256,512]{1,0:T(8,128)(2,1)S(1)}, u32[]{:S(2)}, u32[]{:S(2)}) collective-permute-start(bf16[256,512]{1,0:T(8,128)(2,1)S(1)} %shard_map.133.refs_0_.refs_2_), channel_id=1, source_target_pairs={{0,25},{1,24},{8,0},{9,1},{16,8},{17,9},{24,16},{25,17},{2,27},{3,... | collective-permute-start | bytes 786440 | tf_op jit(solution)/shard_map/ppermute | solution.py:427
  62.5 1.6 %collective-permute-start.16 = (bf16[256,512]{1,0:T(8,128)(2,1)S(1)}, bf16[256,512]{1,0:T(8,128)(2,1)S(1)}, u32[]{:S(2)}, u32[]{:S(2)}) collective-permute-start(bf16[256,512]{1,0:T(8,128)(2,1)S(1)} %shard_map.134.refs_0_), channel_id=1, source_target_pairs={{0,8},{8,0},{16,24},{24,16},{1,9},{9,1},{17,25},{25,17},{2,10},{10... | collective-permute-start | bytes 786440 | tf_op jit(solution)/shard_map/ppermute | solution.py:292
  64.1 3.4 %collective-permute-start.17 = (bf16[256,512]{1,0:T(8,128)(2,1)S(1)}, bf16[256,512]{1,0:T(8,128)(2,1)S(1)}, u32[]{:S(2)}, u32[]{:S(2)}) collective-permute-start(bf16[256,512]{1,0:T(8,128)(2,1)S(1)} %get-tuple-element.49), channel_id=1, source_target_pairs={{0,8},{8,0},{16,24},{24,16},{1,9},{9,1},{17,25},{25,17},{2,10},{10... | collective-permute-start | bytes 786440 | tf_op jit(solution)/shard_map/ppermute | solution.py:292
  67.6 4.4 %collective-permute-start.18 = (bf16[256,128]{1,0:T(8,128)(2,1)S(1)}, bf16[256,128]{1,0:T(8,128)(2,1)S(1)}, u32[]{:S(2)}, u32[]{:S(2)}) collective-permute-start(bf16[256,128]{1,0:T(8,128)(2,1)S(1)} %get-tuple-element.51), channel_id=1, source_target_pairs={{0,1},{1,0},{8,9},{9,8},{16,17},{17,16},{24,25},{25,24},{2,3},{3,2... | collective-permute-start | bytes 196616 | tf_op jit(solution)/shard_map/ppermute | solution.py:476
  68.6 4.9 %collective-permute-start.19 = (bf16[256,128]{1,0:T(8,128)(2,1)S(1)}, bf16[256,128]{1,0:T(8,128)(2,1)S(1)}, u32[]{:S(2)}, u32[]{:S(2)}) collective-permute-start(bf16[256,128]{1,0:T(8,128)(2,1)S(1)} %get-tuple-element.52), channel_id=1, source_target_pairs={{0,16},{1,17},{8,24},{9,25},{16,0},{17,1},{24,8},{25,9},{2,18},{3,... | collective-permute-start | bytes 196616 | tf_op jit(solution)/shard_map/ppermute | solution.py:476
  71.1 5.2 %collective-permute-start.20 = (bf16[256,128]{1,0:T(8,128)(2,1)S(1)}, bf16[256,128]{1,0:T(8,128)(2,1)S(1)}, u32[]{:S(2)}, u32[]{:S(2)}) collective-permute-start(bf16[256,128]{1,0:T(8,128)(2,1)S(1)} %get-tuple-element.53), channel_id=1, source_target_pairs={{0,17},{1,16},{8,25},{9,24},{16,1},{17,0},{24,9},{25,8},{2,19},{3,... | collective-permute-start | bytes 196616 | tf_op jit(solution)/shard_map/ppermute | solution.py:476

commit v14 on v13

--- a/solution.py
+++ b/solution.py
@@ -164,15 +164,17 @@
     out[...] = (kept[...] + arrived[...].astype(WIDE)).astype(LOW)
 
 
-def combine(experts, tokens, high, low, *refs):
+def combine(order, base, high, low, *refs):
     returned, out = refs[:-1], refs[-1]
-    tp = lax.axis_index("tp")
     half = out.shape[1]
-    mixed = tokens[:, part(tp, half)].astype(WIDE)
-    for k in range(experts):
-        rows = returned[k][...]
+    if base.shape[1] == half:
+        mixed = base[...]
+    else:
+        mixed = base[:, part(lax.axis_index("tp"), half)].astype(WIDE)
+    for k, block in zip(order, returned, strict=True):
+        rows = block[...]
         mixed = mixed + (matmul(high[k], rows) + matmul(low[k], rows))
-    out[...] = mixed.astype(LOW)
+    out[...] = mixed.astype(out.dtype)
 
 
 def project(mine, other, gain, weight, out):
@@ -382,7 +384,7 @@
     for k, rows in zip(groups[1], later):
         far_rows[k - 2] = rows
     arriving.append(joined(groups[1]))
-    returned = {0: total(own_away, own_kept)}
+    returned = {0: total(own_away, own_kept, plain=True)}
     arriving[0] = hold(arriving[0], [own_away])
     others = [swap(arriving[0], "tp", 1)]
     high, low, upstream = call(
@@ -396,24 +398,31 @@
     others.append(swap(arriving[1], "tp", 1))
 
     def give_back(group, away, kept):
-        mixed = total(away, kept)
+        mixed = total(away, kept, plain=True)
         for i, k in enumerate(group):
             block = mixed if len(group) == 1 else mixed[i * capacity : (i + 1) * capacity]
             returned[k] = swap(block, "exp", k)
         return mixed
 
     away, kept = through([arriving[0], others[0]], [returned[0], high])
+    mixed = give_back(groups[0], away, kept)
+    away, kept = through([arriving[1], others[1]], [mixed])
     near_away, near_kept = through([near], [away])
-    mixed = give_back(groups[0], away, kept)
-    returned[1] = swap(total(near_away, near_kept, plain=True), "exp", 1)
-    away, kept = through([arriving[1], others[1]], [near_away, mixed])
     give_back(groups[1], away, kept)
-
+    there, rest = [0, *groups[0]], [1, *groups[1]]
+    so_far, near_away = call(
+        functools.partial(combine, there),
+        [shape_of((token_count, half), WIDE)],
+        [token_rows, high, low, *(returned[k] for k in there)],
+        flops=4 * len(there) * token_count * capacity * half,
+        held=[near_away],
+    )
+    returned[1] = swap(total(near_away, near_kept), "exp", 1)
     hidden_half = call(
-        functools.partial(combine, experts),
+        functools.partial(combine, rest),
         [shape_of((token_count, half))],
-        [token_rows, high, low, *(returned[k] for k in range(experts))],
-        flops=4 * 3 * token_count * token_count * half,
+        [so_far, high, low, *(returned[k] for k in rest)],
+        flops=4 * len(rest) * token_count * capacity * half,
     )[0]
 
     hidden_other = swap(hidden_half, "tp", 1)

time: 77.1 us -> 83.7 us (1.086)
  waiting for transfers between devices: 29.9 us -> 35.1 us
  starting transfers between devices: 30.5 us -> 31.9 us
    ppermute x16, waiting for transfers between devices: 22.6 us -> 27.6 us  [swap(): return lax.ppermute(block, axis, [(i, i ^ step) for i in range(size)])]
    ppermute x16, starting transfers between devices: 24.8 us -> 26.2 us  [swap(): return lax.ppermute(block, axis, [(i, i ^ step) for i in range(size)])]
    pallas_call x17 -> x16, Pallas kernels: 13.9 us -> 14 us  [call(): pl.pallas_call(run, out_shape=[*out_shape, *(shape_of(x.shape, x.dtype) f...]
  transfers between devices with their start and end apart: 21 -> 21, of which waited for: 15 -> 16; matrix products, arithmetic and copies ran while one was open for 0% -> 0% of each run, Pallas kernels for 16% -> 15%
where the time goes in v14:
time: 83.7 us; the launch traced here: 83.6 us
  waiting for transfers between devices  35.1 us (42%)
  starting transfers between devices  31.9 us (38%)
  Pallas kernels  14 us (17%)
  local copies, waits for them, and re-layouts  1.02 us (1%)
    ppermute x16, waiting for transfers between devices, swap(): return lax.ppermute(block, axis, [(i, i ^ step) for i in range(size)])  27.6 us
    ppermute x16, starting transfers between devices, swap(): return lax.ppermute(block, axis, [(i, i ^ step) for i in range(size)])  26.2 us
    pallas_call x16, Pallas kernels, call(): pl.pallas_call(run, out_shape=[*out_shape, *(shape_of(x.shape, x.dtype) f...  14 us
    ppermute x3, waiting for transfers between devices, shards(): total = total + lax.ppermute(blocks[k], ('sec', 'tp'), pairs).astype(WIDE)  4.3 us
    ppermute x3, starting transfers between devices, shards(): total = total + lax.ppermute(blocks[k], ('sec', 'tp'), pairs).astype(WIDE)  3.63 us
    ppermute x2, waiting for transfers between devices, cycle(): return lax.ppermute(hidden_half, ('sec', 'tp'), list(targets.items()))  3.14 us
    ppermute x2, starting transfers between devices, cycle(): return lax.ppermute(hidden_half, ('sec', 'tp'), list(targets.items()))  2 us
  transfers between devices with their start and end apart: 21, of which 16 were waited for; matrix products, arithmetic and copies ran while one was open for 0% of the time, Pallas kernels for 15%

profile of v14, /device:TPU:0, one launch (start us, length us, event | category | flops | bytes accessed | tf_op | source)
XLA Modules:
  0.0 83.6 jit_solution(2760600609851407448)
XLA Ops:
  0.7 1.0 %copy-done.1 = bf16[1,256,1024]{2,1,0:T(8,128)(2,1)S(1)} copy-done((bf16[1,256,1024]{2,1,0:T(8,128)(2,1)S(1)}, bf16[1,256,1024]{2,1,0:T(8,128)(2,1)}, u32[]{:S(2)}) %copy-start.1) | copy-done | bytes 524312
  1.7 0.9 %shard_map.123 = (bf16[192,512]{1,0:T(8,128)(2,1)S(1)}, bf16[192,512]{1,0:T(8,128)(2,1)S(1)}, bf16[192,1024]{1,0:T(8,128)(2,1)S(1)}, bf16[192,1024]{1,0:T(8,128)(2,1)S(1)}) custom-call(bf16[256,1024]{1,0:T(8,128)(2,1)S(1)} %bitcast.15, s32[2,256]{1,0:T(2,128)S(1)} %bitcast.18, f32[1,1024]{1,0:T(1,128)S(1)} %copy-done.8, ...), custom_call_target="tpu_custom_call" | custom-call | flops 402653184 | bytes 1841152 | tf_op jit(solution)/shard_map/pallas_call | solution.py:40
  2.6 4.1 %collective-permute-start = (bf16[192,512]{1,0:T(8,128)(2,1)S(1)}, bf16[192,512]{1,0:T(8,128)(2,1)S(1)}, u32[]{:S(2)}, u32[]{:S(2)}) collective-permute-start(bf16[192,512]{1,0:T(8,128)(2,1)S(1)} %get-tuple-element.33), channel_id=1, source_target_pairs={{0,4},{2,6},{4,0},{6,2},{1,5},{3,7},{5,1},{7,3},{8,12},{10,14},{12... | collective-permute-start | bytes 589832 | tf_op jit(solution)/shard_map/ppermute | solution.py:294
  6.7 4.6 %shard_map.124 = (bf16[192,512]{1,0:T(8,128)(2,1)S(1)}, f32[192,512]{1,0:T(8,128)S(1)}, bf16[1024,2048]{1,0:T(8,128)(2,1)S(1)}, bf16[2048,1024]{1,0:T(8,128)(2,1)S(1)}, bf16[192,512]{1,0:T(8,128)(2,1)S(1)}) custom-call(bf16[192,1024]{1,0:T(8,128)(2,1)S(1)} %get-tuple-element.30.refs_0_, ...), custom_call_target="tpu_custom_call", output_to_operand_aliasing={{4}: (3, {})} | custom-call | flops 1610612736 | bytes 17760256 | tf_op jit(solution)/shard_map/pallas_call | solution.py:40
  11.3 1.6 %collective-permute-start.1 = (bf16[192,512]{1,0:T(8,128)(2,1)S(1)}, bf16[192,512]{1,0:T(8,128)(2,1)S(1)}, u32[]{:S(2)}, u32[]{:S(2)}) collective-permute-start(bf16[192,512]{1,0:T(8,128)(2,1)S(1)} %get-tuple-element.32.refs_0_), channel_id=1, source_target_pairs={{0,1},{1,0},{2,3},{3,2},{4,5},{5,4},{6,7},{7,6},{8,9},{9,8},{10,11... | collective-permute-start | bytes 589832 | tf_op jit(solution)/shard_map/ppermute | solution.py:294
  12.9 1.4 %collective-permute-start.6 = (bf16[192,512]{1,0:T(8,128)(2,1)S(1)}, bf16[192,512]{1,0:T(8,128)(2,1)S(1)}, u32[]{:S(2)}, u32[]{:S(2)}) collective-permute-start(bf16[192,512]{1,0:T(8,128)(2,1)S(1)} %get-tuple-element.42), channel_id=1, source_target_pairs={{0,6},{2,4},{4,2},{6,0},{1,7},{3,5},{5,3},{7,1},{8,14},{10,12},{12... | collective-permute-start | bytes 589832 | tf_op jit(solution)/shard_map/ppermute | solution.py:294
  14.2 1.6 %collective-permute-done.refs_1_ = bf16[192,512]{1,0:T(8,128)(2,1)S(1)} collective-permute-done((bf16[192,512]{1,0:T(8,128)(2,1)S(1)}, bf16[192,512]{1,0:T(8,128)(2,1)S(1)}, u32[]{:S(2)}, u32[]{:S(2)}) %collective-permute-start) | collective-permute-done | bytes 196640 | tf_op jit(solution)/shard_map/ppermute | solution.py:294
  15.8 6.8 %collective-permute-start.2 = (bf16[192,512]{1,0:T(8,128)(2,1)S(1)}, bf16[192,512]{1,0:T(8,128)(2,1)S(1)}, u32[]{:S(2)}, u32[]{:S(2)}) collective-permute-start(bf16[192,512]{1,0:T(8,128)(2,1)S(1)} %shard_map.125.refs_4_.refs_0_), channel_id=1, source_target_pairs={{0,1},{1,0},{2,3},{3,2},{4,5},{5,4},{6,7},{7,6},{8,9},{9,8},{10,11... | collective-permute-start | bytes 589832 | tf_op jit(solution)/shard_map/ppermute | solution.py:294
  22.6 0.6 shard_map.126
  23.3 4.8 %collective-permute-done.2.refs_1_ = bf16[192,512]{1,0:T(8,128)(2,1)S(1)} collective-permute-done((bf16[192,512]{1,0:T(8,128)(2,1)S(1)}, bf16[192,512]{1,0:T(8,128)(2,1)S(1)}, u32[]{:S(2)}, u32[]{:S(2)}) %collective-permute-start.2) | collective-permute-done | bytes 196640 | tf_op jit(solution)/shard_map/ppermute | solution.py:294
  28.0 1.8 %shard_map.127 = (bf16[192,512]{1,0:T(8,128)(2,1)S(1)}, f32[192,512]{1,0:T(8,128)S(1)}) custom-call(bf16[192,512]{1,0:T(8,128)(2,1)S(1)} %shard_map.125.refs_4_.refs_0_, bf16[192,512]{1,0:T(8,128)(2,1)S(1)} %collective-permute-done.2.refs_1_, bf16[1024,2048]{1,0:T(8,128)(2,1)S(1)} %get-tuple-element.37.refs_2_.refs_1_, ...), custom_call_target="tpu_custom_call" | custom-call | flops 1610612736 | bytes 9371648 | tf_op jit(solution)/shard_map/pallas_call | solution.py:40
  29.9 2.2 %collective-permute-start.3 = (bf16[192,512]{1,0:T(8,128)(2,1)S(1)}, bf16[192,512]{1,0:T(8,128)(2,1)S(1)}, u32[]{:S(2)}, u32[]{:S(2)}) collective-permute-start(bf16[192,512]{1,0:T(8,128)(2,1)S(1)} %get-tuple-element.40), channel_id=1, source_target_pairs={{0,1},{1,0},{2,3},{3,2},{4,5},{5,4},{6,7},{7,6},{8,9},{9,8},{10,11... | collective-permute-start | bytes 589832 | tf_op jit(solution)/shard_map/ppermute | solution.py:294
  32.0 0.2 collective-permute-start.7
  32.2 4.1 %collective-permute-done.3 = bf16[192,512]{1,0:T(8,128)(2,1)S(1)} collective-permute-done((bf16[192,512]{1,0:T(8,128)(2,1)S(1)}, bf16[192,512]{1,0:T(8,128)(2,1)S(1)}, u32[]{:S(2)}, u32[]{:S(2)}) %collective-permute-start.3) | collective-permute-done | bytes 196640 | tf_op jit(solution)/shard_map/ppermute | solution.py:294
  36.3 0.1 collective-permute-start.4
  36.4 2.0 %collective-permute-done.7.refs_1_ = bf16[192,512]{1,0:T(8,128)(2,1)S(1)} collective-permute-done((bf16[192,512]{1,0:T(8,128)(2,1)S(1)}, bf16[192,512]{1,0:T(8,128)(2,1)S(1)}, u32[]{:S(2)}, u32[]{:S(2)}) %collective-permute-start.7) | collective-permute-done | bytes 196640 | tf_op jit(solution)/shard_map/ppermute | solution.py:294
  38.4 1.8 %shard_map.128 = (bf16[192,512]{1,0:T(8,128)(2,1)S(1)}, f32[192,512]{1,0:T(8,128)S(1)}) custom-call(bf16[192,512]{1,0:T(8,128)(2,1)S(1)} %collective-permute-done.6.refs_0_, bf16[192,512]{1,0:T(8,128)(2,1)S(1)} %collective-permute-done.7.refs_1_, bf16[1024,2048]{1,0:T(8,128)(2,1)S(1)} %get-tuple-element.37.refs_2_.refs_1_, ...), custom_call_target="tpu_custom_call" | custom-call | flops 1610612736 | bytes 9371648 | tf_op jit(solution)/shard_map/pallas_call | solution.py:40
  40.2 1.7 %collective-permute-start.10 = (bf16[192,512]{1,0:T(8,128)(2,1)S(1)}, bf16[192,512]{1,0:T(8,128)(2,1)S(1)}, u32[]{:S(2)}, u32[]{:S(2)}) collective-permute-start(bf16[192,512]{1,0:T(8,128)(2,1)S(1)} %get-tuple-element.43.refs_3_), channel_id=1, source_target_pairs={{0,1},{1,0},{2,3},{3,2},{4,5},{5,4},{6,7},{7,6},{8,9},{9,8},{10,11... | collective-permute-start | bytes 589832 | tf_op jit(solution)/shard_map/ppermute | solution.py:294
  41.9 1.8 %shard_map.129 = (bf16[192,512]{1,0:T(8,128)(2,1)S(1)}, f32[192,512]{1,0:T(8,128)S(1)}) custom-call(bf16[192,1024]{1,0:T(8,128)(2,1)S(1)} %collective-permute-done.5.refs_0_, bf16[1024,2048]{1,0:T(8,128)(2,1)S(1)} %get-tuple-element.37.refs_2_.refs_1_, bf16[2048,1024]{1,0:T(8,128)(2,1)S(1)} %get-tuple-element.38.refs_3_.refs_2_, ...), custom_call_target="tpu_custom_call" | custom-call | flops 1610612736 | bytes 9371648 | tf_op jit(solution)/shard_map/pallas_call | solution.py:40
  43.8 2.9 %collective-permute-done.4.refs_4_ = bf16[192,512]{1,0:T(8,128)(2,1)S(1)} collective-permute-done((bf16[192,512]{1,0:T(8,128)(2,1)S(1)}, bf16[192,512]{1,0:T(8,128)(2,1)S(1)}, u32[]{:S(2)}, u32[]{:S(2)}) %collective-permute-start.4) | collective-permute-done | bytes 196640 | tf_op jit(solution)/shard_map/ppermute | solution.py:294
  46.7 0.4 shard_map.130
  47.1 1.0 %collective-permute-start.8 = (bf16[192,512]{1,0:T(8,128)(2,1)S(1)}, bf16[192,512]{1,0:T(8,128)(2,1)S(1)}, u32[]{:S(2)}, u32[]{:S(2)}) collective-permute-start(bf16[192,512]{1,0:T(8,128)(2,1)S(1)} %get-tuple-element.47), channel_id=1, source_target_pairs={{0,1},{1,0},{2,3},{3,2},{4,5},{5,4},{6,7},{7,6},{8,9},{9,8},{10,11... | collective-permute-start | bytes 589832 | tf_op jit(solution)/shard_map/ppermute | solution.py:294
  48.2 3.1 %collective-permute-start.11 = (bf16[192,512]{1,0:T(8,128)(2,1)S(1)}, bf16[192,512]{1,0:T(8,128)(2,1)S(1)}, u32[]{:S(2)}, u32[]{:S(2)}) collective-permute-start(bf16[192,512]{1,0:T(8,128)(2,1)S(1)} %add_convert_fusion), channel_id=1, source_target_pairs={{0,6},{2,4},{4,2},{6,0},{1,7},{3,5},{5,3},{7,1},{8,14},{10,12},{12... | collective-permute-start | bytes 589832 | tf_op jit(solution)/shard_map/ppermute | solution.py:294
  51.3 1.5 %collective-permute-done.8.refs_1_ = bf16[192,512]{1,0:T(8,128)(2,1)S(1)} collective-permute-done((bf16[192,512]{1,0:T(8,128)(2,1)S(1)}, bf16[192,512]{1,0:T(8,128)(2,1)S(1)}, u32[]{:S(2)}, u32[]{:S(2)}) %collective-permute-start.8) | collective-permute-done | bytes 196640 | tf_op jit(solution)/shard_map/ppermute | solution.py:294
  52.9 0.1 collective-permute-start.9
  53.0 4.0 %collective-permute-done.11.refs_4_ = bf16[192,512]{1,0:T(8,128)(2,1)S(1)} collective-permute-done((bf16[192,512]{1,0:T(8,128)(2,1)S(1)}, bf16[192,512]{1,0:T(8,128)(2,1)S(1)}, u32[]{:S(2)}, u32[]{:S(2)}) %collective-permute-start.11) | collective-permute-done | bytes 196640 | tf_op jit(solution)/shard_map/ppermute | solution.py:294
  57.0 2.1 %collective-permute-done.9.refs_3_ = bf16[192,512]{1,0:T(8,128)(2,1)S(1)} collective-permute-done((bf16[192,512]{1,0:T(8,128)(2,1)S(1)}, bf16[192,512]{1,0:T(8,128)(2,1)S(1)}, u32[]{:S(2)}, u32[]{:S(2)}) %collective-permute-start.9) | collective-permute-done | bytes 196640 | tf_op jit(solution)/shard_map/ppermute | solution.py:294
  59.1 0.4 shard_map.132.refs_0_.refs_2_
  59.5 1.4 %collective-permute-start.12 = (bf16[256,512]{1,0:T(8,128)(2,1)S(1)}, bf16[256,512]{1,0:T(8,128)(2,1)S(1)}, u32[]{:S(2)}, u32[]{:S(2)}) collective-permute-start(bf16[256,512]{1,0:T(8,128)(2,1)S(1)} %shard_map.132.refs_0_.refs_2_), channel_id=1, source_target_pairs={{0,1},{1,0},{2,3},{3,2},{4,5},{5,4},{6,7},{7,6},{8,9},{9,8},{10,11... | collective-permute-start | bytes 786440 | tf_op jit(solution)/shard_map/ppermute | solution.py:294
  60.9 1.5 %collective-permute-start.14 = (bf16[256,512]{1,0:T(8,128)(2,1)S(1)}, bf16[256,512]{1,0:T(8,128)(2,1)S(1)}, u32[]{:S(2)}, u32[]{:S(2)}) collective-permute-start(bf16[256,512]{1,0:T(8,128)(2,1)S(1)} %shard_map.132.refs_0_.refs_2_), channel_id=1, source_target_pairs={{0,16},{1,17},{8,0},{9,1},{16,24},{17,25},{24,8},{25,9},{2,18},{3,... | collective-permute-start | bytes 786440 | tf_op jit(solution)/shard_map/ppermute | solution.py:436
  62.4 0.5 collective-permute-start.15
  62.9 3.0 %collective-permute-done.12.refs_0_.refs_1_ = bf16[256,512]{1,0:T(8,128)(2,1)S(1)} collective-permute-done((bf16[256,512]{1,0:T(8,128)(2,1)S(1)}, bf16[256,512]{1,0:T(8,128)(2,1)S(1)}, u32[]{:S(2)}, u32[]{:S(2)}) %collective-permute-start.12) | collective-permute-done | bytes 262176 | tf_op jit(solution)/shard_map/ppermute | solution.py:294
  65.9 0.3 collective-permute-done.14.refs_2_
  66.3 2.8 %collective-permute-done.15.refs_3_ = bf16[256,512]{1,0:T(8,128)(2,1)S(1)} collective-permute-done((bf16[256,512]{1,0:T(8,128)(2,1)S(1)}, bf16[256,512]{1,0:T(8,128)(2,1)S(1)}, u32[]{:S(2)}, u32[]{:S(2)}) %collective-permute-start.15) | collective-permute-done | bytes 262176 | tf_op jit(solution)/shard_map/ppermute | solution.py:436
  69.1 0.4 collective-permute-start.16
  69.5 0.7 shard_map.134.refs_2_
  70.2 0.5 collective-permute-done.16.refs_1_
  70.8 2.2 %collective-permute-start.17 = (bf16[256,512]{1,0:T(8,128)(2,1)S(1)}, bf16[256,512]{1,0:T(8,128)(2,1)S(1)}, u32[]{:S(2)}, u32[]{:S(2)}) collective-permute-start(bf16[256,512]{1,0:T(8,128)(2,1)S(1)} %get-tuple-element.53), channel_id=1, source_target_pairs={{0,8},{8,0},{16,24},{24,16},{1,9},{9,1},{17,25},{25,17},{2,10},{10... | collective-permute-start | bytes 786440 | tf_op jit(solution)/shard_map/ppermute | solution.py:294
  73.0 1.2 %collective-permute-done.17.refs_1_ = bf16[256,512]{1,0:T(8,128)(2,1)S(1)} collective-permute-done((bf16[256,512]{1,0:T(8,128)(2,1)S(1)}, bf16[256,512]{1,0:T(8,128)(2,1)S(1)}, u32[]{:S(2)}, u32[]{:S(2)}) %collective-permute-start.17) | collective-permute-done | bytes 262176 | tf_op jit(solution)/shard_map/ppermute | solution.py:294
  74.2 0.1 shard_map.137
  74.3 0.8 collective-permute-start.18
  75.0 2.7 %collective-permute-start.19 = (bf16[256,128]{1,0:T(8,128)(2,1)S(1)}, bf16[256,128]{1,0:T(8,128)(2,1)S(1)}, u32[]{:S(2)}, u32[]{:S(2)}) collective-permute-start(bf16[256,128]{1,0:T(8,128)(2,1)S(1)} %get-tuple-element.56), channel_id=1, source_target_pairs={{0,16},{1,17},{8,24},{9,25},{16,0},{17,1},{24,8},{25,9},{2,18},{3,... | collective-permute-start | bytes 196616 | tf_op jit(solution)/shard_map/ppermute | solution.py:485
  77.8 0.1 collective-permute-start.20
  77.9 0.7 shard_map.136
  78.6 0.1 collective-permute-done.18
  78.7 1.4 %collective-permute-done.19 = bf16[256,128]{1,0:T(8,128)(2,1)S(1)} collective-permute-done((bf16[256,128]{1,0:T(8,128)(2,1)S(1)}, bf16[256,128]{1,0:T(8,128)(2,1)S(1)}, u32[]{:S(2)}, u32[]{:S(2)}) %collective-permute-start.19) | collective-permute-done | bytes 65568 | tf_op jit(solution)/shard_map/ppermute | solution.py:485
  80.1 2.8 %collective-permute-done.20 = bf16[256,128]{1,0:T(8,128)(2,1)S(1)} collective-permute-done((bf16[256,128]{1,0:T(8,128)(2,1)S(1)}, bf16[256,128]{1,0:T(8,128)(2,1)S(1)}, u32[]{:S(2)}, u32[]{:S(2)}) %collective-permute-start.20) | collective-permute-done | bytes 65568 | tf_op jit(solution)/shard_map/ppermute | solution.py:485
  82.9 0.7 add_convert_fusion.3
  (32 shorter events, 0.3 us)
Async XLA Ops:
  0.6 1.0 %copy-start.1 = (bf16[1,256,1024]{2,1,0:T(8,128)(2,1)S(1)}, bf16[1,256,1024]{2,1,0:T(8,128)(2,1)}, u32[]{:S(2)}) copy-start(bf16[1,256,1024]{2,1,0:T(8,128)(2,1)} %param.11) | copy-start | bytes 1572868
  0.6 1.0 %copy-start.4 = (s32[1,256,2]{1,2,0:T(2,128)S(1)}, s32[1,256,2]{1,2,0:T(2,128)}, u32[]{:S(2)}) copy-start(s32[1,256,2]{1,2,0:T(2,128)} %param.12) | copy-start | bytes 6148
  0.6 1.0 %copy-start.8 = (f32[1,1024]{1,0:T(1,128)S(1)}, f32[1,1024]{1,0:T(1,128)}, u32[]{:S(2)}) copy-start(f32[1,1024]{1,0:T(1,128)} %refs_2_.2) | copy-start | bytes 12292
  2.6 13.2 %collective-permute-start = (bf16[192,512]{1,0:T(8,128)(2,1)S(1)}, bf16[192,512]{1,0:T(8,128)(2,1)S(1)}, u32[]{:S(2)}, u32[]{:S(2)}) collective-permute-start(bf16[192,512]{1,0:T(8,128)(2,1)S(1)} %get-tuple-element.33), channel_id=1, source_target_pairs={{0,4},{2,6},{4,0},{6,2},{1,5},{3,7},{5,1},{7,3},{8,12},{10,14},{12... | collective-permute-start | bytes 589832 | tf_op jit(solution)/shard_map/ppermute | solution.py:294
  6.7 15.9 %copy-start.2 = (bf16[1,256,512]{2,1,0:T(8,128)(2,1)S(1)}, bf16[1,256,512]{2,1,0:T(8,128)(2,1)}, u32[]{:S(2)}) copy-start(bf16[1,256,512]{2,1,0:T(8,128)(2,1)} %param.21) | copy-start | bytes 786436
  6.7 15.9 %copy-start.5 = (f32[1,256,2]{1,2,0:T(2,128)S(1)}, f32[1,256,2]{1,2,0:T(2,128)}, u32[]{:S(2)}) copy-start(f32[1,256,2]{1,2,0:T(2,128)} %param.13) | copy-start | bytes 6148
  11.3 11.9 %collective-permute-start.1 = (bf16[192,512]{1,0:T(8,128)(2,1)S(1)}, bf16[192,512]{1,0:T(8,128)(2,1)S(1)}, u32[]{:S(2)}, u32[]{:S(2)}) collective-permute-start(bf16[192,512]{1,0:T(8,128)(2,1)S(1)} %get-tuple-element.32.refs_0_), channel_id=1, source_target_pairs={{0,1},{1,0},{2,3},{3,2},{4,5},{5,4},{6,7},{7,6},{8,9},{9,8},{10,11... | collective-permute-start | bytes 589832 | tf_op jit(solution)/shard_map/ppermute | solution.py:294
  12.9 19.2 %collective-permute-start.6 = (bf16[192,512]{1,0:T(8,128)(2,1)S(1)}, bf16[192,512]{1,0:T(8,128)(2,1)S(1)}, u32[]{:S(2)}, u32[]{:S(2)}) collective-permute-start(bf16[192,512]{1,0:T(8,128)(2,1)S(1)} %get-tuple-element.42), channel_id=1, source_target_pairs={{0,6},{2,4},{4,2},{6,0},{1,7},{3,5},{5,3},{7,1},{8,14},{10,12},{12... | collective-permute-start | bytes 589832 | tf_op jit(solution)/shard_map/ppermute | solution.py:294
  15.8 12.3 %collective-permute-start.2 = (bf16[192,512]{1,0:T(8,128)(2,1)S(1)}, bf16[192,512]{1,0:T(8,128)(2,1)S(1)}, u32[]{:S(2)}, u32[]{:S(2)}) collective-permute-start(bf16[192,512]{1,0:T(8,128)(2,1)S(1)} %shard_map.125.refs_4_.refs_0_), channel_id=1, source_target_pairs={{0,1},{1,0},{2,3},{3,2},{4,5},{5,4},{6,7},{7,6},{8,9},{9,8},{10,11... | collective-permute-start | bytes 589832 | tf_op jit(solution)/shard_map/ppermute | solution.py:294
  29.9 6.4 %collective-permute-start.3 = (bf16[192,512]{1,0:T(8,128)(2,1)S(1)}, bf16[192,512]{1,0:T(8,128)(2,1)S(1)}, u32[]{:S(2)}, u32[]{:S(2)}) collective-permute-start(bf16[192,512]{1,0:T(8,128)(2,1)S(1)} %get-tuple-element.40), channel_id=1, source_target_pairs={{0,1},{1,0},{2,3},{3,2},{4,5},{5,4},{6,7},{7,6},{8,9},{9,8},{10,11... | collective-permute-start | bytes 589832 | tf_op jit(solution)/shard_map/ppermute | solution.py:294
  32.0 9.9 %collective-permute-start.5 = (bf16[192,1024]{1,0:T(8,128)(2,1)S(1)}, bf16[192,1024]{1,0:T(8,128)(2,1)S(1)}, u32[]{:S(2)}, u32[]{:S(2)}) collective-permute-start(bf16[192,1024]{1,0:T(8,128)(2,1)S(1)} %get-tuple-element.41), channel_id=1, source_target_pairs={{0,2},{2,0},{4,6},{6,4},{1,3},{3,1},{5,7},{7,5},{8,10},{10,8},{12,... | collective-permute-start | bytes 1179656 | tf_op jit(solution)/shard_map/ppermute | solution.py:294
  32.0 6.3 %collective-permute-start.7 = (bf16[192,512]{1,0:T(8,128)(2,1)S(1)}, bf16[192,512]{1,0:T(8,128)(2,1)S(1)}, u32[]{:S(2)}, u32[]{:S(2)}) collective-permute-start(bf16[192,512]{1,0:T(8,128)(2,1)S(1)} %collective-permute-done.6.refs_0_), channel_id=1, source_target_pairs={{0,1},{1,0},{2,3},{3,2},{4,5},{5,4},{6,7},{7,6},{8,9},{9,8},{10,11... | collective-permute-start | bytes 589832 | tf_op jit(solution)/shard_map/ppermute | solution.py:294
  36.3 10.4 %collective-permute-start.4 = (bf16[192,512]{1,0:T(8,128)(2,1)S(1)}, bf16[192,512]{1,0:T(8,128)(2,1)S(1)}, u32[]{:S(2)}, u32[]{:S(2)}) collective-permute-start(bf16[192,512]{1,0:T(8,128)(2,1)S(1)} %add_convert_fusion.1.refs_4_), channel_id=1, source_target_pairs={{0,4},{2,6},{4,0},{6,2},{1,5},{3,7},{5,1},{7,3},{8,12},{10,14},{12... | collective-permute-start | bytes 589832 | tf_op jit(solution)/shard_map/ppermute | solution.py:294
  40.2 7.9 %collective-permute-start.10 = (bf16[192,512]{1,0:T(8,128)(2,1)S(1)}, bf16[192,512]{1,0:T(8,128)(2,1)S(1)}, u32[]{:S(2)}, u32[]{:S(2)}) collective-permute-start(bf16[192,512]{1,0:T(8,128)(2,1)S(1)} %get-tuple-element.43.refs_3_), channel_id=1, source_target_pairs={{0,1},{1,0},{2,3},{3,2},{4,5},{5,4},{6,7},{7,6},{8,9},{9,8},{10,11... | collective-permute-start | bytes 589832 | tf_op jit(solution)/shard_map/ppermute | solution.py:294
  43.7 25.8 %copy-start = (bf16[1,1024,512]{2,1,0:T(8,128)(2,1)S(1)}, bf16[1,1024,512]{2,1,0:T(8,128)(2,1)}, u32[]{:S(2)}) copy-start(bf16[1,1024,512]{2,1,0:T(8,128)(2,1)} %param.18) | copy-start | bytes 3145732
  43.7 25.8 %copy-start.3 = (f32[1,1024]{1,0:T(1,128)S(1)}, f32[1,1024]{1,0:T(1,128)}, u32[]{:S(2)}) copy-start(f32[1,1024]{1,0:T(1,128)} %refs_2_.3) | copy-start | bytes 12292
  46.7 24.1 %copy-start.6 = (bf16[1,1024,512]{2,1,0:T(8,128)(2,1)S(1)}, bf16[1,1024,512]{2,1,0:T(8,128)(2,1)}, u32[]{:S(2)}) copy-start(bf16[1,1024,512]{2,1,0:T(8,128)(2,1)} %param.19) | copy-start | bytes 3145732
  46.7 24.1 %copy-start.7 = (bf16[1,1024,512]{2,1,0:T(8,128)(2,1)S(1)}, bf16[1,1024,512]{2,1,0:T(8,128)(2,1)}, u32[]{:S(2)}) copy-start(bf16[1,1024,512]{2,1,0:T(8,128)(2,1)} %param.20) | copy-start | bytes 3145732
  47.1 5.7 %collective-permute-start.8 = (bf16[192,512]{1,0:T(8,128)(2,1)S(1)}, bf16[192,512]{1,0:T(8,128)(2,1)S(1)}, u32[]{:S(2)}, u32[]{:S(2)}) collective-permute-start(bf16[192,512]{1,0:T(8,128)(2,1)S(1)} %get-tuple-element.47), channel_id=1, source_target_pairs={{0,1},{1,0},{2,3},{3,2},{4,5},{5,4},{6,7},{7,6},{8,9},{9,8},{10,11... | collective-permute-start | bytes 589832 | tf_op jit(solution)/shard_map/ppermute | solution.py:294
  48.2 8.8 %collective-permute-start.11 = (bf16[192,512]{1,0:T(8,128)(2,1)S(1)}, bf16[192,512]{1,0:T(8,128)(2,1)S(1)}, u32[]{:S(2)}, u32[]{:S(2)}) collective-permute-start(bf16[192,512]{1,0:T(8,128)(2,1)S(1)} %add_convert_fusion), channel_id=1, source_target_pairs={{0,6},{2,4},{4,2},{6,0},{1,7},{3,5},{5,3},{7,1},{8,14},{10,12},{12... | collective-permute-start | bytes 589832 | tf_op jit(solution)/shard_map/ppermute | solution.py:294
  52.9 6.2 %collective-permute-start.9 = (bf16[192,512]{1,0:T(8,128)(2,1)S(1)}, bf16[192,512]{1,0:T(8,128)(2,1)S(1)}, u32[]{:S(2)}, u32[]{:S(2)}) collective-permute-start(bf16[192,512]{1,0:T(8,128)(2,1)S(1)} %shard_map.131), channel_id=1, source_target_pairs={{0,2},{2,0},{4,6},{6,4},{1,3},{3,1},{5,7},{7,5},{8,10},{10,8},{12,... | collective-permute-start | bytes 589832 | tf_op jit(solution)/shard_map/ppermute | solution.py:294
  59.5 6.4 %collective-permute-start.12 = (bf16[256,512]{1,0:T(8,128)(2,1)S(1)}, bf16[256,512]{1,0:T(8,128)(2,1)S(1)}, u32[]{:S(2)}, u32[]{:S(2)}) collective-permute-start(bf16[256,512]{1,0:T(8,128)(2,1)S(1)} %shard_map.132.refs_0_.refs_2_), channel_id=1, source_target_pairs={{0,1},{1,0},{2,3},{3,2},{4,5},{5,4},{6,7},{7,6},{8,9},{9,8},{10,11... | collective-permute-start | bytes 786440 | tf_op jit(solution)/shard_map/ppermute | solution.py:294
  60.9 5.1 %collective-permute-start.13 = (bf16[256,512]{1,0:T(8,128)(2,1)S(1)}, bf16[256,512]{1,0:T(8,128)(2,1)S(1)}, u32[]{:S(2)}, u32[]{:S(2)}) collective-permute-start(bf16[256,512]{1,0:T(8,128)(2,1)S(1)} %shard_map.132.refs_0_.refs_2_), channel_id=1, source_target_pairs={{0,8},{8,0},{16,24},{24,16},{1,9},{9,1},{17,25},{25,17},{2,10},{10... | collective-permute-start | bytes 786440 | tf_op jit(solution)/shard_map/ppermute | solution.py:294
  60.9 5.4 %collective-permute-start.14 = (bf16[256,512]{1,0:T(8,128)(2,1)S(1)}, bf16[256,512]{1,0:T(8,128)(2,1)S(1)}, u32[]{:S(2)}, u32[]{:S(2)}) collective-permute-start(bf16[256,512]{1,0:T(8,128)(2,1)S(1)} %shard_map.132.refs_0_.refs_2_), channel_id=1, source_target_pairs={{0,16},{1,17},{8,0},{9,1},{16,24},{17,25},{24,8},{25,9},{2,18},{3,... | collective-permute-start | bytes 786440 | tf_op jit(solution)/shard_map/ppermute | solution.py:436
  62.4 6.7 %collective-permute-start.15 = (bf16[256,512]{1,0:T(8,128)(2,1)S(1)}, bf16[256,512]{1,0:T(8,128)(2,1)S(1)}, u32[]{:S(2)}, u32[]{:S(2)}) collective-permute-start(bf16[256,512]{1,0:T(8,128)(2,1)S(1)} %shard_map.132.refs_0_.refs_2_), channel_id=1, source_target_pairs={{0,25},{1,24},{8,0},{9,1},{16,8},{17,9},{24,16},{25,17},{2,27},{3,... | collective-permute-start | bytes 786440 | tf_op jit(solution)/shard_map/ppermute | solution.py:436
  69.1 1.6 %collective-permute-start.16 = (bf16[256,512]{1,0:T(8,128)(2,1)S(1)}, bf16[256,512]{1,0:T(8,128)(2,1)S(1)}, u32[]{:S(2)}, u32[]{:S(2)}) collective-permute-start(bf16[256,512]{1,0:T(8,128)(2,1)S(1)} %shard_map.133.refs_0_), channel_id=1, source_target_pairs={{0,8},{8,0},{16,24},{24,16},{1,9},{9,1},{17,25},{25,17},{2,10},{10... | collective-permute-start | bytes 786440 | tf_op jit(solution)/shard_map/ppermute | solution.py:294
  70.8 3.4 %collective-permute-start.17 = (bf16[256,512]{1,0:T(8,128)(2,1)S(1)}, bf16[256,512]{1,0:T(8,128)(2,1)S(1)}, u32[]{:S(2)}, u32[]{:S(2)}) collective-permute-start(bf16[256,512]{1,0:T(8,128)(2,1)S(1)} %get-tuple-element.53), channel_id=1, source_target_pairs={{0,8},{8,0},{16,24},{24,16},{1,9},{9,1},{17,25},{25,17},{2,10},{10... | collective-permute-start | bytes 786440 | tf_op jit(solution)/shard_map/ppermute | solution.py:294
  74.3 4.4 %collective-permute-start.18 = (bf16[256,128]{1,0:T(8,128)(2,1)S(1)}, bf16[256,128]{1,0:T(8,128)(2,1)S(1)}, u32[]{:S(2)}, u32[]{:S(2)}) collective-permute-start(bf16[256,128]{1,0:T(8,128)(2,1)S(1)} %get-tuple-element.55), channel_id=1, source_target_pairs={{0,1},{1,0},{8,9},{9,8},{16,17},{17,16},{24,25},{25,24},{2,3},{3,2... | collective-permute-start | bytes 196616 | tf_op jit(solution)/shard_map/ppermute | solution.py:485
  75.0 5.0 %collective-permute-start.19 = (bf16[256,128]{1,0:T(8,128)(2,1)S(1)}, bf16[256,128]{1,0:T(8,128)(2,1)S(1)}, u32[]{:S(2)}, u32[]{:S(2)}) collective-permute-start(bf16[256,128]{1,0:T(8,128)(2,1)S(1)} %get-tuple-element.56), channel_id=1, source_target_pairs={{0,16},{1,17},{8,24},{9,25},{16,0},{17,1},{24,8},{25,9},{2,18},{3,... | collective-permute-start | bytes 196616 | tf_op jit(solution)/shard_map/ppermute | solution.py:485
  77.8 5.2 %collective-permute-start.20 = (bf16[256,128]{1,0:T(8,128)(2,1)S(1)}, bf16[256,128]{1,0:T(8,128)(2,1)S(1)}, u32[]{:S(2)}, u32[]{:S(2)}) collective-permute-start(bf16[256,128]{1,0:T(8,128)(2,1)S(1)} %get-tuple-element.57), channel_id=1, source_target_pairs={{0,17},{1,16},{8,25},{9,24},{16,1},{17,0},{24,9},{25,8},{2,19},{3,... | collective-permute-start | bytes 196616 | tf_op jit(solution)/shard_map/ppermute | solution.py:485

commit v15 on v14

--- a/solution.py
+++ b/solution.py
@@ -384,7 +384,7 @@
     for k, rows in zip(groups[1], later):
         far_rows[k - 2] = rows
     arriving.append(joined(groups[1]))
-    returned = {0: total(own_away, own_kept, plain=True)}
+    returned = {0: total(own_away, own_kept)}
     arriving[0] = hold(arriving[0], [own_away])
     others = [swap(arriving[0], "tp", 1)]
     high, low, upstream = call(
@@ -397,27 +397,28 @@
     )
     others.append(swap(arriving[1], "tp", 1))
 
-    def give_back(group, away, kept):
-        mixed = total(away, kept, plain=True)
+    def give_back(group, block):
         for i, k in enumerate(group):
-            block = mixed if len(group) == 1 else mixed[i * capacity : (i + 1) * capacity]
-            returned[k] = swap(block, "exp", k)
-        return mixed
-
-    away, kept = through([arriving[0], others[0]], [returned[0], high])
-    mixed = give_back(groups[0], away, kept)
+            rows = block if len(group) == 1 else block[i * capacity : (i + 1) * capacity]
+            returned[k] = swap(rows, "exp", k)
+
+    near_away, near_kept = through([near], [returned[0], high])
+    away, kept = through([arriving[0], others[0]], [near_away])
+    mixed = total(away, kept)
+    give_back(groups[0], mixed)
+    near_total = total(near_away, near_kept, plain=True)
+    returned[1] = swap(near_total, "exp", 1)
     away, kept = through([arriving[1], others[1]], [mixed])
-    near_away, near_kept = through([near], [away])
-    give_back(groups[1], away, kept)
+    last = total(away, kept)
     there, rest = [0, *groups[0]], [1, *groups[1]]
-    so_far, near_away = call(
+    so_far, last = call(
         functools.partial(combine, there),
         [shape_of((token_count, half), WIDE)],
         [token_rows, high, low, *(returned[k] for k in there)],
         flops=4 * len(there) * token_count * capacity * half,
-        held=[near_away],
-    )
-    returned[1] = swap(total(near_away, near_kept), "exp", 1)
+        held=[last],
+    )
+    give_back(groups[1], last)
     hidden_half = call(
         functools.partial(combine, rest),
         [shape_of((token_count, half))],

time: 83.7 us -> 78.7 us (0.940)
  starting transfers between devices: 31.9 us -> 28.9 us
  waiting for transfers between devices: 35.1 us -> 32.8 us
    ppermute x16, starting transfers between devices: 26.2 us -> 23.1 us  [swap(): return lax.ppermute(block, axis, [(i, i ^ step) for i in range(size)])]
    ppermute x16, waiting for transfers between devices: 27.6 us -> 25.5 us  [swap(): return lax.ppermute(block, axis, [(i, i ^ step) for i in range(size)])]
    pallas_call x16 -> x18, Pallas kernels: 14 us -> 14.1 us  [call(): pl.pallas_call(run, out_shape=[*out_shape, *(shape_of(x.shape, x.dtype) f...]
  transfers between devices with their start and end apart: 21 -> 21, of which waited for: 16 -> 14; matrix products, arithmetic and copies ran while one was open for 0% -> 0% of each run, Pallas kernels for 15% -> 16%
where the time goes in v15:
time: 78.7 us; the launch traced here: 78.4 us
  waiting for transfers between devices  32.8 us (42%)
  starting transfers between devices  28.9 us (37%)
  Pallas kernels  14.1 us (18%)
  local copies, waits for them, and re-layouts  1.03 us (1%)
  between operations  0.85 us (1%)
    ppermute x16, waiting for transfers between devices, swap(): return lax.ppermute(block, axis, [(i, i ^ step) for i in range(size)])  25.5 us
    ppermute x16, starting transfers between devices, swap(): return lax.ppermute(block, axis, [(i, i ^ step) for i in range(size)])  23.1 us
    pallas_call x18, Pallas kernels, call(): pl.pallas_call(run, out_shape=[*out_shape, *(shape_of(x.shape, x.dtype) f...  14.1 us
    ppermute x3, waiting for transfers between devices, shards(): total = total + lax.ppermute(blocks[k], ('sec', 'tp'), pairs).astype(WIDE)  4.24 us
    ppermute x3, starting transfers between devices, shards(): total = total + lax.ppermute(blocks[k], ('sec', 'tp'), pairs).astype(WIDE)  3.69 us
    ppermute x2, waiting for transfers between devices, cycle(): return lax.ppermute(hidden_half, ('sec', 'tp'), list(targets.items()))  3.08 us
    ppermute x2, starting transfers between devices, cycle(): return lax.ppermute(hidden_half, ('sec', 'tp'), list(targets.items()))  2.06 us
  transfers between devices with their start and end apart: 21, of which 14 were waited for; matrix products, arithmetic and copies ran while one was open for 0% of the time, Pallas kernels for 16%

profile of v15, /device:TPU:0, one launch (start us, length us, event | category | flops | bytes accessed | tf_op | source)
XLA Modules:
  0.0 78.4 jit_solution(7938092594065968735)
XLA Ops:
  0.7 1.0 %copy-done.1 = bf16[1,256,1024]{2,1,0:T(8,128)(2,1)S(1)} copy-done((bf16[1,256,1024]{2,1,0:T(8,128)(2,1)S(1)}, bf16[1,256,1024]{2,1,0:T(8,128)(2,1)}, u32[]{:S(2)}) %copy-start.1) | copy-done | bytes 524312
  1.7 0.9 %shard_map.123 = (bf16[192,512]{1,0:T(8,128)(2,1)S(1)}, bf16[192,512]{1,0:T(8,128)(2,1)S(1)}, bf16[192,1024]{1,0:T(8,128)(2,1)S(1)}, bf16[192,1024]{1,0:T(8,128)(2,1)S(1)}) custom-call(bf16[256,1024]{1,0:T(8,128)(2,1)S(1)} %bitcast.15, s32[2,256]{1,0:T(2,128)S(1)} %bitcast.18, f32[1,1024]{1,0:T(1,128)S(1)} %copy-done.8, ...), custom_call_target="tpu_custom_call" | custom-call | flops 402653184 | bytes 1841152 | tf_op jit(solution)/shard_map/pallas_call | solution.py:40
  2.6 3.1 %collective-permute-start.3 = (bf16[192,1024]{1,0:T(8,128)(2,1)S(1)}, bf16[192,1024]{1,0:T(8,128)(2,1)S(1)}, u32[]{:S(2)}, u32[]{:S(2)}) collective-permute-start(bf16[192,1024]{1,0:T(8,128)(2,1)S(1)} %get-tuple-element.39), channel_id=1, source_target_pairs={{0,2},{2,0},{4,6},{6,4},{1,3},{3,1},{5,7},{7,5},{8,10},{10,8},{12,... | collective-permute-start | bytes 1179656 | tf_op jit(solution)/shard_map/ppermute | solution.py:294
  5.7 2.6 %collective-permute-start = (bf16[192,512]{1,0:T(8,128)(2,1)S(1)}, bf16[192,512]{1,0:T(8,128)(2,1)S(1)}, u32[]{:S(2)}, u32[]{:S(2)}) collective-permute-start(bf16[192,512]{1,0:T(8,128)(2,1)S(1)} %get-tuple-element.33), channel_id=1, source_target_pairs={{0,4},{2,6},{4,0},{6,2},{1,5},{3,7},{5,1},{7,3},{8,12},{10,14},{12... | collective-permute-start | bytes 589832 | tf_op jit(solution)/shard_map/ppermute | solution.py:294
  8.2 4.6 %shard_map.124 = (bf16[192,512]{1,0:T(8,128)(2,1)S(1)}, f32[192,512]{1,0:T(8,128)S(1)}, bf16[1024,2048]{1,0:T(8,128)(2,1)S(1)}, bf16[2048,1024]{1,0:T(8,128)(2,1)S(1)}, bf16[192,512]{1,0:T(8,128)(2,1)S(1)}) custom-call(bf16[192,1024]{1,0:T(8,128)(2,1)S(1)} %get-tuple-element.30.refs_0_, ...), custom_call_target="tpu_custom_call", output_to_operand_aliasing={{4}: (3, {})} | custom-call | flops 1610612736 | bytes 17760256 | tf_op jit(solution)/shard_map/pallas_call | solution.py:40
  12.9 1.6 %collective-permute-start.1 = (bf16[192,512]{1,0:T(8,128)(2,1)S(1)}, bf16[192,512]{1,0:T(8,128)(2,1)S(1)}, u32[]{:S(2)}, u32[]{:S(2)}) collective-permute-start(bf16[192,512]{1,0:T(8,128)(2,1)S(1)} %get-tuple-element.32.refs_0_), channel_id=1, source_target_pairs={{0,1},{1,0},{2,3},{3,2},{4,5},{5,4},{6,7},{7,6},{8,9},{9,8},{10,11... | collective-permute-start | bytes 589832 | tf_op jit(solution)/shard_map/ppermute | solution.py:294
  14.4 3.8 %collective-permute-done.refs_1_ = bf16[192,512]{1,0:T(8,128)(2,1)S(1)} collective-permute-done((bf16[192,512]{1,0:T(8,128)(2,1)S(1)}, bf16[192,512]{1,0:T(8,128)(2,1)S(1)}, u32[]{:S(2)}, u32[]{:S(2)}) %collective-permute-start) | collective-permute-done | bytes 196640 | tf_op jit(solution)/shard_map/ppermute | solution.py:294
  18.2 1.5 %collective-permute-start.2 = (bf16[192,512]{1,0:T(8,128)(2,1)S(1)}, bf16[192,512]{1,0:T(8,128)(2,1)S(1)}, u32[]{:S(2)}, u32[]{:S(2)}) collective-permute-start(bf16[192,512]{1,0:T(8,128)(2,1)S(1)} %shard_map.125.refs_4_.refs_0_), channel_id=1, source_target_pairs={{0,1},{1,0},{2,3},{3,2},{4,5},{5,4},{6,7},{7,6},{8,9},{9,8},{10,11... | collective-permute-start | bytes 589832 | tf_op jit(solution)/shard_map/ppermute | solution.py:294
  19.8 2.5 %collective-permute-start.6 = (bf16[192,512]{1,0:T(8,128)(2,1)S(1)}, bf16[192,512]{1,0:T(8,128)(2,1)S(1)}, u32[]{:S(2)}, u32[]{:S(2)}) collective-permute-start(bf16[192,512]{1,0:T(8,128)(2,1)S(1)} %get-tuple-element.43), channel_id=1, source_target_pairs={{0,6},{2,4},{4,2},{6,0},{1,7},{3,5},{5,3},{7,1},{8,14},{10,12},{12... | collective-permute-start | bytes 589832 | tf_op jit(solution)/shard_map/ppermute | solution.py:294
  22.2 0.6 shard_map.126
  22.9 1.8 %shard_map.128 = (bf16[192,512]{1,0:T(8,128)(2,1)S(1)}, f32[192,512]{1,0:T(8,128)S(1)}) custom-call(bf16[192,1024]{1,0:T(8,128)(2,1)S(1)} %collective-permute-done.3.refs_0_, bf16[1024,2048]{1,0:T(8,128)(2,1)S(1)} %get-tuple-element.37.refs_1_.refs_2_, bf16[2048,1024]{1,0:T(8,128)(2,1)S(1)} %get-tuple-element.38.refs_2_.refs_3_, ...), custom_call_target="tpu_custom_call" | custom-call | flops 1610612736 | bytes 9371648 | tf_op jit(solution)/shard_map/pallas_call | solution.py:40
  24.8 1.8 %shard_map.129 = (bf16[192,512]{1,0:T(8,128)(2,1)S(1)}, f32[192,512]{1,0:T(8,128)S(1)}) custom-call(bf16[192,512]{1,0:T(8,128)(2,1)S(1)} %shard_map.125.refs_4_.refs_0_, bf16[192,512]{1,0:T(8,128)(2,1)S(1)} %collective-permute-done.2.refs_1_, bf16[1024,2048]{1,0:T(8,128)(2,1)S(1)} %get-tuple-element.37.refs_1_.refs_2_, ...), custom_call_target="tpu_custom_call" | custom-call | flops 1610612736 | bytes 9371648 | tf_op jit(solution)/shard_map/pallas_call | solution.py:40
  26.6 0.8 %collective-permute-start.4 = (bf16[192,512]{1,0:T(8,128)(2,1)S(1)}, bf16[192,512]{1,0:T(8,128)(2,1)S(1)}, u32[]{:S(2)}, u32[]{:S(2)}) collective-permute-start(bf16[192,512]{1,0:T(8,128)(2,1)S(1)} %get-tuple-element.42), channel_id=1, source_target_pairs={{0,1},{1,0},{2,3},{3,2},{4,5},{5,4},{6,7},{7,6},{8,9},{9,8},{10,11... | collective-permute-start | bytes 589832 | tf_op jit(solution)/shard_map/ppermute | solution.py:294
  27.4 1.3 %collective-permute-start.7 = (bf16[192,512]{1,0:T(8,128)(2,1)S(1)}, bf16[192,512]{1,0:T(8,128)(2,1)S(1)}, u32[]{:S(2)}, u32[]{:S(2)}) collective-permute-start(bf16[192,512]{1,0:T(8,128)(2,1)S(1)} %collective-permute-done.6.refs_0_), channel_id=1, source_target_pairs={{0,1},{1,0},{2,3},{3,2},{4,5},{5,4},{6,7},{7,6},{8,9},{9,8},{10,11... | collective-permute-start | bytes 589832 | tf_op jit(solution)/shard_map/ppermute | solution.py:294
  28.7 0.7 collective-permute-start.9
  29.5 5.1 %collective-permute-done.4.refs_1_ = bf16[192,512]{1,0:T(8,128)(2,1)S(1)} collective-permute-done((bf16[192,512]{1,0:T(8,128)(2,1)S(1)}, bf16[192,512]{1,0:T(8,128)(2,1)S(1)}, u32[]{:S(2)}, u32[]{:S(2)}) %collective-permute-start.4) | collective-permute-done | bytes 196640 | tf_op jit(solution)/shard_map/ppermute | solution.py:294
  34.6 0.5 collective-permute-start.5
  35.0 3.2 %collective-permute-done.7.refs_1_ = bf16[192,512]{1,0:T(8,128)(2,1)S(1)} collective-permute-done((bf16[192,512]{1,0:T(8,128)(2,1)S(1)}, bf16[192,512]{1,0:T(8,128)(2,1)S(1)}, u32[]{:S(2)}, u32[]{:S(2)}) %collective-permute-start.7) | collective-permute-done | bytes 196640 | tf_op jit(solution)/shard_map/ppermute | solution.py:294
  38.2 1.8 %shard_map.131 = (bf16[192,512]{1,0:T(8,128)(2,1)S(1)}, f32[192,512]{1,0:T(8,128)S(1)}) custom-call(bf16[192,512]{1,0:T(8,128)(2,1)S(1)} %collective-permute-done.6.refs_0_, bf16[192,512]{1,0:T(8,128)(2,1)S(1)} %collective-permute-done.7.refs_1_, bf16[1024,2048]{1,0:T(8,128)(2,1)S(1)} %get-tuple-element.37.refs_1_.refs_2_, ...), custom_call_target="tpu_custom_call" | custom-call | flops 1610612736 | bytes 9371648 | tf_op jit(solution)/shard_map/pallas_call | solution.py:40
  40.0 0.6 collective-permute-start.8
  40.6 1.3 %collective-permute-done.9 = bf16[192,512]{1,0:T(8,128)(2,1)S(1)} collective-permute-done((bf16[192,512]{1,0:T(8,128)(2,1)S(1)}, bf16[192,512]{1,0:T(8,128)(2,1)S(1)}, u32[]{:S(2)}, u32[]{:S(2)}) %collective-permute-start.9) | collective-permute-done | bytes 196640 | tf_op jit(solution)/shard_map/ppermute | solution.py:294
  42.0 2.6 %collective-permute-start.10 = (bf16[192,512]{1,0:T(8,128)(2,1)S(1)}, bf16[192,512]{1,0:T(8,128)(2,1)S(1)}, u32[]{:S(2)}, u32[]{:S(2)}) collective-permute-start(bf16[192,512]{1,0:T(8,128)(2,1)S(1)} %add_convert_fusion), channel_id=1, source_target_pairs={{0,2},{2,0},{4,6},{6,4},{1,3},{3,1},{5,7},{7,5},{8,10},{10,8},{12,... | collective-permute-start | bytes 589832 | tf_op jit(solution)/shard_map/ppermute | solution.py:294
  44.6 1.2 %collective-permute-done.8.refs_1_ = bf16[192,512]{1,0:T(8,128)(2,1)S(1)} collective-permute-done((bf16[192,512]{1,0:T(8,128)(2,1)S(1)}, bf16[192,512]{1,0:T(8,128)(2,1)S(1)}, u32[]{:S(2)}, u32[]{:S(2)}) %collective-permute-start.8) | collective-permute-done | bytes 196640 | tf_op jit(solution)/shard_map/ppermute | solution.py:294
  45.8 0.4 shard_map.133
  46.3 1.4 %collective-permute-start.11 = (bf16[192,512]{1,0:T(8,128)(2,1)S(1)}, bf16[192,512]{1,0:T(8,128)(2,1)S(1)}, u32[]{:S(2)}, u32[]{:S(2)}) collective-permute-start(bf16[192,512]{1,0:T(8,128)(2,1)S(1)} %get-tuple-element.48), channel_id=1, source_target_pairs={{0,6},{2,4},{4,2},{6,0},{1,7},{3,5},{5,3},{7,1},{8,14},{10,12},{12... | collective-permute-start | bytes 589832 | tf_op jit(solution)/shard_map/ppermute | solution.py:294
  47.7 1.8 %collective-permute-done.10.refs_3_ = bf16[192,512]{1,0:T(8,128)(2,1)S(1)} collective-permute-done((bf16[192,512]{1,0:T(8,128)(2,1)S(1)}, bf16[192,512]{1,0:T(8,128)(2,1)S(1)}, u32[]{:S(2)}, u32[]{:S(2)}) %collective-permute-start.10) | collective-permute-done | bytes 196640 | tf_op jit(solution)/shard_map/ppermute | solution.py:294
  49.5 4.5 %collective-permute-done.11.refs_4_ = bf16[192,512]{1,0:T(8,128)(2,1)S(1)} collective-permute-done((bf16[192,512]{1,0:T(8,128)(2,1)S(1)}, bf16[192,512]{1,0:T(8,128)(2,1)S(1)}, u32[]{:S(2)}, u32[]{:S(2)}) %collective-permute-start.11) | collective-permute-done | bytes 196640 | tf_op jit(solution)/shard_map/ppermute | solution.py:294
  53.9 0.4 shard_map.134.refs_0_.refs_2_
  54.3 1.3 %collective-permute-start.12 = (bf16[256,512]{1,0:T(8,128)(2,1)S(1)}, bf16[256,512]{1,0:T(8,128)(2,1)S(1)}, u32[]{:S(2)}, u32[]{:S(2)}) collective-permute-start(bf16[256,512]{1,0:T(8,128)(2,1)S(1)} %shard_map.134.refs_0_.refs_2_), channel_id=1, source_target_pairs={{0,1},{1,0},{2,3},{3,2},{4,5},{5,4},{6,7},{7,6},{8,9},{9,8},{10,11... | collective-permute-start | bytes 786440 | tf_op jit(solution)/shard_map/ppermute | solution.py:294
  55.7 1.5 %collective-permute-start.14 = (bf16[256,512]{1,0:T(8,128)(2,1)S(1)}, bf16[256,512]{1,0:T(8,128)(2,1)S(1)}, u32[]{:S(2)}, u32[]{:S(2)}) collective-permute-start(bf16[256,512]{1,0:T(8,128)(2,1)S(1)} %shard_map.134.refs_0_.refs_2_), channel_id=1, source_target_pairs={{0,16},{1,17},{8,0},{9,1},{16,24},{17,25},{24,8},{25,9},{2,18},{3,... | collective-permute-start | bytes 786440 | tf_op jit(solution)/shard_map/ppermute | solution.py:437
  57.2 0.6 collective-permute-start.15
  57.7 3.0 %collective-permute-done.12.refs_0_.refs_1_ = bf16[256,512]{1,0:T(8,128)(2,1)S(1)} collective-permute-done((bf16[256,512]{1,0:T(8,128)(2,1)S(1)}, bf16[256,512]{1,0:T(8,128)(2,1)S(1)}, u32[]{:S(2)}, u32[]{:S(2)}) %collective-permute-start.12) | collective-permute-done | bytes 262176 | tf_op jit(solution)/shard_map/ppermute | solution.py:294
  60.8 0.3 collective-permute-done.14.refs_2_
  61.0 2.8 %collective-permute-done.15.refs_3_ = bf16[256,512]{1,0:T(8,128)(2,1)S(1)} collective-permute-done((bf16[256,512]{1,0:T(8,128)(2,1)S(1)}, bf16[256,512]{1,0:T(8,128)(2,1)S(1)}, u32[]{:S(2)}, u32[]{:S(2)}) %collective-permute-start.15) | collective-permute-done | bytes 262176 | tf_op jit(solution)/shard_map/ppermute | solution.py:437
  63.9 0.4 collective-permute-start.16
  64.3 0.7 shard_map.136.refs_2_
  65.0 0.5 collective-permute-done.16.refs_1_
  65.5 0.1 shard_map.137
  65.6 2.2 %collective-permute-start.17 = (bf16[256,512]{1,0:T(8,128)(2,1)S(1)}, bf16[256,512]{1,0:T(8,128)(2,1)S(1)}, u32[]{:S(2)}, u32[]{:S(2)}) collective-permute-start(bf16[256,512]{1,0:T(8,128)(2,1)S(1)} %get-tuple-element.53), channel_id=1, source_target_pairs={{0,8},{8,0},{16,24},{24,16},{1,9},{9,1},{17,25},{25,17},{2,10},{10... | collective-permute-start | bytes 786440 | tf_op jit(solution)/shard_map/ppermute | solution.py:294
  67.8 1.2 %collective-permute-done.17.refs_1_ = bf16[256,512]{1,0:T(8,128)(2,1)S(1)} collective-permute-done((bf16[256,512]{1,0:T(8,128)(2,1)S(1)}, bf16[256,512]{1,0:T(8,128)(2,1)S(1)}, u32[]{:S(2)}, u32[]{:S(2)}) %collective-permute-start.17) | collective-permute-done | bytes 262176 | tf_op jit(solution)/shard_map/ppermute | solution.py:294
  68.9 0.1 shard_map.139
  69.0 0.8 %collective-permute-start.18 = (bf16[256,128]{1,0:T(8,128)(2,1)S(1)}, bf16[256,128]{1,0:T(8,128)(2,1)S(1)}, u32[]{:S(2)}, u32[]{:S(2)}) collective-permute-start(bf16[256,128]{1,0:T(8,128)(2,1)S(1)} %get-tuple-element.55), channel_id=1, source_target_pairs={{0,1},{1,0},{8,9},{9,8},{16,17},{17,16},{24,25},{25,24},{2,3},{3,2... | collective-permute-start | bytes 196616 | tf_op jit(solution)/shard_map/ppermute | solution.py:486
  69.9 2.6 %collective-permute-start.19 = (bf16[256,128]{1,0:T(8,128)(2,1)S(1)}, bf16[256,128]{1,0:T(8,128)(2,1)S(1)}, u32[]{:S(2)}, u32[]{:S(2)}) collective-permute-start(bf16[256,128]{1,0:T(8,128)(2,1)S(1)} %get-tuple-element.56), channel_id=1, source_target_pairs={{0,16},{1,17},{8,24},{9,25},{16,0},{17,1},{24,8},{25,9},{2,18},{3,... | collective-permute-start | bytes 196616 | tf_op jit(solution)/shard_map/ppermute | solution.py:486
  72.5 0.2 collective-permute-start.20
  72.7 0.7 shard_map.138
  73.5 1.4 %collective-permute-done.19 = bf16[256,128]{1,0:T(8,128)(2,1)S(1)} collective-permute-done((bf16[256,128]{1,0:T(8,128)(2,1)S(1)}, bf16[256,128]{1,0:T(8,128)(2,1)S(1)}, u32[]{:S(2)}, u32[]{:S(2)}) %collective-permute-start.19) | collective-permute-done | bytes 65568 | tf_op jit(solution)/shard_map/ppermute | solution.py:486
  74.9 2.8 %collective-permute-done.20 = bf16[256,128]{1,0:T(8,128)(2,1)S(1)} collective-permute-done((bf16[256,128]{1,0:T(8,128)(2,1)S(1)}, bf16[256,128]{1,0:T(8,128)(2,1)S(1)}, u32[]{:S(2)}, u32[]{:S(2)}) %collective-permute-start.20) | collective-permute-done | bytes 65568 | tf_op jit(solution)/shard_map/ppermute | solution.py:486
  77.7 0.7 add_convert_fusion.1
  (32 shorter events, 0.3 us)
Async XLA Ops:
  0.6 1.0 %copy-start.1 = (bf16[1,256,1024]{2,1,0:T(8,128)(2,1)S(1)}, bf16[1,256,1024]{2,1,0:T(8,128)(2,1)}, u32[]{:S(2)}) copy-start(bf16[1,256,1024]{2,1,0:T(8,128)(2,1)} %param.11) | copy-start | bytes 1572868
  0.6 1.0 %copy-start.4 = (s32[1,256,2]{1,2,0:T(2,128)S(1)}, s32[1,256,2]{1,2,0:T(2,128)}, u32[]{:S(2)}) copy-start(s32[1,256,2]{1,2,0:T(2,128)} %param.12) | copy-start | bytes 6148
  0.6 1.0 %copy-start.8 = (f32[1,1024]{1,0:T(1,128)S(1)}, f32[1,1024]{1,0:T(1,128)}, u32[]{:S(2)}) copy-start(f32[1,1024]{1,0:T(1,128)} %refs_2_.2) | copy-start | bytes 12292
  2.6 20.4 %collective-permute-start.3 = (bf16[192,1024]{1,0:T(8,128)(2,1)S(1)}, bf16[192,1024]{1,0:T(8,128)(2,1)S(1)}, u32[]{:S(2)}, u32[]{:S(2)}) collective-permute-start(bf16[192,1024]{1,0:T(8,128)(2,1)S(1)} %get-tuple-element.39), channel_id=1, source_target_pairs={{0,2},{2,0},{4,6},{6,4},{1,3},{3,1},{5,7},{7,5},{8,10},{10,8},{12,... | collective-permute-start | bytes 1179656 | tf_op jit(solution)/shard_map/ppermute | solution.py:294
  5.7 12.6 %collective-permute-start = (bf16[192,512]{1,0:T(8,128)(2,1)S(1)}, bf16[192,512]{1,0:T(8,128)(2,1)S(1)}, u32[]{:S(2)}, u32[]{:S(2)}) collective-permute-start(bf16[192,512]{1,0:T(8,128)(2,1)S(1)} %get-tuple-element.33), channel_id=1, source_target_pairs={{0,4},{2,6},{4,0},{6,2},{1,5},{3,7},{5,1},{7,3},{8,12},{10,14},{12... | collective-permute-start | bytes 589832 | tf_op jit(solution)/shard_map/ppermute | solution.py:294
  8.2 14.0 %copy-start.2 = (bf16[1,256,512]{2,1,0:T(8,128)(2,1)S(1)}, bf16[1,256,512]{2,1,0:T(8,128)(2,1)}, u32[]{:S(2)}) copy-start(bf16[1,256,512]{2,1,0:T(8,128)(2,1)} %param.21) | copy-start | bytes 786436
  8.2 14.0 %copy-start.5 = (f32[1,256,2]{1,2,0:T(2,128)S(1)}, f32[1,256,2]{1,2,0:T(2,128)}, u32[]{:S(2)}) copy-start(f32[1,256,2]{1,2,0:T(2,128)} %param.13) | copy-start | bytes 6148
  12.9 10.0 %collective-permute-start.1 = (bf16[192,512]{1,0:T(8,128)(2,1)S(1)}, bf16[192,512]{1,0:T(8,128)(2,1)S(1)}, u32[]{:S(2)}, u32[]{:S(2)}) collective-permute-start(bf16[192,512]{1,0:T(8,128)(2,1)S(1)} %get-tuple-element.32.refs_0_), channel_id=1, source_target_pairs={{0,1},{1,0},{2,3},{3,2},{4,5},{5,4},{6,7},{7,6},{8,9},{9,8},{10,11... | collective-permute-start | bytes 589832 | tf_op jit(solution)/shard_map/ppermute | solution.py:294
  18.2 6.5 %collective-permute-start.2 = (bf16[192,512]{1,0:T(8,128)(2,1)S(1)}, bf16[192,512]{1,0:T(8,128)(2,1)S(1)}, u32[]{:S(2)}, u32[]{:S(2)}) collective-permute-start(bf16[192,512]{1,0:T(8,128)(2,1)S(1)} %shard_map.125.refs_4_.refs_0_), channel_id=1, source_target_pairs={{0,1},{1,0},{2,3},{3,2},{4,5},{5,4},{6,7},{7,6},{8,9},{9,8},{10,11... | collective-permute-start | bytes 589832 | tf_op jit(solution)/shard_map/ppermute | solution.py:294
  19.8 7.7 %collective-permute-start.6 = (bf16[192,512]{1,0:T(8,128)(2,1)S(1)}, bf16[192,512]{1,0:T(8,128)(2,1)S(1)}, u32[]{:S(2)}, u32[]{:S(2)}) collective-permute-start(bf16[192,512]{1,0:T(8,128)(2,1)S(1)} %get-tuple-element.43), channel_id=1, source_target_pairs={{0,6},{2,4},{4,2},{6,0},{1,7},{3,5},{5,3},{7,1},{8,14},{10,12},{12... | collective-permute-start | bytes 589832 | tf_op jit(solution)/shard_map/ppermute | solution.py:294
  26.6 7.9 %collective-permute-start.4 = (bf16[192,512]{1,0:T(8,128)(2,1)S(1)}, bf16[192,512]{1,0:T(8,128)(2,1)S(1)}, u32[]{:S(2)}, u32[]{:S(2)}) collective-permute-start(bf16[192,512]{1,0:T(8,128)(2,1)S(1)} %get-tuple-element.42), channel_id=1, source_target_pairs={{0,1},{1,0},{2,3},{3,2},{4,5},{5,4},{6,7},{7,6},{8,9},{9,8},{10,11... | collective-permute-start | bytes 589832 | tf_op jit(solution)/shard_map/ppermute | solution.py:294
  27.4 10.8 %collective-permute-start.7 = (bf16[192,512]{1,0:T(8,128)(2,1)S(1)}, bf16[192,512]{1,0:T(8,128)(2,1)S(1)}, u32[]{:S(2)}, u32[]{:S(2)}) collective-permute-start(bf16[192,512]{1,0:T(8,128)(2,1)S(1)} %collective-permute-done.6.refs_0_), channel_id=1, source_target_pairs={{0,1},{1,0},{2,3},{3,2},{4,5},{5,4},{6,7},{7,6},{8,9},{9,8},{10,11... | collective-permute-start | bytes 589832 | tf_op jit(solution)/shard_map/ppermute | solution.py:294
  28.7 13.3 %collective-permute-start.9 = (bf16[192,512]{1,0:T(8,128)(2,1)S(1)}, bf16[192,512]{1,0:T(8,128)(2,1)S(1)}, u32[]{:S(2)}, u32[]{:S(2)}) collective-permute-start(bf16[192,512]{1,0:T(8,128)(2,1)S(1)} %get-tuple-element.40.refs_4_), channel_id=1, source_target_pairs={{0,1},{1,0},{2,3},{3,2},{4,5},{5,4},{6,7},{7,6},{8,9},{9,8},{10,11... | collective-permute-start | bytes 589832 | tf_op jit(solution)/shard_map/ppermute | solution.py:294
  34.6 11.3 %collective-permute-start.5 = (bf16[192,512]{1,0:T(8,128)(2,1)S(1)}, bf16[192,512]{1,0:T(8,128)(2,1)S(1)}, u32[]{:S(2)}, u32[]{:S(2)}) collective-permute-start(bf16[192,512]{1,0:T(8,128)(2,1)S(1)} %shard_map.130.refs_4_), channel_id=1, source_target_pairs={{0,4},{2,6},{4,0},{6,2},{1,5},{3,7},{5,1},{7,3},{8,12},{10,14},{12... | collective-permute-start | bytes 589832 | tf_op jit(solution)/shard_map/ppermute | solution.py:294
  40.0 24.3 %copy-start = (bf16[1,1024,512]{2,1,0:T(8,128)(2,1)S(1)}, bf16[1,1024,512]{2,1,0:T(8,128)(2,1)}, u32[]{:S(2)}) copy-start(bf16[1,1024,512]{2,1,0:T(8,128)(2,1)} %param.18) | copy-start | bytes 3145732
  40.0 24.3 %copy-start.3 = (f32[1,1024]{1,0:T(1,128)S(1)}, f32[1,1024]{1,0:T(1,128)}, u32[]{:S(2)}) copy-start(f32[1,1024]{1,0:T(1,128)} %refs_2_.3) | copy-start | bytes 12292
  40.0 5.7 %collective-permute-start.8 = (bf16[192,512]{1,0:T(8,128)(2,1)S(1)}, bf16[192,512]{1,0:T(8,128)(2,1)S(1)}, u32[]{:S(2)}, u32[]{:S(2)}) collective-permute-start(bf16[192,512]{1,0:T(8,128)(2,1)S(1)} %get-tuple-element.45), channel_id=1, source_target_pairs={{0,1},{1,0},{2,3},{3,2},{4,5},{5,4},{6,7},{7,6},{8,9},{9,8},{10,11... | collective-permute-start | bytes 589832 | tf_op jit(solution)/shard_map/ppermute | solution.py:294
  42.0 23.5 %copy-start.6 = (bf16[1,1024,512]{2,1,0:T(8,128)(2,1)S(1)}, bf16[1,1024,512]{2,1,0:T(8,128)(2,1)}, u32[]{:S(2)}) copy-start(bf16[1,1024,512]{2,1,0:T(8,128)(2,1)} %param.19) | copy-start | bytes 3145732
  42.0 23.5 %copy-start.7 = (bf16[1,1024,512]{2,1,0:T(8,128)(2,1)S(1)}, bf16[1,1024,512]{2,1,0:T(8,128)(2,1)}, u32[]{:S(2)}) copy-start(bf16[1,1024,512]{2,1,0:T(8,128)(2,1)} %param.20) | copy-start | bytes 3145732
  42.0 7.4 %collective-permute-start.10 = (bf16[192,512]{1,0:T(8,128)(2,1)S(1)}, bf16[192,512]{1,0:T(8,128)(2,1)S(1)}, u32[]{:S(2)}, u32[]{:S(2)}) collective-permute-start(bf16[192,512]{1,0:T(8,128)(2,1)S(1)} %add_convert_fusion), channel_id=1, source_target_pairs={{0,2},{2,0},{4,6},{6,4},{1,3},{3,1},{5,7},{7,5},{8,10},{10,8},{12,... | collective-permute-start | bytes 589832 | tf_op jit(solution)/shard_map/ppermute | solution.py:294
  46.3 7.7 %collective-permute-start.11 = (bf16[192,512]{1,0:T(8,128)(2,1)S(1)}, bf16[192,512]{1,0:T(8,128)(2,1)S(1)}, u32[]{:S(2)}, u32[]{:S(2)}) collective-permute-start(bf16[192,512]{1,0:T(8,128)(2,1)S(1)} %get-tuple-element.48), channel_id=1, source_target_pairs={{0,6},{2,4},{4,2},{6,0},{1,7},{3,5},{5,3},{7,1},{8,14},{10,12},{12... | collective-permute-start | bytes 589832 | tf_op jit(solution)/shard_map/ppermute | solution.py:294
  54.3 6.4 %collective-permute-start.12 = (bf16[256,512]{1,0:T(8,128)(2,1)S(1)}, bf16[256,512]{1,0:T(8,128)(2,1)S(1)}, u32[]{:S(2)}, u32[]{:S(2)}) collective-permute-start(bf16[256,512]{1,0:T(8,128)(2,1)S(1)} %shard_map.134.refs_0_.refs_2_), channel_id=1, source_target_pairs={{0,1},{1,0},{2,3},{3,2},{4,5},{5,4},{6,7},{7,6},{8,9},{9,8},{10,11... | collective-permute-start | bytes 786440 | tf_op jit(solution)/shard_map/ppermute | solution.py:294
  55.7 5.1 %collective-permute-start.13 = (bf16[256,512]{1,0:T(8,128)(2,1)S(1)}, bf16[256,512]{1,0:T(8,128)(2,1)S(1)}, u32[]{:S(2)}, u32[]{:S(2)}) collective-permute-start(bf16[256,512]{1,0:T(8,128)(2,1)S(1)} %shard_map.134.refs_0_.refs_2_), channel_id=1, source_target_pairs={{0,8},{8,0},{16,24},{24,16},{1,9},{9,1},{17,25},{25,17},{2,10},{10... | collective-permute-start | bytes 786440 | tf_op jit(solution)/shard_map/ppermute | solution.py:294
  55.7 5.4 %collective-permute-start.14 = (bf16[256,512]{1,0:T(8,128)(2,1)S(1)}, bf16[256,512]{1,0:T(8,128)(2,1)S(1)}, u32[]{:S(2)}, u32[]{:S(2)}) collective-permute-start(bf16[256,512]{1,0:T(8,128)(2,1)S(1)} %shard_map.134.refs_0_.refs_2_), channel_id=1, source_target_pairs={{0,16},{1,17},{8,0},{9,1},{16,24},{17,25},{24,8},{25,9},{2,18},{3,... | collective-permute-start | bytes 786440 | tf_op jit(solution)/shard_map/ppermute | solution.py:437
  57.2 6.7 %collective-permute-start.15 = (bf16[256,512]{1,0:T(8,128)(2,1)S(1)}, bf16[256,512]{1,0:T(8,128)(2,1)S(1)}, u32[]{:S(2)}, u32[]{:S(2)}) collective-permute-start(bf16[256,512]{1,0:T(8,128)(2,1)S(1)} %shard_map.134.refs_0_.refs_2_), channel_id=1, source_target_pairs={{0,25},{1,24},{8,0},{9,1},{16,8},{17,9},{24,16},{25,17},{2,27},{3,... | collective-permute-start | bytes 786440 | tf_op jit(solution)/shard_map/ppermute | solution.py:437
  63.9 1.6 %collective-permute-start.16 = (bf16[256,512]{1,0:T(8,128)(2,1)S(1)}, bf16[256,512]{1,0:T(8,128)(2,1)S(1)}, u32[]{:S(2)}, u32[]{:S(2)}) collective-permute-start(bf16[256,512]{1,0:T(8,128)(2,1)S(1)} %shard_map.135.refs_0_), channel_id=1, source_target_pairs={{0,8},{8,0},{16,24},{24,16},{1,9},{9,1},{17,25},{25,17},{2,10},{10... | collective-permute-start | bytes 786440 | tf_op jit(solution)/shard_map/ppermute | solution.py:294
  65.6 3.4 %collective-permute-start.17 = (bf16[256,512]{1,0:T(8,128)(2,1)S(1)}, bf16[256,512]{1,0:T(8,128)(2,1)S(1)}, u32[]{:S(2)}, u32[]{:S(2)}) collective-permute-start(bf16[256,512]{1,0:T(8,128)(2,1)S(1)} %get-tuple-element.53), channel_id=1, source_target_pairs={{0,8},{8,0},{16,24},{24,16},{1,9},{9,1},{17,25},{25,17},{2,10},{10... | collective-permute-start | bytes 786440 | tf_op jit(solution)/shard_map/ppermute | solution.py:294
  69.0 4.4 %collective-permute-start.18 = (bf16[256,128]{1,0:T(8,128)(2,1)S(1)}, bf16[256,128]{1,0:T(8,128)(2,1)S(1)}, u32[]{:S(2)}, u32[]{:S(2)}) collective-permute-start(bf16[256,128]{1,0:T(8,128)(2,1)S(1)} %get-tuple-element.55), channel_id=1, source_target_pairs={{0,1},{1,0},{8,9},{9,8},{16,17},{17,16},{24,25},{25,24},{2,3},{3,2... | collective-permute-start | bytes 196616 | tf_op jit(solution)/shard_map/ppermute | solution.py:486
  69.9 5.0 %collective-permute-start.19 = (bf16[256,128]{1,0:T(8,128)(2,1)S(1)}, bf16[256,128]{1,0:T(8,128)(2,1)S(1)}, u32[]{:S(2)}, u32[]{:S(2)}) collective-permute-start(bf16[256,128]{1,0:T(8,128)(2,1)S(1)} %get-tuple-element.56), channel_id=1, source_target_pairs={{0,16},{1,17},{8,24},{9,25},{16,0},{17,1},{24,8},{25,9},{2,18},{3,... | collective-permute-start | bytes 196616 | tf_op jit(solution)/shard_map/ppermute | solution.py:486
  72.5 5.2 %collective-permute-start.20 = (bf16[256,128]{1,0:T(8,128)(2,1)S(1)}, bf16[256,128]{1,0:T(8,128)(2,1)S(1)}, u32[]{:S(2)}, u32[]{:S(2)}) collective-permute-start(bf16[256,128]{1,0:T(8,128)(2,1)S(1)} %get-tuple-element.57), channel_id=1, source_target_pairs={{0,17},{1,16},{8,25},{9,24},{16,1},{17,0},{24,9},{25,8},{2,19},{3,... | collective-permute-start | bytes 196616 | tf_op jit(solution)/shard_map/ppermute | solution.py:486

commit v16 on v13

--- a/solution.py
+++ b/solution.py
@@ -206,12 +206,11 @@
 
 
 def attend(
-    first, second, queries, upstream, key_w, value_w, away, kept, low_ref, values, keys, dkeys, dvalues
+    first, second, queries, upstream, key_w, value_w, away, low_ref, values, dkeys, dvalues, keys
 ):
     tp = lax.axis_index("tp")
     sec = lax.axis_index("sec")
     token_count, half = first.shape
-    width = 2 * half
     scale = 1.0 / math.sqrt(HD)
 
     @pl.when(sec != 0)
@@ -242,20 +241,33 @@
             dkeys[at] = (matmul(dscore, queries[at]) * scale).astype(LOW)
         for i, low in enumerate(lows):
             low_ref[i] = low
-        side = sec % 2
-        pairs = lax.axis_size("sec") // 2
-        block = width // (2 * pairs)
-        for target, parity in ((away, 1 - side), (kept, side)):
-            for i in range(pairs):
-                rows = part(2 * i + parity, block)
-                value = matmul(dkeys[...], key_w[rows, :], NT)
-                value = value + matmul(dvalues[...], value_w[rows, :], NT)
-                target[:, i * block : (i + 1) * block] = value.astype(target.dtype)
+        terms(dkeys, dvalues, key_w, value_w, 1 - sec % 2, away)
 
     @pl.when(sec == 0)
     def _():
         away[...] = jnp.zeros_like(away)
-        kept[...] = jnp.zeros_like(kept)
+
+
+def terms(dkeys, dvalues, key_w, value_w, parity, out):
+    pairs = lax.axis_size("sec") // 2
+    block = out.shape[1] // pairs
+    for i in range(pairs):
+        rows = part(2 * i + parity, block)
+        value = matmul(dkeys[...], key_w[rows, :], NT)
+        value = value + matmul(dvalues[...], value_w[rows, :], NT)
+        out[:, i * block : (i + 1) * block] = value.astype(out.dtype)
+
+
+def keep(dkeys, dvalues, key_w, value_w, out):
+    sec = lax.axis_index("sec")
+
+    @pl.when(sec != 0)
+    def _():
+        terms(dkeys, dvalues, key_w, value_w, sec % 2, out)
+
+    @pl.when(sec == 0)
+    def _():
+        out[...] = jnp.zeros_like(out)
 
 
 def contexts(low_ref, values, hidden, out):
@@ -364,7 +376,7 @@
     near = swap(near_rows, "exp", 1)
     later = [far_rows[k - 2] for k in groups[1]]
     loads = max(1, units // 512) + 1
-    own_away, own_kept, weight_first, weight_second, *later = call(
+    own_away, own_kept, weight_first, weight_second = call(
         expert_first,
         [
             row_half,
@@ -377,13 +389,12 @@
         flops=4 * capacity * model_width * units,
         remote=(1, 2),
         limit=44,
-        held=later,
-    )
+    )
+    returned = {0: total(own_away, own_kept)}
+    arriving[0], *later = call(idle, [], [], after=[own_away], held=[arriving[0], *later])
     for k, rows in zip(groups[1], later):
         far_rows[k - 2] = rows
     arriving.append(joined(groups[1]))
-    returned = {0: total(own_away, own_kept)}
-    arriving[0] = hold(arriving[0], [own_away])
     others = [swap(arriving[0], "tp", 1)]
     high, low, upstream = call(
         functools.partial(mixing, experts),
@@ -404,9 +415,10 @@
 
     away, kept = through([arriving[0], others[0]], [returned[0], high])
     near_away, near_kept = through([near], [away])
+    near_away = hold(near_away, [others[1]])
     mixed = give_back(groups[0], away, kept)
     returned[1] = swap(total(near_away, near_kept, plain=True), "exp", 1)
-    away, kept = through([arriving[1], others[1]], [near_away, mixed])
+    away, kept = through([arriving[1], others[1]], [mixed])
     give_back(groups[1], away, kept)
 
     hidden_half = call(
@@ -439,18 +451,23 @@
         flops=2 * token_count * model_width * local_width,
     )[0]
     heads = token_count // SEQ * (local_width // HD)
-    away, kept, lows, values = call(
+    away, lows, values, dkeys, dvalues = call(
         attend,
         [
             shape_of((token_count, model_width // 2)),
-            shape_of((token_count, model_width // 2), WIDE),
             shape_of((heads, SEQ, SEQ)),
-            shape_of((token_count, local_width)),
+            *[shape_of((token_count, local_width))] * 3,
         ],
         [first, second, queries, upstream, key_weight[0], value_weight[0]],
-        [pltpu.VMEM((token_count, local_width), LOW)] * 3,
-        flops=10 * token_count * model_width * local_width,
-    )
+        [pltpu.VMEM((token_count, local_width), LOW)],
+        flops=8 * token_count * model_width * local_width,
+    )
+    kept = call(
+        keep,
+        [shape_of((token_count, model_width // 2), WIDE)],
+        [dkeys, dvalues, key_weight[0], value_weight[0]],
+        flops=2 * token_count * model_width * local_width,
+    )[0]
     context = call(
         contexts,
         [shape_of((token_count, local_width))],

time: 77.1 us -> 77.5 us (level)
  starting transfers between devices: 30.5 us -> 34.4 us
  waiting for transfers between devices: 29.9 us -> 26.5 us
    ppermute x16, starting transfers between devices: 24.8 us -> 28.8 us  [swap(): return lax.ppermute(block, axis, [(i, i ^ step) for i in range(size)])]
    ppermute x16, waiting for transfers between devices: 22.6 us -> 20.5 us  [swap(): return lax.ppermute(block, axis, [(i, i ^ step) for i in range(size)])]
    ppermute x3, waiting for transfers between devices: 4.36 us -> 2.88 us  [shards(): total = total + lax.ppermute(blocks[k], ('sec', 'tp'), pairs).astype(WIDE)]
    pallas_call x17 -> x19, Pallas kernels: 13.9 us -> 13.9 us  [call(): pl.pallas_call(run, out_shape=[*out_shape, *(shape_of(x.shape, x.dtype) f...]
  transfers between devices with their start and end apart: 21 -> 21, of which waited for: 15 -> 14; matrix products, arithmetic and copies ran while one was open for 0% -> 0% of each run, Pallas kernels for 16% -> 16%
where the time goes in v16:
time: 77.5 us; the launch traced here: 77.4 us
  starting transfers between devices  34.4 us (44%)
  waiting for transfers between devices  26.5 us (34%)
  Pallas kernels  13.9 us (18%)
  local copies, waits for them, and re-layouts  1.03 us (1%)
  between operations  0.82 us (1%)
    ppermute x16, starting transfers between devices, swap(): return lax.ppermute(block, axis, [(i, i ^ step) for i in range(size)])  28.8 us
    ppermute x16, waiting for transfers between devices, swap(): return lax.ppermute(block, axis, [(i, i ^ step) for i in range(size)])  20.5 us
    pallas_call x19, Pallas kernels, call(): pl.pallas_call(run, out_shape=[*out_shape, *(shape_of(x.shape, x.dtype) f...  13.9 us
    ppermute x3, starting transfers between devices, shards(): total = total + lax.ppermute(blocks[k], ('sec', 'tp'), pairs).astype(WIDE)  3.6 us
    ppermute x2, waiting for transfers between devices, cycle(): return lax.ppermute(hidden_half, ('sec', 'tp'), list(targets.items()))  3.17 us
    ppermute x3, waiting for transfers between devices, shards(): total = total + lax.ppermute(blocks[k], ('sec', 'tp'), pairs).astype(WIDE)  2.88 us
    ppermute x2, starting transfers between devices, cycle(): return lax.ppermute(hidden_half, ('sec', 'tp'), list(targets.items()))  1.97 us
  transfers between devices with their start and end apart: 21, of which 14 were waited for; matrix products, arithmetic and copies ran while one was open for 0% of the time, Pallas kernels for 16%

profile of v16, /device:TPU:0, one launch (start us, length us, event | category | flops | bytes accessed | tf_op | source)
XLA Modules:
  0.0 77.4 jit_solution(13507111248235498636)
XLA Ops:
  0.7 1.0 %copy-done.3 = bf16[1,256,1024]{2,1,0:T(8,128)(2,1)S(1)} copy-done((bf16[1,256,1024]{2,1,0:T(8,128)(2,1)S(1)}, bf16[1,256,1024]{2,1,0:T(8,128)(2,1)}, u32[]{:S(2)}) %copy-start.3) | copy-done | bytes 524312
  1.7 0.9 %shard_map.123 = (bf16[192,512]{1,0:T(8,128)(2,1)S(1)}, bf16[192,512]{1,0:T(8,128)(2,1)S(1)}, bf16[192,1024]{1,0:T(8,128)(2,1)S(1)}, bf16[192,1024]{1,0:T(8,128)(2,1)S(1)}) custom-call(bf16[256,1024]{1,0:T(8,128)(2,1)S(1)} %bitcast.19, s32[2,256]{1,0:T(2,128)S(1)} %bitcast.22, f32[1,1024]{1,0:T(1,128)S(1)} %copy-done.8, ...), custom_call_target="tpu_custom_call" | custom-call | flops 402653184 | bytes 1841152 | tf_op jit(solution)/shard_map/pallas_call | solution.py:40
  2.6 4.1 %collective-permute-start = (bf16[192,512]{1,0:T(8,128)(2,1)S(1)}, bf16[192,512]{1,0:T(8,128)(2,1)S(1)}, u32[]{:S(2)}, u32[]{:S(2)}) collective-permute-start(bf16[192,512]{1,0:T(8,128)(2,1)S(1)} %get-tuple-element.32), channel_id=1, source_target_pairs={{0,4},{2,6},{4,0},{6,2},{1,5},{3,7},{5,1},{7,3},{8,12},{10,14},{12... | collective-permute-start | bytes 589832 | tf_op jit(solution)/shard_map/ppermute | solution.py:304
  6.7 1.6 %collective-permute-start.2 = (bf16[192,1024]{1,0:T(8,128)(2,1)S(1)}, bf16[192,1024]{1,0:T(8,128)(2,1)S(1)}, u32[]{:S(2)}, u32[]{:S(2)}) collective-permute-start(bf16[192,1024]{1,0:T(8,128)(2,1)S(1)} %get-tuple-element.38), channel_id=1, source_target_pairs={{0,2},{2,0},{4,6},{6,4},{1,3},{3,1},{5,7},{7,5},{8,10},{10,8},{12,... | collective-permute-start | bytes 1179656 | tf_op jit(solution)/shard_map/ppermute | solution.py:304
  8.2 4.6 %shard_map.124 = (bf16[192,512]{1,0:T(8,128)(2,1)S(1)}, f32[192,512]{1,0:T(8,128)S(1)}, bf16[1024,2048]{1,0:T(8,128)(2,1)S(1)}, bf16[2048,1024]{1,0:T(8,128)(2,1)S(1)}) custom-call(bf16[192,1024]{1,0:T(8,128)(2,1)S(1)} %get-tuple-element.30.refs_0_, bf16[1024,2048]{1,0:T(8,128)(2,1)} %bitcast.25, bf16[2048,1024]{1,0:T(8,128)(2,1)} %bitcast.26), custom_call_target="tpu_custom_call" | custom-call | flops 1610612736 | bytes 17760256 | tf_op jit(solution)/shard_map/pallas_call | solution.py:40
  12.9 1.6 %collective-permute-start.1 = (bf16[192,512]{1,0:T(8,128)(2,1)S(1)}, bf16[192,512]{1,0:T(8,128)(2,1)S(1)}, u32[]{:S(2)}, u32[]{:S(2)}) collective-permute-start(bf16[192,512]{1,0:T(8,128)(2,1)S(1)} %get-tuple-element.31.refs_0_), channel_id=1, source_target_pairs={{0,1},{1,0},{2,3},{3,2},{4,5},{5,4},{6,7},{7,6},{8,9},{9,8},{10,11... | collective-permute-start | bytes 589832 | tf_op jit(solution)/shard_map/ppermute | solution.py:304
  14.4 1.4 %collective-permute-done.refs_1_ = bf16[192,512]{1,0:T(8,128)(2,1)S(1)} collective-permute-done((bf16[192,512]{1,0:T(8,128)(2,1)S(1)}, bf16[192,512]{1,0:T(8,128)(2,1)S(1)}, u32[]{:S(2)}, u32[]{:S(2)}) %collective-permute-start) | collective-permute-done | bytes 196640 | tf_op jit(solution)/shard_map/ppermute | solution.py:304
  15.9 3.5 %collective-permute-start.4 = (bf16[192,512]{1,0:T(8,128)(2,1)S(1)}, bf16[192,512]{1,0:T(8,128)(2,1)S(1)}, u32[]{:S(2)}, u32[]{:S(2)}) collective-permute-start(bf16[192,512]{1,0:T(8,128)(2,1)S(1)} %get-tuple-element.43), channel_id=1, source_target_pairs={{0,6},{2,4},{4,2},{6,0},{1,7},{3,5},{5,3},{7,1},{8,14},{10,12},{12... | collective-permute-start | bytes 589832 | tf_op jit(solution)/shard_map/ppermute | solution.py:304
  19.4 1.5 %collective-permute-start.3 = (bf16[192,512]{1,0:T(8,128)(2,1)S(1)}, bf16[192,512]{1,0:T(8,128)(2,1)S(1)}, u32[]{:S(2)}, u32[]{:S(2)}) collective-permute-start(bf16[192,512]{1,0:T(8,128)(2,1)S(1)} %get-tuple-element.34.refs_4_.refs_0_), channel_id=1, source_target_pairs={{0,1},{1,0},{2,3},{3,2},{4,5},{5,4},{6,7},{7,6},{8,9},{9,8},{10,11... | collective-permute-start | bytes 589832 | tf_op jit(solution)/shard_map/ppermute | solution.py:304
  21.0 0.6 shard_map.126
  21.6 3.8 %collective-permute-done.4.refs_0_ = bf16[192,512]{1,0:T(8,128)(2,1)S(1)} collective-permute-done((bf16[192,512]{1,0:T(8,128)(2,1)S(1)}, bf16[192,512]{1,0:T(8,128)(2,1)S(1)}, u32[]{:S(2)}, u32[]{:S(2)}) %collective-permute-start.4) | collective-permute-done | bytes 196640 | tf_op jit(solution)/shard_map/ppermute | solution.py:304
  25.4 1.5 %collective-permute-start.5 = (bf16[192,512]{1,0:T(8,128)(2,1)S(1)}, bf16[192,512]{1,0:T(8,128)(2,1)S(1)}, u32[]{:S(2)}, u32[]{:S(2)}) collective-permute-start(bf16[192,512]{1,0:T(8,128)(2,1)S(1)} %collective-permute-done.4.refs_0_), channel_id=1, source_target_pairs={{0,1},{1,0},{2,3},{3,2},{4,5},{5,4},{6,7},{7,6},{8,9},{9,8},{10,11... | collective-permute-start | bytes 589832 | tf_op jit(solution)/shard_map/ppermute | solution.py:304
  26.9 1.8 %shard_map.128 = (bf16[192,512]{1,0:T(8,128)(2,1)S(1)}, f32[192,512]{1,0:T(8,128)S(1)}) custom-call(bf16[192,512]{1,0:T(8,128)(2,1)S(1)} %get-tuple-element.34.refs_4_.refs_0_, bf16[192,512]{1,0:T(8,128)(2,1)S(1)} %collective-permute-done.3.refs_1_, bf16[1024,2048]{1,0:T(8,128)(2,1)S(1)} %get-tuple-element.39.refs_2_.refs_1_, ...), custom_call_target="tpu_custom_call" | custom-call | flops 1610612736 | bytes 9371648 | tf_op jit(solution)/shard_map/pallas_call | solution.py:40
  28.8 0.6 collective-permute-start.8
  29.3 1.8 %shard_map.129 = (bf16[192,512]{1,0:T(8,128)(2,1)S(1)}, f32[192,512]{1,0:T(8,128)S(1)}) custom-call(bf16[192,1024]{1,0:T(8,128)(2,1)S(1)} %collective-permute-done.2.refs_0_, bf16[1024,2048]{1,0:T(8,128)(2,1)S(1)} %get-tuple-element.39.refs_2_.refs_1_, bf16[2048,1024]{1,0:T(8,128)(2,1)S(1)} %get-tuple-element.40.refs_3_.refs_2_, ...), custom_call_target="tpu_custom_call" | custom-call | flops 1610612736 | bytes 9371648 | tf_op jit(solution)/shard_map/pallas_call | solution.py:40
  31.2 1.3 %collective-permute-done.5.refs_0_.refs_1_ = bf16[192,512]{1,0:T(8,128)(2,1)S(1)} collective-permute-done((bf16[192,512]{1,0:T(8,128)(2,1)S(1)}, bf16[192,512]{1,0:T(8,128)(2,1)S(1)}, u32[]{:S(2)}, u32[]{:S(2)}) %collective-permute-start.5) | collective-permute-done | bytes 196640 | tf_op jit(solution)/shard_map/ppermute | solution.py:304
  32.5 2.3 %collective-permute-start.6 = (bf16[192,512]{1,0:T(8,128)(2,1)S(1)}, bf16[192,512]{1,0:T(8,128)(2,1)S(1)}, u32[]{:S(2)}, u32[]{:S(2)}) collective-permute-start(bf16[192,512]{1,0:T(8,128)(2,1)S(1)} %shard_map.130), channel_id=1, source_target_pairs={{0,1},{1,0},{2,3},{3,2},{4,5},{5,4},{6,7},{7,6},{8,9},{9,8},{10,11... | collective-permute-start | bytes 589832 | tf_op jit(solution)/shard_map/ppermute | solution.py:304
  34.8 1.9 %collective-permute-done.8.refs_1_ = bf16[192,512]{1,0:T(8,128)(2,1)S(1)} collective-permute-done((bf16[192,512]{1,0:T(8,128)(2,1)S(1)}, bf16[192,512]{1,0:T(8,128)(2,1)S(1)}, u32[]{:S(2)}, u32[]{:S(2)}) %collective-permute-start.8) | collective-permute-done | bytes 196640 | tf_op jit(solution)/shard_map/ppermute | solution.py:304
  36.8 2.3 %collective-permute-start.9 = (bf16[192,512]{1,0:T(8,128)(2,1)S(1)}, bf16[192,512]{1,0:T(8,128)(2,1)S(1)}, u32[]{:S(2)}, u32[]{:S(2)}) collective-permute-start(bf16[192,512]{1,0:T(8,128)(2,1)S(1)} %shard_map.131.refs_4_), channel_id=1, source_target_pairs={{0,4},{2,6},{4,0},{6,2},{1,5},{3,7},{5,1},{7,3},{8,12},{10,14},{12... | collective-permute-start | bytes 589832 | tf_op jit(solution)/shard_map/ppermute | solution.py:304
  39.0 1.8 %shard_map.132 = (bf16[192,512]{1,0:T(8,128)(2,1)S(1)}, f32[192,512]{1,0:T(8,128)S(1)}) custom-call(bf16[192,512]{1,0:T(8,128)(2,1)S(1)} %collective-permute-done.4.refs_0_, bf16[192,512]{1,0:T(8,128)(2,1)S(1)} %collective-permute-done.5.refs_0_.refs_1_, bf16[1024,2048]{1,0:T(8,128)(2,1)S(1)} %get-tuple-element.39.refs_2_.refs_1_, ...), custom_call_target="tpu_custom_call" | custom-call | flops 1610612736 | bytes 9371648 | tf_op jit(solution)/shard_map/pallas_call | solution.py:40
  40.9 0.0 copy-start.2
  40.9 0.0 copy-start.5
  40.9 0.0 copy-start
  40.9 1.4 %collective-permute-start.10 = (bf16[192,512]{1,0:T(8,128)(2,1)S(1)}, bf16[192,512]{1,0:T(8,128)(2,1)S(1)}, u32[]{:S(2)}, u32[]{:S(2)}) collective-permute-start(bf16[192,512]{1,0:T(8,128)(2,1)S(1)} %get-tuple-element.47), channel_id=1, source_target_pairs={{0,1},{1,0},{2,3},{3,2},{4,5},{5,4},{6,7},{7,6},{8,9},{9,8},{10,11... | collective-permute-start | bytes 589832 | tf_op jit(solution)/shard_map/ppermute | solution.py:304
  42.4 2.0 %collective-permute-start.7 = (bf16[192,512]{1,0:T(8,128)(2,1)S(1)}, bf16[192,512]{1,0:T(8,128)(2,1)S(1)}, u32[]{:S(2)}, u32[]{:S(2)}) collective-permute-start(bf16[192,512]{1,0:T(8,128)(2,1)S(1)} %add_convert_fusion), channel_id=1, source_target_pairs={{0,2},{2,0},{4,6},{6,4},{1,3},{3,1},{5,7},{7,5},{8,10},{10,8},{12,... | collective-permute-start | bytes 589832 | tf_op jit(solution)/shard_map/ppermute | solution.py:304
  44.4 2.3 %collective-permute-done.10.refs_1_ = bf16[192,512]{1,0:T(8,128)(2,1)S(1)} collective-permute-done((bf16[192,512]{1,0:T(8,128)(2,1)S(1)}, bf16[192,512]{1,0:T(8,128)(2,1)S(1)}, u32[]{:S(2)}, u32[]{:S(2)}) %collective-permute-start.10) | collective-permute-done | bytes 196640 | tf_op jit(solution)/shard_map/ppermute | solution.py:304
  46.7 2.6 %collective-permute-start.11 = (bf16[192,512]{1,0:T(8,128)(2,1)S(1)}, bf16[192,512]{1,0:T(8,128)(2,1)S(1)}, u32[]{:S(2)}, u32[]{:S(2)}) collective-permute-start(bf16[192,512]{1,0:T(8,128)(2,1)S(1)} %shard_map.133), channel_id=1, source_target_pairs={{0,6},{2,4},{4,2},{6,0},{1,7},{3,5},{5,3},{7,1},{8,14},{10,12},{12... | collective-permute-start | bytes 589832 | tf_op jit(solution)/shard_map/ppermute | solution.py:304
  49.3 1.6 %collective-permute-done.7.refs_4_ = bf16[192,512]{1,0:T(8,128)(2,1)S(1)} collective-permute-done((bf16[192,512]{1,0:T(8,128)(2,1)S(1)}, bf16[192,512]{1,0:T(8,128)(2,1)S(1)}, u32[]{:S(2)}, u32[]{:S(2)}) %collective-permute-start.7) | collective-permute-done | bytes 196640 | tf_op jit(solution)/shard_map/ppermute | solution.py:304
  51.0 3.4 %collective-permute-done.11.refs_6_ = bf16[192,512]{1,0:T(8,128)(2,1)S(1)} collective-permute-done((bf16[192,512]{1,0:T(8,128)(2,1)S(1)}, bf16[192,512]{1,0:T(8,128)(2,1)S(1)}, u32[]{:S(2)}, u32[]{:S(2)}) %collective-permute-start.11) | collective-permute-done | bytes 196640 | tf_op jit(solution)/shard_map/ppermute | solution.py:304
  54.3 0.7 shard_map.134.refs_0_.refs_2_
  55.0 1.4 %collective-permute-start.12 = (bf16[256,512]{1,0:T(8,128)(2,1)S(1)}, bf16[256,512]{1,0:T(8,128)(2,1)S(1)}, u32[]{:S(2)}, u32[]{:S(2)}) collective-permute-start(bf16[256,512]{1,0:T(8,128)(2,1)S(1)} %shard_map.134.refs_0_.refs_2_), channel_id=1, source_target_pairs={{0,1},{1,0},{2,3},{3,2},{4,5},{5,4},{6,7},{7,6},{8,9},{9,8},{10,11... | collective-permute-start | bytes 786440 | tf_op jit(solution)/shard_map/ppermute | solution.py:304
  56.4 1.5 %collective-permute-start.14 = (bf16[256,512]{1,0:T(8,128)(2,1)S(1)}, bf16[256,512]{1,0:T(8,128)(2,1)S(1)}, u32[]{:S(2)}, u32[]{:S(2)}) collective-permute-start(bf16[256,512]{1,0:T(8,128)(2,1)S(1)} %shard_map.134.refs_0_.refs_2_), channel_id=1, source_target_pairs={{0,16},{1,17},{8,0},{9,1},{16,24},{17,25},{24,8},{25,9},{2,18},{3,... | collective-permute-start | bytes 786440 | tf_op jit(solution)/shard_map/ppermute | solution.py:439
  57.9 0.5 collective-permute-start.15
  58.4 3.0 %collective-permute-done.12.refs_0_.refs_1_ = bf16[256,512]{1,0:T(8,128)(2,1)S(1)} collective-permute-done((bf16[256,512]{1,0:T(8,128)(2,1)S(1)}, bf16[256,512]{1,0:T(8,128)(2,1)S(1)}, u32[]{:S(2)}, u32[]{:S(2)}) %collective-permute-start.12) | collective-permute-done | bytes 262176 | tf_op jit(solution)/shard_map/ppermute | solution.py:304
  61.5 0.4 collective-permute-done.14.refs_2_
  61.8 2.8 %collective-permute-done.15.refs_3_ = bf16[256,512]{1,0:T(8,128)(2,1)S(1)} collective-permute-done((bf16[256,512]{1,0:T(8,128)(2,1)S(1)}, bf16[256,512]{1,0:T(8,128)(2,1)S(1)}, u32[]{:S(2)}, u32[]{:S(2)}) %collective-permute-start.15) | collective-permute-done | bytes 262176 | tf_op jit(solution)/shard_map/ppermute | solution.py:439
  64.7 0.4 collective-permute-start.16
  65.1 0.7 shard_map.136.refs_2_
  65.8 0.5 collective-permute-done.16.refs_1_
  66.3 2.0 %collective-permute-start.17 = (bf16[256,512]{1,0:T(8,128)(2,1)S(1)}, bf16[256,512]{1,0:T(8,128)(2,1)S(1)}, u32[]{:S(2)}, u32[]{:S(2)}) collective-permute-start(bf16[256,512]{1,0:T(8,128)(2,1)S(1)} %get-tuple-element.53), channel_id=1, source_target_pairs={{0,8},{8,0},{16,24},{24,16},{1,9},{9,1},{17,25},{25,17},{2,10},{10... | collective-permute-start | bytes 786440 | tf_op jit(solution)/shard_map/ppermute | solution.py:304
  68.3 1.1 %collective-permute-done.17.refs_1_ = bf16[256,512]{1,0:T(8,128)(2,1)S(1)} collective-permute-done((bf16[256,512]{1,0:T(8,128)(2,1)S(1)}, bf16[256,512]{1,0:T(8,128)(2,1)S(1)}, u32[]{:S(2)}, u32[]{:S(2)}) %collective-permute-start.17) | collective-permute-done | bytes 262176 | tf_op jit(solution)/shard_map/ppermute | solution.py:304
  69.4 0.1 shard_map.140
  69.5 2.9 %collective-permute-start.20 = (bf16[256,128]{1,0:T(8,128)(2,1)S(1)}, bf16[256,128]{1,0:T(8,128)(2,1)S(1)}, u32[]{:S(2)}, u32[]{:S(2)}) collective-permute-start(bf16[256,128]{1,0:T(8,128)(2,1)S(1)} %get-tuple-element.57), channel_id=1, source_target_pairs={{0,17},{1,16},{8,25},{9,24},{16,1},{17,0},{24,9},{25,8},{2,19},{3,... | collective-permute-start | bytes 196616 | tf_op jit(solution)/shard_map/ppermute | solution.py:493
  72.5 0.7 collective-permute-start.18
  73.1 0.7 shard_map.138
  73.9 1.2 %collective-permute-done.20 = bf16[256,128]{1,0:T(8,128)(2,1)S(1)} collective-permute-done((bf16[256,128]{1,0:T(8,128)(2,1)S(1)}, bf16[256,128]{1,0:T(8,128)(2,1)S(1)}, u32[]{:S(2)}, u32[]{:S(2)}) %collective-permute-start.20) | collective-permute-done | bytes 65568 | tf_op jit(solution)/shard_map/ppermute | solution.py:493
  75.1 1.6 %collective-permute-done.19 = bf16[256,128]{1,0:T(8,128)(2,1)S(1)} collective-permute-done((bf16[256,128]{1,0:T(8,128)(2,1)S(1)}, bf16[256,128]{1,0:T(8,128)(2,1)S(1)}, u32[]{:S(2)}, u32[]{:S(2)}) %collective-permute-start.19) | collective-permute-done | bytes 65568 | tf_op jit(solution)/shard_map/ppermute | solution.py:493
  76.7 0.7 add_convert_fusion.1
  (33 shorter events, 0.3 us)
Async XLA Ops:
  0.6 1.0 %copy-start.3 = (bf16[1,256,1024]{2,1,0:T(8,128)(2,1)S(1)}, bf16[1,256,1024]{2,1,0:T(8,128)(2,1)}, u32[]{:S(2)}) copy-start(bf16[1,256,1024]{2,1,0:T(8,128)(2,1)} %param.11) | copy-start | bytes 1572868
  0.6 1.0 %copy-start.6 = (s32[1,256,2]{1,2,0:T(2,128)S(1)}, s32[1,256,2]{1,2,0:T(2,128)}, u32[]{:S(2)}) copy-start(s32[1,256,2]{1,2,0:T(2,128)} %param.12) | copy-start | bytes 6148
  0.6 1.0 %copy-start.8 = (f32[1,1024]{1,0:T(1,128)S(1)}, f32[1,1024]{1,0:T(1,128)}, u32[]{:S(2)}) copy-start(f32[1,1024]{1,0:T(1,128)} %refs_2_.2) | copy-start | bytes 12292
  2.6 13.3 %collective-permute-start = (bf16[192,512]{1,0:T(8,128)(2,1)S(1)}, bf16[192,512]{1,0:T(8,128)(2,1)S(1)}, u32[]{:S(2)}, u32[]{:S(2)}) collective-permute-start(bf16[192,512]{1,0:T(8,128)(2,1)S(1)} %get-tuple-element.32), channel_id=1, source_target_pairs={{0,4},{2,6},{4,0},{6,2},{1,5},{3,7},{5,1},{7,3},{8,12},{10,14},{12... | collective-permute-start | bytes 589832 | tf_op jit(solution)/shard_map/ppermute | solution.py:304
  6.7 22.7 %collective-permute-start.2 = (bf16[192,1024]{1,0:T(8,128)(2,1)S(1)}, bf16[192,1024]{1,0:T(8,128)(2,1)S(1)}, u32[]{:S(2)}, u32[]{:S(2)}) collective-permute-start(bf16[192,1024]{1,0:T(8,128)(2,1)S(1)} %get-tuple-element.38), channel_id=1, source_target_pairs={{0,2},{2,0},{4,6},{6,4},{1,3},{3,1},{5,7},{7,5},{8,10},{10,8},{12,... | collective-permute-start | bytes 1179656 | tf_op jit(solution)/shard_map/ppermute | solution.py:304
  8.2 12.7 %copy-start.4 = (bf16[1,256,512]{2,1,0:T(8,128)(2,1)S(1)}, bf16[1,256,512]{2,1,0:T(8,128)(2,1)}, u32[]{:S(2)}) copy-start(bf16[1,256,512]{2,1,0:T(8,128)(2,1)} %param.21) | copy-start | bytes 786436
  8.2 12.7 %copy-start.7 = (f32[1,256,2]{1,2,0:T(2,128)S(1)}, f32[1,256,2]{1,2,0:T(2,128)}, u32[]{:S(2)}) copy-start(f32[1,256,2]{1,2,0:T(2,128)} %param.13) | copy-start | bytes 6148
  12.9 8.7 %collective-permute-start.1 = (bf16[192,512]{1,0:T(8,128)(2,1)S(1)}, bf16[192,512]{1,0:T(8,128)(2,1)S(1)}, u32[]{:S(2)}, u32[]{:S(2)}) collective-permute-start(bf16[192,512]{1,0:T(8,128)(2,1)S(1)} %get-tuple-element.31.refs_0_), channel_id=1, source_target_pairs={{0,1},{1,0},{2,3},{3,2},{4,5},{5,4},{6,7},{7,6},{8,9},{9,8},{10,11... | collective-permute-start | bytes 589832 | tf_op jit(solution)/shard_map/ppermute | solution.py:304
  15.9 9.5 %collective-permute-start.4 = (bf16[192,512]{1,0:T(8,128)(2,1)S(1)}, bf16[192,512]{1,0:T(8,128)(2,1)S(1)}, u32[]{:S(2)}, u32[]{:S(2)}) collective-permute-start(bf16[192,512]{1,0:T(8,128)(2,1)S(1)} %get-tuple-element.43), channel_id=1, source_target_pairs={{0,6},{2,4},{4,2},{6,0},{1,7},{3,5},{5,3},{7,1},{8,14},{10,12},{12... | collective-permute-start | bytes 589832 | tf_op jit(solution)/shard_map/ppermute | solution.py:304
  19.4 7.5 %collective-permute-start.3 = (bf16[192,512]{1,0:T(8,128)(2,1)S(1)}, bf16[192,512]{1,0:T(8,128)(2,1)S(1)}, u32[]{:S(2)}, u32[]{:S(2)}) collective-permute-start(bf16[192,512]{1,0:T(8,128)(2,1)S(1)} %get-tuple-element.34.refs_4_.refs_0_), channel_id=1, source_target_pairs={{0,1},{1,0},{2,3},{3,2},{4,5},{5,4},{6,7},{7,6},{8,9},{9,8},{10,11... | collective-permute-start | bytes 589832 | tf_op jit(solution)/shard_map/ppermute | solution.py:304
  25.4 7.1 %collective-permute-start.5 = (bf16[192,512]{1,0:T(8,128)(2,1)S(1)}, bf16[192,512]{1,0:T(8,128)(2,1)S(1)}, u32[]{:S(2)}, u32[]{:S(2)}) collective-permute-start(bf16[192,512]{1,0:T(8,128)(2,1)S(1)} %collective-permute-done.4.refs_0_), channel_id=1, source_target_pairs={{0,1},{1,0},{2,3},{3,2},{4,5},{5,4},{6,7},{7,6},{8,9},{9,8},{10,11... | collective-permute-start | bytes 589832 | tf_op jit(solution)/shard_map/ppermute | solution.py:304
  28.8 8.0 %collective-permute-start.8 = (bf16[192,512]{1,0:T(8,128)(2,1)S(1)}, bf16[192,512]{1,0:T(8,128)(2,1)S(1)}, u32[]{:S(2)}, u32[]{:S(2)}) collective-permute-start(bf16[192,512]{1,0:T(8,128)(2,1)S(1)} %get-tuple-element.41.refs_3_), channel_id=1, source_target_pairs={{0,1},{1,0},{2,3},{3,2},{4,5},{5,4},{6,7},{7,6},{8,9},{9,8},{10,11... | collective-permute-start | bytes 589832 | tf_op jit(solution)/shard_map/ppermute | solution.py:304
  32.5 9.8 %collective-permute-start.6 = (bf16[192,512]{1,0:T(8,128)(2,1)S(1)}, bf16[192,512]{1,0:T(8,128)(2,1)S(1)}, u32[]{:S(2)}, u32[]{:S(2)}) collective-permute-start(bf16[192,512]{1,0:T(8,128)(2,1)S(1)} %shard_map.130), channel_id=1, source_target_pairs={{0,1},{1,0},{2,3},{3,2},{4,5},{5,4},{6,7},{7,6},{8,9},{9,8},{10,11... | collective-permute-start | bytes 589832 | tf_op jit(solution)/shard_map/ppermute | solution.py:304
  36.8 12.6 %collective-permute-start.9 = (bf16[192,512]{1,0:T(8,128)(2,1)S(1)}, bf16[192,512]{1,0:T(8,128)(2,1)S(1)}, u32[]{:S(2)}, u32[]{:S(2)}) collective-permute-start(bf16[192,512]{1,0:T(8,128)(2,1)S(1)} %shard_map.131.refs_4_), channel_id=1, source_target_pairs={{0,4},{2,6},{4,0},{6,2},{1,5},{3,7},{5,1},{7,3},{8,12},{10,14},{12... | collective-permute-start | bytes 589832 | tf_op jit(solution)/shard_map/ppermute | solution.py:304
  40.9 24.2 %copy-start.2 = (bf16[1,1024,512]{2,1,0:T(8,128)(2,1)S(1)}, bf16[1,1024,512]{2,1,0:T(8,128)(2,1)}, u32[]{:S(2)}) copy-start(bf16[1,1024,512]{2,1,0:T(8,128)(2,1)} %param.18) | copy-start | bytes 3145732
  40.9 24.2 %copy-start.5 = (f32[1,1024]{1,0:T(1,128)S(1)}, f32[1,1024]{1,0:T(1,128)}, u32[]{:S(2)}) copy-start(f32[1,1024]{1,0:T(1,128)} %refs_2_.3) | copy-start | bytes 12292
  40.9 25.4 %copy-start = (bf16[1,1024,512]{2,1,0:T(8,128)(2,1)S(1)}, bf16[1,1024,512]{2,1,0:T(8,128)(2,1)}, u32[]{:S(2)}) copy-start(bf16[1,1024,512]{2,1,0:T(8,128)(2,1)} %param.19) | copy-start | bytes 3145732
  40.9 25.4 %copy-start.1 = (bf16[1,1024,512]{2,1,0:T(8,128)(2,1)S(1)}, bf16[1,1024,512]{2,1,0:T(8,128)(2,1)}, u32[]{:S(2)}) copy-start(bf16[1,1024,512]{2,1,0:T(8,128)(2,1)} %param.20) | copy-start | bytes 3145732
  40.9 5.7 %collective-permute-start.10 = (bf16[192,512]{1,0:T(8,128)(2,1)S(1)}, bf16[192,512]{1,0:T(8,128)(2,1)S(1)}, u32[]{:S(2)}, u32[]{:S(2)}) collective-permute-start(bf16[192,512]{1,0:T(8,128)(2,1)S(1)} %get-tuple-element.47), channel_id=1, source_target_pairs={{0,1},{1,0},{2,3},{3,2},{4,5},{5,4},{6,7},{7,6},{8,9},{9,8},{10,11... | collective-permute-start | bytes 589832 | tf_op jit(solution)/shard_map/ppermute | solution.py:304
  42.4 8.6 %collective-permute-start.7 = (bf16[192,512]{1,0:T(8,128)(2,1)S(1)}, bf16[192,512]{1,0:T(8,128)(2,1)S(1)}, u32[]{:S(2)}, u32[]{:S(2)}) collective-permute-start(bf16[192,512]{1,0:T(8,128)(2,1)S(1)} %add_convert_fusion), channel_id=1, source_target_pairs={{0,2},{2,0},{4,6},{6,4},{1,3},{3,1},{5,7},{7,5},{8,10},{10,8},{12,... | collective-permute-start | bytes 589832 | tf_op jit(solution)/shard_map/ppermute | solution.py:304
  46.7 7.6 %collective-permute-start.11 = (bf16[192,512]{1,0:T(8,128)(2,1)S(1)}, bf16[192,512]{1,0:T(8,128)(2,1)S(1)}, u32[]{:S(2)}, u32[]{:S(2)}) collective-permute-start(bf16[192,512]{1,0:T(8,128)(2,1)S(1)} %shard_map.133), channel_id=1, source_target_pairs={{0,6},{2,4},{4,2},{6,0},{1,7},{3,5},{5,3},{7,1},{8,14},{10,12},{12... | collective-permute-start | bytes 589832 | tf_op jit(solution)/shard_map/ppermute | solution.py:304
  55.0 6.4 %collective-permute-start.12 = (bf16[256,512]{1,0:T(8,128)(2,1)S(1)}, bf16[256,512]{1,0:T(8,128)(2,1)S(1)}, u32[]{:S(2)}, u32[]{:S(2)}) collective-permute-start(bf16[256,512]{1,0:T(8,128)(2,1)S(1)} %shard_map.134.refs_0_.refs_2_), channel_id=1, source_target_pairs={{0,1},{1,0},{2,3},{3,2},{4,5},{5,4},{6,7},{7,6},{8,9},{9,8},{10,11... | collective-permute-start | bytes 786440 | tf_op jit(solution)/shard_map/ppermute | solution.py:304
  56.4 5.0 %collective-permute-start.13 = (bf16[256,512]{1,0:T(8,128)(2,1)S(1)}, bf16[256,512]{1,0:T(8,128)(2,1)S(1)}, u32[]{:S(2)}, u32[]{:S(2)}) collective-permute-start(bf16[256,512]{1,0:T(8,128)(2,1)S(1)} %shard_map.134.refs_0_.refs_2_), channel_id=1, source_target_pairs={{0,8},{8,0},{16,24},{24,16},{1,9},{9,1},{17,25},{25,17},{2,10},{10... | collective-permute-start | bytes 786440 | tf_op jit(solution)/shard_map/ppermute | solution.py:304
  56.4 5.4 %collective-permute-start.14 = (bf16[256,512]{1,0:T(8,128)(2,1)S(1)}, bf16[256,512]{1,0:T(8,128)(2,1)S(1)}, u32[]{:S(2)}, u32[]{:S(2)}) collective-permute-start(bf16[256,512]{1,0:T(8,128)(2,1)S(1)} %shard_map.134.refs_0_.refs_2_), channel_id=1, source_target_pairs={{0,16},{1,17},{8,0},{9,1},{16,24},{17,25},{24,8},{25,9},{2,18},{3,... | collective-permute-start | bytes 786440 | tf_op jit(solution)/shard_map/ppermute | solution.py:439
  57.9 6.7 %collective-permute-start.15 = (bf16[256,512]{1,0:T(8,128)(2,1)S(1)}, bf16[256,512]{1,0:T(8,128)(2,1)S(1)}, u32[]{:S(2)}, u32[]{:S(2)}) collective-permute-start(bf16[256,512]{1,0:T(8,128)(2,1)S(1)} %shard_map.134.refs_0_.refs_2_), channel_id=1, source_target_pairs={{0,25},{1,24},{8,0},{9,1},{16,8},{17,9},{24,16},{25,17},{2,27},{3,... | collective-permute-start | bytes 786440 | tf_op jit(solution)/shard_map/ppermute | solution.py:439
  64.7 1.6 %collective-permute-start.16 = (bf16[256,512]{1,0:T(8,128)(2,1)S(1)}, bf16[256,512]{1,0:T(8,128)(2,1)S(1)}, u32[]{:S(2)}, u32[]{:S(2)}) collective-permute-start(bf16[256,512]{1,0:T(8,128)(2,1)S(1)} %shard_map.135.refs_0_), channel_id=1, source_target_pairs={{0,8},{8,0},{16,24},{24,16},{1,9},{9,1},{17,25},{25,17},{2,10},{10... | collective-permute-start | bytes 786440 | tf_op jit(solution)/shard_map/ppermute | solution.py:304
  66.3 3.1 %collective-permute-start.17 = (bf16[256,512]{1,0:T(8,128)(2,1)S(1)}, bf16[256,512]{1,0:T(8,128)(2,1)S(1)}, u32[]{:S(2)}, u32[]{:S(2)}) collective-permute-start(bf16[256,512]{1,0:T(8,128)(2,1)S(1)} %get-tuple-element.53), channel_id=1, source_target_pairs={{0,8},{8,0},{16,24},{24,16},{1,9},{9,1},{17,25},{25,17},{2,10},{10... | collective-permute-start | bytes 786440 | tf_op jit(solution)/shard_map/ppermute | solution.py:304
  69.5 5.5 %collective-permute-start.20 = (bf16[256,128]{1,0:T(8,128)(2,1)S(1)}, bf16[256,128]{1,0:T(8,128)(2,1)S(1)}, u32[]{:S(2)}, u32[]{:S(2)}) collective-permute-start(bf16[256,128]{1,0:T(8,128)(2,1)S(1)} %get-tuple-element.57), channel_id=1, source_target_pairs={{0,17},{1,16},{8,25},{9,24},{16,1},{17,0},{24,9},{25,8},{2,19},{3,... | collective-permute-start | bytes 196616 | tf_op jit(solution)/shard_map/ppermute | solution.py:493
  72.5 4.3 %collective-permute-start.19 = (bf16[256,128]{1,0:T(8,128)(2,1)S(1)}, bf16[256,128]{1,0:T(8,128)(2,1)S(1)}, u32[]{:S(2)}, u32[]{:S(2)}) collective-permute-start(bf16[256,128]{1,0:T(8,128)(2,1)S(1)} %get-tuple-element.56), channel_id=1, source_target_pairs={{0,16},{1,17},{8,24},{9,25},{16,0},{17,1},{24,8},{25,9},{2,18},{3,... | collective-permute-start | bytes 196616 | tf_op jit(solution)/shard_map/ppermute | solution.py:493
  72.5 4.3 %collective-permute-start.18 = (bf16[256,128]{1,0:T(8,128)(2,1)S(1)}, bf16[256,128]{1,0:T(8,128)(2,1)S(1)}, u32[]{:S(2)}, u32[]{:S(2)}) collective-permute-start(bf16[256,128]{1,0:T(8,128)(2,1)S(1)} %get-tuple-element.55), channel_id=1, source_target_pairs={{0,1},{1,0},{8,9},{9,8},{16,17},{17,16},{24,25},{25,24},{2,3},{3,2... | collective-permute-start | bytes 196616 | tf_op jit(solution)/shard_map/ppermute | solution.py:493

commit v17 on v16

--- a/solution.py
+++ b/solution.py
@@ -376,7 +376,7 @@
     near = swap(near_rows, "exp", 1)
     later = [far_rows[k - 2] for k in groups[1]]
     loads = max(1, units // 512) + 1
-    own_away, own_kept, weight_first, weight_second = call(
+    own_away, own_kept, weight_first, weight_second, *later = call(
         expert_first,
         [
             row_half,
@@ -389,12 +389,13 @@
         flops=4 * capacity * model_width * units,
         remote=(1, 2),
         limit=44,
-    )
-    returned = {0: total(own_away, own_kept)}
-    arriving[0], *later = call(idle, [], [], after=[own_away], held=[arriving[0], *later])
+        held=later,
+    )
     for k, rows in zip(groups[1], later):
         far_rows[k - 2] = rows
     arriving.append(joined(groups[1]))
+    returned = {0: total(own_away, own_kept)}
+    arriving[0] = hold(arriving[0], [own_away])
     others = [swap(arriving[0], "tp", 1)]
     high, low, upstream = call(
         functools.partial(mixing, experts),
@@ -415,10 +416,9 @@
 
     away, kept = through([arriving[0], others[0]], [returned[0], high])
     near_away, near_kept = through([near], [away])
-    near_away = hold(near_away, [others[1]])
     mixed = give_back(groups[0], away, kept)
     returned[1] = swap(total(near_away, near_kept, plain=True), "exp", 1)
-    away, kept = through([arriving[1], others[1]], [mixed])
+    away, kept = through([arriving[1], others[1]], [near_away, mixed])
     give_back(groups[1], away, kept)
 
     hidden_half = call(

time: 77.5 us -> 76.8 us (level)
  starting transfers between devices: 34.4 us -> 30.3 us
  waiting for transfers between devices: 26.5 us -> 29.9 us
    ppermute x16, starting transfers between devices: 28.8 us -> 24.6 us  [swap(): return lax.ppermute(block, axis, [(i, i ^ step) for i in range(size)])]
    ppermute x16, waiting for transfers between devices: 20.5 us -> 22.5 us  [swap(): return lax.ppermute(block, axis, [(i, i ^ step) for i in range(size)])]
    ppermute x3, waiting for transfers between devices: 2.88 us -> 4.36 us  [shards(): total = total + lax.ppermute(blocks[k], ('sec', 'tp'), pairs).astype(WIDE)]
    pallas_call x19 -> x18, Pallas kernels: 13.9 us -> 14 us  [call(): pl.pallas_call(run, out_shape=[*out_shape, *(shape_of(x.shape, x.dtype) f...]
  transfers between devices with their start and end apart: 21 -> 21, of which waited for: 14 -> 15; matrix products, arithmetic and copies ran while one was open for 0% -> 0% of each run, Pallas kernels for 16% -> 16%
where the time goes in v17:
time: 76.8 us; the launch traced here: 76.7 us
  starting transfers between devices  30.3 us (39%)
  waiting for transfers between devices  29.9 us (39%)
  Pallas kernels  14 us (18%)
  local copies, waits for them, and re-layouts  1.03 us (1%)
  between operations  0.82 us (1%)
    ppermute x16, starting transfers between devices, swap(): return lax.ppermute(block, axis, [(i, i ^ step) for i in range(size)])  24.6 us
    ppermute x16, waiting for transfers between devices, swap(): return lax.ppermute(block, axis, [(i, i ^ step) for i in range(size)])  22.5 us
    pallas_call x18, Pallas kernels, call(): pl.pallas_call(run, out_shape=[*out_shape, *(shape_of(x.shape, x.dtype) f...  14 us
    ppermute x3, waiting for transfers between devices, shards(): total = total + lax.ppermute(blocks[k], ('sec', 'tp'), pairs).astype(WIDE)  4.36 us
    ppermute x3, starting transfers between devices, shards(): total = total + lax.ppermute(blocks[k], ('sec', 'tp'), pairs).astype(WIDE)  3.57 us
    ppermute x2, waiting for transfers between devices, cycle(): return lax.ppermute(hidden_half, ('sec', 'tp'), list(targets.items()))  2.98 us
    ppermute x2, starting transfers between devices, cycle(): return lax.ppermute(hidden_half, ('sec', 'tp'), list(targets.items()))  2.16 us
  transfers between devices with their start and end apart: 21, of which 15 were waited for; matrix products, arithmetic and copies ran while one was open for 0% of the time, Pallas kernels for 16%

profile of v17, /device:TPU:0, one launch (start us, length us, event | category | flops | bytes accessed | tf_op | source)
XLA Modules:
  0.0 76.7 jit_solution(7504106826215927784)
XLA Ops:
  0.7 1.0 %copy-done.3 = bf16[1,256,1024]{2,1,0:T(8,128)(2,1)S(1)} copy-done((bf16[1,256,1024]{2,1,0:T(8,128)(2,1)S(1)}, bf16[1,256,1024]{2,1,0:T(8,128)(2,1)}, u32[]{:S(2)}) %copy-start.3) | copy-done | bytes 524312
  1.7 0.9 %shard_map.123 = (bf16[192,512]{1,0:T(8,128)(2,1)S(1)}, bf16[192,512]{1,0:T(8,128)(2,1)S(1)}, bf16[192,1024]{1,0:T(8,128)(2,1)S(1)}, bf16[192,1024]{1,0:T(8,128)(2,1)S(1)}) custom-call(bf16[256,1024]{1,0:T(8,128)(2,1)S(1)} %bitcast.19, s32[2,256]{1,0:T(2,128)S(1)} %bitcast.22, f32[1,1024]{1,0:T(1,128)S(1)} %copy-done.8, ...), custom_call_target="tpu_custom_call" | custom-call | flops 402653184 | bytes 1841152 | tf_op jit(solution)/shard_map/pallas_call | solution.py:40
  2.6 4.1 %collective-permute-start = (bf16[192,512]{1,0:T(8,128)(2,1)S(1)}, bf16[192,512]{1,0:T(8,128)(2,1)S(1)}, u32[]{:S(2)}, u32[]{:S(2)}) collective-permute-start(bf16[192,512]{1,0:T(8,128)(2,1)S(1)} %get-tuple-element.32), channel_id=1, source_target_pairs={{0,4},{2,6},{4,0},{6,2},{1,5},{3,7},{5,1},{7,3},{8,12},{10,14},{12... | collective-permute-start | bytes 589832 | tf_op jit(solution)/shard_map/ppermute | solution.py:304
  6.7 1.6 %collective-permute-start.2 = (bf16[192,1024]{1,0:T(8,128)(2,1)S(1)}, bf16[192,1024]{1,0:T(8,128)(2,1)S(1)}, u32[]{:S(2)}, u32[]{:S(2)}) collective-permute-start(bf16[192,1024]{1,0:T(8,128)(2,1)S(1)} %get-tuple-element.36), channel_id=1, source_target_pairs={{0,2},{2,0},{4,6},{6,4},{1,3},{3,1},{5,7},{7,5},{8,10},{10,8},{12,... | collective-permute-start | bytes 1179656 | tf_op jit(solution)/shard_map/ppermute | solution.py:304
  8.2 4.6 %shard_map.124 = (bf16[192,512]{1,0:T(8,128)(2,1)S(1)}, f32[192,512]{1,0:T(8,128)S(1)}, bf16[1024,2048]{1,0:T(8,128)(2,1)S(1)}, bf16[2048,1024]{1,0:T(8,128)(2,1)S(1)}, bf16[192,512]{1,0:T(8,128)(2,1)S(1)}) custom-call(bf16[192,1024]{1,0:T(8,128)(2,1)S(1)} %get-tuple-element.29.refs_0_, ...), custom_call_target="tpu_custom_call", output_to_operand_aliasing={{4}: (3, {})} | custom-call | flops 1610612736 | bytes 17760256 | tf_op jit(solution)/shard_map/pallas_call | solution.py:40
  12.9 1.6 %collective-permute-start.1 = (bf16[192,512]{1,0:T(8,128)(2,1)S(1)}, bf16[192,512]{1,0:T(8,128)(2,1)S(1)}, u32[]{:S(2)}, u32[]{:S(2)}) collective-permute-start(bf16[192,512]{1,0:T(8,128)(2,1)S(1)} %get-tuple-element.31.refs_0_), channel_id=1, source_target_pairs={{0,1},{1,0},{2,3},{3,2},{4,5},{5,4},{6,7},{7,6},{8,9},{9,8},{10,11... | collective-permute-start | bytes 589832 | tf_op jit(solution)/shard_map/ppermute | solution.py:304
  14.4 1.4 %collective-permute-done.refs_1_ = bf16[192,512]{1,0:T(8,128)(2,1)S(1)} collective-permute-done((bf16[192,512]{1,0:T(8,128)(2,1)S(1)}, bf16[192,512]{1,0:T(8,128)(2,1)S(1)}, u32[]{:S(2)}, u32[]{:S(2)}) %collective-permute-start) | collective-permute-done | bytes 196640 | tf_op jit(solution)/shard_map/ppermute | solution.py:304
  15.9 1.6 %collective-permute-start.3 = (bf16[192,512]{1,0:T(8,128)(2,1)S(1)}, bf16[192,512]{1,0:T(8,128)(2,1)S(1)}, u32[]{:S(2)}, u32[]{:S(2)}) collective-permute-start(bf16[192,512]{1,0:T(8,128)(2,1)S(1)} %shard_map.125.refs_4_.refs_0_), channel_id=1, source_target_pairs={{0,1},{1,0},{2,3},{3,2},{4,5},{5,4},{6,7},{7,6},{8,9},{9,8},{10,11... | collective-permute-start | bytes 589832 | tf_op jit(solution)/shard_map/ppermute | solution.py:304
  17.5 3.5 %collective-permute-start.8 = (bf16[192,512]{1,0:T(8,128)(2,1)S(1)}, bf16[192,512]{1,0:T(8,128)(2,1)S(1)}, u32[]{:S(2)}, u32[]{:S(2)}) collective-permute-start(bf16[192,512]{1,0:T(8,128)(2,1)S(1)} %get-tuple-element.43), channel_id=1, source_target_pairs={{0,6},{2,4},{4,2},{6,0},{1,7},{3,5},{5,3},{7,1},{8,14},{10,12},{12... | collective-permute-start | bytes 589832 | tf_op jit(solution)/shard_map/ppermute | solution.py:304
  21.0 0.6 shard_map.126
  21.6 1.6 %collective-permute-done.3.refs_1_ = bf16[192,512]{1,0:T(8,128)(2,1)S(1)} collective-permute-done((bf16[192,512]{1,0:T(8,128)(2,1)S(1)}, bf16[192,512]{1,0:T(8,128)(2,1)S(1)}, u32[]{:S(2)}, u32[]{:S(2)}) %collective-permute-start.3) | collective-permute-done | bytes 196640 | tf_op jit(solution)/shard_map/ppermute | solution.py:304
  23.2 1.8 %shard_map.128 = (bf16[192,512]{1,0:T(8,128)(2,1)S(1)}, f32[192,512]{1,0:T(8,128)S(1)}) custom-call(bf16[192,512]{1,0:T(8,128)(2,1)S(1)} %shard_map.125.refs_4_.refs_0_, bf16[192,512]{1,0:T(8,128)(2,1)S(1)} %collective-permute-done.3.refs_1_, bf16[1024,2048]{1,0:T(8,128)(2,1)S(1)} %get-tuple-element.37.refs_2_.refs_1_, ...), custom_call_target="tpu_custom_call" | custom-call | flops 1610612736 | bytes 9371648 | tf_op jit(solution)/shard_map/pallas_call | solution.py:40
  25.0 1.6 %collective-permute-start.6 = (bf16[192,512]{1,0:T(8,128)(2,1)S(1)}, bf16[192,512]{1,0:T(8,128)(2,1)S(1)}, u32[]{:S(2)}, u32[]{:S(2)}) collective-permute-start(bf16[192,512]{1,0:T(8,128)(2,1)S(1)} %get-tuple-element.39.refs_3_), channel_id=1, source_target_pairs={{0,1},{1,0},{2,3},{3,2},{4,5},{5,4},{6,7},{7,6},{8,9},{9,8},{10,11... | collective-permute-start | bytes 589832 | tf_op jit(solution)/shard_map/ppermute | solution.py:304
  26.6 0.5 collective-permute-start.9
  27.1 1.8 %shard_map.129 = (bf16[192,512]{1,0:T(8,128)(2,1)S(1)}, f32[192,512]{1,0:T(8,128)S(1)}) custom-call(bf16[192,1024]{1,0:T(8,128)(2,1)S(1)} %collective-permute-done.2.refs_0_, bf16[1024,2048]{1,0:T(8,128)(2,1)S(1)} %get-tuple-element.37.refs_2_.refs_1_, bf16[2048,1024]{1,0:T(8,128)(2,1)S(1)} %get-tuple-element.38.refs_3_.refs_2_, ...), custom_call_target="tpu_custom_call" | custom-call | flops 1610612736 | bytes 9371648 | tf_op jit(solution)/shard_map/pallas_call | solution.py:40
  29.0 1.6 %collective-permute-start.4 = (bf16[192,512]{1,0:T(8,128)(2,1)S(1)}, bf16[192,512]{1,0:T(8,128)(2,1)S(1)}, u32[]{:S(2)}, u32[]{:S(2)}) collective-permute-start(bf16[192,512]{1,0:T(8,128)(2,1)S(1)} %get-tuple-element.41.refs_4_), channel_id=1, source_target_pairs={{0,1},{1,0},{2,3},{3,2},{4,5},{5,4},{6,7},{7,6},{8,9},{9,8},{10,11... | collective-permute-start | bytes 589832 | tf_op jit(solution)/shard_map/ppermute | solution.py:304
  30.5 2.4 %collective-permute-done.6.refs_1_ = bf16[192,512]{1,0:T(8,128)(2,1)S(1)} collective-permute-done((bf16[192,512]{1,0:T(8,128)(2,1)S(1)}, bf16[192,512]{1,0:T(8,128)(2,1)S(1)}, u32[]{:S(2)}, u32[]{:S(2)}) %collective-permute-start.6) | collective-permute-done | bytes 196640 | tf_op jit(solution)/shard_map/ppermute | solution.py:304
  33.0 0.1 collective-permute-start.7
  33.1 4.0 %collective-permute-done.9.refs_1_ = bf16[192,512]{1,0:T(8,128)(2,1)S(1)} collective-permute-done((bf16[192,512]{1,0:T(8,128)(2,1)S(1)}, bf16[192,512]{1,0:T(8,128)(2,1)S(1)}, u32[]{:S(2)}, u32[]{:S(2)}) %collective-permute-start.9) | collective-permute-done | bytes 196640 | tf_op jit(solution)/shard_map/ppermute | solution.py:304
  37.1 1.8 %shard_map.131 = (bf16[192,512]{1,0:T(8,128)(2,1)S(1)}, f32[192,512]{1,0:T(8,128)S(1)}) custom-call(bf16[192,512]{1,0:T(8,128)(2,1)S(1)} %collective-permute-done.8.refs_0_, bf16[192,512]{1,0:T(8,128)(2,1)S(1)} %collective-permute-done.9.refs_1_, bf16[1024,2048]{1,0:T(8,128)(2,1)S(1)} %get-tuple-element.37.refs_2_.refs_1_, ...), custom_call_target="tpu_custom_call" | custom-call | flops 1610612736 | bytes 9371648 | tf_op jit(solution)/shard_map/pallas_call | solution.py:40
  38.9 0.0 copy-start.2
  39.0 1.2 %collective-permute-start.10 = (bf16[192,512]{1,0:T(8,128)(2,1)S(1)}, bf16[192,512]{1,0:T(8,128)(2,1)S(1)}, u32[]{:S(2)}, u32[]{:S(2)}) collective-permute-start(bf16[192,512]{1,0:T(8,128)(2,1)S(1)} %get-tuple-element.45), channel_id=1, source_target_pairs={{0,1},{1,0},{2,3},{3,2},{4,5},{5,4},{6,7},{7,6},{8,9},{9,8},{10,11... | collective-permute-start | bytes 589832 | tf_op jit(solution)/shard_map/ppermute | solution.py:304
  40.2 0.7 collective-permute-done.4
  40.9 0.5 collective-permute-start.5
  41.4 3.3 %collective-permute-done.10.refs_1_ = bf16[192,512]{1,0:T(8,128)(2,1)S(1)} collective-permute-done((bf16[192,512]{1,0:T(8,128)(2,1)S(1)}, bf16[192,512]{1,0:T(8,128)(2,1)S(1)}, u32[]{:S(2)}, u32[]{:S(2)}) %collective-permute-start.10) | collective-permute-done | bytes 196640 | tf_op jit(solution)/shard_map/ppermute | solution.py:304
  44.7 3.1 %collective-permute-start.11 = (bf16[192,512]{1,0:T(8,128)(2,1)S(1)}, bf16[192,512]{1,0:T(8,128)(2,1)S(1)}, u32[]{:S(2)}, u32[]{:S(2)}) collective-permute-start(bf16[192,512]{1,0:T(8,128)(2,1)S(1)} %shard_map.132), channel_id=1, source_target_pairs={{0,6},{2,4},{4,2},{6,0},{1,7},{3,5},{5,3},{7,1},{8,14},{10,12},{12... | collective-permute-start | bytes 589832 | tf_op jit(solution)/shard_map/ppermute | solution.py:304
  47.8 4.5 %collective-permute-done.11.refs_6_ = bf16[192,512]{1,0:T(8,128)(2,1)S(1)} collective-permute-done((bf16[192,512]{1,0:T(8,128)(2,1)S(1)}, bf16[192,512]{1,0:T(8,128)(2,1)S(1)}, u32[]{:S(2)}, u32[]{:S(2)}) %collective-permute-start.11) | collective-permute-done | bytes 196640 | tf_op jit(solution)/shard_map/ppermute | solution.py:304
  52.3 0.7 shard_map.133.refs_0_.refs_2_
  53.0 1.2 %collective-permute-start.12 = (bf16[256,512]{1,0:T(8,128)(2,1)S(1)}, bf16[256,512]{1,0:T(8,128)(2,1)S(1)}, u32[]{:S(2)}, u32[]{:S(2)}) collective-permute-start(bf16[256,512]{1,0:T(8,128)(2,1)S(1)} %shard_map.133.refs_0_.refs_2_), channel_id=1, source_target_pairs={{0,1},{1,0},{2,3},{3,2},{4,5},{5,4},{6,7},{7,6},{8,9},{9,8},{10,11... | collective-permute-start | bytes 786440 | tf_op jit(solution)/shard_map/ppermute | solution.py:304
  54.3 1.5 %collective-permute-start.14 = (bf16[256,512]{1,0:T(8,128)(2,1)S(1)}, bf16[256,512]{1,0:T(8,128)(2,1)S(1)}, u32[]{:S(2)}, u32[]{:S(2)}) collective-permute-start(bf16[256,512]{1,0:T(8,128)(2,1)S(1)} %shard_map.133.refs_0_.refs_2_), channel_id=1, source_target_pairs={{0,16},{1,17},{8,0},{9,1},{16,24},{17,25},{24,8},{25,9},{2,18},{3,... | collective-permute-start | bytes 786440 | tf_op jit(solution)/shard_map/ppermute | solution.py:439
  55.7 0.7 collective-permute-start.15
  56.4 3.0 %collective-permute-done.12.refs_0_.refs_1_ = bf16[256,512]{1,0:T(8,128)(2,1)S(1)} collective-permute-done((bf16[256,512]{1,0:T(8,128)(2,1)S(1)}, bf16[256,512]{1,0:T(8,128)(2,1)S(1)}, u32[]{:S(2)}, u32[]{:S(2)}) %collective-permute-start.12) | collective-permute-done | bytes 262176 | tf_op jit(solution)/shard_map/ppermute | solution.py:304
  59.5 0.2 collective-permute-done.14.refs_2_
  59.6 2.8 %collective-permute-done.15.refs_3_ = bf16[256,512]{1,0:T(8,128)(2,1)S(1)} collective-permute-done((bf16[256,512]{1,0:T(8,128)(2,1)S(1)}, bf16[256,512]{1,0:T(8,128)(2,1)S(1)}, u32[]{:S(2)}, u32[]{:S(2)}) %collective-permute-start.15) | collective-permute-done | bytes 262176 | tf_op jit(solution)/shard_map/ppermute | solution.py:439
  62.5 0.4 collective-permute-start.16
  62.9 0.7 shard_map.135.refs_2_
  63.6 0.5 collective-permute-done.16.refs_1_
  64.1 2.0 %collective-permute-start.17 = (bf16[256,512]{1,0:T(8,128)(2,1)S(1)}, bf16[256,512]{1,0:T(8,128)(2,1)S(1)}, u32[]{:S(2)}, u32[]{:S(2)}) collective-permute-start(bf16[256,512]{1,0:T(8,128)(2,1)S(1)} %get-tuple-element.51), channel_id=1, source_target_pairs={{0,8},{8,0},{16,24},{24,16},{1,9},{9,1},{17,25},{25,17},{2,10},{10... | collective-permute-start | bytes 786440 | tf_op jit(solution)/shard_map/ppermute | solution.py:304
  66.1 1.1 %collective-permute-done.17.refs_1_ = bf16[256,512]{1,0:T(8,128)(2,1)S(1)} collective-permute-done((bf16[256,512]{1,0:T(8,128)(2,1)S(1)}, bf16[256,512]{1,0:T(8,128)(2,1)S(1)}, u32[]{:S(2)}, u32[]{:S(2)}) %collective-permute-start.17) | collective-permute-done | bytes 262176 | tf_op jit(solution)/shard_map/ppermute | solution.py:304
  67.2 0.1 shard_map.139
  67.4 0.9 %collective-permute-start.18 = (bf16[256,128]{1,0:T(8,128)(2,1)S(1)}, bf16[256,128]{1,0:T(8,128)(2,1)S(1)}, u32[]{:S(2)}, u32[]{:S(2)}) collective-permute-start(bf16[256,128]{1,0:T(8,128)(2,1)S(1)} %get-tuple-element.53), channel_id=1, source_target_pairs={{0,1},{1,0},{8,9},{9,8},{16,17},{17,16},{24,25},{25,24},{2,3},{3,2... | collective-permute-start | bytes 196616 | tf_op jit(solution)/shard_map/ppermute | solution.py:493
  68.3 2.5 %collective-permute-start.19 = (bf16[256,128]{1,0:T(8,128)(2,1)S(1)}, bf16[256,128]{1,0:T(8,128)(2,1)S(1)}, u32[]{:S(2)}, u32[]{:S(2)}) collective-permute-start(bf16[256,128]{1,0:T(8,128)(2,1)S(1)} %get-tuple-element.54), channel_id=1, source_target_pairs={{0,16},{1,17},{8,24},{9,25},{16,0},{17,1},{24,8},{25,9},{2,18},{3,... | collective-permute-start | bytes 196616 | tf_op jit(solution)/shard_map/ppermute | solution.py:493
  70.8 0.1 collective-permute-start.20
  70.9 0.7 shard_map.137
  71.6 0.1 collective-permute-done.18
  71.8 1.4 %collective-permute-done.19 = bf16[256,128]{1,0:T(8,128)(2,1)S(1)} collective-permute-done((bf16[256,128]{1,0:T(8,128)(2,1)S(1)}, bf16[256,128]{1,0:T(8,128)(2,1)S(1)}, u32[]{:S(2)}, u32[]{:S(2)}) %collective-permute-start.19) | collective-permute-done | bytes 65568 | tf_op jit(solution)/shard_map/ppermute | solution.py:493
  73.2 2.8 %collective-permute-done.20 = bf16[256,128]{1,0:T(8,128)(2,1)S(1)} collective-permute-done((bf16[256,128]{1,0:T(8,128)(2,1)S(1)}, bf16[256,128]{1,0:T(8,128)(2,1)S(1)}, u32[]{:S(2)}, u32[]{:S(2)}) %collective-permute-start.20) | collective-permute-done | bytes 65568 | tf_op jit(solution)/shard_map/ppermute | solution.py:493
  76.0 0.7 add_convert_fusion.1
  (32 shorter events, 0.3 us)
Async XLA Ops:
  0.6 1.0 %copy-start.3 = (bf16[1,256,1024]{2,1,0:T(8,128)(2,1)S(1)}, bf16[1,256,1024]{2,1,0:T(8,128)(2,1)}, u32[]{:S(2)}) copy-start(bf16[1,256,1024]{2,1,0:T(8,128)(2,1)} %param.11) | copy-start | bytes 1572868
  0.6 1.0 %copy-start.6 = (s32[1,256,2]{1,2,0:T(2,128)S(1)}, s32[1,256,2]{1,2,0:T(2,128)}, u32[]{:S(2)}) copy-start(s32[1,256,2]{1,2,0:T(2,128)} %param.12) | copy-start | bytes 6148
  0.6 1.0 %copy-start.8 = (f32[1,1024]{1,0:T(1,128)S(1)}, f32[1,1024]{1,0:T(1,128)}, u32[]{:S(2)}) copy-start(f32[1,1024]{1,0:T(1,128)} %refs_2_.2) | copy-start | bytes 12292
  2.6 13.3 %collective-permute-start = (bf16[192,512]{1,0:T(8,128)(2,1)S(1)}, bf16[192,512]{1,0:T(8,128)(2,1)S(1)}, u32[]{:S(2)}, u32[]{:S(2)}) collective-permute-start(bf16[192,512]{1,0:T(8,128)(2,1)S(1)} %get-tuple-element.32), channel_id=1, source_target_pairs={{0,4},{2,6},{4,0},{6,2},{1,5},{3,7},{5,1},{7,3},{8,12},{10,14},{12... | collective-permute-start | bytes 589832 | tf_op jit(solution)/shard_map/ppermute | solution.py:304
  6.7 20.5 %collective-permute-start.2 = (bf16[192,1024]{1,0:T(8,128)(2,1)S(1)}, bf16[192,1024]{1,0:T(8,128)(2,1)S(1)}, u32[]{:S(2)}, u32[]{:S(2)}) collective-permute-start(bf16[192,1024]{1,0:T(8,128)(2,1)S(1)} %get-tuple-element.36), channel_id=1, source_target_pairs={{0,2},{2,0},{4,6},{6,4},{1,3},{3,1},{5,7},{7,5},{8,10},{10,8},{12,... | collective-permute-start | bytes 1179656 | tf_op jit(solution)/shard_map/ppermute | solution.py:304
  8.2 12.7 %copy-start.4 = (bf16[1,256,512]{2,1,0:T(8,128)(2,1)S(1)}, bf16[1,256,512]{2,1,0:T(8,128)(2,1)}, u32[]{:S(2)}) copy-start(bf16[1,256,512]{2,1,0:T(8,128)(2,1)} %param.21) | copy-start | bytes 786436
  8.2 12.7 %copy-start.7 = (f32[1,256,2]{1,2,0:T(2,128)S(1)}, f32[1,256,2]{1,2,0:T(2,128)}, u32[]{:S(2)}) copy-start(f32[1,256,2]{1,2,0:T(2,128)} %param.13) | copy-start | bytes 6148
  12.9 8.7 %collective-permute-start.1 = (bf16[192,512]{1,0:T(8,128)(2,1)S(1)}, bf16[192,512]{1,0:T(8,128)(2,1)S(1)}, u32[]{:S(2)}, u32[]{:S(2)}) collective-permute-start(bf16[192,512]{1,0:T(8,128)(2,1)S(1)} %get-tuple-element.31.refs_0_), channel_id=1, source_target_pairs={{0,1},{1,0},{2,3},{3,2},{4,5},{5,4},{6,7},{7,6},{8,9},{9,8},{10,11... | collective-permute-start | bytes 589832 | tf_op jit(solution)/shard_map/ppermute | solution.py:304
  15.9 7.3 %collective-permute-start.3 = (bf16[192,512]{1,0:T(8,128)(2,1)S(1)}, bf16[192,512]{1,0:T(8,128)(2,1)S(1)}, u32[]{:S(2)}, u32[]{:S(2)}) collective-permute-start(bf16[192,512]{1,0:T(8,128)(2,1)S(1)} %shard_map.125.refs_4_.refs_0_), channel_id=1, source_target_pairs={{0,1},{1,0},{2,3},{3,2},{4,5},{5,4},{6,7},{7,6},{8,9},{9,8},{10,11... | collective-permute-start | bytes 589832 | tf_op jit(solution)/shard_map/ppermute | solution.py:304
  17.5 9.2 %collective-permute-start.8 = (bf16[192,512]{1,0:T(8,128)(2,1)S(1)}, bf16[192,512]{1,0:T(8,128)(2,1)S(1)}, u32[]{:S(2)}, u32[]{:S(2)}) collective-permute-start(bf16[192,512]{1,0:T(8,128)(2,1)S(1)} %get-tuple-element.43), channel_id=1, source_target_pairs={{0,6},{2,4},{4,2},{6,0},{1,7},{3,5},{5,3},{7,1},{8,14},{10,12},{12... | collective-permute-start | bytes 589832 | tf_op jit(solution)/shard_map/ppermute | solution.py:304
  25.0 7.9 %collective-permute-start.6 = (bf16[192,512]{1,0:T(8,128)(2,1)S(1)}, bf16[192,512]{1,0:T(8,128)(2,1)S(1)}, u32[]{:S(2)}, u32[]{:S(2)}) collective-permute-start(bf16[192,512]{1,0:T(8,128)(2,1)S(1)} %get-tuple-element.39.refs_3_), channel_id=1, source_target_pairs={{0,1},{1,0},{2,3},{3,2},{4,5},{5,4},{6,7},{7,6},{8,9},{9,8},{10,11... | collective-permute-start | bytes 589832 | tf_op jit(solution)/shard_map/ppermute | solution.py:304
  26.6 10.5 %collective-permute-start.9 = (bf16[192,512]{1,0:T(8,128)(2,1)S(1)}, bf16[192,512]{1,0:T(8,128)(2,1)S(1)}, u32[]{:S(2)}, u32[]{:S(2)}) collective-permute-start(bf16[192,512]{1,0:T(8,128)(2,1)S(1)} %collective-permute-done.8.refs_0_), channel_id=1, source_target_pairs={{0,1},{1,0},{2,3},{3,2},{4,5},{5,4},{6,7},{7,6},{8,9},{9,8},{10,11... | collective-permute-start | bytes 589832 | tf_op jit(solution)/shard_map/ppermute | solution.py:304
  29.0 11.9 %collective-permute-start.4 = (bf16[192,512]{1,0:T(8,128)(2,1)S(1)}, bf16[192,512]{1,0:T(8,128)(2,1)S(1)}, u32[]{:S(2)}, u32[]{:S(2)}) collective-permute-start(bf16[192,512]{1,0:T(8,128)(2,1)S(1)} %get-tuple-element.41.refs_4_), channel_id=1, source_target_pairs={{0,1},{1,0},{2,3},{3,2},{4,5},{5,4},{6,7},{7,6},{8,9},{9,8},{10,11... | collective-permute-start | bytes 589832 | tf_op jit(solution)/shard_map/ppermute | solution.py:304
  33.0 14.8 %collective-permute-start.7 = (bf16[192,512]{1,0:T(8,128)(2,1)S(1)}, bf16[192,512]{1,0:T(8,128)(2,1)S(1)}, u32[]{:S(2)}, u32[]{:S(2)}) collective-permute-start(bf16[192,512]{1,0:T(8,128)(2,1)S(1)} %shard_map.130.refs_5_), channel_id=1, source_target_pairs={{0,4},{2,6},{4,0},{6,2},{1,5},{3,7},{5,1},{7,3},{8,12},{10,14},{12... | collective-permute-start | bytes 589832 | tf_op jit(solution)/shard_map/ppermute | solution.py:304
  38.9 24.0 %copy-start.2 = (bf16[1,1024,512]{2,1,0:T(8,128)(2,1)S(1)}, bf16[1,1024,512]{2,1,0:T(8,128)(2,1)}, u32[]{:S(2)}) copy-start(bf16[1,1024,512]{2,1,0:T(8,128)(2,1)} %param.18) | copy-start | bytes 3145732
  38.9 24.0 %copy-start.5 = (f32[1,1024]{1,0:T(1,128)S(1)}, f32[1,1024]{1,0:T(1,128)}, u32[]{:S(2)}) copy-start(f32[1,1024]{1,0:T(1,128)} %refs_2_.3) | copy-start | bytes 12292
  38.9 25.2 %copy-start = (bf16[1,1024,512]{2,1,0:T(8,128)(2,1)S(1)}, bf16[1,1024,512]{2,1,0:T(8,128)(2,1)}, u32[]{:S(2)}) copy-start(bf16[1,1024,512]{2,1,0:T(8,128)(2,1)} %param.19) | copy-start | bytes 3145732
  38.9 25.1 %copy-start.1 = (bf16[1,1024,512]{2,1,0:T(8,128)(2,1)S(1)}, bf16[1,1024,512]{2,1,0:T(8,128)(2,1)}, u32[]{:S(2)}) copy-start(bf16[1,1024,512]{2,1,0:T(8,128)(2,1)} %param.20) | copy-start | bytes 3145732
  39.0 5.7 %collective-permute-start.10 = (bf16[192,512]{1,0:T(8,128)(2,1)S(1)}, bf16[192,512]{1,0:T(8,128)(2,1)S(1)}, u32[]{:S(2)}, u32[]{:S(2)}) collective-permute-start(bf16[192,512]{1,0:T(8,128)(2,1)S(1)} %get-tuple-element.45), channel_id=1, source_target_pairs={{0,1},{1,0},{2,3},{3,2},{4,5},{5,4},{6,7},{7,6},{8,9},{9,8},{10,11... | collective-permute-start | bytes 589832 | tf_op jit(solution)/shard_map/ppermute | solution.py:304
  40.9 6.9 %collective-permute-start.5 = (bf16[192,512]{1,0:T(8,128)(2,1)S(1)}, bf16[192,512]{1,0:T(8,128)(2,1)S(1)}, u32[]{:S(2)}, u32[]{:S(2)}) collective-permute-start(bf16[192,512]{1,0:T(8,128)(2,1)S(1)} %add_convert_fusion), channel_id=1, source_target_pairs={{0,2},{2,0},{4,6},{6,4},{1,3},{3,1},{5,7},{7,5},{8,10},{10,8},{12,... | collective-permute-start | bytes 589832 | tf_op jit(solution)/shard_map/ppermute | solution.py:304
  44.7 7.6 %collective-permute-start.11 = (bf16[192,512]{1,0:T(8,128)(2,1)S(1)}, bf16[192,512]{1,0:T(8,128)(2,1)S(1)}, u32[]{:S(2)}, u32[]{:S(2)}) collective-permute-start(bf16[192,512]{1,0:T(8,128)(2,1)S(1)} %shard_map.132), channel_id=1, source_target_pairs={{0,6},{2,4},{4,2},{6,0},{1,7},{3,5},{5,3},{7,1},{8,14},{10,12},{12... | collective-permute-start | bytes 589832 | tf_op jit(solution)/shard_map/ppermute | solution.py:304
  53.0 6.4 %collective-permute-start.12 = (bf16[256,512]{1,0:T(8,128)(2,1)S(1)}, bf16[256,512]{1,0:T(8,128)(2,1)S(1)}, u32[]{:S(2)}, u32[]{:S(2)}) collective-permute-start(bf16[256,512]{1,0:T(8,128)(2,1)S(1)} %shard_map.133.refs_0_.refs_2_), channel_id=1, source_target_pairs={{0,1},{1,0},{2,3},{3,2},{4,5},{5,4},{6,7},{7,6},{8,9},{9,8},{10,11... | collective-permute-start | bytes 786440 | tf_op jit(solution)/shard_map/ppermute | solution.py:304
  54.3 5.2 %collective-permute-start.13 = (bf16[256,512]{1,0:T(8,128)(2,1)S(1)}, bf16[256,512]{1,0:T(8,128)(2,1)S(1)}, u32[]{:S(2)}, u32[]{:S(2)}) collective-permute-start(bf16[256,512]{1,0:T(8,128)(2,1)S(1)} %shard_map.133.refs_0_.refs_2_), channel_id=1, source_target_pairs={{0,8},{8,0},{16,24},{24,16},{1,9},{9,1},{17,25},{25,17},{2,10},{10... | collective-permute-start | bytes 786440 | tf_op jit(solution)/shard_map/ppermute | solution.py:304
  54.3 5.4 %collective-permute-start.14 = (bf16[256,512]{1,0:T(8,128)(2,1)S(1)}, bf16[256,512]{1,0:T(8,128)(2,1)S(1)}, u32[]{:S(2)}, u32[]{:S(2)}) collective-permute-start(bf16[256,512]{1,0:T(8,128)(2,1)S(1)} %shard_map.133.refs_0_.refs_2_), channel_id=1, source_target_pairs={{0,16},{1,17},{8,0},{9,1},{16,24},{17,25},{24,8},{25,9},{2,18},{3,... | collective-permute-start | bytes 786440 | tf_op jit(solution)/shard_map/ppermute | solution.py:439
  55.7 6.7 %collective-permute-start.15 = (bf16[256,512]{1,0:T(8,128)(2,1)S(1)}, bf16[256,512]{1,0:T(8,128)(2,1)S(1)}, u32[]{:S(2)}, u32[]{:S(2)}) collective-permute-start(bf16[256,512]{1,0:T(8,128)(2,1)S(1)} %shard_map.133.refs_0_.refs_2_), channel_id=1, source_target_pairs={{0,25},{1,24},{8,0},{9,1},{16,8},{17,9},{24,16},{25,17},{2,27},{3,... | collective-permute-start | bytes 786440 | tf_op jit(solution)/shard_map/ppermute | solution.py:439
  62.5 1.6 %collective-permute-start.16 = (bf16[256,512]{1,0:T(8,128)(2,1)S(1)}, bf16[256,512]{1,0:T(8,128)(2,1)S(1)}, u32[]{:S(2)}, u32[]{:S(2)}) collective-permute-start(bf16[256,512]{1,0:T(8,128)(2,1)S(1)} %shard_map.134.refs_0_), channel_id=1, source_target_pairs={{0,8},{8,0},{16,24},{24,16},{1,9},{9,1},{17,25},{25,17},{2,10},{10... | collective-permute-start | bytes 786440 | tf_op jit(solution)/shard_map/ppermute | solution.py:304
  64.1 3.1 %collective-permute-start.17 = (bf16[256,512]{1,0:T(8,128)(2,1)S(1)}, bf16[256,512]{1,0:T(8,128)(2,1)S(1)}, u32[]{:S(2)}, u32[]{:S(2)}) collective-permute-start(bf16[256,512]{1,0:T(8,128)(2,1)S(1)} %get-tuple-element.51), channel_id=1, source_target_pairs={{0,8},{8,0},{16,24},{24,16},{1,9},{9,1},{17,25},{25,17},{2,10},{10... | collective-permute-start | bytes 786440 | tf_op jit(solution)/shard_map/ppermute | solution.py:304
  67.4 4.4 %collective-permute-start.18 = (bf16[256,128]{1,0:T(8,128)(2,1)S(1)}, bf16[256,128]{1,0:T(8,128)(2,1)S(1)}, u32[]{:S(2)}, u32[]{:S(2)}) collective-permute-start(bf16[256,128]{1,0:T(8,128)(2,1)S(1)} %get-tuple-element.53), channel_id=1, source_target_pairs={{0,1},{1,0},{8,9},{9,8},{16,17},{17,16},{24,25},{25,24},{2,3},{3,2... | collective-permute-start | bytes 196616 | tf_op jit(solution)/shard_map/ppermute | solution.py:493
  68.3 4.9 %collective-permute-start.19 = (bf16[256,128]{1,0:T(8,128)(2,1)S(1)}, bf16[256,128]{1,0:T(8,128)(2,1)S(1)}, u32[]{:S(2)}, u32[]{:S(2)}) collective-permute-start(bf16[256,128]{1,0:T(8,128)(2,1)S(1)} %get-tuple-element.54), channel_id=1, source_target_pairs={{0,16},{1,17},{8,24},{9,25},{16,0},{17,1},{24,8},{25,9},{2,18},{3,... | collective-permute-start | bytes 196616 | tf_op jit(solution)/shard_map/ppermute | solution.py:493
  70.8 5.2 %collective-permute-start.20 = (bf16[256,128]{1,0:T(8,128)(2,1)S(1)}, bf16[256,128]{1,0:T(8,128)(2,1)S(1)}, u32[]{:S(2)}, u32[]{:S(2)}) collective-permute-start(bf16[256,128]{1,0:T(8,128)(2,1)S(1)} %get-tuple-element.55), channel_id=1, source_target_pairs={{0,17},{1,16},{8,25},{9,24},{16,1},{17,0},{24,9},{25,8},{2,19},{3,... | collective-permute-start | bytes 196616 | tf_op jit(solution)/shard_map/ppermute | solution.py:493

commit v18 on v17

--- a/solution.py
+++ b/solution.py
@@ -195,10 +195,10 @@
     out[...] = value.astype(LOW)
 
 
-def choose(own, beside, *refs):
+def choose(order, *refs):
     sec = lax.axis_index("sec")
-    moved, out = refs[:-1], refs[-1]
-    for i, source in enumerate((own, beside, *moved)):
+    out = refs[-1]
+    for i, source in zip(order, refs[:-1], strict=True):
 
         @pl.when(sec == i)
         def _():
@@ -438,9 +438,16 @@
                 targets[a * tp_size + t] = b * tp_size + (t ^ crossed if a == 0 else t)
         return lax.ppermute(hidden_half, ("sec", "tp"), list(targets.items()))
 
-    moved = [[cycle([0, 2 * i, 2 * i + 1, 1], 0), cycle([0, 2 * i + 1, 2 * i, 1], 1)] for i in range(1, sections // 2)]
     beside = swap(hidden_half, "sec", 1)
-    first = call(choose, [shape_of(hidden_half.shape)], [hidden_other, beside, *sum(moved, [])])[0]
+    choices = {}
+    for i in range(1, sections // 2):
+        choices[2 * i] = cycle([0, 2 * i, 2 * i + 1, 1], 0)
+        choices.setdefault(0, hidden_other)
+        choices[2 * i + 1] = cycle([0, 2 * i + 1, 2 * i, 1], 1)
+    choices |= {0: hidden_other, 1: beside}
+    first = call(
+        functools.partial(choose, list(choices)), [shape_of(hidden_half.shape)], list(choices.values())
+    )[0]
     second = swap(first, "sec", 1)
 
     local_width = query_weight.shape[2]
@@ -484,7 +491,7 @@
         [kept, swap(away, "sec", 1)],
     )
     total = blocks[0]
-    for k in range(1, count):
+    for k in range(count - 1, 0, -1):
         pairs = []
         for i in range(both):
             section, t = i // tp_size, i % tp_size

time: 76.8 us -> 75.4 us (0.982)
  waiting for transfers between devices: 29.9 us -> 28.9 us
    ppermute x3, waiting for transfers between devices: 4.36 us -> 2.9 us  [shards(): total = total + lax.ppermute(blocks[k], ('sec', 'tp'), pairs).astype(WIDE)]
  transfers between devices with their start and end apart: 21 -> 21, of which waited for: 15 -> 14; matrix products, arithmetic and copies ran while one was open for 0% -> 0% of each run, Pallas kernels for 16% -> 16%
where the time goes in v18:
time: 75.4 us; the launch traced here: 75.2 us
  starting transfers between devices  29.8 us (40%)
  waiting for transfers between devices  28.9 us (38%)
  Pallas kernels  13.9 us (18%)
  local copies, waits for them, and re-layouts  1.03 us (1%)
  between operations  0.84 us (1%)
    ppermute x16, starting transfers between devices, swap(): return lax.ppermute(block, axis, [(i, i ^ step) for i in range(size)])  24.5 us
    ppermute x16, waiting for transfers between devices, swap(): return lax.ppermute(block, axis, [(i, i ^ step) for i in range(size)])  23 us
    pallas_call x18, Pallas kernels, call(): pl.pallas_call(run, out_shape=[*out_shape, *(shape_of(x.shape, x.dtype) f...  13.9 us
    ppermute x3, starting transfers between devices, shards(): total = total + lax.ppermute(blocks[k], ('sec', 'tp'), pairs).astype(WIDE)  3.77 us
    ppermute x2, waiting for transfers between devices, cycle(): return lax.ppermute(hidden_half, ('sec', 'tp'), list(targets.items()))  2.98 us
    ppermute x3, waiting for transfers between devices, shards(): total = total + lax.ppermute(blocks[k], ('sec', 'tp'), pairs).astype(WIDE)  2.9 us
  transfers between devices with their start and end apart: 21, of which 14 were waited for; matrix products, arithmetic and copies ran while one was open for 0% of the time, Pallas kernels for 16%

profile of v18, /device:TPU:0, one launch (start us, length us, event | category | flops | bytes accessed | tf_op | source)
XLA Modules:
  0.0 75.2 jit_solution(4850639694781038279)
XLA Ops:
  0.7 1.0 %copy-done.3 = bf16[1,256,1024]{2,1,0:T(8,128)(2,1)S(1)} copy-done((bf16[1,256,1024]{2,1,0:T(8,128)(2,1)S(1)}, bf16[1,256,1024]{2,1,0:T(8,128)(2,1)}, u32[]{:S(2)}) %copy-start.3) | copy-done | bytes 524312
  1.7 0.9 %shard_map.123 = (bf16[192,512]{1,0:T(8,128)(2,1)S(1)}, bf16[192,512]{1,0:T(8,128)(2,1)S(1)}, bf16[192,1024]{1,0:T(8,128)(2,1)S(1)}, bf16[192,1024]{1,0:T(8,128)(2,1)S(1)}) custom-call(bf16[256,1024]{1,0:T(8,128)(2,1)S(1)} %bitcast.19, s32[2,256]{1,0:T(2,128)S(1)} %bitcast.22, f32[1,1024]{1,0:T(1,128)S(1)} %copy-done.8, ...), custom_call_target="tpu_custom_call" | custom-call | flops 402653184 | bytes 1841152 | tf_op jit(solution)/shard_map/pallas_call | solution.py:40
  2.6 4.1 %collective-permute-start = (bf16[192,512]{1,0:T(8,128)(2,1)S(1)}, bf16[192,512]{1,0:T(8,128)(2,1)S(1)}, u32[]{:S(2)}, u32[]{:S(2)}) collective-permute-start(bf16[192,512]{1,0:T(8,128)(2,1)S(1)} %get-tuple-element.32), channel_id=1, source_target_pairs={{0,4},{2,6},{4,0},{6,2},{1,5},{3,7},{5,1},{7,3},{8,12},{10,14},{12... | collective-permute-start | bytes 589832 | tf_op jit(solution)/shard_map/ppermute | solution.py:304
  6.7 1.6 %collective-permute-start.2 = (bf16[192,1024]{1,0:T(8,128)(2,1)S(1)}, bf16[192,1024]{1,0:T(8,128)(2,1)S(1)}, u32[]{:S(2)}, u32[]{:S(2)}) collective-permute-start(bf16[192,1024]{1,0:T(8,128)(2,1)S(1)} %get-tuple-element.36), channel_id=1, source_target_pairs={{0,2},{2,0},{4,6},{6,4},{1,3},{3,1},{5,7},{7,5},{8,10},{10,8},{12,... | collective-permute-start | bytes 1179656 | tf_op jit(solution)/shard_map/ppermute | solution.py:304
  8.2 4.6 %shard_map.124 = (bf16[192,512]{1,0:T(8,128)(2,1)S(1)}, f32[192,512]{1,0:T(8,128)S(1)}, bf16[1024,2048]{1,0:T(8,128)(2,1)S(1)}, bf16[2048,1024]{1,0:T(8,128)(2,1)S(1)}, bf16[192,512]{1,0:T(8,128)(2,1)S(1)}) custom-call(bf16[192,1024]{1,0:T(8,128)(2,1)S(1)} %get-tuple-element.29.refs_0_, ...), custom_call_target="tpu_custom_call", output_to_operand_aliasing={{4}: (3, {})} | custom-call | flops 1610612736 | bytes 17760256 | tf_op jit(solution)/shard_map/pallas_call | solution.py:40
  12.9 1.6 %collective-permute-start.1 = (bf16[192,512]{1,0:T(8,128)(2,1)S(1)}, bf16[192,512]{1,0:T(8,128)(2,1)S(1)}, u32[]{:S(2)}, u32[]{:S(2)}) collective-permute-start(bf16[192,512]{1,0:T(8,128)(2,1)S(1)} %get-tuple-element.31.refs_0_), channel_id=1, source_target_pairs={{0,1},{1,0},{2,3},{3,2},{4,5},{5,4},{6,7},{7,6},{8,9},{9,8},{10,11... | collective-permute-start | bytes 589832 | tf_op jit(solution)/shard_map/ppermute | solution.py:304
  14.4 1.4 %collective-permute-done.refs_1_ = bf16[192,512]{1,0:T(8,128)(2,1)S(1)} collective-permute-done((bf16[192,512]{1,0:T(8,128)(2,1)S(1)}, bf16[192,512]{1,0:T(8,128)(2,1)S(1)}, u32[]{:S(2)}, u32[]{:S(2)}) %collective-permute-start) | collective-permute-done | bytes 196640 | tf_op jit(solution)/shard_map/ppermute | solution.py:304
  15.9 1.6 %collective-permute-start.3 = (bf16[192,512]{1,0:T(8,128)(2,1)S(1)}, bf16[192,512]{1,0:T(8,128)(2,1)S(1)}, u32[]{:S(2)}, u32[]{:S(2)}) collective-permute-start(bf16[192,512]{1,0:T(8,128)(2,1)S(1)} %shard_map.125.refs_4_.refs_0_), channel_id=1, source_target_pairs={{0,1},{1,0},{2,3},{3,2},{4,5},{5,4},{6,7},{7,6},{8,9},{9,8},{10,11... | collective-permute-start | bytes 589832 | tf_op jit(solution)/shard_map/ppermute | solution.py:304
  17.5 3.5 %collective-permute-start.8 = (bf16[192,512]{1,0:T(8,128)(2,1)S(1)}, bf16[192,512]{1,0:T(8,128)(2,1)S(1)}, u32[]{:S(2)}, u32[]{:S(2)}) collective-permute-start(bf16[192,512]{1,0:T(8,128)(2,1)S(1)} %get-tuple-element.43), channel_id=1, source_target_pairs={{0,6},{2,4},{4,2},{6,0},{1,7},{3,5},{5,3},{7,1},{8,14},{10,12},{12... | collective-permute-start | bytes 589832 | tf_op jit(solution)/shard_map/ppermute | solution.py:304
  21.0 0.6 shard_map.126
  21.6 1.6 %collective-permute-done.3.refs_1_ = bf16[192,512]{1,0:T(8,128)(2,1)S(1)} collective-permute-done((bf16[192,512]{1,0:T(8,128)(2,1)S(1)}, bf16[192,512]{1,0:T(8,128)(2,1)S(1)}, u32[]{:S(2)}, u32[]{:S(2)}) %collective-permute-start.3) | collective-permute-done | bytes 196640 | tf_op jit(solution)/shard_map/ppermute | solution.py:304
  23.2 1.8 %shard_map.128 = (bf16[192,512]{1,0:T(8,128)(2,1)S(1)}, f32[192,512]{1,0:T(8,128)S(1)}) custom-call(bf16[192,512]{1,0:T(8,128)(2,1)S(1)} %shard_map.125.refs_4_.refs_0_, bf16[192,512]{1,0:T(8,128)(2,1)S(1)} %collective-permute-done.3.refs_1_, bf16[1024,2048]{1,0:T(8,128)(2,1)S(1)} %get-tuple-element.37.refs_2_.refs_1_, ...), custom_call_target="tpu_custom_call" | custom-call | flops 1610612736 | bytes 9371648 | tf_op jit(solution)/shard_map/pallas_call | solution.py:40
  25.0 1.6 %collective-permute-start.6 = (bf16[192,512]{1,0:T(8,128)(2,1)S(1)}, bf16[192,512]{1,0:T(8,128)(2,1)S(1)}, u32[]{:S(2)}, u32[]{:S(2)}) collective-permute-start(bf16[192,512]{1,0:T(8,128)(2,1)S(1)} %get-tuple-element.39.refs_3_), channel_id=1, source_target_pairs={{0,1},{1,0},{2,3},{3,2},{4,5},{5,4},{6,7},{7,6},{8,9},{9,8},{10,11... | collective-permute-start | bytes 589832 | tf_op jit(solution)/shard_map/ppermute | solution.py:304
  26.6 0.5 collective-permute-start.9
  27.1 1.8 %shard_map.129 = (bf16[192,512]{1,0:T(8,128)(2,1)S(1)}, f32[192,512]{1,0:T(8,128)S(1)}) custom-call(bf16[192,1024]{1,0:T(8,128)(2,1)S(1)} %collective-permute-done.2.refs_0_, bf16[1024,2048]{1,0:T(8,128)(2,1)S(1)} %get-tuple-element.37.refs_2_.refs_1_, bf16[2048,1024]{1,0:T(8,128)(2,1)S(1)} %get-tuple-element.38.refs_3_.refs_2_, ...), custom_call_target="tpu_custom_call" | custom-call | flops 1610612736 | bytes 9371648 | tf_op jit(solution)/shard_map/pallas_call | solution.py:40
  29.0 1.6 %collective-permute-start.4 = (bf16[192,512]{1,0:T(8,128)(2,1)S(1)}, bf16[192,512]{1,0:T(8,128)(2,1)S(1)}, u32[]{:S(2)}, u32[]{:S(2)}) collective-permute-start(bf16[192,512]{1,0:T(8,128)(2,1)S(1)} %get-tuple-element.41.refs_4_), channel_id=1, source_target_pairs={{0,1},{1,0},{2,3},{3,2},{4,5},{5,4},{6,7},{7,6},{8,9},{9,8},{10,11... | collective-permute-start | bytes 589832 | tf_op jit(solution)/shard_map/ppermute | solution.py:304
  30.5 2.4 %collective-permute-done.6.refs_1_ = bf16[192,512]{1,0:T(8,128)(2,1)S(1)} collective-permute-done((bf16[192,512]{1,0:T(8,128)(2,1)S(1)}, bf16[192,512]{1,0:T(8,128)(2,1)S(1)}, u32[]{:S(2)}, u32[]{:S(2)}) %collective-permute-start.6) | collective-permute-done | bytes 196640 | tf_op jit(solution)/shard_map/ppermute | solution.py:304
  33.0 0.1 collective-permute-start.7
  33.1 4.0 %collective-permute-done.9.refs_1_ = bf16[192,512]{1,0:T(8,128)(2,1)S(1)} collective-permute-done((bf16[192,512]{1,0:T(8,128)(2,1)S(1)}, bf16[192,512]{1,0:T(8,128)(2,1)S(1)}, u32[]{:S(2)}, u32[]{:S(2)}) %collective-permute-start.9) | collective-permute-done | bytes 196640 | tf_op jit(solution)/shard_map/ppermute | solution.py:304
  37.1 1.8 %shard_map.131 = (bf16[192,512]{1,0:T(8,128)(2,1)S(1)}, f32[192,512]{1,0:T(8,128)S(1)}) custom-call(bf16[192,512]{1,0:T(8,128)(2,1)S(1)} %collective-permute-done.8.refs_0_, bf16[192,512]{1,0:T(8,128)(2,1)S(1)} %collective-permute-done.9.refs_1_, bf16[1024,2048]{1,0:T(8,128)(2,1)S(1)} %get-tuple-element.37.refs_2_.refs_1_, ...), custom_call_target="tpu_custom_call" | custom-call | flops 1610612736 | bytes 9371648 | tf_op jit(solution)/shard_map/pallas_call | solution.py:40
  38.9 0.0 copy-start.2
  38.9 0.0 copy-start
  38.9 0.0 copy-start.1
  39.0 1.2 %collective-permute-start.10 = (bf16[192,512]{1,0:T(8,128)(2,1)S(1)}, bf16[192,512]{1,0:T(8,128)(2,1)S(1)}, u32[]{:S(2)}, u32[]{:S(2)}) collective-permute-start(bf16[192,512]{1,0:T(8,128)(2,1)S(1)} %get-tuple-element.45), channel_id=1, source_target_pairs={{0,1},{1,0},{2,3},{3,2},{4,5},{5,4},{6,7},{7,6},{8,9},{9,8},{10,11... | collective-permute-start | bytes 589832 | tf_op jit(solution)/shard_map/ppermute | solution.py:304
  40.2 0.7 collective-permute-done.4
  40.9 0.5 collective-permute-start.5
  41.4 3.3 %collective-permute-done.10.refs_1_ = bf16[192,512]{1,0:T(8,128)(2,1)S(1)} collective-permute-done((bf16[192,512]{1,0:T(8,128)(2,1)S(1)}, bf16[192,512]{1,0:T(8,128)(2,1)S(1)}, u32[]{:S(2)}, u32[]{:S(2)}) %collective-permute-start.10) | collective-permute-done | bytes 196640 | tf_op jit(solution)/shard_map/ppermute | solution.py:304
  44.7 3.1 %collective-permute-start.11 = (bf16[192,512]{1,0:T(8,128)(2,1)S(1)}, bf16[192,512]{1,0:T(8,128)(2,1)S(1)}, u32[]{:S(2)}, u32[]{:S(2)}) collective-permute-start(bf16[192,512]{1,0:T(8,128)(2,1)S(1)} %shard_map.132), channel_id=1, source_target_pairs={{0,6},{2,4},{4,2},{6,0},{1,7},{3,5},{5,3},{7,1},{8,14},{10,12},{12... | collective-permute-start | bytes 589832 | tf_op jit(solution)/shard_map/ppermute | solution.py:304
  47.8 4.5 %collective-permute-done.11.refs_6_ = bf16[192,512]{1,0:T(8,128)(2,1)S(1)} collective-permute-done((bf16[192,512]{1,0:T(8,128)(2,1)S(1)}, bf16[192,512]{1,0:T(8,128)(2,1)S(1)}, u32[]{:S(2)}, u32[]{:S(2)}) %collective-permute-start.11) | collective-permute-done | bytes 196640 | tf_op jit(solution)/shard_map/ppermute | solution.py:304
  52.3 0.7 shard_map.133.refs_0_.refs_2_
  53.0 1.2 %collective-permute-start.13 = (bf16[256,512]{1,0:T(8,128)(2,1)S(1)}, bf16[256,512]{1,0:T(8,128)(2,1)S(1)}, u32[]{:S(2)}, u32[]{:S(2)}) collective-permute-start(bf16[256,512]{1,0:T(8,128)(2,1)S(1)} %shard_map.133.refs_0_.refs_2_), channel_id=1, source_target_pairs={{0,1},{1,0},{2,3},{3,2},{4,5},{5,4},{6,7},{7,6},{8,9},{9,8},{10,11... | collective-permute-start | bytes 786440 | tf_op jit(solution)/shard_map/ppermute | solution.py:304
  54.3 1.5 %collective-permute-start.12 = (bf16[256,512]{1,0:T(8,128)(2,1)S(1)}, bf16[256,512]{1,0:T(8,128)(2,1)S(1)}, u32[]{:S(2)}, u32[]{:S(2)}) collective-permute-start(bf16[256,512]{1,0:T(8,128)(2,1)S(1)} %shard_map.133.refs_0_.refs_2_), channel_id=1, source_target_pairs={{0,16},{1,17},{8,0},{9,1},{16,24},{17,25},{24,8},{25,9},{2,18},{3,... | collective-permute-start | bytes 786440 | tf_op jit(solution)/shard_map/ppermute | solution.py:439
  55.7 0.5 collective-permute-start.15
  56.3 3.2 %collective-permute-done.13.refs_1_ = bf16[256,512]{1,0:T(8,128)(2,1)S(1)} collective-permute-done((bf16[256,512]{1,0:T(8,128)(2,1)S(1)}, bf16[256,512]{1,0:T(8,128)(2,1)S(1)}, u32[]{:S(2)}, u32[]{:S(2)}) %collective-permute-start.13) | collective-permute-done | bytes 262176 | tf_op jit(solution)/shard_map/ppermute | solution.py:304
  59.5 0.2 collective-permute-done.12.refs_0_
  59.6 2.8 %collective-permute-done.14.refs_2_ = bf16[256,512]{1,0:T(8,128)(2,1)S(1)} collective-permute-done((bf16[256,512]{1,0:T(8,128)(2,1)S(1)}, bf16[256,512]{1,0:T(8,128)(2,1)S(1)}, u32[]{:S(2)}, u32[]{:S(2)}) %collective-permute-start.14) | collective-permute-done | bytes 262176 | tf_op jit(solution)/shard_map/ppermute | solution.py:439
  62.5 0.1 collective-permute-start.16
  62.6 0.7 shard_map.135.refs_2_
  63.3 0.8 %collective-permute-done.16.refs_1_ = bf16[256,512]{1,0:T(8,128)(2,1)S(1)} collective-permute-done((bf16[256,512]{1,0:T(8,128)(2,1)S(1)}, bf16[256,512]{1,0:T(8,128)(2,1)S(1)}, u32[]{:S(2)}, u32[]{:S(2)}) %collective-permute-start.16) | collective-permute-done | bytes 262176 | tf_op jit(solution)/shard_map/ppermute | solution.py:304
  64.1 1.8 %collective-permute-start.17 = (bf16[256,512]{1,0:T(8,128)(2,1)S(1)}, bf16[256,512]{1,0:T(8,128)(2,1)S(1)}, u32[]{:S(2)}, u32[]{:S(2)}) collective-permute-start(bf16[256,512]{1,0:T(8,128)(2,1)S(1)} %get-tuple-element.51), channel_id=1, source_target_pairs={{0,8},{8,0},{16,24},{24,16},{1,9},{9,1},{17,25},{25,17},{2,10},{10... | collective-permute-start | bytes 786440 | tf_op jit(solution)/shard_map/ppermute | solution.py:304
  65.9 1.1 %collective-permute-done.17.refs_1_ = bf16[256,512]{1,0:T(8,128)(2,1)S(1)} collective-permute-done((bf16[256,512]{1,0:T(8,128)(2,1)S(1)}, bf16[256,512]{1,0:T(8,128)(2,1)S(1)}, u32[]{:S(2)}, u32[]{:S(2)}) %collective-permute-start.17) | collective-permute-done | bytes 262176 | tf_op jit(solution)/shard_map/ppermute | solution.py:304
  67.0 0.1 shard_map.139
  67.1 3.1 %collective-permute-start.18 = (bf16[256,128]{1,0:T(8,128)(2,1)S(1)}, bf16[256,128]{1,0:T(8,128)(2,1)S(1)}, u32[]{:S(2)}, u32[]{:S(2)}) collective-permute-start(bf16[256,128]{1,0:T(8,128)(2,1)S(1)} %get-tuple-element.53), channel_id=1, source_target_pairs={{0,17},{1,16},{8,25},{9,24},{16,1},{17,0},{24,9},{25,8},{2,19},{3,... | collective-permute-start | bytes 196616 | tf_op jit(solution)/shard_map/ppermute | solution.py:500
  70.3 0.6 collective-permute-start.20
  70.9 0.7 shard_map.137
  71.6 1.2 %collective-permute-done.18 = bf16[256,128]{1,0:T(8,128)(2,1)S(1)} collective-permute-done((bf16[256,128]{1,0:T(8,128)(2,1)S(1)}, bf16[256,128]{1,0:T(8,128)(2,1)S(1)}, u32[]{:S(2)}, u32[]{:S(2)}) %collective-permute-start.18) | collective-permute-done | bytes 65568 | tf_op jit(solution)/shard_map/ppermute | solution.py:500
  72.9 1.7 %collective-permute-done.19 = bf16[256,128]{1,0:T(8,128)(2,1)S(1)} collective-permute-done((bf16[256,128]{1,0:T(8,128)(2,1)S(1)}, bf16[256,128]{1,0:T(8,128)(2,1)S(1)}, u32[]{:S(2)}, u32[]{:S(2)}) %collective-permute-start.19) | collective-permute-done | bytes 65568 | tf_op jit(solution)/shard_map/ppermute | solution.py:500
  74.6 0.7 add_convert_fusion.1
  (32 shorter events, 0.3 us)
Async XLA Ops:
  0.6 1.0 %copy-start.3 = (bf16[1,256,1024]{2,1,0:T(8,128)(2,1)S(1)}, bf16[1,256,1024]{2,1,0:T(8,128)(2,1)}, u32[]{:S(2)}) copy-start(bf16[1,256,1024]{2,1,0:T(8,128)(2,1)} %param.11) | copy-start | bytes 1572868
  0.6 1.0 %copy-start.6 = (s32[1,256,2]{1,2,0:T(2,128)S(1)}, s32[1,256,2]{1,2,0:T(2,128)}, u32[]{:S(2)}) copy-start(s32[1,256,2]{1,2,0:T(2,128)} %param.12) | copy-start | bytes 6148
  0.6 1.0 %copy-start.8 = (f32[1,1024]{1,0:T(1,128)S(1)}, f32[1,1024]{1,0:T(1,128)}, u32[]{:S(2)}) copy-start(f32[1,1024]{1,0:T(1,128)} %refs_2_.2) | copy-start | bytes 12292
  2.6 13.3 %collective-permute-start = (bf16[192,512]{1,0:T(8,128)(2,1)S(1)}, bf16[192,512]{1,0:T(8,128)(2,1)S(1)}, u32[]{:S(2)}, u32[]{:S(2)}) collective-permute-start(bf16[192,512]{1,0:T(8,128)(2,1)S(1)} %get-tuple-element.32), channel_id=1, source_target_pairs={{0,4},{2,6},{4,0},{6,2},{1,5},{3,7},{5,1},{7,3},{8,12},{10,14},{12... | collective-permute-start | bytes 589832 | tf_op jit(solution)/shard_map/ppermute | solution.py:304
  6.7 20.5 %collective-permute-start.2 = (bf16[192,1024]{1,0:T(8,128)(2,1)S(1)}, bf16[192,1024]{1,0:T(8,128)(2,1)S(1)}, u32[]{:S(2)}, u32[]{:S(2)}) collective-permute-start(bf16[192,1024]{1,0:T(8,128)(2,1)S(1)} %get-tuple-element.36), channel_id=1, source_target_pairs={{0,2},{2,0},{4,6},{6,4},{1,3},{3,1},{5,7},{7,5},{8,10},{10,8},{12,... | collective-permute-start | bytes 1179656 | tf_op jit(solution)/shard_map/ppermute | solution.py:304
  8.2 12.7 %copy-start.4 = (bf16[1,256,512]{2,1,0:T(8,128)(2,1)S(1)}, bf16[1,256,512]{2,1,0:T(8,128)(2,1)}, u32[]{:S(2)}) copy-start(bf16[1,256,512]{2,1,0:T(8,128)(2,1)} %param.21) | copy-start | bytes 786436
  8.2 12.7 %copy-start.7 = (f32[1,256,2]{1,2,0:T(2,128)S(1)}, f32[1,256,2]{1,2,0:T(2,128)}, u32[]{:S(2)}) copy-start(f32[1,256,2]{1,2,0:T(2,128)} %param.13) | copy-start | bytes 6148
  12.9 8.7 %collective-permute-start.1 = (bf16[192,512]{1,0:T(8,128)(2,1)S(1)}, bf16[192,512]{1,0:T(8,128)(2,1)S(1)}, u32[]{:S(2)}, u32[]{:S(2)}) collective-permute-start(bf16[192,512]{1,0:T(8,128)(2,1)S(1)} %get-tuple-element.31.refs_0_), channel_id=1, source_target_pairs={{0,1},{1,0},{2,3},{3,2},{4,5},{5,4},{6,7},{7,6},{8,9},{9,8},{10,11... | collective-permute-start | bytes 589832 | tf_op jit(solution)/shard_map/ppermute | solution.py:304
  15.9 7.3 %collective-permute-start.3 = (bf16[192,512]{1,0:T(8,128)(2,1)S(1)}, bf16[192,512]{1,0:T(8,128)(2,1)S(1)}, u32[]{:S(2)}, u32[]{:S(2)}) collective-permute-start(bf16[192,512]{1,0:T(8,128)(2,1)S(1)} %shard_map.125.refs_4_.refs_0_), channel_id=1, source_target_pairs={{0,1},{1,0},{2,3},{3,2},{4,5},{5,4},{6,7},{7,6},{8,9},{9,8},{10,11... | collective-permute-start | bytes 589832 | tf_op jit(solution)/shard_map/ppermute | solution.py:304
  17.5 9.2 %collective-permute-start.8 = (bf16[192,512]{1,0:T(8,128)(2,1)S(1)}, bf16[192,512]{1,0:T(8,128)(2,1)S(1)}, u32[]{:S(2)}, u32[]{:S(2)}) collective-permute-start(bf16[192,512]{1,0:T(8,128)(2,1)S(1)} %get-tuple-element.43), channel_id=1, source_target_pairs={{0,6},{2,4},{4,2},{6,0},{1,7},{3,5},{5,3},{7,1},{8,14},{10,12},{12... | collective-permute-start | bytes 589832 | tf_op jit(solution)/shard_map/ppermute | solution.py:304
  25.0 7.9 %collective-permute-start.6 = (bf16[192,512]{1,0:T(8,128)(2,1)S(1)}, bf16[192,512]{1,0:T(8,128)(2,1)S(1)}, u32[]{:S(2)}, u32[]{:S(2)}) collective-permute-start(bf16[192,512]{1,0:T(8,128)(2,1)S(1)} %get-tuple-element.39.refs_3_), channel_id=1, source_target_pairs={{0,1},{1,0},{2,3},{3,2},{4,5},{5,4},{6,7},{7,6},{8,9},{9,8},{10,11... | collective-permute-start | bytes 589832 | tf_op jit(solution)/shard_map/ppermute | solution.py:304
  26.6 10.5 %collective-permute-start.9 = (bf16[192,512]{1,0:T(8,128)(2,1)S(1)}, bf16[192,512]{1,0:T(8,128)(2,1)S(1)}, u32[]{:S(2)}, u32[]{:S(2)}) collective-permute-start(bf16[192,512]{1,0:T(8,128)(2,1)S(1)} %collective-permute-done.8.refs_0_), channel_id=1, source_target_pairs={{0,1},{1,0},{2,3},{3,2},{4,5},{5,4},{6,7},{7,6},{8,9},{9,8},{10,11... | collective-permute-start | bytes 589832 | tf_op jit(solution)/shard_map/ppermute | solution.py:304
  29.0 11.9 %collective-permute-start.4 = (bf16[192,512]{1,0:T(8,128)(2,1)S(1)}, bf16[192,512]{1,0:T(8,128)(2,1)S(1)}, u32[]{:S(2)}, u32[]{:S(2)}) collective-permute-start(bf16[192,512]{1,0:T(8,128)(2,1)S(1)} %get-tuple-element.41.refs_4_), channel_id=1, source_target_pairs={{0,1},{1,0},{2,3},{3,2},{4,5},{5,4},{6,7},{7,6},{8,9},{9,8},{10,11... | collective-permute-start | bytes 589832 | tf_op jit(solution)/shard_map/ppermute | solution.py:304
  33.0 14.8 %collective-permute-start.7 = (bf16[192,512]{1,0:T(8,128)(2,1)S(1)}, bf16[192,512]{1,0:T(8,128)(2,1)S(1)}, u32[]{:S(2)}, u32[]{:S(2)}) collective-permute-start(bf16[192,512]{1,0:T(8,128)(2,1)S(1)} %shard_map.130.refs_5_), channel_id=1, source_target_pairs={{0,4},{2,6},{4,0},{6,2},{1,5},{3,7},{5,1},{7,3},{8,12},{10,14},{12... | collective-permute-start | bytes 589832 | tf_op jit(solution)/shard_map/ppermute | solution.py:304
  38.9 23.7 %copy-start.2 = (bf16[1,1024,512]{2,1,0:T(8,128)(2,1)S(1)}, bf16[1,1024,512]{2,1,0:T(8,128)(2,1)}, u32[]{:S(2)}) copy-start(bf16[1,1024,512]{2,1,0:T(8,128)(2,1)} %param.18) | copy-start | bytes 3145732
  38.9 23.6 %copy-start.5 = (f32[1,1024]{1,0:T(1,128)S(1)}, f32[1,1024]{1,0:T(1,128)}, u32[]{:S(2)}) copy-start(f32[1,1024]{1,0:T(1,128)} %refs_2_.3) | copy-start | bytes 12292
  38.9 25.2 %copy-start = (bf16[1,1024,512]{2,1,0:T(8,128)(2,1)S(1)}, bf16[1,1024,512]{2,1,0:T(8,128)(2,1)}, u32[]{:S(2)}) copy-start(bf16[1,1024,512]{2,1,0:T(8,128)(2,1)} %param.19) | copy-start | bytes 3145732
  38.9 25.1 %copy-start.1 = (bf16[1,1024,512]{2,1,0:T(8,128)(2,1)S(1)}, bf16[1,1024,512]{2,1,0:T(8,128)(2,1)}, u32[]{:S(2)}) copy-start(bf16[1,1024,512]{2,1,0:T(8,128)(2,1)} %param.20) | copy-start | bytes 3145732
  39.0 5.7 %collective-permute-start.10 = (bf16[192,512]{1,0:T(8,128)(2,1)S(1)}, bf16[192,512]{1,0:T(8,128)(2,1)S(1)}, u32[]{:S(2)}, u32[]{:S(2)}) collective-permute-start(bf16[192,512]{1,0:T(8,128)(2,1)S(1)} %get-tuple-element.45), channel_id=1, source_target_pairs={{0,1},{1,0},{2,3},{3,2},{4,5},{5,4},{6,7},{7,6},{8,9},{9,8},{10,11... | collective-permute-start | bytes 589832 | tf_op jit(solution)/shard_map/ppermute | solution.py:304
  40.9 6.9 %collective-permute-start.5 = (bf16[192,512]{1,0:T(8,128)(2,1)S(1)}, bf16[192,512]{1,0:T(8,128)(2,1)S(1)}, u32[]{:S(2)}, u32[]{:S(2)}) collective-permute-start(bf16[192,512]{1,0:T(8,128)(2,1)S(1)} %add_convert_fusion), channel_id=1, source_target_pairs={{0,2},{2,0},{4,6},{6,4},{1,3},{3,1},{5,7},{7,5},{8,10},{10,8},{12,... | collective-permute-start | bytes 589832 | tf_op jit(solution)/shard_map/ppermute | solution.py:304
  44.7 7.6 %collective-permute-start.11 = (bf16[192,512]{1,0:T(8,128)(2,1)S(1)}, bf16[192,512]{1,0:T(8,128)(2,1)S(1)}, u32[]{:S(2)}, u32[]{:S(2)}) collective-permute-start(bf16[192,512]{1,0:T(8,128)(2,1)S(1)} %shard_map.132), channel_id=1, source_target_pairs={{0,6},{2,4},{4,2},{6,0},{1,7},{3,5},{5,3},{7,1},{8,14},{10,12},{12... | collective-permute-start | bytes 589832 | tf_op jit(solution)/shard_map/ppermute | solution.py:304
  53.0 6.4 %collective-permute-start.13 = (bf16[256,512]{1,0:T(8,128)(2,1)S(1)}, bf16[256,512]{1,0:T(8,128)(2,1)S(1)}, u32[]{:S(2)}, u32[]{:S(2)}) collective-permute-start(bf16[256,512]{1,0:T(8,128)(2,1)S(1)} %shard_map.133.refs_0_.refs_2_), channel_id=1, source_target_pairs={{0,1},{1,0},{2,3},{3,2},{4,5},{5,4},{6,7},{7,6},{8,9},{9,8},{10,11... | collective-permute-start | bytes 786440 | tf_op jit(solution)/shard_map/ppermute | solution.py:304
  54.3 5.4 %collective-permute-start.12 = (bf16[256,512]{1,0:T(8,128)(2,1)S(1)}, bf16[256,512]{1,0:T(8,128)(2,1)S(1)}, u32[]{:S(2)}, u32[]{:S(2)}) collective-permute-start(bf16[256,512]{1,0:T(8,128)(2,1)S(1)} %shard_map.133.refs_0_.refs_2_), channel_id=1, source_target_pairs={{0,16},{1,17},{8,0},{9,1},{16,24},{17,25},{24,8},{25,9},{2,18},{3,... | collective-permute-start | bytes 786440 | tf_op jit(solution)/shard_map/ppermute | solution.py:439
  55.7 6.7 %collective-permute-start.14 = (bf16[256,512]{1,0:T(8,128)(2,1)S(1)}, bf16[256,512]{1,0:T(8,128)(2,1)S(1)}, u32[]{:S(2)}, u32[]{:S(2)}) collective-permute-start(bf16[256,512]{1,0:T(8,128)(2,1)S(1)} %shard_map.133.refs_0_.refs_2_), channel_id=1, source_target_pairs={{0,25},{1,24},{8,0},{9,1},{16,8},{17,9},{24,16},{25,17},{2,27},{3,... | collective-permute-start | bytes 786440 | tf_op jit(solution)/shard_map/ppermute | solution.py:439
  55.7 6.7 %collective-permute-start.15 = (bf16[256,512]{1,0:T(8,128)(2,1)S(1)}, bf16[256,512]{1,0:T(8,128)(2,1)S(1)}, u32[]{:S(2)}, u32[]{:S(2)}) collective-permute-start(bf16[256,512]{1,0:T(8,128)(2,1)S(1)} %shard_map.133.refs_0_.refs_2_), channel_id=1, source_target_pairs={{0,8},{8,0},{16,24},{24,16},{1,9},{9,1},{17,25},{25,17},{2,10},{10... | collective-permute-start | bytes 786440 | tf_op jit(solution)/shard_map/ppermute | solution.py:304
  62.5 1.6 %collective-permute-start.16 = (bf16[256,512]{1,0:T(8,128)(2,1)S(1)}, bf16[256,512]{1,0:T(8,128)(2,1)S(1)}, u32[]{:S(2)}, u32[]{:S(2)}) collective-permute-start(bf16[256,512]{1,0:T(8,128)(2,1)S(1)} %shard_map.134.refs_0_), channel_id=1, source_target_pairs={{0,8},{8,0},{16,24},{24,16},{1,9},{9,1},{17,25},{25,17},{2,10},{10... | collective-permute-start | bytes 786440 | tf_op jit(solution)/shard_map/ppermute | solution.py:304
  64.1 2.9 %collective-permute-start.17 = (bf16[256,512]{1,0:T(8,128)(2,1)S(1)}, bf16[256,512]{1,0:T(8,128)(2,1)S(1)}, u32[]{:S(2)}, u32[]{:S(2)}) collective-permute-start(bf16[256,512]{1,0:T(8,128)(2,1)S(1)} %get-tuple-element.51), channel_id=1, source_target_pairs={{0,8},{8,0},{16,24},{24,16},{1,9},{9,1},{17,25},{25,17},{2,10},{10... | collective-permute-start | bytes 786440 | tf_op jit(solution)/shard_map/ppermute | solution.py:304
  67.1 5.7 %collective-permute-start.18 = (bf16[256,128]{1,0:T(8,128)(2,1)S(1)}, bf16[256,128]{1,0:T(8,128)(2,1)S(1)}, u32[]{:S(2)}, u32[]{:S(2)}) collective-permute-start(bf16[256,128]{1,0:T(8,128)(2,1)S(1)} %get-tuple-element.53), channel_id=1, source_target_pairs={{0,17},{1,16},{8,25},{9,24},{16,1},{17,0},{24,9},{25,8},{2,19},{3,... | collective-permute-start | bytes 196616 | tf_op jit(solution)/shard_map/ppermute | solution.py:500
  70.3 4.3 %collective-permute-start.19 = (bf16[256,128]{1,0:T(8,128)(2,1)S(1)}, bf16[256,128]{1,0:T(8,128)(2,1)S(1)}, u32[]{:S(2)}, u32[]{:S(2)}) collective-permute-start(bf16[256,128]{1,0:T(8,128)(2,1)S(1)} %get-tuple-element.54), channel_id=1, source_target_pairs={{0,16},{1,17},{8,24},{9,25},{16,0},{17,1},{24,8},{25,9},{2,18},{3,... | collective-permute-start | bytes 196616 | tf_op jit(solution)/shard_map/ppermute | solution.py:500
  70.3 4.3 %collective-permute-start.20 = (bf16[256,128]{1,0:T(8,128)(2,1)S(1)}, bf16[256,128]{1,0:T(8,128)(2,1)S(1)}, u32[]{:S(2)}, u32[]{:S(2)}) collective-permute-start(bf16[256,128]{1,0:T(8,128)(2,1)S(1)} %get-tuple-element.55), channel_id=1, source_target_pairs={{0,1},{1,0},{8,9},{9,8},{16,17},{17,16},{24,25},{25,24},{2,3},{3,2... | collective-permute-start | bytes 196616 | tf_op jit(solution)/shard_map/ppermute | solution.py:500

commit v19 on v18

--- a/solution.py
+++ b/solution.py
@@ -456,6 +456,7 @@
         [shape_of((token_count, local_width))],
         [hidden_half, hidden_other, attn_gain, query_weight[0]],
         flops=2 * token_count * model_width * local_width,
+        after=list(choices.values())[:1],
     )[0]
     heads = token_count // SEQ * (local_width // HD)
     away, lows, values, dkeys, dvalues = call(

time: 75.4 us -> 74.5 us (0.988)
  waiting for transfers between devices: 28.9 us -> 28.1 us
    ppermute x2, waiting for transfers between devices: 2.98 us -> 1.85 us  [cycle(): return lax.ppermute(hidden_half, ('sec', 'tp'), list(targets.items()))]
  transfers between devices with their start and end apart: 21 -> 21, of which waited for: 14 -> 13; matrix products, arithmetic and copies ran while one was open for 0% -> 0% of each run, Pallas kernels for 16% -> 16%
where the time goes in v19:
time: 74.5 us; the launch traced here: 74.3 us
  starting transfers between devices  29.7 us (40%)
  waiting for transfers between devices  28.1 us (38%)
  Pallas kernels  13.9 us (19%)
  local copies, waits for them, and re-layouts  1.03 us (1%)
  between operations  0.84 us (1%)
    ppermute x16, starting transfers between devices, swap(): return lax.ppermute(block, axis, [(i, i ^ step) for i in range(size)])  24.8 us
    ppermute x16, waiting for transfers between devices, swap(): return lax.ppermute(block, axis, [(i, i ^ step) for i in range(size)])  23.5 us
    pallas_call x18, Pallas kernels, call(): pl.pallas_call(run, out_shape=[*out_shape, *(shape_of(x.shape, x.dtype) f...  13.9 us
    ppermute x3, starting transfers between devices, shards(): total = total + lax.ppermute(blocks[k], ('sec', 'tp'), pairs).astype(WIDE)  3.77 us
    ppermute x3, waiting for transfers between devices, shards(): total = total + lax.ppermute(blocks[k], ('sec', 'tp'), pairs).astype(WIDE)  2.71 us
    ppermute x2, waiting for transfers between devices, cycle(): return lax.ppermute(hidden_half, ('sec', 'tp'), list(targets.items()))  1.85 us
  transfers between devices with their start and end apart: 21, of which 13 were waited for; matrix products, arithmetic and copies ran while one was open for 0% of the time, Pallas kernels for 16%

profile of v19, /device:TPU:0, one launch (start us, length us, event | category | flops | bytes accessed | tf_op | source)
XLA Modules:
  0.0 74.3 jit_solution(15407155293190242604)
XLA Ops:
  0.7 1.0 %copy-done.3 = bf16[1,256,1024]{2,1,0:T(8,128)(2,1)S(1)} copy-done((bf16[1,256,1024]{2,1,0:T(8,128)(2,1)S(1)}, bf16[1,256,1024]{2,1,0:T(8,128)(2,1)}, u32[]{:S(2)}) %copy-start.3) | copy-done | bytes 524312
  1.7 0.9 %shard_map.123 = (bf16[192,512]{1,0:T(8,128)(2,1)S(1)}, bf16[192,512]{1,0:T(8,128)(2,1)S(1)}, bf16[192,1024]{1,0:T(8,128)(2,1)S(1)}, bf16[192,1024]{1,0:T(8,128)(2,1)S(1)}) custom-call(bf16[256,1024]{1,0:T(8,128)(2,1)S(1)} %bitcast.19, s32[2,256]{1,0:T(2,128)S(1)} %bitcast.22, f32[1,1024]{1,0:T(1,128)S(1)} %copy-done.8, ...), custom_call_target="tpu_custom_call" | custom-call | flops 402653184 | bytes 1841152 | tf_op jit(solution)/shard_map/pallas_call | solution.py:40
  2.6 4.1 %collective-permute-start = (bf16[192,512]{1,0:T(8,128)(2,1)S(1)}, bf16[192,512]{1,0:T(8,128)(2,1)S(1)}, u32[]{:S(2)}, u32[]{:S(2)}) collective-permute-start(bf16[192,512]{1,0:T(8,128)(2,1)S(1)} %get-tuple-element.32), channel_id=1, source_target_pairs={{0,4},{2,6},{4,0},{6,2},{1,5},{3,7},{5,1},{7,3},{8,12},{10,14},{12... | collective-permute-start | bytes 589832 | tf_op jit(solution)/shard_map/ppermute | solution.py:304
  6.7 1.6 %collective-permute-start.2 = (bf16[192,1024]{1,0:T(8,128)(2,1)S(1)}, bf16[192,1024]{1,0:T(8,128)(2,1)S(1)}, u32[]{:S(2)}, u32[]{:S(2)}) collective-permute-start(bf16[192,1024]{1,0:T(8,128)(2,1)S(1)} %get-tuple-element.36), channel_id=1, source_target_pairs={{0,2},{2,0},{4,6},{6,4},{1,3},{3,1},{5,7},{7,5},{8,10},{10,8},{12,... | collective-permute-start | bytes 1179656 | tf_op jit(solution)/shard_map/ppermute | solution.py:304
  8.2 4.6 %shard_map.124 = (bf16[192,512]{1,0:T(8,128)(2,1)S(1)}, f32[192,512]{1,0:T(8,128)S(1)}, bf16[1024,2048]{1,0:T(8,128)(2,1)S(1)}, bf16[2048,1024]{1,0:T(8,128)(2,1)S(1)}, bf16[192,512]{1,0:T(8,128)(2,1)S(1)}) custom-call(bf16[192,1024]{1,0:T(8,128)(2,1)S(1)} %get-tuple-element.29.refs_0_, ...), custom_call_target="tpu_custom_call", output_to_operand_aliasing={{4}: (3, {})} | custom-call | flops 1610612736 | bytes 17760256 | tf_op jit(solution)/shard_map/pallas_call | solution.py:40
  12.9 1.6 %collective-permute-start.1 = (bf16[192,512]{1,0:T(8,128)(2,1)S(1)}, bf16[192,512]{1,0:T(8,128)(2,1)S(1)}, u32[]{:S(2)}, u32[]{:S(2)}) collective-permute-start(bf16[192,512]{1,0:T(8,128)(2,1)S(1)} %get-tuple-element.31.refs_0_), channel_id=1, source_target_pairs={{0,1},{1,0},{2,3},{3,2},{4,5},{5,4},{6,7},{7,6},{8,9},{9,8},{10,11... | collective-permute-start | bytes 589832 | tf_op jit(solution)/shard_map/ppermute | solution.py:304
  14.4 1.4 %collective-permute-done.refs_1_ = bf16[192,512]{1,0:T(8,128)(2,1)S(1)} collective-permute-done((bf16[192,512]{1,0:T(8,128)(2,1)S(1)}, bf16[192,512]{1,0:T(8,128)(2,1)S(1)}, u32[]{:S(2)}, u32[]{:S(2)}) %collective-permute-start) | collective-permute-done | bytes 196640 | tf_op jit(solution)/shard_map/ppermute | solution.py:304
  15.9 1.6 %collective-permute-start.3 = (bf16[192,512]{1,0:T(8,128)(2,1)S(1)}, bf16[192,512]{1,0:T(8,128)(2,1)S(1)}, u32[]{:S(2)}, u32[]{:S(2)}) collective-permute-start(bf16[192,512]{1,0:T(8,128)(2,1)S(1)} %shard_map.125.refs_4_.refs_0_), channel_id=1, source_target_pairs={{0,1},{1,0},{2,3},{3,2},{4,5},{5,4},{6,7},{7,6},{8,9},{9,8},{10,11... | collective-permute-start | bytes 589832 | tf_op jit(solution)/shard_map/ppermute | solution.py:304
  17.5 3.5 %collective-permute-start.8 = (bf16[192,512]{1,0:T(8,128)(2,1)S(1)}, bf16[192,512]{1,0:T(8,128)(2,1)S(1)}, u32[]{:S(2)}, u32[]{:S(2)}) collective-permute-start(bf16[192,512]{1,0:T(8,128)(2,1)S(1)} %get-tuple-element.43), channel_id=1, source_target_pairs={{0,6},{2,4},{4,2},{6,0},{1,7},{3,5},{5,3},{7,1},{8,14},{10,12},{12... | collective-permute-start | bytes 589832 | tf_op jit(solution)/shard_map/ppermute | solution.py:304
  21.0 0.6 shard_map.126
  21.6 1.6 %collective-permute-done.3.refs_1_ = bf16[192,512]{1,0:T(8,128)(2,1)S(1)} collective-permute-done((bf16[192,512]{1,0:T(8,128)(2,1)S(1)}, bf16[192,512]{1,0:T(8,128)(2,1)S(1)}, u32[]{:S(2)}, u32[]{:S(2)}) %collective-permute-start.3) | collective-permute-done | bytes 196640 | tf_op jit(solution)/shard_map/ppermute | solution.py:304
  23.2 1.8 %shard_map.128 = (bf16[192,512]{1,0:T(8,128)(2,1)S(1)}, f32[192,512]{1,0:T(8,128)S(1)}) custom-call(bf16[192,512]{1,0:T(8,128)(2,1)S(1)} %shard_map.125.refs_4_.refs_0_, bf16[192,512]{1,0:T(8,128)(2,1)S(1)} %collective-permute-done.3.refs_1_, bf16[1024,2048]{1,0:T(8,128)(2,1)S(1)} %get-tuple-element.37.refs_2_.refs_1_, ...), custom_call_target="tpu_custom_call" | custom-call | flops 1610612736 | bytes 9371648 | tf_op jit(solution)/shard_map/pallas_call | solution.py:40
  25.0 1.6 %collective-permute-start.6 = (bf16[192,512]{1,0:T(8,128)(2,1)S(1)}, bf16[192,512]{1,0:T(8,128)(2,1)S(1)}, u32[]{:S(2)}, u32[]{:S(2)}) collective-permute-start(bf16[192,512]{1,0:T(8,128)(2,1)S(1)} %get-tuple-element.39.refs_3_), channel_id=1, source_target_pairs={{0,1},{1,0},{2,3},{3,2},{4,5},{5,4},{6,7},{7,6},{8,9},{9,8},{10,11... | collective-permute-start | bytes 589832 | tf_op jit(solution)/shard_map/ppermute | solution.py:304
  26.6 0.5 collective-permute-start.9
  27.1 1.8 %shard_map.129 = (bf16[192,512]{1,0:T(8,128)(2,1)S(1)}, f32[192,512]{1,0:T(8,128)S(1)}) custom-call(bf16[192,1024]{1,0:T(8,128)(2,1)S(1)} %collective-permute-done.2.refs_0_, bf16[1024,2048]{1,0:T(8,128)(2,1)S(1)} %get-tuple-element.37.refs_2_.refs_1_, bf16[2048,1024]{1,0:T(8,128)(2,1)S(1)} %get-tuple-element.38.refs_3_.refs_2_, ...), custom_call_target="tpu_custom_call" | custom-call | flops 1610612736 | bytes 9371648 | tf_op jit(solution)/shard_map/pallas_call | solution.py:40
  29.0 1.6 %collective-permute-start.4 = (bf16[192,512]{1,0:T(8,128)(2,1)S(1)}, bf16[192,512]{1,0:T(8,128)(2,1)S(1)}, u32[]{:S(2)}, u32[]{:S(2)}) collective-permute-start(bf16[192,512]{1,0:T(8,128)(2,1)S(1)} %get-tuple-element.41.refs_4_), channel_id=1, source_target_pairs={{0,1},{1,0},{2,3},{3,2},{4,5},{5,4},{6,7},{7,6},{8,9},{9,8},{10,11... | collective-permute-start | bytes 589832 | tf_op jit(solution)/shard_map/ppermute | solution.py:304
  30.5 2.4 %collective-permute-done.6.refs_1_ = bf16[192,512]{1,0:T(8,128)(2,1)S(1)} collective-permute-done((bf16[192,512]{1,0:T(8,128)(2,1)S(1)}, bf16[192,512]{1,0:T(8,128)(2,1)S(1)}, u32[]{:S(2)}, u32[]{:S(2)}) %collective-permute-start.6) | collective-permute-done | bytes 196640 | tf_op jit(solution)/shard_map/ppermute | solution.py:304
  33.0 0.1 collective-permute-start.7
  33.1 4.0 %collective-permute-done.9.refs_1_ = bf16[192,512]{1,0:T(8,128)(2,1)S(1)} collective-permute-done((bf16[192,512]{1,0:T(8,128)(2,1)S(1)}, bf16[192,512]{1,0:T(8,128)(2,1)S(1)}, u32[]{:S(2)}, u32[]{:S(2)}) %collective-permute-start.9) | collective-permute-done | bytes 196640 | tf_op jit(solution)/shard_map/ppermute | solution.py:304
  37.1 1.8 %shard_map.131 = (bf16[192,512]{1,0:T(8,128)(2,1)S(1)}, f32[192,512]{1,0:T(8,128)S(1)}) custom-call(bf16[192,512]{1,0:T(8,128)(2,1)S(1)} %collective-permute-done.8.refs_0_, bf16[192,512]{1,0:T(8,128)(2,1)S(1)} %collective-permute-done.9.refs_1_, bf16[1024,2048]{1,0:T(8,128)(2,1)S(1)} %get-tuple-element.37.refs_2_.refs_1_, ...), custom_call_target="tpu_custom_call" | custom-call | flops 1610612736 | bytes 9371648 | tf_op jit(solution)/shard_map/pallas_call | solution.py:40
  38.9 0.0 copy-start.2
  38.9 0.0 copy-start.5
  38.9 0.0 copy-start
  38.9 0.0 copy-start.1
  39.0 1.2 %collective-permute-start.10 = (bf16[192,512]{1,0:T(8,128)(2,1)S(1)}, bf16[192,512]{1,0:T(8,128)(2,1)S(1)}, u32[]{:S(2)}, u32[]{:S(2)}) collective-permute-start(bf16[192,512]{1,0:T(8,128)(2,1)S(1)} %get-tuple-element.45), channel_id=1, source_target_pairs={{0,1},{1,0},{2,3},{3,2},{4,5},{5,4},{6,7},{7,6},{8,9},{9,8},{10,11... | collective-permute-start | bytes 589832 | tf_op jit(solution)/shard_map/ppermute | solution.py:304
  40.2 0.7 collective-permute-done.4
  40.9 0.5 collective-permute-start.5
  41.4 3.3 %collective-permute-done.10.refs_1_ = bf16[192,512]{1,0:T(8,128)(2,1)S(1)} collective-permute-done((bf16[192,512]{1,0:T(8,128)(2,1)S(1)}, bf16[192,512]{1,0:T(8,128)(2,1)S(1)}, u32[]{:S(2)}, u32[]{:S(2)}) %collective-permute-start.10) | collective-permute-done | bytes 196640 | tf_op jit(solution)/shard_map/ppermute | solution.py:304
  44.7 3.1 %collective-permute-start.11 = (bf16[192,512]{1,0:T(8,128)(2,1)S(1)}, bf16[192,512]{1,0:T(8,128)(2,1)S(1)}, u32[]{:S(2)}, u32[]{:S(2)}) collective-permute-start(bf16[192,512]{1,0:T(8,128)(2,1)S(1)} %shard_map.132), channel_id=1, source_target_pairs={{0,6},{2,4},{4,2},{6,0},{1,7},{3,5},{5,3},{7,1},{8,14},{10,12},{12... | collective-permute-start | bytes 589832 | tf_op jit(solution)/shard_map/ppermute | solution.py:304
  47.8 4.5 %collective-permute-done.11.refs_6_ = bf16[192,512]{1,0:T(8,128)(2,1)S(1)} collective-permute-done((bf16[192,512]{1,0:T(8,128)(2,1)S(1)}, bf16[192,512]{1,0:T(8,128)(2,1)S(1)}, u32[]{:S(2)}, u32[]{:S(2)}) %collective-permute-start.11) | collective-permute-done | bytes 196640 | tf_op jit(solution)/shard_map/ppermute | solution.py:304
  52.3 0.7 shard_map.133.refs_0_.refs_2_
  53.0 1.1 %collective-permute-start.12 = (bf16[256,512]{1,0:T(8,128)(2,1)S(1)}, bf16[256,512]{1,0:T(8,128)(2,1)S(1)}, u32[]{:S(2)}, u32[]{:S(2)}) collective-permute-start(bf16[256,512]{1,0:T(8,128)(2,1)S(1)} %shard_map.133.refs_0_.refs_2_), channel_id=1, source_target_pairs={{0,16},{1,17},{8,0},{9,1},{16,24},{17,25},{24,8},{25,9},{2,18},{3,... | collective-permute-start | bytes 786440 | tf_op jit(solution)/shard_map/ppermute | solution.py:439
  54.2 1.5 %collective-permute-start.13 = (bf16[256,512]{1,0:T(8,128)(2,1)S(1)}, bf16[256,512]{1,0:T(8,128)(2,1)S(1)}, u32[]{:S(2)}, u32[]{:S(2)}) collective-permute-start(bf16[256,512]{1,0:T(8,128)(2,1)S(1)} %shard_map.133.refs_0_.refs_2_), channel_id=1, source_target_pairs={{0,1},{1,0},{2,3},{3,2},{4,5},{5,4},{6,7},{7,6},{8,9},{9,8},{10,11... | collective-permute-start | bytes 786440 | tf_op jit(solution)/shard_map/ppermute | solution.py:304
  55.7 0.5 collective-permute-start.15
  56.2 1.9 %collective-permute-done.12.refs_0_.refs_4_ = bf16[256,512]{1,0:T(8,128)(2,1)S(1)} collective-permute-done((bf16[256,512]{1,0:T(8,128)(2,1)S(1)}, bf16[256,512]{1,0:T(8,128)(2,1)S(1)}, u32[]{:S(2)}, u32[]{:S(2)}) %collective-permute-start.12) | collective-permute-done | bytes 262176 | tf_op jit(solution)/shard_map/ppermute | solution.py:439
  58.1 3.7 %collective-permute-done.13.refs_1_ = bf16[256,512]{1,0:T(8,128)(2,1)S(1)} collective-permute-done((bf16[256,512]{1,0:T(8,128)(2,1)S(1)}, bf16[256,512]{1,0:T(8,128)(2,1)S(1)}, u32[]{:S(2)}, u32[]{:S(2)}) %collective-permute-start.13) | collective-permute-done | bytes 262176 | tf_op jit(solution)/shard_map/ppermute | solution.py:304
  61.8 0.1 collective-permute-start.16
  61.9 0.7 shard_map.135.refs_2_
  62.6 0.8 %collective-permute-done.16.refs_1_ = bf16[256,512]{1,0:T(8,128)(2,1)S(1)} collective-permute-done((bf16[256,512]{1,0:T(8,128)(2,1)S(1)}, bf16[256,512]{1,0:T(8,128)(2,1)S(1)}, u32[]{:S(2)}, u32[]{:S(2)}) %collective-permute-start.16) | collective-permute-done | bytes 262176 | tf_op jit(solution)/shard_map/ppermute | solution.py:304
  63.4 1.8 %collective-permute-start.17 = (bf16[256,512]{1,0:T(8,128)(2,1)S(1)}, bf16[256,512]{1,0:T(8,128)(2,1)S(1)}, u32[]{:S(2)}, u32[]{:S(2)}) collective-permute-start(bf16[256,512]{1,0:T(8,128)(2,1)S(1)} %get-tuple-element.51), channel_id=1, source_target_pairs={{0,8},{8,0},{16,24},{24,16},{1,9},{9,1},{17,25},{25,17},{2,10},{10... | collective-permute-start | bytes 786440 | tf_op jit(solution)/shard_map/ppermute | solution.py:304
  65.2 1.1 %collective-permute-done.17.refs_1_ = bf16[256,512]{1,0:T(8,128)(2,1)S(1)} collective-permute-done((bf16[256,512]{1,0:T(8,128)(2,1)S(1)}, bf16[256,512]{1,0:T(8,128)(2,1)S(1)}, u32[]{:S(2)}, u32[]{:S(2)}) %collective-permute-start.17) | collective-permute-done | bytes 262176 | tf_op jit(solution)/shard_map/ppermute | solution.py:304
  66.4 0.1 shard_map.139
  66.5 2.9 %collective-permute-start.18 = (bf16[256,128]{1,0:T(8,128)(2,1)S(1)}, bf16[256,128]{1,0:T(8,128)(2,1)S(1)}, u32[]{:S(2)}, u32[]{:S(2)}) collective-permute-start(bf16[256,128]{1,0:T(8,128)(2,1)S(1)} %get-tuple-element.53), channel_id=1, source_target_pairs={{0,17},{1,16},{8,25},{9,24},{16,1},{17,0},{24,9},{25,8},{2,19},{3,... | collective-permute-start | bytes 196616 | tf_op jit(solution)/shard_map/ppermute | solution.py:501
  69.4 0.8 %collective-permute-start.20 = (bf16[256,128]{1,0:T(8,128)(2,1)S(1)}, bf16[256,128]{1,0:T(8,128)(2,1)S(1)}, u32[]{:S(2)}, u32[]{:S(2)}) collective-permute-start(bf16[256,128]{1,0:T(8,128)(2,1)S(1)} %get-tuple-element.55), channel_id=1, source_target_pairs={{0,1},{1,0},{8,9},{9,8},{16,17},{17,16},{24,25},{25,24},{2,3},{3,2... | collective-permute-start | bytes 196616 | tf_op jit(solution)/shard_map/ppermute | solution.py:501
  70.2 0.7 shard_map.137
  71.0 0.8 %collective-permute-done.18 = bf16[256,128]{1,0:T(8,128)(2,1)S(1)} collective-permute-done((bf16[256,128]{1,0:T(8,128)(2,1)S(1)}, bf16[256,128]{1,0:T(8,128)(2,1)S(1)}, u32[]{:S(2)}, u32[]{:S(2)}) %collective-permute-start.18) | collective-permute-done | bytes 65568 | tf_op jit(solution)/shard_map/ppermute | solution.py:501
  71.8 1.9 %collective-permute-done.19 = bf16[256,128]{1,0:T(8,128)(2,1)S(1)} collective-permute-done((bf16[256,128]{1,0:T(8,128)(2,1)S(1)}, bf16[256,128]{1,0:T(8,128)(2,1)S(1)}, u32[]{:S(2)}, u32[]{:S(2)}) %collective-permute-start.19) | collective-permute-done | bytes 65568 | tf_op jit(solution)/shard_map/ppermute | solution.py:501
  73.7 0.7 add_convert_fusion.1
  (32 shorter events, 0.3 us)
Async XLA Ops:
  0.6 1.0 %copy-start.3 = (bf16[1,256,1024]{2,1,0:T(8,128)(2,1)S(1)}, bf16[1,256,1024]{2,1,0:T(8,128)(2,1)}, u32[]{:S(2)}) copy-start(bf16[1,256,1024]{2,1,0:T(8,128)(2,1)} %param.11) | copy-start | bytes 1572868
  0.6 1.0 %copy-start.6 = (s32[1,256,2]{1,2,0:T(2,128)S(1)}, s32[1,256,2]{1,2,0:T(2,128)}, u32[]{:S(2)}) copy-start(s32[1,256,2]{1,2,0:T(2,128)} %param.12) | copy-start | bytes 6148
  0.6 1.0 %copy-start.8 = (f32[1,1024]{1,0:T(1,128)S(1)}, f32[1,1024]{1,0:T(1,128)}, u32[]{:S(2)}) copy-start(f32[1,1024]{1,0:T(1,128)} %refs_2_.2) | copy-start | bytes 12292
  2.6 13.3 %collective-permute-start = (bf16[192,512]{1,0:T(8,128)(2,1)S(1)}, bf16[192,512]{1,0:T(8,128)(2,1)S(1)}, u32[]{:S(2)}, u32[]{:S(2)}) collective-permute-start(bf16[192,512]{1,0:T(8,128)(2,1)S(1)} %get-tuple-element.32), channel_id=1, source_target_pairs={{0,4},{2,6},{4,0},{6,2},{1,5},{3,7},{5,1},{7,3},{8,12},{10,14},{12... | collective-permute-start | bytes 589832 | tf_op jit(solution)/shard_map/ppermute | solution.py:304
  6.7 20.5 %collective-permute-start.2 = (bf16[192,1024]{1,0:T(8,128)(2,1)S(1)}, bf16[192,1024]{1,0:T(8,128)(2,1)S(1)}, u32[]{:S(2)}, u32[]{:S(2)}) collective-permute-start(bf16[192,1024]{1,0:T(8,128)(2,1)S(1)} %get-tuple-element.36), channel_id=1, source_target_pairs={{0,2},{2,0},{4,6},{6,4},{1,3},{3,1},{5,7},{7,5},{8,10},{10,8},{12,... | collective-permute-start | bytes 1179656 | tf_op jit(solution)/shard_map/ppermute | solution.py:304
  8.2 12.7 %copy-start.4 = (bf16[1,256,512]{2,1,0:T(8,128)(2,1)S(1)}, bf16[1,256,512]{2,1,0:T(8,128)(2,1)}, u32[]{:S(2)}) copy-start(bf16[1,256,512]{2,1,0:T(8,128)(2,1)} %param.21) | copy-start | bytes 786436
  8.2 12.7 %copy-start.7 = (f32[1,256,2]{1,2,0:T(2,128)S(1)}, f32[1,256,2]{1,2,0:T(2,128)}, u32[]{:S(2)}) copy-start(f32[1,256,2]{1,2,0:T(2,128)} %param.13) | copy-start | bytes 6148
  12.9 8.7 %collective-permute-start.1 = (bf16[192,512]{1,0:T(8,128)(2,1)S(1)}, bf16[192,512]{1,0:T(8,128)(2,1)S(1)}, u32[]{:S(2)}, u32[]{:S(2)}) collective-permute-start(bf16[192,512]{1,0:T(8,128)(2,1)S(1)} %get-tuple-element.31.refs_0_), channel_id=1, source_target_pairs={{0,1},{1,0},{2,3},{3,2},{4,5},{5,4},{6,7},{7,6},{8,9},{9,8},{10,11... | collective-permute-start | bytes 589832 | tf_op jit(solution)/shard_map/ppermute | solution.py:304
  15.9 7.3 %collective-permute-start.3 = (bf16[192,512]{1,0:T(8,128)(2,1)S(1)}, bf16[192,512]{1,0:T(8,128)(2,1)S(1)}, u32[]{:S(2)}, u32[]{:S(2)}) collective-permute-start(bf16[192,512]{1,0:T(8,128)(2,1)S(1)} %shard_map.125.refs_4_.refs_0_), channel_id=1, source_target_pairs={{0,1},{1,0},{2,3},{3,2},{4,5},{5,4},{6,7},{7,6},{8,9},{9,8},{10,11... | collective-permute-start | bytes 589832 | tf_op jit(solution)/shard_map/ppermute | solution.py:304
  17.5 9.2 %collective-permute-start.8 = (bf16[192,512]{1,0:T(8,128)(2,1)S(1)}, bf16[192,512]{1,0:T(8,128)(2,1)S(1)}, u32[]{:S(2)}, u32[]{:S(2)}) collective-permute-start(bf16[192,512]{1,0:T(8,128)(2,1)S(1)} %get-tuple-element.43), channel_id=1, source_target_pairs={{0,6},{2,4},{4,2},{6,0},{1,7},{3,5},{5,3},{7,1},{8,14},{10,12},{12... | collective-permute-start | bytes 589832 | tf_op jit(solution)/shard_map/ppermute | solution.py:304
  25.0 7.9 %collective-permute-start.6 = (bf16[192,512]{1,0:T(8,128)(2,1)S(1)}, bf16[192,512]{1,0:T(8,128)(2,1)S(1)}, u32[]{:S(2)}, u32[]{:S(2)}) collective-permute-start(bf16[192,512]{1,0:T(8,128)(2,1)S(1)} %get-tuple-element.39.refs_3_), channel_id=1, source_target_pairs={{0,1},{1,0},{2,3},{3,2},{4,5},{5,4},{6,7},{7,6},{8,9},{9,8},{10,11... | collective-permute-start | bytes 589832 | tf_op jit(solution)/shard_map/ppermute | solution.py:304
  26.6 10.5 %collective-permute-start.9 = (bf16[192,512]{1,0:T(8,128)(2,1)S(1)}, bf16[192,512]{1,0:T(8,128)(2,1)S(1)}, u32[]{:S(2)}, u32[]{:S(2)}) collective-permute-start(bf16[192,512]{1,0:T(8,128)(2,1)S(1)} %collective-permute-done.8.refs_0_), channel_id=1, source_target_pairs={{0,1},{1,0},{2,3},{3,2},{4,5},{5,4},{6,7},{7,6},{8,9},{9,8},{10,11... | collective-permute-start | bytes 589832 | tf_op jit(solution)/shard_map/ppermute | solution.py:304
  29.0 11.9 %collective-permute-start.4 = (bf16[192,512]{1,0:T(8,128)(2,1)S(1)}, bf16[192,512]{1,0:T(8,128)(2,1)S(1)}, u32[]{:S(2)}, u32[]{:S(2)}) collective-permute-start(bf16[192,512]{1,0:T(8,128)(2,1)S(1)} %get-tuple-element.41.refs_4_), channel_id=1, source_target_pairs={{0,1},{1,0},{2,3},{3,2},{4,5},{5,4},{6,7},{7,6},{8,9},{9,8},{10,11... | collective-permute-start | bytes 589832 | tf_op jit(solution)/shard_map/ppermute | solution.py:304
  33.0 14.8 %collective-permute-start.7 = (bf16[192,512]{1,0:T(8,128)(2,1)S(1)}, bf16[192,512]{1,0:T(8,128)(2,1)S(1)}, u32[]{:S(2)}, u32[]{:S(2)}) collective-permute-start(bf16[192,512]{1,0:T(8,128)(2,1)S(1)} %shard_map.130.refs_5_), channel_id=1, source_target_pairs={{0,4},{2,6},{4,0},{6,2},{1,5},{3,7},{5,1},{7,3},{8,12},{10,14},{12... | collective-permute-start | bytes 589832 | tf_op jit(solution)/shard_map/ppermute | solution.py:304
  38.9 23.0 %copy-start.2 = (bf16[1,1024,512]{2,1,0:T(8,128)(2,1)S(1)}, bf16[1,1024,512]{2,1,0:T(8,128)(2,1)}, u32[]{:S(2)}) copy-start(bf16[1,1024,512]{2,1,0:T(8,128)(2,1)} %param.18) | copy-start | bytes 3145732
  38.9 23.0 %copy-start.5 = (f32[1,1024]{1,0:T(1,128)S(1)}, f32[1,1024]{1,0:T(1,128)}, u32[]{:S(2)}) copy-start(f32[1,1024]{1,0:T(1,128)} %refs_2_.3) | copy-start | bytes 12292
  38.9 24.5 %copy-start = (bf16[1,1024,512]{2,1,0:T(8,128)(2,1)S(1)}, bf16[1,1024,512]{2,1,0:T(8,128)(2,1)}, u32[]{:S(2)}) copy-start(bf16[1,1024,512]{2,1,0:T(8,128)(2,1)} %param.19) | copy-start | bytes 3145732
  38.9 24.5 %copy-start.1 = (bf16[1,1024,512]{2,1,0:T(8,128)(2,1)S(1)}, bf16[1,1024,512]{2,1,0:T(8,128)(2,1)}, u32[]{:S(2)}) copy-start(bf16[1,1024,512]{2,1,0:T(8,128)(2,1)} %param.20) | copy-start | bytes 3145732
  39.0 5.7 %collective-permute-start.10 = (bf16[192,512]{1,0:T(8,128)(2,1)S(1)}, bf16[192,512]{1,0:T(8,128)(2,1)S(1)}, u32[]{:S(2)}, u32[]{:S(2)}) collective-permute-start(bf16[192,512]{1,0:T(8,128)(2,1)S(1)} %get-tuple-element.45), channel_id=1, source_target_pairs={{0,1},{1,0},{2,3},{3,2},{4,5},{5,4},{6,7},{7,6},{8,9},{9,8},{10,11... | collective-permute-start | bytes 589832 | tf_op jit(solution)/shard_map/ppermute | solution.py:304
  40.9 6.9 %collective-permute-start.5 = (bf16[192,512]{1,0:T(8,128)(2,1)S(1)}, bf16[192,512]{1,0:T(8,128)(2,1)S(1)}, u32[]{:S(2)}, u32[]{:S(2)}) collective-permute-start(bf16[192,512]{1,0:T(8,128)(2,1)S(1)} %add_convert_fusion), channel_id=1, source_target_pairs={{0,2},{2,0},{4,6},{6,4},{1,3},{3,1},{5,7},{7,5},{8,10},{10,8},{12,... | collective-permute-start | bytes 589832 | tf_op jit(solution)/shard_map/ppermute | solution.py:304
  44.7 7.6 %collective-permute-start.11 = (bf16[192,512]{1,0:T(8,128)(2,1)S(1)}, bf16[192,512]{1,0:T(8,128)(2,1)S(1)}, u32[]{:S(2)}, u32[]{:S(2)}) collective-permute-start(bf16[192,512]{1,0:T(8,128)(2,1)S(1)} %shard_map.132), channel_id=1, source_target_pairs={{0,6},{2,4},{4,2},{6,0},{1,7},{3,5},{5,3},{7,1},{8,14},{10,12},{12... | collective-permute-start | bytes 589832 | tf_op jit(solution)/shard_map/ppermute | solution.py:304
  53.0 5.0 %collective-permute-start.12 = (bf16[256,512]{1,0:T(8,128)(2,1)S(1)}, bf16[256,512]{1,0:T(8,128)(2,1)S(1)}, u32[]{:S(2)}, u32[]{:S(2)}) collective-permute-start(bf16[256,512]{1,0:T(8,128)(2,1)S(1)} %shard_map.133.refs_0_.refs_2_), channel_id=1, source_target_pairs={{0,16},{1,17},{8,0},{9,1},{16,24},{17,25},{24,8},{25,9},{2,18},{3,... | collective-permute-start | bytes 786440 | tf_op jit(solution)/shard_map/ppermute | solution.py:439
  54.2 7.6 %collective-permute-start.13 = (bf16[256,512]{1,0:T(8,128)(2,1)S(1)}, bf16[256,512]{1,0:T(8,128)(2,1)S(1)}, u32[]{:S(2)}, u32[]{:S(2)}) collective-permute-start(bf16[256,512]{1,0:T(8,128)(2,1)S(1)} %shard_map.133.refs_0_.refs_2_), channel_id=1, source_target_pairs={{0,1},{1,0},{2,3},{3,2},{4,5},{5,4},{6,7},{7,6},{8,9},{9,8},{10,11... | collective-permute-start | bytes 786440 | tf_op jit(solution)/shard_map/ppermute | solution.py:304
  55.7 6.1 %collective-permute-start.14 = (bf16[256,512]{1,0:T(8,128)(2,1)S(1)}, bf16[256,512]{1,0:T(8,128)(2,1)S(1)}, u32[]{:S(2)}, u32[]{:S(2)}) collective-permute-start(bf16[256,512]{1,0:T(8,128)(2,1)S(1)} %shard_map.133.refs_0_.refs_2_), channel_id=1, source_target_pairs={{0,25},{1,24},{8,0},{9,1},{16,8},{17,9},{24,16},{25,17},{2,27},{3,... | collective-permute-start | bytes 786440 | tf_op jit(solution)/shard_map/ppermute | solution.py:439
  55.7 6.1 %collective-permute-start.15 = (bf16[256,512]{1,0:T(8,128)(2,1)S(1)}, bf16[256,512]{1,0:T(8,128)(2,1)S(1)}, u32[]{:S(2)}, u32[]{:S(2)}) collective-permute-start(bf16[256,512]{1,0:T(8,128)(2,1)S(1)} %shard_map.133.refs_0_.refs_2_), channel_id=1, source_target_pairs={{0,8},{8,0},{16,24},{24,16},{1,9},{9,1},{17,25},{25,17},{2,10},{10... | collective-permute-start | bytes 786440 | tf_op jit(solution)/shard_map/ppermute | solution.py:304
  61.8 1.6 %collective-permute-start.16 = (bf16[256,512]{1,0:T(8,128)(2,1)S(1)}, bf16[256,512]{1,0:T(8,128)(2,1)S(1)}, u32[]{:S(2)}, u32[]{:S(2)}) collective-permute-start(bf16[256,512]{1,0:T(8,128)(2,1)S(1)} %shard_map.134.refs_0_), channel_id=1, source_target_pairs={{0,8},{8,0},{16,24},{24,16},{1,9},{9,1},{17,25},{25,17},{2,10},{10... | collective-permute-start | bytes 786440 | tf_op jit(solution)/shard_map/ppermute | solution.py:304
  63.4 2.9 %collective-permute-start.17 = (bf16[256,512]{1,0:T(8,128)(2,1)S(1)}, bf16[256,512]{1,0:T(8,128)(2,1)S(1)}, u32[]{:S(2)}, u32[]{:S(2)}) collective-permute-start(bf16[256,512]{1,0:T(8,128)(2,1)S(1)} %get-tuple-element.51), channel_id=1, source_target_pairs={{0,8},{8,0},{16,24},{24,16},{1,9},{9,1},{17,25},{25,17},{2,10},{10... | collective-permute-start | bytes 786440 | tf_op jit(solution)/shard_map/ppermute | solution.py:304
  66.5 5.3 %collective-permute-start.18 = (bf16[256,128]{1,0:T(8,128)(2,1)S(1)}, bf16[256,128]{1,0:T(8,128)(2,1)S(1)}, u32[]{:S(2)}, u32[]{:S(2)}) collective-permute-start(bf16[256,128]{1,0:T(8,128)(2,1)S(1)} %get-tuple-element.53), channel_id=1, source_target_pairs={{0,17},{1,16},{8,25},{9,24},{16,1},{17,0},{24,9},{25,8},{2,19},{3,... | collective-permute-start | bytes 196616 | tf_op jit(solution)/shard_map/ppermute | solution.py:501
  69.4 4.3 %collective-permute-start.19 = (bf16[256,128]{1,0:T(8,128)(2,1)S(1)}, bf16[256,128]{1,0:T(8,128)(2,1)S(1)}, u32[]{:S(2)}, u32[]{:S(2)}) collective-permute-start(bf16[256,128]{1,0:T(8,128)(2,1)S(1)} %get-tuple-element.54), channel_id=1, source_target_pairs={{0,16},{1,17},{8,24},{9,25},{16,0},{17,1},{24,8},{25,9},{2,18},{3,... | collective-permute-start | bytes 196616 | tf_op jit(solution)/shard_map/ppermute | solution.py:501
  69.4 4.3 %collective-permute-start.20 = (bf16[256,128]{1,0:T(8,128)(2,1)S(1)}, bf16[256,128]{1,0:T(8,128)(2,1)S(1)}, u32[]{:S(2)}, u32[]{:S(2)}) collective-permute-start(bf16[256,128]{1,0:T(8,128)(2,1)S(1)} %get-tuple-element.55), channel_id=1, source_target_pairs={{0,1},{1,0},{8,9},{9,8},{16,17},{17,16},{24,25},{25,24},{2,3},{3,2... | collective-permute-start | bytes 196616 | tf_op jit(solution)/shard_map/ppermute | solution.py:501

commit v20 on v19

--- a/solution.py
+++ b/solution.py
@@ -164,15 +164,17 @@
     out[...] = (kept[...] + arrived[...].astype(WIDE)).astype(LOW)
 
 
-def combine(experts, tokens, high, low, *refs):
+def combine(order, base, high, low, *refs):
     returned, out = refs[:-1], refs[-1]
-    tp = lax.axis_index("tp")
     half = out.shape[1]
-    mixed = tokens[:, part(tp, half)].astype(WIDE)
-    for k in range(experts):
-        rows = returned[k][...]
+    if base.shape[1] == half:
+        mixed = base[...]
+    else:
+        mixed = base[:, part(lax.axis_index("tp"), half)].astype(WIDE)
+    for k, block in zip(order, returned, strict=True):
+        rows = block[...]
         mixed = mixed + (matmul(high[k], rows) + matmul(low[k], rows))
-    out[...] = mixed.astype(LOW)
+    out[...] = mixed.astype(out.dtype)
 
 
 def project(mine, other, gain, weight, out):
@@ -421,11 +423,18 @@
     away, kept = through([arriving[1], others[1]], [near_away, mixed])
     give_back(groups[1], away, kept)
 
+    there, rest = [0, *groups[0], 1], groups[1]
+    so_far = call(
+        functools.partial(combine, there),
+        [shape_of((token_count, half), WIDE)],
+        [token_rows, high, low, *(returned[k] for k in there)],
+        flops=4 * len(there) * token_count * capacity * half,
+    )[0]
     hidden_half = call(
-        functools.partial(combine, experts),
+        functools.partial(combine, rest),
         [shape_of((token_count, half))],
-        [token_rows, high, low, *(returned[k] for k in range(experts))],
-        flops=4 * 3 * token_count * token_count * half,
+        [so_far, high, low, *(returned[k] for k in rest)],
+        flops=4 * len(rest) * token_count * capacity * half,
     )[0]
 
     hidden_other = swap(hidden_half, "tp", 1)
@@ -492,7 +501,7 @@
         [kept, swap(away, "sec", 1)],
     )
     total = blocks[0]
-    for k in range(count - 1, 0, -1):
+    for k in range(1, count):
         pairs = []
         for i in range(both):
             section, t = i // tp_size, i % tp_size

time: 74.5 us -> 74.1 us (level)
    pallas_call x18 -> x19, Pallas kernels: 13.9 us -> 14.1 us  [call(): pl.pallas_call(run, out_shape=[*out_shape, *(shape_of(x.shape, x.dtype) f...]
  transfers between devices with their start and end apart: 21 -> 21, of which waited for: 13 -> 13; matrix products, arithmetic and copies ran while one was open for 0% -> 0% of each run, Pallas kernels for 16% -> 17%
where the time goes in v20:
time: 74.1 us; the launch traced here: 73.9 us
  starting transfers between devices  29.8 us (40%)
  waiting for transfers between devices  27.5 us (37%)
  Pallas kernels  14.1 us (19%)
  local copies, waits for them, and re-layouts  1.03 us (1%)
  between operations  0.85 us (1%)
    ppermute x16, starting transfers between devices, swap(): return lax.ppermute(block, axis, [(i, i ^ step) for i in range(size)])  24.8 us
    ppermute x16, waiting for transfers between devices, swap(): return lax.ppermute(block, axis, [(i, i ^ step) for i in range(size)])  22.9 us
    pallas_call x19, Pallas kernels, call(): pl.pallas_call(run, out_shape=[*out_shape, *(shape_of(x.shape, x.dtype) f...  14.1 us
    ppermute x3, starting transfers between devices, shards(): total = total + lax.ppermute(blocks[k], ('sec', 'tp'), pairs).astype(WIDE)  3.78 us
    ppermute x3, waiting for transfers between devices, shards(): total = total + lax.ppermute(blocks[k], ('sec', 'tp'), pairs).astype(WIDE)  2.7 us
    ppermute x2, waiting for transfers between devices, cycle(): return lax.ppermute(hidden_half, ('sec', 'tp'), list(targets.items()))  1.85 us
  transfers between devices with their start and end apart: 21, of which 13 were waited for; matrix products, arithmetic and copies ran while one was open for 0% of the time, Pallas kernels for 17%

profile of v20, /device:TPU:0, one launch (start us, length us, event | category | flops | bytes accessed | tf_op | source)
XLA Modules:
  0.0 73.9 jit_solution(17828221674956560578)
XLA Ops:
  0.7 1.0 %copy-done.3 = bf16[1,256,1024]{2,1,0:T(8,128)(2,1)S(1)} copy-done((bf16[1,256,1024]{2,1,0:T(8,128)(2,1)S(1)}, bf16[1,256,1024]{2,1,0:T(8,128)(2,1)}, u32[]{:S(2)}) %copy-start.3) | copy-done | bytes 524312
  1.7 0.9 %shard_map.123 = (bf16[192,512]{1,0:T(8,128)(2,1)S(1)}, bf16[192,512]{1,0:T(8,128)(2,1)S(1)}, bf16[192,1024]{1,0:T(8,128)(2,1)S(1)}, bf16[192,1024]{1,0:T(8,128)(2,1)S(1)}) custom-call(bf16[256,1024]{1,0:T(8,128)(2,1)S(1)} %bitcast.19, s32[2,256]{1,0:T(2,128)S(1)} %bitcast.22, f32[1,1024]{1,0:T(1,128)S(1)} %copy-done.8, ...), custom_call_target="tpu_custom_call" | custom-call | flops 402653184 | bytes 1841152 | tf_op jit(solution)/shard_map/pallas_call | solution.py:40
  2.6 4.1 %collective-permute-start = (bf16[192,512]{1,0:T(8,128)(2,1)S(1)}, bf16[192,512]{1,0:T(8,128)(2,1)S(1)}, u32[]{:S(2)}, u32[]{:S(2)}) collective-permute-start(bf16[192,512]{1,0:T(8,128)(2,1)S(1)} %get-tuple-element.32), channel_id=1, source_target_pairs={{0,4},{2,6},{4,0},{6,2},{1,5},{3,7},{5,1},{7,3},{8,12},{10,14},{12... | collective-permute-start | bytes 589832 | tf_op jit(solution)/shard_map/ppermute | solution.py:306
  6.7 1.6 %collective-permute-start.5 = (bf16[192,1024]{1,0:T(8,128)(2,1)S(1)}, bf16[192,1024]{1,0:T(8,128)(2,1)S(1)}, u32[]{:S(2)}, u32[]{:S(2)}) collective-permute-start(bf16[192,1024]{1,0:T(8,128)(2,1)S(1)} %get-tuple-element.40), channel_id=1, source_target_pairs={{0,2},{2,0},{4,6},{6,4},{1,3},{3,1},{5,7},{7,5},{8,10},{10,8},{12,... | collective-permute-start | bytes 1179656 | tf_op jit(solution)/shard_map/ppermute | solution.py:306
  8.2 4.6 %shard_map.124 = (bf16[192,512]{1,0:T(8,128)(2,1)S(1)}, f32[192,512]{1,0:T(8,128)S(1)}, bf16[1024,2048]{1,0:T(8,128)(2,1)S(1)}, bf16[2048,1024]{1,0:T(8,128)(2,1)S(1)}, bf16[192,512]{1,0:T(8,128)(2,1)S(1)}) custom-call(bf16[192,1024]{1,0:T(8,128)(2,1)S(1)} %get-tuple-element.29.refs_0_, ...), custom_call_target="tpu_custom_call", output_to_operand_aliasing={{4}: (3, {})} | custom-call | flops 1610612736 | bytes 17760256 | tf_op jit(solution)/shard_map/pallas_call | solution.py:40
  12.9 1.6 %collective-permute-start.1 = (bf16[192,512]{1,0:T(8,128)(2,1)S(1)}, bf16[192,512]{1,0:T(8,128)(2,1)S(1)}, u32[]{:S(2)}, u32[]{:S(2)}) collective-permute-start(bf16[192,512]{1,0:T(8,128)(2,1)S(1)} %get-tuple-element.31.refs_0_), channel_id=1, source_target_pairs={{0,1},{1,0},{2,3},{3,2},{4,5},{5,4},{6,7},{7,6},{8,9},{9,8},{10,11... | collective-permute-start | bytes 589832 | tf_op jit(solution)/shard_map/ppermute | solution.py:306
  14.4 1.4 %collective-permute-done.refs_1_ = bf16[192,512]{1,0:T(8,128)(2,1)S(1)} collective-permute-done((bf16[192,512]{1,0:T(8,128)(2,1)S(1)}, bf16[192,512]{1,0:T(8,128)(2,1)S(1)}, u32[]{:S(2)}, u32[]{:S(2)}) %collective-permute-start) | collective-permute-done | bytes 196640 | tf_op jit(solution)/shard_map/ppermute | solution.py:306
  15.9 1.6 %collective-permute-start.2 = (bf16[192,512]{1,0:T(8,128)(2,1)S(1)}, bf16[192,512]{1,0:T(8,128)(2,1)S(1)}, u32[]{:S(2)}, u32[]{:S(2)}) collective-permute-start(bf16[192,512]{1,0:T(8,128)(2,1)S(1)} %shard_map.125.refs_4_.refs_0_), channel_id=1, source_target_pairs={{0,1},{1,0},{2,3},{3,2},{4,5},{5,4},{6,7},{7,6},{8,9},{9,8},{10,11... | collective-permute-start | bytes 589832 | tf_op jit(solution)/shard_map/ppermute | solution.py:306
  17.5 3.5 %collective-permute-start.8 = (bf16[192,512]{1,0:T(8,128)(2,1)S(1)}, bf16[192,512]{1,0:T(8,128)(2,1)S(1)}, u32[]{:S(2)}, u32[]{:S(2)}) collective-permute-start(bf16[192,512]{1,0:T(8,128)(2,1)S(1)} %get-tuple-element.43), channel_id=1, source_target_pairs={{0,6},{2,4},{4,2},{6,0},{1,7},{3,5},{5,3},{7,1},{8,14},{10,12},{12... | collective-permute-start | bytes 589832 | tf_op jit(solution)/shard_map/ppermute | solution.py:306
  21.0 0.6 shard_map.126
  21.6 1.6 %collective-permute-done.2.refs_1_ = bf16[192,512]{1,0:T(8,128)(2,1)S(1)} collective-permute-done((bf16[192,512]{1,0:T(8,128)(2,1)S(1)}, bf16[192,512]{1,0:T(8,128)(2,1)S(1)}, u32[]{:S(2)}, u32[]{:S(2)}) %collective-permute-start.2) | collective-permute-done | bytes 196640 | tf_op jit(solution)/shard_map/ppermute | solution.py:306
  23.2 1.8 %shard_map.128 = (bf16[192,512]{1,0:T(8,128)(2,1)S(1)}, f32[192,512]{1,0:T(8,128)S(1)}) custom-call(bf16[192,512]{1,0:T(8,128)(2,1)S(1)} %shard_map.125.refs_4_.refs_0_, bf16[192,512]{1,0:T(8,128)(2,1)S(1)} %collective-permute-done.2.refs_1_, bf16[1024,2048]{1,0:T(8,128)(2,1)S(1)} %get-tuple-element.36.refs_2_.refs_1_, ...), custom_call_target="tpu_custom_call" | custom-call | flops 1610612736 | bytes 9371648 | tf_op jit(solution)/shard_map/pallas_call | solution.py:40
  25.0 1.6 %collective-permute-start.3 = (bf16[192,512]{1,0:T(8,128)(2,1)S(1)}, bf16[192,512]{1,0:T(8,128)(2,1)S(1)}, u32[]{:S(2)}, u32[]{:S(2)}) collective-permute-start(bf16[192,512]{1,0:T(8,128)(2,1)S(1)} %get-tuple-element.39.refs_3_), channel_id=1, source_target_pairs={{0,1},{1,0},{2,3},{3,2},{4,5},{5,4},{6,7},{7,6},{8,9},{9,8},{10,11... | collective-permute-start | bytes 589832 | tf_op jit(solution)/shard_map/ppermute | solution.py:306
  26.6 0.5 collective-permute-start.9
  27.1 1.8 %shard_map.130 = (bf16[192,512]{1,0:T(8,128)(2,1)S(1)}, f32[192,512]{1,0:T(8,128)S(1)}) custom-call(bf16[192,1024]{1,0:T(8,128)(2,1)S(1)} %collective-permute-done.5.refs_0_, bf16[1024,2048]{1,0:T(8,128)(2,1)S(1)} %get-tuple-element.36.refs_2_.refs_1_, bf16[2048,1024]{1,0:T(8,128)(2,1)S(1)} %get-tuple-element.37.refs_3_.refs_2_, ...), custom_call_target="tpu_custom_call" | custom-call | flops 1610612736 | bytes 9371648 | tf_op jit(solution)/shard_map/pallas_call | solution.py:40
  29.0 1.6 %collective-permute-start.6 = (bf16[192,512]{1,0:T(8,128)(2,1)S(1)}, bf16[192,512]{1,0:T(8,128)(2,1)S(1)}, u32[]{:S(2)}, u32[]{:S(2)}) collective-permute-start(bf16[192,512]{1,0:T(8,128)(2,1)S(1)} %get-tuple-element.42.refs_4_), channel_id=1, source_target_pairs={{0,1},{1,0},{2,3},{3,2},{4,5},{5,4},{6,7},{7,6},{8,9},{9,8},{10,11... | collective-permute-start | bytes 589832 | tf_op jit(solution)/shard_map/ppermute | solution.py:306
  30.5 2.4 %collective-permute-done.3.refs_1_ = bf16[192,512]{1,0:T(8,128)(2,1)S(1)} collective-permute-done((bf16[192,512]{1,0:T(8,128)(2,1)S(1)}, bf16[192,512]{1,0:T(8,128)(2,1)S(1)}, u32[]{:S(2)}, u32[]{:S(2)}) %collective-permute-start.3) | collective-permute-done | bytes 196640 | tf_op jit(solution)/shard_map/ppermute | solution.py:306
  33.0 0.1 collective-permute-start.4
  33.1 4.0 %collective-permute-done.9.refs_1_ = bf16[192,512]{1,0:T(8,128)(2,1)S(1)} collective-permute-done((bf16[192,512]{1,0:T(8,128)(2,1)S(1)}, bf16[192,512]{1,0:T(8,128)(2,1)S(1)}, u32[]{:S(2)}, u32[]{:S(2)}) %collective-permute-start.9) | collective-permute-done | bytes 196640 | tf_op jit(solution)/shard_map/ppermute | solution.py:306
  37.1 1.8 %shard_map.132 = (bf16[192,512]{1,0:T(8,128)(2,1)S(1)}, f32[192,512]{1,0:T(8,128)S(1)}) custom-call(bf16[192,512]{1,0:T(8,128)(2,1)S(1)} %collective-permute-done.8.refs_0_, bf16[192,512]{1,0:T(8,128)(2,1)S(1)} %collective-permute-done.9.refs_1_, bf16[1024,2048]{1,0:T(8,128)(2,1)S(1)} %get-tuple-element.36.refs_2_.refs_1_, ...), custom_call_target="tpu_custom_call" | custom-call | flops 1610612736 | bytes 9371648 | tf_op jit(solution)/shard_map/pallas_call | solution.py:40
  38.9 0.0 copy-start.2
  38.9 1.2 %collective-permute-start.10 = (bf16[192,512]{1,0:T(8,128)(2,1)S(1)}, bf16[192,512]{1,0:T(8,128)(2,1)S(1)}, u32[]{:S(2)}, u32[]{:S(2)}) collective-permute-start(bf16[192,512]{1,0:T(8,128)(2,1)S(1)} %get-tuple-element.45), channel_id=1, source_target_pairs={{0,1},{1,0},{2,3},{3,2},{4,5},{5,4},{6,7},{7,6},{8,9},{9,8},{10,11... | collective-permute-start | bytes 589832 | tf_op jit(solution)/shard_map/ppermute | solution.py:306
  40.2 0.7 collective-permute-done.6
  40.9 0.5 collective-permute-start.7
  41.5 3.2 %collective-permute-done.10.refs_1_ = bf16[192,512]{1,0:T(8,128)(2,1)S(1)} collective-permute-done((bf16[192,512]{1,0:T(8,128)(2,1)S(1)}, bf16[192,512]{1,0:T(8,128)(2,1)S(1)}, u32[]{:S(2)}, u32[]{:S(2)}) %collective-permute-start.10) | collective-permute-done | bytes 196640 | tf_op jit(solution)/shard_map/ppermute | solution.py:306
  44.7 0.0 copy-start
  44.7 0.0 copy-start.1
  44.7 3.1 %collective-permute-start.11 = (bf16[192,512]{1,0:T(8,128)(2,1)S(1)}, bf16[192,512]{1,0:T(8,128)(2,1)S(1)}, u32[]{:S(2)}, u32[]{:S(2)}) collective-permute-start(bf16[192,512]{1,0:T(8,128)(2,1)S(1)} %shard_map.133), channel_id=1, source_target_pairs={{0,6},{2,4},{4,2},{6,0},{1,7},{3,5},{5,3},{7,1},{8,14},{10,12},{12... | collective-permute-start | bytes 589832 | tf_op jit(solution)/shard_map/ppermute | solution.py:306
  47.8 0.6 shard_map.131.refs_0_
  48.4 3.9 %collective-permute-done.11.refs_3_ = bf16[192,512]{1,0:T(8,128)(2,1)S(1)} collective-permute-done((bf16[192,512]{1,0:T(8,128)(2,1)S(1)}, bf16[192,512]{1,0:T(8,128)(2,1)S(1)}, u32[]{:S(2)}, u32[]{:S(2)}) %collective-permute-start.11) | collective-permute-done | bytes 196640 | tf_op jit(solution)/shard_map/ppermute | solution.py:306
  52.3 0.3 shard_map.134.refs_0_.refs_2_
  52.6 1.1 %collective-permute-start.12 = (bf16[256,512]{1,0:T(8,128)(2,1)S(1)}, bf16[256,512]{1,0:T(8,128)(2,1)S(1)}, u32[]{:S(2)}, u32[]{:S(2)}) collective-permute-start(bf16[256,512]{1,0:T(8,128)(2,1)S(1)} %shard_map.134.refs_0_.refs_2_), channel_id=1, source_target_pairs={{0,16},{1,17},{8,0},{9,1},{16,24},{17,25},{24,8},{25,9},{2,18},{3,... | collective-permute-start | bytes 786440 | tf_op jit(solution)/shard_map/ppermute | solution.py:448
  53.8 1.5 %collective-permute-start.13 = (bf16[256,512]{1,0:T(8,128)(2,1)S(1)}, bf16[256,512]{1,0:T(8,128)(2,1)S(1)}, u32[]{:S(2)}, u32[]{:S(2)}) collective-permute-start(bf16[256,512]{1,0:T(8,128)(2,1)S(1)} %shard_map.134.refs_0_.refs_2_), channel_id=1, source_target_pairs={{0,1},{1,0},{2,3},{3,2},{4,5},{5,4},{6,7},{7,6},{8,9},{9,8},{10,11... | collective-permute-start | bytes 786440 | tf_op jit(solution)/shard_map/ppermute | solution.py:306
  55.3 0.5 collective-permute-start.15
  55.8 1.9 %collective-permute-done.12.refs_0_.refs_4_ = bf16[256,512]{1,0:T(8,128)(2,1)S(1)} collective-permute-done((bf16[256,512]{1,0:T(8,128)(2,1)S(1)}, bf16[256,512]{1,0:T(8,128)(2,1)S(1)}, u32[]{:S(2)}, u32[]{:S(2)}) %collective-permute-start.12) | collective-permute-done | bytes 262176 | tf_op jit(solution)/shard_map/ppermute | solution.py:448
  57.7 3.7 %collective-permute-done.13.refs_1_ = bf16[256,512]{1,0:T(8,128)(2,1)S(1)} collective-permute-done((bf16[256,512]{1,0:T(8,128)(2,1)S(1)}, bf16[256,512]{1,0:T(8,128)(2,1)S(1)}, u32[]{:S(2)}, u32[]{:S(2)}) %collective-permute-start.13) | collective-permute-done | bytes 262176 | tf_op jit(solution)/shard_map/ppermute | solution.py:306
  61.4 0.1 collective-permute-start.16
  61.5 0.7 shard_map.136.refs_2_
  62.2 0.8 %collective-permute-done.16.refs_1_ = bf16[256,512]{1,0:T(8,128)(2,1)S(1)} collective-permute-done((bf16[256,512]{1,0:T(8,128)(2,1)S(1)}, bf16[256,512]{1,0:T(8,128)(2,1)S(1)}, u32[]{:S(2)}, u32[]{:S(2)}) %collective-permute-start.16) | collective-permute-done | bytes 262176 | tf_op jit(solution)/shard_map/ppermute | solution.py:306
  63.0 1.8 %collective-permute-start.17 = (bf16[256,512]{1,0:T(8,128)(2,1)S(1)}, bf16[256,512]{1,0:T(8,128)(2,1)S(1)}, u32[]{:S(2)}, u32[]{:S(2)}) collective-permute-start(bf16[256,512]{1,0:T(8,128)(2,1)S(1)} %get-tuple-element.51), channel_id=1, source_target_pairs={{0,8},{8,0},{16,24},{24,16},{1,9},{9,1},{17,25},{25,17},{2,10},{10... | collective-permute-start | bytes 786440 | tf_op jit(solution)/shard_map/ppermute | solution.py:306
  64.8 1.1 %collective-permute-done.17.refs_1_ = bf16[256,512]{1,0:T(8,128)(2,1)S(1)} collective-permute-done((bf16[256,512]{1,0:T(8,128)(2,1)S(1)}, bf16[256,512]{1,0:T(8,128)(2,1)S(1)}, u32[]{:S(2)}, u32[]{:S(2)}) %collective-permute-start.17) | collective-permute-done | bytes 262176 | tf_op jit(solution)/shard_map/ppermute | solution.py:306
  66.0 0.1 shard_map.140
  66.1 2.9 %collective-permute-start.20 = (bf16[256,128]{1,0:T(8,128)(2,1)S(1)}, bf16[256,128]{1,0:T(8,128)(2,1)S(1)}, u32[]{:S(2)}, u32[]{:S(2)}) collective-permute-start(bf16[256,128]{1,0:T(8,128)(2,1)S(1)} %get-tuple-element.55), channel_id=1, source_target_pairs={{0,17},{1,16},{8,25},{9,24},{16,1},{17,0},{24,9},{25,8},{2,19},{3,... | collective-permute-start | bytes 196616 | tf_op jit(solution)/shard_map/ppermute | solution.py:510
  69.0 0.8 %collective-permute-start.18 = (bf16[256,128]{1,0:T(8,128)(2,1)S(1)}, bf16[256,128]{1,0:T(8,128)(2,1)S(1)}, u32[]{:S(2)}, u32[]{:S(2)}) collective-permute-start(bf16[256,128]{1,0:T(8,128)(2,1)S(1)} %get-tuple-element.53), channel_id=1, source_target_pairs={{0,1},{1,0},{8,9},{9,8},{16,17},{17,16},{24,25},{25,24},{2,3},{3,2... | collective-permute-start | bytes 196616 | tf_op jit(solution)/shard_map/ppermute | solution.py:510
  69.8 0.7 shard_map.138
  70.6 0.8 %collective-permute-done.20 = bf16[256,128]{1,0:T(8,128)(2,1)S(1)} collective-permute-done((bf16[256,128]{1,0:T(8,128)(2,1)S(1)}, bf16[256,128]{1,0:T(8,128)(2,1)S(1)}, u32[]{:S(2)}, u32[]{:S(2)}) %collective-permute-start.20) | collective-permute-done | bytes 65568 | tf_op jit(solution)/shard_map/ppermute | solution.py:510
  71.4 1.9 %collective-permute-done.19 = bf16[256,128]{1,0:T(8,128)(2,1)S(1)} collective-permute-done((bf16[256,128]{1,0:T(8,128)(2,1)S(1)}, bf16[256,128]{1,0:T(8,128)(2,1)S(1)}, u32[]{:S(2)}, u32[]{:S(2)}) %collective-permute-start.19) | collective-permute-done | bytes 65568 | tf_op jit(solution)/shard_map/ppermute | solution.py:510
  73.3 0.7 add_convert_fusion.1
  (33 shorter events, 0.3 us)
Async XLA Ops:
  0.6 1.0 %copy-start.3 = (bf16[1,256,1024]{2,1,0:T(8,128)(2,1)S(1)}, bf16[1,256,1024]{2,1,0:T(8,128)(2,1)}, u32[]{:S(2)}) copy-start(bf16[1,256,1024]{2,1,0:T(8,128)(2,1)} %param.11) | copy-start | bytes 1572868
  0.6 1.0 %copy-start.6 = (s32[1,256,2]{1,2,0:T(2,128)S(1)}, s32[1,256,2]{1,2,0:T(2,128)}, u32[]{:S(2)}) copy-start(s32[1,256,2]{1,2,0:T(2,128)} %param.12) | copy-start | bytes 6148
  0.6 1.0 %copy-start.8 = (f32[1,1024]{1,0:T(1,128)S(1)}, f32[1,1024]{1,0:T(1,128)}, u32[]{:S(2)}) copy-start(f32[1,1024]{1,0:T(1,128)} %refs_2_.2) | copy-start | bytes 12292
  2.6 13.3 %collective-permute-start = (bf16[192,512]{1,0:T(8,128)(2,1)S(1)}, bf16[192,512]{1,0:T(8,128)(2,1)S(1)}, u32[]{:S(2)}, u32[]{:S(2)}) collective-permute-start(bf16[192,512]{1,0:T(8,128)(2,1)S(1)} %get-tuple-element.32), channel_id=1, source_target_pairs={{0,4},{2,6},{4,0},{6,2},{1,5},{3,7},{5,1},{7,3},{8,12},{10,14},{12... | collective-permute-start | bytes 589832 | tf_op jit(solution)/shard_map/ppermute | solution.py:306
  6.7 20.5 %collective-permute-start.5 = (bf16[192,1024]{1,0:T(8,128)(2,1)S(1)}, bf16[192,1024]{1,0:T(8,128)(2,1)S(1)}, u32[]{:S(2)}, u32[]{:S(2)}) collective-permute-start(bf16[192,1024]{1,0:T(8,128)(2,1)S(1)} %get-tuple-element.40), channel_id=1, source_target_pairs={{0,2},{2,0},{4,6},{6,4},{1,3},{3,1},{5,7},{7,5},{8,10},{10,8},{12,... | collective-permute-start | bytes 1179656 | tf_op jit(solution)/shard_map/ppermute | solution.py:306
  8.2 12.7 %copy-start.4 = (bf16[1,256,512]{2,1,0:T(8,128)(2,1)S(1)}, bf16[1,256,512]{2,1,0:T(8,128)(2,1)}, u32[]{:S(2)}) copy-start(bf16[1,256,512]{2,1,0:T(8,128)(2,1)} %param.21) | copy-start | bytes 786436
  8.2 12.7 %copy-start.7 = (f32[1,256,2]{1,2,0:T(2,128)S(1)}, f32[1,256,2]{1,2,0:T(2,128)}, u32[]{:S(2)}) copy-start(f32[1,256,2]{1,2,0:T(2,128)} %param.13) | copy-start | bytes 6148
  12.9 8.7 %collective-permute-start.1 = (bf16[192,512]{1,0:T(8,128)(2,1)S(1)}, bf16[192,512]{1,0:T(8,128)(2,1)S(1)}, u32[]{:S(2)}, u32[]{:S(2)}) collective-permute-start(bf16[192,512]{1,0:T(8,128)(2,1)S(1)} %get-tuple-element.31.refs_0_), channel_id=1, source_target_pairs={{0,1},{1,0},{2,3},{3,2},{4,5},{5,4},{6,7},{7,6},{8,9},{9,8},{10,11... | collective-permute-start | bytes 589832 | tf_op jit(solution)/shard_map/ppermute | solution.py:306
  15.9 7.3 %collective-permute-start.2 = (bf16[192,512]{1,0:T(8,128)(2,1)S(1)}, bf16[192,512]{1,0:T(8,128)(2,1)S(1)}, u32[]{:S(2)}, u32[]{:S(2)}) collective-permute-start(bf16[192,512]{1,0:T(8,128)(2,1)S(1)} %shard_map.125.refs_4_.refs_0_), channel_id=1, source_target_pairs={{0,1},{1,0},{2,3},{3,2},{4,5},{5,4},{6,7},{7,6},{8,9},{9,8},{10,11... | collective-permute-start | bytes 589832 | tf_op jit(solution)/shard_map/ppermute | solution.py:306
  17.5 9.2 %collective-permute-start.8 = (bf16[192,512]{1,0:T(8,128)(2,1)S(1)}, bf16[192,512]{1,0:T(8,128)(2,1)S(1)}, u32[]{:S(2)}, u32[]{:S(2)}) collective-permute-start(bf16[192,512]{1,0:T(8,128)(2,1)S(1)} %get-tuple-element.43), channel_id=1, source_target_pairs={{0,6},{2,4},{4,2},{6,0},{1,7},{3,5},{5,3},{7,1},{8,14},{10,12},{12... | collective-permute-start | bytes 589832 | tf_op jit(solution)/shard_map/ppermute | solution.py:306
  25.0 7.9 %collective-permute-start.3 = (bf16[192,512]{1,0:T(8,128)(2,1)S(1)}, bf16[192,512]{1,0:T(8,128)(2,1)S(1)}, u32[]{:S(2)}, u32[]{:S(2)}) collective-permute-start(bf16[192,512]{1,0:T(8,128)(2,1)S(1)} %get-tuple-element.39.refs_3_), channel_id=1, source_target_pairs={{0,1},{1,0},{2,3},{3,2},{4,5},{5,4},{6,7},{7,6},{8,9},{9,8},{10,11... | collective-permute-start | bytes 589832 | tf_op jit(solution)/shard_map/ppermute | solution.py:306
  26.6 10.5 %collective-permute-start.9 = (bf16[192,512]{1,0:T(8,128)(2,1)S(1)}, bf16[192,512]{1,0:T(8,128)(2,1)S(1)}, u32[]{:S(2)}, u32[]{:S(2)}) collective-permute-start(bf16[192,512]{1,0:T(8,128)(2,1)S(1)} %collective-permute-done.8.refs_0_), channel_id=1, source_target_pairs={{0,1},{1,0},{2,3},{3,2},{4,5},{5,4},{6,7},{7,6},{8,9},{9,8},{10,11... | collective-permute-start | bytes 589832 | tf_op jit(solution)/shard_map/ppermute | solution.py:306
  29.0 11.9 %collective-permute-start.6 = (bf16[192,512]{1,0:T(8,128)(2,1)S(1)}, bf16[192,512]{1,0:T(8,128)(2,1)S(1)}, u32[]{:S(2)}, u32[]{:S(2)}) collective-permute-start(bf16[192,512]{1,0:T(8,128)(2,1)S(1)} %get-tuple-element.42.refs_4_), channel_id=1, source_target_pairs={{0,1},{1,0},{2,3},{3,2},{4,5},{5,4},{6,7},{7,6},{8,9},{9,8},{10,11... | collective-permute-start | bytes 589832 | tf_op jit(solution)/shard_map/ppermute | solution.py:306
  33.0 14.8 %collective-permute-start.4 = (bf16[192,512]{1,0:T(8,128)(2,1)S(1)}, bf16[192,512]{1,0:T(8,128)(2,1)S(1)}, u32[]{:S(2)}, u32[]{:S(2)}) collective-permute-start(bf16[192,512]{1,0:T(8,128)(2,1)S(1)} %shard_map.129.refs_5_), channel_id=1, source_target_pairs={{0,4},{2,6},{4,0},{6,2},{1,5},{3,7},{5,1},{7,3},{8,12},{10,14},{12... | collective-permute-start | bytes 589832 | tf_op jit(solution)/shard_map/ppermute | solution.py:306
  38.9 22.6 %copy-start.2 = (bf16[1,1024,512]{2,1,0:T(8,128)(2,1)S(1)}, bf16[1,1024,512]{2,1,0:T(8,128)(2,1)}, u32[]{:S(2)}) copy-start(bf16[1,1024,512]{2,1,0:T(8,128)(2,1)} %param.18) | copy-start | bytes 3145732
  38.9 22.6 %copy-start.5 = (f32[1,1024]{1,0:T(1,128)S(1)}, f32[1,1024]{1,0:T(1,128)}, u32[]{:S(2)}) copy-start(f32[1,1024]{1,0:T(1,128)} %refs_2_.3) | copy-start | bytes 12292
  38.9 5.7 %collective-permute-start.10 = (bf16[192,512]{1,0:T(8,128)(2,1)S(1)}, bf16[192,512]{1,0:T(8,128)(2,1)S(1)}, u32[]{:S(2)}, u32[]{:S(2)}) collective-permute-start(bf16[192,512]{1,0:T(8,128)(2,1)S(1)} %get-tuple-element.45), channel_id=1, source_target_pairs={{0,1},{1,0},{2,3},{3,2},{4,5},{5,4},{6,7},{7,6},{8,9},{9,8},{10,11... | collective-permute-start | bytes 589832 | tf_op jit(solution)/shard_map/ppermute | solution.py:306
  40.9 6.9 %collective-permute-start.7 = (bf16[192,512]{1,0:T(8,128)(2,1)S(1)}, bf16[192,512]{1,0:T(8,128)(2,1)S(1)}, u32[]{:S(2)}, u32[]{:S(2)}) collective-permute-start(bf16[192,512]{1,0:T(8,128)(2,1)S(1)} %add_convert_fusion), channel_id=1, source_target_pairs={{0,2},{2,0},{4,6},{6,4},{1,3},{3,1},{5,7},{7,5},{8,10},{10,8},{12,... | collective-permute-start | bytes 589832 | tf_op jit(solution)/shard_map/ppermute | solution.py:306
  44.7 18.3 %copy-start = (bf16[1,1024,512]{2,1,0:T(8,128)(2,1)S(1)}, bf16[1,1024,512]{2,1,0:T(8,128)(2,1)}, u32[]{:S(2)}) copy-start(bf16[1,1024,512]{2,1,0:T(8,128)(2,1)} %param.19) | copy-start | bytes 3145732
  44.7 18.3 %copy-start.1 = (bf16[1,1024,512]{2,1,0:T(8,128)(2,1)S(1)}, bf16[1,1024,512]{2,1,0:T(8,128)(2,1)}, u32[]{:S(2)}) copy-start(bf16[1,1024,512]{2,1,0:T(8,128)(2,1)} %param.20) | copy-start | bytes 3145732
  44.7 7.6 %collective-permute-start.11 = (bf16[192,512]{1,0:T(8,128)(2,1)S(1)}, bf16[192,512]{1,0:T(8,128)(2,1)S(1)}, u32[]{:S(2)}, u32[]{:S(2)}) collective-permute-start(bf16[192,512]{1,0:T(8,128)(2,1)S(1)} %shard_map.133), channel_id=1, source_target_pairs={{0,6},{2,4},{4,2},{6,0},{1,7},{3,5},{5,3},{7,1},{8,14},{10,12},{12... | collective-permute-start | bytes 589832 | tf_op jit(solution)/shard_map/ppermute | solution.py:306
  52.6 5.0 %collective-permute-start.12 = (bf16[256,512]{1,0:T(8,128)(2,1)S(1)}, bf16[256,512]{1,0:T(8,128)(2,1)S(1)}, u32[]{:S(2)}, u32[]{:S(2)}) collective-permute-start(bf16[256,512]{1,0:T(8,128)(2,1)S(1)} %shard_map.134.refs_0_.refs_2_), channel_id=1, source_target_pairs={{0,16},{1,17},{8,0},{9,1},{16,24},{17,25},{24,8},{25,9},{2,18},{3,... | collective-permute-start | bytes 786440 | tf_op jit(solution)/shard_map/ppermute | solution.py:448
  53.8 7.6 %collective-permute-start.13 = (bf16[256,512]{1,0:T(8,128)(2,1)S(1)}, bf16[256,512]{1,0:T(8,128)(2,1)S(1)}, u32[]{:S(2)}, u32[]{:S(2)}) collective-permute-start(bf16[256,512]{1,0:T(8,128)(2,1)S(1)} %shard_map.134.refs_0_.refs_2_), channel_id=1, source_target_pairs={{0,1},{1,0},{2,3},{3,2},{4,5},{5,4},{6,7},{7,6},{8,9},{9,8},{10,11... | collective-permute-start | bytes 786440 | tf_op jit(solution)/shard_map/ppermute | solution.py:306
  55.3 6.1 %collective-permute-start.14 = (bf16[256,512]{1,0:T(8,128)(2,1)S(1)}, bf16[256,512]{1,0:T(8,128)(2,1)S(1)}, u32[]{:S(2)}, u32[]{:S(2)}) collective-permute-start(bf16[256,512]{1,0:T(8,128)(2,1)S(1)} %shard_map.134.refs_0_.refs_2_), channel_id=1, source_target_pairs={{0,25},{1,24},{8,0},{9,1},{16,8},{17,9},{24,16},{25,17},{2,27},{3,... | collective-permute-start | bytes 786440 | tf_op jit(solution)/shard_map/ppermute | solution.py:448
  55.3 6.1 %collective-permute-start.15 = (bf16[256,512]{1,0:T(8,128)(2,1)S(1)}, bf16[256,512]{1,0:T(8,128)(2,1)S(1)}, u32[]{:S(2)}, u32[]{:S(2)}) collective-permute-start(bf16[256,512]{1,0:T(8,128)(2,1)S(1)} %shard_map.134.refs_0_.refs_2_), channel_id=1, source_target_pairs={{0,8},{8,0},{16,24},{24,16},{1,9},{9,1},{17,25},{25,17},{2,10},{10... | collective-permute-start | bytes 786440 | tf_op jit(solution)/shard_map/ppermute | solution.py:306
  61.4 1.6 %collective-permute-start.16 = (bf16[256,512]{1,0:T(8,128)(2,1)S(1)}, bf16[256,512]{1,0:T(8,128)(2,1)S(1)}, u32[]{:S(2)}, u32[]{:S(2)}) collective-permute-start(bf16[256,512]{1,0:T(8,128)(2,1)S(1)} %shard_map.135.refs_0_), channel_id=1, source_target_pairs={{0,8},{8,0},{16,24},{24,16},{1,9},{9,1},{17,25},{25,17},{2,10},{10... | collective-permute-start | bytes 786440 | tf_op jit(solution)/shard_map/ppermute | solution.py:306
  63.0 2.9 %collective-permute-start.17 = (bf16[256,512]{1,0:T(8,128)(2,1)S(1)}, bf16[256,512]{1,0:T(8,128)(2,1)S(1)}, u32[]{:S(2)}, u32[]{:S(2)}) collective-permute-start(bf16[256,512]{1,0:T(8,128)(2,1)S(1)} %get-tuple-element.51), channel_id=1, source_target_pairs={{0,8},{8,0},{16,24},{24,16},{1,9},{9,1},{17,25},{25,17},{2,10},{10... | collective-permute-start | bytes 786440 | tf_op jit(solution)/shard_map/ppermute | solution.py:306
  66.1 5.3 %collective-permute-start.20 = (bf16[256,128]{1,0:T(8,128)(2,1)S(1)}, bf16[256,128]{1,0:T(8,128)(2,1)S(1)}, u32[]{:S(2)}, u32[]{:S(2)}) collective-permute-start(bf16[256,128]{1,0:T(8,128)(2,1)S(1)} %get-tuple-element.55), channel_id=1, source_target_pairs={{0,17},{1,16},{8,25},{9,24},{16,1},{17,0},{24,9},{25,8},{2,19},{3,... | collective-permute-start | bytes 196616 | tf_op jit(solution)/shard_map/ppermute | solution.py:510
  69.0 4.3 %collective-permute-start.19 = (bf16[256,128]{1,0:T(8,128)(2,1)S(1)}, bf16[256,128]{1,0:T(8,128)(2,1)S(1)}, u32[]{:S(2)}, u32[]{:S(2)}) collective-permute-start(bf16[256,128]{1,0:T(8,128)(2,1)S(1)} %get-tuple-element.54), channel_id=1, source_target_pairs={{0,16},{1,17},{8,24},{9,25},{16,0},{17,1},{24,8},{25,9},{2,18},{3,... | collective-permute-start | bytes 196616 | tf_op jit(solution)/shard_map/ppermute | solution.py:510
  69.0 4.3 %collective-permute-start.18 = (bf16[256,128]{1,0:T(8,128)(2,1)S(1)}, bf16[256,128]{1,0:T(8,128)(2,1)S(1)}, u32[]{:S(2)}, u32[]{:S(2)}) collective-permute-start(bf16[256,128]{1,0:T(8,128)(2,1)S(1)} %get-tuple-element.53), channel_id=1, source_target_pairs={{0,1},{1,0},{8,9},{9,8},{16,17},{17,16},{24,25},{25,24},{2,3},{3,2... | collective-permute-start | bytes 196616 | tf_op jit(solution)/shard_map/ppermute | solution.py:510
